TPU v7x, 32 devices: a whole 2x2x4 slice. The times are simulated.
32 devices in a mesh: wide: 16 (over z, y, x), narrow: 2 (over core).
Axes of the slice: x: 2, y: 2, z: 4, core: 2. Of those that a mesh axis runs over, the one named last changes fastest.
Arguments:
- tokens: int32 [128, 20, 16], P('wide'), may hold values from 0 to 511
- actions: int32 [128, 20], P('wide'), may hold values from 0 to 17
- game_ids: int32 [128], P('wide'), may hold values from 0 to 25
- valid_steps: int32 [128, 20], P('wide'), may hold values from 0 to 1, as said below
- rewards: int32 [128, 20], P('wide'), may hold values from 0 to 2
- end_flags: int32 [128, 20], P('wide'), may hold values from 0 to 1
- embed_table: float32 [896, 256], P(None, 'wide'), may hold values from -6 to 6
- table_first: float32 [896, 256], P(None, 'wide'), may hold values from -0.0009765625 to 0.0009765625
- table_second: float32 [896, 256], P(None, 'wide'), may hold values from 5.154044e-09 to 2.0616175e-08
- attn_weight: float32 [2, 3, 256, 256], P(None, None, 'wide', 'narrow'), may hold values from -0.375 to 0.375
- attn_first: float32 [2, 3, 256, 256], P(None, None, 'wide', 'narrow'), may hold values from -0.0009765625 to 0.0009765625
- attn_second: float32 [2, 3, 256, 256], P(None, None, 'wide', 'narrow'), may hold values from 5.154044e-09 to 2.0616175e-08
- proj_weight: float32 [2, 256, 256], P(None, 'narrow', 'wide'), may hold values from -3 to 3
- proj_first: float32 [2, 256, 256], P(None, 'narrow', 'wide'), may hold values from -0.0009765625 to 0.0009765625
- proj_second: float32 [2, 256, 256], P(None, 'narrow', 'wide'), may hold values from 5.154044e-09 to 2.0616175e-08
- up_weight: float32 [2, 256, 1024], P(None, 'wide', 'narrow'), may hold values from -0.375 to 0.375
- up_first: float32 [2, 256, 1024], P(None, 'wide', 'narrow'), may hold values from -0.0009765625 to 0.0009765625
- up_second: float32 [2, 256, 1024], P(None, 'wide', 'narrow'), may hold values from 5.154044e-09 to 2.0616175e-08
- up_bias: float32 [2, 1024], P(None, 'narrow'), may hold values from -0.35 to 0.35
- bias_first: float32 [2, 1024], P(None, 'narrow'), may hold values from -0.00030517578 to 0.00030517578
- bias_second: float32 [2, 1024], P(None, 'narrow'), may hold values from 4.1232354e-10 to 1.6492941e-09
- down_weight: float32 [2, 1024, 256], P(None, 'narrow', 'wide'), may hold values from -0.1875 to 0.1875
- down_first: float32 [2, 1024, 256], P(None, 'narrow', 'wide'), may hold values from -0.0009765625 to 0.0009765625
- down_second: float32 [2, 1024, 256], P(None, 'narrow', 'wide'), may hold values from 5.154044e-09 to 2.0616175e-08
- vectors: float32 [14, 256], replicated, may hold values from -0.5 to 2.4
- vectors_first: float32 [14, 256], replicated, may hold values from -0.0034179688 to 0.0034179688
- vectors_second: float32 [14, 256], replicated, may hold values from 4.6386397e-08 to 1.8554559e-07
- head_weight: float32 [256, 512], P('wide', 'narrow'), may hold values from -0.32 to 0.32
- head_first: float32 [256, 512], P('wide', 'narrow'), may hold values from -0.0009765625 to 0.0009765625
- head_second: float32 [256, 512], P('wide', 'narrow'), may hold values from 5.154044e-09 to 2.0616175e-08
- side_weight: float32 [256, 5], P('wide'), may hold values from -0.375 to 0.375
- side_first: float32 [256, 5], P('wide'), may hold values from -0.0009765625 to 0.0009765625
- side_second: float32 [256, 5], P('wide'), may hold values from 5.154044e-09 to 2.0616175e-08
Outputs:
- loss_sum: float32 [], replicated
- valid_total: float32 [], replicated
- grad_norm: float32 [], replicated
- table_new: float32 [896, 256], P(None, 'wide')
- table_first_new: float32 [896, 256], P(None, 'wide')
- table_second_new: float32 [896, 256], P(None, 'wide')
- attn_new: float32 [2, 3, 256, 256], P(None, None, 'wide', 'narrow')
- attn_first_new: float32 [2, 3, 256, 256], P(None, None, 'wide', 'narrow')
- attn_second_new: float32 [2, 3, 256, 256], P(None, None, 'wide', 'narrow')
- proj_new: float32 [2, 256, 256], P(None, 'narrow', 'wide')
- proj_first_new: float32 [2, 256, 256], P(None, 'narrow', 'wide')
- proj_second_new: float32 [2, 256, 256], P(None, 'narrow', 'wide')
- up_new: float32 [2, 256, 1024], P(None, 'wide', 'narrow')
- up_first_new: float32 [2, 256, 1024], P(None, 'wide', 'narrow')
- up_second_new: float32 [2, 256, 1024], P(None, 'wide', 'narrow')
- bias_new: float32 [2, 1024], P(None, 'narrow')
- bias_first_new: float32 [2, 1024], P(None, 'narrow')
- bias_second_new: float32 [2, 1024], P(None, 'narrow')
- down_new: float32 [2, 1024, 256], P(None, 'narrow', 'wide')
- down_first_new: float32 [2, 1024, 256], P(None, 'narrow', 'wide')
- down_second_new: float32 [2, 1024, 256], P(None, 'narrow', 'wide')
- vectors_new: float32 [14, 256], replicated
- vectors_first_new: float32 [14, 256], replicated
- vectors_second_new: float32 [14, 256], replicated
- head_new: float32 [256, 512], P('wide', 'narrow')
- head_first_new: float32 [256, 512], P('wide', 'narrow')
- head_second_new: float32 [256, 512], P('wide', 'narrow')
- side_new: float32 [256, 5], P('wide')
- side_first_new: float32 [256, 5], P('wide')
- side_second_new: float32 [256, 5], P('wide')
Inputs may be any that keep to these rules, and one draw needn't show every extreme that they name: `valid_steps`: frame 0 of every sequence is valid.
All inputs are finite; a program needn't handle non-finite values.
Results may differ from a plain program's by a relative error of at most 0.0098.
Values may be sent and summed in bfloat16 or wider, within the bound.
No kernel may reach another device: no remote copies, remote signals or barrier semaphores. Data moves between devices by JAX's collectives and lax.ppermute only.
A program may use at most 192 MiB of HBM per device.

v0:
```python
import jax
import jax.numpy as jnp
from jax import lax
from jax.sharding import PartitionSpec as P

HEAD_DIM = 64
VOCAB = 512
ACTIONS = 18
GAMES = 26
OBS = 16
FRAMES = 20
L = 2
MICRO = 2
STEP_NUMBER = 5
FRAME_TOKENS = 17
LENGTH = 340
ROWS = 896


EPS_NORM = 1e-05
BETA_ONE = 0.5
BETA_TWO = 0.5
RATE_TABLE = 0.5
RATE_MATRIX = 0.05
RATE_VECTOR = 0.2
DECAY_RATE = 0.01
EPS_ADAM = 1e-08
CLIP_AT = 0.1


def combined_all(part, axis, combine):
    gathered = jax.tree.map(lambda a: lax.all_gather(a, axis), part)

    def take(source):
        return jax.tree.map(lambda a: lax.dynamic_index_in_dim(a, source, 0, False), gathered)

    return lax.fori_loop(
        1, lax.axis_size(axis), lambda source, state: combine(state, take(source)), take(0)
    )


def layer_norm(stream, gain, offset):
    row_mean = jnp.mean(stream, axis=-1, keepdims=True)
    centred = stream - row_mean
    variance = jnp.mean(centred * centred, axis=-1, keepdims=True)
    return centred * lax.rsqrt(variance + EPS_NORM) * gain + offset


def arrange(tokens, actions, valid_steps):
    seq_count = tokens.shape[0]
    row_ids = jnp.concatenate([tokens, actions[:, :, None] + VOCAB], axis=2).reshape(
        seq_count, LENGTH
    )
    first_next = jnp.concatenate([tokens[:, 1:, 0], jnp.zeros((seq_count, 1), jnp.int32)], axis=1)
    targets = jnp.concatenate(
        [tokens[:, :, 1:], jnp.zeros((seq_count, FRAMES, 1), jnp.int32), first_next[:, :, None]],
        axis=2,
    ).reshape(seq_count, LENGTH)
    valid_float = valid_steps.astype(jnp.float32)
    next_valid = jnp.concatenate(
        [valid_float[:, 1:], jnp.zeros((seq_count, 1), jnp.float32)], axis=1
    )
    row_weight = jnp.concatenate(
        [
            jnp.broadcast_to(valid_float[:, :, None], (seq_count, FRAMES, OBS - 1)),
            jnp.zeros((seq_count, FRAMES, 1), jnp.float32),
            next_valid[:, :, None],
        ],
        axis=2,
    ).reshape(seq_count, LENGTH)
    return (row_ids, targets, row_weight, valid_float)


def side_loss(side_logits, rewards, end_flags, valid_float):
    reward_logits = side_logits[..., :3]
    end_logits = side_logits[..., 3:]
    reward_pick = jnp.sum(
        jnp.where(rewards[..., None] == jnp.arange(3), reward_logits, 0.0), axis=-1
    )
    end_pick = jnp.sum(jnp.where(end_flags[..., None] == jnp.arange(2), end_logits, 0.0), axis=-1)
    terms = (
        jax.nn.logsumexp(reward_logits, axis=-1)
        - reward_pick
        + jax.nn.logsumexp(end_logits, axis=-1)
        - end_pick
    )
    return jnp.sum(valid_float * terms)


def narrow_total(partial_sum):
    return lax.psum(partial_sum.astype(jnp.bfloat16), "narrow").astype(jnp.float32)


def narrow_back(partial_sum):
    return lax.psum(partial_sum.astype(jnp.bfloat16), "narrow").astype(jnp.float32)


def combine_stats(earlier, later):
    peak = jnp.maximum(earlier[0], later[0])
    total_exp = earlier[1] * jnp.exp(earlier[0] - peak) + later[1] * jnp.exp(later[0] - peak)
    return (peak, total_exp, earlier[2] + later[2])


def layer_copy(attn_weight, proj_weight, up_weight, down_weight, index):
    return (
        lax.all_gather(attn_weight[index].astype(jnp.bfloat16), "wide", axis=1, tiled=True),
        lax.all_gather(proj_weight[index].astype(jnp.bfloat16), "wide", axis=1, tiled=True),
        lax.all_gather(up_weight[index].astype(jnp.bfloat16), "wide", axis=0, tiled=True),
        lax.all_gather(down_weight[index].astype(jnp.bfloat16), "wide", axis=1, tiled=True),
    )


def embed_rows(row_ids, game_ids, seq_count):
    rows_iota = jnp.arange(ROWS)
    game_rows = VOCAB + ACTIONS + game_ids
    place_rows = VOCAB + ACTIONS + GAMES + jnp.arange(LENGTH)
    hits = (
        (row_ids[:, :, None] == rows_iota)
        | (game_rows[:, None, None] == rows_iota)
        | (place_rows[None, :, None] == rows_iota)
    )
    return hits.reshape(seq_count * LENGTH, ROWS).astype(jnp.bfloat16)


def project(normed16, attn16, seq_count):
    projected = jnp.einsum(
        "td,jde->jte", normed16, attn16, preferred_element_type=jnp.float32
    ).astype(jnp.bfloat16)
    return projected.reshape(3, seq_count, LENGTH, -1, HEAD_DIM)


def attend_scores(query, keys):
    scores = jnp.einsum("bqhe,bkhe->bhqk", query, keys, preferred_element_type=jnp.float32) * 0.125
    causal = jnp.arange(LENGTH)[:, None] >= jnp.arange(LENGTH)[None, :]
    return jnp.where(causal, scores, -1e30)


def layer_forward(stream, weights_now, vectors, bias_row, index, seq_count):
    attn16, proj16, up16, down16 = weights_now
    layer_vec = vectors[6 * index : 6 * index + 6]
    normed16 = layer_norm(stream, layer_vec[0], layer_vec[1]).astype(jnp.bfloat16)
    projected = project(normed16, attn16, seq_count)
    scores = attend_scores(projected[0], projected[1])
    row_peak = jnp.max(scores, axis=-1, keepdims=True)
    expanded = jnp.exp(scores - row_peak)
    row_total = jnp.sum(expanded, axis=-1, keepdims=True)
    probs16 = (expanded / row_total).astype(jnp.bfloat16)
    head_out = (
        jnp.einsum("bhqk,bkhe->bqhe", probs16, projected[2], preferred_element_type=jnp.float32)
        .astype(jnp.bfloat16)
        .reshape(stream.shape[0], -1)
    )
    middle = stream + (
        narrow_total(jnp.dot(head_out, proj16, preferred_element_type=jnp.float32)) + layer_vec[2]
    )
    normed16 = layer_norm(middle, layer_vec[3], layer_vec[4]).astype(jnp.bfloat16)
    up_proj = jnp.dot(normed16, up16, preferred_element_type=jnp.float32) + bias_row
    hidden = jax.nn.gelu(up_proj).astype(jnp.bfloat16)
    result = middle + (
        narrow_total(jnp.dot(hidden, down16, preferred_element_type=jnp.float32)) + layer_vec[5]
    )
    return (middle, result, row_peak + jnp.log(row_total))


def layer_backward(
    grad_in, stream, middle, log_total, weights_now, vectors, bias_row, index, seq_count
):
    attn16, proj16, up16, down16 = weights_now
    layer_vec = vectors[6 * index : 6 * index + 6]
    row_count = stream.shape[0]
    grad_out16 = grad_in.astype(jnp.bfloat16)
    normed, norm_pull = jax.vjp(layer_norm, middle, layer_vec[3], layer_vec[4])
    normed16 = normed.astype(jnp.bfloat16)
    up_proj = jnp.dot(normed16, up16, preferred_element_type=jnp.float32) + bias_row
    activated, gelu_pull = jax.vjp(jax.nn.gelu, up_proj)
    hidden = activated.astype(jnp.bfloat16)
    grad_down = jnp.einsum("tf,td->fd", hidden, grad_out16, preferred_element_type=jnp.float32)
    grad_hidden = jnp.einsum("td,fd->tf", grad_out16, down16, preferred_element_type=jnp.float32)
    grad_up = gelu_pull(grad_hidden)[0].astype(jnp.bfloat16)
    grad_upw = jnp.einsum("td,tf->df", normed16, grad_up, preferred_element_type=jnp.float32)
    grad_normed = narrow_back(
        jnp.einsum("tf,df->td", grad_up, up16, preferred_element_type=jnp.float32)
    )
    grad_mid, grad_gain_two, grad_shift_two = norm_pull(grad_normed)
    grad_mid = grad_in + grad_mid
    grad_att16 = grad_mid.astype(jnp.bfloat16)
    normed, norm_pull = jax.vjp(layer_norm, stream, layer_vec[0], layer_vec[1])
    normed16 = normed.astype(jnp.bfloat16)
    projected = project(normed16, attn16, seq_count)
    query, keys, values = (projected[0], projected[1], projected[2])
    attn_probs = jnp.exp(attend_scores(query, keys) - log_total)
    probs16 = attn_probs.astype(jnp.bfloat16)
    head_out = (
        jnp.einsum("bhqk,bkhe->bqhe", probs16, values, preferred_element_type=jnp.float32)
        .astype(jnp.bfloat16)
        .reshape(row_count, -1)
    )
    grad_proj = jnp.einsum("te,td->ed", head_out, grad_att16, preferred_element_type=jnp.float32)
    grad_heads = (
        jnp.einsum("td,ed->te", grad_att16, proj16, preferred_element_type=jnp.float32)
        .astype(jnp.bfloat16)
        .reshape(query.shape)
    )
    grad_probs = jnp.einsum(
        "bqhe,bkhe->bhqk", grad_heads, values, preferred_element_type=jnp.float32
    )
    inner = jnp.sum(attn_probs * grad_probs, axis=-1, keepdims=True)
    grad_scores = (attn_probs * (grad_probs - inner)).astype(jnp.bfloat16)
    grad_query = (
        jnp.einsum("bhqk,bkhe->bqhe", grad_scores, keys, preferred_element_type=jnp.float32) * 0.125
    )
    grad_keys = (
        jnp.einsum("bhqk,bqhe->bkhe", grad_scores, query, preferred_element_type=jnp.float32)
        * 0.125
    )
    grad_values = jnp.einsum(
        "bhqk,bqhe->bkhe", probs16, grad_heads, preferred_element_type=jnp.float32
    )
    grad_projected = (
        jnp.stack([grad_query, grad_keys, grad_values])
        .astype(jnp.bfloat16)
        .reshape(3, row_count, -1)
    )
    grad_attn = jnp.einsum(
        "td,jte->jde", normed16, grad_projected, preferred_element_type=jnp.float32
    )
    grad_normed = narrow_back(
        jnp.einsum("jte,jde->td", grad_projected, attn16, preferred_element_type=jnp.float32)
    )
    grad_stream, grad_gain_one, grad_shift_one = norm_pull(grad_normed)
    vector_grads = jnp.stack(
        [
            grad_gain_one,
            grad_shift_one,
            jnp.sum(grad_att16.astype(jnp.float32), axis=0),
            grad_gain_two,
            grad_shift_two,
            jnp.sum(grad_out16.astype(jnp.float32), axis=0),
        ]
    )
    bias_grad = jnp.sum(grad_up.astype(jnp.float32), axis=0)
    return (
        grad_mid + grad_stream,
        (grad_attn, grad_proj, grad_upw, grad_down),
        vector_grads,
        bias_grad,
    )


def head_pass(
    stream,
    vectors,
    head16,
    side16,
    targets,
    row_weight,
    rewards,
    end_flags,
    valid_float,
    inverse,
    seq_count,
):
    final_norm, final_pull = jax.vjp(layer_norm, stream, vectors[6 * L], vectors[6 * L + 1])
    final16 = final_norm.astype(jnp.bfloat16)
    logits = jnp.dot(final16, head16, preferred_element_type=jnp.float32)
    part_vocab = head16.shape[1]
    offset = lax.axis_index("narrow") * part_vocab
    columns = offset + jnp.arange(part_vocab)
    target_hit = targets.reshape(-1)[:, None] == columns[None, :]
    local_peak = jnp.max(logits, axis=1)
    local_total = jnp.sum(jnp.exp(logits - local_peak[:, None]), axis=1)
    local_pick = jnp.sum(jnp.where(target_hit, logits, 0.0), axis=1)
    peak, total_exp, picked = combined_all(
        (local_peak, local_total, local_pick), "narrow", combine_stats
    )
    log_total = peak + jnp.log(total_exp)
    flat_weight = row_weight.reshape(-1)
    token_loss = jnp.sum(flat_weight * (log_total - picked))
    grad_logits = (
        (jnp.exp(logits - log_total[:, None]) - target_hit.astype(jnp.float32))
        * (flat_weight * inverse)[:, None]
    ).astype(jnp.bfloat16)
    grad_head = jnp.einsum("td,tv->dv", final16, grad_logits, preferred_element_type=jnp.float32)
    grad_final = narrow_back(
        jnp.einsum("tv,dv->td", grad_logits, head16, preferred_element_type=jnp.float32)
    )
    acting = final16.reshape(seq_count, FRAMES, FRAME_TOKENS, -1)[:, :, OBS]
    side_logits = jnp.einsum("sfd,dc->sfc", acting, side16, preferred_element_type=jnp.float32)
    side_value, side_pull = jax.vjp(
        lambda values: side_loss(values, rewards, end_flags, valid_float), side_logits
    )
    grad_side16 = side_pull(inverse)[0].astype(jnp.bfloat16)
    grad_sidew = jnp.einsum("sfd,sfc->dc", acting, grad_side16, preferred_element_type=jnp.float32)
    grad_acting = jnp.einsum("sfc,dc->sfd", grad_side16, side16, preferred_element_type=jnp.float32)
    grad_final = grad_final.reshape(seq_count, FRAMES, FRAME_TOKENS, -1) + jnp.pad(
        grad_acting[:, :, None, :], ((0, 0), (0, 0), (OBS, 0), (0, 0))
    )
    grad_stream, grad_gain, grad_shift = final_pull(grad_final.reshape(final_norm.shape))
    return (
        token_loss + side_value,
        grad_stream,
        grad_head,
        grad_sidew,
        jnp.stack([grad_gain, grad_shift]),
    )


def adam(weight, moment, second, gradient, step_rate, decay_rate):
    moment_new = BETA_ONE * moment + (1.0 - BETA_ONE) * gradient
    second_new = BETA_TWO * second + (1.0 - BETA_TWO) * gradient * gradient
    moment_hat = moment_new / (1.0 - BETA_ONE**STEP_NUMBER)
    second_hat = second_new / (1.0 - BETA_TWO**STEP_NUMBER)
    weight_new = weight - step_rate * (
        moment_hat / (jnp.sqrt(second_hat) + EPS_ADAM) + decay_rate * weight
    )
    return (weight_new, moment_new, second_new)


def per_device(
    tokens,
    actions,
    game_ids,
    valid_steps,
    rewards,
    end_flags,
    embed_table,
    table_first,
    table_second,
    attn_weight,
    attn_first,
    attn_second,
    proj_weight,
    proj_first,
    proj_second,
    up_weight,
    up_first,
    up_second,
    up_bias,
    bias_first,
    bias_second,
    down_weight,
    down_first,
    down_second,
    vectors,
    vectors_first,
    vectors_second,
    head_weight,
    head_first,
    head_second,
    side_weight,
    side_first,
    side_second,
):
    layer_count = attn_weight.shape[0]
    micro_seqs = tokens.shape[0] // MICRO
    row_ids, targets, row_weight, valid_float = arrange(tokens, actions, valid_steps)
    total_valid = lax.psum(jnp.sum(valid_float), "wide")
    inverse = 1.0 / total_valid
    table16, head16, side16 = (
        lax.all_gather(embed_table.astype(jnp.bfloat16), "wide", axis=1, tiled=True),
        lax.all_gather(head_weight.astype(jnp.bfloat16), "wide", axis=0, tiled=True),
        lax.all_gather(side_weight.astype(jnp.bfloat16), "wide", axis=0, tiled=True),
    )
    own_seqs = tokens.shape[0]
    row_ids, targets, row_weight, valid_float = (row_ids, targets, row_weight, valid_float)
    own_games, own_rewards, own_ends = (game_ids, rewards, end_flags)
    layer_acc = [None] * layer_count
    vector_acc = jnp.zeros_like(vectors)
    bias_acc = jnp.zeros(up_bias.shape, jnp.float32)
    table_acc = jnp.zeros(table16.shape, jnp.float32)
    head_acc = jnp.zeros(head16.shape, jnp.float32)
    side_acc = jnp.zeros(side16.shape, jnp.float32)
    loss_acc = jnp.zeros((), jnp.float32)
    for micro_index in range(own_seqs // micro_seqs):
        lower = micro_index * micro_seqs
        upper = lower + micro_seqs
        hits = embed_rows(row_ids[lower:upper], own_games[lower:upper], micro_seqs)
        stream = jnp.dot(hits, table16, preferred_element_type=jnp.float32)
        kept = []
        for index in range(layer_count):
            weights_now = layer_copy(attn_weight, proj_weight, up_weight, down_weight, index)
            middle, result, log_total = layer_forward(
                stream, weights_now, vectors, up_bias[index], index, micro_seqs
            )
            kept.append((stream, middle, log_total))
            stream = result
        loss_part, grad_stream, grad_head, grad_side, final_grads = head_pass(
            stream,
            vectors,
            head16,
            side16,
            targets[lower:upper],
            row_weight[lower:upper],
            own_rewards[lower:upper],
            own_ends[lower:upper],
            valid_float[lower:upper],
            inverse,
            micro_seqs,
        )
        loss_acc = loss_acc + loss_part
        head_acc = head_acc + grad_head
        side_acc = side_acc + grad_side
        vector_acc = vector_acc.at[6 * layer_count :].add(final_grads)
        for index in reversed(range(layer_count)):
            weights_now = layer_copy(attn_weight, proj_weight, up_weight, down_weight, index)
            saved_stream, saved_middle, saved_total = kept[index]
            grad_stream, layer_grads, vector_grads, bias_grad = layer_backward(
                grad_stream,
                saved_stream,
                saved_middle,
                saved_total,
                weights_now,
                vectors,
                up_bias[index],
                index,
                micro_seqs,
            )
            layer_acc[index] = (
                layer_grads
                if layer_acc[index] is None
                else jax.tree.map(jnp.add, layer_acc[index], layer_grads)
            )
            vector_acc = vector_acc.at[6 * index : 6 * index + 6].add(vector_grads)
            bias_acc = bias_acc.at[index].add(bias_grad)
        table_acc = table_acc + jnp.einsum(
            "tr,td->rd", hits, grad_stream.astype(jnp.bfloat16), preferred_element_type=jnp.float32
        )
    stacked = [jnp.stack([entry[member] for entry in layer_acc]) for member in range(4)]
    attn_grad, proj_grad, up_grad, down_grad, table_grad, head_grad, side_grad = (
        lax.psum_scatter(stacked[0], "wide", scatter_dimension=2, tiled=True),
        lax.psum_scatter(stacked[1], "wide", scatter_dimension=2, tiled=True),
        lax.psum_scatter(stacked[2], "wide", scatter_dimension=1, tiled=True),
        lax.psum_scatter(stacked[3], "wide", scatter_dimension=2, tiled=True),
        lax.psum_scatter(table_acc, "wide", scatter_dimension=1, tiled=True),
        lax.psum_scatter(head_acc, "wide", scatter_dimension=0, tiled=True),
        lax.psum_scatter(side_acc, "wide", scatter_dimension=0, tiled=True),
    )
    vector_grad, bias_grad = lax.psum((vector_acc, bias_acc), "wide")
    narrow_first = lax.axis_index("narrow") == 0
    wide_first = lax.axis_index("wide") == 0
    shared = sum(
        (
            jnp.sum(member * member)
            for member in (attn_grad, proj_grad, up_grad, down_grad, head_grad)
        )
    )
    shared = shared + jnp.where(
        narrow_first, jnp.sum(table_grad * table_grad) + jnp.sum(side_grad * side_grad), 0.0
    )
    shared = shared + jnp.where(wide_first, jnp.sum(bias_grad * bias_grad), 0.0)
    shared = shared + jnp.where(narrow_first & wide_first, jnp.sum(vector_grad * vector_grad), 0.0)
    loss_term = jnp.where(narrow_first, loss_acc, 0.0)
    square_total, loss_sum = lax.psum((shared, loss_term), ("wide", "narrow"))
    grad_norm = jnp.sqrt(square_total)
    clip_factor = jnp.minimum(1.0, CLIP_AT / (grad_norm + 1e-06))
    results = []
    results.extend(
        adam(
            embed_table, table_first, table_second, clip_factor * table_grad, RATE_TABLE, DECAY_RATE
        )
    )
    results.extend(
        adam(attn_weight, attn_first, attn_second, clip_factor * attn_grad, RATE_MATRIX, DECAY_RATE)
    )
    results.extend(
        adam(proj_weight, proj_first, proj_second, clip_factor * proj_grad, RATE_MATRIX, DECAY_RATE)
    )
    results.extend(
        adam(up_weight, up_first, up_second, clip_factor * up_grad, RATE_MATRIX, DECAY_RATE)
    )
    results.extend(
        adam(up_bias, bias_first, bias_second, clip_factor * bias_grad, RATE_VECTOR, 0.0)
    )
    results.extend(
        adam(down_weight, down_first, down_second, clip_factor * down_grad, RATE_MATRIX, DECAY_RATE)
    )
    results.extend(
        adam(vectors, vectors_first, vectors_second, clip_factor * vector_grad, RATE_VECTOR, 0.0)
    )
    results.extend(
        adam(head_weight, head_first, head_second, clip_factor * head_grad, RATE_MATRIX, DECAY_RATE)
    )
    results.extend(
        adam(side_weight, side_first, side_second, clip_factor * side_grad, RATE_MATRIX, DECAY_RATE)
    )
    return (loss_sum, total_valid, grad_norm) + tuple(results)


def solution(mesh):
    placed = (
        P("wide", None, None),
        P("wide", None),
        P("wide"),
        P("wide", None),
        P("wide", None),
        P("wide", None),
        P(None, "wide"),
        P(None, "wide"),
        P(None, "wide"),
        P(None, None, "wide", "narrow"),
        P(None, None, "wide", "narrow"),
        P(None, None, "wide", "narrow"),
        P(None, "narrow", "wide"),
        P(None, "narrow", "wide"),
        P(None, "narrow", "wide"),
        P(None, "wide", "narrow"),
        P(None, "wide", "narrow"),
        P(None, "wide", "narrow"),
        P(None, "narrow"),
        P(None, "narrow"),
        P(None, "narrow"),
        P(None, "narrow", "wide"),
        P(None, "narrow", "wide"),
        P(None, "narrow", "wide"),
        P(),
        P(),
        P(),
        P("wide", "narrow"),
        P("wide", "narrow"),
        P("wide", "narrow"),
        P("wide", None),
        P("wide", None),
        P("wide", None),
    )
    return jax.shard_map(
        per_device,
        mesh=mesh,
        in_specs=placed,
        out_specs=(
            P(),
            P(),
            P(),
            P(None, "wide"),
            P(None, "wide"),
            P(None, "wide"),
            P(None, None, "wide", "narrow"),
            P(None, None, "wide", "narrow"),
            P(None, None, "wide", "narrow"),
            P(None, "narrow", "wide"),
            P(None, "narrow", "wide"),
            P(None, "narrow", "wide"),
            P(None, "wide", "narrow"),
            P(None, "wide", "narrow"),
            P(None, "wide", "narrow"),
            P(None, "narrow"),
            P(None, "narrow"),
            P(None, "narrow"),
            P(None, "narrow", "wide"),
            P(None, "narrow", "wide"),
            P(None, "narrow", "wide"),
            P(),
            P(),
            P(),
            P("wide", "narrow"),
            P("wide", "narrow"),
            P("wide", "narrow"),
            P("wide", None),
            P("wide", None),
            P("wide", None),
        ),
        check_vma=False,
    )
```

profile of v0, /device:TPU:0, one launch (start us, length us, event | category | flops | bytes accessed | tf_op | source)
XLA Modules:
  0.0 1460.4 jit_solution(14442174605900270029)
XLA Ops:
  14.0 45.0 %all-gather.1 = bf16[1,128,256]{1,2,0:T(8,128)(2,1)} all-gather(bf16[1,128,16]{1,2,0:T(8,128)(2,1)S(1)} %get-tuple-element.527), channel_id=3, replica_groups=mesh['wide'=16,'narrow'=2] {'wide'}, dimensions={2}, use_global_device_ids=true | all-gather | bytes 69632 | tf_op jit(solution)/shard_map/all_gather | solution.py:107
  60.3 36.6 %all-gather = bf16[1,3,256,128]{3,2,1,0:T(8,128)(2,1)S(1)} all-gather(bf16[1,3,16,128]{3,2,1,0:T(8,128)(2,1)S(1)} %get-tuple-element.501), channel_id=2, replica_groups=mesh['wide'=16,'narrow'=2] {'wide'}, dimensions={2}, use_global_device_ids=true | all-gather | bytes 208896 | tf_op jit(solution)/shard_map/all_gather | solution.py:106
  97.2 42.4 %all_gather.46 = bf16[896,256]{0,1:T(8,128)(2,1)} all-gather(bf16[896,16]{0,1:T(8,128)(2,1)S(1)} %convert_element_type.460), channel_id=1, replica_groups=mesh['wide'=16,'narrow'=2] {'wide'}, dimensions={1}, use_global_device_ids=true | all-gather | bytes 487424 | tf_op jit(solution)/shard_map/all_gather | solution.py:360
  144.0 4.2 fusion.1
  204.7 37.0 %all-gather.3 = bf16[1,512,256]{1,2,0:T(8,128)(2,1)S(1)} all-gather(bf16[1,512,16]{1,2,0:T(8,128)(2,1)S(1)} %get-tuple-element.499), channel_id=5, replica_groups=mesh['wide'=16,'narrow'=2] {'wide'}, dimensions={2}, use_global_device_ids=true | all-gather | bytes 278528 | tf_op jit(solution)/shard_map/all_gather | solution.py:109
  242.4 38.7 %all-gather.2 = bf16[1,256,512]{2,1,0:T(8,128)(2,1)S(1)} all-gather(bf16[1,16,512]{2,1,0:T(8,128)(2,1)S(1)} %get-tuple-element.497), channel_id=4, replica_groups=mesh['wide'=16,'narrow'=2] {'wide'}, dimensions={1}, use_global_device_ids=true | all-gather | bytes 278528 | tf_op jit(solution)/shard_map/all_gather | solution.py:108
  291.6 36.0 %all-gather.5 = bf16[1,128,256]{1,2,0:T(8,128)(2,1)S(1)} all-gather(bf16[1,128,16]{1,2,0:T(8,128)(2,1)S(1)} %copy-done.282), channel_id=7, replica_groups=mesh['wide'=16,'narrow'=2] {'wide'}, dimensions={2}, use_global_device_ids=true | all-gather | bytes 69632 | tf_op jit(solution)/shard_map/all_gather | solution.py:107
  327.6 38.7 %all-gather.4 = bf16[1,3,256,128]{3,2,1,0:T(8,128)(2,1)S(1)} all-gather(bf16[1,3,16,128]{3,2,1,0:T(8,128)(2,1)S(1)} %copy-done.240), channel_id=6, replica_groups=mesh['wide'=16,'narrow'=2] {'wide'}, dimensions={2}, use_global_device_ids=true | all-gather | bytes 208896 | tf_op jit(solution)/shard_map/all_gather | solution.py:106
  422.2 37.4 %psum.170 = f32[]{:T(128)} all-reduce(f32[]{:T(128)} %convert_reduce_fusion.20), channel_id=1, replica_groups=mesh['wide'=16,'narrow'=2] {'wide'}, use_global_device_ids=true, to_apply=%region_60.61 | all-reduce | flops 1 | bytes 8 | tf_op jit(solution)/shard_map/psum | solution.py:357
  459.9 37.6 %all-gather.14 = bf16[16,16,5]{1,2,0:T(8,128)(2,1)S(1)} all-gather(bf16[1,16,5]{1,2,0:T(8,128)(2,1)S(1)} %convert_bitcast_fusion), channel_id=1, replica_groups=mesh['wide'=16,'narrow'=2] {'wide'}, dimensions={0}, use_global_device_ids=true | all-gather | bytes 2720 | tf_op jit(solution)/shard_map/all_gather | solution.py:362
  503.2 37.1 %all-gather.7 = bf16[1,512,256]{1,2,0:T(8,128)(2,1)S(1)} all-gather(bf16[1,512,16]{1,2,0:T(8,128)(2,1)S(1)} %copy-done.226), channel_id=9, replica_groups=mesh['wide'=16,'narrow'=2] {'wide'}, dimensions={2}, use_global_device_ids=true | all-gather | bytes 278528 | tf_op jit(solution)/shard_map/all_gather | solution.py:109
  540.3 38.7 %all-gather.6 = bf16[1,256,512]{2,1,0:T(8,128)(2,1)S(1)} all-gather(bf16[1,16,512]{2,1,0:T(8,128)(2,1)S(1)} %copy-done.227), channel_id=8, replica_groups=mesh['wide'=16,'narrow'=2] {'wide'}, dimensions={1}, use_global_device_ids=true | all-gather | bytes 278528 | tf_op jit(solution)/shard_map/all_gather | solution.py:108
  589.3 38.6 %all_gather.102 = bf16[256,256]{1,0:T(8,128)(2,1)} all-gather(bf16[16,256]{1,0:T(8,128)(2,1)S(1)} %convert_element_type.494), channel_id=1, replica_groups=mesh['wide'=16,'narrow'=2] {'wide'}, dimensions={0}, use_global_device_ids=true | all-gather | bytes 139264 | tf_op jit(solution)/shard_map/all_gather | solution.py:361
  647.1 3.2 fusion.295
  658.9 4.1 exponential_reduce_fusion.1
  671.2 4.8 all-reduce.21
  701.9 3.6 fusion.83
  731.8 8.4 all-reduce.52.cloned.1.call-done
  754.0 4.5 multiply_reduce_fusion.4
  772.4 4.0 fusion.112
  784.1 9.7 all-reduce.50.cloned.1.call-done
  793.9 4.0 convert_reduce_fusion.8
  799.8 4.1 convert_reduce_fusion.15
  808.7 3.9 fusion.108
  812.6 3.3 multiply_reduce_fusion.3
  823.5 3.9 fusion.110
  827.4 3.3 multiply_reduce_fusion.1
  870.4 3.8 fusion.113
  883.7 3.2 fusion.115
  890.1 3.1 fusion.114
  900.5 47.3 %reduce-scatter.9.cloned.1.call-done = f32[16,256]{1,0:T(8,128)} async-done(((f32[256,256]{1,0:T(8,128)}), f32[16,256]{1,0:T(8,128)}) %reduce-scatter.9.cloned.1.call-update) | async-done | bytes 16400 | tf_op jit(solution)/shard_map/reduce_scatter | solution.py:435
  952.7 14.1 all-reduce.48.cloned.1.call-done
  966.8 3.3 fusion.88
  974.9 3.2 convert_reduce_fusion.3
  988.3 3.1 fusion.252
  996.4 12.7 all-reduce.46.cloned.1.call-done
  1009.2 4.0 convert_reduce_fusion.6
  1013.2 3.6 fusion.89
  1016.9 6.0 convert_reduce_fusion.13
  1030.2 4.0 fusion.109
  1034.2 3.3 multiply_reduce_fusion.2
  1047.5 4.0 fusion.111
  1051.5 3.3 multiply_reduce_fusion
  1130.2 64.8 %reduce-scatter.7.cloned.1.call-done = f32[2,16,512]{2,1,0:T(8,128)} async-done(((f32[2,256,512]{2,1,0:T(8,128)}), f32[2,16,512]{2,1,0:T(8,128)}) %reduce-scatter.7.cloned.1.call-update) | async-done | bytes 65552 | tf_op jit(solution)/shard_map/reduce_scatter | solution.py:432
  1199.2 73.0 %all-reduce.19 = (f32[2,512]{1,0:T(2,128)S(1)}, f32[14,256]{1,0:T(8,128)S(1)}) all-reduce(f32[2,512]{1,0:T(2,128)S(1)} %scatter-add.34, f32[14,256]{1,0:T(8,128)S(1)} %scatter-add.44), channel_id=1, replica_groups=mesh['wide'=16,'narrow'=2] {'wide'}, use_global_device_ids=true, to_apply=%region_113.114 | all-reduce | flops 4608 | bytes 36864 | tf_op jit(solution)/shard_map/psum | solution.py:438
  1274.7 50.7 %all-reduce.42.cloned.1.call-done = (f32[2,3,256,128]{3,0,1,2:T(2,128)}, f32[2,128,256]{1,0,2:T(2,128)}, f32[2,512,256]{1,0,2:T(2,128)}) async-done(((f32[2,3,256,128]{3,0,1,2:T(2,128)}, f32[2,128,256]{1,0,2:T(2,128)}, f32[2,512,256]{1,0,2:T(2,128)}), (f32[2,3,256,128]{3,0,1,2:T(2,128)}, f32[2,128,256]{1,0,2:T(2,128)}, f32[2,512,256]{1,0,2:T(2,128)})) %all-reduce.42.cloned.1.call-update) | async-done | bytes 2097168
  1332.9 71.4 %reduce-scatter.11.cloned.1.call-done = f32[896,16]{0,1:T(8,128)} async-done(((f32[896,256]{0,1:T(8,128)}), f32[896,16]{0,1:T(8,128)}) %reduce-scatter.11.cloned.1.call-update) | async-done | bytes 57360 | tf_op jit(solution)/shard_map/reduce_scatter | solution.py:434
  1407.1 36.9 %all-reduce.18 = (f32[]{:T(128)}, f32[]{:T(128)}) all-reduce(f32[]{:T(128)S(6)} %select_n.146, f32[]{:T(128)S(6)} %add.1086), channel_id=1, replica_groups=mesh['wide'=16,'narrow'=2] {'wide','narrow'}, use_global_device_ids=true, to_apply=%region_58.59 | all-reduce | flops 2 | bytes 16 | tf_op jit(solution)/shard_map/psum | solution.py:453
  (1098 shorter events, 478.4 us)
Async XLA Ops:
  7.2 274.5 %all-reduce.60.cloned.1.call-start = ((), (), s32[]{:S(2)}) async-start(), calls=%async_computation.17 | async-start | bytes 2785280 | tf_op jit(solution)/shard_map/psum | solution.py:91
  11.7 155.5 %copy-start.235 = (f32[1,256]{1,0:T(1,128)}, f32[1,256]{1,0:T(1,128)S(1)}, u32[]{:S(2)}) copy-start(f32[1,256]{1,0:T(1,128)S(1)} %get-tuple-element.514) | copy-start | bytes 3076
  11.8 155.5 %copy-start.257 = (f32[1,256]{1,0:T(1,128)}, f32[1,256]{1,0:T(1,128)S(1)}, u32[]{:S(2)}) copy-start(f32[1,256]{1,0:T(1,128)S(1)} %get-tuple-element.513) | copy-start | bytes 3076
  11.8 273.4 %copy-start.261 = (f32[1,256]{1,0:T(1,128)}, f32[1,256]{1,0:T(1,128)S(1)}, u32[]{:S(2)}) copy-start(f32[1,256]{1,0:T(1,128)S(1)} %get-tuple-element.511) | copy-start | bytes 3076
  204.0 162.3 %all-reduce.58.cloned.1.call-start = ((), (), s32[]{:S(2)}) async-start(), calls=%async_computation.16 | async-start | bytes 2785280 | tf_op jit(solution)/shard_map/psum | solution.py:91
  291.5 287.4 %all-reduce.56.cloned.1.call-start = ((), (), s32[]{:S(2)}) async-start(), calls=%async_computation.15 | async-start | bytes 2785280 | tf_op jit(solution)/shard_map/psum | solution.py:91
  421.5 157.5 %copy-start.304 = (f32[1,256]{1,0:T(1,128)S(1)}, f32[1,256]{1,0:T(1,128)}, u32[]{:S(2)}) copy-start(f32[1,256]{1,0:T(1,128)} %get-tuple-element.506) | copy-start | bytes 3076
  421.5 209.1 %all-reduce.54.cloned.1.call-start = ((), (), s32[]{:S(2)}) async-start(), calls=%async_computation.14 | async-start | bytes 2785280 | tf_op jit(solution)/shard_map/psum | solution.py:91
  459.6 170.2 %copy-start.189 = (f32[8,20]{1,0:T(8,128)}, f32[8,20]{1,0:T(8,128)S(1)}, u32[]{:S(2)}) copy-start(f32[8,20]{1,0:T(8,128)S(1)} %convert_element_type.459) | copy-start | bytes 1924
  589.3 151.0 %all-reduce.52.cloned.1.call-start = ((), (), s32[]{:S(2)}) async-start(), calls=%async_computation.13 | async-start | bytes 3342336 | tf_op jit(solution)/shard_map/psum | solution.py:95
  721.8 72.0 %all-reduce.50.cloned.1.call-start = ((), (), s32[]{:S(2)}) async-start(), calls=%async_computation.12 | async-start | bytes 2785280 | tf_op jit(solution)/shard_map/psum | solution.py:95
  772.3 126.7 %reduce-scatter.13.cloned.1.call-start = ((), (), s32[]{:S(2)}) async-start(), calls=%async_computation.7 | async-start | bytes 139264
  781.5 166.3 %reduce-scatter.9.cloned.1.call-start = ((), (), s32[]{:S(2)}) async-start(), calls=%async_computation.5 | async-start | bytes 278528 | tf_op jit(solution)/shard_map/reduce_scatter | solution.py:435
  783.9 182.9 %all-reduce.48.cloned.1.call-start = ((), (), s32[]{:S(2)}) async-start(), calls=%async_computation.11 | async-start | bytes 2785280 | tf_op jit(solution)/shard_map/psum | solution.py:95
  870.3 138.7 %all-reduce.46.cloned.1.call-start = ((), (), s32[]{:S(2)}) async-start(), calls=%async_computation.10 | async-start | bytes 2785280 | tf_op jit(solution)/shard_map/psum | solution.py:95
  987.5 130.2 %all-reduce.44.cloned.1.call-start = ((), (), s32[]{:S(2)}) async-start(), calls=%async_computation.9 | async-start | bytes 2785280 | tf_op jit(solution)/shard_map/psum | solution.py:95
  1092.2 102.7 %reduce-scatter.7.cloned.1.call-start = ((), (), s32[]{:S(2)}) async-start(), calls=%async_computation.4 | async-start | bytes 1114112 | tf_op jit(solution)/shard_map/reduce_scatter | solution.py:432
  1102.3 223.1 %all-reduce.42.cloned.1.call-start = ((), (), s32[]{:S(2)}) async-start(), calls=%async_computation.8 | async-start | bytes 4194304
  1117.4 287.0 %reduce-scatter.11.cloned.1.call-start = ((), (), s32[]{:S(2)}) async-start(), calls=%async_computation.6 | async-start | bytes 974848 | tf_op jit(solution)/shard_map/reduce_scatter | solution.py:434
  1126.6 318.2 %copy-start.252 = (f32[16,5]{0,1:T(8,128)S(1)}, f32[16,5]{0,1:T(8,128)}, u32[]{:S(2)}) copy-start(f32[16,5]{0,1:T(8,128)} %copy-done.251) | copy-start | bytes 964
  1126.6 318.2 %copy-start.278 = (f32[16,5]{0,1:T(8,128)S(1)}, f32[16,5]{0,1:T(8,128)}, u32[]{:S(2)}) copy-start(f32[16,5]{0,1:T(8,128)} %param.83) | copy-start | bytes 964
  1126.6 318.2 %copy-start.307 = (f32[16,5]{0,1:T(8,128)S(1)}, f32[16,5]{0,1:T(8,128)}, u32[]{:S(2)}) copy-start(f32[16,5]{0,1:T(8,128)} %param.84) | copy-start | bytes 964
  1126.6 318.9 %copy-start.280 = (f32[2,512]{1,0:T(2,128)S(1)}, f32[2,512]{1,0:T(2,128)}, u32[]{:S(2)}) copy-start(f32[2,512]{1,0:T(2,128)} %param.71) | copy-start | bytes 12292
  1126.6 320.2 %copy-start.232 = (f32[14,256]{1,0:T(8,128)S(1)}, f32[14,256]{1,0:T(8,128)}, u32[]{:S(2)}) copy-start(f32[14,256]{1,0:T(8,128)} %param.77) | copy-start | bytes 43012
  1126.6 320.2 %copy-start.271 = (f32[14,256]{1,0:T(8,128)S(1)}, f32[14,256]{1,0:T(8,128)}, u32[]{:S(2)}) copy-start(f32[14,256]{1,0:T(8,128)} %param.78) | copy-start | bytes 43012
  1126.6 320.2 %copy-start.272 = (f32[14,256]{1,0:T(8,128)S(1)}, f32[14,256]{1,0:T(8,128)}, u32[]{:S(2)}) copy-start(f32[14,256]{1,0:T(8,128)} %param.79) | copy-start | bytes 43012
  1126.6 320.8 %copy-start.222 = (f32[2,128,16]{1,2,0:T(8,128)S(1)}, f32[2,128,16]{1,2,0:T(8,128)}, u32[]{:S(2)}) copy-start(f32[2,128,16]{1,2,0:T(8,128)} %param.65) | copy-start | bytes 49156
  1126.6 320.8 %copy-start.273 = (f32[2,128,16]{1,2,0:T(8,128)S(1)}, f32[2,128,16]{1,2,0:T(8,128)}, u32[]{:S(2)}) copy-start(f32[2,128,16]{1,2,0:T(8,128)} %param.66) | copy-start | bytes 49156
  1126.6 320.8 %copy-start.274 = (f32[2,128,16]{1,2,0:T(8,128)S(1)}, f32[2,128,16]{1,2,0:T(8,128)}, u32[]{:S(2)}) copy-start(f32[2,128,16]{1,2,0:T(8,128)} %param.67) | copy-start | bytes 49156
  1126.7 321.4 %copy-start.166 = (f32[2,3,16,128]{3,2,1,0:T(8,128)S(1)}, f32[2,3,16,128]{3,2,1,0:T(8,128)}, u32[]{:S(2)}) copy-start(f32[2,3,16,128]{3,2,1,0:T(8,128)} %param.62) | copy-start | bytes 147460
  1126.7 321.4 %copy-start.241 = (f32[2,3,16,128]{3,2,1,0:T(8,128)S(1)}, f32[2,3,16,128]{3,2,1,0:T(8,128)}, u32[]{:S(2)}) copy-start(f32[2,3,16,128]{3,2,1,0:T(8,128)} %param.63) | copy-start | bytes 147460
  1126.7 321.4 %copy-start.242 = (f32[2,3,16,128]{3,2,1,0:T(8,128)S(1)}, f32[2,3,16,128]{3,2,1,0:T(8,128)}, u32[]{:S(2)}) copy-start(f32[2,3,16,128]{3,2,1,0:T(8,128)} %param.64) | copy-start | bytes 147460
  1126.7 322.0 %copy-start.149 = (f32[2,512,16]{1,2,0:T(8,128)S(1)}, f32[2,512,16]{1,2,0:T(8,128)}, u32[]{:S(2)}) copy-start(f32[2,512,16]{1,2,0:T(8,128)} %param.74) | copy-start | bytes 196612
  1126.7 322.0 %copy-start.228 = (f32[2,512,16]{1,2,0:T(8,128)S(1)}, f32[2,512,16]{1,2,0:T(8,128)}, u32[]{:S(2)}) copy-start(f32[2,512,16]{1,2,0:T(8,128)} %param.75) | copy-start | bytes 196612
  1126.7 322.0 %copy-start.229 = (f32[2,512,16]{1,2,0:T(8,128)S(1)}, f32[2,512,16]{1,2,0:T(8,128)}, u32[]{:S(2)}) copy-start(f32[2,512,16]{1,2,0:T(8,128)} %param.76) | copy-start | bytes 196612
  1126.7 318.1 %copy-start.308 = (f32[16,5]{0,1:T(8,128)S(1)}, f32[16,5]{0,1:T(8,128)}, u32[]{:S(2)}) copy-start(f32[16,5]{0,1:T(8,128)} %param.85) | copy-start | bytes 964
  1126.7 318.7 %copy-start.309 = (f32[2,512]{1,0:T(2,128)S(1)}, f32[2,512]{1,0:T(2,128)}, u32[]{:S(2)}) copy-start(f32[2,512]{1,0:T(2,128)} %param.72) | copy-start | bytes 12292
  1126.8 322.7 %copy-start.224 = (f32[16,256]{1,0:T(8,128)S(1)}, f32[16,256]{1,0:T(8,128)}, u32[]{:S(2)}) copy-start(f32[16,256]{1,0:T(8,128)} %param.80) | copy-start | bytes 49156
  1126.8 322.7 %copy-start.225 = (f32[16,256]{1,0:T(8,128)S(1)}, f32[16,256]{1,0:T(8,128)}, u32[]{:S(2)}) copy-start(f32[16,256]{1,0:T(8,128)} %reduce-scatter.9.cloned.1.call-done) | copy-start | bytes 49156
  1126.8 322.7 %copy-start.275 = (f32[16,256]{1,0:T(8,128)S(1)}, f32[16,256]{1,0:T(8,128)}, u32[]{:S(2)}) copy-start(f32[16,256]{1,0:T(8,128)} %param.81) | copy-start | bytes 49156
  1126.8 322.7 %copy-start.276 = (f32[16,256]{1,0:T(8,128)S(1)}, f32[16,256]{1,0:T(8,128)}, u32[]{:S(2)}) copy-start(f32[16,256]{1,0:T(8,128)} %param.82) | copy-start | bytes 49156
  1126.8 323.3 %copy-start.153 = (f32[896,16]{0,1:T(8,128)S(1)}, f32[896,16]{0,1:T(8,128)}, u32[]{:S(2)}) copy-start(f32[896,16]{0,1:T(8,128)} %param.59) | copy-start | bytes 172036
  1126.8 323.3 %copy-start.233 = (f32[896,16]{0,1:T(8,128)S(1)}, f32[896,16]{0,1:T(8,128)}, u32[]{:S(2)}) copy-start(f32[896,16]{0,1:T(8,128)} %param.60) | copy-start | bytes 172036
  1126.8 323.3 %copy-start.234 = (f32[896,16]{0,1:T(8,128)S(1)}, f32[896,16]{0,1:T(8,128)}, u32[]{:S(2)}) copy-start(f32[896,16]{0,1:T(8,128)} %param.61) | copy-start | bytes 172036
  1126.9 324.8 %copy-start.151 = (f32[2,16,512]{2,1,0:T(8,128)S(1)}, f32[2,16,512]{2,1,0:T(8,128)}, u32[]{:S(2)}) copy-start(f32[2,16,512]{2,1,0:T(8,128)} %param.68) | copy-start | bytes 196612
  1126.9 324.8 %copy-start.230 = (f32[2,16,512]{2,1,0:T(8,128)S(1)}, f32[2,16,512]{2,1,0:T(8,128)}, u32[]{:S(2)}) copy-start(f32[2,16,512]{2,1,0:T(8,128)} %param.69) | copy-start | bytes 196612
  1126.9 324.7 %copy-start.231 = (f32[2,16,512]{2,1,0:T(8,128)S(1)}, f32[2,16,512]{2,1,0:T(8,128)}, u32[]{:S(2)}) copy-start(f32[2,16,512]{2,1,0:T(8,128)} %param.70) | copy-start | bytes 196612
  1195.0 256.7 %copy-start.152 = (f32[2,16,512]{2,1,0:T(8,128)S(1)}, f32[2,16,512]{2,1,0:T(8,128)}, u32[]{:S(2)}) copy-start(f32[2,16,512]{2,1,0:T(8,128)} %reduce-scatter.7.cloned.1.call-done) | copy-start | bytes 196612
  (295 other events, 2669.1 us)
Sparse Core Ops, SparseCore 0:
  204.1 16.0 all-reduce.59
  291.7 16.1 all-reduce.57
  421.6 16.1 all-reduce.55
  589.4 16.1 all-reduce.53
  722.0 18.2 all-reduce.51
  772.4 21.3 all-reduce.49
  796.0 76.9 reduce-scatter.12
  875.4 72.3 reduce-scatter.8
  950.2 16.5 all-reduce.47
  987.7 21.3 all-reduce.45
  1092.4 21.4 all-reduce.43
  1116.0 78.9 reduce-scatter.6
  1201.6 123.6 all-reduce.41
  1327.5 76.8 reduce-scatter.10
where the time goes:
time: 1480 us; the launch traced here: 1460 us
  blocking collectives  579 us (39%)
  waiting for transfers between devices  279 us (19%)
  local copies, waits for them, and re-layouts  270 us (18%)
  matrix products  169 us (11%)
  other arithmetic  132 us (9%)
  between operations  30.7 us (2%)
    all_gather x2, blocking collectives, layer_copy(): lax.all_gather(proj_weight[index].astype(jnp.bfloat16), 'wide', axis=1, t...  81 us
    all_gather x2, blocking collectives, layer_copy(): lax.all_gather(up_weight[index].astype(jnp.bfloat16), 'wide', axis=0, til...  77.4 us
    all_gather x2, blocking collectives, layer_copy(): lax.all_gather(attn_weight[index].astype(jnp.bfloat16), 'wide', axis=1, t...  75.3 us
    all_gather x2, blocking collectives, layer_copy(): lax.all_gather(down_weight[index].astype(jnp.bfloat16), 'wide', axis=1, t...  74.1 us
    psum x1, blocking collectives, per_device(): vector_grad, bias_grad = lax.psum((vector_acc, bias_acc), 'wide')  73 us
    reduce_scatter x1, waiting for transfers between devices, per_device(): lax.psum_scatter(table_acc, 'wide', scatter_dimension=1, tiled=True)  71.4 us
    reduce_scatter x1, waiting for transfers between devices, per_device(): lax.psum_scatter(stacked[2], 'wide', scatter_dimension=1, tiled=True)  64.8 us
    unnamed x683, local copies, waits for them, and re-layouts  55.1 us
  transfers between devices with their start and end apart: 14, of which 8 were waited for; matrix products, arithmetic and copies ran while one was open for 13% of the time, Pallas kernels for 0%

commit v1 on v0

v1 whole, which is shorter than its diff:
```python
import functools

import jax
import jax.numpy as jnp
from jax import lax
from jax.experimental import pallas as pl
from jax.experimental.pallas import tpu as pltpu
from jax.sharding import PartitionSpec as P

D = 256
HEADS = 4
HEAD_DIM = 64
FF = 1024
VOCAB = 512
ACTIONS = 18
GAMES = 26
OBS = 16
FRAMES = 20
STEP_NUMBER = 5
FRAME_TOKENS = 17
LENGTH = 340
ROWS = 896
NVEC = 14

EPS_NORM = 1e-05
BETA_ONE = 0.5
BETA_TWO = 0.5
RATE_TABLE = 0.5
RATE_MATRIX = 0.05
RATE_VECTOR = 0.2
DECAY_RATE = 0.01
EPS_ADAM = 1e-08
CLIP_AT = 0.1

SEQ = 352
KEYS = 384
QBLOCKS = ((0, 128, 128), (128, 128, 256), (256, 96, 384))

COL_QKV, COL_PROJ, COL_UP, COL_DOWN, COL_LAYER = 0, 768, 1024, 2048, 3072
HALF_LAYER = (
    (0, 128, 0),
    (128, 128, 256),
    (256, 128, 512),
    (384, 128, COL_PROJ),
    (512, 512, COL_UP),
    (1024, 512, COL_DOWN),
)
HALF_LAYER_COLS = 1536
COL_TABLE, COL_SMALL, COL_FIRST = 3072, 3968, 4096
HALF_FIRST = HALF_LAYER + ((1536, 512, COL_TABLE),)
HALF_FIRST_COLS = 2048
COL_HEAD, COL_SECOND = 3072, 3584
HALF_SECOND = HALF_LAYER + ((1536, 256, COL_HEAD),)
HALF_SECOND_COLS = 1792
SMALL_BIAS, SMALL_SIDE, SMALL_SCALAR = 14, 22, 32

F32, BF16 = jnp.float32, jnp.bfloat16
VMEM_BYTES = 60 * 1024 * 1024


def dot_nn(a, b):
    return lax.dot_general(a, b, (((1,), (0,)), ((), ())), preferred_element_type=F32)


def dot_nt(a, b):
    return lax.dot_general(a, b, (((1,), (1,)), ((), ())), preferred_element_type=F32)


def dot_tn(a, b):
    return lax.dot_general(a, b, (((0,), (0,)), ((), ())), preferred_element_type=F32)


def normalise(x):
    centred = x - jnp.mean(x, axis=1, keepdims=True)
    scale = lax.rsqrt(jnp.mean(centred * centred, axis=1, keepdims=True) + EPS_NORM)
    return centred * scale, scale


def normalise_back(grad, xhat, scale, gain):
    inner = grad * gain
    mean_one = jnp.mean(inner, axis=1, keepdims=True)
    mean_two = jnp.mean(inner * xhat, axis=1, keepdims=True)
    return scale * (inner - mean_one - xhat * mean_two)


def column_sum(a):
    return jnp.sum(a, axis=0, keepdims=True)


def head_masks(a, scale=None):
    lane = lax.broadcasted_iota(jnp.int32, (1, D), 1)
    zero = jnp.zeros((), a.dtype)
    if scale is not None:
        a = a * jnp.asarray(scale, a.dtype)
    return [
        jnp.where((lane >= h * HEAD_DIM) & (lane < (h + 1) * HEAD_DIM), a, zero)
        for h in range(HEADS)
    ]


def assemble(pieces_mine, pieces_other, place_ref, w_ref, halves):
    me, core = place_ref[0], place_ref[1]
    is_first = core == 0
    for p in range(4):
        for z in range(4):
            row = pl.multiple_of((me ^ (4 * z + p)) * 16, 16)
            for src, width, dest in halves:
                mine = pieces_mine[p][z, :, src : src + width]
                other = pieces_other[p][z, :, src : src + width]
                w_ref[pl.ds(row, 16), dest : dest + width] = jnp.where(is_first, mine, other)
                w_ref[pl.ds(row, 16), dest + width : dest + 2 * width] = jnp.where(
                    is_first, other, mine
                )


def disperse(g_ref, place_ref, keep_ref, send_ref, halves):
    me, core = place_ref[0], place_ref[1]
    is_first = core == 0
    for p in range(4):
        for z in range(4):
            row = pl.multiple_of((me ^ (4 * z + p)) * 16, 16)
            for src, width, dest in halves:
                low = g_ref[pl.ds(row, 16), dest : dest + width]
                high = g_ref[pl.ds(row, 16), dest + width : dest + 2 * width]
                keep_ref[p, z, :, src : src + width] = jnp.where(is_first, low, high)
                send_ref[p, z, :, src : src + width] = jnp.where(is_first, high, low).astype(BF16)


def make_hits(meta):
    lane = lax.broadcasted_iota(jnp.int32, (SEQ, 640), 1)
    place = lax.broadcasted_iota(jnp.int32, (SEQ, ROWS), 0) + (VOCAB + ACTIONS + GAMES)
    place_hit = place == lax.broadcasted_iota(jnp.int32, (SEQ, ROWS), 1)
    hit = (lane == meta[:, 0:1]) | (lane == meta[:, 1:2]) | place_hit[:, :640]
    one, zero = jnp.ones((), F32), jnp.zeros((), F32)
    return jnp.concatenate(
        [jnp.where(hit, one, zero).astype(BF16), jnp.where(place_hit[:, 640:], one, zero).astype(BF16)],
        axis=1,
    )


def layer_forward(x, w_ref, vec, bias, kept):
    x_ref, qkv_ref, p_refs, o_ref, m_ref, h_ref, gp_ref = kept
    normed16 = (normalise(x)[0] * vec[0:1] + vec[1:2]).astype(BF16)
    qkv_ref[0:SEQ] = dot_nn(normed16, w_ref[:, COL_QKV : COL_QKV + 768]).astype(BF16)
    qkv_ref[SEQ:KEYS] = jnp.zeros((KEYS - SEQ, 768), BF16)
    values = head_masks(qkv_ref[:, 512:768])
    for (first, count, seen), p_ref in zip(QBLOCKS, p_refs):
        queries = jnp.concatenate(head_masks(qkv_ref[first : first + count, 0:256], 0.125), axis=0)
        scores = dot_nt(queries, qkv_ref[0:seen, 256:512]).reshape(HEADS, count, seen)
        row = lax.broadcasted_iota(jnp.int32, (count, seen), 0) + first
        causal = row >= lax.broadcasted_iota(jnp.int32, (count, seen), 1)
        scores = jnp.where(causal[None], scores, -1e30)
        expanded = jnp.exp(scores - jnp.max(scores, axis=2, keepdims=True))
        probs = expanded * (1.0 / jnp.sum(expanded, axis=2, keepdims=True))
        probs16 = probs.astype(BF16)
        p_ref[...] = probs16.reshape(HEADS * count, seen)
        out = dot_nn(
            jnp.concatenate([probs16[h] for h in range(HEADS)], axis=1),
            jnp.concatenate([values[h][0:seen] for h in range(HEADS)], axis=0),
        )
        o_ref[first : first + count] = out.astype(BF16)
    middle = x + (dot_nt(o_ref[...], w_ref[:, COL_PROJ : COL_PROJ + 256]) + vec[2:3])
    m_ref[...] = middle
    normed16 = (normalise(middle)[0] * vec[3:4] + vec[4:5]).astype(BF16)
    total = middle + vec[5:6]
    for chunk in range(4):
        cols = slice(256 * chunk, 256 * chunk + 256)
        up = dot_nn(normed16, w_ref[:, COL_UP + 256 * chunk : COL_UP + 256 * chunk + 256])
        up = up + bias[:, cols]
        square = up * up
        slope = 0.7978845608028654 + 0.1070322244089 * square
        bent = jnp.tanh(up * (0.7978845608028654 + 0.0356774081363 * square))
        half = 0.5 + 0.5 * bent
        hidden = up * half
        gp_ref[:, cols] = (half + hidden * (1.0 - bent) * slope).astype(BF16)
        hidden16 = hidden.astype(BF16)
        h_ref[:, cols] = hidden16
        total = total + dot_nt(
            hidden16, w_ref[:, COL_DOWN + 256 * chunk : COL_DOWN + 256 * chunk + 256]
        )
    return total


def layer_backward(grad_in, w_ref, vec, kept, g_ref, v_ref, v_row, bias_row, dkv_ref):
    x_ref, qkv_ref, p_refs, o_ref, m_ref, h_ref, gp_ref = kept
    grad_out16 = grad_in.astype(BF16)
    v_ref[v_row + 5 : v_row + 6] += column_sum(grad_out16.astype(F32))
    xhat, scale = normalise(m_ref[...])
    normed16 = (xhat * vec[3:4] + vec[4:5]).astype(BF16)
    grad_normed = None
    for chunk in range(4):
        cols = slice(256 * chunk, 256 * chunk + 256)
        cols_up = slice(COL_UP + 256 * chunk, COL_UP + 256 * chunk + 256)
        cols_down = slice(COL_DOWN + 256 * chunk, COL_DOWN + 256 * chunk + 256)
        grad_hidden = dot_nn(grad_out16, w_ref[:, cols_down])
        grad_up16 = (grad_hidden * gp_ref[:, cols].astype(F32)).astype(BF16)
        g_ref[:, cols_down] += dot_tn(grad_out16, h_ref[:, cols])
        g_ref[:, cols_up] += dot_tn(normed16, grad_up16)
        v_ref[bias_row + chunk : bias_row + chunk + 1] += column_sum(grad_up16.astype(F32))
        part = dot_nt(grad_up16, w_ref[:, cols_up])
        grad_normed = part if grad_normed is None else grad_normed + part
    v_ref[v_row + 3 : v_row + 4] += column_sum(grad_normed * xhat)
    v_ref[v_row + 4 : v_row + 5] += column_sum(grad_normed)
    grad_mid = grad_in + normalise_back(grad_normed, xhat, scale, vec[3:4])
    grad_att16 = grad_mid.astype(BF16)
    v_ref[v_row + 2 : v_row + 3] += column_sum(grad_att16.astype(F32))
    g_ref[:, COL_PROJ : COL_PROJ + 256] += dot_tn(grad_att16, o_ref[...])
    grad_heads = dot_nn(grad_att16, w_ref[:, COL_PROJ : COL_PROJ + 256]).astype(BF16)
    keys = head_masks(qkv_ref[:, 256:512], 0.125)
    dkv_ref[...] = jnp.zeros(dkv_ref.shape, F32)
    grad_query = []
    for (first, count, seen), p_ref in zip(QBLOCKS, p_refs):
        rows = slice(first, first + count)
        queries = jnp.concatenate(head_masks(qkv_ref[rows, 0:256], 0.125), axis=0)
        grads = jnp.concatenate(head_masks(grad_heads[rows]), axis=0)
        grad_probs = dot_nt(grads, qkv_ref[0:seen, 512:768])
        probs16 = p_ref[...]
        probs = probs16.astype(F32)
        inner = jnp.sum(probs * grad_probs, axis=1, keepdims=True)
        grad_scores = (probs * (grad_probs - inner)).astype(BF16)
        grad_query.append(
            dot_nn(
                jnp.concatenate(
                    [grad_scores[h * count : (h + 1) * count] for h in range(HEADS)], axis=1
                ),
                jnp.concatenate([keys[h][0:seen] for h in range(HEADS)], axis=0),
            ).astype(BF16)
        )
        dkv_ref[0:seen, 0:256] += dot_tn(grad_scores, queries)
        dkv_ref[0:seen, 256:512] += dot_tn(probs16, grads)
    grad_qkv = jnp.concatenate(
        [jnp.concatenate(grad_query, axis=0), dkv_ref[0:SEQ].astype(BF16)], axis=1
    )
    xhat, scale = normalise(x_ref[...])
    normed16 = (xhat * vec[0:1] + vec[1:2]).astype(BF16)
    g_ref[:, COL_QKV : COL_QKV + 768] += dot_tn(normed16, grad_qkv)
    grad_normed = dot_nt(grad_qkv, w_ref[:, COL_QKV : COL_QKV + 768])
    v_ref[v_row : v_row + 1] += column_sum(grad_normed * xhat)
    v_ref[v_row + 1 : v_row + 2] += column_sum(grad_normed)
    return grad_mid + normalise_back(grad_normed, xhat, scale, vec[0:1])


def first_forward_kernel(*refs):
    place_ref, meta_ref, vec_ref, bias_ref = refs[0:4]
    mine, other = refs[4:8], refs[8:12]
    w_out, next_ref = refs[12:14]
    x_ref, qkv_ref, p0, p1, p2, o_ref, m_ref, h_ref, gp_ref = refs[14:23]
    w_ref = refs[23]

    @pl.when(pl.program_id(0) == 0)
    def _():
        assemble(mine, other, place_ref, w_ref, HALF_FIRST)
        w_out[...] = w_ref[...]

    x = dot_nt(make_hits(meta_ref[0]), w_ref[:, COL_TABLE : COL_TABLE + ROWS])
    x_ref[0] = x
    kept = (
        x_ref.at[0],
        qkv_ref.at[0],
        (p0.at[0], p1.at[0], p2.at[0]),
        o_ref.at[0],
        m_ref.at[0],
        h_ref.at[0],
        gp_ref.at[0],
    )
    next_ref[0] = layer_forward(x, w_ref, vec_ref[0:6], bias_ref[0:1], kept)


def middle_kernel(*refs):
    place_ref, meta_ref, vec_ref, bias_ref, side_ref, in_ref = refs[0:6]
    mine, other = refs[6:10], refs[10:14]
    grad_ref, keep_ref, send_ref, v_out, side_out, scalar_ref = refs[14:20]
    w_ref, g_ref, v_ref, dkv_ref = refs[20:24]
    qkv_ref, p0, p1, p2, o_ref, m_ref, h_ref, gp_ref = refs[24:32]
    step = pl.program_id(0)

    @pl.when(step == 0)
    def _():
        assemble(mine, other, place_ref, w_ref, HALF_SECOND)
        w_ref[:, COL_SECOND:] = side_ref[...]
        g_ref[...] = jnp.zeros(g_ref.shape, F32)
        v_ref[...] = jnp.zeros(v_ref.shape, F32)
        scalar_ref[...] = jnp.zeros(scalar_ref.shape, F32)

    x_ref = in_ref.at[0]
    kept = (x_ref, qkv_ref, (p0, p1, p2), o_ref, m_ref, h_ref, gp_ref)
    last = layer_forward(x_ref[...], w_ref, vec_ref[6:12], bias_ref[1:2], kept)

    meta = meta_ref[0]
    xhat, scale = normalise(last)
    gain = vec_ref[12:13]
    final16 = (xhat * gain + vec_ref[13:14]).astype(BF16)
    both = dot_nn(final16, w_ref[:, COL_HEAD : COL_HEAD + VOCAB + 128])
    logits, side = both[:, :VOCAB], both[:, VOCAB:]
    weight = meta[:, 3:4].astype(F32)
    peak = jnp.max(logits, axis=1, keepdims=True)
    expanded = jnp.exp(logits - peak)
    total = jnp.sum(expanded, axis=1, keepdims=True)
    hit = lax.broadcasted_iota(jnp.int32, (SEQ, VOCAB), 1) == meta[:, 2:3]
    picked = jnp.sum(jnp.where(hit, logits, 0.0), axis=1, keepdims=True)
    loss = column_sum(weight * (peak + jnp.log(total) - picked))
    grad_logits = expanded * (weight / total) - jnp.where(hit, weight, 0.0)

    lane = lax.broadcasted_iota(jnp.int32, (SEQ, 128), 1)
    is_reward, is_end = lane < 3, (lane == 3) | (lane == 4)
    side_weight = meta[:, 4:5].astype(F32)
    reward_peak = jnp.max(jnp.where(is_reward, side, -1e30), axis=1, keepdims=True)
    end_peak = jnp.max(jnp.where(is_end, side, -1e30), axis=1, keepdims=True)
    side_peak = jnp.where(is_reward, reward_peak, end_peak)
    expanded = jnp.where(is_reward | is_end, jnp.exp(jnp.where(is_reward | is_end, side - side_peak, 0.0)), 0.0)
    reward_total = jnp.sum(jnp.where(is_reward, expanded, 0.0), axis=1, keepdims=True)
    end_total = jnp.sum(jnp.where(is_end, expanded, 0.0), axis=1, keepdims=True)
    side_hit = (lane == meta[:, 5:6]) | (lane == meta[:, 6:7])
    side_picked = jnp.sum(jnp.where(side_hit, side, 0.0), axis=1, keepdims=True)
    side_terms = reward_peak + jnp.log(reward_total) + end_peak + jnp.log(end_total) - side_picked
    loss = loss + column_sum(side_weight * side_terms)
    grad_side = expanded * jnp.where(is_reward, side_weight / reward_total, side_weight / end_total)
    grad_side = grad_side - jnp.where(side_hit, side_weight, 0.0)
    valid = column_sum(side_weight)
    scalar_lane = lax.broadcasted_iota(jnp.int32, (8, 128), 1)
    scalar_row = lax.broadcasted_iota(jnp.int32, (8, 128), 0) == 0
    scalar_ref[...] += jnp.where(scalar_row & (scalar_lane == SMALL_SCALAR), loss, 0.0)
    scalar_ref[...] += jnp.where(scalar_row & (scalar_lane == SMALL_SCALAR + 1), valid, 0.0)

    grad_both = jnp.concatenate([grad_logits.astype(BF16), grad_side.astype(BF16)], axis=1)
    g_ref[:, COL_HEAD : COL_HEAD + VOCAB + 128] += dot_tn(final16, grad_both)
    grad_final = dot_nt(grad_both, w_ref[:, COL_HEAD : COL_HEAD + VOCAB + 128])
    v_ref[12:13] += column_sum(grad_final * xhat)
    v_ref[13:14] += column_sum(grad_final)
    grad_last = normalise_back(grad_final, xhat, scale, gain)
    grad_ref[0] = layer_backward(
        grad_last, w_ref, vec_ref[6:12], kept, g_ref, v_ref, 6, SMALL_BIAS + 4, dkv_ref
    )

    @pl.when(step == pl.num_programs(0) - 1)
    def _():
        disperse(g_ref, place_ref, keep_ref, send_ref, HALF_SECOND)
        v_out[...] = v_ref[...]
        side_out[...] = g_ref[:, COL_SECOND:]


def first_backward_kernel(*refs):
    place_ref, meta_ref, vec_ref, w_ref, grad_ref, v_in, side_in = refs[0:7]
    x_ref, qkv_ref, p0, p1, p2, o_ref, m_ref, h_ref, gp_ref = refs[7:16]
    keep_ref, send_ref = refs[16:18]
    g_ref, v_ref, dkv_ref = refs[18:21]
    step = pl.program_id(0)

    @pl.when(step == 0)
    def _():
        g_ref[...] = jnp.zeros(g_ref.shape, F32)
        v_ref[...] = v_in[...]

    kept = (
        x_ref.at[0],
        qkv_ref.at[0],
        (p0.at[0], p1.at[0], p2.at[0]),
        o_ref.at[0],
        m_ref.at[0],
        h_ref.at[0],
        gp_ref.at[0],
    )
    grad_x = layer_backward(
        grad_ref[0], w_ref, vec_ref[0:6], kept, g_ref, v_ref, 0, SMALL_BIAS, dkv_ref
    )
    g_ref[:, COL_TABLE : COL_TABLE + ROWS] += dot_tn(grad_x.astype(BF16), make_hits(meta_ref[0]))

    @pl.when(step == pl.num_programs(0) - 1)
    def _():
        lane = lax.broadcasted_iota(jnp.int32, (D, 128), 1)
        small = jnp.transpose(v_ref[...])
        side = pltpu.roll(side_in[...], SMALL_SIDE, 1)
        g_ref[:, COL_SMALL:] = jnp.where(
            lane < SMALL_SIDE, small, jnp.where(lane < SMALL_SIDE + 5, side, 0.0)
        )
        disperse(g_ref, place_ref, keep_ref, send_ref, HALF_FIRST)


def pack_kernel(place_ref, table, attn, proj, up, down, head, side, first, second, pad_ref):
    is_first = place_ref[1] == 0
    rows = side.shape[0]
    eye = (
        lax.broadcasted_iota(jnp.int32, (rows, rows), 0)
        == lax.broadcasted_iota(jnp.int32, (rows, rows), 1)
    )
    eye = jnp.where(eye, 1.0, 0.0).astype(BF16)

    def turned(a):
        return dot_nt(eye, a.astype(BF16)).astype(BF16)

    for layer, out in enumerate((first, second)):
        for j in range(3):
            out[:, 128 * j : 128 * j + 128] = attn[layer, j].astype(BF16)
        out[:, 384:512] = turned(proj[layer])
        out[:, 512:1024] = up[layer].astype(BF16)
        out[:, 1024:1536] = turned(down[layer])
    second[:, 1536:1792] = head[...].astype(BF16)
    pad_ref[...] = jnp.zeros(pad_ref.shape, F32)
    pad_ref[:, 0:5] = side[...]
    low = turned(table[0:512])
    high = jnp.concatenate([turned(table[512:896]), pad_ref[...].astype(BF16)], axis=1)
    first[:, 1536:2048] = jnp.where(is_first, low, high)


def finish_kernel(*refs):
    count = (len(refs) - 4) // 2
    scalar_ref = refs[2 * count]
    out_first, out_second, message = refs[2 * count + 1 :]
    square = jnp.zeros((1, 1), F32)
    for pieces, out in ((refs[:count], out_first), (refs[count : 2 * count], out_second)):
        total = pieces[0][...]
        for piece in pieces[1:]:
            total = total + piece[...].astype(F32)
        out[...] = total
        square = square + jnp.sum(
            jnp.sum(total * total, axis=1, keepdims=True), axis=0, keepdims=True
        )
    message[:, 0:512] = out_first[:, 1536:2048]
    rows = message.shape[0]
    lane = lax.broadcasted_iota(jnp.int32, (rows, 128), 1)
    top = lax.broadcasted_iota(jnp.int32, (rows, 128), 0) == 0
    scalars = scalar_ref[0:1] + jnp.where(lane == SMALL_SCALAR + 2, square, 0.0)
    message[:, 512:640] = jnp.where(top, scalars, 0.0)


def adam_rule(weight, moment, second, gradient, step_rate, decay_rate):
    moment_new = BETA_ONE * moment + (1.0 - BETA_ONE) * gradient
    second_new = BETA_TWO * second + (1.0 - BETA_TWO) * gradient * gradient
    moment_hat = moment_new / (1.0 - BETA_ONE**STEP_NUMBER)
    second_hat = second_new / (1.0 - BETA_TWO**STEP_NUMBER)
    weight_new = weight - step_rate * (
        moment_hat / (jnp.sqrt(second_hat) + EPS_ADAM) + decay_rate * weight
    )
    return (weight_new, moment_new, second_new)


def adam_kernel(*refs):
    place_ref, first, second, swapped = refs[0:4]
    smalls = refs[4:8]
    params = [refs[8 + 3 * i : 11 + 3 * i] for i in range(9)]
    loss_ref, valid_ref, norm_ref = refs[35:38]
    outs = [refs[38 + 3 * i : 41 + 3 * i] for i in range(9)]
    small_ref, turn_ref = refs[65:67]
    me = place_ref[0]
    is_first = place_ref[1] == 0
    rows = first.shape[0]
    for z in range(4):
        for p in range(4):
            row = pl.multiple_of((me ^ (4 * z + p)) * 16, 16)
            small_ref[pl.ds(row, 16)] = smalls[z][p]
    small = jnp.transpose(small_ref[...])
    scalars = jnp.sum(small[SMALL_SCALAR : SMALL_SCALAR + 8], axis=1, keepdims=True)
    loss, valid, square = scalars[0:1], scalars[1:2], scalars[2:3]
    inverse = 1.0 / valid
    norm = jnp.sqrt(square) * inverse
    loss_ref[...], valid_ref[...], norm_ref[...] = loss, valid, norm
    factor = jnp.minimum(1.0, CLIP_AT / (norm + 1e-06)) * inverse
    table, attn, proj, up, bias, down, vectors, head, side = range(9)

    def update(which, index, gradient, step_rate, decay_rate):
        news = adam_rule(
            *(ref[index] for ref in params[which]), factor * gradient, step_rate, decay_rate
        )
        for ref, new in zip(outs[which], news):
            ref[index] = new

    def turned(a, width):
        turn_ref[0:rows, 0:width] = a
        return jnp.transpose(turn_ref[:, 0:width])[:, 0:rows]

    turn_ref[...] = jnp.zeros(turn_ref.shape, F32)
    for layer, grad in enumerate((first, second)):
        for j in range(3):
            update(attn, (layer, j), grad[:, 128 * j : 128 * j + 128], RATE_MATRIX, DECAY_RATE)
        update(proj, (layer,), turned(grad[:, 384:512], 128), RATE_MATRIX, DECAY_RATE)
        update(up, (layer,), grad[:, 512:1024], RATE_MATRIX, DECAY_RATE)
        update(down, (layer,), turned(grad[:, 1024:1536], 512), RATE_MATRIX, DECAY_RATE)
        for i in range(2):
            low = SMALL_BIAS + 4 * layer + i
            row = jnp.where(is_first, small[low : low + 1], small[low + 2 : low + 3])
            index = (slice(layer, layer + 1), slice(256 * i, 256 * i + 256))
            update(bias, index, row, RATE_VECTOR, 0.0)
    whole = (slice(None), slice(None))
    update(head, whole, second[:, 1536:1792], RATE_MATRIX, DECAY_RATE)
    mine, theirs = first[:, 1536:2048], swapped[:, 0:512]
    low, high = jnp.where(is_first, mine, theirs), jnp.where(is_first, theirs, mine)
    update(table, (slice(0, 512),), turned(low, 512), RATE_TABLE, DECAY_RATE)
    update(table, (slice(512, 896),), turned(high[:, 0:384], 384), RATE_TABLE, DECAY_RATE)
    update(vectors, whole, small[0:NVEC], RATE_VECTOR, 0.0)
    side_grad = high[:, 384 + SMALL_SIDE : 384 + SMALL_SIDE + 5]
    update(side, whole, side_grad, RATE_MATRIX, DECAY_RATE)


def swap(a, axis, distance):
    size = lax.axis_size(axis)
    return lax.ppermute(a, axis, [(i, i ^ distance) for i in range(size)])


def gather(piece, n_high):
    column = jnp.stack([piece] + [swap(piece, "wide", 4 * k) for k in range(1, n_high)])
    mine = [column] + [swap(column, "wide", p) for p in range(1, 4)]
    other = [swap(a, "narrow", 1) for a in mine]
    return mine, other


def in_blocks(parts, wide):
    n_high, rows, cols = parts[0].shape
    if rows == 16:
        return parts
    whole = jnp.stack(parts, axis=1).reshape(4 * n_high, rows, cols)
    whole = whole[wide ^ jnp.arange(4 * n_high)].reshape(4, 4, 16, cols)
    return [whole[:, p] for p in range(4)]


def in_pieces(blocks, wide, n_high):
    cols = blocks.shape[-1]
    if n_high == 4:
        return blocks
    rows = 64 // n_high
    whole = blocks.transpose(1, 0, 2, 3).reshape(4 * n_high, rows, cols)
    whole = whole[wide ^ jnp.arange(4 * n_high)]
    return whole.reshape(n_high, 4, rows, cols).transpose(1, 0, 2, 3)


def scatter(keep, send, n_high):
    received = swap(send, "narrow", 1)
    sums = [keep[p] + received[p].astype(F32) for p in range(4)]
    own = sums[0]
    for p in range(1, 4):
        own = own + swap(sums[p].astype(BF16), "wide", p).astype(F32)
    return [own[0]] + [swap(own[k].astype(BF16), "wide", 4 * k) for k in range(1, n_high)]


def full_spec(a):
    return pl.BlockSpec(a.shape, lambda *_: (0,) * len(a.shape))


def row_spec(shape):
    return pl.BlockSpec((1,) + shape, lambda i: (i,) + (0,) * len(shape))


def shaped(shape, dtype):
    return jax.ShapeDtypeStruct(shape, dtype)


VMEM_SPEC = pl.BlockSpec(memory_space=pltpu.VMEM)
SMEM_SPEC = pl.BlockSpec(memory_space=pltpu.SMEM)


def call(kernel, grid, in_specs, out_specs, out_shape, scratch, flops, bytes_accessed, name):
    extra = {"grid": grid} if grid else {}
    return pl.pallas_call(
        kernel,
        in_specs=in_specs,
        out_specs=out_specs,
        out_shape=out_shape,
        scratch_shapes=scratch,
        compiler_params=pltpu.CompilerParams(vmem_limit_bytes=VMEM_BYTES),
        cost_estimate=pl.CostEstimate(
            flops=flops, bytes_accessed=bytes_accessed, transcendentals=0
        ),
        name=name,
        **extra,
    )


KEPT = (
    ((SEQ, D), F32),
    ((KEYS, 768), BF16),
    ((HEADS * 128, 128), BF16),
    ((HEADS * 128, 256), BF16),
    ((HEADS * 96, 384), BF16),
    ((SEQ, D), BF16),
    ((SEQ, D), F32),
    ((SEQ, FF), BF16),
    ((SEQ, FF), BF16),
)


def make_meta(tokens, actions, game_ids, valid_steps, rewards, end_flags):
    count = tokens.shape[0]
    frames = tokens.shape[1]

    def last(a, fill):
        return jnp.concatenate(
            [jnp.full((count, frames, OBS), fill, jnp.int32), a[:, :, None]], axis=2
        )

    zero = jnp.zeros((count, 1), jnp.int32)
    ids = jnp.concatenate([tokens, actions[:, :, None] + VOCAB], axis=2)
    following = jnp.concatenate([tokens[:, 1:, 0], zero], axis=1)
    targets = jnp.concatenate(
        [tokens[:, :, 1:], jnp.zeros((count, frames, 1), jnp.int32), following[:, :, None]], axis=2
    )
    next_valid = jnp.concatenate([valid_steps[:, 1:], zero], axis=1)
    weights = jnp.concatenate(
        [
            jnp.broadcast_to(valid_steps[:, :, None], (count, frames, OBS - 1)),
            jnp.zeros((count, frames, 1), jnp.int32),
            next_valid[:, :, None],
        ],
        axis=2,
    )
    games = jnp.broadcast_to(
        (VOCAB + ACTIONS + game_ids)[:, None, None], (count, frames, FRAME_TOKENS)
    )
    columns = [ids, games, targets, weights, last(valid_steps, 0), last(rewards, 0), last(end_flags + 3, 3)]
    stacked = jnp.stack(columns + [jnp.zeros_like(ids)], axis=-1).reshape(count, LENGTH, 8)
    stacked = jnp.pad(stacked, ((0, 0), (0, SEQ - LENGTH), (0, 0)))
    padding = (jnp.arange(SEQ) >= LENGTH)[None, :, None] & (jnp.arange(8) < 2)
    return jnp.where(padding, -1, stacked)


def per_device(
    tokens,
    actions,
    game_ids,
    valid_steps,
    rewards,
    end_flags,
    embed_table,
    table_first,
    table_second,
    attn_weight,
    attn_first,
    attn_second,
    proj_weight,
    proj_first,
    proj_second,
    up_weight,
    up_first,
    up_second,
    up_bias,
    bias_first,
    bias_second,
    down_weight,
    down_first,
    down_second,
    vectors,
    vectors_first,
    vectors_second,
    head_weight,
    head_first,
    head_second,
    side_weight,
    side_first,
    side_second,
):
    n_high = lax.axis_size("wide") // 4
    wide, core = lax.axis_index("wide"), lax.axis_index("narrow")
    rows = side_weight.shape[0]
    place = jnp.stack([jnp.where(rows == 16, wide, 0), core]).astype(jnp.int32)

    matrices = (
        embed_table,
        attn_weight,
        proj_weight,
        up_weight,
        down_weight,
        head_weight,
        side_weight,
    )
    piece_first, piece_second = call(
        pack_kernel,
        None,
        [SMEM_SPEC] + [VMEM_SPEC] * 7,
        [VMEM_SPEC] * 2,
        [shaped((rows, HALF_FIRST_COLS), BF16), shaped((rows, HALF_SECOND_COLS), BF16)],
        [pltpu.VMEM((rows, 128), F32)],
        10**6,
        10**6,
        "pack",
    )(place, *matrices)
    first_parts = gather(piece_first, n_high)
    second_parts = gather(piece_second, n_high)
    first_parts = [in_blocks(parts, wide) for parts in first_parts]
    second_parts = [in_blocks(parts, wide) for parts in second_parts]

    count = tokens.shape[0] // lax.axis_size("narrow")
    own = [
        lax.dynamic_slice_in_dim(a, core * count, count, 0)
        for a in (tokens, actions, game_ids, valid_steps, rewards, end_flags)
    ]
    meta = make_meta(*own)
    other_bias = swap(up_bias, "narrow", 1)
    all_bias = jnp.where(
        core == 0,
        jnp.concatenate([up_bias, other_bias], axis=1),
        jnp.concatenate([other_bias, up_bias], axis=1),
    )

    kept_specs = [row_spec(shape) for shape, _ in KEPT]
    kept_shapes = [shaped((count,) + shape, dtype) for shape, dtype in KEPT]
    row_f32 = shaped((count, SEQ, D), F32)
    blocks_first = [full_spec(a) for a in first_parts[0] + first_parts[1]]
    blocks_second = [full_spec(a) for a in second_parts[0] + second_parts[1]]
    w_spec = pl.BlockSpec((D, COL_FIRST), lambda i: (0, 0))
    results = call(
        first_forward_kernel,
        (count,),
        [SMEM_SPEC, row_spec((SEQ, 8)), full_spec(vectors), full_spec(all_bias)] + blocks_first,
        [w_spec, row_spec((SEQ, D))] + kept_specs,
        [shaped((D, COL_FIRST), BF16), row_f32] + kept_shapes,
        [pltpu.VMEM((D, COL_FIRST), BF16)],
        4 * 10**9,
        20 * 10**6,
        "first_forward",
    )(place, meta, vectors, all_bias, *first_parts[0], *first_parts[1])
    w_first, stream = results[0:2]
    kept = results[2:]
    side_copy = w_first[:, COL_SMALL:]

    blocks = lambda cols: pl.BlockSpec((4, 4, 16, cols), lambda i: (0, 0, 0, 0))
    small_spec = pl.BlockSpec((128, D), lambda i: (0, 0))
    side_spec = pl.BlockSpec((D, 128), lambda i: (0, 0))
    scalar_spec = pl.BlockSpec((8, 128), lambda i: (0, 0))
    grad_stream, keep_second, send_second, small_grads, side_grad, scalars = call(
        middle_kernel,
        (count,),
        [
            SMEM_SPEC,
            row_spec((SEQ, 8)),
            full_spec(vectors),
            full_spec(all_bias),
            side_spec,
            row_spec((SEQ, D)),
        ]
        + blocks_second,
        [
            row_spec((SEQ, D)),
            blocks(HALF_SECOND_COLS),
            blocks(HALF_SECOND_COLS),
            small_spec,
            side_spec,
            scalar_spec,
        ],
        [
            row_f32,
            shaped((4, 4, 16, HALF_SECOND_COLS), F32),
            shaped((4, 4, 16, HALF_SECOND_COLS), BF16),
            shaped((128, D), F32),
            shaped((D, 128), F32),
            shaped((8, 128), F32),
        ],
        [
            pltpu.VMEM((D, COL_SECOND + 128), BF16),
            pltpu.VMEM((D, COL_SECOND + 128), F32),
            pltpu.VMEM((128, D), F32),
            pltpu.VMEM((KEYS, 512), F32),
        ]
        + [pltpu.VMEM(shape, dtype) for shape, dtype in KEPT[1:]],
        15 * 10**9,
        20 * 10**6,
        "middle",
    )(place, meta, vectors, all_bias, side_copy, stream, *second_parts[0], *second_parts[1])
    second_pieces = scatter(
        in_pieces(keep_second, wide, n_high), in_pieces(send_second, wide, n_high), n_high
    )

    keep_first, send_first = call(
        first_backward_kernel,
        (count,),
        [SMEM_SPEC, row_spec((SEQ, 8)), full_spec(vectors), w_spec, row_spec((SEQ, D)), small_spec, side_spec]
        + kept_specs,
        [blocks(HALF_FIRST_COLS), blocks(HALF_FIRST_COLS)],
        [
            shaped((4, 4, 16, HALF_FIRST_COLS), F32),
            shaped((4, 4, 16, HALF_FIRST_COLS), BF16),
        ],
        [
            pltpu.VMEM((D, COL_FIRST), F32),
            pltpu.VMEM((128, D), F32),
            pltpu.VMEM((KEYS, 512), F32),
        ],
        8 * 10**9,
        20 * 10**6,
        "first_backward",
    )(place, meta, vectors, w_first, grad_stream, small_grads, side_grad, *kept)
    first_pieces = scatter(
        in_pieces(keep_first, wide, n_high), in_pieces(send_first, wide, n_high), n_high
    )

    grad_first, grad_second, message = call(
        finish_kernel,
        None,
        [VMEM_SPEC] * (2 * n_high + 1),
        [VMEM_SPEC] * 3,
        [
            shaped((rows, HALF_FIRST_COLS), F32),
            shaped((rows, HALF_SECOND_COLS), F32),
            shaped((rows, 640), F32),
        ],
        [],
        10**6,
        10**6,
        "finish",
    )(*first_pieces, *second_pieces, scalars)
    swapped = swap(message, "narrow", 1)
    small = jnp.where(core == 1, message[:, 384:512], swapped[:, 384:512])
    small = small + message[:, 512:640] + swapped[:, 512:640]
    plane = jnp.stack([small] + [swap(small, "wide", p) for p in range(1, 4)])
    columns = [plane] + [swap(plane, "wide", 4 * k) for k in range(1, n_high)]
    if rows != 16:
        parts = in_blocks([jnp.stack([column[p] for column in columns]) for p in range(4)], wide)
        columns = [jnp.stack([parts[p][z] for p in range(4)]) for z in range(4)]

    params = (
        embed_table,
        table_first,
        table_second,
        attn_weight,
        attn_first,
        attn_second,
        proj_weight,
        proj_first,
        proj_second,
        up_weight,
        up_first,
        up_second,
        up_bias,
        bias_first,
        bias_second,
        down_weight,
        down_first,
        down_second,
        vectors,
        vectors_first,
        vectors_second,
        head_weight,
        head_first,
        head_second,
        side_weight,
        side_first,
        side_second,
    )
    results = call(
        adam_kernel,
        None,
        [SMEM_SPEC] + [VMEM_SPEC] * 34,
        [VMEM_SPEC] * 30,
        [shaped((1, 1), F32)] * 3 + [shaped(a.shape, F32) for a in params],
        [pltpu.VMEM((D, 128), F32), pltpu.VMEM((128, 512), F32)],
        10**6,
        10**6,
        "adam",
    )(place, grad_first, grad_second, swapped, *columns, *params)
    return tuple(a.reshape(()) for a in results[0:3]) + tuple(results[3:])


def solution(mesh):
    placed = (
        P("wide", None, None),
        P("wide", None),
        P("wide"),
        P("wide", None),
        P("wide", None),
        P("wide", None),
        P(None, "wide"),
        P(None, "wide"),
        P(None, "wide"),
        P(None, None, "wide", "narrow"),
        P(None, None, "wide", "narrow"),
        P(None, None, "wide", "narrow"),
        P(None, "narrow", "wide"),
        P(None, "narrow", "wide"),
        P(None, "narrow", "wide"),
        P(None, "wide", "narrow"),
        P(None, "wide", "narrow"),
        P(None, "wide", "narrow"),
        P(None, "narrow"),
        P(None, "narrow"),
        P(None, "narrow"),
        P(None, "narrow", "wide"),
        P(None, "narrow", "wide"),
        P(None, "narrow", "wide"),
        P(),
        P(),
        P(),
        P("wide", "narrow"),
        P("wide", "narrow"),
        P("wide", "narrow"),
        P("wide", None),
        P("wide", None),
        P("wide", None),
    )
    return jax.shard_map(
        per_device,
        mesh=mesh,
        in_specs=placed,
        out_specs=(P(), P(), P()) + placed[6:],
        check_vma=False,
    )
```

time: 1480 us -> 216 us (0.15); the launches traced: 1460 us -> 215 us
  blocking collectives: 579 us -> 0 us
  waiting for transfers between devices: 279 us -> 24.4 us
  local copies, waits for them, and re-layouts: 270 us -> 43 us
  matrix products: 169 us -> 0 us
  other arithmetic: 132 us -> 5.57 us
  Pallas kernels: 0 us -> 93.1 us
  starting transfers between devices: 1.41 us -> 48 us
  between operations: 30.7 us -> 1.32 us
    all_gather x11 -> x0, blocking collectives: 426 us -> none  [the longest x2 81 us: layer_copy(): lax.all_gather(proj_weight[index].astype(jnp.bfloat16), 'wide', axis=1, t...]
    reduce_scatter x3 -> x0, waiting for transfers between devices: 184 us -> none  [the longest x1 71.4 us: per_device(): lax.psum_scatter(table_acc, 'wide', scatter_dimension=1, tiled=True)]
    dot_general x92 -> x0, matrix products: 169 us -> none  [the longest x4 15.7 us: layer_backward(): jnp.einsum('bhqk,bqhe->bkhe', probs16, grad_heads, preferred_element_type...]
    psum x3 -> x0, blocking collectives: 147 us -> none  [the longest x1 73 us: per_device(): vector_grad, bias_grad = lax.psum((vector_acc, bias_acc), 'wide')]
    pallas_call x0 -> x6, Pallas kernels: none -> 93.1 us  [the longest x1 39.3 us: per_device(): call(middle_kernel, (count,), [SMEM_SPEC, row_spec((SEQ, 8)), full_spec(v...]
    reduce_sum x53 -> x0, other arithmetic: 85.7 us -> none  [the longest x10 29.4 us: layer_norm(): return centred * lax.rsqrt(variance + EPS_NORM) * gain + offset]
    squeeze x32 -> x2, local copies, waits for them, and re-layouts: 69.3 us -> 1.32 us  [scatter(): own[0]]
    unnamed x16 -> x0, waiting for transfers between devices: 50.9 us -> none
  transfers between devices with their start and end apart: 14 -> 42, of which waited for: 8 -> 11; matrix products, arithmetic and copies ran while one was open for 13% -> 12% of each run, Pallas kernels for 0% -> 21%
where the time goes in v1:
time: 216 us; the launch traced here: 215 us
  Pallas kernels  93.1 us (43%)
  starting transfers between devices  48 us (22%)
  local copies, waits for them, and re-layouts  43 us (20%)
  waiting for transfers between devices  24.4 us (11%)
  other arithmetic  5.57 us (3%)
    ppermute x42, starting transfers between devices, swap(): return lax.ppermute(a, axis, [(i, i ^ distance) for i in range(size)])  48 us
    pallas_call x1, Pallas kernels, per_device(): call(middle_kernel, (count,), [SMEM_SPEC, row_spec((SEQ, 8)), full_spec(v...  39.3 us
    unnamed x123, local copies, waits for them, and re-layouts  29 us
    pallas_call x1, Pallas kernels, per_device(): call(first_backward_kernel, (count,), [SMEM_SPEC, row_spec((SEQ, 8)), ful...  25.6 us
    ppermute x42, waiting for transfers between devices, swap(): return lax.ppermute(a, axis, [(i, i ^ distance) for i in range(size)])  24.4 us
    pallas_call x1, Pallas kernels, per_device(): call(first_forward_kernel, (count,), [SMEM_SPEC, row_spec((SEQ, 8)), full...  18.7 us
    another operation x9, local copies, waits for them, and re-layouts, make_meta(): jnp.stack(columns + [jnp.zeros_like(ids)], axis=-1)  10.2 us
    pallas_call x1, Pallas kernels, per_device(): call(adam_kernel, None, [SMEM_SPEC] + [VMEM_SPEC] * 34, [VMEM_SPEC] * 30,...  5.4 us
  transfers between devices with their start and end apart: 42, of which 11 were waited for; matrix products, arithmetic and copies ran while one was open for 12% of the time, Pallas kernels for 21%

profile of v1, /device:TPU:0, one launch (start us, length us, event | category | flops | bytes accessed | tf_op | source)
XLA Modules:
  0.0 215.5 jit_solution(16690896533600921168)
XLA Ops:
  0.7 1.9 copy.204.down.refs_23_
  2.7 1.8 copy.202.table.refs_8_
  4.5 1.5 copy.203.proj.refs_14_
  5.9 1.4 copy.205.side.refs_32_
  7.9 2.2 %pack.1 = (bf16[16,2048]{1,0:T(8,128)(2,1)}, bf16[16,1792]{1,0:T(8,128)(2,1)}) custom-call(s32[2]{0:T(128)} %pad_add_fusion.3.place_ref.refs_0_, f32[896,16]{1,0:T(8,128)} %copy.202.table.refs_8_, f32[2,3,16,128]{3,2,1,0:T(8,128)} %refs_11_.1, f32[2,128,16]{2,1,0:T(8,128)} %copy.203.proj.refs_14_, f32[2,16,512]{2,1,0:T(8,128)} %refs_17_.1, ...), custom_call_target="tpu_custom_call" | custom-call | flops 1000000 | bytes 1000000 | tf_op jit(solution)/shard_map/pack/pallas_call | solution.py:663
  10.1 3.0 %collective-permute-start.1 = (bf16[16,2048]{1,0:T(8,128)(2,1)}, bf16[16,2048]{1,0:T(8,128)(2,1)S(1)}, u32[]{:S(2)}, u32[]{:S(2)}) collective-permute-start(bf16[16,2048]{1,0:T(8,128)(2,1)} %get-tuple-element.84), channel_id=1, source_target_pairs={{0,8},{2,10},{4,12},{6,14},{8,0},{10,2},{12,4},{14,6},{16,24},{18,... | collective-permute-start | bytes 196616 | tf_op jit(solution)/shard_map/ppermute | solution.py:496
  13.2 2.6 %collective-permute-start.2 = (bf16[16,2048]{1,0:T(8,128)(2,1)}, bf16[16,2048]{1,0:T(8,128)(2,1)S(1)}, u32[]{:S(2)}, u32[]{:S(2)}) collective-permute-start(bf16[16,2048]{1,0:T(8,128)(2,1)} %get-tuple-element.84), channel_id=1, source_target_pairs={{0,16},{2,18},{4,20},{6,22},{8,24},{10,26},{12,28},{14,30},{16,0},... | collective-permute-start | bytes 196616 | tf_op jit(solution)/shard_map/ppermute | solution.py:496
  16.2 3.9 %collective-permute-start.13 = (bf16[16,1792]{1,0:T(8,128)(2,1)}, bf16[16,1792]{1,0:T(8,128)(2,1)S(1)}, u32[]{:S(2)}, u32[]{:S(2)}) collective-permute-start(bf16[16,1792]{1,0:T(8,128)(2,1)} %get-tuple-element.87), channel_id=1, source_target_pairs={{0,24},{2,26},{4,28},{6,30},{8,16},{10,18},{12,20},{14,22},{16,8},... | collective-permute-start | bytes 172040 | tf_op jit(solution)/shard_map/ppermute | solution.py:496
  21.9 2.2 %collective-permute-done.12 = bf16[16,1792]{1,0:T(8,128)(2,1)S(1)} collective-permute-done((bf16[16,1792]{1,0:T(8,128)(2,1)}, bf16[16,1792]{1,0:T(8,128)(2,1)S(1)}, u32[]{:S(2)}, u32[]{:S(2)}) %collective-permute-start.12) | collective-permute-done | bytes 57376 | tf_op jit(solution)/shard_map/ppermute | solution.py:496
  24.9 1.6 collective-permute-start.14
  26.5 1.5 collective-permute-start.15
  28.9 1.7 collective-permute-start.6
  31.2 1.3 collective-permute-start.5
  34.0 1.2 stack.103
  35.4 1.2 stack.104
  36.8 1.2 stack.105
  39.9 3.7 %stack.84 = s32[4,340,8]{2,1,0:T(8,128)S(1)} concatenate(s32[4,340,1]{2,1,0:T(8,128)S(1)} %stack.100, s32[4,340,1]{2,1,0:T(8,128)} %stack_broadcast_in_dim.8, s32[4,340,1]{2,1,0:T(8,128)S(1)} %stack.101, s32[4,340,1]{2,1,0:T(8,128)S(1)} %stack.102, s32[4,340,1]{2,1,0:T(8,128)} %stack.103, s32[4,340,1]{2,1,0:T(8,128)} %stack.104, s32[4,340,1]{2,1,0:T(8,128)} %stack.105, ...), dimensions={2} | concatenate | bytes 87040 | tf_op jit(solution)/shard_map/stack | solution.py:608
  43.7 1.7 collective-permute-start.16
  48.1 3.3 %collective-permute-done.16.refs_9_ = bf16[4,16,1792]{2,1,0:T(8,128)(2,1)S(1)} collective-permute-done((bf16[4,16,1792]{2,1,0:T(8,128)(2,1)S(1)}, bf16[4,16,1792]{2,1,0:T(8,128)(2,1)S(1)}, u32[]{:S(2)}, u32[]{:S(2)}) %collective-permute-start.16) | collective-permute-done | bytes 229408 | tf_op jit(solution)/shard_map/ppermute | solution.py:496
  53.3 18.7 %first_forward.1 = (bf16[256,4096]{1,0:T(8,128)(2,1)}, f32[4,352,256]{2,1,0:T(8,128)}, f32[4,352,256]{2,1,0:T(8,128)}, bf16[4,384,768]{2,1,0:T(8,128)(2,1)}, bf1...) custom-call(s32[2]{0:T(128)} %pad_add_fusion.3.place_ref.refs_0_, ...), custom_call_target="tpu_custom_call" | custom-call | flops 4000000000 | bytes 20000000 | tf_op jit(solution)/shard_map/first_forward/pallas_call | solution.py:698
  72.0 1.5 slice.105.refs_4_
  74.5 39.3 %middle.1 = (f32[4,352,256]{2,1,0:T(8,128)}, f32[4,4,16,1792]{3,2,1,0:T(8,128)}, bf16[4,4,16,1792]{3,2,1,0:T(8,128)(2,1)}, f32[128,256]{1,0:T(8,128)}, f32[256,128]{1,0:T(8,128)}, /*index=5*/f32[8,128]{1,0:T(8,128)}) custom-call(s32[2]{0:T(128)} %pad_add_fusion.3.place_ref.refs_0_, s32[4,352,8]{2,1,0:T(8,128)} %pad_select_fusion.refs_1_, ...), custom_call_target="tpu_custom_call" | custom-call | flops 15000000512 | bytes 20000000 | tf_op jit(solution)/shard_map/middle/pallas_call | solution.py:717
  114.3 25.6 %first_backward.1 = (f32[4,4,16,2048]{3,2,1,0:T(8,128)}, bf16[4,4,16,2048]{3,2,1,0:T(8,128)(2,1)}) custom-call(s32[2]{0:T(128)} %pad_add_fusion.3.place_ref.refs_0_, s32[4,352,8]{2,1,0:T(8,128)} %pad_select_fusion.refs_1_, f32[14,256]{1,0:T(8,128)} %refs_26_.1, bf16[256,4096]{1,0:T(8,128)(2,1)} %get-tuple-element.85.refs_3_, ...), custom_call_target="tpu_custom_call" | custom-call | flops 8000000000 | bytes 20000000 | tf_op jit(solution)/shard_map/first_backward/pallas_call | solution.py:760
  141.9 1.8 collective-permute-start.31
  144.5 1.1 collective-permute-start.23
  145.6 3.0 %collective-permute-done.29 = bf16[4,16,1792]{2,1,0:T(8,128)(2,1)S(1)} collective-permute-done((bf16[4,16,1792]{2,1,0:T(8,128)(2,1)S(1)}, bf16[4,16,1792]{2,1,0:T(8,128)(2,1)S(1)}, u32[]{:S(2)}, u32[]{:S(2)}) %collective-permute-start.29) | collective-permute-done | bytes 229408 | tf_op jit(solution)/shard_map/ppermute | solution.py:496
  149.7 4.4 %collective-permute-done.30 = bf16[4,16,1792]{2,1,0:T(8,128)(2,1)S(1)} collective-permute-done((bf16[4,16,1792]{2,1,0:T(8,128)(2,1)S(1)}, bf16[4,16,1792]{2,1,0:T(8,128)(2,1)S(1)}, u32[]{:S(2)}, u32[]{:S(2)}) %collective-permute-start.30) | collective-permute-done | bytes 229408 | tf_op jit(solution)/shard_map/ppermute | solution.py:496
  154.3 1.8 collective-permute-start.32
  156.1 1.8 collective-permute-start.33
  159.2 3.0 %collective-permute-start.34 = (bf16[16,1792]{1,0:T(8,128)(2,1)S(1)}, bf16[16,1792]{1,0:T(8,128)(2,1)S(1)}, u32[]{:S(2)}, u32[]{:S(2)}) collective-permute-start(bf16[16,1792]{1,0:T(8,128)(2,1)S(1)} %get-tuple-element.271), channel_id=1, source_target_pairs={{0,24},{2,26},{4,28},{6,30},{8,16},{10,18},{12,20},{14,22},{16,8},... | collective-permute-start | bytes 172040 | tf_op jit(solution)/shard_map/ppermute | solution.py:496
  162.2 2.3 %collective-permute-done.23 = bf16[4,16,2048]{2,1,0:T(8,128)(2,1)S(1)} collective-permute-done((bf16[4,16,2048]{2,1,0:T(8,128)(2,1)S(1)}, bf16[4,16,2048]{2,1,0:T(8,128)(2,1)S(1)}, u32[]{:S(2)}, u32[]{:S(2)}) %collective-permute-start.23) | collective-permute-done | bytes 262176 | tf_op jit(solution)/shard_map/ppermute | solution.py:496
  164.8 1.8 collective-permute-start.25
  166.7 1.8 collective-permute-start.26
  168.5 1.4 collective-permute-start.27
  170.6 4.0 %collective-permute-done.26.refs_2_ = bf16[16,2048]{1,0:T(8,128)(2,1)S(1)} collective-permute-done((bf16[16,2048]{1,0:T(8,128)(2,1)S(1)}, bf16[16,2048]{1,0:T(8,128)(2,1)S(1)}, u32[]{:S(2)}, u32[]{:S(2)}) %collective-permute-start.26) | collective-permute-done | bytes 65568 | tf_op jit(solution)/shard_map/ppermute | solution.py:496
  175.3 1.9 finish.1
  177.2 1.4 collective-permute-done.35.refs_3_
  179.4 1.4 collective-permute-start.36
  181.4 1.4 collective-permute-start.38
  183.0 1.4 collective-permute-done.37
  184.5 1.5 collective-permute-done.38
  186.0 1.3 collective-permute-start.39
  187.3 1.6 collective-permute-start.40
  188.9 1.4 collective-permute-start.41
  197.9 5.4 %adam.1 = (f32[1,1]{1,0:T(1,128)}, f32[1,1]{1,0:T(1,128)}, f32[1,1]{1,0:T(1,128)}, f32[896,16]{1,0:T(8,128)}, f32[896,16]{1,0:T(8,128)}, /*index=5*/f32[896,16]{...) custom-call(s32[2]{0:T(128)} %pad_add_fusion.3.place_ref.refs_0_, ...), custom_call_target="tpu_custom_call" | custom-call | flops 1000000 | bytes 1000000 | tf_op jit(solution)/shard_map/adam/pallas_call | solution.py:836
  203.4 2.0 copy.224
  205.3 1.8 copy.225
  207.2 1.8 copy.226
  (213 shorter events, 37.1 us)
Async XLA Ops:
  2.7 29.8 %copy-start.47 = (s32[8]{0:T(128)S(1)}, s32[8]{0:T(128)}, u32[]{:S(2)}) copy-start(s32[8]{0:T(128)} %param.35) | copy-start | bytes 100
  10.1 16.4 %collective-permute-start.1 = (bf16[16,2048]{1,0:T(8,128)(2,1)}, bf16[16,2048]{1,0:T(8,128)(2,1)S(1)}, u32[]{:S(2)}, u32[]{:S(2)}) collective-permute-start(bf16[16,2048]{1,0:T(8,128)(2,1)} %get-tuple-element.84), channel_id=1, source_target_pairs={{0,8},{2,10},{4,12},{6,14},{8,0},{10,2},{12,4},{14,6},{16,24},{18,... | collective-permute-start | bytes 196616 | tf_op jit(solution)/shard_map/ppermute | solution.py:496
  13.2 14.9 %collective-permute-start.2 = (bf16[16,2048]{1,0:T(8,128)(2,1)}, bf16[16,2048]{1,0:T(8,128)(2,1)S(1)}, u32[]{:S(2)}, u32[]{:S(2)}) collective-permute-start(bf16[16,2048]{1,0:T(8,128)(2,1)} %get-tuple-element.84), channel_id=1, source_target_pairs={{0,16},{2,18},{4,20},{6,22},{8,24},{10,26},{12,28},{14,30},{16,0},... | collective-permute-start | bytes 196616 | tf_op jit(solution)/shard_map/ppermute | solution.py:496
  15.7 5.1 %collective-permute-start.11 = (bf16[16,1792]{1,0:T(8,128)(2,1)}, bf16[16,1792]{1,0:T(8,128)(2,1)S(1)}, u32[]{:S(2)}, u32[]{:S(2)}) collective-permute-start(bf16[16,1792]{1,0:T(8,128)(2,1)} %get-tuple-element.87), channel_id=1, source_target_pairs={{0,8},{2,10},{4,12},{6,14},{8,0},{10,2},{12,4},{14,6},{16,24},{18,... | collective-permute-start | bytes 172040 | tf_op jit(solution)/shard_map/ppermute | solution.py:496
  16.2 7.9 %collective-permute-start.12 = (bf16[16,1792]{1,0:T(8,128)(2,1)}, bf16[16,1792]{1,0:T(8,128)(2,1)S(1)}, u32[]{:S(2)}, u32[]{:S(2)}) collective-permute-start(bf16[16,1792]{1,0:T(8,128)(2,1)} %get-tuple-element.87), channel_id=1, source_target_pairs={{0,16},{2,18},{4,20},{6,22},{8,24},{10,26},{12,28},{14,30},{16,0},... | collective-permute-start | bytes 172040 | tf_op jit(solution)/shard_map/ppermute | solution.py:496
  16.2 7.9 %collective-permute-start.13 = (bf16[16,1792]{1,0:T(8,128)(2,1)}, bf16[16,1792]{1,0:T(8,128)(2,1)S(1)}, u32[]{:S(2)}, u32[]{:S(2)}) collective-permute-start(bf16[16,1792]{1,0:T(8,128)(2,1)} %get-tuple-element.87), channel_id=1, source_target_pairs={{0,24},{2,26},{4,28},{6,30},{8,16},{10,18},{12,20},{14,22},{16,8},... | collective-permute-start | bytes 172040 | tf_op jit(solution)/shard_map/ppermute | solution.py:496
  20.9 7.2 %collective-permute-start.3 = (bf16[16,2048]{1,0:T(8,128)(2,1)}, bf16[16,2048]{1,0:T(8,128)(2,1)S(1)}, u32[]{:S(2)}, u32[]{:S(2)}) collective-permute-start(bf16[16,2048]{1,0:T(8,128)(2,1)} %get-tuple-element.84), channel_id=1, source_target_pairs={{0,24},{2,26},{4,28},{6,30},{8,16},{10,18},{12,20},{14,22},{16,8},... | collective-permute-start | bytes 196616 | tf_op jit(solution)/shard_map/ppermute | solution.py:496
  24.1 7.1 %collective-permute-start = (f32[2,512]{1,0:T(2,128)S(1)}, f32[2,512]{1,0:T(2,128)S(1)}, u32[]{:S(2)}, u32[]{:S(2)}) collective-permute-start(f32[2,512]{1,0:T(2,128)S(1)} %copy-done.26), channel_id=1, source_target_pairs={{0,1},{1,0},{2,3},{3,2},{4,5},{5,4},{6,7},{7,6},{8,9},{9,8},{10,11... | collective-permute-start | bytes 12296 | tf_op jit(solution)/shard_map/ppermute | solution.py:496
  24.9 18.8 %collective-permute-start.14 = (bf16[4,16,1792]{2,1,0:T(8,128)(2,1)S(1)}, bf16[4,16,1792]{2,1,0:T(8,128)(2,1)}, u32[]{:S(2)}, u32[]{:S(2)}) collective-permute-start(bf16[4,16,1792]{2,1,0:T(8,128)(2,1)S(1)} %pad_maximum_fusion.1.refs_6_), channel_id=1, source_target_pairs={{0,2},{2,0},{4,6},{6,4},{8,10},{10,8},{12,14},{14,12},{16,18},{18,... | collective-permute-start | bytes 688136 | tf_op jit(solution)/shard_map/ppermute | solution.py:496
  26.5 19.0 %collective-permute-start.15 = (bf16[4,16,1792]{2,1,0:T(8,128)(2,1)S(1)}, bf16[4,16,1792]{2,1,0:T(8,128)(2,1)}, u32[]{:S(2)}, u32[]{:S(2)}) collective-permute-start(bf16[4,16,1792]{2,1,0:T(8,128)(2,1)S(1)} %pad_maximum_fusion.1.refs_6_), channel_id=1, source_target_pairs={{0,4},{2,6},{4,0},{6,2},{8,12},{10,14},{12,8},{14,10},{16,20},{18,... | collective-permute-start | bytes 688136 | tf_op jit(solution)/shard_map/ppermute | solution.py:496
  28.9 16.6 %collective-permute-start.6 = (bf16[4,16,2048]{2,1,0:T(8,128)(2,1)S(1)}, bf16[4,16,2048]{2,1,0:T(8,128)(2,1)}, u32[]{:S(2)}, u32[]{:S(2)}) collective-permute-start(bf16[4,16,2048]{2,1,0:T(8,128)(2,1)S(1)} %pad_maximum_fusion.refs_4_), channel_id=1, source_target_pairs={{0,6},{2,4},{4,2},{6,0},{8,14},{10,12},{12,10},{14,8},{16,22},{18,... | collective-permute-start | bytes 786440 | tf_op jit(solution)/shard_map/ppermute | solution.py:496
  30.7 15.3 %collective-permute-start.4 = (bf16[4,16,2048]{2,1,0:T(8,128)(2,1)S(1)}, bf16[4,16,2048]{2,1,0:T(8,128)(2,1)}, u32[]{:S(2)}, u32[]{:S(2)}) collective-permute-start(bf16[4,16,2048]{2,1,0:T(8,128)(2,1)S(1)} %pad_maximum_fusion.refs_4_), channel_id=1, source_target_pairs={{0,2},{2,0},{4,6},{6,4},{8,10},{10,8},{12,14},{14,12},{16,18},{18,... | collective-permute-start | bytes 786440 | tf_op jit(solution)/shard_map/ppermute | solution.py:496
  31.2 14.9 %collective-permute-start.5 = (bf16[4,16,2048]{2,1,0:T(8,128)(2,1)S(1)}, bf16[4,16,2048]{2,1,0:T(8,128)(2,1)}, u32[]{:S(2)}, u32[]{:S(2)}) collective-permute-start(bf16[4,16,2048]{2,1,0:T(8,128)(2,1)S(1)} %pad_maximum_fusion.refs_4_), channel_id=1, source_target_pairs={{0,4},{2,6},{4,0},{6,2},{8,12},{10,14},{12,8},{14,10},{16,20},{18,... | collective-permute-start | bytes 786440 | tf_op jit(solution)/shard_map/ppermute | solution.py:496
  43.7 7.6 %collective-permute-start.16 = (bf16[4,16,1792]{2,1,0:T(8,128)(2,1)S(1)}, bf16[4,16,1792]{2,1,0:T(8,128)(2,1)S(1)}, u32[]{:S(2)}, u32[]{:S(2)}) collective-permute-start(bf16[4,16,1792]{2,1,0:T(8,128)(2,1)S(1)} %pad_maximum_fusion.1.refs_6_), channel_id=1, source_target_pairs={{0,6},{2,4},{4,2},{6,0},{8,14},{10,12},{12,10},{14,8},{16,22},{18,... | collective-permute-start | bytes 688136 | tf_op jit(solution)/shard_map/ppermute | solution.py:496
  45.5 5.8 %collective-permute-start.7 = (bf16[4,16,2048]{2,1,0:T(8,128)(2,1)S(1)}, bf16[4,16,2048]{2,1,0:T(8,128)(2,1)S(1)}, u32[]{:S(2)}, u32[]{:S(2)}) collective-permute-start(bf16[4,16,2048]{2,1,0:T(8,128)(2,1)S(1)} %pad_maximum_fusion.refs_4_), channel_id=1, source_target_pairs={{0,1},{1,0},{2,3},{3,2},{4,5},{5,4},{6,7},{7,6},{8,9},{9,8},{10,11... | collective-permute-start | bytes 786440 | tf_op jit(solution)/shard_map/ppermute | solution.py:496
  45.5 6.3 %collective-permute-start.10 = (bf16[4,16,2048]{2,1,0:T(8,128)(2,1)}, bf16[4,16,2048]{2,1,0:T(8,128)(2,1)S(1)}, u32[]{:S(2)}, u32[]{:S(2)}) collective-permute-start(bf16[4,16,2048]{2,1,0:T(8,128)(2,1)} %collective-permute-done.6.refs_7_), channel_id=1, source_target_pairs={{0,1},{1,0},{2,3},{3,2},{4,5},{5,4},{6,7},{7,6},{8,9},{9,8},{10,11... | collective-permute-start | bytes 786440 | tf_op jit(solution)/shard_map/ppermute | solution.py:496
  46.0 5.9 %collective-permute-start.8 = (bf16[4,16,2048]{2,1,0:T(8,128)(2,1)}, bf16[4,16,2048]{2,1,0:T(8,128)(2,1)S(1)}, u32[]{:S(2)}, u32[]{:S(2)}) collective-permute-start(bf16[4,16,2048]{2,1,0:T(8,128)(2,1)} %collective-permute-done.4.refs_5_), channel_id=1, source_target_pairs={{0,1},{1,0},{2,3},{3,2},{4,5},{5,4},{6,7},{7,6},{8,9},{9,8},{10,11... | collective-permute-start | bytes 786440 | tf_op jit(solution)/shard_map/ppermute | solution.py:496
  46.1 6.3 %collective-permute-start.9 = (bf16[4,16,2048]{2,1,0:T(8,128)(2,1)}, bf16[4,16,2048]{2,1,0:T(8,128)(2,1)S(1)}, u32[]{:S(2)}, u32[]{:S(2)}) collective-permute-start(bf16[4,16,2048]{2,1,0:T(8,128)(2,1)} %collective-permute-done.5.refs_6_), channel_id=1, source_target_pairs={{0,1},{1,0},{2,3},{3,2},{4,5},{5,4},{6,7},{7,6},{8,9},{9,8},{10,11... | collective-permute-start | bytes 786440 | tf_op jit(solution)/shard_map/ppermute | solution.py:496
  51.3 22.2 %collective-permute-start.17 = (bf16[4,16,1792]{2,1,0:T(8,128)(2,1)S(1)}, bf16[4,16,1792]{2,1,0:T(8,128)(2,1)S(1)}, u32[]{:S(2)}, u32[]{:S(2)}) collective-permute-start(bf16[4,16,1792]{2,1,0:T(8,128)(2,1)S(1)} %pad_maximum_fusion.1.refs_6_), channel_id=1, source_target_pairs={{0,1},{1,0},{2,3},{3,2},{4,5},{5,4},{6,7},{7,6},{8,9},{9,8},{10,11... | collective-permute-start | bytes 688136 | tf_op jit(solution)/shard_map/ppermute | solution.py:496
  51.3 22.1 %collective-permute-start.18 = (bf16[4,16,1792]{2,1,0:T(8,128)(2,1)}, bf16[4,16,1792]{2,1,0:T(8,128)(2,1)S(1)}, u32[]{:S(2)}, u32[]{:S(2)}) collective-permute-start(bf16[4,16,1792]{2,1,0:T(8,128)(2,1)} %collective-permute-done.14.refs_7_), channel_id=1, source_target_pairs={{0,1},{1,0},{2,3},{3,2},{4,5},{5,4},{6,7},{7,6},{8,9},{9,8},{10,11... | collective-permute-start | bytes 688136 | tf_op jit(solution)/shard_map/ppermute | solution.py:496
  51.8 21.7 %collective-permute-start.19 = (bf16[4,16,1792]{2,1,0:T(8,128)(2,1)}, bf16[4,16,1792]{2,1,0:T(8,128)(2,1)S(1)}, u32[]{:S(2)}, u32[]{:S(2)}) collective-permute-start(bf16[4,16,1792]{2,1,0:T(8,128)(2,1)} %collective-permute-done.15.refs_8_), channel_id=1, source_target_pairs={{0,1},{1,0},{2,3},{3,2},{4,5},{5,4},{6,7},{7,6},{8,9},{9,8},{10,11... | collective-permute-start | bytes 688136 | tf_op jit(solution)/shard_map/ppermute | solution.py:496
  51.9 21.6 %collective-permute-start.20 = (bf16[4,16,1792]{2,1,0:T(8,128)(2,1)S(1)}, bf16[4,16,1792]{2,1,0:T(8,128)(2,1)S(1)}, u32[]{:S(2)}, u32[]{:S(2)}) collective-permute-start(bf16[4,16,1792]{2,1,0:T(8,128)(2,1)S(1)} %collective-permute-done.16.refs_9_), channel_id=1, source_target_pairs={{0,1},{1,0},{2,3},{3,2},{4,5},{5,4},{6,7},{7,6},{8,9},{9,8},{10,11... | collective-permute-start | bytes 688136 | tf_op jit(solution)/shard_map/ppermute | solution.py:496
  113.8 26.2 %collective-permute-start.28 = (bf16[4,4,16,1792]{3,2,1,0:T(8,128)(2,1)}, bf16[4,4,16,1792]{3,2,1,0:T(8,128)(2,1)S(1)}, u32[]{:S(2)}, u32[]{:S(2)}) collective-permute-start(bf16[4,4,16,1792]{3,2,1,0:T(8,128)(2,1)} %get-tuple-element.103), channel_id=1, source_target_pairs={{0,1},{1,0},{2,3},{3,2},{4,5},{5,4},{6,7},{7,6},{8,9},{9,8},{10,11... | collective-permute-start | bytes 2752520 | tf_op jit(solution)/shard_map/ppermute | solution.py:496
  139.9 3.8 %collective-permute-start.21 = (bf16[4,4,16,2048]{3,2,1,0:T(8,128)(2,1)}, bf16[4,4,16,2048]{3,2,1,0:T(8,128)(2,1)S(1)}, u32[]{:S(2)}, u32[]{:S(2)}) collective-permute-start(bf16[4,4,16,2048]{3,2,1,0:T(8,128)(2,1)} %get-tuple-element.101), channel_id=1, source_target_pairs={{0,1},{1,0},{2,3},{3,2},{4,5},{5,4},{6,7},{7,6},{8,9},{9,8},{10,11... | collective-permute-start | bytes 3145736 | tf_op jit(solution)/shard_map/ppermute | solution.py:496
  140.2 8.5 %collective-permute-start.29 = (bf16[4,16,1792]{2,1,0:T(8,128)(2,1)S(1)}, bf16[4,16,1792]{2,1,0:T(8,128)(2,1)S(1)}, u32[]{:S(2)}, u32[]{:S(2)}) collective-permute-start(bf16[4,16,1792]{2,1,0:T(8,128)(2,1)S(1)} %get-tuple-element.265), channel_id=1, source_target_pairs={{0,2},{2,0},{4,6},{6,4},{8,10},{10,8},{12,14},{14,12},{16,18},{18,... | collective-permute-start | bytes 688136 | tf_op jit(solution)/shard_map/ppermute | solution.py:496
  140.8 13.4 %collective-permute-start.30 = (bf16[4,16,1792]{2,1,0:T(8,128)(2,1)S(1)}, bf16[4,16,1792]{2,1,0:T(8,128)(2,1)S(1)}, u32[]{:S(2)}, u32[]{:S(2)}) collective-permute-start(bf16[4,16,1792]{2,1,0:T(8,128)(2,1)S(1)} %get-tuple-element.267), channel_id=1, source_target_pairs={{0,4},{2,6},{4,0},{6,2},{8,12},{10,14},{12,8},{14,10},{16,20},{18,... | collective-permute-start | bytes 688136 | tf_op jit(solution)/shard_map/ppermute | solution.py:496
  141.9 12.2 %collective-permute-start.31 = (bf16[4,16,1792]{2,1,0:T(8,128)(2,1)S(1)}, bf16[4,16,1792]{2,1,0:T(8,128)(2,1)S(1)}, u32[]{:S(2)}, u32[]{:S(2)}) collective-permute-start(bf16[4,16,1792]{2,1,0:T(8,128)(2,1)S(1)} %get-tuple-element.266), channel_id=1, source_target_pairs={{0,6},{2,4},{4,2},{6,0},{8,14},{10,12},{12,10},{14,8},{16,22},{18,... | collective-permute-start | bytes 688136 | tf_op jit(solution)/shard_map/ppermute | solution.py:496
  143.9 15.3 %collective-permute-start.22 = (bf16[4,16,2048]{2,1,0:T(8,128)(2,1)S(1)}, bf16[4,16,2048]{2,1,0:T(8,128)(2,1)S(1)}, u32[]{:S(2)}, u32[]{:S(2)}) collective-permute-start(bf16[4,16,2048]{2,1,0:T(8,128)(2,1)S(1)} %get-tuple-element.262), channel_id=1, source_target_pairs={{0,2},{2,0},{4,6},{6,4},{8,10},{10,8},{12,14},{14,12},{16,18},{18,... | collective-permute-start | bytes 786440 | tf_op jit(solution)/shard_map/ppermute | solution.py:496
  144.5 20.1 %collective-permute-start.23 = (bf16[4,16,2048]{2,1,0:T(8,128)(2,1)S(1)}, bf16[4,16,2048]{2,1,0:T(8,128)(2,1)S(1)}, u32[]{:S(2)}, u32[]{:S(2)}) collective-permute-start(bf16[4,16,2048]{2,1,0:T(8,128)(2,1)S(1)} %get-tuple-element.264), channel_id=1, source_target_pairs={{0,4},{2,6},{4,0},{6,2},{8,12},{10,14},{12,8},{14,10},{16,20},{18,... | collective-permute-start | bytes 786440 | tf_op jit(solution)/shard_map/ppermute | solution.py:496
  148.6 15.9 %collective-permute-start.24 = (bf16[4,16,2048]{2,1,0:T(8,128)(2,1)S(1)}, bf16[4,16,2048]{2,1,0:T(8,128)(2,1)S(1)}, u32[]{:S(2)}, u32[]{:S(2)}) collective-permute-start(bf16[4,16,2048]{2,1,0:T(8,128)(2,1)S(1)} %get-tuple-element.263), channel_id=1, source_target_pairs={{0,6},{2,4},{4,2},{6,0},{8,14},{10,12},{12,10},{14,8},{16,22},{18,... | collective-permute-start | bytes 786440 | tf_op jit(solution)/shard_map/ppermute | solution.py:496
  154.3 14.2 %collective-permute-start.32 = (bf16[16,1792]{1,0:T(8,128)(2,1)S(1)}, bf16[16,1792]{1,0:T(8,128)(2,1)S(1)}, u32[]{:S(2)}, u32[]{:S(2)}) collective-permute-start(bf16[16,1792]{1,0:T(8,128)(2,1)S(1)} %get-tuple-element.273), channel_id=1, source_target_pairs={{0,8},{2,10},{4,12},{6,14},{8,0},{10,2},{12,4},{14,6},{16,24},{18,... | collective-permute-start | bytes 172040 | tf_op jit(solution)/shard_map/ppermute | solution.py:496
  156.1 14.4 %collective-permute-start.33 = (bf16[16,1792]{1,0:T(8,128)(2,1)S(1)}, bf16[16,1792]{1,0:T(8,128)(2,1)S(1)}, u32[]{:S(2)}, u32[]{:S(2)}) collective-permute-start(bf16[16,1792]{1,0:T(8,128)(2,1)S(1)} %get-tuple-element.272), channel_id=1, source_target_pairs={{0,16},{2,18},{4,20},{6,22},{8,24},{10,26},{12,28},{14,30},{16,0},... | collective-permute-start | bytes 172040 | tf_op jit(solution)/shard_map/ppermute | solution.py:496
  159.2 31.2 %copy-start.13 = (f32[2,512,16]{1,2,0:T(8,128)S(1)}, f32[2,512,16]{1,2,0:T(8,128)}, u32[]{:S(2)}) copy-start(f32[2,512,16]{1,2,0:T(8,128)} %param.55) | copy-start | bytes 196612
  159.2 32.2 %copy-start.14 = (f32[2,512,16]{1,2,0:T(8,128)S(1)}, f32[2,512,16]{1,2,0:T(8,128)}, u32[]{:S(2)}) copy-start(f32[2,512,16]{1,2,0:T(8,128)} %param.56) | copy-start | bytes 196612
  159.2 11.3 %collective-permute-start.34 = (bf16[16,1792]{1,0:T(8,128)(2,1)S(1)}, bf16[16,1792]{1,0:T(8,128)(2,1)S(1)}, u32[]{:S(2)}, u32[]{:S(2)}) collective-permute-start(bf16[16,1792]{1,0:T(8,128)(2,1)S(1)} %get-tuple-element.271), channel_id=1, source_target_pairs={{0,24},{2,26},{4,28},{6,30},{8,16},{10,18},{12,20},{14,22},{16,8},... | collective-permute-start | bytes 172040 | tf_op jit(solution)/shard_map/ppermute | solution.py:496
  164.8 30.3 %copy-start.28 = (f32[2,128,16]{1,2,0:T(8,128)S(1)}, f32[2,128,16]{1,2,0:T(8,128)}, u32[]{:S(2)}) copy-start(f32[2,128,16]{1,2,0:T(8,128)} %param.47) | copy-start | bytes 49156
  164.8 31.0 %copy-start.32 = (f32[16,5]{0,1:T(8,128)S(1)}, f32[16,5]{0,1:T(8,128)}, u32[]{:S(2)}) copy-start(f32[16,5]{0,1:T(8,128)} %param.64) | copy-start | bytes 964
  164.8 31.7 %copy-start.33 = (f32[16,5]{0,1:T(8,128)S(1)}, f32[16,5]{0,1:T(8,128)}, u32[]{:S(2)}) copy-start(f32[16,5]{0,1:T(8,128)} %param.65) | copy-start | bytes 964
  164.8 5.7 %collective-permute-start.25 = (bf16[16,2048]{1,0:T(8,128)(2,1)S(1)}, bf16[16,2048]{1,0:T(8,128)(2,1)S(1)}, u32[]{:S(2)}, u32[]{:S(2)}) collective-permute-start(bf16[16,2048]{1,0:T(8,128)(2,1)S(1)} %get-tuple-element.270), channel_id=1, source_target_pairs={{0,8},{2,10},{4,12},{6,14},{8,0},{10,2},{12,4},{14,6},{16,24},{18,... | collective-permute-start | bytes 196616 | tf_op jit(solution)/shard_map/ppermute | solution.py:496
  166.7 8.0 %collective-permute-start.26 = (bf16[16,2048]{1,0:T(8,128)(2,1)S(1)}, bf16[16,2048]{1,0:T(8,128)(2,1)S(1)}, u32[]{:S(2)}, u32[]{:S(2)}) collective-permute-start(bf16[16,2048]{1,0:T(8,128)(2,1)S(1)} %get-tuple-element.269), channel_id=1, source_target_pairs={{0,16},{2,18},{4,20},{6,22},{8,24},{10,26},{12,28},{14,30},{16,0},... | collective-permute-start | bytes 196616 | tf_op jit(solution)/shard_map/ppermute | solution.py:496
  168.5 6.1 %collective-permute-start.27 = (bf16[16,2048]{1,0:T(8,128)(2,1)S(1)}, bf16[16,2048]{1,0:T(8,128)(2,1)S(1)}, u32[]{:S(2)}, u32[]{:S(2)}) collective-permute-start(bf16[16,2048]{1,0:T(8,128)(2,1)S(1)} %get-tuple-element.268), channel_id=1, source_target_pairs={{0,24},{2,26},{4,28},{6,30},{8,16},{10,18},{12,20},{14,22},{16,8},... | collective-permute-start | bytes 196616 | tf_op jit(solution)/shard_map/ppermute | solution.py:496
  177.2 1.4 collective-permute-start.35
  179.4 3.7 %collective-permute-start.36 = (f32[16,128]{1,0:T(8,128)S(1)}, f32[16,128]{1,0:T(8,128)S(1)}, u32[]{:S(2)}, u32[]{:S(2)}) collective-permute-start(f32[16,128]{1,0:T(8,128)S(1)} %slice_add_fusion), channel_id=1, source_target_pairs={{0,2},{2,0},{4,6},{6,4},{8,10},{10,8},{12,14},{14,12},{16,18},{18,... | collective-permute-start | bytes 24584 | tf_op jit(solution)/shard_map/ppermute | solution.py:496
  180.8 3.7 %collective-permute-start.37 = (f32[16,128]{1,0:T(8,128)S(1)}, f32[16,128]{1,0:T(8,128)S(1)}, u32[]{:S(2)}, u32[]{:S(2)}) collective-permute-start(f32[16,128]{1,0:T(8,128)S(1)} %slice_add_fusion), channel_id=1, source_target_pairs={{0,4},{2,6},{4,0},{6,2},{8,12},{10,14},{12,8},{14,10},{16,20},{18,... | collective-permute-start | bytes 24584 | tf_op jit(solution)/shard_map/ppermute | solution.py:496
  181.4 4.5 %collective-permute-start.38 = (f32[16,128]{1,0:T(8,128)S(1)}, f32[16,128]{1,0:T(8,128)S(1)}, u32[]{:S(2)}, u32[]{:S(2)}) collective-permute-start(f32[16,128]{1,0:T(8,128)S(1)} %slice_add_fusion), channel_id=1, source_target_pairs={{0,6},{2,4},{4,2},{6,0},{8,14},{10,12},{12,10},{14,8},{16,22},{18,... | collective-permute-start | bytes 24584 | tf_op jit(solution)/shard_map/ppermute | solution.py:496
  186.0 11.2 %collective-permute-start.39 = (f32[4,16,128]{2,1,0:T(8,128)S(1)}, f32[4,16,128]{2,1,0:T(8,128)S(1)}, u32[]{:S(2)}, u32[]{:S(2)}) collective-permute-start(f32[4,16,128]{2,1,0:T(8,128)S(1)} %pad_maximum_fusion.2.refs_4_), channel_id=1, source_target_pairs={{0,8},{2,10},{4,12},{6,14},{8,0},{10,2},{12,4},{14,6},{16,24},{18,... | collective-permute-start | bytes 98312 | tf_op jit(solution)/shard_map/ppermute | solution.py:496
  187.3 9.9 %collective-permute-start.40 = (f32[4,16,128]{2,1,0:T(8,128)S(1)}, f32[4,16,128]{2,1,0:T(8,128)S(1)}, u32[]{:S(2)}, u32[]{:S(2)}) collective-permute-start(f32[4,16,128]{2,1,0:T(8,128)S(1)} %pad_maximum_fusion.2.refs_4_), channel_id=1, source_target_pairs={{0,16},{2,18},{4,20},{6,22},{8,24},{10,26},{12,28},{14,30},{16,0},... | collective-permute-start | bytes 98312 | tf_op jit(solution)/shard_map/ppermute | solution.py:496
  188.9 8.3 %collective-permute-start.41 = (f32[4,16,128]{2,1,0:T(8,128)S(1)}, f32[4,16,128]{2,1,0:T(8,128)S(1)}, u32[]{:S(2)}, u32[]{:S(2)}) collective-permute-start(f32[4,16,128]{2,1,0:T(8,128)S(1)} %pad_maximum_fusion.2.refs_4_), channel_id=1, source_target_pairs={{0,24},{2,26},{4,28},{6,30},{8,16},{10,18},{12,20},{14,22},{16,8},... | collective-permute-start | bytes 98312 | tf_op jit(solution)/shard_map/ppermute | solution.py:496
  (42 other events, 437.2 us)

commit v2 on v1

v2 whole, which is shorter than its diff:
```python
import functools

import jax
import jax.numpy as jnp
from jax import lax
from jax.experimental import pallas as pl
from jax.experimental.pallas import tpu as pltpu
from jax.sharding import PartitionSpec as P

D = 256
HEADS = 4
HEAD_DIM = 64
FF = 1024
VOCAB = 512
ACTIONS = 18
GAMES = 26
OBS = 16
FRAMES = 20
STEP_NUMBER = 5
FRAME_TOKENS = 17
LENGTH = 340
ROWS = 896
NVEC = 14

EPS_NORM = 1e-05
BETA_ONE = 0.5
BETA_TWO = 0.5
RATE_TABLE = 0.5
RATE_MATRIX = 0.05
RATE_VECTOR = 0.2
DECAY_RATE = 0.01
EPS_ADAM = 1e-08
CLIP_AT = 0.1

SEQ = 352
KEYS = 384
QBLOCKS = ((0, 128, 128), (128, 128, 256), (256, 96, 384))

COL_QKV, COL_PROJ, COL_UP, COL_DOWN, COL_LAYER = 0, 768, 1024, 2048, 3072
HALF_ATTENTION = ((0, 128, 0), (128, 128, 256), (256, 128, 512), (384, 128, COL_PROJ))
HALF_LAYER = HALF_ATTENTION + ((512, 512, COL_UP), (1024, 512, COL_DOWN))
COL_TABLE, COL_SMALL, COL_FIRST = 3072, 3968, 4096
HALF_FIRST = HALF_LAYER + ((1536, 512, COL_TABLE),)
HALF_FIRST_COLS = 2048
COL_HEAD, COL_SECOND = 3072, 3584
HALF_SECOND = HALF_LAYER + ((1536, 256, COL_HEAD),)
HALF_SECOND_COLS = 1792
GRAD_UP, GRAD_DOWN = 0, 1024
HALF_GRAD_FF = ((0, 512, GRAD_UP), (512, 512, GRAD_DOWN))
GRAD_TABLE, GRAD_SMALL = 1024, 1920
HALF_GRAD_REST = HALF_ATTENTION + ((512, 512, GRAD_TABLE),)
HALF_GRAD_COLS = 1024
SMALL_ROWS, SMALL_BIAS, SMALL_SIDE = 32, 14, 22

F32, BF16 = jnp.float32, jnp.bfloat16
VMEM_BYTES = 60 * 1024 * 1024


def dot_nn(a, b):
    return lax.dot_general(a, b, (((1,), (0,)), ((), ())), preferred_element_type=F32)


def dot_nt(a, b):
    return lax.dot_general(a, b, (((1,), (1,)), ((), ())), preferred_element_type=F32)


def dot_tn(a, b):
    return lax.dot_general(a, b, (((0,), (0,)), ((), ())), preferred_element_type=F32)


def normalise(x):
    centred = x - jnp.mean(x, axis=1, keepdims=True)
    scale = lax.rsqrt(jnp.mean(centred * centred, axis=1, keepdims=True) + EPS_NORM)
    return centred * scale, scale


def normalise_back(grad, xhat, scale, gain):
    inner = grad * gain
    mean_one = jnp.mean(inner, axis=1, keepdims=True)
    mean_two = jnp.mean(inner * xhat, axis=1, keepdims=True)
    return scale * (inner - mean_one - xhat * mean_two)


def column_sum(a):
    return jnp.sum(a, axis=0, keepdims=True)


def head_masks(a, scale=None):
    lane = lax.broadcasted_iota(jnp.int32, (1, D), 1)
    zero = jnp.zeros((), a.dtype)
    if scale is not None:
        a = a * jnp.asarray(scale, a.dtype)
    return [
        jnp.where((lane >= h * HEAD_DIM) & (lane < (h + 1) * HEAD_DIM), a, zero)
        for h in range(HEADS)
    ]


def assemble(pieces_mine, pieces_other, place_ref, w_ref, halves):
    me, core = place_ref[0], place_ref[1]
    is_first = core == 0
    for p in range(4):
        for z in range(4):
            row = pl.multiple_of((me ^ (4 * z + p)) * 16, 16)
            for src, width, dest in halves:
                mine = pieces_mine[p][z, :, src : src + width]
                other = pieces_other[p][z, :, src : src + width]
                w_ref[pl.ds(row, 16), dest : dest + width] = jnp.where(is_first, mine, other)
                w_ref[pl.ds(row, 16), dest + width : dest + 2 * width] = jnp.where(
                    is_first, other, mine
                )


def disperse(g_ref, place_ref, keep_ref, send_ref, halves):
    me, core = place_ref[0], place_ref[1]
    is_first = core == 0
    for p in range(4):
        for z in range(4):
            row = pl.multiple_of((me ^ (4 * z + p)) * 16, 16)
            for src, width, dest in halves:
                low = g_ref[pl.ds(row, 16), dest : dest + width]
                high = g_ref[pl.ds(row, 16), dest + width : dest + 2 * width]
                keep_ref[p, z, :, src : src + width] = jnp.where(is_first, low, high)
                send_ref[p, z, :, src : src + width] = jnp.where(is_first, high, low).astype(BF16)


def make_hits(meta):
    lane = lax.broadcasted_iota(jnp.int32, (SEQ, 640), 1)
    place = lax.broadcasted_iota(jnp.int32, (SEQ, ROWS), 0) + (VOCAB + ACTIONS + GAMES)
    place_hit = place == lax.broadcasted_iota(jnp.int32, (SEQ, ROWS), 1)
    hit = (lane == meta[:, 0:1]) | (lane == meta[:, 1:2]) | place_hit[:, :640]
    one, zero = jnp.ones((), F32), jnp.zeros((), F32)
    return jnp.concatenate(
        [jnp.where(hit, one, zero).astype(BF16), jnp.where(place_hit[:, 640:], one, zero).astype(BF16)],
        axis=1,
    )


def layer_forward(x, w_ref, vec, bias, kept):
    x_ref, qkv_ref, p_refs, o_ref, m_ref, h_ref, gp_ref = kept
    normed16 = (normalise(x)[0] * vec[0:1] + vec[1:2]).astype(BF16)
    qkv_ref[0:SEQ] = dot_nn(normed16, w_ref[:, COL_QKV : COL_QKV + 768]).astype(BF16)
    qkv_ref[SEQ:KEYS] = jnp.zeros((KEYS - SEQ, 768), BF16)
    values = head_masks(qkv_ref[:, 512:768])
    for (first, count, seen), p_ref in zip(QBLOCKS, p_refs):
        queries = jnp.concatenate(head_masks(qkv_ref[first : first + count, 0:256], 0.125), axis=0)
        scores = dot_nt(queries, qkv_ref[0:seen, 256:512]).reshape(HEADS, count, seen)
        row = lax.broadcasted_iota(jnp.int32, (count, seen), 0) + first
        causal = row >= lax.broadcasted_iota(jnp.int32, (count, seen), 1)
        scores = jnp.where(causal[None], scores, -1e30)
        expanded = jnp.exp(scores - jnp.max(scores, axis=2, keepdims=True))
        probs = expanded * (1.0 / jnp.sum(expanded, axis=2, keepdims=True))
        probs16 = probs.astype(BF16)
        p_ref[...] = probs16.reshape(HEADS * count, seen)
        out = dot_nn(
            jnp.concatenate([probs16[h] for h in range(HEADS)], axis=1),
            jnp.concatenate([values[h][0:seen] for h in range(HEADS)], axis=0),
        )
        o_ref[first : first + count] = out.astype(BF16)
    middle = x + (dot_nt(o_ref[...], w_ref[:, COL_PROJ : COL_PROJ + 256]) + vec[2:3])
    m_ref[...] = middle
    normed16 = (normalise(middle)[0] * vec[3:4] + vec[4:5]).astype(BF16)
    total = middle + vec[5:6]
    for chunk in range(4):
        cols = slice(256 * chunk, 256 * chunk + 256)
        up = dot_nn(normed16, w_ref[:, COL_UP + 256 * chunk : COL_UP + 256 * chunk + 256])
        up = up + bias[:, cols]
        square = up * up
        slope = 0.7978845608028654 + 0.1070322244089 * square
        bent = jnp.tanh(up * (0.7978845608028654 + 0.0356774081363 * square))
        half = 0.5 + 0.5 * bent
        hidden = up * half
        gp_ref[:, cols] = (half + hidden * (1.0 - bent) * slope).astype(BF16)
        hidden16 = hidden.astype(BF16)
        h_ref[:, cols] = hidden16
        total = total + dot_nt(
            hidden16, w_ref[:, COL_DOWN + 256 * chunk : COL_DOWN + 256 * chunk + 256]
        )
    return total


def ff_backward(grad_in, w_ref, vec, kept, g_ref, g_up, g_down, v_ref, v_row, bias_row):
    m_ref, h_ref, gp_ref = kept
    grad_out16 = grad_in.astype(BF16)
    v_ref[v_row + 5 : v_row + 6] += column_sum(grad_out16.astype(F32))
    xhat, scale = normalise(m_ref[...])
    normed16 = (xhat * vec[3:4] + vec[4:5]).astype(BF16)
    grad_normed = None
    for chunk in range(4):
        start = 256 * chunk
        cols = slice(start, start + 256)
        grad_hidden = dot_nn(grad_out16, w_ref[:, COL_DOWN + start : COL_DOWN + start + 256])
        grad_up16 = (grad_hidden * gp_ref[:, cols].astype(F32)).astype(BF16)
        g_ref[:, g_down + start : g_down + start + 256] += dot_tn(grad_out16, h_ref[:, cols])
        g_ref[:, g_up + start : g_up + start + 256] += dot_tn(normed16, grad_up16)
        v_ref[bias_row + chunk : bias_row + chunk + 1] += column_sum(grad_up16.astype(F32))
        part = dot_nt(grad_up16, w_ref[:, COL_UP + start : COL_UP + start + 256])
        grad_normed = part if grad_normed is None else grad_normed + part
    v_ref[v_row + 3 : v_row + 4] += column_sum(grad_normed * xhat)
    v_ref[v_row + 4 : v_row + 5] += column_sum(grad_normed)
    return grad_in + normalise_back(grad_normed, xhat, scale, vec[3:4])


def attention_backward(grad_mid, w_ref, vec, kept, g_ref, v_ref, v_row, dkv_ref):
    x_ref, qkv_ref, p_refs, o_ref = kept
    grad_att16 = grad_mid.astype(BF16)
    v_ref[v_row + 2 : v_row + 3] += column_sum(grad_att16.astype(F32))
    g_ref[:, COL_PROJ : COL_PROJ + 256] += dot_tn(grad_att16, o_ref[...])
    grad_heads = dot_nn(grad_att16, w_ref[:, COL_PROJ : COL_PROJ + 256]).astype(BF16)
    keys = head_masks(qkv_ref[:, 256:512], 0.125)
    dkv_ref[...] = jnp.zeros(dkv_ref.shape, F32)
    grad_query = []
    for (first, count, seen), p_ref in zip(QBLOCKS, p_refs):
        rows = slice(first, first + count)
        queries = jnp.concatenate(head_masks(qkv_ref[rows, 0:256], 0.125), axis=0)
        grads = jnp.concatenate(head_masks(grad_heads[rows]), axis=0)
        grad_probs = dot_nt(grads, qkv_ref[0:seen, 512:768])
        probs16 = p_ref[...]
        probs = probs16.astype(F32)
        inner = jnp.sum(probs * grad_probs, axis=1, keepdims=True)
        grad_scores = (probs * (grad_probs - inner)).astype(BF16)
        grad_query.append(
            dot_nn(
                jnp.concatenate(
                    [grad_scores[h * count : (h + 1) * count] for h in range(HEADS)], axis=1
                ),
                jnp.concatenate([keys[h][0:seen] for h in range(HEADS)], axis=0),
            ).astype(BF16)
        )
        dkv_ref[0:seen, 0:256] += dot_tn(grad_scores, queries)
        dkv_ref[0:seen, 256:512] += dot_tn(probs16, grads)
    grad_qkv = jnp.concatenate(
        [jnp.concatenate(grad_query, axis=0), dkv_ref[0:SEQ].astype(BF16)], axis=1
    )
    xhat, scale = normalise(x_ref[...])
    normed16 = (xhat * vec[0:1] + vec[1:2]).astype(BF16)
    g_ref[:, COL_QKV : COL_QKV + 768] += dot_tn(normed16, grad_qkv)
    grad_normed = dot_nt(grad_qkv, w_ref[:, COL_QKV : COL_QKV + 768])
    v_ref[v_row : v_row + 1] += column_sum(grad_normed * xhat)
    v_ref[v_row + 1 : v_row + 2] += column_sum(grad_normed)
    return grad_mid + normalise_back(grad_normed, xhat, scale, vec[0:1])


def own_bias(place_ref, mine, other):
    is_first = place_ref[1] == 0
    return jnp.concatenate(
        [jnp.where(is_first, mine, other), jnp.where(is_first, other, mine)], axis=1
    )


def prepare_kernel(place_ref, games_ref, tokens, actions, valid, rewards, ends, after, out, x_ref):
    count = out.shape[0]
    frames = tokens.shape[2]
    base = place_ref[1] * count
    row = lax.broadcasted_iota(jnp.int32, (SEQ, frames), 0)
    start = lax.broadcasted_iota(jnp.int32, (SEQ, frames), 1) * FRAME_TOKENS
    here = jnp.where((row >= start) & (row < start + FRAME_TOKENS), 1.0, 0.0).astype(BF16)
    coming = jnp.where((row >= start - FRAME_TOKENS) & (row < start), 1.0, 0.0).astype(BF16)
    passed = jnp.sum(jnp.where(row >= start + FRAME_TOKENS, 1, 0), axis=1, keepdims=True)
    place = lax.broadcasted_iota(jnp.int32, (SEQ, 1), 0)
    spot = place - passed * FRAME_TOKENS
    lane = lax.broadcasted_iota(jnp.int32, (SEQ, 24), 1)
    wide_lane = lax.broadcasted_iota(jnp.int32, (SEQ, 128), 1)
    inside = place < LENGTH
    x_ref[...] = jnp.zeros(x_ref.shape, jnp.int32)
    for s in range(count):
        x_ref[0:OBS] = tokens[base + s]
        x_ref[16:17] = actions[pl.ds(base + s, 1)] + VOCAB
        x_ref[17:18] = valid[pl.ds(base + s, 1)]
        x_ref[18:19] = rewards[pl.ds(base + s, 1)]
        x_ref[19:20] = ends[pl.ds(base + s, 1)] + 3
        high = (x_ref[...] >> 4).astype(F32).astype(BF16)
        low = (x_ref[...] & 15).astype(F32).astype(BF16)
        now = dot_nt(here, high) * 16.0 + dot_nt(here, low)
        soon = dot_nt(coming, high) * 16.0 + dot_nt(coming, low)

        def pick(condition, a):
            return jnp.sum(jnp.where(condition, a, 0.0), axis=1, keepdims=True).astype(jnp.int32)

        ids = jnp.where(inside, pick(lane == spot, now), -1)
        game = jnp.where(inside, games_ref[base + s] + (VOCAB + ACTIONS), -1)
        target = pick((lane == spot + 1) & (spot < 15), now)
        target = target + pick((lane == 0) & (spot == 16), soon)
        weight = pick((lane == 17) & (spot < 15), now) + pick((lane == 17) & (spot == 16), soon)
        side = pick((lane == 17) & (spot == 16), now)
        reward, end = pick(lane == 18, now), pick(lane == 19, now)
        result = jnp.zeros((SEQ, 128), jnp.int32)
        for c, column in enumerate((ids, game, target, weight, side, reward, end)):
            result = jnp.where(wide_lane == c, column, result)
        out[s] = result


def first_forward_kernel(*refs):
    place_ref, meta_ref, vec_ref, bias_ref, bias_other = refs[0:5]
    mine, other = refs[5:9], refs[9:13]
    w_out, side_out, next_ref = refs[14:17]
    x_ref, qkv_ref, p0, p1, p2, o_ref, m_ref, h_ref, gp_ref = refs[17:26]
    w_ref = refs[26]

    @pl.when(pl.program_id(0) == 0)
    def _():
        assemble(mine, other, place_ref, w_ref, HALF_FIRST)
        w_out[...] = w_ref[...]
        side_out[...] = w_ref[:, COL_SMALL:]

    x = dot_nt(make_hits(meta_ref[0]), w_ref[:, COL_TABLE : COL_TABLE + ROWS])
    x_ref[0] = x
    kept = (
        x_ref.at[0],
        qkv_ref.at[0],
        (p0.at[0], p1.at[0], p2.at[0]),
        o_ref.at[0],
        m_ref.at[0],
        h_ref.at[0],
        gp_ref.at[0],
    )
    bias = own_bias(place_ref, bias_ref[0:1], bias_other[0:1])
    next_ref[0] = layer_forward(x, w_ref, vec_ref[0:6], bias, kept)


def middle_kernel(*refs):
    place_ref, meta_ref, vec_ref, bias_ref, bias_other, side_ref, in_ref = refs[0:7]
    mine, other = refs[7:11], refs[11:15]
    grad_ref, keep_ref, send_ref, v_out, scalar_ref = refs[15:20]
    w_ref, g_ref, v_ref, dkv_ref = refs[20:24]
    qkv_ref, p0, p1, p2, o_ref, m_ref, h_ref, gp_ref = refs[24:32]
    step = pl.program_id(0)

    @pl.when(step == 0)
    def _():
        assemble(mine, other, place_ref, w_ref, HALF_SECOND)
        w_ref[:, COL_SECOND:] = side_ref[...]
        g_ref[...] = jnp.zeros(g_ref.shape, F32)
        v_ref[...] = jnp.zeros(v_ref.shape, F32)
        scalar_ref[...] = jnp.zeros(scalar_ref.shape, F32)

    x_ref = in_ref.at[0]
    kept = (x_ref, qkv_ref, (p0, p1, p2), o_ref, m_ref, h_ref, gp_ref)
    bias = own_bias(place_ref, bias_ref[1:2], bias_other[1:2])
    last = layer_forward(x_ref[...], w_ref, vec_ref[6:12], bias, kept)

    meta = meta_ref[0]
    xhat, scale = normalise(last)
    gain = vec_ref[12:13]
    final16 = (xhat * gain + vec_ref[13:14]).astype(BF16)
    both = dot_nn(final16, w_ref[:, COL_HEAD : COL_HEAD + VOCAB + 128])
    logits, side = both[:, :VOCAB], both[:, VOCAB:]
    weight = meta[:, 3:4].astype(F32)
    peak = jnp.max(logits, axis=1, keepdims=True)
    expanded = jnp.exp(logits - peak)
    total = jnp.sum(expanded, axis=1, keepdims=True)
    hit = lax.broadcasted_iota(jnp.int32, (SEQ, VOCAB), 1) == meta[:, 2:3]
    picked = jnp.sum(jnp.where(hit, logits, 0.0), axis=1, keepdims=True)
    loss = column_sum(weight * (peak + jnp.log(total) - picked))
    grad_logits = expanded * (weight / total) - jnp.where(hit, weight, 0.0)

    lane = lax.broadcasted_iota(jnp.int32, (SEQ, 128), 1)
    is_reward, is_end = lane < 3, (lane == 3) | (lane == 4)
    side_weight = meta[:, 4:5].astype(F32)
    reward_peak = jnp.max(jnp.where(is_reward, side, -1e30), axis=1, keepdims=True)
    end_peak = jnp.max(jnp.where(is_end, side, -1e30), axis=1, keepdims=True)
    side_peak = jnp.where(is_reward, reward_peak, end_peak)
    is_side = is_reward | is_end
    expanded = jnp.where(is_side, jnp.exp(jnp.where(is_side, side - side_peak, 0.0)), 0.0)
    reward_total = jnp.sum(jnp.where(is_reward, expanded, 0.0), axis=1, keepdims=True)
    end_total = jnp.sum(jnp.where(is_end, expanded, 0.0), axis=1, keepdims=True)
    side_hit = (lane == meta[:, 5:6]) | (lane == meta[:, 6:7])
    side_picked = jnp.sum(jnp.where(side_hit, side, 0.0), axis=1, keepdims=True)
    side_terms = reward_peak + jnp.log(reward_total) + end_peak + jnp.log(end_total) - side_picked
    loss = loss + column_sum(side_weight * side_terms)
    grad_side = expanded * jnp.where(is_reward, side_weight / reward_total, side_weight / end_total)
    grad_side = grad_side - jnp.where(side_hit, side_weight, 0.0)
    valid = column_sum(side_weight)
    scalar_lane = lax.broadcasted_iota(jnp.int32, (8, 128), 1)
    scalar_row = lax.broadcasted_iota(jnp.int32, (8, 128), 0) == 0
    scalar_ref[...] += jnp.where(scalar_row & (scalar_lane == 0), loss, 0.0)
    scalar_ref[...] += jnp.where(scalar_row & (scalar_lane == 1), valid, 0.0)

    grad_both = jnp.concatenate([grad_logits.astype(BF16), grad_side.astype(BF16)], axis=1)
    g_ref[:, COL_HEAD : COL_HEAD + VOCAB + 128] += dot_tn(final16, grad_both)
    grad_final = dot_nt(grad_both, w_ref[:, COL_HEAD : COL_HEAD + VOCAB + 128])
    v_ref[12:13] += column_sum(grad_final * xhat)
    v_ref[13:14] += column_sum(grad_final)
    grad_last = normalise_back(grad_final, xhat, scale, gain)
    vec = vec_ref[6:12]
    grad_mid = ff_backward(
        grad_last,
        w_ref,
        vec,
        (m_ref, h_ref, gp_ref),
        g_ref,
        COL_UP,
        COL_DOWN,
        v_ref,
        6,
        SMALL_BIAS + 4,
    )
    grad_ref[0] = attention_backward(
        grad_mid, w_ref, vec, (x_ref, qkv_ref, (p0, p1, p2), o_ref), g_ref, v_ref, 6, dkv_ref
    )

    @pl.when(step == pl.num_programs(0) - 1)
    def _():
        disperse(g_ref, place_ref, keep_ref, send_ref, HALF_SECOND)
        v_ref[SMALL_SIDE : SMALL_SIDE + 5] = jnp.transpose(g_ref[:, COL_SECOND:])[0:5]
        v_out[...] = v_ref[...]


def ff_backward_kernel(*refs):
    place_ref, vec_ref, w_ref, grad_ref, v_in, m_ref, h_ref, gp_ref = refs[0:8]
    mid_ref, keep_ref, send_ref, v_out = refs[8:12]
    g_ref, v_ref = refs[12:14]
    step = pl.program_id(0)

    @pl.when(step == 0)
    def _():
        g_ref[...] = jnp.zeros(g_ref.shape, F32)
        v_ref[...] = v_in[...]

    mid_ref[0] = ff_backward(
        grad_ref[0],
        w_ref,
        vec_ref[0:6],
        (m_ref.at[0], h_ref.at[0], gp_ref.at[0]),
        g_ref,
        GRAD_UP,
        GRAD_DOWN,
        v_ref,
        0,
        SMALL_BIAS,
    )

    @pl.when(step == pl.num_programs(0) - 1)
    def _():
        disperse(g_ref, place_ref, keep_ref, send_ref, HALF_GRAD_FF)
        v_out[...] = v_ref[...]


def attention_backward_kernel(*refs):
    place_ref, meta_ref, vec_ref, w_ref, mid_ref, v_in = refs[0:6]
    x_ref, qkv_ref, p0, p1, p2, o_ref = refs[6:12]
    keep_ref, send_ref, v_out = refs[13:16]
    g_ref, v_ref, dkv_ref = refs[16:19]
    step = pl.program_id(0)

    @pl.when(step == 0)
    def _():
        g_ref[...] = jnp.zeros(g_ref.shape, F32)
        v_ref[...] = v_in[...]

    kept = (x_ref.at[0], qkv_ref.at[0], (p0.at[0], p1.at[0], p2.at[0]), o_ref.at[0])
    grad_x = attention_backward(
        mid_ref[0], w_ref, vec_ref[0:6], kept, g_ref, v_ref, 0, dkv_ref
    )
    g_ref[:, GRAD_TABLE : GRAD_TABLE + ROWS] += dot_tn(grad_x.astype(BF16), make_hits(meta_ref[0]))

    @pl.when(step == pl.num_programs(0) - 1)
    def _():
        for block in range(16):
            quarter = slice(8 * (block // 4), 8 * (block // 4) + 8)
            g_ref[16 * block : 16 * block + 8, GRAD_SMALL:] = v_ref[quarter, 0:128]
            g_ref[16 * block + 8 : 16 * block + 16, GRAD_SMALL:] = v_ref[quarter, 128:256]
        disperse(g_ref, place_ref, keep_ref, send_ref, HALF_GRAD_REST)
        v_out[...] = v_ref[...]


def pack_layer(attn, proj, up, down, layer, out):
    for j in range(3):
        out[:, 128 * j : 128 * j + 128] = attn[layer, j].astype(BF16)
    out[:, 384:512] = proj[layer].astype(BF16)
    out[:, 512:1024] = up[layer].astype(BF16)
    out[:, 1024:1536] = down[layer].astype(BF16)


def pack_first_kernel(place_ref, table, attn, proj, up, down, side, out, pad_ref):
    pack_layer(attn, proj, up, down, 0, out)
    rows = side.shape[1]
    eye = (
        lax.broadcasted_iota(jnp.int32, (rows, rows), 0)
        == lax.broadcasted_iota(jnp.int32, (rows, rows), 1)
    )
    eye = jnp.where(eye, 1.0, 0.0).astype(BF16)
    pad_ref[...] = jnp.zeros(pad_ref.shape, F32)
    pad_ref[:, 0:5] = dot_nt(eye, side[...].astype(BF16))
    high = jnp.concatenate([table[:, 512:896], pad_ref[...]], axis=1)
    out[:, 1536:2048] = jnp.where(place_ref[1] == 0, table[:, 0:512], high).astype(BF16)


def pack_second_kernel(attn, proj, up, down, head, after, out):
    pack_layer(attn, proj, up, down, 1, out)
    out[:, 1536:1792] = head[...].astype(BF16)


def finish_kernel(*refs):
    count = (len(refs) - 5) // 2
    place_ref = refs[0]
    scalar_ref = refs[2 * count + 1]
    out_rest, out_other, message = refs[2 * count + 2 :]
    square = jnp.zeros((1, 1), F32)
    for pieces, out in ((refs[1 : count + 1], out_rest), (refs[count + 1 : 2 * count + 1], out_other)):
        total = pieces[0][...]
        for piece in pieces[1:]:
            total = total + piece[...].astype(F32)
        out[...] = total
        square = square + column_sum(jnp.sum(total * total, axis=1, keepdims=True))
    small = out_rest[:, 896:1024]
    extra = column_sum(jnp.sum(small * small, axis=1, keepdims=True))
    square = square - jnp.where(place_ref[1] == 0, 0.0, extra)
    rows = message.shape[0]
    message[:, 0:512] = out_rest[:, 512:1024]
    lane = lax.broadcasted_iota(jnp.int32, (rows, 128), 1)
    top = lax.broadcasted_iota(jnp.int32, (rows, 128), 0) == 0
    scalars = scalar_ref[0:1] + jnp.where(lane == 2, square, 0.0)
    message[:, 512:640] = jnp.where(top, scalars, 0.0)


def adam_rule(weight, moment, second, gradient, step_rate, decay_rate):
    moment_new = BETA_ONE * moment + (1.0 - BETA_ONE) * gradient
    second_new = BETA_TWO * second + (1.0 - BETA_TWO) * gradient * gradient
    moment_hat = moment_new / (1.0 - BETA_ONE**STEP_NUMBER)
    second_hat = second_new / (1.0 - BETA_TWO**STEP_NUMBER)
    weight_new = weight - step_rate * (
        moment_hat / (jnp.sqrt(second_hat) + EPS_ADAM) + decay_rate * weight
    )
    return (weight_new, moment_new, second_new)


def adam_kernel(*refs):
    place_ref, rest, others, swapped, near, far = refs[0:6]
    params = [refs[6 + 3 * i : 9 + 3 * i] for i in range(9)]
    loss_ref, valid_ref, norm_ref = refs[33:36]
    outs = [refs[36 + 3 * i : 39 + 3 * i] for i in range(9)]
    small_ref = refs[63]
    me, wide = place_ref[0], place_ref[2]
    is_first = place_ref[1] == 0
    rows = rest.shape[0]
    for k in range(4):
        source, at = ((near, 0), (near, 16), (far, 0), (far, 16))[k]
        row = pl.multiple_of(((me >> 2) ^ k) * 8, 8)
        small_ref[pl.ds(row, 8), 0:128] = source[at : at + 8]
        small_ref[pl.ds(row, 8), 128:256] = source[at + 8 : at + 16]
    scalars = near[32:33] + far[32:33]
    small = small_ref[...]
    loss, valid, square = scalars[:, 0:1], scalars[:, 1:2], scalars[:, 2:3]
    square = square + column_sum(jnp.sum(small * small, axis=1, keepdims=True))
    inverse = 1.0 / valid
    norm = jnp.sqrt(square) * inverse
    loss_ref[...], valid_ref[...], norm_ref[...] = loss, valid, norm
    factor = jnp.minimum(1.0, CLIP_AT / (norm + 1e-06)) * inverse
    table, attn, proj, up, bias, down, vectors, head, side = range(9)

    def update(which, index, gradient, step_rate, decay_rate):
        news = adam_rule(
            *(ref[index] for ref in params[which]), factor * gradient, step_rate, decay_rate
        )
        for ref, new in zip(outs[which], news):
            ref[index] = new

    layers = ((rest, others, 1792), (others, others, 512))
    for layer, (attention, feed, at) in enumerate(layers):
        for j in range(3):
            update(attn, (layer, j), attention[:, 128 * j : 128 * j + 128], RATE_MATRIX, DECAY_RATE)
        update(proj, (layer,), attention[:, 384:512], RATE_MATRIX, DECAY_RATE)
        update(up, (layer,), feed[:, at : at + 512], RATE_MATRIX, DECAY_RATE)
        update(down, (layer,), feed[:, at + 512 : at + 1024], RATE_MATRIX, DECAY_RATE)
        for i in range(2):
            low = SMALL_BIAS + 4 * layer + i
            row = jnp.where(is_first, small[low : low + 1], small[low + 2 : low + 3])
            index = (slice(layer, layer + 1), slice(256 * i, 256 * i + 256))
            update(bias, index, row, RATE_VECTOR, 0.0)
    whole = (slice(None), slice(None))
    update(head, whole, others[:, 1536:1792], RATE_MATRIX, DECAY_RATE)
    mine, theirs = rest[:, 512:1024], swapped[:, 0:512]
    low, high = jnp.where(is_first, mine, theirs), jnp.where(is_first, theirs, mine)
    update(table, (slice(None), slice(0, 512)), low, RATE_TABLE, DECAY_RATE)
    update(table, (slice(None), slice(512, 896)), high[:, 0:384], RATE_TABLE, DECAY_RATE)
    update(vectors, whole, small[0:NVEC], RATE_VECTOR, 0.0)
    turned = pltpu.roll(small[SMALL_SIDE : SMALL_SIDE + 8], lax.rem(D - wide * rows, D), 1)
    update(side, whole, turned[0:5, 0:rows], RATE_MATRIX, DECAY_RATE)


def swap(a, axis, distance):
    size = lax.axis_size(axis)
    return lax.ppermute(a, axis, [(i, i ^ distance) for i in range(size)])


def gather_column(piece, n_high):
    return jnp.stack([piece] + [swap(piece, "wide", 4 * k) for k in range(1, n_high)])


def gather_plane(column):
    return [column] + [swap(column, "wide", p) for p in range(1, 4)]


def gather_cores(mine):
    return [swap(a, "narrow", 1) for a in mine]


def in_blocks(parts, wide):
    n_high, rows, cols = parts[0].shape
    if rows == 16:
        return parts
    whole = jnp.stack(parts, axis=1).reshape(4 * n_high, rows, cols)
    whole = whole[wide ^ jnp.arange(4 * n_high)].reshape(4, 4, 16, cols)
    return [whole[:, p] for p in range(4)]


def in_pieces(blocks, wide, n_high):
    cols = blocks.shape[-1]
    if n_high == 4:
        return blocks
    rows = 64 // n_high
    whole = blocks.transpose(1, 0, 2, 3).reshape(4 * n_high, rows, cols)
    whole = whole[wide ^ jnp.arange(4 * n_high)]
    return whole.reshape(n_high, 4, rows, cols).transpose(1, 0, 2, 3)


def add_cores(keep, send, wide, n_high):
    keep, send = in_pieces(keep, wide, n_high), in_pieces(send, wide, n_high)
    received = swap(send, "narrow", 1)
    return [keep[p] + received[p].astype(F32) for p in range(4)]


def swap_plane(sums):
    return [swap(sums[p].astype(BF16), "wide", p) for p in range(1, 4)]


def add_plane(own, received):
    for a in received:
        own = own + a.astype(F32)
    return own


def column_pieces(own):
    return [own[0]] + [swap(own[k].astype(BF16), "wide", 4 * k) for k in range(1, own.shape[0])]


def full_spec(a):
    return pl.BlockSpec(a.shape, lambda *_: (0,) * len(a.shape))


def row_spec(shape):
    return pl.BlockSpec((1,) + shape, lambda i: (i,) + (0,) * len(shape))


def shaped(shape, dtype):
    return jax.ShapeDtypeStruct(shape, dtype)


VMEM_SPEC = pl.BlockSpec(memory_space=pltpu.VMEM)
ANY_SPEC = pl.BlockSpec(memory_space=pl.ANY)
SMEM_SPEC = pl.BlockSpec(memory_space=pltpu.SMEM)


def call(kernel, grid, in_specs, out_specs, out_shape, scratch, flops, bytes_accessed, name):
    extra = {"grid": grid} if grid else {}
    return pl.pallas_call(
        kernel,
        in_specs=in_specs,
        out_specs=out_specs,
        out_shape=out_shape,
        scratch_shapes=scratch,
        compiler_params=pltpu.CompilerParams(vmem_limit_bytes=VMEM_BYTES),
        cost_estimate=pl.CostEstimate(
            flops=flops, bytes_accessed=bytes_accessed, transcendentals=0
        ),
        name=name,
        **extra,
    )


KEPT = (
    ((SEQ, D), F32),
    ((KEYS, 768), BF16),
    ((HEADS * 128, 128), BF16),
    ((HEADS * 128, 256), BF16),
    ((HEADS * 96, 384), BF16),
    ((SEQ, D), BF16),
    ((SEQ, D), F32),
    ((SEQ, FF), BF16),
    ((SEQ, FF), BF16),
)


def per_device(
    tokens,
    actions,
    game_ids,
    valid_steps,
    rewards,
    end_flags,
    embed_table,
    table_first,
    table_second,
    attn_weight,
    attn_first,
    attn_second,
    proj_weight,
    proj_first,
    proj_second,
    up_weight,
    up_first,
    up_second,
    up_bias,
    bias_first,
    bias_second,
    down_weight,
    down_first,
    down_second,
    vectors,
    vectors_first,
    vectors_second,
    head_weight,
    head_first,
    head_second,
    side_weight,
    side_first,
    side_second,
):
    n_high = lax.axis_size("wide") // 4
    wide, core = lax.axis_index("wide"), lax.axis_index("narrow")
    rows = side_weight.shape[0]
    fast = rows == 16
    place = jnp.stack([wide if fast else jnp.zeros_like(wide), core, wide]).astype(jnp.int32)

    def flat(a):
        return jnp.swapaxes(a, -1, -2)

    params = (
        (flat(embed_table), flat(table_first), flat(table_second)),
        (attn_weight, attn_first, attn_second),
        (flat(proj_weight), flat(proj_first), flat(proj_second)),
        (up_weight, up_first, up_second),
        (up_bias, bias_first, bias_second),
        (flat(down_weight), flat(down_first), flat(down_second)),
        (vectors, vectors_first, vectors_second),
        (head_weight, head_first, head_second),
        (flat(side_weight), flat(side_first), flat(side_second)),
    )
    table, attn, proj, up, _, down, _, head, side = (group[0] for group in params)

    piece_first = call(
        pack_first_kernel,
        None,
        [SMEM_SPEC] + [VMEM_SPEC] * 6,
        VMEM_SPEC,
        shaped((rows, HALF_FIRST_COLS), BF16),
        [pltpu.VMEM((rows, 128), F32)],
        10**6,
        10**6,
        "pack_first",
    )(place, table, attn, proj, up, down, side)
    first_mine = gather_plane(gather_column(piece_first, n_high))
    first_other = gather_cores(first_mine)
    piece_second = call(
        pack_second_kernel,
        None,
        [VMEM_SPEC] * 5 + [ANY_SPEC],
        VMEM_SPEC,
        shaped((rows, HALF_SECOND_COLS), BF16),
        [],
        10**6,
        10**6,
        "pack_second",
    )(attn, proj, up, down, head, first_mine[1])
    second_column = gather_column(piece_second, n_high)
    second_mine = gather_plane(second_column)
    first_parts = in_blocks(first_mine, wide) + in_blocks(first_other, wide)
    other_bias = swap(up_bias, "narrow", 1)

    count = tokens.shape[0] // lax.axis_size("narrow")
    meta = call(
        prepare_kernel,
        None,
        [SMEM_SPEC] * 2 + [VMEM_SPEC] * 5 + [ANY_SPEC],
        VMEM_SPEC,
        shaped((count, SEQ, 128), jnp.int32),
        [pltpu.VMEM((24, FRAMES), jnp.int32)],
        10**6,
        10**6,
        "prepare",
    )(place, game_ids, flat(tokens), actions, valid_steps, rewards, end_flags, first_mine[1])

    kept_specs = [row_spec(shape) for shape, _ in KEPT]
    kept_shapes = [shaped((count,) + shape, dtype) for shape, dtype in KEPT]
    row_f32 = shaped((count, SEQ, D), F32)
    meta_spec = row_spec((SEQ, 128))
    vec_specs = [full_spec(vectors), full_spec(up_bias), full_spec(up_bias)]
    w_spec = pl.BlockSpec((D, COL_FIRST), lambda i: (0, 0))
    side_spec = pl.BlockSpec((D, 128), lambda i: (0, 0))
    results = call(
        first_forward_kernel,
        (count,),
        [SMEM_SPEC, meta_spec] + vec_specs + [full_spec(a) for a in first_parts] + [ANY_SPEC],
        [w_spec, side_spec, row_spec((SEQ, D))] + kept_specs,
        [shaped((D, COL_FIRST), BF16), shaped((D, 128), BF16), row_f32] + kept_shapes,
        [pltpu.VMEM((D, COL_FIRST), BF16)],
        4 * 10**9,
        20 * 10**6,
        "first_forward",
    )(place, meta, vectors, up_bias, other_bias, *first_parts, second_column)
    w_first, side_copy, stream = results[0:3]
    kept = results[3:]
    received, side_copy = lax.optimization_barrier((second_mine[1:], side_copy))
    second_mine = second_mine[0:1] + received
    second_other = gather_cores(second_mine)
    second_parts = in_blocks(second_mine, wide) + in_blocks(second_other, wide)

    def blocks(cols):
        return pl.BlockSpec((4, 4, 16, cols), lambda i: (0, 0, 0, 0))

    def block_shapes(cols):
        return [shaped((4, 4, 16, cols), F32), shaped((4, 4, 16, cols), BF16)]

    small_spec = pl.BlockSpec((SMALL_ROWS, D), lambda i: (0, 0))
    small_shape = shaped((SMALL_ROWS, D), F32)
    scalar_spec = pl.BlockSpec((8, 128), lambda i: (0, 0))
    grad_stream, keep_second, send_second, small_grads, scalars = call(
        middle_kernel,
        (count,),
        [SMEM_SPEC, meta_spec]
        + vec_specs
        + [side_spec, row_spec((SEQ, D))]
        + [full_spec(a) for a in second_parts],
        [row_spec((SEQ, D))] + [blocks(HALF_SECOND_COLS)] * 2 + [small_spec, scalar_spec],
        [row_f32] + block_shapes(HALF_SECOND_COLS) + [small_shape, shaped((8, 128), F32)],
        [
            pltpu.VMEM((D, COL_SECOND + 128), BF16),
            pltpu.VMEM((D, COL_SECOND + 128), F32),
            pltpu.VMEM((SMALL_ROWS, D), F32),
            pltpu.VMEM((KEYS, 512), F32),
        ]
        + [pltpu.VMEM(shape, dtype) for shape, dtype in KEPT[1:]],
        15 * 10**9,
        20 * 10**6,
        "middle",
    )(place, meta, vectors, up_bias, other_bias, side_copy, stream, *second_parts)
    second_sums = add_cores(keep_second, send_second, wide, n_high)

    grad_mid, keep_ff, send_ff, small_grads = call(
        ff_backward_kernel,
        (count,),
        [SMEM_SPEC, full_spec(vectors), w_spec, row_spec((SEQ, D)), small_spec] + kept_specs[6:9],
        [row_spec((SEQ, D))] + [blocks(HALF_GRAD_COLS)] * 2 + [small_spec],
        [row_f32] + block_shapes(HALF_GRAD_COLS) + [small_shape],
        [pltpu.VMEM((D, 2048), F32), pltpu.VMEM((SMALL_ROWS, D), F32)],
        4 * 10**9,
        10 * 10**6,
        "ff_backward",
    )(place, vectors, w_first, grad_stream, small_grads, *kept[6:9])
    ff_sums = add_cores(keep_ff, send_ff, wide, n_high)
    other_sums = [jnp.concatenate(pair, axis=-1) for pair in zip(second_sums, ff_sums)]
    others_received = swap_plane(other_sums)

    keep_rest, send_rest, small_grads = call(
        attention_backward_kernel,
        (count,),
        [SMEM_SPEC, meta_spec, full_spec(vectors), w_spec, row_spec((SEQ, D)), small_spec]
        + kept_specs[0:6]
        + [ANY_SPEC],
        [blocks(HALF_GRAD_COLS)] * 2 + [small_spec],
        block_shapes(HALF_GRAD_COLS) + [small_shape],
        [
            pltpu.VMEM((D, 2048), F32),
            pltpu.VMEM((SMALL_ROWS, D), F32),
            pltpu.VMEM((KEYS, 512), F32),
        ],
        6 * 10**9,
        20 * 10**6,
        "attention_backward",
    )(place, meta, vectors, w_first, grad_mid, small_grads, *kept[0:6], other_sums[0])
    others_received, keep_rest = lax.optimization_barrier((others_received, keep_rest))
    rest_sums = add_cores(keep_rest, send_rest, wide, n_high)
    rest_received = swap_plane(rest_sums)
    other_pieces = column_pieces(add_plane(other_sums[0], others_received))
    rest_pieces = column_pieces(add_plane(rest_sums[0], rest_received))

    grad_rest, grad_others, message = call(
        finish_kernel,
        None,
        [SMEM_SPEC] + [VMEM_SPEC] * (2 * n_high + 1),
        [VMEM_SPEC] * 3,
        [
            shaped((rows, HALF_GRAD_COLS), F32),
            shaped((rows, HALF_GRAD_COLS + HALF_SECOND_COLS), F32),
            shaped((rows, 640), F32),
        ],
        [],
        10**6,
        10**6,
        "finish",
    )(place, *rest_pieces, *other_pieces, scalars)

    swapped = swap(message, "narrow", 1)
    if fast:
        sums = message[0:8, 512:640] + swapped[0:8, 512:640]
        quarter = jnp.where(core == 1, message[:, 384:512], swapped[:, 384:512])
        for distance in (1, 2):
            beside = swap(jnp.concatenate([quarter, sums]), "wide", distance)
            quarter = jnp.where(wide & distance == 0, quarter, beside[0:16])
            sums = sums + beside[16:24]
        beside = swap(jnp.concatenate([quarter, sums]), "wide", 4)
        near = jnp.concatenate([quarter, beside[0:16], sums + beside[16:24]])
        far = swap(near, "wide", 8)
    else:
        sums = lax.psum(message[:, 512:640], ("wide", "narrow"))
        total = lax.psum(small_grads, ("wide", "narrow"))
        total = total.reshape(4, 8, 2, 128).transpose(0, 2, 1, 3).reshape(4, 16, 128)
        ends = jnp.pad(sums, ((0, 8 - rows), (0, 0)))
        near = jnp.concatenate([total[0], total[1], ends])
        far = jnp.concatenate([total[2], total[3], jnp.zeros_like(ends)])

    flat_params = [a for group in params for a in group]
    results = call(
        adam_kernel,
        None,
        [SMEM_SPEC] + [VMEM_SPEC] * 32,
        [VMEM_SPEC] * 30,
        [shaped((1, 1), F32)] * 3 + [shaped(a.shape, F32) for a in flat_params],
        [pltpu.VMEM((SMALL_ROWS, D), F32)],
        10**6,
        10**6,
        "adam",
    )(place, grad_rest, grad_others, swapped, near, far, *flat_params)
    news = list(results[3:])
    for group in (0, 2, 5, 8):
        for member in range(3 * group, 3 * group + 3):
            news[member] = flat(news[member])
    return tuple(a.reshape(()) for a in results[0:3]) + tuple(news)


def solution(mesh):
    placed = (
        P("wide", None, None),
        P("wide", None),
        P("wide"),
        P("wide", None),
        P("wide", None),
        P("wide", None),
        P(None, "wide"),
        P(None, "wide"),
        P(None, "wide"),
        P(None, None, "wide", "narrow"),
        P(None, None, "wide", "narrow"),
        P(None, None, "wide", "narrow"),
        P(None, "narrow", "wide"),
        P(None, "narrow", "wide"),
        P(None, "narrow", "wide"),
        P(None, "wide", "narrow"),
        P(None, "wide", "narrow"),
        P(None, "wide", "narrow"),
        P(None, "narrow"),
        P(None, "narrow"),
        P(None, "narrow"),
        P(None, "narrow", "wide"),
        P(None, "narrow", "wide"),
        P(None, "narrow", "wide"),
        P(),
        P(),
        P(),
        P("wide", "narrow"),
        P("wide", "narrow"),
        P("wide", "narrow"),
        P("wide", None),
        P("wide", None),
        P("wide", None),
    )
    return jax.shard_map(
        per_device,
        mesh=mesh,
        in_specs=placed,
        out_specs=(P(), P(), P()) + placed[6:],
        check_vma=False,
    )
```

time: 216 us -> 187 us (0.87)
  local copies, waits for them, and re-layouts: 43 us -> 5.32 us
  waiting for transfers between devices: 24.4 us -> 37 us
  starting transfers between devices: 48 us -> 39.3 us
  Pallas kernels: 93.1 us -> 96.4 us
    unnamed x123 -> x58, local copies, waits for them, and re-layouts: 29 us -> 3.97 us
    ppermute x42 -> x41, waiting for transfers between devices: 24.4 us -> 37 us  [swap(): return lax.ppermute(a, axis, [(i, i ^ distance) for i in range(size)])]
    another operation x9 -> x0, local copies, waits for them, and re-layouts: 10.2 us -> none  [make_meta(): jnp.stack(columns + [jnp.zeros_like(ids)], axis=-1)]
    ppermute x42 -> x41, starting transfers between devices: 48 us -> 39.3 us  [swap(): return lax.ppermute(a, axis, [(i, i ^ distance) for i in range(size)])]
    pallas_call x6 -> x9, Pallas kernels: 93.1 us -> 96.4 us  [the longest x1 39.1 us: per_device(): call(middle_kernel, (count,), [SMEM_SPEC, meta_spec] + vec_specs + [side_...]
  transfers between devices with their start and end apart: 42 -> 41, of which waited for: 11 -> 18; matrix products, arithmetic and copies ran while one was open for 12% -> 3% of each run, Pallas kernels for 21% -> 27%
where the time goes in v2:
time: 187 us; the launch traced here: 186 us
  Pallas kernels  96.4 us (52%)
  starting transfers between devices  39.3 us (21%)
  waiting for transfers between devices  37 us (20%)
  other arithmetic  6.65 us (4%)
  local copies, waits for them, and re-layouts  5.32 us (3%)
    ppermute x41, starting transfers between devices, swap(): return lax.ppermute(a, axis, [(i, i ^ distance) for i in range(size)])  39.3 us
    pallas_call x1, Pallas kernels, per_device(): call(middle_kernel, (count,), [SMEM_SPEC, meta_spec] + vec_specs + [side_...  39.1 us
    ppermute x41, waiting for transfers between devices, swap(): return lax.ppermute(a, axis, [(i, i ^ distance) for i in range(size)])  37 us
    pallas_call x1, Pallas kernels, per_device(): call(first_forward_kernel, (count,), [SMEM_SPEC, meta_spec] + vec_specs +...  18.8 us
    pallas_call x1, Pallas kernels, per_device(): call(attention_backward_kernel, (count,), [SMEM_SPEC, meta_spec, full_spe...  16.8 us
    pallas_call x1, Pallas kernels, per_device(): call(ff_backward_kernel, (count,), [SMEM_SPEC, full_spec(vectors), w_spec...  10.2 us
    unnamed x58, local copies, waits for them, and re-layouts  3.97 us
    pallas_call x1, Pallas kernels, per_device(): call(prepare_kernel, None, [SMEM_SPEC] * 2 + [VMEM_SPEC] * 5 + [ANY_SPEC]...  3.8 us
  transfers between devices with their start and end apart: 41, of which 18 were waited for; matrix products, arithmetic and copies ran while one was open for 3% of the time, Pallas kernels for 27%

profile of v2, /device:TPU:0, one launch (start us, length us, event | category | flops | bytes accessed | tf_op | source)
XLA Modules:
  0.0 186.0 jit_solution(6865797227664889704)
XLA Ops:
  1.3 1.7 pack_first.1
  3.0 5.0 %collective-permute-start.2 = (bf16[16,2048]{1,0:T(8,128)(2,1)}, bf16[16,2048]{1,0:T(8,128)(2,1)S(1)}, u32[]{:S(2)}, u32[]{:S(2)}) collective-permute-start(bf16[16,2048]{1,0:T(8,128)(2,1)} %pack_first.1), channel_id=1, source_target_pairs={{0,24},{2,26},{4,28},{6,30},{8,16},{10,18},{12,20},{14,22},{16,8},... | collective-permute-start | bytes 196616 | tf_op jit(solution)/shard_map/ppermute | solution.py:584
  8.6 2.5 %collective-permute-done.2 = bf16[16,2048]{1,0:T(8,128)(2,1)S(1)} collective-permute-done((bf16[16,2048]{1,0:T(8,128)(2,1)}, bf16[16,2048]{1,0:T(8,128)(2,1)S(1)}, u32[]{:S(2)}, u32[]{:S(2)}) %collective-permute-start.2) | collective-permute-done | bytes 65568 | tf_op jit(solution)/shard_map/ppermute | solution.py:584
  11.1 1.8 collective-permute-done
  12.9 1.0 collective-permute-done.1
  13.9 0.9 pad_maximum_fusion.4.refs_5_
  14.8 1.6 collective-permute-start.3
  16.3 1.5 collective-permute-start.11
  18.3 5.8 %collective-permute-done.3.after.refs_6_ = bf16[4,16,2048]{2,1,0:T(8,128)(2,1)S(1)} collective-permute-done((bf16[4,16,2048]{2,1,0:T(8,128)(2,1)S(1)}, bf16[4,16,2048]{2,1,0:T(8,128)(2,1)S(1)}, u32[]{:S(2)}, u32[]{:S(2)}) %collective-permute-start.3) | collective-permute-done | bytes 262176 | tf_op jit(solution)/shard_map/ppermute | solution.py:584
  24.1 0.7 copy-done.1
  24.8 1.5 pack_second.1
  26.3 1.5 collective-permute-start.5
  27.8 1.2 collective-permute-start.6
  29.0 1.7 collective-permute-start.7
  31.3 2.4 %collective-permute-done.6 = bf16[16,1792]{1,0:T(8,128)(2,1)S(1)} collective-permute-done((bf16[16,1792]{1,0:T(8,128)(2,1)}, bf16[16,1792]{1,0:T(8,128)(2,1)S(1)}, u32[]{:S(2)}, u32[]{:S(2)}) %collective-permute-start.6) | collective-permute-done | bytes 57376 | tf_op jit(solution)/shard_map/ppermute | solution.py:584
  33.7 3.8 %prepare.1.refs_1_ = s32[4,352,128]{2,1,0:T(8,128)} custom-call(s32[3]{0:T(128)} %pad_add_fusion.place_ref.refs_0_, s32[8]{0:T(128)} %games_ref.1, s32[8,16,20]{2,1,0:T(8,128)} %bitcast.93, s32[8,20]{1,0:T(8,128)} %actions.1, s32[8,20]{1,0:T(8,128)} %valid.1, s32[8,20]{1,0:T(8,128)} %rewards.1, s32[8,20]{1,0:T(8,128)} %ends.1, bf16[4,16,2048]{2,1,0:T(8,128)(2,1)} %copy-done.1), custom_call_target="tpu_custom_call" | custom-call | flops 1000000 | bytes 1000000 | tf_op jit(solution)/shard_map/prepare/pallas_call | solution.py:772
  38.1 0.8 pad_maximum_fusion.5.refs_13_.refs_7_
  39.0 2.5 %collective-permute-start.10 = (bf16[4,16,1792]{2,1,0:T(8,128)(2,1)S(1)}, bf16[4,16,1792]{2,1,0:T(8,128)(2,1)S(1)}, u32[]{:S(2)}, u32[]{:S(2)}) collective-permute-start(bf16[4,16,1792]{2,1,0:T(8,128)(2,1)S(1)} %pad_maximum_fusion.5.refs_13_.refs_7_), channel_id=1, source_target_pairs={{0,6},{2,4},{4,2},{6,0},{8,14},{10,12},{12,10},{14,8},{16,22},{18,... | collective-permute-start | bytes 688136 | tf_op jit(solution)/shard_map/ppermute | solution.py:584
  43.2 0.7 copy-done.20
  43.9 18.8 %first_forward.1 = (bf16[256,4096]{1,0:T(8,128)(2,1)}, bf16[256,128]{1,0:T(8,128)(2,1)}, f32[4,352,256]{2,1,0:T(8,128)}, f32[4,352,256]{2,1,0:T(8,128)}, bf16[4,...) custom-call(s32[3]{0:T(128)} %pad_add_fusion.place_ref.refs_0_, ...), custom_call_target="tpu_custom_call" | custom-call | flops 4000000000 | bytes 20000000 | tf_op jit(solution)/shard_map/first_forward/pallas_call | solution.py:791
  63.4 0.9 collective-permute-done.18.refs_12_
  65.7 39.1 %middle.1 = (f32[4,352,256]{2,1,0:T(8,128)}, f32[4,4,16,1792]{3,2,1,0:T(8,128)}, bf16[4,4,16,1792]{3,2,1,0:T(8,128)(2,1)}, f32[32,256]{1,0:T(8,128)}, f32[8,128]{1,0:T(8,128)}) custom-call(s32[3]{0:T(128)} %pad_add_fusion.place_ref.refs_0_, s32[4,352,128]{2,1,0:T(8,128)} %prepare.1.refs_1_, f32[14,256]{1,0:T(8,128)} %refs_24_.1, f32[2,512]{1,0:T(2,128)} %refs_18_.1, ...), custom_call_target="tpu_custom_call" | custom-call | flops 15000000512 | bytes 20000000 | tf_op jit(solution)/shard_map/middle/pallas_call | solution.py:818
  105.1 10.2 %ff_backward.1 = (f32[4,352,256]{2,1,0:T(8,128)}, f32[4,4,16,1024]{3,2,1,0:T(8,128)}, bf16[4,4,16,1024]{3,2,1,0:T(8,128)(2,1)}, f32[32,256]{1,0:T(8,128)}) custom-call(s32[3]{0:T(128)} %pad_add_fusion.place_ref.refs_0_, f32[14,256]{1,0:T(8,128)} %refs_24_.1, bf16[256,4096]{1,0:T(8,128)(2,1)} %get-tuple-element.102.refs_2_.refs_3_, ...), custom_call_target="tpu_custom_call" | custom-call | flops 4000000000 | bytes 10000000 | tf_op jit(solution)/shard_map/ff_backward/pallas_call | solution.py:840
  115.7 1.8 collective-permute-done.22
  117.5 1.3 add_bitcast_fusion.1
  119.1 2.5 %collective-permute-start.25 = (bf16[4,16,2816]{2,1,0:T(8,128)(2,1)S(1)}, bf16[4,16,2816]{2,1,0:T(8,128)(2,1)S(1)}, u32[]{:S(2)}, u32[]{:S(2)}) collective-permute-start(bf16[4,16,2816]{2,1,0:T(8,128)(2,1)S(1)} %pad_maximum_fusion.3), channel_id=1, source_target_pairs={{0,6},{2,4},{4,2},{6,0},{8,14},{10,12},{12,10},{14,8},{16,22},{18,... | collective-permute-start | bytes 1081352 | tf_op jit(solution)/shard_map/ppermute | solution.py:584
  122.8 0.9 pad_maximum_fusion.refs_12_
  123.7 16.8 %attention_backward.1 = (f32[4,4,16,1024]{3,2,1,0:T(8,128)}, bf16[4,4,16,1024]{3,2,1,0:T(8,128)(2,1)}, f32[32,256]{1,0:T(8,128)}) custom-call(s32[3]{0:T(128)} %pad_add_fusion.place_ref.refs_0_, s32[4,352,128]{2,1,0:T(8,128)} %prepare.1.refs_1_, f32[14,256]{1,0:T(8,128)} %refs_24_.1, bf16[256,4096]{1,0:T(8,128)(2,1)} %get-tuple-element.102.refs_2_.refs_3_, ...), custom_call_target="tpu_custom_call" | custom-call | flops 6000000000 | bytes 20000000 | tf_op jit(solution)/shard_map/attention_backward/pallas_call | solution.py:855
  140.9 2.5 %collective-permute-start.34 = (bf16[16,2816]{1,0:T(8,128)(2,1)S(1)}, bf16[16,2816]{1,0:T(8,128)(2,1)S(1)}, u32[]{:S(2)}, u32[]{:S(2)}) collective-permute-start(bf16[16,2816]{1,0:T(8,128)(2,1)S(1)} %get-tuple-element.174), channel_id=1, source_target_pairs={{0,16},{2,18},{4,20},{6,22},{8,24},{10,26},{12,28},{14,30},{16,0},... | collective-permute-start | bytes 270344 | tf_op jit(solution)/shard_map/ppermute | solution.py:584
  143.5 1.6 collective-permute-start.27
  145.1 1.5 collective-permute-start.28
  147.7 1.5 collective-permute-done.27
  149.2 2.0 %collective-permute-start.35 = (bf16[16,2816]{1,0:T(8,128)(2,1)S(1)}, bf16[16,2816]{1,0:T(8,128)(2,1)S(1)}, u32[]{:S(2)}, u32[]{:S(2)}) collective-permute-start(bf16[16,2816]{1,0:T(8,128)(2,1)S(1)} %get-tuple-element.173), channel_id=1, source_target_pairs={{0,24},{2,26},{4,28},{6,30},{8,16},{10,18},{12,20},{14,22},{16,8},... | collective-permute-start | bytes 270344 | tf_op jit(solution)/shard_map/ppermute | solution.py:584
  151.2 1.8 collective-permute-done.28
  153.5 2.1 %collective-permute-start.31 = (bf16[16,1024]{1,0:T(8,128)(2,1)S(1)}, bf16[16,1024]{1,0:T(8,128)(2,1)S(1)}, u32[]{:S(2)}, u32[]{:S(2)}) collective-permute-start(bf16[16,1024]{1,0:T(8,128)(2,1)S(1)} %get-tuple-element.177), channel_id=1, source_target_pairs={{0,16},{2,18},{4,20},{6,22},{8,24},{10,26},{12,28},{14,30},{16,0},... | collective-permute-start | bytes 98312 | tf_op jit(solution)/shard_map/ppermute | solution.py:584
  155.6 2.0 %collective-permute-start.32 = (bf16[16,1024]{1,0:T(8,128)(2,1)S(1)}, bf16[16,1024]{1,0:T(8,128)(2,1)S(1)}, u32[]{:S(2)}, u32[]{:S(2)}) collective-permute-start(bf16[16,1024]{1,0:T(8,128)(2,1)S(1)} %get-tuple-element.176), channel_id=1, source_target_pairs={{0,24},{2,26},{4,28},{6,30},{8,16},{10,18},{12,20},{14,22},{16,8},... | collective-permute-start | bytes 98312 | tf_op jit(solution)/shard_map/ppermute | solution.py:584
  158.7 2.6 %collective-permute-done.32.refs_4_ = bf16[16,1024]{1,0:T(8,128)(2,1)S(1)} collective-permute-done((bf16[16,1024]{1,0:T(8,128)(2,1)S(1)}, bf16[16,1024]{1,0:T(8,128)(2,1)S(1)}, u32[]{:S(2)}, u32[]{:S(2)}) %collective-permute-start.32) | collective-permute-done | bytes 32800 | tf_op jit(solution)/shard_map/ppermute | solution.py:584
  161.9 1.9 %finish.1 = (f32[16,1024]{1,0:T(8,128)}, f32[16,2816]{1,0:T(8,128)}, f32[16,640]{1,0:T(8,128)}) custom-call(s32[3]{0:T(128)} %pad_add_fusion.place_ref.refs_0_, f32[16,1024]{1,0:T(8,128)} %slice_bitcast_fusion.4.refs_1_, bf16[16,1024]{1,0:T(8,128)(2,1)} %copy-done.10, bf16[16,1024]{1,0:T(8,128)(2,1)} %copy-done.11, bf16[16,1024]{1,0:T(8,128)(2,1)} %copy-done.12, ...), custom_call_target="tpu_custom_call" | custom-call | flops 1000000 | bytes 1000000 | tf_op jit(solution)/shard_map/finish/pallas_call | solution.py:878
  163.9 1.4 collective-permute-done.36.refs_3_
  165.3 0.7 slice_add_fusion.3
  166.0 0.7 slice_select_fusion.2
  166.7 1.2 collective-permute-start.37
  167.9 2.5 %collective-permute-done.37 = f32[24,128]{1,0:T(8,128)S(1)} collective-permute-done((f32[24,128]{1,0:T(8,128)S(1)}, f32[24,128]{1,0:T(8,128)S(1)}, u32[]{:S(2)}, u32[]{:S(2)}) %collective-permute-start.37) | collective-permute-done | bytes 12320 | tf_op jit(solution)/shard_map/ppermute | solution.py:584
  170.4 1.6 collective-permute-start.38
  172.0 2.2 %collective-permute-done.38 = f32[24,128]{1,0:T(8,128)S(1)} collective-permute-done((f32[24,128]{1,0:T(8,128)S(1)}, f32[24,128]{1,0:T(8,128)S(1)}, u32[]{:S(2)}, u32[]{:S(2)}) %collective-permute-start.38) | collective-permute-done | bytes 12320 | tf_op jit(solution)/shard_map/ppermute | solution.py:584
  174.3 3.7 %collective-permute-done.39 = f32[24,128]{1,0:T(8,128)S(1)} collective-permute-done((f32[24,128]{1,0:T(8,128)S(1)}, f32[24,128]{1,0:T(8,128)S(1)}, u32[]{:S(2)}, u32[]{:S(2)}) %collective-permute-start.39) | collective-permute-done | bytes 12320 | tf_op jit(solution)/shard_map/ppermute | solution.py:584
  178.5 4.2 %collective-permute-done.40.refs_5_ = f32[40,128]{1,0:T(8,128)S(1)} collective-permute-done((f32[40,128]{1,0:T(8,128)S(1)}, f32[40,128]{1,0:T(8,128)S(1)}, u32[]{:S(2)}, u32[]{:S(2)}) %collective-permute-start.40) | collective-permute-done | bytes 20512 | tf_op jit(solution)/shard_map/ppermute | solution.py:584
  183.3 2.5 %adam.1 = (f32[1,1]{1,0:T(1,128)}, f32[1,1]{1,0:T(1,128)}, f32[1,1]{1,0:T(1,128)}, f32[16,896]{1,0:T(8,128)}, f32[16,896]{1,0:T(8,128)}, /*index=5*/f32[16,896]{...) custom-call(s32[3]{0:T(128)} %pad_add_fusion.place_ref.refs_0_, ...), custom_call_target="tpu_custom_call" | custom-call | flops 1000000 | bytes 1000000 | tf_op jit(solution)/shard_map/adam/pallas_call | solution.py:914
  (129 shorter events, 13.7 us)
Async XLA Ops:
  0.7 36.8 %copy-start.14 = (f32[2,512]{1,0:T(2,128)S(1)}, f32[2,512]{1,0:T(2,128)}, u32[]{:S(2)}) copy-start(f32[2,512]{1,0:T(2,128)} %refs_18_.1) | copy-start | bytes 12292
  3.0 8.2 %collective-permute-start.2 = (bf16[16,2048]{1,0:T(8,128)(2,1)}, bf16[16,2048]{1,0:T(8,128)(2,1)S(1)}, u32[]{:S(2)}, u32[]{:S(2)}) collective-permute-start(bf16[16,2048]{1,0:T(8,128)(2,1)} %pack_first.1), channel_id=1, source_target_pairs={{0,24},{2,26},{4,28},{6,30},{8,16},{10,18},{12,20},{14,22},{16,8},... | collective-permute-start | bytes 196616 | tf_op jit(solution)/shard_map/ppermute | solution.py:584
  8.0 4.9 %collective-permute-start = (bf16[16,2048]{1,0:T(8,128)(2,1)}, bf16[16,2048]{1,0:T(8,128)(2,1)S(1)}, u32[]{:S(2)}, u32[]{:S(2)}) collective-permute-start(bf16[16,2048]{1,0:T(8,128)(2,1)} %pack_first.1), channel_id=1, source_target_pairs={{0,8},{2,10},{4,12},{6,14},{8,0},{10,2},{12,4},{14,6},{16,24},{18,... | collective-permute-start | bytes 196616 | tf_op jit(solution)/shard_map/ppermute | solution.py:584
  8.0 5.8 %collective-permute-start.1 = (bf16[16,2048]{1,0:T(8,128)(2,1)}, bf16[16,2048]{1,0:T(8,128)(2,1)S(1)}, u32[]{:S(2)}, u32[]{:S(2)}) collective-permute-start(bf16[16,2048]{1,0:T(8,128)(2,1)} %pack_first.1), channel_id=1, source_target_pairs={{0,16},{2,18},{4,20},{6,22},{8,24},{10,26},{12,28},{14,30},{16,0},... | collective-permute-start | bytes 196616 | tf_op jit(solution)/shard_map/ppermute | solution.py:584
  14.8 27.8 %copy-start.3 = (bf16[4,16,2048]{2,1,0:T(8,128)(2,1)}, bf16[4,16,2048]{2,1,0:T(8,128)(2,1)S(1)}, u32[]{:S(2)}) copy-start(bf16[4,16,2048]{2,1,0:T(8,128)(2,1)S(1)} %pad_maximum_fusion.4.refs_5_) | copy-start | bytes 786436
  14.8 9.3 %collective-permute-start.3 = (bf16[4,16,2048]{2,1,0:T(8,128)(2,1)S(1)}, bf16[4,16,2048]{2,1,0:T(8,128)(2,1)S(1)}, u32[]{:S(2)}, u32[]{:S(2)}) collective-permute-start(bf16[4,16,2048]{2,1,0:T(8,128)(2,1)S(1)} %pad_maximum_fusion.4.refs_5_), channel_id=1, source_target_pairs={{0,2},{2,0},{4,6},{6,4},{8,10},{10,8},{12,14},{14,12},{16,18},{18,... | collective-permute-start | bytes 786440 | tf_op jit(solution)/shard_map/ppermute | solution.py:584
  16.3 14.4 %collective-permute-start.11 = (bf16[4,16,2048]{2,1,0:T(8,128)(2,1)S(1)}, bf16[4,16,2048]{2,1,0:T(8,128)(2,1)S(1)}, u32[]{:S(2)}, u32[]{:S(2)}) collective-permute-start(bf16[4,16,2048]{2,1,0:T(8,128)(2,1)S(1)} %pad_maximum_fusion.4.refs_5_), channel_id=1, source_target_pairs={{0,4},{2,6},{4,0},{6,2},{8,12},{10,14},{12,8},{14,10},{16,20},{18,... | collective-permute-start | bytes 786440 | tf_op jit(solution)/shard_map/ppermute | solution.py:584
  17.9 12.9 %collective-permute-start.12 = (bf16[4,16,2048]{2,1,0:T(8,128)(2,1)S(1)}, bf16[4,16,2048]{2,1,0:T(8,128)(2,1)S(1)}, u32[]{:S(2)}, u32[]{:S(2)}) collective-permute-start(bf16[4,16,2048]{2,1,0:T(8,128)(2,1)S(1)} %pad_maximum_fusion.4.refs_5_), channel_id=1, source_target_pairs={{0,6},{2,4},{4,2},{6,0},{8,14},{10,12},{12,10},{14,8},{16,22},{18,... | collective-permute-start | bytes 786440 | tf_op jit(solution)/shard_map/ppermute | solution.py:584
  26.3 4.9 %collective-permute-start.5 = (bf16[16,1792]{1,0:T(8,128)(2,1)}, bf16[16,1792]{1,0:T(8,128)(2,1)S(1)}, u32[]{:S(2)}, u32[]{:S(2)}) collective-permute-start(bf16[16,1792]{1,0:T(8,128)(2,1)} %pack_second.1), channel_id=1, source_target_pairs={{0,8},{2,10},{4,12},{6,14},{8,0},{10,2},{12,4},{14,6},{16,24},{18,... | collective-permute-start | bytes 172040 | tf_op jit(solution)/shard_map/ppermute | solution.py:584
  27.8 5.9 %collective-permute-start.6 = (bf16[16,1792]{1,0:T(8,128)(2,1)}, bf16[16,1792]{1,0:T(8,128)(2,1)S(1)}, u32[]{:S(2)}, u32[]{:S(2)}) collective-permute-start(bf16[16,1792]{1,0:T(8,128)(2,1)} %pack_second.1), channel_id=1, source_target_pairs={{0,16},{2,18},{4,20},{6,22},{8,24},{10,26},{12,28},{14,30},{16,0},... | collective-permute-start | bytes 172040 | tf_op jit(solution)/shard_map/ppermute | solution.py:584
  29.0 8.5 %collective-permute-start.7 = (bf16[16,1792]{1,0:T(8,128)(2,1)}, bf16[16,1792]{1,0:T(8,128)(2,1)S(1)}, u32[]{:S(2)}, u32[]{:S(2)}) collective-permute-start(bf16[16,1792]{1,0:T(8,128)(2,1)} %pack_second.1), channel_id=1, source_target_pairs={{0,24},{2,26},{4,28},{6,30},{8,16},{10,18},{12,20},{14,22},{16,8},... | collective-permute-start | bytes 172040 | tf_op jit(solution)/shard_map/ppermute | solution.py:584
  30.7 11.8 %copy-start.15 = (bf16[4,16,2048]{2,1,0:T(8,128)(2,1)}, bf16[4,16,2048]{2,1,0:T(8,128)(2,1)S(1)}, u32[]{:S(2)}) copy-start(bf16[4,16,2048]{2,1,0:T(8,128)(2,1)S(1)} %collective-permute-done.11.refs_7_) | copy-start | bytes 786436
  30.7 10.8 %collective-permute-start.13 = (bf16[4,16,2048]{2,1,0:T(8,128)(2,1)S(1)}, bf16[4,16,2048]{2,1,0:T(8,128)(2,1)S(1)}, u32[]{:S(2)}, u32[]{:S(2)}) collective-permute-start(bf16[4,16,2048]{2,1,0:T(8,128)(2,1)S(1)} %pad_maximum_fusion.4.refs_5_), channel_id=1, source_target_pairs={{0,1},{1,0},{2,3},{3,2},{4,5},{5,4},{6,7},{7,6},{8,9},{9,8},{10,11... | collective-permute-start | bytes 786440 | tf_op jit(solution)/shard_map/ppermute | solution.py:584
  30.7 11.8 %copy-start.16 = (bf16[4,16,2048]{2,1,0:T(8,128)(2,1)}, bf16[4,16,2048]{2,1,0:T(8,128)(2,1)S(1)}, u32[]{:S(2)}) copy-start(bf16[4,16,2048]{2,1,0:T(8,128)(2,1)S(1)} %collective-permute-done.12.refs_8_) | copy-start | bytes 786436
  30.7 11.3 %collective-permute-start.14 = (bf16[4,16,2048]{2,1,0:T(8,128)(2,1)}, bf16[4,16,2048]{2,1,0:T(8,128)(2,1)S(1)}, u32[]{:S(2)}, u32[]{:S(2)}) collective-permute-start(bf16[4,16,2048]{2,1,0:T(8,128)(2,1)} %copy-done.1), channel_id=1, source_target_pairs={{0,1},{1,0},{2,3},{3,2},{4,5},{5,4},{6,7},{7,6},{8,9},{9,8},{10,11... | collective-permute-start | bytes 786440 | tf_op jit(solution)/shard_map/ppermute | solution.py:584
  31.2 11.3 %collective-permute-start.15 = (bf16[4,16,2048]{2,1,0:T(8,128)(2,1)S(1)}, bf16[4,16,2048]{2,1,0:T(8,128)(2,1)S(1)}, u32[]{:S(2)}, u32[]{:S(2)}) collective-permute-start(bf16[4,16,2048]{2,1,0:T(8,128)(2,1)S(1)} %collective-permute-done.11.refs_7_), channel_id=1, source_target_pairs={{0,1},{1,0},{2,3},{3,2},{4,5},{5,4},{6,7},{7,6},{8,9},{9,8},{10,11... | collective-permute-start | bytes 786440 | tf_op jit(solution)/shard_map/ppermute | solution.py:584
  33.7 8.8 %collective-permute-start.16 = (bf16[4,16,2048]{2,1,0:T(8,128)(2,1)S(1)}, bf16[4,16,2048]{2,1,0:T(8,128)(2,1)S(1)}, u32[]{:S(2)}, u32[]{:S(2)}) collective-permute-start(bf16[4,16,2048]{2,1,0:T(8,128)(2,1)S(1)} %collective-permute-done.12.refs_8_), channel_id=1, source_target_pairs={{0,1},{1,0},{2,3},{3,2},{4,5},{5,4},{6,7},{7,6},{8,9},{9,8},{10,11... | collective-permute-start | bytes 786440 | tf_op jit(solution)/shard_map/ppermute | solution.py:584
  37.5 1.4 collective-permute-start.4
  39.0 23.8 %collective-permute-start.10 = (bf16[4,16,1792]{2,1,0:T(8,128)(2,1)S(1)}, bf16[4,16,1792]{2,1,0:T(8,128)(2,1)S(1)}, u32[]{:S(2)}, u32[]{:S(2)}) collective-permute-start(bf16[4,16,1792]{2,1,0:T(8,128)(2,1)S(1)} %pad_maximum_fusion.5.refs_13_.refs_7_), channel_id=1, source_target_pairs={{0,6},{2,4},{4,2},{6,0},{8,14},{10,12},{12,10},{14,8},{16,22},{18,... | collective-permute-start | bytes 688136 | tf_op jit(solution)/shard_map/ppermute | solution.py:584
  41.5 21.3 %collective-permute-start.8 = (bf16[4,16,1792]{2,1,0:T(8,128)(2,1)S(1)}, bf16[4,16,1792]{2,1,0:T(8,128)(2,1)S(1)}, u32[]{:S(2)}, u32[]{:S(2)}) collective-permute-start(bf16[4,16,1792]{2,1,0:T(8,128)(2,1)S(1)} %pad_maximum_fusion.5.refs_13_.refs_7_), channel_id=1, source_target_pairs={{0,2},{2,0},{4,6},{6,4},{8,10},{10,8},{12,14},{14,12},{16,18},{18,... | collective-permute-start | bytes 688136 | tf_op jit(solution)/shard_map/ppermute | solution.py:584
  42.0 20.7 %collective-permute-start.9 = (bf16[4,16,1792]{2,1,0:T(8,128)(2,1)S(1)}, bf16[4,16,1792]{2,1,0:T(8,128)(2,1)S(1)}, u32[]{:S(2)}, u32[]{:S(2)}) collective-permute-start(bf16[4,16,1792]{2,1,0:T(8,128)(2,1)S(1)} %pad_maximum_fusion.5.refs_13_.refs_7_), channel_id=1, source_target_pairs={{0,4},{2,6},{4,0},{6,2},{8,12},{10,14},{12,8},{14,10},{16,20},{18,... | collective-permute-start | bytes 688136 | tf_op jit(solution)/shard_map/ppermute | solution.py:584
  42.5 20.9 %collective-permute-start.17 = (bf16[4,16,1792]{2,1,0:T(8,128)(2,1)S(1)}, bf16[4,16,1792]{2,1,0:T(8,128)(2,1)S(1)}, u32[]{:S(2)}, u32[]{:S(2)}) collective-permute-start(bf16[4,16,1792]{2,1,0:T(8,128)(2,1)S(1)} %pad_maximum_fusion.5.refs_13_.refs_7_), channel_id=1, source_target_pairs={{0,1},{1,0},{2,3},{3,2},{4,5},{5,4},{6,7},{7,6},{8,9},{9,8},{10,11... | collective-permute-start | bytes 688136 | tf_op jit(solution)/shard_map/ppermute | solution.py:584
  62.8 1.6 collective-permute-start.18
  62.8 1.8 collective-permute-start.19
  63.3 1.6 collective-permute-start.20
  104.8 14.0 %collective-permute-start.21 = (bf16[4,4,16,1792]{3,2,1,0:T(8,128)(2,1)}, bf16[4,4,16,1792]{3,2,1,0:T(8,128)(2,1)S(1)}, u32[]{:S(2)}, u32[]{:S(2)}) collective-permute-start(bf16[4,4,16,1792]{3,2,1,0:T(8,128)(2,1)} %get-tuple-element.101), channel_id=1, source_target_pairs={{0,1},{1,0},{2,3},{3,2},{4,5},{5,4},{6,7},{7,6},{8,9},{9,8},{10,11... | collective-permute-start | bytes 2752520 | tf_op jit(solution)/shard_map/ppermute | solution.py:584
  115.3 2.2 %collective-permute-start.22 = (bf16[4,4,16,1024]{3,2,1,0:T(8,128)(2,1)}, bf16[4,4,16,1024]{3,2,1,0:T(8,128)(2,1)S(1)}, u32[]{:S(2)}, u32[]{:S(2)}) collective-permute-start(bf16[4,4,16,1024]{3,2,1,0:T(8,128)(2,1)} %get-tuple-element.109), channel_id=1, source_target_pairs={{0,1},{1,0},{2,3},{3,2},{4,5},{5,4},{6,7},{7,6},{8,9},{9,8},{10,11... | collective-permute-start | bytes 1572872 | tf_op jit(solution)/shard_map/ppermute | solution.py:584
  119.1 21.6 %collective-permute-start.25 = (bf16[4,16,2816]{2,1,0:T(8,128)(2,1)S(1)}, bf16[4,16,2816]{2,1,0:T(8,128)(2,1)S(1)}, u32[]{:S(2)}, u32[]{:S(2)}) collective-permute-start(bf16[4,16,2816]{2,1,0:T(8,128)(2,1)S(1)} %pad_maximum_fusion.3), channel_id=1, source_target_pairs={{0,6},{2,4},{4,2},{6,0},{8,14},{10,12},{12,10},{14,8},{16,22},{18,... | collective-permute-start | bytes 1081352 | tf_op jit(solution)/shard_map/ppermute | solution.py:584
  121.6 19.0 %collective-permute-start.24 = (bf16[4,16,2816]{2,1,0:T(8,128)(2,1)S(1)}, bf16[4,16,2816]{2,1,0:T(8,128)(2,1)S(1)}, u32[]{:S(2)}, u32[]{:S(2)}) collective-permute-start(bf16[4,16,2816]{2,1,0:T(8,128)(2,1)S(1)} %pad_maximum_fusion.2), channel_id=1, source_target_pairs={{0,4},{2,6},{4,0},{6,2},{8,12},{10,14},{12,8},{14,10},{16,20},{18,... | collective-permute-start | bytes 1081352 | tf_op jit(solution)/shard_map/ppermute | solution.py:584
  122.2 18.5 %collective-permute-start.23 = (bf16[4,16,2816]{2,1,0:T(8,128)(2,1)S(1)}, bf16[4,16,2816]{2,1,0:T(8,128)(2,1)S(1)}, u32[]{:S(2)}, u32[]{:S(2)}) collective-permute-start(bf16[4,16,2816]{2,1,0:T(8,128)(2,1)S(1)} %pad_maximum_fusion.1), channel_id=1, source_target_pairs={{0,2},{2,0},{4,6},{6,4},{8,10},{10,8},{12,14},{14,12},{16,18},{18,... | collective-permute-start | bytes 1081352 | tf_op jit(solution)/shard_map/ppermute | solution.py:584
  140.6 2.8 %collective-permute-start.26 = (bf16[4,4,16,1024]{3,2,1,0:T(8,128)(2,1)}, bf16[4,4,16,1024]{3,2,1,0:T(8,128)(2,1)S(1)}, u32[]{:S(2)}, u32[]{:S(2)}) collective-permute-start(bf16[4,4,16,1024]{3,2,1,0:T(8,128)(2,1)} %get-tuple-element.120), channel_id=1, source_target_pairs={{0,1},{1,0},{2,3},{3,2},{4,5},{5,4},{6,7},{7,6},{8,9},{9,8},{10,11... | collective-permute-start | bytes 1572872 | tf_op jit(solution)/shard_map/ppermute | solution.py:584
  140.9 14.7 %collective-permute-start.33 = (bf16[16,2816]{1,0:T(8,128)(2,1)S(1)}, bf16[16,2816]{1,0:T(8,128)(2,1)S(1)}, u32[]{:S(2)}, u32[]{:S(2)}) collective-permute-start(bf16[16,2816]{1,0:T(8,128)(2,1)S(1)} %get-tuple-element.175), channel_id=1, source_target_pairs={{0,8},{2,10},{4,12},{6,14},{8,0},{10,2},{12,4},{14,6},{16,24},{18,... | collective-permute-start | bytes 270344 | tf_op jit(solution)/shard_map/ppermute | solution.py:584
  140.9 17.2 %collective-permute-start.34 = (bf16[16,2816]{1,0:T(8,128)(2,1)S(1)}, bf16[16,2816]{1,0:T(8,128)(2,1)S(1)}, u32[]{:S(2)}, u32[]{:S(2)}) collective-permute-start(bf16[16,2816]{1,0:T(8,128)(2,1)S(1)} %get-tuple-element.174), channel_id=1, source_target_pairs={{0,16},{2,18},{4,20},{6,22},{8,24},{10,26},{12,28},{14,30},{16,0},... | collective-permute-start | bytes 270344 | tf_op jit(solution)/shard_map/ppermute | solution.py:584
  143.5 5.7 %collective-permute-start.27 = (bf16[4,16,1024]{2,1,0:T(8,128)(2,1)S(1)}, bf16[4,16,1024]{2,1,0:T(8,128)(2,1)S(1)}, u32[]{:S(2)}, u32[]{:S(2)}) collective-permute-start(bf16[4,16,1024]{2,1,0:T(8,128)(2,1)S(1)} %get-tuple-element.166), channel_id=1, source_target_pairs={{0,2},{2,0},{4,6},{6,4},{8,10},{10,8},{12,14},{14,12},{16,18},{18,... | collective-permute-start | bytes 393224 | tf_op jit(solution)/shard_map/ppermute | solution.py:584
  145.1 7.8 %collective-permute-start.28 = (bf16[4,16,1024]{2,1,0:T(8,128)(2,1)S(1)}, bf16[4,16,1024]{2,1,0:T(8,128)(2,1)S(1)}, u32[]{:S(2)}, u32[]{:S(2)}) collective-permute-start(bf16[4,16,1024]{2,1,0:T(8,128)(2,1)S(1)} %get-tuple-element.168), channel_id=1, source_target_pairs={{0,4},{2,6},{4,0},{6,2},{8,12},{10,14},{12,8},{14,10},{16,20},{18,... | collective-permute-start | bytes 393224 | tf_op jit(solution)/shard_map/ppermute | solution.py:584
  146.6 6.3 %collective-permute-start.29 = (bf16[4,16,1024]{2,1,0:T(8,128)(2,1)S(1)}, bf16[4,16,1024]{2,1,0:T(8,128)(2,1)S(1)}, u32[]{:S(2)}, u32[]{:S(2)}) collective-permute-start(bf16[4,16,1024]{2,1,0:T(8,128)(2,1)S(1)} %get-tuple-element.167), channel_id=1, source_target_pairs={{0,6},{2,4},{4,2},{6,0},{8,14},{10,12},{12,10},{14,8},{16,22},{18,... | collective-permute-start | bytes 393224 | tf_op jit(solution)/shard_map/ppermute | solution.py:584
  149.2 9.0 %collective-permute-start.35 = (bf16[16,2816]{1,0:T(8,128)(2,1)S(1)}, bf16[16,2816]{1,0:T(8,128)(2,1)S(1)}, u32[]{:S(2)}, u32[]{:S(2)}) collective-permute-start(bf16[16,2816]{1,0:T(8,128)(2,1)S(1)} %get-tuple-element.173), channel_id=1, source_target_pairs={{0,24},{2,26},{4,28},{6,30},{8,16},{10,18},{12,20},{14,22},{16,8},... | collective-permute-start | bytes 270344 | tf_op jit(solution)/shard_map/ppermute | solution.py:584
  153.1 5.1 %collective-permute-start.30 = (bf16[16,1024]{1,0:T(8,128)(2,1)S(1)}, bf16[16,1024]{1,0:T(8,128)(2,1)S(1)}, u32[]{:S(2)}, u32[]{:S(2)}) collective-permute-start(bf16[16,1024]{1,0:T(8,128)(2,1)S(1)} %get-tuple-element.178), channel_id=1, source_target_pairs={{0,8},{2,10},{4,12},{6,14},{8,0},{10,2},{12,4},{14,6},{16,24},{18,... | collective-permute-start | bytes 98312 | tf_op jit(solution)/shard_map/ppermute | solution.py:584
  153.5 5.2 %collective-permute-start.31 = (bf16[16,1024]{1,0:T(8,128)(2,1)S(1)}, bf16[16,1024]{1,0:T(8,128)(2,1)S(1)}, u32[]{:S(2)}, u32[]{:S(2)}) collective-permute-start(bf16[16,1024]{1,0:T(8,128)(2,1)S(1)} %get-tuple-element.177), channel_id=1, source_target_pairs={{0,16},{2,18},{4,20},{6,22},{8,24},{10,26},{12,28},{14,30},{16,0},... | collective-permute-start | bytes 98312 | tf_op jit(solution)/shard_map/ppermute | solution.py:584
  155.6 5.7 %copy-start.5 = (bf16[16,2816]{1,0:T(8,128)(2,1)}, bf16[16,2816]{1,0:T(8,128)(2,1)S(1)}, u32[]{:S(2)}) copy-start(bf16[16,2816]{1,0:T(8,128)(2,1)S(1)} %collective-permute-done.33.refs_6_) | copy-start | bytes 270340
  155.6 5.7 %collective-permute-start.32 = (bf16[16,1024]{1,0:T(8,128)(2,1)S(1)}, bf16[16,1024]{1,0:T(8,128)(2,1)S(1)}, u32[]{:S(2)}, u32[]{:S(2)}) collective-permute-start(bf16[16,1024]{1,0:T(8,128)(2,1)S(1)} %get-tuple-element.176), channel_id=1, source_target_pairs={{0,24},{2,26},{4,28},{6,30},{8,16},{10,18},{12,20},{14,22},{16,8},... | collective-permute-start | bytes 98312 | tf_op jit(solution)/shard_map/ppermute | solution.py:584
  163.9 1.4 collective-permute-start.36
  165.3 17.4 %copy-start.9 = (f32[16,640]{1,0:T(8,128)}, f32[16,640]{1,0:T(8,128)S(1)}, u32[]{:S(2)}) copy-start(f32[16,640]{1,0:T(8,128)S(1)} %collective-permute-done.36.refs_3_) | copy-start | bytes 122884
  166.7 3.7 %collective-permute-start.37 = (f32[24,128]{1,0:T(8,128)S(1)}, f32[24,128]{1,0:T(8,128)S(1)}, u32[]{:S(2)}, u32[]{:S(2)}) collective-permute-start(f32[24,128]{1,0:T(8,128)S(1)} %pad_maximum_fusion.7), channel_id=1, source_target_pairs={{0,2},{2,0},{4,6},{6,4},{8,10},{10,8},{12,14},{14,12},{16,18},{18,... | collective-permute-start | bytes 36872 | tf_op jit(solution)/shard_map/ppermute | solution.py:584
  170.4 3.8 %collective-permute-start.38 = (f32[24,128]{1,0:T(8,128)S(1)}, f32[24,128]{1,0:T(8,128)S(1)}, u32[]{:S(2)}, u32[]{:S(2)}) collective-permute-start(f32[24,128]{1,0:T(8,128)S(1)} %pad_maximum_fusion.8), channel_id=1, source_target_pairs={{0,4},{2,6},{4,0},{6,2},{8,12},{10,14},{12,8},{14,10},{16,20},{18,... | collective-permute-start | bytes 36872 | tf_op jit(solution)/shard_map/ppermute | solution.py:584
  174.2 3.8 %collective-permute-start.39 = (f32[24,128]{1,0:T(8,128)S(1)}, f32[24,128]{1,0:T(8,128)S(1)}, u32[]{:S(2)}, u32[]{:S(2)}) collective-permute-start(f32[24,128]{1,0:T(8,128)S(1)} %pad_maximum_fusion.9), channel_id=1, source_target_pairs={{0,8},{2,10},{4,12},{6,14},{8,0},{10,2},{12,4},{14,6},{16,24},{18,... | collective-permute-start | bytes 36872 | tf_op jit(solution)/shard_map/ppermute | solution.py:584
  178.0 4.8 %copy-start.8 = (f32[40,128]{1,0:T(8,128)}, f32[40,128]{1,0:T(8,128)S(1)}, u32[]{:S(2)}) copy-start(f32[40,128]{1,0:T(8,128)S(1)} %pad_maximum_fusion.6.refs_4_) | copy-start | bytes 61444
  178.0 4.7 %collective-permute-start.40 = (f32[40,128]{1,0:T(8,128)S(1)}, f32[40,128]{1,0:T(8,128)S(1)}, u32[]{:S(2)}, u32[]{:S(2)}) collective-permute-start(f32[40,128]{1,0:T(8,128)S(1)} %pad_maximum_fusion.6.refs_4_), channel_id=1, source_target_pairs={{0,16},{2,18},{4,20},{6,22},{8,24},{10,26},{12,28},{14,30},{16,0},... | collective-permute-start | bytes 61448 | tf_op jit(solution)/shard_map/ppermute | solution.py:584
  (22 other events, 41.3 us)

commit v3 on v2

v3 whole, which is shorter than its diff:
```python
import functools

import jax
import jax.numpy as jnp
from jax import lax
from jax.experimental import pallas as pl
from jax.experimental.pallas import tpu as pltpu
from jax.sharding import PartitionSpec as P

D = 256
HEADS = 4
HEAD_DIM = 64
FF = 1024
VOCAB = 512
ACTIONS = 18
GAMES = 26
OBS = 16
FRAMES = 20
STEP_NUMBER = 5
FRAME_TOKENS = 17
LENGTH = 340
ROWS = 896
NVEC = 14

EPS_NORM = 1e-05
BETA_ONE = 0.5
BETA_TWO = 0.5
RATE_TABLE = 0.5
RATE_MATRIX = 0.05
RATE_VECTOR = 0.2
DECAY_RATE = 0.01
EPS_ADAM = 1e-08
CLIP_AT = 0.1

SEQ = 352
KEYS = 384
QBLOCKS = ((0, 128, 128), (128, 128, 256), (256, 96, 384))

COL_QKV, COL_PROJ, COL_UP, COL_DOWN, COL_LAYER = 0, 768, 1024, 2048, 3072
HALF_ATTENTION = ((0, 128, 0), (128, 128, 256), (256, 128, 512), (384, 128, COL_PROJ))
HALF_LAYER = HALF_ATTENTION + ((512, 512, COL_UP), (1024, 512, COL_DOWN))
COL_TABLE, COL_SMALL, COL_FIRST = 3072, 3968, 4096
HALF_FIRST = HALF_LAYER + ((1536, 512, COL_TABLE),)
HALF_FIRST_COLS = 2048
COL_HEAD, COL_SECOND = 3072, 3584
HALF_SECOND = HALF_LAYER + ((1536, 256, COL_HEAD),)
HALF_SECOND_COLS = 1792
GRAD_UP, GRAD_DOWN = 0, 1024
HALF_GRAD_FF = ((0, 512, GRAD_UP), (512, 512, GRAD_DOWN))
GRAD_TABLE, GRAD_SMALL = 1024, 1920
HALF_GRAD_REST = HALF_ATTENTION + ((512, 512, GRAD_TABLE),)
HALF_GRAD_COLS = 1024
SMALL_ROWS, SMALL_BIAS, SMALL_SIDE = 32, 14, 22

F32, BF16 = jnp.float32, jnp.bfloat16
VMEM_BYTES = 60 * 1024 * 1024


def dot_nn(a, b):
    return lax.dot_general(a, b, (((1,), (0,)), ((), ())), preferred_element_type=F32)


def dot_nt(a, b):
    return lax.dot_general(a, b, (((1,), (1,)), ((), ())), preferred_element_type=F32)


def dot_tn(a, b):
    return lax.dot_general(a, b, (((0,), (0,)), ((), ())), preferred_element_type=F32)


def tiles(rows, size):
    return [slice(first, first + size) for first in range(0, rows, size)]


def normalise(x):
    centred = x - jnp.mean(x, axis=1, keepdims=True)
    scale = lax.rsqrt(jnp.mean(centred * centred, axis=1, keepdims=True) + EPS_NORM)
    return centred * scale, scale


def normalise_back(grad, xhat, scale, gain):
    inner = grad * gain
    mean_one = jnp.mean(inner, axis=1, keepdims=True)
    mean_two = jnp.mean(inner * xhat, axis=1, keepdims=True)
    return scale * (inner - mean_one - xhat * mean_two)


def column_sum(a):
    return jnp.sum(a, axis=0, keepdims=True)


def fold(a):
    return jnp.sum(a.reshape(a.shape[0] // 8, 8, a.shape[1]), axis=0)


def plus(total, a):
    return a if total is None else total + a


def split_heads(source_ref, column, row, count, target_ref, target_row):
    for h in range(HEADS):
        lanes = slice(h * HEAD_DIM, (h + 1) * HEAD_DIM)
        target_ref[target_row + h * count : target_row + (h + 1) * count, lanes] = source_ref[
            row : row + count, column + h * HEAD_DIM : column + (h + 1) * HEAD_DIM
        ]


def assemble(pieces_mine, pieces_other, place_ref, w_ref, halves):
    me, core = place_ref[0], place_ref[1]
    is_first = core == 0
    for p in range(4):
        for z in range(4):
            row = pl.multiple_of((me ^ (4 * z + p)) * 16, 16)
            for src, width, dest in halves:
                mine = pieces_mine[p][z, :, src : src + width]
                other = pieces_other[p][z, :, src : src + width]
                if dest == COL_QKV:
                    mine, other = mine * 0.125, other * 0.125
                w_ref[pl.ds(row, 16), dest : dest + width] = jnp.where(is_first, mine, other)
                w_ref[pl.ds(row, 16), dest + width : dest + 2 * width] = jnp.where(
                    is_first, other, mine
                )


def disperse(g_ref, place_ref, keep_ref, send_ref, halves, scaled=True):
    me, core = place_ref[0], place_ref[1]
    is_first = core == 0
    for p in range(4):
        for z in range(4):
            row = pl.multiple_of((me ^ (4 * z + p)) * 16, 16)
            for src, width, dest in halves:
                low = g_ref[pl.ds(row, 16), dest : dest + width]
                high = g_ref[pl.ds(row, 16), dest + width : dest + 2 * width]
                if scaled and dest == COL_QKV:
                    low, high = low * 0.125, high * 0.125
                keep_ref[p, z, :, src : src + width] = jnp.where(is_first, low, high)
                send_ref[p, z, :, src : src + width] = jnp.where(is_first, high, low).astype(BF16)


def make_hits(meta_ref, hits_ref):
    for rows in tiles(SEQ, 32):
        lane = lax.broadcasted_iota(jnp.int32, (32, ROWS), 1)
        place = lax.broadcasted_iota(jnp.int32, (32, 1), 0) + (VOCAB + ACTIONS + GAMES + rows.start)
        meta = meta_ref[rows]
        hit = (lane == meta[:, 0:1]) | (lane == meta[:, 1:2]) | (lane == place)
        hits_ref[rows] = jnp.where(hit, 1.0, 0.0).astype(BF16)


def lower_norm(x_ref, gain, offset, out_ref):
    for rows in tiles(SEQ, 32):
        out_ref[rows] = (normalise(x_ref[rows])[0] * gain + offset).astype(BF16)


def layer_forward(x_ref, w_ref, vec, bias, kept, work):
    qkv_ref, p_ref, o_ref, m_ref, h_ref, gp_ref, a_ref, c_ref = kept
    qs_ref, kv_ref, score_refs, u_ref, y_ref = work
    lower_norm(x_ref, vec[0:1], vec[1:2], a_ref)
    for j in range(3):
        cols = slice(256 * j, 256 * j + 256)
        qkv_ref[0:SEQ, cols] = dot_nn(a_ref[...], w_ref[:, cols]).astype(BF16)
    qkv_ref[SEQ:KEYS] = jnp.zeros((KEYS - SEQ, 768), BF16)
    split_heads(qkv_ref, 512, 0, KEYS, kv_ref, 0)
    for (first, count, seen), s_ref in zip(QBLOCKS, score_refs):
        base = HEADS * first
        split_heads(qkv_ref, 0, first, count, qs_ref, base)
        s_ref[...] = dot_nt(
            qs_ref[base : base + HEADS * count], qkv_ref[0:seen, 256:512]
        )
        for rows in tiles(HEADS * count, 32):
            row = lax.broadcasted_iota(jnp.int32, (32, 128), 0) + rows.start % count
            causal = row >= lax.broadcasted_iota(jnp.int32, (32, 128), 1)
            scores = jnp.where(causal, s_ref[rows, seen - 128 :], -1e30)
            if seen > 128:
                scores = jnp.concatenate([s_ref[rows, : seen - 128], scores], axis=1)
            expanded = jnp.exp(scores - jnp.max(scores, axis=1, keepdims=True))
            probs = expanded * (1.0 / jnp.sum(expanded, axis=1, keepdims=True))
            p_ref[base + rows.start : base + rows.stop, 0:seen] = probs.astype(BF16)
        out = dot_nn(
            jnp.concatenate(
                [p_ref[base + h * count : base + (h + 1) * count, 0:seen] for h in range(HEADS)],
                axis=1,
            ),
            jnp.concatenate([kv_ref[h * KEYS : h * KEYS + seen] for h in range(HEADS)], axis=0),
        )
        o_ref[first : first + count] = out.astype(BF16)
    y_ref[...] = dot_nt(o_ref[...], w_ref[:, COL_PROJ : COL_PROJ + 256])
    for rows in tiles(SEQ, 32):
        middle = x_ref[rows] + (y_ref[rows] + vec[2:3])
        m_ref[rows] = middle
        c_ref[rows] = (normalise(middle)[0] * vec[3:4] + vec[4:5]).astype(BF16)
    for chunk in range(4):
        cols = slice(256 * chunk, 256 * chunk + 256)
        u_ref[chunk] = dot_nn(c_ref[...], w_ref[:, COL_UP + cols.start : COL_UP + cols.stop])
        for rows in tiles(SEQ, 32):
            up = u_ref[chunk, rows] + bias[:, cols]
            square = up * up
            bent = jnp.tanh(up * (0.7978845608028654 + 0.0356774081363 * square))
            half = 0.5 + 0.5 * bent
            hidden = up * half
            slope = 0.7978845608028654 + 0.1070322244089 * square
            gp_ref[rows, cols] = (half + hidden * (1.0 - bent) * slope).astype(BF16)
            h_ref[rows, cols] = hidden.astype(BF16)
    y_ref[...] = dot_nt(h_ref[...], w_ref[:, COL_DOWN : COL_DOWN + FF])


def add_gradient(g_ref, column, left_ref, right_ref, left_turned):
    left_turned[...] = jnp.transpose(left_ref[...])
    for first in range(0, right_ref.shape[1], 256):
        cols = slice(first, min(first + 256, right_ref.shape[1]))
        g_ref[:, column + cols.start : column + cols.stop] += dot_nn(
            left_turned[...], right_ref[0:SEQ, cols]
        )


def ff_backward(grad_ref, grad16_ref, w_ref, vec, kept, g_ref, g_up, g_down, v_ref, v_row, bias_row, work, mid_ref, mid16_ref):
    m_ref, h_ref, gp_ref, c_ref = kept
    u_ref, y_ref, du_ref, turned_ref = work
    for chunk in range(4):
        cols = slice(256 * chunk, 256 * chunk + 256)
        u_ref[chunk] = dot_nn(
            grad16_ref[...], w_ref[:, COL_DOWN + cols.start : COL_DOWN + cols.stop]
        )
        total = None
        for rows in tiles(SEQ, 32):
            grad_up = u_ref[chunk, rows] * gp_ref[rows, cols].astype(F32)
            total = plus(total, fold(grad_up))
            du_ref[rows, cols] = grad_up.astype(BF16)
        v_ref[bias_row + chunk] += total
    add_gradient(g_ref, g_down, grad16_ref, h_ref, turned_ref.at[0])
    add_gradient(g_ref, g_up, c_ref, du_ref, turned_ref.at[1])
    y_ref[...] = dot_nt(du_ref[...], w_ref[:, COL_UP : COL_UP + FF])
    totals = [None] * 3
    for rows in tiles(SEQ, 32):
        xhat, scale = normalise(m_ref[rows])
        grad = y_ref[rows]
        mid = grad_ref[rows] + normalise_back(grad, xhat, scale, vec[3:4])
        mid_ref[rows] = mid
        if mid16_ref is not None:
            mid16_ref[rows] = mid.astype(BF16)
        for i, a in enumerate((mid, grad * xhat, grad)):
            totals[i] = plus(totals[i], fold(a))
    for i in range(3):
        v_ref[v_row + 2 + i] += totals[i]


def attention_backward(mid_ref, mid16_ref, w_ref, vec, kept, g_ref, v_ref, v_row, work, out_ref, out16_ref):
    x_ref, qkv_ref, p_ref, o_ref, a_ref = kept
    qs_ref, kv_ref, dos_ref, ds_ref, dkv_ref, dqkv_ref, score_refs, y_ref, turned_ref = work
    add_gradient(g_ref, COL_PROJ, mid16_ref, o_ref, turned_ref.at[0])
    dqkv_ref[:, 0:256] = dot_nn(mid16_ref[...], w_ref[:, COL_PROJ : COL_PROJ + 256]).astype(BF16)
    split_heads(qkv_ref, 256, 0, KEYS, kv_ref, 0)
    dkv_ref[...] = jnp.zeros(dkv_ref.shape, F32)
    for first, count, seen in QBLOCKS:
        split_heads(dqkv_ref, 0, first, count, dos_ref, HEADS * first)
    for (first, count, seen), s_ref in zip(QBLOCKS, score_refs):
        base = HEADS * first
        block = slice(base, base + HEADS * count)
        s_ref[...] = dot_nt(dos_ref[block], qkv_ref[0:seen, 512:768])
        for rows in tiles(HEADS * count, 32):
            here = slice(base + rows.start, base + rows.stop)
            probs, grad = p_ref[here, 0:seen].astype(F32), s_ref[rows]
            inner = jnp.sum(probs * grad, axis=1, keepdims=True)
            ds_ref[here, 0:seen] = (probs * (grad - inner)).astype(BF16)
        grad_query = dot_nn(
            jnp.concatenate(
                [ds_ref[base + h * count : base + (h + 1) * count, 0:seen] for h in range(HEADS)],
                axis=1,
            ),
            jnp.concatenate([kv_ref[h * KEYS : h * KEYS + seen] for h in range(HEADS)], axis=0),
        )
        dqkv_ref[first : first + count, 0:256] = grad_query.astype(BF16)
        dkv_ref[0:seen, 0:256] += dot_tn(ds_ref[block, 0:seen], qs_ref[block])
        dkv_ref[0:seen, 256:512] += dot_tn(p_ref[block, 0:seen], dos_ref[block])
    for rows in tiles(SEQ, 32):
        dqkv_ref[rows, 256:768] = dkv_ref[rows].astype(BF16)
    add_gradient(g_ref, COL_QKV, a_ref, dqkv_ref, turned_ref.at[1])
    y_ref[...] = dot_nt(dqkv_ref[...], w_ref[:, COL_QKV : COL_QKV + 768])
    totals = [None] * 2
    for rows in tiles(SEQ, 32):
        xhat, scale = normalise(x_ref[rows])
        grad = y_ref[rows]
        out = mid_ref[rows] + normalise_back(grad, xhat, scale, vec[0:1])
        if out_ref is not None:
            out_ref[rows] = out
        if out16_ref is not None:
            out16_ref[rows] = out.astype(BF16)
        for i, a in enumerate((grad * xhat, grad)):
            totals[i] = plus(totals[i], fold(a))
    for i in range(2):
        v_ref[v_row + i] += totals[i]


def own_bias(place_ref, mine, other):
    is_first = place_ref[1] == 0
    return jnp.concatenate(
        [jnp.where(is_first, mine, other), jnp.where(is_first, other, mine)], axis=1
    )


def prepare_kernel(place_ref, games_ref, tokens, actions, valid, rewards, ends, after, out, x_ref):
    count = out.shape[0]
    frames = tokens.shape[2]
    base = place_ref[1] * count
    row = lax.broadcasted_iota(jnp.int32, (SEQ, frames), 0)
    start = lax.broadcasted_iota(jnp.int32, (SEQ, frames), 1) * FRAME_TOKENS
    here = jnp.where((row >= start) & (row < start + FRAME_TOKENS), 1.0, 0.0).astype(BF16)
    coming = jnp.where((row >= start - FRAME_TOKENS) & (row < start), 1.0, 0.0).astype(BF16)
    passed = jnp.sum(jnp.where(row >= start + FRAME_TOKENS, 1, 0), axis=1, keepdims=True)
    place = lax.broadcasted_iota(jnp.int32, (SEQ, 1), 0)
    spot = place - passed * FRAME_TOKENS
    lane = lax.broadcasted_iota(jnp.int32, (SEQ, 24), 1)
    wide_lane = lax.broadcasted_iota(jnp.int32, (SEQ, 128), 1)
    inside = place < LENGTH
    x_ref[...] = jnp.zeros(x_ref.shape, jnp.int32)
    for s in range(count):
        x_ref[0:OBS] = tokens[base + s]
        x_ref[16:17] = actions[pl.ds(base + s, 1)] + VOCAB
        x_ref[17:18] = valid[pl.ds(base + s, 1)]
        x_ref[18:19] = rewards[pl.ds(base + s, 1)]
        x_ref[19:20] = ends[pl.ds(base + s, 1)] + 3
        high = (x_ref[...] >> 4).astype(F32).astype(BF16)
        low = (x_ref[...] & 15).astype(F32).astype(BF16)
        now = dot_nt(here, high) * 16.0 + dot_nt(here, low)
        soon = dot_nt(coming, high) * 16.0 + dot_nt(coming, low)

        def pick(condition, a):
            return jnp.sum(jnp.where(condition, a, 0.0), axis=1, keepdims=True).astype(jnp.int32)

        ids = jnp.where(inside, pick(lane == spot, now), -1)
        game = jnp.where(inside, games_ref[base + s] + (VOCAB + ACTIONS), -1)
        target = pick((lane == spot + 1) & (spot < 15), now)
        target = target + pick((lane == 0) & (spot == 16), soon)
        weight = pick((lane == 17) & (spot < 15), now) + pick((lane == 17) & (spot == 16), soon)
        side = pick((lane == 17) & (spot == 16), now)
        reward, end = pick(lane == 18, now), pick(lane == 19, now)
        result = jnp.zeros((SEQ, 128), jnp.int32)
        for c, column in enumerate((ids, game, target, weight, side, reward, end)):
            result = jnp.where(wide_lane == c, column, result)
        out[s] = result


def first_forward_kernel(*refs):
    place_ref, meta_ref, vec_ref, bias_ref, bias_other = refs[0:5]
    mine, other = refs[5:9], refs[9:13]
    w_out, side_out, next_ref, hits_ref, x_ref = refs[13:18]
    kept = [ref.at[0] for ref in refs[18:26]]
    w_ref, qs_ref, kv_ref, s0, s1, s2, u_ref, y_ref = refs[26:34]

    @pl.when(pl.program_id(0) == 0)
    def _():
        assemble(mine, other, place_ref, w_ref, HALF_FIRST)
        w_out[...] = w_ref[...]
        side_out[...] = w_ref[:, COL_SMALL:]
        qs_ref[...] = jnp.zeros(qs_ref.shape, BF16)
        kv_ref[...] = jnp.zeros(kv_ref.shape, BF16)

    make_hits(meta_ref.at[0], hits_ref.at[0])
    x_ref[0] = dot_nt(hits_ref[0], w_ref[:, COL_TABLE : COL_TABLE + ROWS])
    bias = own_bias(place_ref, bias_ref[0:1], bias_other[0:1])
    vec = vec_ref[0:6]
    layer_forward(x_ref.at[0], w_ref, vec, bias, kept, (qs_ref, kv_ref, (s0, s1, s2), u_ref, y_ref))
    m_ref = kept[3]
    for rows in tiles(SEQ, 32):
        next_ref[0, rows] = m_ref[rows] + (y_ref[rows] + vec[5:6])


def codebook_losses(logits, meta):
    weight = meta[:, 3:4].astype(F32)
    peak = jnp.max(logits, axis=1, keepdims=True)
    expanded = jnp.exp(logits - peak)
    total = jnp.sum(expanded, axis=1, keepdims=True)
    hit = lax.broadcasted_iota(jnp.int32, logits.shape, 1) == meta[:, 2:3]
    picked = jnp.sum(jnp.where(hit, logits, 0.0), axis=1, keepdims=True)
    loss = weight * (peak + jnp.log(total) - picked)
    return loss, expanded * (weight / total) - jnp.where(hit, weight, 0.0)


def side_losses(side, meta):
    lane = lax.broadcasted_iota(jnp.int32, side.shape, 1)
    is_reward, is_end = lane < 3, (lane == 3) | (lane == 4)
    is_side = lane < 5
    weight = meta[:, 4:5].astype(F32)
    reward_peak = jnp.max(jnp.where(is_reward, side, -1e30), axis=1, keepdims=True)
    end_peak = jnp.max(jnp.where(is_end, side, -1e30), axis=1, keepdims=True)
    shifted = jnp.where(is_side, side - jnp.where(is_reward, reward_peak, end_peak), 0.0)
    expanded = jnp.where(is_side, jnp.exp(shifted), 0.0)
    reward_total = jnp.sum(jnp.where(is_reward, expanded, 0.0), axis=1, keepdims=True)
    end_total = jnp.sum(jnp.where(is_end, expanded, 0.0), axis=1, keepdims=True)
    hit = (lane == meta[:, 5:6]) | (lane == meta[:, 6:7])
    picked = jnp.sum(jnp.where(hit, side, 0.0), axis=1, keepdims=True)
    terms = reward_peak + jnp.log(reward_total) + end_peak + jnp.log(end_total) - picked
    grad = expanded * jnp.where(is_reward, weight / reward_total, weight / end_total)
    return weight * terms, grad - jnp.where(hit, weight, 0.0), weight


def middle_kernel(*refs):
    place_ref, meta_ref, vec_ref, bias_ref, bias_other, side_ref, in_ref = refs[0:7]
    mine, other = refs[7:11], refs[11:15]
    grad_ref, keep_ref, send_ref, v_out, scalar_ref = refs[15:20]
    w_ref, g_ref, v_ref = refs[20:23]
    kept = refs[23:31]
    qkv_ref, p_ref, o_ref, m_ref, h_ref, gp_ref, a_ref, c_ref = kept
    qs_ref, kv_ref, s0, s1, s2, u_ref, y_ref = refs[31:38]
    du_ref, turned_ref, dos_ref, ds_ref, dkv_ref, dqkv_ref = refs[38:44]
    last_ref, final_ref, logit_ref, dlogit_ref, up_ref, up16_ref, mid_ref, mid16_ref = refs[44:52]
    scores = (s0, s1, s2)
    step = pl.program_id(0)

    @pl.when(step == 0)
    def _():
        assemble(mine, other, place_ref, w_ref, HALF_SECOND)
        w_ref[:, COL_SECOND:] = side_ref[...]
        g_ref[...] = jnp.zeros(g_ref.shape, F32)
        v_ref[...] = jnp.zeros(v_ref.shape, F32)
        scalar_ref[...] = jnp.zeros(scalar_ref.shape, F32)
        for ref in (qs_ref, kv_ref, dos_ref):
            ref[...] = jnp.zeros(ref.shape, BF16)

    x_ref = in_ref.at[0]
    vec = vec_ref[6:12]
    bias = own_bias(place_ref, bias_ref[1:2], bias_other[1:2])
    layer_forward(x_ref, w_ref, vec, bias, kept, (qs_ref, kv_ref, scores, u_ref, y_ref))

    gain, offset = vec_ref[12:13], vec_ref[13:14]
    for rows in tiles(SEQ, 32):
        last = m_ref[rows] + (y_ref[rows] + vec[5:6])
        last_ref[rows] = last
        final_ref[rows] = (normalise(last)[0] * gain + offset).astype(BF16)
    cols_head = slice(COL_HEAD, COL_HEAD + VOCAB + 128)
    logit_ref[...] = dot_nn(final_ref[...], w_ref[:, cols_head])
    loss, valid = None, None
    for rows in tiles(SEQ, 32):
        meta = meta_ref[0, rows]
        token_loss, grad = codebook_losses(logit_ref[rows, :VOCAB], meta)
        dlogit_ref[rows, :VOCAB] = grad.astype(BF16)
        side_loss, grad, weight = side_losses(logit_ref[rows, VOCAB:], meta)
        dlogit_ref[rows, VOCAB:] = grad.astype(BF16)
        loss, valid = plus(loss, token_loss + side_loss), plus(valid, weight)
    scalar_lane = lax.broadcasted_iota(jnp.int32, (8, 128), 1)
    scalar_row = lax.broadcasted_iota(jnp.int32, (8, 128), 0) == 0
    scalar_ref[...] += jnp.where(scalar_row & (scalar_lane == 0), column_sum(loss), 0.0)
    scalar_ref[...] += jnp.where(scalar_row & (scalar_lane == 1), column_sum(valid), 0.0)
    add_gradient(g_ref, COL_HEAD, final_ref, dlogit_ref, turned_ref.at[0])
    y_ref[...] = dot_nt(dlogit_ref[...], w_ref[:, cols_head])
    totals = [None] * 3
    for rows in tiles(SEQ, 32):
        xhat, scale = normalise(last_ref[rows])
        grad = y_ref[rows]
        up = normalise_back(grad, xhat, scale, gain)
        up_ref[rows] = up
        up16_ref[rows] = up.astype(BF16)
        for i, a in enumerate((up, grad * xhat, grad)):
            totals[i] = plus(totals[i], fold(a))
    for i in range(3):
        v_ref[11 + i] += totals[i]
    ff_backward(
        up_ref,
        up16_ref,
        w_ref,
        vec,
        (m_ref, h_ref, gp_ref, c_ref),
        g_ref,
        COL_UP,
        COL_DOWN,
        v_ref,
        6,
        SMALL_BIAS + 4,
        (u_ref, y_ref, du_ref, turned_ref),
        mid_ref,
        mid16_ref,
    )
    attention_backward(
        mid_ref,
        mid16_ref,
        w_ref,
        vec,
        (x_ref, qkv_ref, p_ref, o_ref, a_ref),
        g_ref,
        v_ref,
        6,
        (qs_ref, kv_ref, dos_ref, ds_ref, dkv_ref, dqkv_ref, scores, y_ref, turned_ref),
        grad_ref.at[0],
        None,
    )

    @pl.when(step == pl.num_programs(0) - 1)
    def _():
        disperse(g_ref, place_ref, keep_ref, send_ref, HALF_SECOND)
        side = jnp.transpose(g_ref[:, COL_SECOND:])
        for i in range(5):
            v_ref[SMALL_SIDE + i, 0:1] = side[i : i + 1]
        v_out[...] = v_ref[...]


def ff_backward_kernel(*refs):
    place_ref, vec_ref, w_ref, grad_ref, v_in = refs[0:5]
    kept = [ref.at[0] for ref in refs[5:9]]
    mid_ref, keep_ref, send_ref, v_out = refs[9:13]
    g_ref, v_ref, grad16_ref, u_ref, y_ref, du_ref, turned_ref = refs[13:20]
    step = pl.program_id(0)

    @pl.when(step == 0)
    def _():
        g_ref[...] = jnp.zeros(g_ref.shape, F32)
        v_ref[...] = v_in[...]

    total = None
    for rows in tiles(SEQ, 32):
        grad = grad_ref[0, rows]
        grad16_ref[rows] = grad.astype(BF16)
        total = plus(total, fold(grad))
    v_ref[5] += total
    ff_backward(
        grad_ref.at[0],
        grad16_ref,
        w_ref,
        vec_ref[0:6],
        kept,
        g_ref,
        GRAD_UP,
        GRAD_DOWN,
        v_ref,
        0,
        SMALL_BIAS,
        (u_ref, y_ref, du_ref, turned_ref),
        mid_ref.at[0],
        None,
    )

    @pl.when(step == pl.num_programs(0) - 1)
    def _():
        disperse(g_ref, place_ref, keep_ref, send_ref, HALF_GRAD_FF, False)
        v_out[...] = v_ref[...]


def attention_backward_kernel(*refs):
    place_ref, vec_ref, w_ref, mid_ref, hits_ref, v_in = refs[0:6]
    kept = [ref.at[0] for ref in refs[6:11]]
    keep_ref, send_ref, v_out = refs[12:15]
    g_ref, v_ref, mid16_ref, out16_ref = refs[15:19]
    qs_ref, kv_ref, s0, s1, s2, y_ref = refs[19:25]
    turned_ref, dos_ref, ds_ref, dkv_ref, dqkv_ref = refs[25:30]
    qkv_ref = kept[1]
    step = pl.program_id(0)

    @pl.when(step == 0)
    def _():
        g_ref[...] = jnp.zeros(g_ref.shape, F32)
        v_ref[...] = v_in[...]
        for ref in (qs_ref, kv_ref, dos_ref):
            ref[...] = jnp.zeros(ref.shape, BF16)

    for first, count, _ in QBLOCKS:
        split_heads(qkv_ref, 0, first, count, qs_ref, HEADS * first)
    for rows in tiles(SEQ, 32):
        mid16_ref[rows] = mid_ref[0, rows].astype(BF16)
    attention_backward(
        mid_ref.at[0],
        mid16_ref,
        w_ref,
        vec_ref[0:6],
        kept,
        g_ref,
        v_ref,
        0,
        (qs_ref, kv_ref, dos_ref, ds_ref, dkv_ref, dqkv_ref, (s0, s1, s2), y_ref, turned_ref),
        None,
        out16_ref,
    )
    add_gradient(g_ref, GRAD_TABLE, out16_ref, hits_ref.at[0], turned_ref.at[0])

    @pl.when(step == pl.num_programs(0) - 1)
    def _():
        small = jnp.sum(v_ref[...], axis=1)
        v_out[...] = small
        for block in range(16):
            quarter = small[8 * (block // 4) : 8 * (block // 4) + 8]
            g_ref[16 * block : 16 * block + 8, GRAD_SMALL:] = quarter[:, 0:128]
            g_ref[16 * block + 8 : 16 * block + 16, GRAD_SMALL:] = quarter[:, 128:256]
        disperse(g_ref, place_ref, keep_ref, send_ref, HALF_GRAD_REST)


def pack_layer(attn, proj, up, down, layer, out):
    for j in range(3):
        out[:, 128 * j : 128 * j + 128] = attn[layer, j].astype(BF16)
    out[:, 384:512] = proj[layer].astype(BF16)
    out[:, 512:1024] = up[layer].astype(BF16)
    out[:, 1024:1536] = down[layer].astype(BF16)


def pack_kernel(place_ref, table, attn, proj, up, down, head, side, first, second, pad_ref):
    pack_layer(attn, proj, up, down, 0, first)
    pack_layer(attn, proj, up, down, 1, second)
    second[:, 1536:1792] = head[...].astype(BF16)
    rows = side.shape[1]
    eye = (
        lax.broadcasted_iota(jnp.int32, (rows, rows), 0)
        == lax.broadcasted_iota(jnp.int32, (rows, rows), 1)
    )
    eye = jnp.where(eye, 1.0, 0.0).astype(BF16)
    pad_ref[...] = jnp.zeros(pad_ref.shape, F32)
    pad_ref[:, 0:5] = dot_nt(eye, side[...].astype(BF16))
    high = jnp.concatenate([table[:, 512:896], pad_ref[...]], axis=1)
    first[:, 1536:2048] = jnp.where(place_ref[1] == 0, table[:, 0:512], high).astype(BF16)


def finish_kernel(*refs):
    count = (len(refs) - 6) // 2
    place_ref = refs[0]
    scalar_ref = refs[2 * count + 1]
    out_rest, out_other, out_table, out_small = refs[2 * count + 2 :]
    square = jnp.zeros((1, 1), F32)
    for pieces, out in ((refs[1 : count + 1], out_rest), (refs[count + 1 : 2 * count + 1], out_other)):
        total = pieces[0][...]
        for piece in pieces[1:]:
            total = total + piece[...].astype(F32)
        out[...] = total
        square = square + column_sum(jnp.sum(total * total, axis=1, keepdims=True))
    small = out_rest[:, 896:1024]
    extra = column_sum(jnp.sum(small * small, axis=1, keepdims=True))
    square = square - jnp.where(place_ref[1] == 0, 0.0, extra)
    out_table[...] = out_rest[:, 512:1024]
    rows = small.shape[0]
    out_small[0:rows] = small
    lane = lax.broadcasted_iota(jnp.int32, (8, 128), 1)
    top = lax.broadcasted_iota(jnp.int32, (8, 128), 0) == 0
    out_small[rows : rows + 8] = scalar_ref[...] + jnp.where(top & (lane == 2), square, 0.0)


def adam_rule(weight, moment, second, gradient, step_rate, decay_rate):
    moment_new = BETA_ONE * moment + (1.0 - BETA_ONE) * gradient
    second_new = BETA_TWO * second + (1.0 - BETA_TWO) * gradient * gradient
    moment_hat = moment_new / (1.0 - BETA_ONE**STEP_NUMBER)
    second_hat = second_new / (1.0 - BETA_TWO**STEP_NUMBER)
    weight_new = weight - step_rate * (
        moment_hat / (jnp.sqrt(second_hat) + EPS_ADAM) + decay_rate * weight
    )
    return (weight_new, moment_new, second_new)


def adam_kernel(*refs):
    place_ref, rest, others, swapped = refs[0:4]
    quarters = refs[4:8]
    params = [refs[8 + 3 * i : 11 + 3 * i] for i in range(9)]
    loss_ref, valid_ref, norm_ref = refs[35:38]
    outs = [refs[38 + 3 * i : 41 + 3 * i] for i in range(9)]
    small_ref = refs[65]
    me, wide = place_ref[0], place_ref[2]
    is_first = place_ref[1] == 0
    rows = rest.shape[0]
    for k in range(4):
        row = pl.multiple_of(((me >> 2) ^ k) * 8, 8)
        small_ref[pl.ds(row, 8), 0:128] = quarters[k][0:8]
        small_ref[pl.ds(row, 8), 128:256] = quarters[k][8:16]
    tops = [quarter[16:17] for quarter in quarters]
    scalars = (tops[0] + tops[1]) + (tops[2] + tops[3])
    small = small_ref[...]
    loss, valid, square = scalars[:, 0:1], scalars[:, 1:2], scalars[:, 2:3]
    square = square + column_sum(jnp.sum(small * small, axis=1, keepdims=True))
    inverse = 1.0 / valid
    norm = jnp.sqrt(square) * inverse
    loss_ref[...], valid_ref[...], norm_ref[...] = loss, valid, norm
    factor = jnp.minimum(1.0, CLIP_AT / (norm + 1e-06)) * inverse
    table, attn, proj, up, bias, down, vectors, head, side = range(9)

    def update(which, index, gradient, step_rate, decay_rate):
        news = adam_rule(
            *(ref[index] for ref in params[which]), factor * gradient, step_rate, decay_rate
        )
        for ref, new in zip(outs[which], news):
            ref[index] = new

    layers = ((rest, others, 1792), (others, others, 512))
    for layer, (attention, feed, at) in enumerate(layers):
        for j in range(3):
            update(attn, (layer, j), attention[:, 128 * j : 128 * j + 128], RATE_MATRIX, DECAY_RATE)
        update(proj, (layer,), attention[:, 384:512], RATE_MATRIX, DECAY_RATE)
        update(up, (layer,), feed[:, at : at + 512], RATE_MATRIX, DECAY_RATE)
        update(down, (layer,), feed[:, at + 512 : at + 1024], RATE_MATRIX, DECAY_RATE)
        for i in range(2):
            low = SMALL_BIAS + 4 * layer + i
            row = jnp.where(is_first, small[low : low + 1], small[low + 2 : low + 3])
            index = (slice(layer, layer + 1), slice(256 * i, 256 * i + 256))
            update(bias, index, row, RATE_VECTOR, 0.0)
    whole = (slice(None), slice(None))
    update(head, whole, others[:, 1536:1792], RATE_MATRIX, DECAY_RATE)
    mine, theirs = rest[:, 512:1024], swapped[:, 0:512]
    low, high = jnp.where(is_first, mine, theirs), jnp.where(is_first, theirs, mine)
    update(table, (slice(None), slice(0, 512)), low, RATE_TABLE, DECAY_RATE)
    update(table, (slice(None), slice(512, 896)), high[:, 0:384], RATE_TABLE, DECAY_RATE)
    update(vectors, whole, small[0:NVEC], RATE_VECTOR, 0.0)
    turned = pltpu.roll(small[SMALL_SIDE : SMALL_SIDE + 8], lax.rem(D - wide * rows, D), 1)
    update(side, whole, turned[0:5, 0:rows], RATE_MATRIX, DECAY_RATE)


def swap(a, axis, distance):
    size = lax.axis_size(axis)
    return lax.ppermute(a, axis, [(i, i ^ distance) for i in range(size)])


def swap_column(piece, n_high):
    return [piece] + [swap(piece, "wide", 4 * k) for k in range(1, n_high)]


def gather_plane(column):
    return [column] + [swap(column, "wide", p) for p in range(1, 4)]


def gather_cores(mine):
    return [swap(a, "narrow", 1) for a in mine]


def in_blocks(parts, wide):
    n_high, rows, cols = parts[0].shape
    if rows == 16:
        return parts
    whole = jnp.stack(parts, axis=1).reshape(4 * n_high, rows, cols)
    whole = whole[wide ^ jnp.arange(4 * n_high)].reshape(4, 4, 16, cols)
    return [whole[:, p] for p in range(4)]


def in_pieces(blocks, wide, n_high):
    cols = blocks.shape[-1]
    if n_high == 4:
        return blocks
    rows = 64 // n_high
    whole = blocks.transpose(1, 0, 2, 3).reshape(4 * n_high, rows, cols)
    whole = whole[wide ^ jnp.arange(4 * n_high)]
    return whole.reshape(n_high, 4, rows, cols).transpose(1, 0, 2, 3)


def add_cores(keep, send, wide, n_high):
    keep, send = in_pieces(keep, wide, n_high), in_pieces(send, wide, n_high)
    received = swap(send, "narrow", 1)
    return [keep[p] + received[p].astype(F32) for p in range(4)]


def swap_plane(sums):
    return [swap(sums[p].astype(BF16), "wide", p) for p in range(1, 4)]


def add_plane(own, received):
    for a in received:
        own = own + a.astype(F32)
    return own


def column_pieces(own):
    return [own[0]] + [swap(own[k].astype(BF16), "wide", 4 * k) for k in range(1, own.shape[0])]


def full_spec(a):
    return pl.BlockSpec(a.shape, lambda *_: (0,) * len(a.shape))


def row_spec(shape):
    return pl.BlockSpec((1,) + shape, lambda i: (i,) + (0,) * len(shape))


def shaped(shape, dtype):
    return jax.ShapeDtypeStruct(shape, dtype)


VMEM_SPEC = pl.BlockSpec(memory_space=pltpu.VMEM)
ANY_SPEC = pl.BlockSpec(memory_space=pl.ANY)
SMEM_SPEC = pl.BlockSpec(memory_space=pltpu.SMEM)


def call(kernel, grid, in_specs, out_specs, out_shape, scratch, flops, bytes_accessed, name):
    extra = {"grid": grid} if grid else {}
    return pl.pallas_call(
        kernel,
        in_specs=in_specs,
        out_specs=out_specs,
        out_shape=out_shape,
        scratch_shapes=scratch,
        compiler_params=pltpu.CompilerParams(vmem_limit_bytes=VMEM_BYTES),
        cost_estimate=pl.CostEstimate(
            flops=flops, bytes_accessed=bytes_accessed, transcendentals=0
        ),
        name=name,
        **extra,
    )


KEPT = (
    ((KEYS, 768), BF16),
    ((HEADS * SEQ, KEYS), BF16),
    ((SEQ, D), BF16),
    ((SEQ, D), F32),
    ((SEQ, FF), BF16),
    ((SEQ, FF), BF16),
    ((SEQ, D), BF16),
    ((SEQ, D), BF16),
)
FORWARD_WORK = [
    pltpu.VMEM((HEADS * SEQ, D), BF16),
    pltpu.VMEM((HEADS * KEYS, D), BF16),
    pltpu.VMEM((HEADS * 128, 128), F32),
    pltpu.VMEM((HEADS * 128, 256), F32),
    pltpu.VMEM((HEADS * 96, 384), F32),
    pltpu.VMEM((4, SEQ, 256), F32),
    pltpu.VMEM((SEQ, D), F32),
]
FF_WORK = pltpu.VMEM((SEQ, FF), BF16)
TURNED_WORK = pltpu.VMEM((2, D, SEQ), BF16)
ATTENTION_WORK = [
    pltpu.VMEM((HEADS * SEQ, D), BF16),
    pltpu.VMEM((HEADS * SEQ, KEYS), BF16),
    pltpu.VMEM((KEYS, 512), F32),
    pltpu.VMEM((SEQ, 768), BF16),
]


def per_device(
    tokens,
    actions,
    game_ids,
    valid_steps,
    rewards,
    end_flags,
    embed_table,
    table_first,
    table_second,
    attn_weight,
    attn_first,
    attn_second,
    proj_weight,
    proj_first,
    proj_second,
    up_weight,
    up_first,
    up_second,
    up_bias,
    bias_first,
    bias_second,
    down_weight,
    down_first,
    down_second,
    vectors,
    vectors_first,
    vectors_second,
    head_weight,
    head_first,
    head_second,
    side_weight,
    side_first,
    side_second,
):
    n_high = lax.axis_size("wide") // 4
    wide, core = lax.axis_index("wide"), lax.axis_index("narrow")
    rows = side_weight.shape[0]
    fast = rows == 16
    place = jnp.stack([wide if fast else jnp.zeros_like(wide), core, wide]).astype(jnp.int32)

    def flat(a):
        return jnp.swapaxes(a, -1, -2)

    params = (
        (flat(embed_table), flat(table_first), flat(table_second)),
        (attn_weight, attn_first, attn_second),
        (flat(proj_weight), flat(proj_first), flat(proj_second)),
        (up_weight, up_first, up_second),
        (up_bias, bias_first, bias_second),
        (flat(down_weight), flat(down_first), flat(down_second)),
        (vectors, vectors_first, vectors_second),
        (head_weight, head_first, head_second),
        (flat(side_weight), flat(side_first), flat(side_second)),
    )
    table, attn, proj, up, _, down, _, head, side = (group[0] for group in params)

    piece_first, piece_second = call(
        pack_kernel,
        None,
        [SMEM_SPEC] + [VMEM_SPEC] * 7,
        [VMEM_SPEC] * 2,
        [shaped((rows, HALF_FIRST_COLS), BF16), shaped((rows, HALF_SECOND_COLS), BF16)],
        [pltpu.VMEM((rows, 128), F32)],
        10**6,
        10**6,
        "pack",
    )(place, table, attn, proj, up, down, head, side)
    first_column = swap_column(piece_first, n_high)

    count = tokens.shape[0] // lax.axis_size("narrow")
    meta = call(
        prepare_kernel,
        None,
        [SMEM_SPEC] * 2 + [VMEM_SPEC] * 5 + [ANY_SPEC],
        VMEM_SPEC,
        shaped((count, SEQ, 128), jnp.int32),
        [pltpu.VMEM((24, FRAMES), jnp.int32)],
        10**6,
        10**6,
        "prepare",
    )(place, game_ids, flat(tokens), actions, valid_steps, rewards, end_flags, piece_first)
    first_column, meta = lax.optimization_barrier((first_column, meta))
    first_mine = gather_plane(jnp.stack(first_column))
    piece_second, beside = lax.optimization_barrier((piece_second, first_mine[1]))
    first_mine = [first_mine[0], beside] + first_mine[2:]
    first_other = gather_cores(first_mine)
    second_column = jnp.stack(swap_column(piece_second, n_high))
    second_mine = gather_plane(second_column)
    first_parts = in_blocks(first_mine, wide) + in_blocks(first_other, wide)
    other_bias = swap(up_bias, "narrow", 1)

    kept_specs = [row_spec(shape) for shape, _ in KEPT]
    kept_shapes = [shaped((count,) + shape, dtype) for shape, dtype in KEPT]
    row_f32 = shaped((count, SEQ, D), F32)
    meta_spec = row_spec((SEQ, 128))
    vec_specs = [full_spec(vectors), full_spec(up_bias), full_spec(up_bias)]
    w_spec = pl.BlockSpec((D, COL_FIRST), lambda i: (0, 0))
    side_spec = pl.BlockSpec((D, 128), lambda i: (0, 0))
    hits_spec = row_spec((SEQ, ROWS))
    results = call(
        first_forward_kernel,
        (count,),
        [SMEM_SPEC, meta_spec] + vec_specs + [full_spec(a) for a in first_parts],
        [w_spec, side_spec, row_spec((SEQ, D)), hits_spec, row_spec((SEQ, D))] + kept_specs,
        [shaped((D, COL_FIRST), BF16), shaped((D, 128), BF16), row_f32]
        + [shaped((count, SEQ, ROWS), BF16), row_f32]
        + kept_shapes,
        [pltpu.VMEM((D, COL_FIRST), BF16)] + FORWARD_WORK,
        4 * 10**9,
        20 * 10**6,
        "first_forward",
    )(place, meta, vectors, up_bias, other_bias, *first_parts)
    w_first, side_copy, stream, hits, stream_first = results[0:5]
    kept = results[5:]
    kept_qkv, kept_p, kept_o, kept_m, kept_h, kept_gp, kept_a, kept_c = kept
    received, side_copy = lax.optimization_barrier((second_mine[1:], side_copy))
    second_mine = second_mine[0:1] + received
    second_other = gather_cores(second_mine)
    second_parts = in_blocks(second_mine, wide) + in_blocks(second_other, wide)

    def blocks(cols):
        return pl.BlockSpec((4, 4, 16, cols), lambda i: (0, 0, 0, 0))

    def block_shapes(cols):
        return [shaped((4, 4, 16, cols), F32), shaped((4, 4, 16, cols), BF16)]

    small_spec = pl.BlockSpec((SMALL_ROWS, 8, D), lambda i: (0, 0, 0))
    small_shape = shaped((SMALL_ROWS, 8, D), F32)
    small_scratch = pltpu.VMEM((SMALL_ROWS, 8, D), F32)
    scalar_spec = pl.BlockSpec((8, 128), lambda i: (0, 0))
    grad_stream, keep_second, send_second, small_grads, scalars = call(
        middle_kernel,
        (count,),
        [SMEM_SPEC, meta_spec]
        + vec_specs
        + [side_spec, row_spec((SEQ, D))]
        + [full_spec(a) for a in second_parts],
        [row_spec((SEQ, D))] + [blocks(HALF_SECOND_COLS)] * 2 + [small_spec, scalar_spec],
        [row_f32] + block_shapes(HALF_SECOND_COLS) + [small_shape, shaped((8, 128), F32)],
        [
            pltpu.VMEM((D, COL_SECOND + 128), BF16),
            pltpu.VMEM((D, COL_SECOND + 128), F32),
            small_scratch,
        ]
        + [pltpu.VMEM(shape, dtype) for shape, dtype in KEPT]
        + FORWARD_WORK
        + [FF_WORK, TURNED_WORK]
        + ATTENTION_WORK
        + [
            pltpu.VMEM((SEQ, D), F32),
            pltpu.VMEM((SEQ, D), BF16),
            pltpu.VMEM((SEQ, VOCAB + 128), F32),
            pltpu.VMEM((SEQ, VOCAB + 128), BF16),
            pltpu.VMEM((SEQ, D), F32),
            pltpu.VMEM((SEQ, D), BF16),
            pltpu.VMEM((SEQ, D), F32),
            pltpu.VMEM((SEQ, D), BF16),
        ],
        15 * 10**9,
        20 * 10**6,
        "middle",
    )(place, meta, vectors, up_bias, other_bias, side_copy, stream, *second_parts)
    second_sums = add_cores(keep_second, send_second, wide, n_high)

    kept_ff = (kept_m, kept_h, kept_gp, kept_c)
    grad_mid, keep_ff, send_ff, small_grads = call(
        ff_backward_kernel,
        (count,),
        [SMEM_SPEC, full_spec(vectors), w_spec, row_spec((SEQ, D)), small_spec]
        + [row_spec(a.shape[1:]) for a in kept_ff],
        [row_spec((SEQ, D))] + [blocks(HALF_GRAD_COLS)] * 2 + [small_spec],
        [row_f32] + block_shapes(HALF_GRAD_COLS) + [small_shape],
        [
            pltpu.VMEM((D, 2048), F32),
            small_scratch,
            pltpu.VMEM((SEQ, D), BF16),
            pltpu.VMEM((4, SEQ, 256), F32),
            pltpu.VMEM((SEQ, D), F32),
            FF_WORK,
            TURNED_WORK,
        ],
        4 * 10**9,
        10 * 10**6,
        "ff_backward",
    )(place, vectors, w_first, grad_stream, small_grads, *kept_ff)
    ff_sums = add_cores(keep_ff, send_ff, wide, n_high)
    other_sums = [jnp.concatenate(pair, axis=-1) for pair in zip(second_sums, ff_sums)]
    others_received = swap_plane(other_sums)

    kept_attention = (stream_first, kept_qkv, kept_p, kept_o, kept_a)
    keep_rest, send_rest, small_grads = call(
        attention_backward_kernel,
        (count,),
        [SMEM_SPEC, full_spec(vectors), w_spec, row_spec((SEQ, D)), hits_spec, small_spec]
        + [row_spec(a.shape[1:]) for a in kept_attention]
        + [ANY_SPEC],
        [blocks(HALF_GRAD_COLS)] * 2 + [pl.BlockSpec((SMALL_ROWS, D), lambda i: (0, 0))],
        block_shapes(HALF_GRAD_COLS) + [shaped((SMALL_ROWS, D), F32)],
        [
            pltpu.VMEM((D, 2048), F32),
            small_scratch,
            pltpu.VMEM((SEQ, D), BF16),
            pltpu.VMEM((SEQ, D), BF16),
        ]
        + FORWARD_WORK[0:5]
        + [pltpu.VMEM((SEQ, D), F32), TURNED_WORK]
        + ATTENTION_WORK,
        6 * 10**9,
        20 * 10**6,
        "attention_backward",
    )(place, vectors, w_first, grad_mid, hits, small_grads, *kept_attention, other_sums[0])
    others_received, keep_rest = lax.optimization_barrier((others_received, keep_rest))
    rest_sums = add_cores(keep_rest, send_rest, wide, n_high)
    rest_received = swap_plane(rest_sums)
    other_pieces = column_pieces(add_plane(other_sums[0], others_received))
    rest_pieces = column_pieces(add_plane(rest_sums[0], rest_received))

    grad_rest, grad_others, table_part, small = call(
        finish_kernel,
        None,
        [SMEM_SPEC] + [VMEM_SPEC] * (2 * n_high + 1),
        [VMEM_SPEC] * 4,
        [
            shaped((rows, HALF_GRAD_COLS), F32),
            shaped((rows, HALF_GRAD_COLS + HALF_SECOND_COLS), F32),
            shaped((rows, 512), F32),
            shaped((rows + 8, 128), F32),
        ],
        [],
        10**6,
        10**6,
        "finish",
    )(place, *rest_pieces, *other_pieces, scalars)

    if fast:
        is_small = (jnp.arange(rows + 8) < rows)[:, None]
        beside = swap(small, "narrow", 1)
        small = jnp.where(is_small, jnp.where(core == 1, small, beside), small + beside)
        plane = [small] + [swap(small, "wide", p) for p in range(1, 4)]
        chosen = jnp.where(
            wide & 2 == 0,
            jnp.where(wide & 1 == 0, plane[0], plane[1]),
            jnp.where(wide & 1 == 0, plane[2], plane[3]),
        )
        small = jnp.where(is_small, chosen, (plane[0] + plane[1]) + (plane[2] + plane[3]))
        quarters = [small] + [swap(small, "wide", 4 * k) for k in range(1, 4)]
    else:
        sums = lax.psum(small[rows:], ("wide", "narrow"))
        total = lax.psum(small_grads, ("wide", "narrow"))
        total = total.reshape(4, 8, 2, 128).transpose(0, 2, 1, 3).reshape(4, 16, 128)
        ends = [sums] + [jnp.zeros_like(sums)] * 3
        quarters = [jnp.concatenate(pair) for pair in zip(total, ends)]
    swapped = swap(table_part, "narrow", 1)

    flat_params = [a for group in params for a in group]
    results = call(
        adam_kernel,
        None,
        [SMEM_SPEC] + [VMEM_SPEC] * 34,
        [VMEM_SPEC] * 30,
        [shaped((1, 1), F32)] * 3 + [shaped(a.shape, F32) for a in flat_params],
        [pltpu.VMEM((SMALL_ROWS, D), F32)],
        10**6,
        10**6,
        "adam",
    )(place, grad_rest, grad_others, swapped, *quarters, *flat_params)
    news = list(results[3:])
    for group in (0, 2, 5, 8):
        for member in range(3 * group, 3 * group + 3):
            news[member] = flat(news[member])
    return tuple(a.reshape(()) for a in results[0:3]) + tuple(news)


def solution(mesh):
    placed = (
        P("wide", None, None),
        P("wide", None),
        P("wide"),
        P("wide", None),
        P("wide", None),
        P("wide", None),
        P(None, "wide"),
        P(None, "wide"),
        P(None, "wide"),
        P(None, None, "wide", "narrow"),
        P(None, None, "wide", "narrow"),
        P(None, None, "wide", "narrow"),
        P(None, "narrow", "wide"),
        P(None, "narrow", "wide"),
        P(None, "narrow", "wide"),
        P(None, "wide", "narrow"),
        P(None, "wide", "narrow"),
        P(None, "wide", "narrow"),
        P(None, "narrow"),
        P(None, "narrow"),
        P(None, "narrow"),
        P(None, "narrow", "wide"),
        P(None, "narrow", "wide"),
        P(None, "narrow", "wide"),
        P(),
        P(),
        P(),
        P("wide", "narrow"),
        P("wide", "narrow"),
        P("wide", "narrow"),
        P("wide", None),
        P("wide", None),
        P("wide", None),
    )
    return jax.shard_map(
        per_device,
        mesh=mesh,
        in_specs=placed,
        out_specs=(P(), P(), P()) + placed[6:],
        check_vma=False,
    )
```

time: 187 us -> 190 us (1.016)
  Pallas kernels: 96.4 us -> 104 us
  waiting for transfers between devices: 37 us -> 30.2 us
  starting transfers between devices: 39.3 us -> 43.1 us
    pallas_call x1, Pallas kernels: 39.1 us -> 46.1 us  [per_device(): call(middle_kernel, (count,), [SMEM_SPEC, meta_spec] + vec_specs + [side_...]
    ppermute x41 -> x44, waiting for transfers between devices: 37 us -> 30.2 us  [swap(): return lax.ppermute(a, axis, [(i, i ^ distance) for i in range(size)])]
    ppermute x41 -> x44, starting transfers between devices: 39.3 us -> 43.1 us  [swap(): return lax.ppermute(a, axis, [(i, i ^ distance) for i in range(size)])]
    pallas_call x4 -> x3, Pallas kernels: 22.6 us -> 21.8 us  [the longest x1 17.5 us: per_device(): call(attention_backward_kernel, (count,), [SMEM_SPEC, full_spec(vectors),...]
    unnamed x58 -> x60, local copies, waits for them, and re-layouts: 3.97 us -> 3.29 us
  transfers between devices with their start and end apart: 41 -> 44, of which waited for: 18 -> 20; matrix products, arithmetic and copies ran while one was open for 3% -> 3% of each run, Pallas kernels for 27% -> 27%
where the time goes in v3:
time: 190 us; the launch traced here: 189 us
  Pallas kernels  104 us (55%)
  starting transfers between devices  43.1 us (23%)
  waiting for transfers between devices  30.2 us (16%)
  other arithmetic  6.04 us (3%)
  local copies, waits for them, and re-layouts  4.63 us (2%)
    pallas_call x1, Pallas kernels, per_device(): call(middle_kernel, (count,), [SMEM_SPEC, meta_spec] + vec_specs + [side_...  46.1 us
    ppermute x44, starting transfers between devices, swap(): return lax.ppermute(a, axis, [(i, i ^ distance) for i in range(size)])  43.1 us
    ppermute x44, waiting for transfers between devices, swap(): return lax.ppermute(a, axis, [(i, i ^ distance) for i in range(size)])  30.2 us
    pallas_call x1, Pallas kernels, per_device(): call(first_forward_kernel, (count,), [SMEM_SPEC, meta_spec] + vec_specs +...  20.4 us
    pallas_call x1, Pallas kernels, per_device(): call(attention_backward_kernel, (count,), [SMEM_SPEC, full_spec(vectors),...  17.5 us
    pallas_call x1, Pallas kernels, per_device(): call(ff_backward_kernel, (count,), [SMEM_SPEC, full_spec(vectors), w_spec...  9.86 us
  transfers between devices with their start and end apart: 44, of which 20 were waited for; matrix products, arithmetic and copies ran while one was open for 3% of the time, Pallas kernels for 27%

profile of v3, /device:TPU:0, one launch (start us, length us, event | category | flops | bytes accessed | tf_op | source)
XLA Modules:
  0.0 189.2 jit_solution(18065499536138330975)
XLA Ops:
  1.3 1.7 pack.1
  3.0 3.0 %collective-permute-start = (bf16[16,2048]{1,0:T(8,128)(2,1)}, bf16[16,2048]{1,0:T(8,128)(2,1)S(1)}, u32[]{:S(2)}, u32[]{:S(2)}) collective-permute-start(bf16[16,2048]{1,0:T(8,128)(2,1)} %get-tuple-element.108.after), channel_id=1, source_target_pairs={{0,8},{2,10},{4,12},{6,14},{8,0},{10,2},{12,4},{14,6},{16,24},{18,... | collective-permute-start | bytes 196616 | tf_op jit(solution)/shard_map/ppermute | solution.py:698
  6.0 2.6 %collective-permute-start.1 = (bf16[16,2048]{1,0:T(8,128)(2,1)}, bf16[16,2048]{1,0:T(8,128)(2,1)S(1)}, u32[]{:S(2)}, u32[]{:S(2)}) collective-permute-start(bf16[16,2048]{1,0:T(8,128)(2,1)} %get-tuple-element.108.after), channel_id=1, source_target_pairs={{0,16},{2,18},{4,20},{6,22},{8,24},{10,26},{12,28},{14,30},{16,0},... | collective-permute-start | bytes 196616 | tf_op jit(solution)/shard_map/ppermute | solution.py:698
  8.6 3.8 %prepare.1.refs_1_ = s32[4,352,128]{2,1,0:T(8,128)} custom-call(s32[3]{0:T(128)} %pad_add_fusion.place_ref.refs_0_, s32[8]{0:T(128)} %games_ref.1, s32[8,16,20]{2,1,0:T(8,128)} %bitcast.92, s32[8,20]{1,0:T(8,128)} %actions.1, s32[8,20]{1,0:T(8,128)} %valid.1, s32[8,20]{1,0:T(8,128)} %rewards.1, s32[8,20]{1,0:T(8,128)} %ends.1, ...), custom_call_target="tpu_custom_call" | custom-call | flops 1000000 | bytes 1000000 | tf_op jit(solution)/shard_map/prepare/pallas_call | solution.py:886
  12.4 1.1 collective-permute-done.1
  13.5 1.4 collective-permute-done.2
  14.9 0.9 pad_maximum_fusion.4.refs_5_
  15.8 1.6 collective-permute-start.4
  17.4 1.5 collective-permute-start.11
  19.4 5.7 %collective-permute-done.4.refs_6_ = bf16[4,16,2048]{2,1,0:T(8,128)(2,1)S(1)} collective-permute-done((bf16[4,16,2048]{2,1,0:T(8,128)(2,1)S(1)}, bf16[4,16,2048]{2,1,0:T(8,128)(2,1)S(1)}, u32[]{:S(2)}, u32[]{:S(2)}) %collective-permute-start.4) | collective-permute-done | bytes 262176 | tf_op jit(solution)/shard_map/ppermute | solution.py:698
  25.1 2.3 %collective-permute-start.6 = (bf16[16,1792]{1,0:T(8,128)(2,1)}, bf16[16,1792]{1,0:T(8,128)(2,1)S(1)}, u32[]{:S(2)}, u32[]{:S(2)}) collective-permute-start(bf16[16,1792]{1,0:T(8,128)(2,1)} %get-tuple-element.112), channel_id=1, source_target_pairs={{0,16},{2,18},{4,20},{6,22},{8,24},{10,26},{12,28},{14,30},{16,0},... | collective-permute-start | bytes 172040 | tf_op jit(solution)/shard_map/ppermute | solution.py:698
  27.5 2.0 %collective-permute-start.7 = (bf16[16,1792]{1,0:T(8,128)(2,1)}, bf16[16,1792]{1,0:T(8,128)(2,1)S(1)}, u32[]{:S(2)}, u32[]{:S(2)}) collective-permute-start(bf16[16,1792]{1,0:T(8,128)(2,1)} %get-tuple-element.112), channel_id=1, source_target_pairs={{0,24},{2,26},{4,28},{6,30},{8,16},{10,18},{12,20},{14,22},{16,8},... | collective-permute-start | bytes 172040 | tf_op jit(solution)/shard_map/ppermute | solution.py:698
  30.5 3.1 %collective-permute-done.7 = bf16[16,1792]{1,0:T(8,128)(2,1)S(1)} collective-permute-done((bf16[16,1792]{1,0:T(8,128)(2,1)}, bf16[16,1792]{1,0:T(8,128)(2,1)S(1)}, u32[]{:S(2)}, u32[]{:S(2)}) %collective-permute-start.7) | collective-permute-done | bytes 57376 | tf_op jit(solution)/shard_map/ppermute | solution.py:698
  33.6 0.8 pad_maximum_fusion.5.refs_7_
  35.0 2.4 %collective-permute-start.10 = (bf16[4,16,1792]{2,1,0:T(8,128)(2,1)S(1)}, bf16[4,16,1792]{2,1,0:T(8,128)(2,1)S(1)}, u32[]{:S(2)}, u32[]{:S(2)}) collective-permute-start(bf16[4,16,1792]{2,1,0:T(8,128)(2,1)S(1)} %pad_maximum_fusion.5.refs_7_), channel_id=1, source_target_pairs={{0,6},{2,4},{4,2},{6,0},{8,14},{10,12},{12,10},{14,8},{16,22},{18,... | collective-permute-start | bytes 688136 | tf_op jit(solution)/shard_map/ppermute | solution.py:698
  39.3 0.7 copy-done.21
  40.0 20.4 %first_forward.1 = (bf16[256,4096]{1,0:T(8,128)(2,1)}, bf16[256,128]{1,0:T(8,128)(2,1)}, f32[4,352,256]{2,1,0:T(8,128)}, bf16[4,352,896]{2,1,0:T(8,128)(2,1)}, f...) custom-call(s32[3]{0:T(128)} %pad_add_fusion.place_ref.refs_0_, ...), custom_call_target="tpu_custom_call" | custom-call | flops 4000000000 | bytes 20000000 | tf_op jit(solution)/shard_map/first_forward/pallas_call | solution.py:915
  61.1 0.9 collective-permute-done.18.refs_12_
  63.4 46.1 %middle.1 = (f32[4,352,256]{2,1,0:T(8,128)}, f32[4,4,16,1792]{3,2,1,0:T(8,128)}, bf16[4,4,16,1792]{3,2,1,0:T(8,128)(2,1)}, f32[32,8,256]{2,1,0:T(8,128)}, f32[8,128]{1,0:T(8,128)}) custom-call(s32[3]{0:T(128)} %pad_add_fusion.place_ref.refs_0_, s32[4,352,128]{2,1,0:T(8,128)} %prepare.1.refs_1_, f32[14,256]{1,0:T(8,128)} %refs_26_.1, f32[2,512]{1,0:T(2,128)} %refs_20_.1, ...), custom_call_target="tpu_custom_call" | custom-call | flops 15000000512 | bytes 20000000 | tf_op jit(solution)/shard_map/middle/pallas_call | solution.py:946
  109.8 9.9 %ff_backward.1 = (f32[4,352,256]{2,1,0:T(8,128)}, f32[4,4,16,1024]{3,2,1,0:T(8,128)}, bf16[4,4,16,1024]{3,2,1,0:T(8,128)(2,1)}, f32[32,8,256]{2,1,0:T(8,128)}) custom-call(s32[3]{0:T(128)} %pad_add_fusion.place_ref.refs_0_, f32[14,256]{1,0:T(8,128)} %refs_26_.1, bf16[256,4096]{1,0:T(8,128)(2,1)} %get-tuple-element.122.refs_2_, ...), custom_call_target="tpu_custom_call" | custom-call | flops 4000000000 | bytes 10000000 | tf_op jit(solution)/shard_map/ff_backward/pallas_call | solution.py:981
  120.0 1.8 collective-permute-done.22
  121.8 1.3 add_bitcast_fusion.1
  123.4 2.5 %collective-permute-start.25 = (bf16[4,16,2816]{2,1,0:T(8,128)(2,1)S(1)}, bf16[4,16,2816]{2,1,0:T(8,128)(2,1)S(1)}, u32[]{:S(2)}, u32[]{:S(2)}) collective-permute-start(bf16[4,16,2816]{2,1,0:T(8,128)(2,1)S(1)} %pad_maximum_fusion.3), channel_id=1, source_target_pairs={{0,6},{2,4},{4,2},{6,0},{8,14},{10,12},{12,10},{14,8},{16,22},{18,... | collective-permute-start | bytes 1081352 | tf_op jit(solution)/shard_map/ppermute | solution.py:698
  127.2 0.9 pad_maximum_fusion.refs_11_
  128.1 17.5 %attention_backward.1 = (f32[4,4,16,1024]{3,2,1,0:T(8,128)}, bf16[4,4,16,1024]{3,2,1,0:T(8,128)(2,1)}, f32[32,256]{1,0:T(8,128)}) custom-call(s32[3]{0:T(128)} %pad_add_fusion.place_ref.refs_0_, f32[14,256]{1,0:T(8,128)} %refs_26_.1, bf16[256,4096]{1,0:T(8,128)(2,1)} %get-tuple-element.122.refs_2_, f32[4,352,256]{2,1,0:T(8,128)} %get-tuple-element.131.refs_3_, ...), custom_call_target="tpu_custom_call" | custom-call | flops 6000000000 | bytes 20000000 | tf_op jit(solution)/shard_map/attention_backward/pallas_call | solution.py:1006
  146.0 2.6 %collective-permute-start.34 = (bf16[16,2816]{1,0:T(8,128)(2,1)S(1)}, bf16[16,2816]{1,0:T(8,128)(2,1)S(1)}, u32[]{:S(2)}, u32[]{:S(2)}) collective-permute-start(bf16[16,2816]{1,0:T(8,128)(2,1)S(1)} %get-tuple-element.196), channel_id=1, source_target_pairs={{0,16},{2,18},{4,20},{6,22},{8,24},{10,26},{12,28},{14,30},{16,0},... | collective-permute-start | bytes 270344 | tf_op jit(solution)/shard_map/ppermute | solution.py:698
  148.7 1.6 collective-permute-start.27
  150.2 1.5 collective-permute-start.28
  152.2 0.7 slice_bitcast_fusion.refs_5_
  152.9 1.5 collective-permute-done.27
  154.4 1.8 collective-permute-start.35
  156.2 1.9 collective-permute-done.28
  158.6 2.0 %collective-permute-start.31 = (bf16[16,1024]{1,0:T(8,128)(2,1)S(1)}, bf16[16,1024]{1,0:T(8,128)(2,1)S(1)}, u32[]{:S(2)}, u32[]{:S(2)}) collective-permute-start(bf16[16,1024]{1,0:T(8,128)(2,1)S(1)} %get-tuple-element.199), channel_id=1, source_target_pairs={{0,16},{2,18},{4,20},{6,22},{8,24},{10,26},{12,28},{14,30},{16,0},... | collective-permute-start | bytes 98312 | tf_op jit(solution)/shard_map/ppermute | solution.py:698
  160.6 2.0 %collective-permute-start.32 = (bf16[16,1024]{1,0:T(8,128)(2,1)S(1)}, bf16[16,1024]{1,0:T(8,128)(2,1)S(1)}, u32[]{:S(2)}, u32[]{:S(2)}) collective-permute-start(bf16[16,1024]{1,0:T(8,128)(2,1)S(1)} %get-tuple-element.198), channel_id=1, source_target_pairs={{0,24},{2,26},{4,28},{6,30},{8,16},{10,18},{12,20},{14,22},{16,8},... | collective-permute-start | bytes 98312 | tf_op jit(solution)/shard_map/ppermute | solution.py:698
  162.6 0.6 slice_bitcast_fusion.4.refs_1_
  163.8 2.5 %collective-permute-done.32.refs_4_ = bf16[16,1024]{1,0:T(8,128)(2,1)S(1)} collective-permute-done((bf16[16,1024]{1,0:T(8,128)(2,1)S(1)}, bf16[16,1024]{1,0:T(8,128)(2,1)S(1)}, u32[]{:S(2)}, u32[]{:S(2)}) %collective-permute-start.32) | collective-permute-done | bytes 32800 | tf_op jit(solution)/shard_map/ppermute | solution.py:698
  166.9 1.9 %finish.1 = (f32[16,1024]{1,0:T(8,128)}, f32[16,2816]{1,0:T(8,128)}, f32[16,512]{1,0:T(8,128)}, f32[24,128]{1,0:T(8,128)}) custom-call(s32[3]{0:T(128)} %pad_add_fusion.place_ref.refs_0_, f32[16,1024]{1,0:T(8,128)} %slice_bitcast_fusion.4.refs_1_, bf16[16,1024]{1,0:T(8,128)(2,1)} %copy-done.9, bf16[16,1024]{1,0:T(8,128)(2,1)} %copy-done.10, ...), custom_call_target="tpu_custom_call" | custom-call | flops 1000000 | bytes 1000000 | tf_op jit(solution)/shard_map/finish/pallas_call | solution.py:1033
  168.9 1.4 collective-permute-done.37
  170.3 0.8 add_select_fusion.1
  171.0 1.2 collective-permute-start.38
  172.3 0.9 collective-permute-start.39
  173.1 1.4 collective-permute-start.40
  174.7 1.2 collective-permute-done.39
  176.0 1.8 collective-permute-done.40
  177.8 2.6 %collective-permute-start.42 = (f32[24,128]{1,0:T(8,128)S(1)}, f32[24,128]{1,0:T(8,128)S(1)}, u32[]{:S(2)}, u32[]{:S(2)}) collective-permute-start(f32[24,128]{1,0:T(8,128)S(1)} %add_select_fusion.refs_4_), channel_id=1, source_target_pairs={{0,16},{2,18},{4,20},{6,22},{8,24},{10,26},{12,28},{14,30},{16,0},... | collective-permute-start | bytes 36872 | tf_op jit(solution)/shard_map/ppermute | solution.py:698
  180.4 1.8 collective-permute-start.43
  182.5 3.4 %collective-permute-done.43.refs_7_ = f32[24,128]{1,0:T(8,128)S(1)} collective-permute-done((f32[24,128]{1,0:T(8,128)S(1)}, f32[24,128]{1,0:T(8,128)S(1)}, u32[]{:S(2)}, u32[]{:S(2)}) %collective-permute-start.43) | collective-permute-done | bytes 12320 | tf_op jit(solution)/shard_map/ppermute | solution.py:698
  186.5 2.5 %adam.1 = (f32[1,1]{1,0:T(1,128)}, f32[1,1]{1,0:T(1,128)}, f32[1,1]{1,0:T(1,128)}, f32[16,896]{1,0:T(8,128)}, f32[16,896]{1,0:T(8,128)}, /*index=5*/f32[16,896]{...) custom-call(s32[3]{0:T(128)} %pad_add_fusion.place_ref.refs_0_, ...), custom_call_target="tpu_custom_call" | custom-call | flops 1000000 | bytes 1000000 | tf_op jit(solution)/shard_map/adam/pallas_call | solution.py:1071
  (127 shorter events, 12.1 us)
Async XLA Ops:
  3.0 9.4 %collective-permute-start = (bf16[16,2048]{1,0:T(8,128)(2,1)}, bf16[16,2048]{1,0:T(8,128)(2,1)S(1)}, u32[]{:S(2)}, u32[]{:S(2)}) collective-permute-start(bf16[16,2048]{1,0:T(8,128)(2,1)} %get-tuple-element.108.after), channel_id=1, source_target_pairs={{0,8},{2,10},{4,12},{6,14},{8,0},{10,2},{12,4},{14,6},{16,24},{18,... | collective-permute-start | bytes 196616 | tf_op jit(solution)/shard_map/ppermute | solution.py:698
  6.0 7.5 %collective-permute-start.1 = (bf16[16,2048]{1,0:T(8,128)(2,1)}, bf16[16,2048]{1,0:T(8,128)(2,1)S(1)}, u32[]{:S(2)}, u32[]{:S(2)}) collective-permute-start(bf16[16,2048]{1,0:T(8,128)(2,1)} %get-tuple-element.108.after), channel_id=1, source_target_pairs={{0,16},{2,18},{4,20},{6,22},{8,24},{10,26},{12,28},{14,30},{16,0},... | collective-permute-start | bytes 196616 | tf_op jit(solution)/shard_map/ppermute | solution.py:698
  8.6 6.3 %collective-permute-start.2 = (bf16[16,2048]{1,0:T(8,128)(2,1)}, bf16[16,2048]{1,0:T(8,128)(2,1)S(1)}, u32[]{:S(2)}, u32[]{:S(2)}) collective-permute-start(bf16[16,2048]{1,0:T(8,128)(2,1)} %get-tuple-element.108.after), channel_id=1, source_target_pairs={{0,24},{2,26},{4,28},{6,30},{8,16},{10,18},{12,20},{14,22},{16,8},... | collective-permute-start | bytes 196616 | tf_op jit(solution)/shard_map/ppermute | solution.py:698
  15.8 22.7 %copy-start.2 = (bf16[4,16,2048]{2,1,0:T(8,128)(2,1)}, bf16[4,16,2048]{2,1,0:T(8,128)(2,1)S(1)}, u32[]{:S(2)}) copy-start(bf16[4,16,2048]{2,1,0:T(8,128)(2,1)S(1)} %pad_maximum_fusion.4.refs_5_) | copy-start | bytes 786436
  15.8 9.3 %collective-permute-start.4 = (bf16[4,16,2048]{2,1,0:T(8,128)(2,1)S(1)}, bf16[4,16,2048]{2,1,0:T(8,128)(2,1)S(1)}, u32[]{:S(2)}, u32[]{:S(2)}) collective-permute-start(bf16[4,16,2048]{2,1,0:T(8,128)(2,1)S(1)} %pad_maximum_fusion.4.refs_5_), channel_id=1, source_target_pairs={{0,2},{2,0},{4,6},{6,4},{8,10},{10,8},{12,14},{14,12},{16,18},{18,... | collective-permute-start | bytes 786440 | tf_op jit(solution)/shard_map/ppermute | solution.py:698
  17.4 12.1 %collective-permute-start.11 = (bf16[4,16,2048]{2,1,0:T(8,128)(2,1)S(1)}, bf16[4,16,2048]{2,1,0:T(8,128)(2,1)S(1)}, u32[]{:S(2)}, u32[]{:S(2)}) collective-permute-start(bf16[4,16,2048]{2,1,0:T(8,128)(2,1)S(1)} %pad_maximum_fusion.4.refs_5_), channel_id=1, source_target_pairs={{0,4},{2,6},{4,0},{6,2},{8,12},{10,14},{12,8},{14,10},{16,20},{18,... | collective-permute-start | bytes 786440 | tf_op jit(solution)/shard_map/ppermute | solution.py:698
  18.9 10.6 %collective-permute-start.12 = (bf16[4,16,2048]{2,1,0:T(8,128)(2,1)S(1)}, bf16[4,16,2048]{2,1,0:T(8,128)(2,1)S(1)}, u32[]{:S(2)}, u32[]{:S(2)}) collective-permute-start(bf16[4,16,2048]{2,1,0:T(8,128)(2,1)S(1)} %pad_maximum_fusion.4.refs_5_), channel_id=1, source_target_pairs={{0,6},{2,4},{4,2},{6,0},{8,14},{10,12},{12,10},{14,8},{16,22},{18,... | collective-permute-start | bytes 786440 | tf_op jit(solution)/shard_map/ppermute | solution.py:698
  25.1 13.5 %copy-start.15 = (bf16[4,16,2048]{2,1,0:T(8,128)(2,1)}, bf16[4,16,2048]{2,1,0:T(8,128)(2,1)S(1)}, u32[]{:S(2)}) copy-start(bf16[4,16,2048]{2,1,0:T(8,128)(2,1)S(1)} %collective-permute-done.4.refs_6_) | copy-start | bytes 786436
  25.1 4.9 %collective-permute-start.5 = (bf16[16,1792]{1,0:T(8,128)(2,1)}, bf16[16,1792]{1,0:T(8,128)(2,1)S(1)}, u32[]{:S(2)}, u32[]{:S(2)}) collective-permute-start(bf16[16,1792]{1,0:T(8,128)(2,1)} %get-tuple-element.112), channel_id=1, source_target_pairs={{0,8},{2,10},{4,12},{6,14},{8,0},{10,2},{12,4},{14,6},{16,24},{18,... | collective-permute-start | bytes 172040 | tf_op jit(solution)/shard_map/ppermute | solution.py:698
  25.1 5.3 %collective-permute-start.6 = (bf16[16,1792]{1,0:T(8,128)(2,1)}, bf16[16,1792]{1,0:T(8,128)(2,1)S(1)}, u32[]{:S(2)}, u32[]{:S(2)}) collective-permute-start(bf16[16,1792]{1,0:T(8,128)(2,1)} %get-tuple-element.112), channel_id=1, source_target_pairs={{0,16},{2,18},{4,20},{6,22},{8,24},{10,26},{12,28},{14,30},{16,0},... | collective-permute-start | bytes 172040 | tf_op jit(solution)/shard_map/ppermute | solution.py:698
  27.5 6.2 %collective-permute-start.7 = (bf16[16,1792]{1,0:T(8,128)(2,1)}, bf16[16,1792]{1,0:T(8,128)(2,1)S(1)}, u32[]{:S(2)}, u32[]{:S(2)}) collective-permute-start(bf16[16,1792]{1,0:T(8,128)(2,1)} %get-tuple-element.112), channel_id=1, source_target_pairs={{0,24},{2,26},{4,28},{6,30},{8,16},{10,18},{12,20},{14,22},{16,8},... | collective-permute-start | bytes 172040 | tf_op jit(solution)/shard_map/ppermute | solution.py:698
  29.5 9.1 %copy-start.16 = (bf16[4,16,2048]{2,1,0:T(8,128)(2,1)}, bf16[4,16,2048]{2,1,0:T(8,128)(2,1)S(1)}, u32[]{:S(2)}) copy-start(bf16[4,16,2048]{2,1,0:T(8,128)(2,1)S(1)} %collective-permute-done.11.refs_7_) | copy-start | bytes 786436
  29.5 8.0 %collective-permute-start.13 = (bf16[4,16,2048]{2,1,0:T(8,128)(2,1)S(1)}, bf16[4,16,2048]{2,1,0:T(8,128)(2,1)S(1)}, u32[]{:S(2)}, u32[]{:S(2)}) collective-permute-start(bf16[4,16,2048]{2,1,0:T(8,128)(2,1)S(1)} %pad_maximum_fusion.4.refs_5_), channel_id=1, source_target_pairs={{0,1},{1,0},{2,3},{3,2},{4,5},{5,4},{6,7},{7,6},{8,9},{9,8},{10,11... | collective-permute-start | bytes 786440 | tf_op jit(solution)/shard_map/ppermute | solution.py:698
  29.5 8.5 %collective-permute-start.14 = (bf16[4,16,2048]{2,1,0:T(8,128)(2,1)S(1)}, bf16[4,16,2048]{2,1,0:T(8,128)(2,1)S(1)}, u32[]{:S(2)}, u32[]{:S(2)}) collective-permute-start(bf16[4,16,2048]{2,1,0:T(8,128)(2,1)S(1)} %collective-permute-done.4.refs_6_), channel_id=1, source_target_pairs={{0,1},{1,0},{2,3},{3,2},{4,5},{5,4},{6,7},{7,6},{8,9},{9,8},{10,11... | collective-permute-start | bytes 786440 | tf_op jit(solution)/shard_map/ppermute | solution.py:698
  30.0 8.5 %collective-permute-start.15 = (bf16[4,16,2048]{2,1,0:T(8,128)(2,1)S(1)}, bf16[4,16,2048]{2,1,0:T(8,128)(2,1)S(1)}, u32[]{:S(2)}, u32[]{:S(2)}) collective-permute-start(bf16[4,16,2048]{2,1,0:T(8,128)(2,1)S(1)} %collective-permute-done.11.refs_7_), channel_id=1, source_target_pairs={{0,1},{1,0},{2,3},{3,2},{4,5},{5,4},{6,7},{7,6},{8,9},{9,8},{10,11... | collective-permute-start | bytes 786440 | tf_op jit(solution)/shard_map/ppermute | solution.py:698
  30.4 8.1 %collective-permute-start.16 = (bf16[4,16,2048]{2,1,0:T(8,128)(2,1)S(1)}, bf16[4,16,2048]{2,1,0:T(8,128)(2,1)S(1)}, u32[]{:S(2)}, u32[]{:S(2)}) collective-permute-start(bf16[4,16,2048]{2,1,0:T(8,128)(2,1)S(1)} %collective-permute-done.12.refs_8_), channel_id=1, source_target_pairs={{0,1},{1,0},{2,3},{3,2},{4,5},{5,4},{6,7},{7,6},{8,9},{9,8},{10,11... | collective-permute-start | bytes 786440 | tf_op jit(solution)/shard_map/ppermute | solution.py:698
  33.6 1.4 collective-permute-start.3
  34.5 25.9 %copy-start.3 = (bf16[4,16,1792]{2,1,0:T(8,128)(2,1)}, bf16[4,16,1792]{2,1,0:T(8,128)(2,1)S(1)}, u32[]{:S(2)}) copy-start(bf16[4,16,1792]{2,1,0:T(8,128)(2,1)S(1)} %pad_maximum_fusion.5.refs_7_) | copy-start | bytes 688132
  35.0 25.4 %collective-permute-start.10 = (bf16[4,16,1792]{2,1,0:T(8,128)(2,1)S(1)}, bf16[4,16,1792]{2,1,0:T(8,128)(2,1)S(1)}, u32[]{:S(2)}, u32[]{:S(2)}) collective-permute-start(bf16[4,16,1792]{2,1,0:T(8,128)(2,1)S(1)} %pad_maximum_fusion.5.refs_7_), channel_id=1, source_target_pairs={{0,6},{2,4},{4,2},{6,0},{8,14},{10,12},{12,10},{14,8},{16,22},{18,... | collective-permute-start | bytes 688136 | tf_op jit(solution)/shard_map/ppermute | solution.py:698
  37.5 23.0 %collective-permute-start.8 = (bf16[4,16,1792]{2,1,0:T(8,128)(2,1)S(1)}, bf16[4,16,1792]{2,1,0:T(8,128)(2,1)S(1)}, u32[]{:S(2)}, u32[]{:S(2)}) collective-permute-start(bf16[4,16,1792]{2,1,0:T(8,128)(2,1)S(1)} %pad_maximum_fusion.5.refs_7_), channel_id=1, source_target_pairs={{0,2},{2,0},{4,6},{6,4},{8,10},{10,8},{12,14},{14,12},{16,18},{18,... | collective-permute-start | bytes 688136 | tf_op jit(solution)/shard_map/ppermute | solution.py:698
  38.0 22.4 %collective-permute-start.9 = (bf16[4,16,1792]{2,1,0:T(8,128)(2,1)S(1)}, bf16[4,16,1792]{2,1,0:T(8,128)(2,1)S(1)}, u32[]{:S(2)}, u32[]{:S(2)}) collective-permute-start(bf16[4,16,1792]{2,1,0:T(8,128)(2,1)S(1)} %pad_maximum_fusion.5.refs_7_), channel_id=1, source_target_pairs={{0,4},{2,6},{4,0},{6,2},{8,12},{10,14},{12,8},{14,10},{16,20},{18,... | collective-permute-start | bytes 688136 | tf_op jit(solution)/shard_map/ppermute | solution.py:698
  38.5 22.6 %collective-permute-start.17 = (bf16[4,16,1792]{2,1,0:T(8,128)(2,1)S(1)}, bf16[4,16,1792]{2,1,0:T(8,128)(2,1)S(1)}, u32[]{:S(2)}, u32[]{:S(2)}) collective-permute-start(bf16[4,16,1792]{2,1,0:T(8,128)(2,1)S(1)} %pad_maximum_fusion.5.refs_7_), channel_id=1, source_target_pairs={{0,1},{1,0},{2,3},{3,2},{4,5},{5,4},{6,7},{7,6},{8,9},{9,8},{10,11... | collective-permute-start | bytes 688136 | tf_op jit(solution)/shard_map/ppermute | solution.py:698
  60.5 1.6 collective-permute-start.18
  60.5 1.8 collective-permute-start.19
  61.0 1.6 collective-permute-start.20
  109.5 13.7 %collective-permute-start.21 = (bf16[4,4,16,1792]{3,2,1,0:T(8,128)(2,1)}, bf16[4,4,16,1792]{3,2,1,0:T(8,128)(2,1)S(1)}, u32[]{:S(2)}, u32[]{:S(2)}) collective-permute-start(bf16[4,4,16,1792]{3,2,1,0:T(8,128)(2,1)} %get-tuple-element.121), channel_id=1, source_target_pairs={{0,1},{1,0},{2,3},{3,2},{4,5},{5,4},{6,7},{7,6},{8,9},{9,8},{10,11... | collective-permute-start | bytes 2752520 | tf_op jit(solution)/shard_map/ppermute | solution.py:698
  119.7 2.2 %collective-permute-start.22 = (bf16[4,4,16,1024]{3,2,1,0:T(8,128)(2,1)}, bf16[4,4,16,1024]{3,2,1,0:T(8,128)(2,1)S(1)}, u32[]{:S(2)}, u32[]{:S(2)}) collective-permute-start(bf16[4,4,16,1024]{3,2,1,0:T(8,128)(2,1)} %get-tuple-element.130), channel_id=1, source_target_pairs={{0,1},{1,0},{2,3},{3,2},{4,5},{5,4},{6,7},{7,6},{8,9},{9,8},{10,11... | collective-permute-start | bytes 1572872 | tf_op jit(solution)/shard_map/ppermute | solution.py:698
  123.4 22.2 %collective-permute-start.25 = (bf16[4,16,2816]{2,1,0:T(8,128)(2,1)S(1)}, bf16[4,16,2816]{2,1,0:T(8,128)(2,1)S(1)}, u32[]{:S(2)}, u32[]{:S(2)}) collective-permute-start(bf16[4,16,2816]{2,1,0:T(8,128)(2,1)S(1)} %pad_maximum_fusion.3), channel_id=1, source_target_pairs={{0,6},{2,4},{4,2},{6,0},{8,14},{10,12},{12,10},{14,8},{16,22},{18,... | collective-permute-start | bytes 1081352 | tf_op jit(solution)/shard_map/ppermute | solution.py:698
  126.0 19.7 %collective-permute-start.24 = (bf16[4,16,2816]{2,1,0:T(8,128)(2,1)S(1)}, bf16[4,16,2816]{2,1,0:T(8,128)(2,1)S(1)}, u32[]{:S(2)}, u32[]{:S(2)}) collective-permute-start(bf16[4,16,2816]{2,1,0:T(8,128)(2,1)S(1)} %pad_maximum_fusion.2), channel_id=1, source_target_pairs={{0,4},{2,6},{4,0},{6,2},{8,12},{10,14},{12,8},{14,10},{16,20},{18,... | collective-permute-start | bytes 1081352 | tf_op jit(solution)/shard_map/ppermute | solution.py:698
  126.6 19.1 %collective-permute-start.23 = (bf16[4,16,2816]{2,1,0:T(8,128)(2,1)S(1)}, bf16[4,16,2816]{2,1,0:T(8,128)(2,1)S(1)}, u32[]{:S(2)}, u32[]{:S(2)}) collective-permute-start(bf16[4,16,2816]{2,1,0:T(8,128)(2,1)S(1)} %pad_maximum_fusion.1), channel_id=1, source_target_pairs={{0,2},{2,0},{4,6},{6,4},{8,10},{10,8},{12,14},{14,12},{16,18},{18,... | collective-permute-start | bytes 1081352 | tf_op jit(solution)/shard_map/ppermute | solution.py:698
  145.6 3.0 %collective-permute-start.26 = (bf16[4,4,16,1024]{3,2,1,0:T(8,128)(2,1)}, bf16[4,4,16,1024]{3,2,1,0:T(8,128)(2,1)S(1)}, u32[]{:S(2)}, u32[]{:S(2)}) collective-permute-start(bf16[4,4,16,1024]{3,2,1,0:T(8,128)(2,1)} %get-tuple-element.141), channel_id=1, source_target_pairs={{0,1},{1,0},{2,3},{3,2},{4,5},{5,4},{6,7},{7,6},{8,9},{9,8},{10,11... | collective-permute-start | bytes 1572872 | tf_op jit(solution)/shard_map/ppermute | solution.py:698
  145.9 14.7 %collective-permute-start.33 = (bf16[16,2816]{1,0:T(8,128)(2,1)S(1)}, bf16[16,2816]{1,0:T(8,128)(2,1)S(1)}, u32[]{:S(2)}, u32[]{:S(2)}) collective-permute-start(bf16[16,2816]{1,0:T(8,128)(2,1)S(1)} %get-tuple-element.197), channel_id=1, source_target_pairs={{0,8},{2,10},{4,12},{6,14},{8,0},{10,2},{12,4},{14,6},{16,24},{18,... | collective-permute-start | bytes 270344 | tf_op jit(solution)/shard_map/ppermute | solution.py:698
  146.0 17.3 %collective-permute-start.34 = (bf16[16,2816]{1,0:T(8,128)(2,1)S(1)}, bf16[16,2816]{1,0:T(8,128)(2,1)S(1)}, u32[]{:S(2)}, u32[]{:S(2)}) collective-permute-start(bf16[16,2816]{1,0:T(8,128)(2,1)S(1)} %get-tuple-element.196), channel_id=1, source_target_pairs={{0,16},{2,18},{4,20},{6,22},{8,24},{10,26},{12,28},{14,30},{16,0},... | collective-permute-start | bytes 270344 | tf_op jit(solution)/shard_map/ppermute | solution.py:698
  148.7 5.8 %collective-permute-start.27 = (bf16[4,16,1024]{2,1,0:T(8,128)(2,1)S(1)}, bf16[4,16,1024]{2,1,0:T(8,128)(2,1)S(1)}, u32[]{:S(2)}, u32[]{:S(2)}) collective-permute-start(bf16[4,16,1024]{2,1,0:T(8,128)(2,1)S(1)} %get-tuple-element.188), channel_id=1, source_target_pairs={{0,2},{2,0},{4,6},{6,4},{8,10},{10,8},{12,14},{14,12},{16,18},{18,... | collective-permute-start | bytes 393224 | tf_op jit(solution)/shard_map/ppermute | solution.py:698
  150.2 7.8 %collective-permute-start.28 = (bf16[4,16,1024]{2,1,0:T(8,128)(2,1)S(1)}, bf16[4,16,1024]{2,1,0:T(8,128)(2,1)S(1)}, u32[]{:S(2)}, u32[]{:S(2)}) collective-permute-start(bf16[4,16,1024]{2,1,0:T(8,128)(2,1)S(1)} %get-tuple-element.190), channel_id=1, source_target_pairs={{0,4},{2,6},{4,0},{6,2},{8,12},{10,14},{12,8},{14,10},{16,20},{18,... | collective-permute-start | bytes 393224 | tf_op jit(solution)/shard_map/ppermute | solution.py:698
  151.7 6.3 %collective-permute-start.29 = (bf16[4,16,1024]{2,1,0:T(8,128)(2,1)S(1)}, bf16[4,16,1024]{2,1,0:T(8,128)(2,1)S(1)}, u32[]{:S(2)}, u32[]{:S(2)}) collective-permute-start(bf16[4,16,1024]{2,1,0:T(8,128)(2,1)S(1)} %get-tuple-element.189), channel_id=1, source_target_pairs={{0,6},{2,4},{4,2},{6,0},{8,14},{10,12},{12,10},{14,8},{16,22},{18,... | collective-permute-start | bytes 393224 | tf_op jit(solution)/shard_map/ppermute | solution.py:698
  154.4 8.9 %collective-permute-start.35 = (bf16[16,2816]{1,0:T(8,128)(2,1)S(1)}, bf16[16,2816]{1,0:T(8,128)(2,1)S(1)}, u32[]{:S(2)}, u32[]{:S(2)}) collective-permute-start(bf16[16,2816]{1,0:T(8,128)(2,1)S(1)} %get-tuple-element.195), channel_id=1, source_target_pairs={{0,24},{2,26},{4,28},{6,30},{8,16},{10,18},{12,20},{14,22},{16,8},... | collective-permute-start | bytes 270344 | tf_op jit(solution)/shard_map/ppermute | solution.py:698
  158.2 5.1 %collective-permute-start.30 = (bf16[16,1024]{1,0:T(8,128)(2,1)S(1)}, bf16[16,1024]{1,0:T(8,128)(2,1)S(1)}, u32[]{:S(2)}, u32[]{:S(2)}) collective-permute-start(bf16[16,1024]{1,0:T(8,128)(2,1)S(1)} %get-tuple-element.200), channel_id=1, source_target_pairs={{0,8},{2,10},{4,12},{6,14},{8,0},{10,2},{12,4},{14,6},{16,24},{18,... | collective-permute-start | bytes 98312 | tf_op jit(solution)/shard_map/ppermute | solution.py:698
  158.6 5.2 %collective-permute-start.31 = (bf16[16,1024]{1,0:T(8,128)(2,1)S(1)}, bf16[16,1024]{1,0:T(8,128)(2,1)S(1)}, u32[]{:S(2)}, u32[]{:S(2)}) collective-permute-start(bf16[16,1024]{1,0:T(8,128)(2,1)S(1)} %get-tuple-element.199), channel_id=1, source_target_pairs={{0,16},{2,18},{4,20},{6,22},{8,24},{10,26},{12,28},{14,30},{16,0},... | collective-permute-start | bytes 98312 | tf_op jit(solution)/shard_map/ppermute | solution.py:698
  160.6 5.7 %collective-permute-start.32 = (bf16[16,1024]{1,0:T(8,128)(2,1)S(1)}, bf16[16,1024]{1,0:T(8,128)(2,1)S(1)}, u32[]{:S(2)}, u32[]{:S(2)}) collective-permute-start(bf16[16,1024]{1,0:T(8,128)(2,1)S(1)} %get-tuple-element.198), channel_id=1, source_target_pairs={{0,24},{2,26},{4,28},{6,30},{8,16},{10,18},{12,20},{14,22},{16,8},... | collective-permute-start | bytes 98312 | tf_op jit(solution)/shard_map/ppermute | solution.py:698
  168.9 1.4 collective-permute-start.37
  171.0 3.7 %collective-permute-start.38 = (f32[24,128]{1,0:T(8,128)S(1)}, f32[24,128]{1,0:T(8,128)S(1)}, u32[]{:S(2)}, u32[]{:S(2)}) collective-permute-start(f32[24,128]{1,0:T(8,128)S(1)} %add_select_fusion.1), channel_id=1, source_target_pairs={{0,2},{2,0},{4,6},{6,4},{8,10},{10,8},{12,14},{14,12},{16,18},{18,... | collective-permute-start | bytes 36872 | tf_op jit(solution)/shard_map/ppermute | solution.py:698
  172.3 3.7 %collective-permute-start.39 = (f32[24,128]{1,0:T(8,128)S(1)}, f32[24,128]{1,0:T(8,128)S(1)}, u32[]{:S(2)}, u32[]{:S(2)}) collective-permute-start(f32[24,128]{1,0:T(8,128)S(1)} %add_select_fusion.1), channel_id=1, source_target_pairs={{0,4},{2,6},{4,0},{6,2},{8,12},{10,14},{12,8},{14,10},{16,20},{18,... | collective-permute-start | bytes 36872 | tf_op jit(solution)/shard_map/ppermute | solution.py:698
  173.1 4.6 %collective-permute-start.40 = (f32[24,128]{1,0:T(8,128)S(1)}, f32[24,128]{1,0:T(8,128)S(1)}, u32[]{:S(2)}, u32[]{:S(2)}) collective-permute-start(f32[24,128]{1,0:T(8,128)S(1)} %add_select_fusion.1), channel_id=1, source_target_pairs={{0,6},{2,4},{4,2},{6,0},{8,14},{10,12},{12,10},{14,8},{16,22},{18,... | collective-permute-start | bytes 36872 | tf_op jit(solution)/shard_map/ppermute | solution.py:698
  174.5 7.7 %collective-permute-start.36 = (f32[16,512]{1,0:T(8,128)}, f32[16,512]{1,0:T(8,128)S(1)}, u32[]{:S(2)}, u32[]{:S(2)}) collective-permute-start(f32[16,512]{1,0:T(8,128)} %get-tuple-element.148), channel_id=1, source_target_pairs={{0,1},{1,0},{2,3},{3,2},{4,5},{5,4},{6,7},{7,6},{8,9},{9,8},{10,11... | collective-permute-start | bytes 98312 | tf_op jit(solution)/shard_map/ppermute | solution.py:698
  177.8 4.4 %collective-permute-start.41 = (f32[24,128]{1,0:T(8,128)S(1)}, f32[24,128]{1,0:T(8,128)S(1)}, u32[]{:S(2)}, u32[]{:S(2)}) collective-permute-start(f32[24,128]{1,0:T(8,128)S(1)} %add_select_fusion.refs_4_), channel_id=1, source_target_pairs={{0,8},{2,10},{4,12},{6,14},{8,0},{10,2},{12,4},{14,6},{16,24},{18,... | collective-permute-start | bytes 36872 | tf_op jit(solution)/shard_map/ppermute | solution.py:698
  177.8 4.7 %collective-permute-start.42 = (f32[24,128]{1,0:T(8,128)S(1)}, f32[24,128]{1,0:T(8,128)S(1)}, u32[]{:S(2)}, u32[]{:S(2)}) collective-permute-start(f32[24,128]{1,0:T(8,128)S(1)} %add_select_fusion.refs_4_), channel_id=1, source_target_pairs={{0,16},{2,18},{4,20},{6,22},{8,24},{10,26},{12,28},{14,30},{16,0},... | collective-permute-start | bytes 36872 | tf_op jit(solution)/shard_map/ppermute | solution.py:698
  180.4 5.5 %collective-permute-start.43 = (f32[24,128]{1,0:T(8,128)S(1)}, f32[24,128]{1,0:T(8,128)S(1)}, u32[]{:S(2)}, u32[]{:S(2)}) collective-permute-start(f32[24,128]{1,0:T(8,128)S(1)} %add_select_fusion.refs_4_), channel_id=1, source_target_pairs={{0,24},{2,26},{4,28},{6,30},{8,16},{10,18},{12,20},{14,22},{16,8},... | collective-permute-start | bytes 36872 | tf_op jit(solution)/shard_map/ppermute | solution.py:698
  (26 other events, 70.4 us)

commit v4 on v3

v4 whole, which is shorter than its diff:
```python
import functools

import jax
import jax.numpy as jnp
from jax import lax
from jax.experimental import pallas as pl
from jax.experimental.pallas import tpu as pltpu
from jax.sharding import PartitionSpec as P

D = 256
HEADS = 4
HEAD_DIM = 64
FF = 1024
VOCAB = 512
ACTIONS = 18
GAMES = 26
OBS = 16
FRAMES = 20
STEP_NUMBER = 5
FRAME_TOKENS = 17
LENGTH = 340
ROWS = 896
NVEC = 14

EPS_NORM = 1e-05
BETA_ONE = 0.5
BETA_TWO = 0.5
RATE_TABLE = 0.5
RATE_MATRIX = 0.05
RATE_VECTOR = 0.2
DECAY_RATE = 0.01
EPS_ADAM = 1e-08
CLIP_AT = 0.1

SEQ = 352
KEYS = 384
BLOCK, BLOCKS = 128, 3
TILE = 32
SIDE_ROWS = 32
QUERIES = HEADS * BLOCK
VALUE_ROWS = 80

COL_QKV, COL_PROJ, COL_UP, COL_DOWN, COL_LAYER = 0, 768, 1024, 2048, 3072
HALF_ATTENTION = ((0, 128, 0), (128, 128, 256), (256, 128, 512), (384, 128, COL_PROJ))
HALF_LAYER = HALF_ATTENTION + ((512, 512, COL_UP), (1024, 512, COL_DOWN))
COL_TABLE, COL_SMALL, COL_FIRST = 3072, 3968, 4096
HALF_FIRST = HALF_LAYER + ((1536, 512, COL_TABLE),)
HALF_FIRST_COLS = 2048
COL_HEAD, COL_SECOND = 3072, 3584
HALF_SECOND = HALF_LAYER + ((1536, 256, COL_HEAD),)
HALF_SECOND_COLS = 1792
GRAD_UP, GRAD_DOWN = 0, 1024
HALF_GRAD_FF = ((0, 512, GRAD_UP), (512, 512, GRAD_DOWN))
GRAD_TABLE, GRAD_SMALL = 1024, 1920
HALF_GRAD_REST = HALF_ATTENTION + ((512, 512, GRAD_TABLE),)
HALF_GRAD_COLS = 1024
SMALL_ROWS, SMALL_BIAS, SMALL_SIDE = 32, 14, 22

F32, BF16 = jnp.float32, jnp.bfloat16
VMEM_BYTES = 60 * 1024 * 1024


def dot_nn(a, b):
    return lax.dot_general(a, b, (((1,), (0,)), ((), ())), preferred_element_type=F32)


def dot_nt(a, b):
    return lax.dot_general(a, b, (((1,), (1,)), ((), ())), preferred_element_type=F32)


def dot_tn(a, b):
    return lax.dot_general(a, b, (((0,), (0,)), ((), ())), preferred_element_type=F32)


def tiles(rows, size):
    return [slice(first, first + size) for first in range(0, rows, size)]


def normalise(x):
    centred = x - jnp.mean(x, axis=1, keepdims=True)
    scale = lax.rsqrt(jnp.mean(centred * centred, axis=1, keepdims=True) + EPS_NORM)
    return centred * scale, scale


def normalise_back(grad, xhat, scale, gain):
    inner = grad * gain
    mean_one = jnp.mean(inner, axis=1, keepdims=True)
    mean_two = jnp.mean(inner * xhat, axis=1, keepdims=True)
    return scale * (inner - mean_one - xhat * mean_two)


def column_sum(a):
    return jnp.sum(a, axis=0, keepdims=True)


def fold(a):
    return jnp.sum(a.reshape(a.shape[0] // 8, 8, a.shape[1]), axis=0)


def plus(total, a):
    return a if total is None else total + a


def block_lanes(i, h=None):
    if h is None:
        return slice(QUERIES * i, QUERIES * (i + 1))
    return slice(QUERIES * i + BLOCK * h, QUERIES * i + BLOCK * (h + 1))


def head_rows(h):
    return slice(HEAD_DIM * h, HEAD_DIM * (h + 1))


def spread_heads(source, target_ref):
    for h in range(HEADS):
        for i in range(BLOCKS):
            target_ref[head_rows(h), block_lanes(i, h)] = source[
                head_rows(h), BLOCK * i : BLOCK * (i + 1)
            ]


def causal_mask():
    key = lax.broadcasted_iota(jnp.int32, (BLOCK, QUERIES), 0)
    query = lax.broadcasted_iota(jnp.int32, (BLOCK, QUERIES), 1) & (BLOCK - 1)
    return jnp.where(key <= query, 0.0, -1e30)


def assemble(pieces_mine, pieces_other, place_ref, w_ref, halves):
    me, core = place_ref[0], place_ref[1]
    is_first = core == 0
    for p in range(4):

        def block(z, _, p=p):
            row = pl.multiple_of((me ^ (4 * z + p)) * 16, 16)
            for src, width, dest in halves:
                mine = pieces_mine[p][z, :, src : src + width]
                other = pieces_other[p][z, :, src : src + width]
                if dest == COL_QKV:
                    mine, other = mine * 0.125, other * 0.125
                w_ref[pl.ds(row, 16), dest : dest + width] = jnp.where(is_first, mine, other)
                w_ref[pl.ds(row, 16), dest + width : dest + 2 * width] = jnp.where(
                    is_first, other, mine
                )
            return 0

        lax.fori_loop(0, 4, block, 0)


def disperse(g_ref, place_ref, keep_ref, send_ref, halves, scaled=True):
    is_first = place_ref[1] == 0

    def block(i, _):
        p, z = i >> 2, i & 3
        row = pl.multiple_of((4 * z + p) * 16, 16)
        for src, width, dest in halves:
            low = g_ref[pl.ds(row, 16), dest : dest + width]
            high = g_ref[pl.ds(row, 16), dest + width : dest + 2 * width]
            if scaled and dest == COL_QKV:
                low, high = low * 0.125, high * 0.125
            keep_ref[p, z, :, src : src + width] = jnp.where(is_first, low, high)
            send_ref[p, z, :, src : src + width] = jnp.where(is_first, high, low).astype(BF16)
        return 0

    lax.fori_loop(0, 16, block, 0)


def make_hits(meta_ref, hits_ref):
    for rows in tiles(SEQ, TILE):
        lane = lax.broadcasted_iota(jnp.int32, (TILE, ROWS), 1)
        place = lax.broadcasted_iota(jnp.int32, (TILE, 1), 0) + (VOCAB + ACTIONS + GAMES + rows.start)
        meta = meta_ref[rows]
        hit = (lane == meta[:, 0:1]) | (lane == meta[:, 1:2]) | (lane == place)
        hits_ref[rows] = jnp.where(hit, 1.0, 0.0).astype(BF16)


def gelu_and_slope(up):
    up = up.astype(BF16)
    square = up * up
    half = jax.nn.sigmoid(up * (BF16(1.5957691216057308) + BF16(0.0713548162726) * square))
    hidden = up * half
    slope = BF16(1.5957691216057308) + BF16(0.2140644488178) * square
    return hidden, half + hidden * (BF16(1.0) - half) * slope


def layer_forward(x_ref, w_ref, vec, bias, kept, work):
    qt_ref, kv_ref, pt_ref, r_ref, ot_ref, o_ref, m_ref, h_ref, gp_ref, a_ref, c_ref = kept
    qst_ref, vt_ref, mask_ref, wqt_ref, u_ref, y_ref = work
    for rows in tiles(SEQ, TILE):
        a_ref[rows] = (normalise(x_ref[rows])[0] * vec[0:1] + vec[1:2]).astype(BF16)
    a_ref[SEQ:KEYS] = jnp.zeros((KEYS - SEQ, D), BF16)
    kv_ref[0:SEQ] = dot_nn(a_ref[0:SEQ], w_ref[:, 256:768]).astype(BF16)
    kv_ref[SEQ:KEYS] = jnp.zeros((KEYS - SEQ, 512), BF16)
    qt_ref[...] = dot_nt(wqt_ref[...], a_ref[...]).astype(BF16)
    spread_heads(qt_ref, qst_ref)
    turned = jnp.transpose(kv_ref[:, 256:512])
    for h in range(HEADS):
        vt_ref[VALUE_ROWS * h : VALUE_ROWS * h + HEAD_DIM] = turned[head_rows(h)]
    for i in range(BLOCKS):
        seen, first = BLOCK * (i + 1), BLOCK * i
        lanes = block_lanes(i)
        scores = dot_nn(kv_ref[0:seen, 0:256], qst_ref[:, lanes])
        last = scores[first:] + mask_ref[...]
        peak = jnp.max(last, axis=0, keepdims=True)
        if i:
            peak = jnp.maximum(peak, jnp.max(scores[0:first], axis=0, keepdims=True))
            pt_ref[0:first, lanes] = jnp.exp(scores[0:first] - peak).astype(BF16)
        pt_ref[first:seen, lanes] = jnp.exp(last - peak).astype(BF16)
        for h in range(HEADS):
            values = vt_ref[VALUE_ROWS * h : VALUE_ROWS * (h + 1), 0:seen]
            out = dot_nn(values, pt_ref[0:seen, block_lanes(i, h)])
            inverse = 1.0 / out[HEAD_DIM : HEAD_DIM + 1]
            r_ref[h : h + 1, first:seen] = inverse
            ot_ref[head_rows(h), first:seen] = (out[0:HEAD_DIM] * inverse).astype(BF16)
    o_ref[...] = jnp.transpose(ot_ref[...])[0:SEQ]
    y_ref[...] = dot_nt(o_ref[...], w_ref[:, COL_PROJ : COL_PROJ + 256])
    for rows in tiles(SEQ, TILE):
        middle = x_ref[rows] + (y_ref[rows] + vec[2:3])
        m_ref[rows] = middle
        c_ref[rows] = (normalise(middle)[0] * vec[3:4] + vec[4:5]).astype(BF16)
    u_ref[...] = dot_nn(c_ref[...], w_ref[:, COL_UP : COL_UP + FF])
    for rows in tiles(SEQ, TILE):
        for first in range(0, FF, 256):
            cols = slice(first, first + 256)
            h_ref[rows, cols], gp_ref[rows, cols] = gelu_and_slope(u_ref[rows, cols] + bias[:, cols])
    y_ref[...] = dot_nt(h_ref[...], w_ref[:, COL_DOWN : COL_DOWN + FF])


def add_gradient(g_ref, column, left, right):
    g_ref[:, column : column + right.shape[1]] += dot_tn(left, right)


def ff_backward(grad_ref, grad16_ref, w_ref, vec, kept, g_ref, g_up, g_down, v_ref, v_row, bias_row, work, mid_ref, mid16_ref):
    m_ref, h_ref, gp_ref, c_ref = kept
    du_ref, ones_ref, u_ref, y_ref = work
    u_ref[...] = dot_nn(grad16_ref[...], w_ref[:, COL_DOWN : COL_DOWN + FF])
    for rows in tiles(SEQ, TILE):
        du_ref[rows] = u_ref[rows].astype(BF16) * gp_ref[rows]
    add_gradient(g_ref, g_down, grad16_ref[...], h_ref[...])
    add_gradient(g_ref, g_up, c_ref[...], du_ref[...])
    bias_grad = dot_nn(ones_ref[...], du_ref[...])
    for chunk in range(4):
        v_ref[bias_row + chunk, 0:1] += bias_grad[0:1, 256 * chunk : 256 * chunk + 256]
    y_ref[...] = dot_nt(du_ref[...], w_ref[:, COL_UP : COL_UP + FF])
    totals = [None] * 3
    for rows in tiles(SEQ, TILE):
        xhat, scale = normalise(m_ref[rows])
        grad = y_ref[rows]
        mid = grad_ref[rows] + normalise_back(grad, xhat, scale, vec[3:4])
        mid_ref[rows] = mid
        if mid16_ref is not None:
            mid16_ref[rows] = mid.astype(BF16)
        for i, a in enumerate((mid, grad * xhat, grad)):
            totals[i] = plus(totals[i], fold(a))
    for i in range(3):
        v_ref[v_row + 2 + i] += totals[i]


def attention_backward(mid_ref, mid16_ref, w_ref, vec, kept, g_ref, v_ref, v_row, work, out_ref):
    x_ref, qt_ref, kv_ref, pt_ref, r_ref, ot_ref, o_ref, a_ref = kept
    dost_ref, qst_ref, kt_ref, dst_ref, dqt_ref, dkv_ref, dqkv_ref, proj_ref, y_ref = work
    add_gradient(g_ref, COL_PROJ, mid16_ref[0:SEQ], o_ref[...])
    grad_o = dot_nt(proj_ref[...], mid16_ref[...]).astype(BF16).astype(F32)
    kt_ref[...] = jnp.transpose(kv_ref[:, 0:256])
    deltas = []
    for h in range(HEADS):
        scaled = grad_o[head_rows(h)] * r_ref[h : h + 1]
        deltas.append(column_sum(scaled * ot_ref[head_rows(h)].astype(F32)))
        scaled = scaled.astype(BF16)
        for i in range(BLOCKS):
            dost_ref[head_rows(h), block_lanes(i, h)] = scaled[:, BLOCK * i : BLOCK * (i + 1)]
    for i in range(BLOCKS):
        seen, first = BLOCK * (i + 1), BLOCK * i
        lanes = block_lanes(i)
        delta = jnp.concatenate([a[:, first:seen] for a in deltas], axis=1)
        grad = dot_nn(kv_ref[0:seen, 256:512], dost_ref[:, lanes])
        dst_ref[0:seen, lanes] = pt_ref[0:seen, lanes] * (grad - delta).astype(BF16)
        for h in range(HEADS):
            out = dot_nn(kt_ref[head_rows(h), 0:seen], dst_ref[0:seen, block_lanes(i, h)])
            dqt_ref[head_rows(h), first:seen] = out.astype(BF16)
        for at, left, right in ((0, dst_ref, qst_ref), (256, pt_ref, dost_ref)):
            out = dot_nt(left[0:seen, lanes], right[:, lanes])
            if i:
                dkv_ref[0:first, at : at + 256] += out[0:first]
            dkv_ref[first:seen, at : at + 256] = out[first:]
    dqkv_ref[:, 0:256] = jnp.transpose(dqt_ref[...])[0:SEQ]
    dqkv_ref[:, 256:768] = dkv_ref[0:SEQ].astype(BF16)
    add_gradient(g_ref, COL_QKV, a_ref[0:SEQ], dqkv_ref[...])
    y_ref[...] = dot_nt(dqkv_ref[...], w_ref[:, COL_QKV : COL_QKV + 768])
    totals = [None] * 2
    for rows in tiles(SEQ, TILE):
        xhat, scale = normalise(x_ref[rows])
        grad = y_ref[rows]
        out = mid_ref[rows] + normalise_back(grad, xhat, scale, vec[0:1])
        out_ref[rows] = out.astype(out_ref.dtype)
        for i, a in enumerate((grad * xhat, grad)):
            totals[i] = plus(totals[i], fold(a))
    for i in range(2):
        v_ref[v_row + i] += totals[i]


def own_bias(place_ref, mine, other):
    is_first = place_ref[1] == 0
    return jnp.concatenate(
        [jnp.where(is_first, mine, other), jnp.where(is_first, other, mine)], axis=1
    )


def prepare_kernel(
    place_ref, games_ref, tokens, actions, valid, rewards, ends, after, out, out_side, x_ref
):
    count = out.shape[0]
    frames = tokens.shape[2]
    base = place_ref[1] * count
    row = lax.broadcasted_iota(jnp.int32, (SEQ, frames), 0)
    start = lax.broadcasted_iota(jnp.int32, (SEQ, frames), 1) * FRAME_TOKENS
    here = jnp.where((row >= start) & (row < start + FRAME_TOKENS), 1.0, 0.0).astype(BF16)
    coming = jnp.where((row >= start - FRAME_TOKENS) & (row < start), 1.0, 0.0).astype(BF16)
    passed = jnp.sum(jnp.where(row >= start + FRAME_TOKENS, 1, 0), axis=1, keepdims=True)
    place = lax.broadcasted_iota(jnp.int32, (SEQ, 1), 0)
    spot = place - passed * FRAME_TOKENS
    lane = lax.broadcasted_iota(jnp.int32, (SEQ, 24), 1)
    wide_lane = lax.broadcasted_iota(jnp.int32, (SEQ, 128), 1)
    inside = place < LENGTH
    one_frame = (
        lax.broadcasted_iota(jnp.int32, (SIDE_ROWS, frames), 0)
        == lax.broadcasted_iota(jnp.int32, (SIDE_ROWS, frames), 1)
    )
    one_frame = jnp.where(one_frame, 1.0, 0.0).astype(BF16)
    side_lane = lax.broadcasted_iota(jnp.int32, (SIDE_ROWS, 128), 1)
    x_ref[...] = jnp.zeros(x_ref.shape, jnp.int32)
    for s in range(count):
        x_ref[0:OBS] = tokens[base + s]
        x_ref[16:17] = actions[pl.ds(base + s, 1)] + VOCAB
        x_ref[17:18] = valid[pl.ds(base + s, 1)]
        x_ref[18:19] = rewards[pl.ds(base + s, 1)]
        x_ref[19:20] = ends[pl.ds(base + s, 1)] + 3
        high = (x_ref[...] >> 4).astype(F32).astype(BF16)
        low = (x_ref[...] & 15).astype(F32).astype(BF16)
        now = dot_nt(here, high) * 16.0 + dot_nt(here, low)
        soon = dot_nt(coming, high) * 16.0 + dot_nt(coming, low)

        def pick(condition, a):
            return jnp.sum(jnp.where(condition, a, 0.0), axis=1, keepdims=True).astype(jnp.int32)

        ids = jnp.where(inside, pick(lane == spot, now), -1)
        game = jnp.where(inside, games_ref[base + s] + (VOCAB + ACTIONS), -1)
        target = pick((lane == spot + 1) & (spot < 15), now)
        target = target + pick((lane == 0) & (spot == 16), soon)
        weight = pick((lane == 17) & (spot < 15), now) + pick((lane == 17) & (spot == 16), soon)
        result = jnp.zeros((SEQ, 128), jnp.int32)
        for c, column in enumerate((ids, game, target, weight)):
            result = jnp.where(wide_lane == c, column, result)
        out[s] = result
        by_frame = dot_nt(one_frame, high) * 16.0 + dot_nt(one_frame, low)
        result = jnp.zeros((SIDE_ROWS, 128), jnp.int32)
        for c in range(3):
            column = by_frame[:, 17 + c : 18 + c].astype(jnp.int32)
            result = jnp.where(side_lane == c, column, result)
        out_side[s] = result


def start_forward(work, w_ref):
    qst_ref, vt_ref, mask_ref, wqt_ref, u_ref, y_ref = work
    qst_ref[...] = jnp.zeros(qst_ref.shape, BF16)
    vt_ref[...] = jnp.ones(vt_ref.shape, BF16)
    mask_ref[...] = causal_mask()
    wqt_ref[...] = jnp.transpose(w_ref[:, 0:256])


def first_forward_kernel(*refs):
    place_ref, meta_ref, vec_ref, bias_ref, bias_other = refs[0:5]
    mine, other = refs[5:9], refs[9:13]
    w_out, side_out, next_ref, hits_ref, x_ref = refs[13:18]
    kept = [ref.at[0] for ref in refs[18:29]]
    w_ref = refs[29]
    work = refs[30:36]

    @pl.when(pl.program_id(0) == 0)
    def _():
        assemble(mine, other, place_ref, w_ref, HALF_FIRST)
        w_out[...] = w_ref[...]
        side_out[...] = w_ref[:, COL_SMALL:]
        start_forward(work, w_ref)

    make_hits(meta_ref.at[0], hits_ref.at[0])
    x_ref[0] = dot_nt(hits_ref[0], w_ref[:, COL_TABLE : COL_TABLE + ROWS])
    bias = own_bias(place_ref, bias_ref[0:1], bias_other[0:1])
    vec = vec_ref[0:6]
    layer_forward(x_ref.at[0], w_ref, vec, bias, kept, work)
    for rows in tiles(SEQ, TILE):
        next_ref[0, rows] = kept[6][rows] + (work[5][rows] + vec[5:6])


def codebook_losses(logits, meta):
    weight = meta[:, 3:4].astype(F32)
    peak = jnp.max(logits, axis=1, keepdims=True)
    expanded = jnp.exp(logits - peak)
    total = jnp.sum(expanded, axis=1, keepdims=True)
    hit = lax.broadcasted_iota(jnp.int32, logits.shape, 1) == meta[:, 2:3]
    hit = jnp.where(hit, weight, 0.0)
    return weight * (peak + jnp.log(total)), hit, expanded * (weight / total) - hit


def side_losses(side, meta):
    lane = lax.broadcasted_iota(jnp.int32, side.shape, 1)
    is_reward, is_end = lane < 3, (lane == 3) | (lane == 4)
    is_side = lane < 5
    weight = meta[:, 0:1].astype(F32)
    reward_peak = jnp.max(jnp.where(is_reward, side, -1e30), axis=1, keepdims=True)
    end_peak = jnp.max(jnp.where(is_end, side, -1e30), axis=1, keepdims=True)
    shifted = jnp.where(is_side, side - jnp.where(is_reward, reward_peak, end_peak), 0.0)
    expanded = jnp.where(is_side, jnp.exp(shifted), 0.0)
    reward_total = jnp.sum(jnp.where(is_reward, expanded, 0.0), axis=1, keepdims=True)
    end_total = jnp.sum(jnp.where(is_end, expanded, 0.0), axis=1, keepdims=True)
    hit = (lane == meta[:, 1:2]) | (lane == meta[:, 2:3])
    picked = jnp.sum(jnp.where(hit, side, 0.0), axis=1, keepdims=True)
    terms = reward_peak + jnp.log(reward_total) + end_peak + jnp.log(end_total) - picked
    grad = expanded * jnp.where(is_reward, weight / reward_total, weight / end_total)
    return weight * terms, grad - jnp.where(hit, weight, 0.0), weight


def frame_ends(shape, frame_axis):
    frame = lax.broadcasted_iota(jnp.int32, shape, frame_axis)
    row = lax.broadcasted_iota(jnp.int32, shape, 1 - frame_axis)
    hit = (row == frame * FRAME_TOKENS + OBS) & (frame < FRAMES)
    return jnp.where(hit, 1.0, 0.0).astype(BF16)


def middle_kernel(*refs):
    place_ref, meta_ref, frame_ref, vec_ref, bias_ref, bias_other, side_ref, in_ref = refs[0:8]
    mine, other = refs[8:12], refs[12:16]
    grad_ref, keep_ref, send_ref, v_out, scalar_ref = refs[16:21]
    refs = refs[1:]
    w_ref, g_ref, v_ref = refs[20:23]
    kept = refs[23:34]
    qt_ref, kv_ref, pt_ref, r_ref, ot_ref, o_ref, m_ref, h_ref, gp_ref, a_ref, c_ref = kept
    forward_work = refs[34:40]
    u_ref, y_ref = forward_work[4:6]
    backward_work = refs[40:47]
    proj_ref = refs[47]
    du_ref, ones_ref, up_ref, up16_ref, mid_ref, mid16_ref = refs[48:54]
    last_ref, final_ref, logit_ref, dlogit_ref, pick_ref, put_ref = refs[54:60]
    dost_ref = backward_work[0]
    step = pl.program_id(0)

    @pl.when(step == 0)
    def _():
        assemble(mine, other, place_ref, w_ref, HALF_SECOND)
        w_ref[:, COL_SECOND:] = side_ref[...]
        g_ref[...] = jnp.zeros(g_ref.shape, F32)
        v_ref[...] = jnp.zeros(v_ref.shape, F32)
        scalar_ref[...] = jnp.zeros(scalar_ref.shape, F32)
        start_forward(forward_work, w_ref)
        dost_ref[...] = jnp.zeros(dost_ref.shape, BF16)
        proj_ref[...] = jnp.transpose(w_ref[:, COL_PROJ : COL_PROJ + 256])
        ones_ref[...] = jnp.ones(ones_ref.shape, BF16)
        mid16_ref[SEQ:KEYS] = jnp.zeros((KEYS - SEQ, D), BF16)
        pick_ref[...] = frame_ends((SIDE_ROWS, SEQ), 0)
        put_ref[...] = frame_ends((SEQ, SIDE_ROWS), 1)

    x_ref = in_ref.at[0]
    vec = vec_ref[6:12]
    bias = own_bias(place_ref, bias_ref[1:2], bias_other[1:2])
    layer_forward(x_ref, w_ref, vec, bias, kept, forward_work)

    gain, offset = vec_ref[12:13], vec_ref[13:14]
    for rows in tiles(SEQ, TILE):
        last = m_ref[rows] + (y_ref[rows] + vec[5:6])
        last_ref[rows] = last
        final_ref[rows] = (normalise(last)[0] * gain + offset).astype(BF16)
    cols_head = slice(COL_HEAD, COL_HEAD + VOCAB + 128)
    logit_ref[...] = dot_nn(final_ref[...], w_ref[:, COL_HEAD : COL_HEAD + VOCAB])
    logs, picked = None, None
    for rows in tiles(SEQ, TILE):
        logits = logit_ref[rows]
        log, hit, grad = codebook_losses(logits, meta_ref[0, rows])
        dlogit_ref[rows, :VOCAB] = grad.astype(BF16)
        logs, picked = plus(logs, log), plus(picked, fold(hit * logits))
    acting = dot_nn(pick_ref[...], final_ref[...]).astype(BF16)
    side = dot_nn(acting, w_ref[:, COL_HEAD + VOCAB : COL_HEAD + VOCAB + 128])
    side_loss, grad, weight = side_losses(side, frame_ref[0])
    dlogit_ref[:, VOCAB:] = dot_nn(put_ref[...], grad.astype(BF16)).astype(BF16)
    loss = column_sum(logs) + column_sum(side_loss)
    loss = loss - jnp.sum(column_sum(picked), axis=1, keepdims=True)
    valid = column_sum(weight)
    scalar_lane = lax.broadcasted_iota(jnp.int32, (8, 128), 1)
    scalar_row = lax.broadcasted_iota(jnp.int32, (8, 128), 0) == 0
    scalar_ref[...] += jnp.where(
        scalar_row,
        jnp.where(scalar_lane == 0, loss, jnp.where(scalar_lane == 1, valid, 0.0)),
        0.0,
    )
    add_gradient(g_ref, COL_HEAD, final_ref[...], dlogit_ref[...])
    y_ref[...] = dot_nt(dlogit_ref[...], w_ref[:, cols_head])
    totals = [None] * 3
    for rows in tiles(SEQ, TILE):
        xhat, scale = normalise(last_ref[rows])
        grad = y_ref[rows]
        up = normalise_back(grad, xhat, scale, gain)
        up_ref[rows] = up
        up16_ref[rows] = up.astype(BF16)
        for i, a in enumerate((up, grad * xhat, grad)):
            totals[i] = plus(totals[i], fold(a))
    for i in range(3):
        v_ref[11 + i] += totals[i]
    ff_backward(
        up_ref,
        up16_ref,
        w_ref,
        vec,
        (m_ref, h_ref, gp_ref, c_ref),
        g_ref,
        COL_UP,
        COL_DOWN,
        v_ref,
        6,
        SMALL_BIAS + 4,
        (du_ref, ones_ref, u_ref, y_ref),
        mid_ref,
        mid16_ref,
    )
    attention_backward(
        mid_ref,
        mid16_ref,
        w_ref,
        vec,
        (x_ref, qt_ref, kv_ref, pt_ref, r_ref, ot_ref, o_ref, a_ref),
        g_ref,
        v_ref,
        6,
        (dost_ref, forward_work[0]) + tuple(backward_work[2:]) + (proj_ref, y_ref),
        grad_ref.at[0],
    )

    @pl.when(step == pl.num_programs(0) - 1)
    def _():
        disperse(g_ref, place_ref, keep_ref, send_ref, HALF_SECOND)
        side = jnp.transpose(g_ref[:, COL_SECOND:])
        for i in range(5):
            v_ref[SMALL_SIDE + i, 0:1] = side[i : i + 1]
        v_out[...] = v_ref[...]


def ff_backward_kernel(*refs):
    place_ref, vec_ref, w_ref, grad_ref, v_in = refs[0:5]
    kept = [ref.at[0] for ref in refs[5:9]]
    mid_ref, keep_ref, send_ref, v_out = refs[9:13]
    g_ref, v_ref, grad16_ref = refs[13:16]
    work = refs[16:20]
    ones_ref = work[1]
    step = pl.program_id(0)

    @pl.when(step == 0)
    def _():
        g_ref[...] = jnp.zeros(g_ref.shape, F32)
        v_ref[...] = v_in[...]
        ones_ref[...] = jnp.ones(ones_ref.shape, BF16)

    total = None
    for rows in tiles(SEQ, TILE):
        grad = grad_ref[0, rows]
        grad16_ref[rows] = grad.astype(BF16)
        total = plus(total, fold(grad))
    v_ref[5] += total
    ff_backward(
        grad_ref.at[0],
        grad16_ref,
        w_ref,
        vec_ref[0:6],
        kept,
        g_ref,
        GRAD_UP,
        GRAD_DOWN,
        v_ref,
        0,
        SMALL_BIAS,
        work,
        mid_ref.at[0],
        None,
    )

    @pl.when(step == pl.num_programs(0) - 1)
    def _():
        disperse(g_ref, place_ref, keep_ref, send_ref, HALF_GRAD_FF, False)
        v_out[...] = v_ref[...]


def attention_backward_kernel(*refs):
    place_ref, vec_ref, w_ref, mid_ref, hits_ref, v_in = refs[0:6]
    kept = [ref.at[0] for ref in refs[6:14]]
    keep_ref, send_ref, v_out = refs[15:18]
    g_ref, v_ref, mid16_ref, out16_ref = refs[18:22]
    work = refs[22:31]
    dost_ref, qst_ref, proj_ref = work[0], work[1], work[7]
    step = pl.program_id(0)

    @pl.when(step == 0)
    def _():
        g_ref[...] = jnp.zeros(g_ref.shape, F32)
        v_ref[...] = v_in[...]
        dost_ref[...] = jnp.zeros(dost_ref.shape, BF16)
        qst_ref[...] = jnp.zeros(qst_ref.shape, BF16)
        proj_ref[...] = jnp.transpose(w_ref[:, COL_PROJ : COL_PROJ + 256])
        mid16_ref[SEQ:KEYS] = jnp.zeros((KEYS - SEQ, D), BF16)

    spread_heads(kept[1], qst_ref)
    for rows in tiles(SEQ, TILE):
        mid16_ref[rows] = mid_ref[0, rows].astype(BF16)
    attention_backward(
        mid_ref.at[0], mid16_ref, w_ref, vec_ref[0:6], kept, g_ref, v_ref, 0, work, out16_ref
    )
    add_gradient(g_ref, GRAD_TABLE, out16_ref[...], hits_ref[0])

    @pl.when(step == pl.num_programs(0) - 1)
    def _():
        small = jnp.sum(v_ref[...], axis=1)
        v_out[...] = small
        for block in range(16):
            quarter = small[8 * (block // 4) : 8 * (block // 4) + 8]
            g_ref[16 * block : 16 * block + 8, GRAD_SMALL:] = quarter[:, 0:128]
            g_ref[16 * block + 8 : 16 * block + 16, GRAD_SMALL:] = quarter[:, 128:256]
        disperse(g_ref, place_ref, keep_ref, send_ref, HALF_GRAD_REST)


def pack_layer(attn, proj, up, down, layer, out, at):
    for j in range(3):
        out[:, at + 128 * j : at + 128 * j + 128] = attn[layer, j].astype(BF16)
    out[:, at + 384 : at + 512] = proj[layer].astype(BF16)
    out[:, at + 512 : at + 1024] = up[layer].astype(BF16)
    out[:, at + 1024 : at + 1536] = down[layer].astype(BF16)


def pack_kernel(place_ref, table, attn, proj, up, down, head, side, out, pad_ref):
    pack_layer(attn, proj, up, down, 0, out, 0)
    pack_layer(attn, proj, up, down, 1, out, HALF_FIRST_COLS)
    out[:, HALF_FIRST_COLS + 1536 :] = head[...].astype(BF16)
    rows = side.shape[1]
    eye = (
        lax.broadcasted_iota(jnp.int32, (rows, rows), 0)
        == lax.broadcasted_iota(jnp.int32, (rows, rows), 1)
    )
    eye = jnp.where(eye, 1.0, 0.0).astype(BF16)
    pad_ref[...] = jnp.zeros(pad_ref.shape, F32)
    pad_ref[:, 0:5] = dot_nt(eye, side[...].astype(BF16))
    high = jnp.concatenate([table[:, 512:896], pad_ref[...]], axis=1)
    out[:, 1536:2048] = jnp.where(place_ref[1] == 0, table[:, 0:512], high).astype(BF16)


def finish_kernel(place_ref, rest, others, scalar_ref, out_rest, out_other, out_table, out_small):
    square = jnp.zeros((1, 1), F32)
    for pieces, out in ((rest, out_rest), (others, out_other)):
        total = pieces[0].astype(F32)
        for i in range(1, pieces.shape[0]):
            total = total + pieces[i].astype(F32)
        out[...] = total
        square = square + column_sum(jnp.sum(total * total, axis=1, keepdims=True))
    small = out_rest[:, 896:1024]
    extra = column_sum(jnp.sum(small * small, axis=1, keepdims=True))
    square = square - jnp.where(place_ref[1] == 0, 0.0, extra)
    out_table[...] = out_rest[:, 512:1024]
    rows = small.shape[0]
    out_small[0:rows] = small
    lane = lax.broadcasted_iota(jnp.int32, (8, 128), 1)
    top = lax.broadcasted_iota(jnp.int32, (8, 128), 0) == 0
    out_small[rows : rows + 8] = scalar_ref[...] + jnp.where(top & (lane == 2), square, 0.0)


def adam_rule(weight, moment, second, gradient, step_rate, decay_rate):
    moment_new = BETA_ONE * moment + (1.0 - BETA_ONE) * gradient
    second_new = BETA_TWO * second + (1.0 - BETA_TWO) * gradient * gradient
    moment_hat = moment_new / (1.0 - BETA_ONE**STEP_NUMBER)
    second_hat = second_new / (1.0 - BETA_TWO**STEP_NUMBER)
    weight_new = weight - step_rate * (
        moment_hat / (jnp.sqrt(second_hat) + EPS_ADAM) + decay_rate * weight
    )
    return (weight_new, moment_new, second_new)


def adam_kernel(fast, place_ref, rest, others, swapped, gathered, *refs):
    rows = rest.shape[0]
    quarters = [gathered.at[4 * z] for z in range(4)] if fast else [refs[0].at[z] for z in range(4)]
    refs = refs if fast else refs[1:]
    params = [refs[3 * i : 3 * i + 3] for i in range(9)]
    loss_ref, valid_ref, norm_ref = refs[27:30]
    outs = [refs[30 + 3 * i : 33 + 3 * i] for i in range(9)]
    small_ref = refs[57]
    wide = place_ref[2]
    is_first = place_ref[1] == 0
    for z in range(4):
        small_ref[8 * z : 8 * z + 8, 0:128] = quarters[z][0:8]
        small_ref[8 * z : 8 * z + 8, 128:256] = quarters[z][8:16]
    scalars = gathered[0, rows : rows + 1]
    for i in range(1, gathered.shape[0]):
        scalars = scalars + gathered[i, rows : rows + 1]
    small = small_ref[...]
    loss, valid, square = scalars[:, 0:1], scalars[:, 1:2], scalars[:, 2:3]
    square = square + column_sum(jnp.sum(small * small, axis=1, keepdims=True))
    inverse = 1.0 / valid
    norm = jnp.sqrt(square) * inverse
    loss_ref[...], valid_ref[...], norm_ref[...] = loss, valid, norm
    factor = jnp.minimum(1.0, CLIP_AT / (norm + 1e-06)) * inverse
    table, attn, proj, up, bias, down, vectors, head, side = range(9)

    def update(which, index, gradient, step_rate, decay_rate):
        news = adam_rule(
            *(ref[index] for ref in params[which]), factor * gradient, step_rate, decay_rate
        )
        for ref, new in zip(outs[which], news):
            ref[index] = new

    layers = ((rest, others, 1792), (others, others, 512))
    for layer, (attention, feed, at) in enumerate(layers):
        for j in range(3):
            update(attn, (layer, j), attention[:, 128 * j : 128 * j + 128], RATE_MATRIX, DECAY_RATE)
        update(proj, (layer,), attention[:, 384:512], RATE_MATRIX, DECAY_RATE)
        update(up, (layer,), feed[:, at : at + 512], RATE_MATRIX, DECAY_RATE)
        update(down, (layer,), feed[:, at + 512 : at + 1024], RATE_MATRIX, DECAY_RATE)
        for i in range(2):
            low = SMALL_BIAS + 4 * layer + i
            row = jnp.where(is_first, small[low : low + 1], small[low + 2 : low + 3])
            index = (slice(layer, layer + 1), slice(256 * i, 256 * i + 256))
            update(bias, index, row, RATE_VECTOR, 0.0)
    whole = (slice(None), slice(None))
    update(head, whole, others[:, 1536:1792], RATE_MATRIX, DECAY_RATE)
    mine, theirs = rest[:, 512:1024], swapped[:, 0:512]
    low, high = jnp.where(is_first, mine, theirs), jnp.where(is_first, theirs, mine)
    update(table, (slice(None), slice(0, 512)), low, RATE_TABLE, DECAY_RATE)
    update(table, (slice(None), slice(512, 896)), high[:, 0:384], RATE_TABLE, DECAY_RATE)
    update(vectors, whole, small[0:NVEC], RATE_VECTOR, 0.0)
    turned = pltpu.roll(small[SMALL_SIDE : SMALL_SIDE + 8], lax.rem(D - wide * rows, D), 1)
    update(side, whole, turned[0:5, 0:rows], RATE_MATRIX, DECAY_RATE)


def swap(a, axis, distance):
    size = lax.axis_size(axis)
    return lax.ppermute(a, axis, [(i, i ^ distance) for i in range(size)])


def swap_column(piece, n_high):
    return [piece] + [swap(piece, "wide", 4 * k) for k in range(1, n_high)]


def gather_plane(column):
    return [column] + [swap(column, "wide", p) for p in range(1, 4)]


def gather_cores(mine):
    return [swap(a, "narrow", 1) for a in mine]


def in_blocks(parts, wide):
    n_high, rows, cols = parts[0].shape
    if rows == 16:
        return parts
    whole = jnp.stack(parts, axis=1).reshape(4 * n_high, rows, cols)
    whole = whole[wide ^ jnp.arange(4 * n_high)].reshape(4, 4, 16, cols)
    return [whole[:, p] for p in range(4)]


def in_pieces(blocks, n_high):
    if n_high == 4:
        return blocks
    cols = blocks.shape[-1]
    whole = blocks.transpose(1, 0, 2, 3).reshape(n_high, 4, 64 // n_high, cols)
    return whole.transpose(1, 0, 2, 3)


def add_cores(keep, send, n_high):
    keep, send = in_pieces(keep, n_high), in_pieces(send, n_high)
    return keep + swap(send, "narrow", 1).astype(F32)


def exchange(a, groups):
    return lax.all_to_all(a, "wide", 0, 0, axis_index_groups=groups)


def plane_groups(n_high):
    return [[4 * h + p for p in range(4)] for h in range(n_high)]


def column_groups(n_high):
    return [[4 * h + p for h in range(n_high)] for p in range(4)]


def full_spec(a):
    return pl.BlockSpec(a.shape, lambda *_: (0,) * len(a.shape))


def row_spec(shape):
    return pl.BlockSpec((1,) + shape, lambda i: (i,) + (0,) * len(shape))


def shaped(shape, dtype):
    return jax.ShapeDtypeStruct(shape, dtype)


VMEM_SPEC = pl.BlockSpec(memory_space=pltpu.VMEM)
ANY_SPEC = pl.BlockSpec(memory_space=pl.ANY)
SMEM_SPEC = pl.BlockSpec(memory_space=pltpu.SMEM)


def call(kernel, grid, in_specs, out_specs, out_shape, scratch, flops, bytes_accessed, name):
    extra = {"grid": grid} if grid else {}
    return pl.pallas_call(
        kernel,
        in_specs=in_specs,
        out_specs=out_specs,
        out_shape=out_shape,
        scratch_shapes=scratch,
        compiler_params=pltpu.CompilerParams(vmem_limit_bytes=VMEM_BYTES),
        cost_estimate=pl.CostEstimate(
            flops=flops, bytes_accessed=bytes_accessed, transcendentals=0
        ),
        name=name,
        **extra,
    )


KEPT = (
    ((D, KEYS), BF16),
    ((KEYS, 512), BF16),
    ((KEYS, BLOCKS * QUERIES), BF16),
    ((8, KEYS), F32),
    ((D, KEYS), BF16),
    ((SEQ, D), BF16),
    ((SEQ, D), F32),
    ((SEQ, FF), BF16),
    ((SEQ, FF), BF16),
    ((KEYS, D), BF16),
    ((SEQ, D), BF16),
)
FORWARD_WORK = [
    pltpu.VMEM((D, BLOCKS * QUERIES), BF16),
    pltpu.VMEM((HEADS * VALUE_ROWS, KEYS), BF16),
    pltpu.VMEM((BLOCK, QUERIES), F32),
    pltpu.VMEM((D, D), BF16),
    pltpu.VMEM((SEQ, FF), F32),
    pltpu.VMEM((SEQ, D), F32),
]
BACKWARD_WORK = [
    pltpu.VMEM((D, BLOCKS * QUERIES), BF16),
    pltpu.VMEM((D, BLOCKS * QUERIES), BF16),
    pltpu.VMEM((D, KEYS), BF16),
    pltpu.VMEM((KEYS, BLOCKS * QUERIES), BF16),
    pltpu.VMEM((D, KEYS), BF16),
    pltpu.VMEM((KEYS, 512), F32),
    pltpu.VMEM((SEQ, 768), BF16),
]
PROJ_WORK = pltpu.VMEM((D, D), BF16)
ONES_WORK = pltpu.VMEM((16, SEQ), BF16)


def per_device(
    tokens,
    actions,
    game_ids,
    valid_steps,
    rewards,
    end_flags,
    embed_table,
    table_first,
    table_second,
    attn_weight,
    attn_first,
    attn_second,
    proj_weight,
    proj_first,
    proj_second,
    up_weight,
    up_first,
    up_second,
    up_bias,
    bias_first,
    bias_second,
    down_weight,
    down_first,
    down_second,
    vectors,
    vectors_first,
    vectors_second,
    head_weight,
    head_first,
    head_second,
    side_weight,
    side_first,
    side_second,
):
    n_high = lax.axis_size("wide") // 4
    wide, core = lax.axis_index("wide"), lax.axis_index("narrow")
    rows = side_weight.shape[0]
    fast = rows == 16
    place = jnp.stack([wide if fast else jnp.zeros_like(wide), core, wide]).astype(jnp.int32)

    def flat(a):
        return jnp.swapaxes(a, -1, -2)

    params = (
        (flat(embed_table), flat(table_first), flat(table_second)),
        (attn_weight, attn_first, attn_second),
        (flat(proj_weight), flat(proj_first), flat(proj_second)),
        (up_weight, up_first, up_second),
        (up_bias, bias_first, bias_second),
        (flat(down_weight), flat(down_first), flat(down_second)),
        (vectors, vectors_first, vectors_second),
        (head_weight, head_first, head_second),
        (flat(side_weight), flat(side_first), flat(side_second)),
    )
    table, attn, proj, up, _, down, _, head, side = (group[0] for group in params)

    piece = call(
        pack_kernel,
        None,
        [SMEM_SPEC] + [VMEM_SPEC] * 7,
        VMEM_SPEC,
        shaped((rows, HALF_FIRST_COLS + HALF_SECOND_COLS), BF16),
        [pltpu.VMEM((rows, 128), F32)],
        10**6,
        10**6,
        "pack",
    )(place, table, attn, proj, up, down, head, side)
    column = swap_column(piece, n_high)

    count = tokens.shape[0] // lax.axis_size("narrow")
    meta, frame_meta = call(
        prepare_kernel,
        None,
        [SMEM_SPEC] * 2 + [VMEM_SPEC] * 5 + [ANY_SPEC],
        [VMEM_SPEC] * 2,
        [shaped((count, SEQ, 128), jnp.int32), shaped((count, SIDE_ROWS, 128), jnp.int32)],
        [pltpu.VMEM((24, FRAMES), jnp.int32)],
        10**6,
        10**6,
        "prepare",
    )(place, game_ids, flat(tokens), actions, valid_steps, rewards, end_flags, piece)
    column, meta = lax.optimization_barrier((column, meta))
    first_mine = gather_plane(jnp.stack([a[:, :HALF_FIRST_COLS] for a in column]))
    second_column = jnp.stack([a[:, HALF_FIRST_COLS:] for a in column])
    second_column, last = lax.optimization_barrier((second_column, first_mine[3]))
    first_mine = first_mine[0:3] + [last]
    first_other = gather_cores(first_mine)
    second_mine = gather_plane(second_column)
    first_parts = in_blocks(first_mine, wide) + in_blocks(first_other, wide)
    other_bias = swap(up_bias, "narrow", 1)

    kept_specs = [row_spec(shape) for shape, _ in KEPT]
    kept_shapes = [shaped((count,) + shape, dtype) for shape, dtype in KEPT]
    row_f32 = shaped((count, SEQ, D), F32)
    meta_spec = row_spec((SEQ, 128))
    vec_specs = [full_spec(vectors), full_spec(up_bias), full_spec(up_bias)]
    w_spec = pl.BlockSpec((D, COL_FIRST), lambda i: (0, 0))
    side_spec = pl.BlockSpec((D, 128), lambda i: (0, 0))
    hits_spec = row_spec((SEQ, ROWS))
    results = call(
        first_forward_kernel,
        (count,),
        [SMEM_SPEC, meta_spec] + vec_specs + [full_spec(a) for a in first_parts],
        [w_spec, side_spec, row_spec((SEQ, D)), hits_spec, row_spec((SEQ, D))] + kept_specs,
        [shaped((D, COL_FIRST), BF16), shaped((D, 128), BF16), row_f32]
        + [shaped((count, SEQ, ROWS), BF16), row_f32]
        + kept_shapes,
        [pltpu.VMEM((D, COL_FIRST), BF16)] + FORWARD_WORK,
        4 * 10**9,
        20 * 10**6,
        "first_forward",
    )(place, meta, vectors, up_bias, other_bias, *first_parts)
    w_first, side_copy, stream, hits, stream_first = results[0:5]
    kept = results[5:]
    received, side_copy = lax.optimization_barrier((second_mine[1:], side_copy))
    second_mine = second_mine[0:1] + received
    second_other = gather_cores(second_mine)
    second_parts = in_blocks(second_mine, wide) + in_blocks(second_other, wide)

    def blocks(cols):
        return pl.BlockSpec((4, 4, 16, cols), lambda i: (0, 0, 0, 0))

    def block_shapes(cols):
        return [shaped((4, 4, 16, cols), F32), shaped((4, 4, 16, cols), BF16)]

    small_spec = pl.BlockSpec((SMALL_ROWS, 8, D), lambda i: (0, 0, 0))
    small_shape = shaped((SMALL_ROWS, 8, D), F32)
    small_scratch = pltpu.VMEM((SMALL_ROWS, 8, D), F32)
    scalar_spec = pl.BlockSpec((8, 128), lambda i: (0, 0))
    grad_stream, keep_second, send_second, small_grads, scalars = call(
        middle_kernel,
        (count,),
        [SMEM_SPEC, meta_spec, row_spec((SIDE_ROWS, 128))]
        + vec_specs
        + [side_spec, row_spec((SEQ, D))]
        + [full_spec(a) for a in second_parts],
        [row_spec((SEQ, D))] + [blocks(HALF_SECOND_COLS)] * 2 + [small_spec, scalar_spec],
        [row_f32] + block_shapes(HALF_SECOND_COLS) + [small_shape, shaped((8, 128), F32)],
        [
            pltpu.VMEM((D, COL_SECOND + 128), BF16),
            pltpu.VMEM((D, COL_SECOND + 128), F32),
            small_scratch,
        ]
        + [pltpu.VMEM(shape, dtype) for shape, dtype in KEPT]
        + FORWARD_WORK
        + BACKWARD_WORK
        + [
            PROJ_WORK,
            pltpu.VMEM((SEQ, FF), BF16),
            ONES_WORK,
            pltpu.VMEM((SEQ, D), F32),
            pltpu.VMEM((SEQ, D), BF16),
            pltpu.VMEM((SEQ, D), F32),
            pltpu.VMEM((KEYS, D), BF16),
            pltpu.VMEM((SEQ, D), F32),
            pltpu.VMEM((SEQ, D), BF16),
            pltpu.VMEM((SEQ, VOCAB), F32),
            pltpu.VMEM((SEQ, VOCAB + 128), BF16),
            pltpu.VMEM((SIDE_ROWS, SEQ), BF16),
            pltpu.VMEM((SEQ, SIDE_ROWS), BF16),
        ],
        15 * 10**9,
        20 * 10**6,
        "middle",
    )(place, meta, frame_meta, vectors, up_bias, other_bias, side_copy, stream, *second_parts)
    second_sums = add_cores(keep_second, send_second, n_high)

    kept_ff = (kept[6], kept[7], kept[8], kept[10])
    grad_mid, keep_ff, send_ff, small_grads = call(
        ff_backward_kernel,
        (count,),
        [SMEM_SPEC, full_spec(vectors), w_spec, row_spec((SEQ, D)), small_spec]
        + [row_spec(a.shape[1:]) for a in kept_ff],
        [row_spec((SEQ, D))] + [blocks(HALF_GRAD_COLS)] * 2 + [small_spec],
        [row_f32] + block_shapes(HALF_GRAD_COLS) + [small_shape],
        [
            pltpu.VMEM((D, 2048), F32),
            small_scratch,
            pltpu.VMEM((SEQ, D), BF16),
            pltpu.VMEM((SEQ, FF), BF16),
            ONES_WORK,
            pltpu.VMEM((SEQ, FF), F32),
            pltpu.VMEM((SEQ, D), F32),
        ],
        4 * 10**9,
        10 * 10**6,
        "ff_backward",
    )(place, vectors, w_first, grad_stream, small_grads, *kept_ff)
    ff_sums = add_cores(keep_ff, send_ff, n_high)
    other_sums = jnp.concatenate([second_sums.astype(BF16), ff_sums.astype(BF16)], axis=-1)
    others = exchange(other_sums, plane_groups(n_high))

    kept_attention = (stream_first,) + tuple(kept[0:6]) + (kept[9],)
    keep_rest, send_rest, small_grads = call(
        attention_backward_kernel,
        (count,),
        [SMEM_SPEC, full_spec(vectors), w_spec, row_spec((SEQ, D)), hits_spec, small_spec]
        + [row_spec(a.shape[1:]) for a in kept_attention]
        + [ANY_SPEC],
        [blocks(HALF_GRAD_COLS)] * 2 + [pl.BlockSpec((SMALL_ROWS, D), lambda i: (0, 0))],
        block_shapes(HALF_GRAD_COLS) + [shaped((SMALL_ROWS, D), F32)],
        [pltpu.VMEM((D, 2048), F32), small_scratch]
        + [pltpu.VMEM((KEYS, D), BF16), pltpu.VMEM((SEQ, D), BF16)]
        + BACKWARD_WORK
        + [PROJ_WORK, pltpu.VMEM((SEQ, D), F32)],
        6 * 10**9,
        20 * 10**6,
        "attention_backward",
    )(place, vectors, w_first, grad_mid, hits, small_grads, *kept_attention, other_sums)
    others, keep_rest = lax.optimization_barrier((others, keep_rest))
    rest_sums = add_cores(keep_rest, send_rest, n_high).astype(BF16)
    rest = exchange(rest_sums, plane_groups(n_high))

    def along_column(parts):
        parts = [parts[p].astype(F32) for p in range(4)]
        total = (parts[0] + parts[1]) + (parts[2] + parts[3])
        return exchange(total.astype(BF16), column_groups(n_high))

    others, rest = along_column(others), along_column(rest)

    grad_rest, grad_others, table_part, small = call(
        finish_kernel,
        None,
        [SMEM_SPEC] + [VMEM_SPEC] * 3,
        [VMEM_SPEC] * 4,
        [
            shaped((rows, HALF_GRAD_COLS), F32),
            shaped((rows, HALF_GRAD_COLS + HALF_SECOND_COLS), F32),
            shaped((rows, 512), F32),
            shaped((rows + 8, 128), F32),
        ],
        [],
        10**6,
        10**6,
        "finish",
    )(place, rest, others, scalars)

    beside = swap(small, "narrow", 1)
    is_small = (jnp.arange(rows + 8) < rows)[:, None]
    small = jnp.where(is_small, jnp.where(core == 1, small, beside), small + beside)
    gathered = exchange(jnp.broadcast_to(small, (4 * n_high,) + small.shape), None)
    quarters = []
    if not fast:
        total = lax.psum(small_grads, ("wide", "narrow"))
        quarters = [total.reshape(4, 8, 2, 128).transpose(0, 2, 1, 3).reshape(4, 16, 128)]
    swapped = swap(table_part, "narrow", 1)

    flat_params = [a for group in params for a in group]
    results = call(
        functools.partial(adam_kernel, fast),
        None,
        [SMEM_SPEC] + [VMEM_SPEC] * (31 + len(quarters)),
        [VMEM_SPEC] * 30,
        [shaped((1, 1), F32)] * 3 + [shaped(a.shape, F32) for a in flat_params],
        [pltpu.VMEM((SMALL_ROWS, D), F32)],
        10**6,
        10**6,
        "adam",
    )(place, grad_rest, grad_others, swapped, gathered, *quarters, *flat_params)
    news = list(results[3:])
    for group in (0, 2, 5, 8):
        for member in range(3 * group, 3 * group + 3):
            news[member] = flat(news[member])
    return tuple(a.reshape(()) for a in results[0:3]) + tuple(news)


def solution(mesh):
    placed = (
        P("wide", None, None),
        P("wide", None),
        P("wide"),
        P("wide", None),
        P("wide", None),
        P("wide", None),
        P(None, "wide"),
        P(None, "wide"),
        P(None, "wide"),
        P(None, None, "wide", "narrow"),
        P(None, None, "wide", "narrow"),
        P(None, None, "wide", "narrow"),
        P(None, "narrow", "wide"),
        P(None, "narrow", "wide"),
        P(None, "narrow", "wide"),
        P(None, "wide", "narrow"),
        P(None, "wide", "narrow"),
        P(None, "wide", "narrow"),
        P(None, "narrow"),
        P(None, "narrow"),
        P(None, "narrow"),
        P(None, "narrow", "wide"),
        P(None, "narrow", "wide"),
        P(None, "narrow", "wide"),
        P(),
        P(),
        P(),
        P("wide", "narrow"),
        P("wide", "narrow"),
        P("wide", "narrow"),
        P("wide", None),
        P("wide", None),
        P("wide", None),
    )
    return jax.shard_map(
        per_device,
        mesh=mesh,
        in_specs=placed,
        out_specs=(P(), P(), P()) + placed[6:],
        check_vma=False,
    )
```

time: 190 us -> 200 us (1.053)
  waiting for transfers between devices: 30.2 us -> 49.4 us
  starting transfers between devices: 43.1 us -> 31.9 us
  blocking collectives: 0 us -> 8.95 us
  Pallas kernels: 104 us -> 95.4 us
    ppermute x44 -> x23, starting transfers between devices: 43.1 us -> 14.9 us  [swap(): return lax.ppermute(a, axis, [(i, i ^ distance) for i in range(size)])]
    all_to_all x0 -> x4, waiting for transfers between devices: none -> 25.5 us  [exchange(): return lax.all_to_all(a, 'wide', 0, 0, axis_index_groups=groups)]
    all_to_all x0 -> x4, starting transfers between devices: none -> 16.9 us  [exchange(): return lax.all_to_all(a, 'wide', 0, 0, axis_index_groups=groups)]
    all_to_all x0 -> x1, blocking collectives: none -> 8.95 us  [exchange(): return lax.all_to_all(a, 'wide', 0, 0, axis_index_groups=groups)]
    pallas_call x4, Pallas kernels: 52.3 us -> 45.1 us  [the longest x1 39 us: per_device(): call(middle_kernel, (count,), [SMEM_SPEC, meta_spec, row_spec((SIDE_ROWS,...]
    ppermute x44 -> x23, waiting for transfers between devices: 30.2 us -> 23.9 us  [swap(): return lax.ppermute(a, axis, [(i, i ^ distance) for i in range(size)])]
    convert_element_type x1 -> x5, other arithmetic: 0.1 us -> 4.75 us  [the longest x1 2.18 us: per_device(): rest_sums = add_cores(keep_rest, send_rest, n_high).astype(BF16)]
  transfers between devices with their start and end apart: 44 -> 27, of which waited for: 20 -> 15; matrix products, arithmetic and copies ran while one was open for 3% -> 1% of each run, Pallas kernels for 27% -> 25%
where the time goes in v4:
time: 200 us; the launch traced here: 199 us
  Pallas kernels  95.4 us (48%)
  waiting for transfers between devices  49.4 us (25%)
  starting transfers between devices  31.9 us (16%)
  blocking collectives  8.95 us (4%)
  other arithmetic  7.53 us (4%)
  local copies, waits for them, and re-layouts  5.16 us (3%)
    pallas_call x1, Pallas kernels, per_device(): call(middle_kernel, (count,), [SMEM_SPEC, meta_spec, row_spec((SIDE_ROWS,...  39 us
    all_to_all x4, waiting for transfers between devices, exchange(): return lax.all_to_all(a, 'wide', 0, 0, axis_index_groups=groups)  25.5 us
    ppermute x23, waiting for transfers between devices, swap(): return lax.ppermute(a, axis, [(i, i ^ distance) for i in range(size)])  23.9 us
    pallas_call x1, Pallas kernels, per_device(): call(first_forward_kernel, (count,), [SMEM_SPEC, meta_spec] + vec_specs +...  19.2 us
    pallas_call x1, Pallas kernels, per_device(): call(attention_backward_kernel, (count,), [SMEM_SPEC, full_spec(vectors),...  17.4 us
    all_to_all x4, starting transfers between devices, exchange(): return lax.all_to_all(a, 'wide', 0, 0, axis_index_groups=groups)  16.9 us
    ppermute x23, starting transfers between devices, swap(): return lax.ppermute(a, axis, [(i, i ^ distance) for i in range(size)])  14.9 us
    pallas_call x1, Pallas kernels, per_device(): call(ff_backward_kernel, (count,), [SMEM_SPEC, full_spec(vectors), w_spec...  10.4 us
  transfers between devices with their start and end apart: 27, of which 15 were waited for; matrix products, arithmetic and copies ran while one was open for 1% of the time, Pallas kernels for 25%

profile of v4, /device:TPU:0, one launch (start us, length us, event | category | flops | bytes accessed | tf_op | source)
XLA Modules:
  0.0 199.5 jit_solution(16630796959171000452)
XLA Ops:
  0.7 0.7 pad_add_fusion.place_ref.refs_0_
  1.4 1.7 pack.1.after
  3.1 3.0 %collective-permute-start = (bf16[16,3840]{1,0:T(8,128)(2,1)}, bf16[16,3840]{1,0:T(8,128)(2,1)S(1)}, u32[]{:S(2)}, u32[]{:S(2)}) collective-permute-start(bf16[16,3840]{1,0:T(8,128)(2,1)} %pack.1.after), channel_id=1, source_target_pairs={{0,8},{2,10},{4,12},{6,14},{8,0},{10,2},{12,4},{14,6},{16,24},{18,... | collective-permute-start | bytes 368648 | tf_op jit(solution)/shard_map/ppermute | solution.py:736
  6.1 2.6 %collective-permute-start.1 = (bf16[16,3840]{1,0:T(8,128)(2,1)}, bf16[16,3840]{1,0:T(8,128)(2,1)S(1)}, u32[]{:S(2)}, u32[]{:S(2)}) collective-permute-start(bf16[16,3840]{1,0:T(8,128)(2,1)} %pack.1.after), channel_id=1, source_target_pairs={{0,16},{2,18},{4,20},{6,22},{8,24},{10,26},{12,28},{14,30},{16,0},... | collective-permute-start | bytes 368648 | tf_op jit(solution)/shard_map/ppermute | solution.py:736
  8.7 3.3 %prepare.1 = (s32[4,352,128]{2,1,0:T(8,128)}, s32[4,32,128]{2,1,0:T(8,128)}) custom-call(s32[3]{0:T(128)} %pad_add_fusion.place_ref.refs_0_, s32[8]{0:T(128)} %games_ref.1, s32[8,16,20]{2,1,0:T(8,128)} %bitcast.56, s32[8,20]{1,0:T(8,128)} %actions.1, s32[8,20]{1,0:T(8,128)} %valid.1, s32[8,20]{1,0:T(8,128)} %rewards.1, s32[8,20]{1,0:T(8,128)} %ends.1, ...), custom_call_target="tpu_custom_call" | custom-call | flops 1000000 | bytes 1000000 | tf_op jit(solution)/shard_map/prepare/pallas_call | solution.py:924
  12.0 6.6 %collective-permute-done.1 = bf16[16,3840]{1,0:T(8,128)(2,1)S(1)} collective-permute-done((bf16[16,3840]{1,0:T(8,128)(2,1)}, bf16[16,3840]{1,0:T(8,128)(2,1)S(1)}, u32[]{:S(2)}, u32[]{:S(2)}) %collective-permute-start.1) | collective-permute-done | bytes 122912 | tf_op jit(solution)/shard_map/ppermute | solution.py:736
  18.7 0.8 slice_bitcast_fusion.6
  19.5 0.8 slice_bitcast_fusion.2
  20.4 2.5 %collective-permute-start.4 = (bf16[4,16,2048]{2,1,0:T(8,128)(2,1)S(1)}, bf16[4,16,2048]{2,1,0:T(8,128)(2,1)S(1)}, u32[]{:S(2)}, u32[]{:S(2)}) collective-permute-start(bf16[4,16,2048]{2,1,0:T(8,128)(2,1)S(1)} %pad_maximum_fusion.1.refs_5_), channel_id=1, source_target_pairs={{0,6},{2,4},{4,2},{6,0},{8,14},{10,12},{12,10},{14,8},{16,22},{18,... | collective-permute-start | bytes 786440 | tf_op jit(solution)/shard_map/ppermute | solution.py:736
  22.9 0.5 collective-permute-start.8
  23.5 0.5 collective-permute-start.9
  24.1 5.8 %collective-permute-done.4.refs_8_ = bf16[4,16,2048]{2,1,0:T(8,128)(2,1)S(1)} collective-permute-done((bf16[4,16,2048]{2,1,0:T(8,128)(2,1)S(1)}, bf16[4,16,2048]{2,1,0:T(8,128)(2,1)S(1)}, u32[]{:S(2)}, u32[]{:S(2)}) %collective-permute-start.4) | collective-permute-done | bytes 262176 | tf_op jit(solution)/shard_map/ppermute | solution.py:736
  30.0 2.8 %collective-permute-done.8.refs_6_ = bf16[4,16,2048]{2,1,0:T(8,128)(2,1)S(1)} collective-permute-done((bf16[4,16,2048]{2,1,0:T(8,128)(2,1)S(1)}, bf16[4,16,2048]{2,1,0:T(8,128)(2,1)S(1)}, u32[]{:S(2)}, u32[]{:S(2)}) %collective-permute-start.8) | collective-permute-done | bytes 262176 | tf_op jit(solution)/shard_map/ppermute | solution.py:736
  32.8 0.5 collective-permute-start.12
  33.4 1.3 collective-permute-done.3.refs_4_.refs_5_
  34.7 1.5 collective-permute-start.5
  36.2 1.0 collective-permute-start.6
  37.2 1.0 collective-permute-start.7
  38.3 0.6 copy-done.12
  38.9 0.7 copy-done.13
  39.6 19.2 %first_forward.1 = (bf16[256,4096]{1,0:T(8,128)(2,1)}, bf16[256,128]{1,0:T(8,128)(2,1)}, f32[4,352,256]{2,1,0:T(8,128)}, bf16[4,352,896]{2,1,0:T(8,128)(2,1)}, f...) custom-call(s32[3]{0:T(128)} %pad_add_fusion.place_ref.refs_0_, ...), custom_call_target="tpu_custom_call" | custom-call | flops 4000000000 | bytes 20000000 | tf_op jit(solution)/shard_map/first_forward/pallas_call | solution.py:953
  58.9 0.5 collective-permute-start.16
  59.5 0.9 collective-permute-done.15.refs_13_
  61.8 39.0 %middle.1 = (f32[4,352,256]{2,1,0:T(8,128)}, f32[4,4,16,1792]{3,2,1,0:T(8,128)}, bf16[4,4,16,1792]{3,2,1,0:T(8,128)(2,1)}, f32[32,8,256]{2,1,0:T(8,128)}, f32[8,128]{1,0:T(8,128)}) custom-call(s32[3]{0:T(128)} %pad_add_fusion.place_ref.refs_0_, s32[4,352,128]{2,1,0:T(8,128)} %get-tuple-element.107.refs_1_, s32[4,32,128]{2,1,0:T(8,128)} %get-tuple-element.108.refs_2_, ...), custom_call_target="tpu_custom_call" | custom-call | flops 15000000512 | bytes 20000000 | tf_op jit(solution)/shard_map/middle/pallas_call | solution.py:983
  101.0 10.4 %ff_backward.1 = (f32[4,352,256]{2,1,0:T(8,128)}, f32[4,4,16,1024]{3,2,1,0:T(8,128)}, bf16[4,4,16,1024]{3,2,1,0:T(8,128)(2,1)}, f32[32,8,256]{2,1,0:T(8,128)}) custom-call(s32[3]{0:T(128)} %pad_add_fusion.place_ref.refs_0_, f32[14,256]{1,0:T(8,128)} %refs_18_.1, bf16[256,4096]{1,0:T(8,128)(2,1)} %get-tuple-element.123.refs_2_, ...), custom_call_target="tpu_custom_call" | custom-call | flops 4000000000 | bytes 10000000 | tf_op jit(solution)/shard_map/ff_backward/pallas_call | solution.py:1022
  111.7 1.9 collective-permute-done.19
  113.6 1.4 add_convert_fusion.2
  115.2 1.3 pad_maximum_fusion.refs_14_
  116.5 3.5 %all-to-all-start = ((bf16[4,4,16,2816]{3,2,1,0:T(8,128)(2,1)}), bf16[4,4,16,2816]{3,2,1,0:T(8,128)(2,1)S(1)}, u32[]{:S(2)}, u32[]{:S(2)}) async-start(bf16[4,4,16,2816]{3,2,1,0:T(8,128)(2,1)} %pad_maximum_fusion.refs_14_), calls=%async_computation | async-start | bytes 2883584 | tf_op jit(solution)/shard_map/all_to_all | solution.py:774
  120.0 17.4 %attention_backward.1 = (f32[4,4,16,1024]{3,2,1,0:T(8,128)}, bf16[4,4,16,1024]{3,2,1,0:T(8,128)(2,1)}, f32[32,256]{1,0:T(8,128)}) custom-call(s32[3]{0:T(128)} %pad_add_fusion.place_ref.refs_0_, f32[14,256]{1,0:T(8,128)} %refs_18_.1, bf16[256,4096]{1,0:T(8,128)(2,1)} %get-tuple-element.123.refs_2_, f32[4,352,256]{2,1,0:T(8,128)} %get-tuple-element.132.refs_3_, ...), custom_call_target="tpu_custom_call" | custom-call | flops 6000000000 | bytes 20000000 | tf_op jit(solution)/shard_map/attention_backward/pallas_call | solution.py:1047
  137.7 0.8 all-to-all-done
  138.5 1.1 collective-permute-done.20
  139.6 2.2 %add_convert_fusion.1 = bf16[4,4,16,1024]{3,2,1,0:T(8,128)(2,1)} fusion(f32[4,4,16,1024]{3,2,1,0:T(8,128)} %get-tuple-element.144, bf16[4,4,16,1024]{3,2,1,0:T(8,128)(2,1)S(1)} %collective-permute-done.20), kind=kLoop, calls=%fused_computation.2 | loop fusion | flops 786432 | bytes 2097152 | tf_op jit(solution)/shard_map/convert_element_type | solution.py:1064
  141.8 4.1 %all-to-all-start.1 = ((bf16[4,4,16,1024]{3,2,1,0:T(8,128)(2,1)}), bf16[4,4,16,1024]{3,2,1,0:T(8,128)(2,1)S(1)}, u32[]{:S(2)}, u32[]{:S(2)}) async-start(bf16[4,4,16,1024]{3,2,1,0:T(8,128)(2,1)} %add_convert_fusion.1), calls=%async_computation.1 | async-start | bytes 1048576 | tf_op jit(solution)/shard_map/all_to_all | solution.py:774
  145.9 0.9 fusion
  146.8 7.4 %all-to-all-done.1 = bf16[4,4,16,1024]{3,2,1,0:T(8,128)(2,1)S(1)} async-done(((bf16[4,4,16,1024]{3,2,1,0:T(8,128)(2,1)}), bf16[4,4,16,1024]{3,2,1,0:T(8,128)(2,1)S(1)}, u32[]{:S(2)}, u32[]{:S(2)}) %all-to-all-start.1) | async-done | bytes 524320 | tf_op jit(solution)/shard_map/all_to_all | solution.py:774
  154.2 5.6 %all-to-all-start.3 = ((bf16[4,16,2816]{2,1,0:T(8,128)(2,1)}), bf16[4,16,2816]{2,1,0:T(8,128)(2,1)S(1)}, u32[]{:S(2)}, u32[]{:S(2)}) async-start(bf16[4,16,2816]{2,1,0:T(8,128)(2,1)} %fusion), calls=%async_computation.3 | async-start | bytes 720896 | tf_op jit(solution)/shard_map/all_to_all | solution.py:774
  159.9 10.1 %all-to-all-done.3.others = bf16[4,16,2816]{2,1,0:T(8,128)(2,1)S(1)} async-done(((bf16[4,16,2816]{2,1,0:T(8,128)(2,1)}), bf16[4,16,2816]{2,1,0:T(8,128)(2,1)S(1)}, u32[]{:S(2)}, u32[]{:S(2)}) %all-to-all-start.3) | async-done | bytes 360480 | tf_op jit(solution)/shard_map/all_to_all | solution.py:774
  170.0 9.0 %all_to_all.25.rest = bf16[4,16,1024]{2,1,0:T(8,128)(2,1)} all-to-all(bf16[4,16,1024]{2,1,0:T(8,128)(2,1)S(1)} %fusion.1), channel_id=1, replica_groups={{0,8,16,24},{2,10,18,26},{4,12,20,28},{6,14,22,30},{1,9,17,25},{3,11,19..., dimensions={0} | all-to-all | bytes 262144 | tf_op jit(solution)/shard_map/all_to_all | solution.py:774
  178.9 1.8 finish.1
  180.8 1.4 collective-permute-done.22
  182.1 0.8 add_select_fusion
  182.9 0.7 broadcast_in_dim.13
  183.6 3.7 %all-to-all-start.4 = ((f32[16,24,128]{2,1,0:T(8,128)}), f32[16,24,128]{2,1,0:T(8,128)S(1)}, u32[]{:S(2)}, u32[]{:S(2)}) async-start(f32[16,24,128]{2,1,0:T(8,128)} %broadcast_in_dim.13), calls=%async_computation.4 | async-start | bytes 393216 | tf_op jit(solution)/shard_map/all_to_all | solution.py:774
  187.4 1.4 collective-permute-done.21.swapped
  188.8 7.3 %all-to-all-done.4.gathered = f32[16,24,128]{2,1,0:T(8,128)S(1)} async-done(((f32[16,24,128]{2,1,0:T(8,128)}), f32[16,24,128]{2,1,0:T(8,128)S(1)}, u32[]{:S(2)}, u32[]{:S(2)}) %all-to-all-start.4) | async-done | bytes 196640 | tf_op jit(solution)/shard_map/all_to_all | solution.py:774
  196.1 0.7 copy-done.2
  196.8 2.5 %adam.1 = (f32[1,1]{1,0:T(1,128)}, f32[1,1]{1,0:T(1,128)}, f32[1,1]{1,0:T(1,128)}, f32[16,896]{1,0:T(8,128)}, f32[16,896]{1,0:T(8,128)}, /*index=5*/f32[16,896]{...) custom-call(s32[3]{0:T(128)} %pad_add_fusion.place_ref.refs_0_, ...), custom_call_target="tpu_custom_call" | custom-call | flops 1000000 | bytes 1000000 | tf_op jit(solution)/shard_map/adam/pallas_call | solution.py:1102
  (75 shorter events, 3.1 us)
Async XLA Ops:
  0.7 32.6 %copy-start.6 = (f32[2,512]{1,0:T(2,128)S(1)}, f32[2,512]{1,0:T(2,128)}, u32[]{:S(2)}) copy-start(f32[2,512]{1,0:T(2,128)} %refs_12_.1) | copy-start | bytes 12292
  3.1 8.9 %collective-permute-start = (bf16[16,3840]{1,0:T(8,128)(2,1)}, bf16[16,3840]{1,0:T(8,128)(2,1)S(1)}, u32[]{:S(2)}, u32[]{:S(2)}) collective-permute-start(bf16[16,3840]{1,0:T(8,128)(2,1)} %pack.1.after), channel_id=1, source_target_pairs={{0,8},{2,10},{4,12},{6,14},{8,0},{10,2},{12,4},{14,6},{16,24},{18,... | collective-permute-start | bytes 368648 | tf_op jit(solution)/shard_map/ppermute | solution.py:736
  6.1 12.5 %collective-permute-start.1 = (bf16[16,3840]{1,0:T(8,128)(2,1)}, bf16[16,3840]{1,0:T(8,128)(2,1)S(1)}, u32[]{:S(2)}, u32[]{:S(2)}) collective-permute-start(bf16[16,3840]{1,0:T(8,128)(2,1)} %pack.1.after), channel_id=1, source_target_pairs={{0,16},{2,18},{4,20},{6,22},{8,24},{10,26},{12,28},{14,30},{16,0},... | collective-permute-start | bytes 368648 | tf_op jit(solution)/shard_map/ppermute | solution.py:736
  8.7 9.9 %collective-permute-start.2 = (bf16[16,3840]{1,0:T(8,128)(2,1)}, bf16[16,3840]{1,0:T(8,128)(2,1)S(1)}, u32[]{:S(2)}, u32[]{:S(2)}) collective-permute-start(bf16[16,3840]{1,0:T(8,128)(2,1)} %pack.1.after), channel_id=1, source_target_pairs={{0,24},{2,26},{4,28},{6,30},{8,16},{10,18},{12,20},{14,22},{16,8},... | collective-permute-start | bytes 368648 | tf_op jit(solution)/shard_map/ppermute | solution.py:736
  20.4 17.8 %copy-start.3 = (bf16[4,16,2048]{2,1,0:T(8,128)(2,1)}, bf16[4,16,2048]{2,1,0:T(8,128)(2,1)S(1)}, u32[]{:S(2)}) copy-start(bf16[4,16,2048]{2,1,0:T(8,128)(2,1)S(1)} %pad_maximum_fusion.1.refs_5_) | copy-start | bytes 786436
  20.4 9.5 %collective-permute-start.4 = (bf16[4,16,2048]{2,1,0:T(8,128)(2,1)S(1)}, bf16[4,16,2048]{2,1,0:T(8,128)(2,1)S(1)}, u32[]{:S(2)}, u32[]{:S(2)}) collective-permute-start(bf16[4,16,2048]{2,1,0:T(8,128)(2,1)S(1)} %pad_maximum_fusion.1.refs_5_), channel_id=1, source_target_pairs={{0,6},{2,4},{4,2},{6,0},{8,14},{10,12},{12,10},{14,8},{16,22},{18,... | collective-permute-start | bytes 786440 | tf_op jit(solution)/shard_map/ppermute | solution.py:736
  22.9 9.8 %collective-permute-start.8 = (bf16[4,16,2048]{2,1,0:T(8,128)(2,1)S(1)}, bf16[4,16,2048]{2,1,0:T(8,128)(2,1)S(1)}, u32[]{:S(2)}, u32[]{:S(2)}) collective-permute-start(bf16[4,16,2048]{2,1,0:T(8,128)(2,1)S(1)} %pad_maximum_fusion.1.refs_5_), channel_id=1, source_target_pairs={{0,2},{2,0},{4,6},{6,4},{8,10},{10,8},{12,14},{14,12},{16,18},{18,... | collective-permute-start | bytes 786440 | tf_op jit(solution)/shard_map/ppermute | solution.py:736
  23.5 9.3 %collective-permute-start.9 = (bf16[4,16,2048]{2,1,0:T(8,128)(2,1)S(1)}, bf16[4,16,2048]{2,1,0:T(8,128)(2,1)S(1)}, u32[]{:S(2)}, u32[]{:S(2)}) collective-permute-start(bf16[4,16,2048]{2,1,0:T(8,128)(2,1)S(1)} %pad_maximum_fusion.1.refs_5_), channel_id=1, source_target_pairs={{0,4},{2,6},{4,0},{6,2},{8,12},{10,14},{12,8},{14,10},{16,20},{18,... | collective-permute-start | bytes 786440 | tf_op jit(solution)/shard_map/ppermute | solution.py:736
  24.0 12.2 %collective-permute-start.10 = (bf16[4,16,2048]{2,1,0:T(8,128)(2,1)S(1)}, bf16[4,16,2048]{2,1,0:T(8,128)(2,1)S(1)}, u32[]{:S(2)}, u32[]{:S(2)}) collective-permute-start(bf16[4,16,2048]{2,1,0:T(8,128)(2,1)S(1)} %pad_maximum_fusion.1.refs_5_), channel_id=1, source_target_pairs={{0,1},{1,0},{2,3},{3,2},{4,5},{5,4},{6,7},{7,6},{8,9},{9,8},{10,11... | collective-permute-start | bytes 786440 | tf_op jit(solution)/shard_map/ppermute | solution.py:736
  24.1 34.7 %copy-start.4 = (bf16[4,16,1792]{2,1,0:T(8,128)(2,1)}, bf16[4,16,1792]{2,1,0:T(8,128)(2,1)S(1)}, u32[]{:S(2)}) copy-start(bf16[4,16,1792]{2,1,0:T(8,128)(2,1)S(1)} %pad_maximum_fusion.2.refs_8_) | copy-start | bytes 688132
  30.0 8.3 %copy-start.7 = (bf16[4,16,2048]{2,1,0:T(8,128)(2,1)}, bf16[4,16,2048]{2,1,0:T(8,128)(2,1)S(1)}, u32[]{:S(2)}) copy-start(bf16[4,16,2048]{2,1,0:T(8,128)(2,1)S(1)} %collective-permute-done.4.refs_8_) | copy-start | bytes 786436
  30.0 7.3 %collective-permute-start.13 = (bf16[4,16,2048]{2,1,0:T(8,128)(2,1)S(1)}, bf16[4,16,2048]{2,1,0:T(8,128)(2,1)S(1)}, u32[]{:S(2)}, u32[]{:S(2)}) collective-permute-start(bf16[4,16,2048]{2,1,0:T(8,128)(2,1)S(1)} %collective-permute-done.4.refs_8_), channel_id=1, source_target_pairs={{0,1},{1,0},{2,3},{3,2},{4,5},{5,4},{6,7},{7,6},{8,9},{9,8},{10,11... | collective-permute-start | bytes 786440 | tf_op jit(solution)/shard_map/ppermute | solution.py:736
  32.8 5.5 %copy-start.8 = (bf16[4,16,2048]{2,1,0:T(8,128)(2,1)}, bf16[4,16,2048]{2,1,0:T(8,128)(2,1)S(1)}, u32[]{:S(2)}) copy-start(bf16[4,16,2048]{2,1,0:T(8,128)(2,1)S(1)} %collective-permute-done.8.refs_6_) | copy-start | bytes 786436
  32.8 5.4 %collective-permute-start.11 = (bf16[4,16,2048]{2,1,0:T(8,128)(2,1)S(1)}, bf16[4,16,2048]{2,1,0:T(8,128)(2,1)S(1)}, u32[]{:S(2)}, u32[]{:S(2)}) collective-permute-start(bf16[4,16,2048]{2,1,0:T(8,128)(2,1)S(1)} %collective-permute-done.8.refs_6_), channel_id=1, source_target_pairs={{0,1},{1,0},{2,3},{3,2},{4,5},{5,4},{6,7},{7,6},{8,9},{9,8},{10,11... | collective-permute-start | bytes 786440 | tf_op jit(solution)/shard_map/ppermute | solution.py:736
  32.8 5.5 %copy-start.9 = (bf16[4,16,2048]{2,1,0:T(8,128)(2,1)}, bf16[4,16,2048]{2,1,0:T(8,128)(2,1)S(1)}, u32[]{:S(2)}) copy-start(bf16[4,16,2048]{2,1,0:T(8,128)(2,1)S(1)} %collective-permute-done.9.refs_7_) | copy-start | bytes 786436
  32.8 5.4 %collective-permute-start.12 = (bf16[4,16,2048]{2,1,0:T(8,128)(2,1)S(1)}, bf16[4,16,2048]{2,1,0:T(8,128)(2,1)S(1)}, u32[]{:S(2)}, u32[]{:S(2)}) collective-permute-start(bf16[4,16,2048]{2,1,0:T(8,128)(2,1)S(1)} %collective-permute-done.9.refs_7_), channel_id=1, source_target_pairs={{0,1},{1,0},{2,3},{3,2},{4,5},{5,4},{6,7},{7,6},{8,9},{9,8},{10,11... | collective-permute-start | bytes 786440 | tf_op jit(solution)/shard_map/ppermute | solution.py:736
  33.3 1.4 collective-permute-start.3
  34.7 3.6 %copy-start.21 = (f32[2,512]{1,0:T(2,128)}, f32[2,512]{1,0:T(2,128)S(1)}, u32[]{:S(2)}) copy-start(f32[2,512]{1,0:T(2,128)S(1)} %collective-permute-done.3.refs_4_.refs_5_) | copy-start | bytes 12292
  34.7 24.1 %collective-permute-start.5 = (bf16[4,16,1792]{2,1,0:T(8,128)(2,1)S(1)}, bf16[4,16,1792]{2,1,0:T(8,128)(2,1)S(1)}, u32[]{:S(2)}, u32[]{:S(2)}) collective-permute-start(bf16[4,16,1792]{2,1,0:T(8,128)(2,1)S(1)} %pad_maximum_fusion.2.refs_8_), channel_id=1, source_target_pairs={{0,2},{2,0},{4,6},{6,4},{8,10},{10,8},{12,14},{14,12},{16,18},{18,... | collective-permute-start | bytes 688136 | tf_op jit(solution)/shard_map/ppermute | solution.py:736
  36.2 2.1 %copy-start.10 = (bf16[4,16,2048]{2,1,0:T(8,128)(2,1)}, bf16[4,16,2048]{2,1,0:T(8,128)(2,1)S(1)}, u32[]{:S(2)}) copy-start(bf16[4,16,2048]{2,1,0:T(8,128)(2,1)S(1)} %collective-permute-done.10.refs_9_) | copy-start | bytes 786436
  36.2 22.6 %collective-permute-start.6 = (bf16[4,16,1792]{2,1,0:T(8,128)(2,1)S(1)}, bf16[4,16,1792]{2,1,0:T(8,128)(2,1)S(1)}, u32[]{:S(2)}, u32[]{:S(2)}) collective-permute-start(bf16[4,16,1792]{2,1,0:T(8,128)(2,1)S(1)} %pad_maximum_fusion.2.refs_8_), channel_id=1, source_target_pairs={{0,4},{2,6},{4,0},{6,2},{8,12},{10,14},{12,8},{14,10},{16,20},{18,... | collective-permute-start | bytes 688136 | tf_op jit(solution)/shard_map/ppermute | solution.py:736
  37.2 1.0 copy-start.11
  37.2 21.6 %collective-permute-start.7 = (bf16[4,16,1792]{2,1,0:T(8,128)(2,1)S(1)}, bf16[4,16,1792]{2,1,0:T(8,128)(2,1)S(1)}, u32[]{:S(2)}, u32[]{:S(2)}) collective-permute-start(bf16[4,16,1792]{2,1,0:T(8,128)(2,1)S(1)} %pad_maximum_fusion.2.refs_8_), channel_id=1, source_target_pairs={{0,6},{2,4},{4,2},{6,0},{8,14},{10,12},{12,10},{14,8},{16,22},{18,... | collective-permute-start | bytes 688136 | tf_op jit(solution)/shard_map/ppermute | solution.py:736
  38.2 0.7 copy-start.12
  38.2 21.3 %collective-permute-start.14 = (bf16[4,16,1792]{2,1,0:T(8,128)(2,1)S(1)}, bf16[4,16,1792]{2,1,0:T(8,128)(2,1)S(1)}, u32[]{:S(2)}, u32[]{:S(2)}) collective-permute-start(bf16[4,16,1792]{2,1,0:T(8,128)(2,1)S(1)} %pad_maximum_fusion.2.refs_8_), channel_id=1, source_target_pairs={{0,1},{1,0},{2,3},{3,2},{4,5},{5,4},{6,7},{7,6},{8,9},{9,8},{10,11... | collective-permute-start | bytes 688136 | tf_op jit(solution)/shard_map/ppermute | solution.py:736
  38.9 0.7 copy-start.13
  58.8 2.3 %copy-start.14 = (bf16[4,16,1792]{2,1,0:T(8,128)(2,1)}, bf16[4,16,1792]{2,1,0:T(8,128)(2,1)S(1)}, u32[]{:S(2)}) copy-start(bf16[4,16,1792]{2,1,0:T(8,128)(2,1)S(1)} %collective-permute-done.5.refs_9_) | copy-start | bytes 688132
  58.8 2.2 %copy-start.15 = (bf16[4,16,1792]{2,1,0:T(8,128)(2,1)}, bf16[4,16,1792]{2,1,0:T(8,128)(2,1)S(1)}, u32[]{:S(2)}) copy-start(bf16[4,16,1792]{2,1,0:T(8,128)(2,1)S(1)} %collective-permute-done.6.refs_10_) | copy-start | bytes 688132
  58.8 2.2 %copy-start.16 = (bf16[4,16,1792]{2,1,0:T(8,128)(2,1)}, bf16[4,16,1792]{2,1,0:T(8,128)(2,1)S(1)}, u32[]{:S(2)}) copy-start(bf16[4,16,1792]{2,1,0:T(8,128)(2,1)S(1)} %collective-permute-done.7.refs_11_) | copy-start | bytes 688132
  58.8 1.6 collective-permute-start.15
  58.9 1.8 collective-permute-start.16
  59.4 1.6 collective-permute-start.17
  59.5 1.6 copy-start.17
  60.4 0.7 copy-start.18
  60.7 0.7 copy-start.19
  61.1 0.7 copy-start.20
  100.7 14.2 %collective-permute-start.18 = (bf16[4,4,16,1792]{3,2,1,0:T(8,128)(2,1)}, bf16[4,4,16,1792]{3,2,1,0:T(8,128)(2,1)S(1)}, u32[]{:S(2)}, u32[]{:S(2)}) collective-permute-start(bf16[4,4,16,1792]{3,2,1,0:T(8,128)(2,1)} %get-tuple-element.122), channel_id=1, source_target_pairs={{0,1},{1,0},{2,3},{3,2},{4,5},{5,4},{6,7},{7,6},{8,9},{9,8},{10,11... | collective-permute-start | bytes 2752520 | tf_op jit(solution)/shard_map/ppermute | solution.py:736
  111.4 3.6 %copy-start = (f32[4,4,16,1792]{3,2,1,0:T(8,128)S(1)}, f32[4,4,16,1792]{3,2,1,0:T(8,128)}, u32[]{:S(2)}) copy-start(f32[4,4,16,1792]{3,2,1,0:T(8,128)} %get-tuple-element.121) | copy-start | bytes 5505028
  111.4 2.2 %collective-permute-start.19 = (bf16[4,4,16,1024]{3,2,1,0:T(8,128)(2,1)}, bf16[4,4,16,1024]{3,2,1,0:T(8,128)(2,1)S(1)}, u32[]{:S(2)}, u32[]{:S(2)}) collective-permute-start(bf16[4,4,16,1024]{3,2,1,0:T(8,128)(2,1)} %get-tuple-element.131), channel_id=1, source_target_pairs={{0,1},{1,0},{2,3},{3,2},{4,5},{5,4},{6,7},{7,6},{8,9},{9,8},{10,11... | collective-permute-start | bytes 1572872 | tf_op jit(solution)/shard_map/ppermute | solution.py:736
  116.5 22.1 %all-to-all-start = ((bf16[4,4,16,2816]{3,2,1,0:T(8,128)(2,1)}), bf16[4,4,16,2816]{3,2,1,0:T(8,128)(2,1)S(1)}, u32[]{:S(2)}, u32[]{:S(2)}) async-start(bf16[4,4,16,2816]{3,2,1,0:T(8,128)(2,1)} %pad_maximum_fusion.refs_14_), calls=%async_computation | async-start | bytes 2883584 | tf_op jit(solution)/shard_map/all_to_all | solution.py:774
  137.4 2.2 %collective-permute-start.20 = (bf16[4,4,16,1024]{3,2,1,0:T(8,128)(2,1)}, bf16[4,4,16,1024]{3,2,1,0:T(8,128)(2,1)S(1)}, u32[]{:S(2)}, u32[]{:S(2)}) collective-permute-start(bf16[4,4,16,1024]{3,2,1,0:T(8,128)(2,1)} %get-tuple-element.145), channel_id=1, source_target_pairs={{0,1},{1,0},{2,3},{3,2},{4,5},{5,4},{6,7},{7,6},{8,9},{9,8},{10,11... | collective-permute-start | bytes 1572872 | tf_op jit(solution)/shard_map/ppermute | solution.py:736
  141.8 12.5 %all-to-all-start.1 = ((bf16[4,4,16,1024]{3,2,1,0:T(8,128)(2,1)}), bf16[4,4,16,1024]{3,2,1,0:T(8,128)(2,1)S(1)}, u32[]{:S(2)}, u32[]{:S(2)}) async-start(bf16[4,4,16,1024]{3,2,1,0:T(8,128)(2,1)} %add_convert_fusion.1), calls=%async_computation.1 | async-start | bytes 1048576 | tf_op jit(solution)/shard_map/all_to_all | solution.py:774
  154.2 15.7 %all-to-all-start.3 = ((bf16[4,16,2816]{2,1,0:T(8,128)(2,1)}), bf16[4,16,2816]{2,1,0:T(8,128)(2,1)S(1)}, u32[]{:S(2)}, u32[]{:S(2)}) async-start(bf16[4,16,2816]{2,1,0:T(8,128)(2,1)} %fusion), calls=%async_computation.3 | async-start | bytes 720896 | tf_op jit(solution)/shard_map/all_to_all | solution.py:774
  170.0 9.0 %copy-start.1 = (bf16[4,16,2816]{2,1,0:T(8,128)(2,1)}, bf16[4,16,2816]{2,1,0:T(8,128)(2,1)S(1)}, u32[]{:S(2)}) copy-start(bf16[4,16,2816]{2,1,0:T(8,128)(2,1)S(1)} %all-to-all-done.3.others) | copy-start | bytes 1081348
  180.8 1.4 collective-permute-start.22
  183.6 12.4 %all-to-all-start.4 = ((f32[16,24,128]{2,1,0:T(8,128)}), f32[16,24,128]{2,1,0:T(8,128)S(1)}, u32[]{:S(2)}, u32[]{:S(2)}) async-start(f32[16,24,128]{2,1,0:T(8,128)} %broadcast_in_dim.13), calls=%async_computation.4 | async-start | bytes 393216 | tf_op jit(solution)/shard_map/all_to_all | solution.py:774
  187.3 1.5 collective-permute-start.21
  188.8 7.3 %copy-start.5 = (f32[16,512]{1,0:T(8,128)}, f32[16,512]{1,0:T(8,128)S(1)}, u32[]{:S(2)}) copy-start(f32[16,512]{1,0:T(8,128)S(1)} %collective-permute-done.21.swapped) | copy-start | bytes 98308
  (1 other events, 0.7 us)

commit v5 on v4

--- a/solution.py
+++ b/solution.py
@@ -57,7 +57,7 @@
 SMALL_ROWS, SMALL_BIAS, SMALL_SIDE = 32, 14, 22
 
 F32, BF16 = jnp.float32, jnp.bfloat16
-VMEM_BYTES = 60 * 1024 * 1024
+MIB = 1024 * 1024
 
 
 def dot_nn(a, b):
@@ -147,17 +147,18 @@
 
 
 def disperse(g_ref, place_ref, keep_ref, send_ref, halves, scaled=True):
-    is_first = place_ref[1] == 0
+    me, core = place_ref[0], place_ref[1]
+    is_first = core == 0
 
     def block(i, _):
         p, z = i >> 2, i & 3
-        row = pl.multiple_of((4 * z + p) * 16, 16)
+        row = pl.multiple_of((me ^ (4 * z + p)) * 16, 16)
         for src, width, dest in halves:
             low = g_ref[pl.ds(row, 16), dest : dest + width]
             high = g_ref[pl.ds(row, 16), dest + width : dest + 2 * width]
             if scaled and dest == COL_QKV:
                 low, high = low * 0.125, high * 0.125
-            keep_ref[p, z, :, src : src + width] = jnp.where(is_first, low, high)
+            keep_ref[p, z, :, src : src + width] = jnp.where(is_first, low, high).astype(BF16)
             send_ref[p, z, :, src : src + width] = jnp.where(is_first, high, low).astype(BF16)
         return 0
 
@@ -183,7 +184,7 @@
 
 
 def layer_forward(x_ref, w_ref, vec, bias, kept, work):
-    qt_ref, kv_ref, pt_ref, r_ref, ot_ref, o_ref, m_ref, h_ref, gp_ref, a_ref, c_ref = kept
+    qt_ref, kv_ref, p0, p1, p2, r_ref, ot_ref, o_ref, m_ref, h_ref, gp_ref, a_ref, c_ref = kept
     qst_ref, vt_ref, mask_ref, wqt_ref, u_ref, y_ref = work
     for rows in tiles(SEQ, TILE):
         a_ref[rows] = (normalise(x_ref[rows])[0] * vec[0:1] + vec[1:2]).astype(BF16)
@@ -195,19 +196,18 @@
     turned = jnp.transpose(kv_ref[:, 256:512])
     for h in range(HEADS):
         vt_ref[VALUE_ROWS * h : VALUE_ROWS * h + HEAD_DIM] = turned[head_rows(h)]
-    for i in range(BLOCKS):
+    for i, pt_ref in enumerate((p0, p1, p2)):
         seen, first = BLOCK * (i + 1), BLOCK * i
-        lanes = block_lanes(i)
-        scores = dot_nn(kv_ref[0:seen, 0:256], qst_ref[:, lanes])
+        scores = dot_nn(kv_ref[0:seen, 0:256], qst_ref[:, block_lanes(i)])
         last = scores[first:] + mask_ref[...]
         peak = jnp.max(last, axis=0, keepdims=True)
         if i:
             peak = jnp.maximum(peak, jnp.max(scores[0:first], axis=0, keepdims=True))
-            pt_ref[0:first, lanes] = jnp.exp(scores[0:first] - peak).astype(BF16)
-        pt_ref[first:seen, lanes] = jnp.exp(last - peak).astype(BF16)
+            pt_ref[0:first] = jnp.exp(scores[0:first] - peak).astype(BF16)
+        pt_ref[first:seen] = jnp.exp(last - peak).astype(BF16)
         for h in range(HEADS):
             values = vt_ref[VALUE_ROWS * h : VALUE_ROWS * (h + 1), 0:seen]
-            out = dot_nn(values, pt_ref[0:seen, block_lanes(i, h)])
+            out = dot_nn(values, pt_ref[:, BLOCK * h : BLOCK * (h + 1)])
             inverse = 1.0 / out[HEAD_DIM : HEAD_DIM + 1]
             r_ref[h : h + 1, first:seen] = inverse
             ot_ref[head_rows(h), first:seen] = (out[0:HEAD_DIM] * inverse).astype(BF16)
@@ -229,10 +229,10 @@
     g_ref[:, column : column + right.shape[1]] += dot_tn(left, right)
 
 
-def ff_backward(grad_ref, grad16_ref, w_ref, vec, kept, g_ref, g_up, g_down, v_ref, v_row, bias_row, work, mid_ref, mid16_ref):
+def ff_backward(grad_ref, grad16_ref, w_ref, w_up, w_down, vec, kept, g_ref, g_up, g_down, v_ref, v_row, bias_row, work, mid_ref, mid16_ref):
     m_ref, h_ref, gp_ref, c_ref = kept
     du_ref, ones_ref, u_ref, y_ref = work
-    u_ref[...] = dot_nn(grad16_ref[...], w_ref[:, COL_DOWN : COL_DOWN + FF])
+    u_ref[...] = dot_nn(grad16_ref[...], w_ref[:, w_down : w_down + FF])
     for rows in tiles(SEQ, TILE):
         du_ref[rows] = u_ref[rows].astype(BF16) * gp_ref[rows]
     add_gradient(g_ref, g_down, grad16_ref[...], h_ref[...])
@@ -240,7 +240,7 @@
     bias_grad = dot_nn(ones_ref[...], du_ref[...])
     for chunk in range(4):
         v_ref[bias_row + chunk, 0:1] += bias_grad[0:1, 256 * chunk : 256 * chunk + 256]
-    y_ref[...] = dot_nt(du_ref[...], w_ref[:, COL_UP : COL_UP + FF])
+    y_ref[...] = dot_nt(du_ref[...], w_ref[:, w_up : w_up + FF])
     totals = [None] * 3
     for rows in tiles(SEQ, TILE):
         xhat, scale = normalise(m_ref[rows])
@@ -256,7 +256,7 @@
 
 
 def attention_backward(mid_ref, mid16_ref, w_ref, vec, kept, g_ref, v_ref, v_row, work, out_ref):
-    x_ref, qt_ref, kv_ref, pt_ref, r_ref, ot_ref, o_ref, a_ref = kept
+    x_ref, qt_ref, kv_ref, p0, p1, p2, r_ref, ot_ref, o_ref, a_ref = kept
     dost_ref, qst_ref, kt_ref, dst_ref, dqt_ref, dkv_ref, dqkv_ref, proj_ref, y_ref = work
     add_gradient(g_ref, COL_PROJ, mid16_ref[0:SEQ], o_ref[...])
     grad_o = dot_nt(proj_ref[...], mid16_ref[...]).astype(BF16).astype(F32)
@@ -268,17 +268,20 @@
         scaled = scaled.astype(BF16)
         for i in range(BLOCKS):
             dost_ref[head_rows(h), block_lanes(i, h)] = scaled[:, BLOCK * i : BLOCK * (i + 1)]
-    for i in range(BLOCKS):
+    for i, pt_ref in enumerate((p0, p1, p2)):
         seen, first = BLOCK * (i + 1), BLOCK * i
         lanes = block_lanes(i)
         delta = jnp.concatenate([a[:, first:seen] for a in deltas], axis=1)
         grad = dot_nn(kv_ref[0:seen, 256:512], dost_ref[:, lanes])
-        dst_ref[0:seen, lanes] = pt_ref[0:seen, lanes] * (grad - delta).astype(BF16)
+        dst_ref[0:seen, lanes] = pt_ref[...] * (grad - delta).astype(BF16)
         for h in range(HEADS):
             out = dot_nn(kt_ref[head_rows(h), 0:seen], dst_ref[0:seen, block_lanes(i, h)])
             dqt_ref[head_rows(h), first:seen] = out.astype(BF16)
-        for at, left, right in ((0, dst_ref, qst_ref), (256, pt_ref, dost_ref)):
-            out = dot_nt(left[0:seen, lanes], right[:, lanes])
+        for at, left, right in (
+            (0, dst_ref[0:seen, lanes], qst_ref),
+            (256, pt_ref[...], dost_ref),
+        ):
+            out = dot_nt(left, right[:, lanes])
             if i:
                 dkv_ref[0:first, at : at + 256] += out[0:first]
             dkv_ref[first:seen, at : at + 256] = out[first:]
@@ -370,15 +373,16 @@
 def first_forward_kernel(*refs):
     place_ref, meta_ref, vec_ref, bias_ref, bias_other = refs[0:5]
     mine, other = refs[5:9], refs[9:13]
-    w_out, side_out, next_ref, hits_ref, x_ref = refs[13:18]
-    kept = [ref.at[0] for ref in refs[18:29]]
-    w_ref = refs[29]
-    work = refs[30:36]
+    w_attention, w_ff, side_out, next_ref, hits_ref, x_ref = refs[13:19]
+    kept = [ref.at[0] for ref in refs[19:32]]
+    w_ref = refs[32]
+    work = refs[33:39]
 
     @pl.when(pl.program_id(0) == 0)
     def _():
         assemble(mine, other, place_ref, w_ref, HALF_FIRST)
-        w_out[...] = w_ref[...]
+        w_attention[...] = w_ref[:, 0:COL_UP]
+        w_ff[...] = w_ref[:, COL_UP:COL_TABLE]
         side_out[...] = w_ref[:, COL_SMALL:]
         start_forward(work, w_ref)
 
@@ -388,7 +392,7 @@
     vec = vec_ref[0:6]
     layer_forward(x_ref.at[0], w_ref, vec, bias, kept, work)
     for rows in tiles(SEQ, TILE):
-        next_ref[0, rows] = kept[6][rows] + (work[5][rows] + vec[5:6])
+        next_ref[0, rows] = kept[8][rows] + (work[5][rows] + vec[5:6])
 
 
 def codebook_losses(logits, meta):
@@ -432,14 +436,14 @@
     grad_ref, keep_ref, send_ref, v_out, scalar_ref = refs[16:21]
     refs = refs[1:]
     w_ref, g_ref, v_ref = refs[20:23]
-    kept = refs[23:34]
-    qt_ref, kv_ref, pt_ref, r_ref, ot_ref, o_ref, m_ref, h_ref, gp_ref, a_ref, c_ref = kept
-    forward_work = refs[34:40]
+    kept = refs[23:36]
+    m_ref, h_ref, gp_ref, a_ref, c_ref = kept[8:13]
+    forward_work = refs[36:42]
     u_ref, y_ref = forward_work[4:6]
-    backward_work = refs[40:47]
-    proj_ref = refs[47]
-    du_ref, ones_ref, up_ref, up16_ref, mid_ref, mid16_ref = refs[48:54]
-    last_ref, final_ref, logit_ref, dlogit_ref, pick_ref, put_ref = refs[54:60]
+    backward_work = refs[42:49]
+    proj_ref = refs[49]
+    du_ref, ones_ref, up_ref, up16_ref, mid_ref, mid16_ref = refs[50:56]
+    last_ref, final_ref, logit_ref, dlogit_ref, pick_ref, put_ref = refs[56:62]
     dost_ref = backward_work[0]
     step = pl.program_id(0)
 
@@ -507,6 +511,8 @@
         up_ref,
         up16_ref,
         w_ref,
+        COL_UP,
+        COL_DOWN,
         vec,
         (m_ref, h_ref, gp_ref, c_ref),
         g_ref,
@@ -524,7 +530,7 @@
         mid16_ref,
         w_ref,
         vec,
-        (x_ref, qt_ref, kv_ref, pt_ref, r_ref, ot_ref, o_ref, a_ref),
+        (x_ref,) + tuple(kept[0:8]) + (a_ref,),
         g_ref,
         v_ref,
         6,
@@ -566,6 +572,8 @@
         grad_ref.at[0],
         grad16_ref,
         w_ref,
+        GRAD_UP,
+        GRAD_DOWN,
         vec_ref[0:6],
         kept,
         g_ref,
@@ -587,10 +595,10 @@
 
 def attention_backward_kernel(*refs):
     place_ref, vec_ref, w_ref, mid_ref, hits_ref, v_in = refs[0:6]
-    kept = [ref.at[0] for ref in refs[6:14]]
-    keep_ref, send_ref, v_out = refs[15:18]
-    g_ref, v_ref, mid16_ref, out16_ref = refs[18:22]
-    work = refs[22:31]
+    kept = [ref.at[0] for ref in refs[6:16]]
+    keep_ref, send_ref, v_out = refs[17:20]
+    g_ref, v_ref, mid16_ref, out16_ref = refs[20:24]
+    work = refs[24:33]
     dost_ref, qst_ref, proj_ref = work[0], work[1], work[7]
     step = pl.program_id(0)
 
@@ -622,18 +630,18 @@
         disperse(g_ref, place_ref, keep_ref, send_ref, HALF_GRAD_REST)
 
 
-def pack_layer(attn, proj, up, down, layer, out, at):
+def pack_layer(attn, proj, up, down, layer, out):
     for j in range(3):
-        out[:, at + 128 * j : at + 128 * j + 128] = attn[layer, j].astype(BF16)
-    out[:, at + 384 : at + 512] = proj[layer].astype(BF16)
-    out[:, at + 512 : at + 1024] = up[layer].astype(BF16)
-    out[:, at + 1024 : at + 1536] = down[layer].astype(BF16)
-
-
-def pack_kernel(place_ref, table, attn, proj, up, down, head, side, out, pad_ref):
-    pack_layer(attn, proj, up, down, 0, out, 0)
-    pack_layer(attn, proj, up, down, 1, out, HALF_FIRST_COLS)
-    out[:, HALF_FIRST_COLS + 1536 :] = head[...].astype(BF16)
+        out[:, 128 * j : 128 * j + 128] = attn[layer, j].astype(BF16)
+    out[:, 384:512] = proj[layer].astype(BF16)
+    out[:, 512:1024] = up[layer].astype(BF16)
+    out[:, 1024:1536] = down[layer].astype(BF16)
+
+
+def pack_kernel(place_ref, table, attn, proj, up, down, head, side, first, second, pad_ref):
+    pack_layer(attn, proj, up, down, 0, first)
+    pack_layer(attn, proj, up, down, 1, second)
+    second[:, 1536:1792] = head[...].astype(BF16)
     rows = side.shape[1]
     eye = (
         lax.broadcasted_iota(jnp.int32, (rows, rows), 0)
@@ -643,15 +651,19 @@
     pad_ref[...] = jnp.zeros(pad_ref.shape, F32)
     pad_ref[:, 0:5] = dot_nt(eye, side[...].astype(BF16))
     high = jnp.concatenate([table[:, 512:896], pad_ref[...]], axis=1)
-    out[:, 1536:2048] = jnp.where(place_ref[1] == 0, table[:, 0:512], high).astype(BF16)
-
-
-def finish_kernel(place_ref, rest, others, scalar_ref, out_rest, out_other, out_table, out_small):
+    first[:, 1536:2048] = jnp.where(place_ref[1] == 0, table[:, 0:512], high).astype(BF16)
+
+
+def finish_kernel(*refs):
+    count = (len(refs) - 6) // 2
+    place_ref = refs[0]
+    scalar_ref = refs[2 * count + 1]
+    out_rest, out_other, out_table, out_small = refs[2 * count + 2 :]
     square = jnp.zeros((1, 1), F32)
-    for pieces, out in ((rest, out_rest), (others, out_other)):
-        total = pieces[0].astype(F32)
-        for i in range(1, pieces.shape[0]):
-            total = total + pieces[i].astype(F32)
+    for pieces, out in ((refs[1 : count + 1], out_rest), (refs[count + 1 : 2 * count + 1], out_other)):
+        total = pieces[0][...]
+        for piece in pieces[1:]:
+            total = total + piece[...].astype(F32)
         out[...] = total
         square = square + column_sum(jnp.sum(total * total, axis=1, keepdims=True))
     small = out_rest[:, 896:1024]
@@ -757,29 +769,38 @@
     return [whole[:, p] for p in range(4)]
 
 
-def in_pieces(blocks, n_high):
+def in_pieces(blocks, wide, n_high):
+    cols = blocks.shape[-1]
     if n_high == 4:
         return blocks
-    cols = blocks.shape[-1]
-    whole = blocks.transpose(1, 0, 2, 3).reshape(n_high, 4, 64 // n_high, cols)
-    return whole.transpose(1, 0, 2, 3)
-
-
-def add_cores(keep, send, n_high):
-    keep, send = in_pieces(keep, n_high), in_pieces(send, n_high)
-    return keep + swap(send, "narrow", 1).astype(F32)
-
-
-def exchange(a, groups):
-    return lax.all_to_all(a, "wide", 0, 0, axis_index_groups=groups)
-
-
-def plane_groups(n_high):
-    return [[4 * h + p for p in range(4)] for h in range(n_high)]
-
-
-def column_groups(n_high):
-    return [[4 * h + p for h in range(n_high)] for p in range(4)]
+    rows = 64 // n_high
+    whole = blocks.transpose(1, 0, 2, 3).reshape(4 * n_high, rows, cols)
+    whole = whole[wide ^ jnp.arange(4 * n_high)]
+    return whole.reshape(n_high, 4, rows, cols).transpose(1, 0, 2, 3)
+
+
+def add_cores(keep, send, wide, n_high):
+    keep, send = in_pieces(keep, wide, n_high), in_pieces(send, wide, n_high)
+    received = swap(send, "narrow", 1)
+    return [keep[p].astype(F32) + received[p].astype(F32) for p in range(4)]
+
+
+def swap_plane(sums):
+    return [swap(sums[p].astype(BF16), "wide", p) for p in range(1, 4)]
+
+
+def add_plane(own, received):
+    for a in received:
+        own = own + a.astype(F32)
+    return own
+
+
+def column_pieces(own):
+    return [own[0]] + [swap(own[k].astype(BF16), "wide", 4 * k) for k in range(1, own.shape[0])]
+
+
+def resident(arrays):
+    return [pltpu.with_memory_space_constraint(a, pltpu.VMEM) for a in arrays]
 
 
 def full_spec(a):
@@ -797,6 +818,18 @@
 VMEM_SPEC = pl.BlockSpec(memory_space=pltpu.VMEM)
 ANY_SPEC = pl.BlockSpec(memory_space=pl.ANY)
 SMEM_SPEC = pl.BlockSpec(memory_space=pltpu.SMEM)
+
+
+VMEM_MIB = {
+    "pack": 58,
+    "prepare": 58,
+    "first_forward": 36,
+    "middle": 34,
+    "ff_backward": 30,
+    "attention_backward": 30,
+    "finish": 58,
+    "adam": 58,
+}
 
 
 def call(kernel, grid, in_specs, out_specs, out_shape, scratch, flops, bytes_accessed, name):
@@ -807,7 +840,7 @@
         out_specs=out_specs,
         out_shape=out_shape,
         scratch_shapes=scratch,
-        compiler_params=pltpu.CompilerParams(vmem_limit_bytes=VMEM_BYTES),
+        compiler_params=pltpu.CompilerParams(vmem_limit_bytes=VMEM_MIB[name] * MIB),
         cost_estimate=pl.CostEstimate(
             flops=flops, bytes_accessed=bytes_accessed, transcendentals=0
         ),
@@ -819,7 +852,9 @@
 KEPT = (
     ((D, KEYS), BF16),
     ((KEYS, 512), BF16),
-    ((KEYS, BLOCKS * QUERIES), BF16),
+    ((BLOCK, QUERIES), BF16),
+    ((2 * BLOCK, QUERIES), BF16),
+    ((3 * BLOCK, QUERIES), BF16),
     ((8, KEYS), F32),
     ((D, KEYS), BF16),
     ((SEQ, D), BF16),
@@ -907,18 +942,19 @@
     )
     table, attn, proj, up, _, down, _, head, side = (group[0] for group in params)
 
-    piece = call(
+    piece_first, piece_second = call(
         pack_kernel,
         None,
         [SMEM_SPEC] + [VMEM_SPEC] * 7,
-        VMEM_SPEC,
-        shaped((rows, HALF_FIRST_COLS + HALF_SECOND_COLS), BF16),
+        [VMEM_SPEC] * 2,
+        [shaped((rows, HALF_FIRST_COLS), BF16), shaped((rows, HALF_SECOND_COLS), BF16)],
         [pltpu.VMEM((rows, 128), F32)],
         10**6,
         10**6,
         "pack",
     )(place, table, attn, proj, up, down, head, side)
-    column = swap_column(piece, n_high)
+    other_bias = swap(up_bias, "narrow", 1)
+    column = swap_column(piece_first, n_high)
 
     count = tokens.shape[0] // lax.axis_size("narrow")
     meta, frame_meta = call(
@@ -931,40 +967,46 @@
         10**6,
         10**6,
         "prepare",
-    )(place, game_ids, flat(tokens), actions, valid_steps, rewards, end_flags, piece)
-    column, meta = lax.optimization_barrier((column, meta))
-    first_mine = gather_plane(jnp.stack([a[:, :HALF_FIRST_COLS] for a in column]))
-    second_column = jnp.stack([a[:, HALF_FIRST_COLS:] for a in column])
-    second_column, last = lax.optimization_barrier((second_column, first_mine[3]))
-    first_mine = first_mine[0:3] + [last]
+    )(place, game_ids, flat(tokens), actions, valid_steps, rewards, end_flags, piece_first)
+    column, meta, other_bias = lax.optimization_barrier((column, meta, other_bias))
+    first_column = jnp.stack(column)
+    beside, above = swap(first_column, "wide", 1), swap(first_column, "wide", 2)
+    beside, first_column, piece_second = lax.optimization_barrier(
+        (beside, first_column, piece_second)
+    )
+    across = swap(first_column, "wide", 3)
+    second_column = jnp.stack(swap_column(piece_second, n_high))
+    second_column, across = lax.optimization_barrier((second_column, across))
+    first_mine = [first_column, beside, above, across]
     first_other = gather_cores(first_mine)
     second_mine = gather_plane(second_column)
     first_parts = in_blocks(first_mine, wide) + in_blocks(first_other, wide)
-    other_bias = swap(up_bias, "narrow", 1)
 
     kept_specs = [row_spec(shape) for shape, _ in KEPT]
     kept_shapes = [shaped((count,) + shape, dtype) for shape, dtype in KEPT]
     row_f32 = shaped((count, SEQ, D), F32)
     meta_spec = row_spec((SEQ, 128))
     vec_specs = [full_spec(vectors), full_spec(up_bias), full_spec(up_bias)]
-    w_spec = pl.BlockSpec((D, COL_FIRST), lambda i: (0, 0))
+    w_attention_spec = pl.BlockSpec((D, 1024), lambda i: (0, 0))
+    w_ff_spec = pl.BlockSpec((D, 2048), lambda i: (0, 0))
     side_spec = pl.BlockSpec((D, 128), lambda i: (0, 0))
     hits_spec = row_spec((SEQ, ROWS))
     results = call(
         first_forward_kernel,
         (count,),
-        [SMEM_SPEC, meta_spec] + vec_specs + [full_spec(a) for a in first_parts],
-        [w_spec, side_spec, row_spec((SEQ, D)), hits_spec, row_spec((SEQ, D))] + kept_specs,
-        [shaped((D, COL_FIRST), BF16), shaped((D, 128), BF16), row_f32]
+        [SMEM_SPEC, meta_spec] + vec_specs + [VMEM_SPEC] * 8,
+        [w_attention_spec, w_ff_spec, side_spec, row_spec((SEQ, D)), hits_spec, row_spec((SEQ, D))]
+        + kept_specs,
+        [shaped((D, 1024), BF16), shaped((D, 2048), BF16), shaped((D, 128), BF16), row_f32]
         + [shaped((count, SEQ, ROWS), BF16), row_f32]
         + kept_shapes,
         [pltpu.VMEM((D, COL_FIRST), BF16)] + FORWARD_WORK,
         4 * 10**9,
         20 * 10**6,
         "first_forward",
-    )(place, meta, vectors, up_bias, other_bias, *first_parts)
-    w_first, side_copy, stream, hits, stream_first = results[0:5]
-    kept = results[5:]
+    )(place, meta, vectors, up_bias, other_bias, *resident(first_parts))
+    w_attention, w_ff, side_copy, stream, hits, stream_first = results[0:6]
+    kept = results[6:]
     received, side_copy = lax.optimization_barrier((second_mine[1:], side_copy))
     second_mine = second_mine[0:1] + received
     second_other = gather_cores(second_mine)
@@ -974,7 +1016,7 @@
         return pl.BlockSpec((4, 4, 16, cols), lambda i: (0, 0, 0, 0))
 
     def block_shapes(cols):
-        return [shaped((4, 4, 16, cols), F32), shaped((4, 4, 16, cols), BF16)]
+        return [shaped((4, 4, 16, cols), BF16)] * 2
 
     small_spec = pl.BlockSpec((SMALL_ROWS, 8, D), lambda i: (0, 0, 0))
     small_shape = shaped((SMALL_ROWS, 8, D), F32)
@@ -986,7 +1028,7 @@
         [SMEM_SPEC, meta_spec, row_spec((SIDE_ROWS, 128))]
         + vec_specs
         + [side_spec, row_spec((SEQ, D))]
-        + [full_spec(a) for a in second_parts],
+        + [VMEM_SPEC] * 8,
         [row_spec((SEQ, D))] + [blocks(HALF_SECOND_COLS)] * 2 + [small_spec, scalar_spec],
         [row_f32] + block_shapes(HALF_SECOND_COLS) + [small_shape, shaped((8, 128), F32)],
         [
@@ -1015,14 +1057,14 @@
         15 * 10**9,
         20 * 10**6,
         "middle",
-    )(place, meta, frame_meta, vectors, up_bias, other_bias, side_copy, stream, *second_parts)
-    second_sums = add_cores(keep_second, send_second, n_high)
-
-    kept_ff = (kept[6], kept[7], kept[8], kept[10])
+    )(place, meta, frame_meta, vectors, up_bias, other_bias, side_copy, stream, *resident(second_parts))
+    second_sums = add_cores(keep_second, send_second, wide, n_high)
+
+    kept_ff = (kept[8], kept[9], kept[10], kept[12])
     grad_mid, keep_ff, send_ff, small_grads = call(
         ff_backward_kernel,
         (count,),
-        [SMEM_SPEC, full_spec(vectors), w_spec, row_spec((SEQ, D)), small_spec]
+        [SMEM_SPEC, full_spec(vectors), w_ff_spec, row_spec((SEQ, D)), small_spec]
         + [row_spec(a.shape[1:]) for a in kept_ff],
         [row_spec((SEQ, D))] + [blocks(HALF_GRAD_COLS)] * 2 + [small_spec],
         [row_f32] + block_shapes(HALF_GRAD_COLS) + [small_shape],
@@ -1038,16 +1080,15 @@
         4 * 10**9,
         10 * 10**6,
         "ff_backward",
-    )(place, vectors, w_first, grad_stream, small_grads, *kept_ff)
-    ff_sums = add_cores(keep_ff, send_ff, n_high)
-    other_sums = jnp.concatenate([second_sums.astype(BF16), ff_sums.astype(BF16)], axis=-1)
-    others = exchange(other_sums, plane_groups(n_high))
-
-    kept_attention = (stream_first,) + tuple(kept[0:6]) + (kept[9],)
+    )(place, vectors, w_ff, grad_stream, small_grads, *kept_ff)
+    ff_sums = add_cores(keep_ff, send_ff, wide, n_high)
+    other_sums = [jnp.concatenate(pair, axis=-1) for pair in zip(second_sums, ff_sums)]
+    others_received = swap_plane(other_sums)
+    kept_attention = (stream_first,) + tuple(kept[0:8]) + (kept[11],)
     keep_rest, send_rest, small_grads = call(
         attention_backward_kernel,
         (count,),
-        [SMEM_SPEC, full_spec(vectors), w_spec, row_spec((SEQ, D)), hits_spec, small_spec]
+        [SMEM_SPEC, full_spec(vectors), w_attention_spec, row_spec((SEQ, D)), hits_spec, small_spec]
         + [row_spec(a.shape[1:]) for a in kept_attention]
         + [ANY_SPEC],
         [blocks(HALF_GRAD_COLS)] * 2 + [pl.BlockSpec((SMALL_ROWS, D), lambda i: (0, 0))],
@@ -1059,22 +1100,17 @@
         6 * 10**9,
         20 * 10**6,
         "attention_backward",
-    )(place, vectors, w_first, grad_mid, hits, small_grads, *kept_attention, other_sums)
-    others, keep_rest = lax.optimization_barrier((others, keep_rest))
-    rest_sums = add_cores(keep_rest, send_rest, n_high).astype(BF16)
-    rest = exchange(rest_sums, plane_groups(n_high))
-
-    def along_column(parts):
-        parts = [parts[p].astype(F32) for p in range(4)]
-        total = (parts[0] + parts[1]) + (parts[2] + parts[3])
-        return exchange(total.astype(BF16), column_groups(n_high))
-
-    others, rest = along_column(others), along_column(rest)
+    )(place, vectors, w_attention, grad_mid, hits, small_grads, *kept_attention, other_sums[0])
+    others_received, keep_rest = lax.optimization_barrier((others_received, keep_rest))
+    rest_sums = add_cores(keep_rest, send_rest, wide, n_high)
+    rest_received = swap_plane(rest_sums)
+    other_pieces = column_pieces(add_plane(other_sums[0], others_received))
+    rest_pieces = column_pieces(add_plane(rest_sums[0], rest_received))
 
     grad_rest, grad_others, table_part, small = call(
         finish_kernel,
         None,
-        [SMEM_SPEC] + [VMEM_SPEC] * 3,
+        [SMEM_SPEC] + [VMEM_SPEC] * (2 * n_high + 1),
         [VMEM_SPEC] * 4,
         [
             shaped((rows, HALF_GRAD_COLS), F32),
@@ -1086,12 +1122,13 @@
         10**6,
         10**6,
         "finish",
-    )(place, rest, others, scalars)
+    )(place, *resident(rest_pieces + other_pieces), scalars)
 
     beside = swap(small, "narrow", 1)
     is_small = (jnp.arange(rows + 8) < rows)[:, None]
     small = jnp.where(is_small, jnp.where(core == 1, small, beside), small + beside)
-    gathered = exchange(jnp.broadcast_to(small, (4 * n_high,) + small.shape), None)
+    small = jnp.broadcast_to(small, (4 * n_high,) + small.shape)
+    gathered = lax.all_to_all(small, "wide", 0, 0)
     quarters = []
     if not fast:
         total = lax.psum(small_grads, ("wide", "narrow"))
@@ -1109,7 +1146,7 @@
         10**6,
         10**6,
         "adam",
-    )(place, grad_rest, grad_others, swapped, gathered, *quarters, *flat_params)
+    )(place, grad_rest, grad_others, *resident([swapped, gathered]), *quarters, *flat_params)
     news = list(results[3:])
     for group in (0, 2, 5, 8):
         for member in range(3 * group, 3 * group + 3):

time: 200 us -> 169 us (0.84)
  waiting for transfers between devices: 49.4 us -> 32 us
  Pallas kernels: 95.4 us -> 82.5 us
  starting transfers between devices: 31.9 us -> 42.7 us
  blocking collectives: 8.95 us -> 0 us
  other arithmetic: 7.53 us -> 4.18 us
    ppermute x23 -> x38, starting transfers between devices: 14.9 us -> 37.6 us  [swap(): return lax.ppermute(a, axis, [(i, i ^ distance) for i in range(size)])]
    all_to_all x4 -> x1, waiting for transfers between devices: 25.5 us -> 7.49 us  [per_device(): gathered = lax.all_to_all(small, 'wide', 0, 0)]
    all_to_all x4 -> x1, starting transfers between devices: 16.9 us -> 5.02 us  [per_device(): gathered = lax.all_to_all(small, 'wide', 0, 0)]
    all_to_all x1 -> x0, blocking collectives: 8.95 us -> none  [exchange(): return lax.all_to_all(a, 'wide', 0, 0, axis_index_groups=groups)]
    convert_element_type x5 -> x1, other arithmetic: 4.75 us -> 0.12 us  [swap_plane(): return [swap(sums[p].astype(BF16), 'wide', p) for p in range(1, 4)]]
    pallas_call x3, Pallas kernels: 14 us -> 9.84 us  [the longest x1 6.64 us: per_device(): call(ff_backward_kernel, (count,), [SMEM_SPEC, full_spec(vectors), w_ff_s...]
    pallas_call x1, Pallas kernels: 17.4 us -> 14.2 us  [per_device(): call(attention_backward_kernel, (count,), [SMEM_SPEC, full_spec(vectors),...]
    pallas_call x1, Pallas kernels: 39 us -> 35.9 us  [per_device(): call(middle_kernel, (count,), [SMEM_SPEC, meta_spec, row_spec((SIDE_ROWS,...]
  transfers between devices with their start and end apart: 27 -> 39, of which waited for: 15 -> 18; matrix products, arithmetic and copies ran while one was open for 1% -> 1% of each run, Pallas kernels for 25% -> 24%
where the time goes in v5:
time: 169 us; the launch traced here: 168 us
  Pallas kernels  82.5 us (49%)
  starting transfers between devices  42.7 us (25%)
  waiting for transfers between devices  32 us (19%)
  local copies, waits for them, and re-layouts  6 us (4%)
  other arithmetic  4.18 us (2%)
    ppermute x38, starting transfers between devices, swap(): return lax.ppermute(a, axis, [(i, i ^ distance) for i in range(size)])  37.6 us
    pallas_call x1, Pallas kernels, per_device(): call(middle_kernel, (count,), [SMEM_SPEC, meta_spec, row_spec((SIDE_ROWS,...  35.9 us
    ppermute x38, waiting for transfers between devices, swap(): return lax.ppermute(a, axis, [(i, i ^ distance) for i in range(size)])  24.5 us
    pallas_call x1, Pallas kernels, per_device(): call(first_forward_kernel, (count,), [SMEM_SPEC, meta_spec] + vec_specs +...  16.8 us
    pallas_call x1, Pallas kernels, per_device(): call(attention_backward_kernel, (count,), [SMEM_SPEC, full_spec(vectors),...  14.2 us
    all_to_all x1, waiting for transfers between devices, per_device(): gathered = lax.all_to_all(small, 'wide', 0, 0)  7.49 us
    pallas_call x1, Pallas kernels, per_device(): call(ff_backward_kernel, (count,), [SMEM_SPEC, full_spec(vectors), w_ff_s...  6.64 us
    unnamed x34, local copies, waits for them, and re-layouts  5.27 us
  transfers between devices with their start and end apart: 39, of which 18 were waited for; matrix products, arithmetic and copies ran while one was open for 1% of the time, Pallas kernels for 24%

profile of v5, /device:TPU:0, one launch (start us, length us, event | category | flops | bytes accessed | tf_op | source)
XLA Modules:
  0.0 168.5 jit_solution(3897944120893157073)
XLA Ops:
  1.3 1.7 %pack.1 = (bf16[16,2048]{1,0:T(8,128)(2,1)}, bf16[16,1792]{1,0:T(8,128)(2,1)}) custom-call(s32[3]{0:T(128)} %pad_add_fusion.place_ref.refs_0_, f32[16,896]{1,0:T(8,128)} %bitcast.86, f32[2,3,16,128]{3,2,1,0:T(8,128)} %refs_3_.5, f32[2,16,128]{2,1,0:T(8,128)} %bitcast.88, f32[2,16,512]{2,1,0:T(8,128)} %refs_9_.1, f32[2,16,512]{2,1,0:T(8,128)} %bitcast.83, ...), custom_call_target="tpu_custom_call" | custom-call | flops 1000000 | bytes 1000000 | tf_op jit(solution)/shard_map/pack/pallas_call | solution.py:945
  3.1 3.0 %collective-permute-start = (bf16[16,2048]{1,0:T(8,128)(2,1)}, bf16[16,2048]{1,0:T(8,128)(2,1)S(1)}, u32[]{:S(2)}, u32[]{:S(2)}) collective-permute-start(bf16[16,2048]{1,0:T(8,128)(2,1)} %get-tuple-element.122.after), channel_id=1, source_target_pairs={{0,8},{2,10},{4,12},{6,14},{8,0},{10,2},{12,4},{14,6},{16,24},{18,... | collective-permute-start | bytes 196616 | tf_op jit(solution)/shard_map/ppermute | solution.py:748
  6.1 2.6 %collective-permute-start.1 = (bf16[16,2048]{1,0:T(8,128)(2,1)}, bf16[16,2048]{1,0:T(8,128)(2,1)S(1)}, u32[]{:S(2)}, u32[]{:S(2)}) collective-permute-start(bf16[16,2048]{1,0:T(8,128)(2,1)} %get-tuple-element.122.after), channel_id=1, source_target_pairs={{0,16},{2,18},{4,20},{6,22},{8,24},{10,26},{12,28},{14,30},{16,0},... | collective-permute-start | bytes 196616 | tf_op jit(solution)/shard_map/ppermute | solution.py:748
  8.7 3.3 %prepare.1 = (s32[4,352,128]{2,1,0:T(8,128)}, s32[4,32,128]{2,1,0:T(8,128)}) custom-call(s32[3]{0:T(128)} %pad_add_fusion.place_ref.refs_0_, s32[8]{0:T(128)} %games_ref.1, s32[8,16,20]{2,1,0:T(8,128)} %bitcast.92, s32[8,20]{1,0:T(8,128)} %actions.1, s32[8,20]{1,0:T(8,128)} %valid.1, s32[8,20]{1,0:T(8,128)} %rewards.1, s32[8,20]{1,0:T(8,128)} %ends.1, ...), custom_call_target="tpu_custom_call" | custom-call | flops 1000000 | bytes 1000000 | tf_op jit(solution)/shard_map/prepare/pallas_call | solution.py:960
  12.0 1.6 collective-permute-done.1
  13.6 1.4 collective-permute-done.2
  15.0 0.9 pad_maximum_fusion.4.refs_5_
  15.9 1.6 collective-permute-start.4
  17.4 1.5 collective-permute-start.12
  18.9 3.4 %collective-permute-done.4.refs_6_ = bf16[4,16,2048]{2,1,0:T(8,128)(2,1)S(1)} collective-permute-done((bf16[4,16,2048]{2,1,0:T(8,128)(2,1)S(1)}, bf16[4,16,2048]{2,1,0:T(8,128)(2,1)S(1)}, u32[]{:S(2)}, u32[]{:S(2)}) %collective-permute-start.4) | collective-permute-done | bytes 262176 | tf_op jit(solution)/shard_map/ppermute | solution.py:748
  22.3 0.7 collective-permute-start.5
  23.0 3.1 %collective-permute-start.6 = (bf16[16,1792]{1,0:T(8,128)(2,1)}, bf16[16,1792]{1,0:T(8,128)(2,1)S(1)}, u32[]{:S(2)}, u32[]{:S(2)}) collective-permute-start(bf16[16,1792]{1,0:T(8,128)(2,1)} %get-tuple-element.127), channel_id=1, source_target_pairs={{0,16},{2,18},{4,20},{6,22},{8,24},{10,26},{12,28},{14,30},{16,0},... | collective-permute-start | bytes 172040 | tf_op jit(solution)/shard_map/ppermute | solution.py:748
  26.7 2.4 %collective-permute-start.8 = (bf16[4,16,2048]{2,1,0:T(8,128)(2,1)S(1)}, bf16[4,16,2048]{2,1,0:T(8,128)(2,1)S(1)}, u32[]{:S(2)}, u32[]{:S(2)}) collective-permute-start(bf16[4,16,2048]{2,1,0:T(8,128)(2,1)S(1)} %pad_maximum_fusion.4.refs_5_), channel_id=1, source_target_pairs={{0,6},{2,4},{4,2},{6,0},{8,14},{10,12},{12,10},{14,8},{16,22},{18,... | collective-permute-start | bytes 786440 | tf_op jit(solution)/shard_map/ppermute | solution.py:748
  29.8 2.5 %collective-permute-done.7 = bf16[16,1792]{1,0:T(8,128)(2,1)S(1)} collective-permute-done((bf16[16,1792]{1,0:T(8,128)(2,1)}, bf16[16,1792]{1,0:T(8,128)(2,1)S(1)}, u32[]{:S(2)}, u32[]{:S(2)}) %collective-permute-start.7) | collective-permute-done | bytes 57376 | tf_op jit(solution)/shard_map/ppermute | solution.py:748
  32.3 0.9 pad_maximum_fusion.5.refs_8_
  33.2 0.8 collective-permute-done.8.refs_8_
  34.0 1.5 collective-permute-start.10
  35.5 1.4 collective-permute-start.11
  37.5 0.7 copy-done
  38.2 0.7 copy-done.2
  38.9 0.7 copy-done.4
  39.6 1.1 copy-done.7
  40.7 16.8 %first_forward.1 = (bf16[256,1024]{1,0:T(8,128)(2,1)S(1)}, bf16[256,2048]{1,0:T(8,128)(2,1)S(1)}, bf16[256,128]{1,0:T(8,128)(2,1)S(1)}, f32[4,352,256]{2,1,0:T(8...) custom-call(s32[3]{0:T(128)S(1)} %copy-done.2, ...), custom_call_target="tpu_custom_call" | custom-call | flops 4000000000 | bytes 20000000 | tf_op jit(solution)/shard_map/first_forward/pallas_call | solution.py:994
  57.5 1.0 copy-done.13
  58.4 0.9 copy-done.15
  61.8 35.9 %middle.1 = (f32[4,352,256]{2,1,0:T(8,128)S(1)}, bf16[4,4,16,1792]{3,2,1,0:T(8,128)(2,1)S(1)}, bf16[4,4,16,1792]{3,2,1,0:T(8,128)(2,1)S(1)}, f32[32,8,256]{2,1,0:T(8,128)S(1)}, f32[8,128]{1,0:T(8,128)S(1)}) custom-call(s32[3]{0:T(128)S(1)} %copy-done.3, s32[4,352,128]{2,1,0:T(8,128)S(1)} %copy-done.8, s32[4,32,128]{2,1,0:T(8,128)S(1)} %copy-done.9, ...), custom_call_target="tpu_custom_call" | custom-call | flops 15000000512 | bytes 20000000 | tf_op jit(solution)/shard_map/middle/pallas_call | solution.py:1025
  98.3 6.6 %ff_backward.1 = (f32[4,352,256]{2,1,0:T(8,128)S(1)}, bf16[4,4,16,1024]{3,2,1,0:T(8,128)(2,1)S(1)}, bf16[4,4,16,1024]{3,2,1,0:T(8,128)(2,1)S(1)}, f32[32,8,256]{2,1,0:T(8,128)S(1)}) custom-call(s32[3]{0:T(128)S(1)} %copy-done.3, f32[14,256]{1,0:T(8,128)S(1)} %copy-done.1, bf16[256,2048]{1,0:T(8,128)(2,1)S(1)} %get-tuple-element.140.refs_2_, ...), custom_call_target="tpu_custom_call" | custom-call | flops 4000000000 | bytes 10000000 | tf_op jit(solution)/shard_map/ff_backward/pallas_call | solution.py:1064
  105.3 1.6 collective-permute-done.22
  107.5 2.5 %collective-permute-start.25 = (bf16[4,16,2816]{2,1,0:T(8,128)(2,1)S(1)}, bf16[4,16,2816]{2,1,0:T(8,128)(2,1)S(1)}, u32[]{:S(2)}, u32[]{:S(2)}) collective-permute-start(bf16[4,16,2816]{2,1,0:T(8,128)(2,1)S(1)} %pad_maximum_fusion.3), channel_id=1, source_target_pairs={{0,6},{2,4},{4,2},{6,0},{8,14},{10,12},{12,10},{14,8},{16,22},{18,... | collective-permute-start | bytes 1081352 | tf_op jit(solution)/shard_map/ppermute | solution.py:748
  111.3 14.2 %attention_backward.1 = (bf16[4,4,16,1024]{3,2,1,0:T(8,128)(2,1)S(1)}, bf16[4,4,16,1024]{3,2,1,0:T(8,128)(2,1)S(1)}, f32[32,256]{1,0:T(8,128)}) custom-call(s32[3]{0:T(128)S(1)} %copy-done.3, f32[14,256]{1,0:T(8,128)S(1)} %copy-done.1, bf16[256,1024]{1,0:T(8,128)(2,1)S(1)} %get-tuple-element.149.refs_2_, f32[4,352,256]{2,1,0:T(8,128)S(1)} %get-tuple-element.150.refs_3_, ...), custom_call_target="tpu_custom_call" | custom-call | flops 6000000000 | bytes 20000000 | tf_op jit(solution)/shard_map/attention_backward/pallas_call | solution.py:1088
  125.4 1.3 collective-permute-done.24
  127.2 3.7 %collective-permute-start.34 = (bf16[16,2816]{1,0:T(8,128)(2,1)S(1)}, bf16[16,2816]{1,0:T(8,128)(2,1)S(1)}, u32[]{:S(2)}, u32[]{:S(2)}) collective-permute-start(bf16[16,2816]{1,0:T(8,128)(2,1)S(1)} %get-tuple-element.220), channel_id=1, source_target_pairs={{0,16},{2,18},{4,20},{6,22},{8,24},{10,26},{12,28},{14,30},{16,0},... | collective-permute-start | bytes 270344 | tf_op jit(solution)/shard_map/ppermute | solution.py:748
  131.0 1.6 collective-permute-start.27
  132.6 0.8 collective-permute-start.28
  133.4 1.2 collective-permute-start.29
  134.6 2.1 %collective-permute-done.27 = bf16[4,16,1024]{2,1,0:T(8,128)(2,1)S(1)} collective-permute-done((bf16[4,16,1024]{2,1,0:T(8,128)(2,1)S(1)}, bf16[4,16,1024]{2,1,0:T(8,128)(2,1)S(1)}, u32[]{:S(2)}, u32[]{:S(2)}) %collective-permute-start.27) | collective-permute-done | bytes 131104 | tf_op jit(solution)/shard_map/ppermute | solution.py:748
  137.4 2.7 %collective-permute-done.28 = bf16[4,16,1024]{2,1,0:T(8,128)(2,1)S(1)} collective-permute-done((bf16[4,16,1024]{2,1,0:T(8,128)(2,1)S(1)}, bf16[4,16,1024]{2,1,0:T(8,128)(2,1)S(1)}, u32[]{:S(2)}, u32[]{:S(2)}) %collective-permute-start.28) | collective-permute-done | bytes 131104 | tf_op jit(solution)/shard_map/ppermute | solution.py:748
  140.5 1.3 collective-permute-start.31
  141.8 2.9 %collective-permute-start.32 = (bf16[16,1024]{1,0:T(8,128)(2,1)S(1)}, bf16[16,1024]{1,0:T(8,128)(2,1)S(1)}, u32[]{:S(2)}, u32[]{:S(2)}) collective-permute-start(bf16[16,1024]{1,0:T(8,128)(2,1)S(1)} %get-tuple-element.222), channel_id=1, source_target_pairs={{0,24},{2,26},{4,28},{6,30},{8,16},{10,18},{12,20},{14,22},{16,8},... | collective-permute-start | bytes 98312 | tf_op jit(solution)/shard_map/ppermute | solution.py:748
  145.3 2.2 %collective-permute-done.32.refs_4_ = bf16[16,1024]{1,0:T(8,128)(2,1)S(1)} collective-permute-done((bf16[16,1024]{1,0:T(8,128)(2,1)S(1)}, bf16[16,1024]{1,0:T(8,128)(2,1)S(1)}, u32[]{:S(2)}, u32[]{:S(2)}) %collective-permute-start.32) | collective-permute-done | bytes 32800 | tf_op jit(solution)/shard_map/ppermute | solution.py:748
  147.5 1.5 finish.1
  149.0 1.4 collective-permute-done.37
  150.3 0.8 add_select_fusion
  151.1 0.7 broadcast_in_dim.13
  151.8 5.0 %all-to-all-start = ((f32[16,24,128]{2,1,0:T(8,128)}), f32[16,24,128]{2,1,0:T(8,128)S(1)}, u32[]{:S(2)}, u32[]{:S(2)}) async-start(f32[16,24,128]{2,1,0:T(8,128)} %broadcast_in_dim.13), calls=%async_computation | async-start | bytes 393216 | tf_op jit(solution)/shard_map/all_to_all | solution.py:1131
  156.9 1.4 collective-permute-done.36.swapped
  158.3 7.5 %all-to-all-done.gathered = f32[16,24,128]{2,1,0:T(8,128)S(1)} async-done(((f32[16,24,128]{2,1,0:T(8,128)}), f32[16,24,128]{2,1,0:T(8,128)S(1)}, u32[]{:S(2)}, u32[]{:S(2)}) %all-to-all-start) | async-done | bytes 196640 | tf_op jit(solution)/shard_map/all_to_all | solution.py:1131
  165.8 2.5 %adam.1 = (f32[1,1]{1,0:T(1,128)}, f32[1,1]{1,0:T(1,128)}, f32[1,1]{1,0:T(1,128)}, f32[16,896]{1,0:T(8,128)}, f32[16,896]{1,0:T(8,128)}, /*index=5*/f32[16,896]{...) custom-call(s32[3]{0:T(128)} %pad_add_fusion.place_ref.refs_0_, ...), custom_call_target="tpu_custom_call" | custom-call | flops 1000000 | bytes 1000000 | tf_op jit(solution)/shard_map/adam/pallas_call | solution.py:1139
  (91 shorter events, 9.8 us)
Async XLA Ops:
  3.1 8.9 %collective-permute-start = (bf16[16,2048]{1,0:T(8,128)(2,1)}, bf16[16,2048]{1,0:T(8,128)(2,1)S(1)}, u32[]{:S(2)}, u32[]{:S(2)}) collective-permute-start(bf16[16,2048]{1,0:T(8,128)(2,1)} %get-tuple-element.122.after), channel_id=1, source_target_pairs={{0,8},{2,10},{4,12},{6,14},{8,0},{10,2},{12,4},{14,6},{16,24},{18,... | collective-permute-start | bytes 196616 | tf_op jit(solution)/shard_map/ppermute | solution.py:748
  6.1 7.5 %collective-permute-start.1 = (bf16[16,2048]{1,0:T(8,128)(2,1)}, bf16[16,2048]{1,0:T(8,128)(2,1)S(1)}, u32[]{:S(2)}, u32[]{:S(2)}) collective-permute-start(bf16[16,2048]{1,0:T(8,128)(2,1)} %get-tuple-element.122.after), channel_id=1, source_target_pairs={{0,16},{2,18},{4,20},{6,22},{8,24},{10,26},{12,28},{14,30},{16,0},... | collective-permute-start | bytes 196616 | tf_op jit(solution)/shard_map/ppermute | solution.py:748
  8.7 6.3 %collective-permute-start.2 = (bf16[16,2048]{1,0:T(8,128)(2,1)}, bf16[16,2048]{1,0:T(8,128)(2,1)S(1)}, u32[]{:S(2)}, u32[]{:S(2)}) collective-permute-start(bf16[16,2048]{1,0:T(8,128)(2,1)} %get-tuple-element.122.after), channel_id=1, source_target_pairs={{0,24},{2,26},{4,28},{6,30},{8,16},{10,18},{12,20},{14,22},{16,8},... | collective-permute-start | bytes 196616 | tf_op jit(solution)/shard_map/ppermute | solution.py:748
  8.7 3.3 %collective-permute-start.3 = (f32[2,512]{1,0:T(2,128)}, f32[2,512]{1,0:T(2,128)S(1)}, u32[]{:S(2)}, u32[]{:S(2)}) collective-permute-start(f32[2,512]{1,0:T(2,128)} %refs_12_.1), channel_id=1, source_target_pairs={{0,1},{1,0},{2,3},{3,2},{4,5},{5,4},{6,7},{7,6},{8,9},{9,8},{10,11... | collective-permute-start | bytes 12296 | tf_op jit(solution)/shard_map/ppermute | solution.py:748
  15.9 6.5 %collective-permute-start.4 = (bf16[4,16,2048]{2,1,0:T(8,128)(2,1)S(1)}, bf16[4,16,2048]{2,1,0:T(8,128)(2,1)S(1)}, u32[]{:S(2)}, u32[]{:S(2)}) collective-permute-start(bf16[4,16,2048]{2,1,0:T(8,128)(2,1)S(1)} %pad_maximum_fusion.4.refs_5_), channel_id=1, source_target_pairs={{0,2},{2,0},{4,6},{6,4},{8,10},{10,8},{12,14},{14,12},{16,18},{18,... | collective-permute-start | bytes 786440 | tf_op jit(solution)/shard_map/ppermute | solution.py:748
  17.4 11.8 %collective-permute-start.12 = (bf16[4,16,2048]{2,1,0:T(8,128)(2,1)S(1)}, bf16[4,16,2048]{2,1,0:T(8,128)(2,1)S(1)}, u32[]{:S(2)}, u32[]{:S(2)}) collective-permute-start(bf16[4,16,2048]{2,1,0:T(8,128)(2,1)S(1)} %pad_maximum_fusion.4.refs_5_), channel_id=1, source_target_pairs={{0,4},{2,6},{4,0},{6,2},{8,12},{10,14},{12,8},{14,10},{16,20},{18,... | collective-permute-start | bytes 786440 | tf_op jit(solution)/shard_map/ppermute | solution.py:748
  22.3 6.8 %collective-permute-start.5 = (bf16[16,1792]{1,0:T(8,128)(2,1)}, bf16[16,1792]{1,0:T(8,128)(2,1)S(1)}, u32[]{:S(2)}, u32[]{:S(2)}) collective-permute-start(bf16[16,1792]{1,0:T(8,128)(2,1)} %get-tuple-element.127), channel_id=1, source_target_pairs={{0,8},{2,10},{4,12},{6,14},{8,0},{10,2},{12,4},{14,6},{16,24},{18,... | collective-permute-start | bytes 172040 | tf_op jit(solution)/shard_map/ppermute | solution.py:748
  23.0 6.7 %collective-permute-start.6 = (bf16[16,1792]{1,0:T(8,128)(2,1)}, bf16[16,1792]{1,0:T(8,128)(2,1)S(1)}, u32[]{:S(2)}, u32[]{:S(2)}) collective-permute-start(bf16[16,1792]{1,0:T(8,128)(2,1)} %get-tuple-element.127), channel_id=1, source_target_pairs={{0,16},{2,18},{4,20},{6,22},{8,24},{10,26},{12,28},{14,30},{16,0},... | collective-permute-start | bytes 172040 | tf_op jit(solution)/shard_map/ppermute | solution.py:748
  26.1 6.2 %collective-permute-start.7 = (bf16[16,1792]{1,0:T(8,128)(2,1)}, bf16[16,1792]{1,0:T(8,128)(2,1)S(1)}, u32[]{:S(2)}, u32[]{:S(2)}) collective-permute-start(bf16[16,1792]{1,0:T(8,128)(2,1)} %get-tuple-element.127), channel_id=1, source_target_pairs={{0,24},{2,26},{4,28},{6,30},{8,16},{10,18},{12,20},{14,22},{16,8},... | collective-permute-start | bytes 172040 | tf_op jit(solution)/shard_map/ppermute | solution.py:748
  26.7 7.3 %collective-permute-start.8 = (bf16[4,16,2048]{2,1,0:T(8,128)(2,1)S(1)}, bf16[4,16,2048]{2,1,0:T(8,128)(2,1)S(1)}, u32[]{:S(2)}, u32[]{:S(2)}) collective-permute-start(bf16[4,16,2048]{2,1,0:T(8,128)(2,1)S(1)} %pad_maximum_fusion.4.refs_5_), channel_id=1, source_target_pairs={{0,6},{2,4},{4,2},{6,0},{8,14},{10,12},{12,10},{14,8},{16,22},{18,... | collective-permute-start | bytes 786440 | tf_op jit(solution)/shard_map/ppermute | solution.py:748
  29.2 6.3 %collective-permute-start.13 = (bf16[4,16,2048]{2,1,0:T(8,128)(2,1)S(1)}, bf16[4,16,2048]{2,1,0:T(8,128)(2,1)S(1)}, u32[]{:S(2)}, u32[]{:S(2)}) collective-permute-start(bf16[4,16,2048]{2,1,0:T(8,128)(2,1)S(1)} %pad_maximum_fusion.4.refs_5_), channel_id=1, source_target_pairs={{0,1},{1,0},{2,3},{3,2},{4,5},{5,4},{6,7},{7,6},{8,9},{9,8},{10,11... | collective-permute-start | bytes 786440 | tf_op jit(solution)/shard_map/ppermute | solution.py:748
  29.2 7.8 %collective-permute-start.14 = (bf16[4,16,2048]{2,1,0:T(8,128)(2,1)S(1)}, bf16[4,16,2048]{2,1,0:T(8,128)(2,1)S(1)}, u32[]{:S(2)}, u32[]{:S(2)}) collective-permute-start(bf16[4,16,2048]{2,1,0:T(8,128)(2,1)S(1)} %collective-permute-done.4.refs_6_), channel_id=1, source_target_pairs={{0,1},{1,0},{2,3},{3,2},{4,5},{5,4},{6,7},{7,6},{8,9},{9,8},{10,11... | collective-permute-start | bytes 786440 | tf_op jit(solution)/shard_map/ppermute | solution.py:748
  29.7 7.8 %collective-permute-start.15 = (bf16[4,16,2048]{2,1,0:T(8,128)(2,1)S(1)}, bf16[4,16,2048]{2,1,0:T(8,128)(2,1)S(1)}, u32[]{:S(2)}, u32[]{:S(2)}) collective-permute-start(bf16[4,16,2048]{2,1,0:T(8,128)(2,1)S(1)} %collective-permute-done.12.refs_7_), channel_id=1, source_target_pairs={{0,1},{1,0},{2,3},{3,2},{4,5},{5,4},{6,7},{7,6},{8,9},{9,8},{10,11... | collective-permute-start | bytes 786440 | tf_op jit(solution)/shard_map/ppermute | solution.py:748
  32.3 29.4 %copy-start.1 = (f32[14,256]{1,0:T(8,128)S(1)}, f32[14,256]{1,0:T(8,128)}, u32[]{:S(2)}) copy-start(f32[14,256]{1,0:T(8,128)} %refs_18_.1) | copy-start | bytes 43012
  32.3 29.4 %copy-start.3 = (s32[3]{0:T(128)S(1)}, s32[3]{0:T(128)}, u32[]{:S(2)}) copy-start(s32[3]{0:T(128)} %pad_add_fusion.place_ref.refs_0_) | copy-start | bytes 40
  32.3 29.4 %copy-start.5 = (f32[2,512]{1,0:T(2,128)S(1)}, f32[2,512]{1,0:T(2,128)}, u32[]{:S(2)}) copy-start(f32[2,512]{1,0:T(2,128)} %refs_12_.1) | copy-start | bytes 12292
  32.3 29.4 %copy-start.9 = (s32[4,32,128]{2,1,0:T(8,128)S(1)}, s32[4,32,128]{2,1,0:T(8,128)}, u32[]{:S(2)}) copy-start(s32[4,32,128]{2,1,0:T(8,128)} %get-tuple-element.120.refs_2_) | copy-start | bytes 196612
  34.0 3.5 %collective-permute-start.16 = (bf16[4,16,2048]{2,1,0:T(8,128)(2,1)S(1)}, bf16[4,16,2048]{2,1,0:T(8,128)(2,1)S(1)}, u32[]{:S(2)}, u32[]{:S(2)}) collective-permute-start(bf16[4,16,2048]{2,1,0:T(8,128)(2,1)S(1)} %collective-permute-done.8.refs_8_), channel_id=1, source_target_pairs={{0,1},{1,0},{2,3},{3,2},{4,5},{5,4},{6,7},{7,6},{8,9},{9,8},{10,11... | collective-permute-start | bytes 786440 | tf_op jit(solution)/shard_map/ppermute | solution.py:748
  34.0 25.3 %collective-permute-start.10 = (bf16[4,16,1792]{2,1,0:T(8,128)(2,1)S(1)}, bf16[4,16,1792]{2,1,0:T(8,128)(2,1)S(1)}, u32[]{:S(2)}, u32[]{:S(2)}) collective-permute-start(bf16[4,16,1792]{2,1,0:T(8,128)(2,1)S(1)} %pad_maximum_fusion.5.refs_8_), channel_id=1, source_target_pairs={{0,4},{2,6},{4,0},{6,2},{8,12},{10,14},{12,8},{14,10},{16,20},{18,... | collective-permute-start | bytes 688136 | tf_op jit(solution)/shard_map/ppermute | solution.py:748
  35.5 23.8 %collective-permute-start.11 = (bf16[4,16,1792]{2,1,0:T(8,128)(2,1)S(1)}, bf16[4,16,1792]{2,1,0:T(8,128)(2,1)S(1)}, u32[]{:S(2)}, u32[]{:S(2)}) collective-permute-start(bf16[4,16,1792]{2,1,0:T(8,128)(2,1)S(1)} %pad_maximum_fusion.5.refs_8_), channel_id=1, source_target_pairs={{0,6},{2,4},{4,2},{6,0},{8,14},{10,12},{12,10},{14,8},{16,22},{18,... | collective-permute-start | bytes 688136 | tf_op jit(solution)/shard_map/ppermute | solution.py:748
  37.0 22.4 %collective-permute-start.9 = (bf16[4,16,1792]{2,1,0:T(8,128)(2,1)S(1)}, bf16[4,16,1792]{2,1,0:T(8,128)(2,1)S(1)}, u32[]{:S(2)}, u32[]{:S(2)}) collective-permute-start(bf16[4,16,1792]{2,1,0:T(8,128)(2,1)S(1)} %pad_maximum_fusion.5.refs_8_), channel_id=1, source_target_pairs={{0,2},{2,0},{4,6},{6,4},{8,10},{10,8},{12,14},{14,12},{16,18},{18,... | collective-permute-start | bytes 688136 | tf_op jit(solution)/shard_map/ppermute | solution.py:748
  37.5 22.9 %collective-permute-start.17 = (bf16[4,16,1792]{2,1,0:T(8,128)(2,1)S(1)}, bf16[4,16,1792]{2,1,0:T(8,128)(2,1)S(1)}, u32[]{:S(2)}, u32[]{:S(2)}) collective-permute-start(bf16[4,16,1792]{2,1,0:T(8,128)(2,1)S(1)} %pad_maximum_fusion.5.refs_8_), channel_id=1, source_target_pairs={{0,1},{1,0},{2,3},{3,2},{4,5},{5,4},{6,7},{7,6},{8,9},{9,8},{10,11... | collective-permute-start | bytes 688136 | tf_op jit(solution)/shard_map/ppermute | solution.py:748
  40.7 21.0 %copy-start.8 = (s32[4,352,128]{2,1,0:T(8,128)S(1)}, s32[4,352,128]{2,1,0:T(8,128)}, u32[]{:S(2)}) copy-start(s32[4,352,128]{2,1,0:T(8,128)} %get-tuple-element.119.refs_1_) | copy-start | bytes 2162692
  59.3 1.7 collective-permute-start.18
  59.9 1.5 collective-permute-start.19
  60.0 1.7 %collective-permute-start.20 = (bf16[4,16,1792]{2,1,0:T(8,128)(2,1)S(1)}, bf16[4,16,1792]{2,1,0:T(8,128)(2,1)S(1)}, u32[]{:S(2)}, u32[]{:S(2)}) collective-permute-start(bf16[4,16,1792]{2,1,0:T(8,128)(2,1)S(1)} %collective-permute-done.11.refs_11_), channel_id=1, source_target_pairs={{0,1},{1,0},{2,3},{3,2},{4,5},{5,4},{6,7},{7,6},{8,9},{9,8},{10,11... | collective-permute-start | bytes 688136 | tf_op jit(solution)/shard_map/ppermute | solution.py:748
  61.7 36.6 %copy-start.10 = (bf16[4,352,1024]{2,1,0:T(8,128)(2,1)S(1)}, bf16[4,352,1024]{2,1,0:T(8,128)(2,1)}, u32[]{:S(2)}) copy-start(bf16[4,352,1024]{2,1,0:T(8,128)(2,1)} %get-tuple-element.144.refs_6_) | copy-start | bytes 8650756
  61.8 36.6 %copy-start.11 = (bf16[4,352,1024]{2,1,0:T(8,128)(2,1)S(1)}, bf16[4,352,1024]{2,1,0:T(8,128)(2,1)}, u32[]{:S(2)}) copy-start(bf16[4,352,1024]{2,1,0:T(8,128)(2,1)} %get-tuple-element.145.refs_7_) | copy-start | bytes 8650756
  97.7 9.4 %collective-permute-start.21 = (bf16[4,4,16,1792]{3,2,1,0:T(8,128)(2,1)S(1)}, bf16[4,4,16,1792]{3,2,1,0:T(8,128)(2,1)S(1)}, u32[]{:S(2)}, u32[]{:S(2)}) collective-permute-start(bf16[4,4,16,1792]{3,2,1,0:T(8,128)(2,1)S(1)} %get-tuple-element.139), channel_id=1, source_target_pairs={{0,1},{1,0},{2,3},{3,2},{4,5},{5,4},{6,7},{7,6},{8,9},{9,8},{10,11... | collective-permute-start | bytes 2752520 | tf_op jit(solution)/shard_map/ppermute | solution.py:748
  105.0 2.0 %collective-permute-start.22 = (bf16[4,4,16,1024]{3,2,1,0:T(8,128)(2,1)S(1)}, bf16[4,4,16,1024]{3,2,1,0:T(8,128)(2,1)S(1)}, u32[]{:S(2)}, u32[]{:S(2)}) collective-permute-start(bf16[4,4,16,1024]{3,2,1,0:T(8,128)(2,1)S(1)} %get-tuple-element.148), channel_id=1, source_target_pairs={{0,1},{1,0},{2,3},{3,2},{4,5},{5,4},{6,7},{7,6},{8,9},{9,8},{10,11... | collective-permute-start | bytes 1572872 | tf_op jit(solution)/shard_map/ppermute | solution.py:748
  107.1 4.1 %copy-start.16 = (bf16[4,384,256]{2,1,0:T(8,128)(2,1)S(1)}, bf16[4,384,256]{2,1,0:T(8,128)(2,1)}, u32[]{:S(2)}) copy-start(bf16[4,384,256]{2,1,0:T(8,128)(2,1)} %copy-done.15) | copy-start | bytes 2359300
  107.4 3.9 %copy-start.14 = (bf16[4,256,512]{2,1,0:T(8,128)(2,1)S(1)}, bf16[4,256,512]{2,1,0:T(8,128)(2,1)}, u32[]{:S(2)}) copy-start(bf16[4,256,512]{2,1,0:T(8,128)(2,1)} %copy-done.13) | copy-start | bytes 3145732
  107.5 18.0 %collective-permute-start.25 = (bf16[4,16,2816]{2,1,0:T(8,128)(2,1)S(1)}, bf16[4,16,2816]{2,1,0:T(8,128)(2,1)S(1)}, u32[]{:S(2)}, u32[]{:S(2)}) collective-permute-start(bf16[4,16,2816]{2,1,0:T(8,128)(2,1)S(1)} %pad_maximum_fusion.3), channel_id=1, source_target_pairs={{0,6},{2,4},{4,2},{6,0},{8,14},{10,12},{12,10},{14,8},{16,22},{18,... | collective-permute-start | bytes 1081352 | tf_op jit(solution)/shard_map/ppermute | solution.py:748
  110.0 16.8 %collective-permute-start.24 = (bf16[4,16,2816]{2,1,0:T(8,128)(2,1)S(1)}, bf16[4,16,2816]{2,1,0:T(8,128)(2,1)S(1)}, u32[]{:S(2)}, u32[]{:S(2)}) collective-permute-start(bf16[4,16,2816]{2,1,0:T(8,128)(2,1)S(1)} %pad_maximum_fusion.2), channel_id=1, source_target_pairs={{0,4},{2,6},{4,0},{6,2},{8,12},{10,14},{12,8},{14,10},{16,20},{18,... | collective-permute-start | bytes 1081352 | tf_op jit(solution)/shard_map/ppermute | solution.py:748
  110.6 16.3 %collective-permute-start.23 = (bf16[4,16,2816]{2,1,0:T(8,128)(2,1)S(1)}, bf16[4,16,2816]{2,1,0:T(8,128)(2,1)S(1)}, u32[]{:S(2)}, u32[]{:S(2)}) collective-permute-start(bf16[4,16,2816]{2,1,0:T(8,128)(2,1)S(1)} %pad_maximum_fusion.1), channel_id=1, source_target_pairs={{0,2},{2,0},{4,6},{6,4},{8,10},{10,8},{12,14},{14,12},{16,18},{18,... | collective-permute-start | bytes 1081352 | tf_op jit(solution)/shard_map/ppermute | solution.py:748
  125.4 5.5 %collective-permute-start.26 = (bf16[4,4,16,1024]{3,2,1,0:T(8,128)(2,1)S(1)}, bf16[4,4,16,1024]{3,2,1,0:T(8,128)(2,1)S(1)}, u32[]{:S(2)}, u32[]{:S(2)}) collective-permute-start(bf16[4,4,16,1024]{3,2,1,0:T(8,128)(2,1)S(1)} %get-tuple-element.165), channel_id=1, source_target_pairs={{0,1},{1,0},{2,3},{3,2},{4,5},{5,4},{6,7},{7,6},{8,9},{9,8},{10,11... | collective-permute-start | bytes 1572872 | tf_op jit(solution)/shard_map/ppermute | solution.py:748
  127.1 14.7 %collective-permute-start.33 = (bf16[16,2816]{1,0:T(8,128)(2,1)S(1)}, bf16[16,2816]{1,0:T(8,128)(2,1)S(1)}, u32[]{:S(2)}, u32[]{:S(2)}) collective-permute-start(bf16[16,2816]{1,0:T(8,128)(2,1)S(1)} %get-tuple-element.221), channel_id=1, source_target_pairs={{0,8},{2,10},{4,12},{6,14},{8,0},{10,2},{12,4},{14,6},{16,24},{18,... | collective-permute-start | bytes 270344 | tf_op jit(solution)/shard_map/ppermute | solution.py:748
  127.2 17.5 %collective-permute-start.34 = (bf16[16,2816]{1,0:T(8,128)(2,1)S(1)}, bf16[16,2816]{1,0:T(8,128)(2,1)S(1)}, u32[]{:S(2)}, u32[]{:S(2)}) collective-permute-start(bf16[16,2816]{1,0:T(8,128)(2,1)S(1)} %get-tuple-element.220), channel_id=1, source_target_pairs={{0,16},{2,18},{4,20},{6,22},{8,24},{10,26},{12,28},{14,30},{16,0},... | collective-permute-start | bytes 270344 | tf_op jit(solution)/shard_map/ppermute | solution.py:748
  131.0 5.7 %collective-permute-start.27 = (bf16[4,16,1024]{2,1,0:T(8,128)(2,1)S(1)}, bf16[4,16,1024]{2,1,0:T(8,128)(2,1)S(1)}, u32[]{:S(2)}, u32[]{:S(2)}) collective-permute-start(bf16[4,16,1024]{2,1,0:T(8,128)(2,1)S(1)} %get-tuple-element.212), channel_id=1, source_target_pairs={{0,2},{2,0},{4,6},{6,4},{8,10},{10,8},{12,14},{14,12},{16,18},{18,... | collective-permute-start | bytes 393224 | tf_op jit(solution)/shard_map/ppermute | solution.py:748
  132.6 7.5 %collective-permute-start.28 = (bf16[4,16,1024]{2,1,0:T(8,128)(2,1)S(1)}, bf16[4,16,1024]{2,1,0:T(8,128)(2,1)S(1)}, u32[]{:S(2)}, u32[]{:S(2)}) collective-permute-start(bf16[4,16,1024]{2,1,0:T(8,128)(2,1)S(1)} %get-tuple-element.214), channel_id=1, source_target_pairs={{0,4},{2,6},{4,0},{6,2},{8,12},{10,14},{12,8},{14,10},{16,20},{18,... | collective-permute-start | bytes 393224 | tf_op jit(solution)/shard_map/ppermute | solution.py:748
  133.4 6.7 %collective-permute-start.29 = (bf16[4,16,1024]{2,1,0:T(8,128)(2,1)S(1)}, bf16[4,16,1024]{2,1,0:T(8,128)(2,1)S(1)}, u32[]{:S(2)}, u32[]{:S(2)}) collective-permute-start(bf16[4,16,1024]{2,1,0:T(8,128)(2,1)S(1)} %get-tuple-element.213), channel_id=1, source_target_pairs={{0,6},{2,4},{4,2},{6,0},{8,14},{10,12},{12,10},{14,8},{16,22},{18,... | collective-permute-start | bytes 393224 | tf_op jit(solution)/shard_map/ppermute | solution.py:748
  136.7 8.0 %collective-permute-start.35 = (bf16[16,2816]{1,0:T(8,128)(2,1)S(1)}, bf16[16,2816]{1,0:T(8,128)(2,1)S(1)}, u32[]{:S(2)}, u32[]{:S(2)}) collective-permute-start(bf16[16,2816]{1,0:T(8,128)(2,1)S(1)} %get-tuple-element.219), channel_id=1, source_target_pairs={{0,24},{2,26},{4,28},{6,30},{8,16},{10,18},{12,20},{14,22},{16,8},... | collective-permute-start | bytes 270344 | tf_op jit(solution)/shard_map/ppermute | solution.py:748
  140.2 4.5 %collective-permute-start.30 = (bf16[16,1024]{1,0:T(8,128)(2,1)S(1)}, bf16[16,1024]{1,0:T(8,128)(2,1)S(1)}, u32[]{:S(2)}, u32[]{:S(2)}) collective-permute-start(bf16[16,1024]{1,0:T(8,128)(2,1)S(1)} %get-tuple-element.224), channel_id=1, source_target_pairs={{0,8},{2,10},{4,12},{6,14},{8,0},{10,2},{12,4},{14,6},{16,24},{18,... | collective-permute-start | bytes 98312 | tf_op jit(solution)/shard_map/ppermute | solution.py:748
  140.5 4.8 %collective-permute-start.31 = (bf16[16,1024]{1,0:T(8,128)(2,1)S(1)}, bf16[16,1024]{1,0:T(8,128)(2,1)S(1)}, u32[]{:S(2)}, u32[]{:S(2)}) collective-permute-start(bf16[16,1024]{1,0:T(8,128)(2,1)S(1)} %get-tuple-element.223), channel_id=1, source_target_pairs={{0,16},{2,18},{4,20},{6,22},{8,24},{10,26},{12,28},{14,30},{16,0},... | collective-permute-start | bytes 98312 | tf_op jit(solution)/shard_map/ppermute | solution.py:748
  141.8 5.7 %collective-permute-start.32 = (bf16[16,1024]{1,0:T(8,128)(2,1)S(1)}, bf16[16,1024]{1,0:T(8,128)(2,1)S(1)}, u32[]{:S(2)}, u32[]{:S(2)}) collective-permute-start(bf16[16,1024]{1,0:T(8,128)(2,1)S(1)} %get-tuple-element.222), channel_id=1, source_target_pairs={{0,24},{2,26},{4,28},{6,30},{8,16},{10,18},{12,20},{14,22},{16,8},... | collective-permute-start | bytes 98312 | tf_op jit(solution)/shard_map/ppermute | solution.py:748
  148.9 1.4 collective-permute-start.37
  151.8 14.0 %all-to-all-start = ((f32[16,24,128]{2,1,0:T(8,128)}), f32[16,24,128]{2,1,0:T(8,128)S(1)}, u32[]{:S(2)}, u32[]{:S(2)}) async-start(f32[16,24,128]{2,1,0:T(8,128)} %broadcast_in_dim.13), calls=%async_computation | async-start | bytes 393216 | tf_op jit(solution)/shard_map/all_to_all | solution.py:1131
  156.8 1.5 collective-permute-start.36
  (8 other events, 9.5 us)

commit v6 on v5

--- a/solution.py
+++ b/solution.py
@@ -72,6 +72,11 @@
     return lax.dot_general(a, b, (((0,), (0,)), ((), ())), preferred_element_type=F32)
 
 
+def places(fast):
+    wide, core = lax.axis_index("wide"), lax.axis_index("narrow")
+    return (wide if fast else 0), core, wide
+
+
 def tiles(rows, size):
     return [slice(first, first + size) for first in range(0, rows, size)]
 
@@ -125,8 +130,8 @@
     return jnp.where(key <= query, 0.0, -1e30)
 
 
-def assemble(pieces_mine, pieces_other, place_ref, w_ref, halves):
-    me, core = place_ref[0], place_ref[1]
+def assemble(pieces_mine, pieces_other, place, w_ref, halves):
+    me, core, _ = place
     is_first = core == 0
     for p in range(4):
 
@@ -146,8 +151,8 @@
         lax.fori_loop(0, 4, block, 0)
 
 
-def disperse(g_ref, place_ref, keep_ref, send_ref, halves, scaled=True):
-    me, core = place_ref[0], place_ref[1]
+def disperse(g_ref, place, keep_ref, send_ref, halves, scaled=True):
+    me, core, _ = place
     is_first = core == 0
 
     def block(i, _):
@@ -301,19 +306,19 @@
         v_ref[v_row + i] += totals[i]
 
 
-def own_bias(place_ref, mine, other):
-    is_first = place_ref[1] == 0
+def own_bias(place, mine, other):
+    is_first = place[1] == 0
     return jnp.concatenate(
         [jnp.where(is_first, mine, other), jnp.where(is_first, other, mine)], axis=1
     )
 
 
 def prepare_kernel(
-    place_ref, games_ref, tokens, actions, valid, rewards, ends, after, out, out_side, x_ref
+    fast, games_ref, tokens, actions, valid, rewards, ends, out, out_side, x_ref
 ):
     count = out.shape[0]
     frames = tokens.shape[2]
-    base = place_ref[1] * count
+    base = places(fast)[1] * count
     row = lax.broadcasted_iota(jnp.int32, (SEQ, frames), 0)
     start = lax.broadcasted_iota(jnp.int32, (SEQ, frames), 1) * FRAME_TOKENS
     here = jnp.where((row >= start) & (row < start + FRAME_TOKENS), 1.0, 0.0).astype(BF16)
@@ -370,8 +375,9 @@
     wqt_ref[...] = jnp.transpose(w_ref[:, 0:256])
 
 
-def first_forward_kernel(*refs):
-    place_ref, meta_ref, vec_ref, bias_ref, bias_other = refs[0:5]
+def first_forward_kernel(fast, *refs):
+    refs = (places(fast),) + refs
+    place, meta_ref, vec_ref, bias_ref, bias_other = refs[0:5]
     mine, other = refs[5:9], refs[9:13]
     w_attention, w_ff, side_out, next_ref, hits_ref, x_ref = refs[13:19]
     kept = [ref.at[0] for ref in refs[19:32]]
@@ -380,7 +386,7 @@
 
     @pl.when(pl.program_id(0) == 0)
     def _():
-        assemble(mine, other, place_ref, w_ref, HALF_FIRST)
+        assemble(mine, other, place, w_ref, HALF_FIRST)
         w_attention[...] = w_ref[:, 0:COL_UP]
         w_ff[...] = w_ref[:, COL_UP:COL_TABLE]
         side_out[...] = w_ref[:, COL_SMALL:]
@@ -388,7 +394,7 @@
 
     make_hits(meta_ref.at[0], hits_ref.at[0])
     x_ref[0] = dot_nt(hits_ref[0], w_ref[:, COL_TABLE : COL_TABLE + ROWS])
-    bias = own_bias(place_ref, bias_ref[0:1], bias_other[0:1])
+    bias = own_bias(place, bias_ref[0:1], bias_other[0:1])
     vec = vec_ref[0:6]
     layer_forward(x_ref.at[0], w_ref, vec, bias, kept, work)
     for rows in tiles(SEQ, TILE):
@@ -430,8 +436,9 @@
     return jnp.where(hit, 1.0, 0.0).astype(BF16)
 
 
-def middle_kernel(*refs):
-    place_ref, meta_ref, frame_ref, vec_ref, bias_ref, bias_other, side_ref, in_ref = refs[0:8]
+def middle_kernel(fast, *refs):
+    refs = (places(fast),) + refs
+    place, meta_ref, frame_ref, vec_ref, bias_ref, bias_other, side_ref, in_ref = refs[0:8]
     mine, other = refs[8:12], refs[12:16]
     grad_ref, keep_ref, send_ref, v_out, scalar_ref = refs[16:21]
     refs = refs[1:]
@@ -440,16 +447,16 @@
     m_ref, h_ref, gp_ref, a_ref, c_ref = kept[8:13]
     forward_work = refs[36:42]
     u_ref, y_ref = forward_work[4:6]
-    backward_work = refs[42:49]
-    proj_ref = refs[49]
-    du_ref, ones_ref, up_ref, up16_ref, mid_ref, mid16_ref = refs[50:56]
-    last_ref, final_ref, logit_ref, dlogit_ref, pick_ref, put_ref = refs[56:62]
+    backward_work = refs[42:48]
+    proj_ref = refs[48]
+    du_ref, ones_ref, up_ref, up16_ref, mid_ref, mid16_ref = refs[49:55]
+    last_ref, final_ref, logit_ref, dlogit_ref, pick_ref, put_ref = refs[55:61]
     dost_ref = backward_work[0]
     step = pl.program_id(0)
 
     @pl.when(step == 0)
     def _():
-        assemble(mine, other, place_ref, w_ref, HALF_SECOND)
+        assemble(mine, other, place, w_ref, HALF_SECOND)
         w_ref[:, COL_SECOND:] = side_ref[...]
         g_ref[...] = jnp.zeros(g_ref.shape, F32)
         v_ref[...] = jnp.zeros(v_ref.shape, F32)
@@ -464,7 +471,7 @@
 
     x_ref = in_ref.at[0]
     vec = vec_ref[6:12]
-    bias = own_bias(place_ref, bias_ref[1:2], bias_other[1:2])
+    bias = own_bias(place, bias_ref[1:2], bias_other[1:2])
     layer_forward(x_ref, w_ref, vec, bias, kept, forward_work)
 
     gain, offset = vec_ref[12:13], vec_ref[13:14]
@@ -534,21 +541,22 @@
         g_ref,
         v_ref,
         6,
-        (dost_ref, forward_work[0]) + tuple(backward_work[2:]) + (proj_ref, y_ref),
+        (dost_ref, forward_work[0]) + tuple(backward_work[1:]) + (proj_ref, y_ref),
         grad_ref.at[0],
     )
 
     @pl.when(step == pl.num_programs(0) - 1)
     def _():
-        disperse(g_ref, place_ref, keep_ref, send_ref, HALF_SECOND)
+        disperse(g_ref, place, keep_ref, send_ref, HALF_SECOND)
         side = jnp.transpose(g_ref[:, COL_SECOND:])
         for i in range(5):
             v_ref[SMALL_SIDE + i, 0:1] = side[i : i + 1]
         v_out[...] = v_ref[...]
 
 
-def ff_backward_kernel(*refs):
-    place_ref, vec_ref, w_ref, grad_ref, v_in = refs[0:5]
+def ff_backward_kernel(fast, *refs):
+    refs = (places(fast),) + refs
+    place, vec_ref, w_ref, grad_ref, v_in = refs[0:5]
     kept = [ref.at[0] for ref in refs[5:9]]
     mid_ref, keep_ref, send_ref, v_out = refs[9:13]
     g_ref, v_ref, grad16_ref = refs[13:16]
@@ -589,12 +597,13 @@
 
     @pl.when(step == pl.num_programs(0) - 1)
     def _():
-        disperse(g_ref, place_ref, keep_ref, send_ref, HALF_GRAD_FF, False)
+        disperse(g_ref, place, keep_ref, send_ref, HALF_GRAD_FF, False)
         v_out[...] = v_ref[...]
 
 
-def attention_backward_kernel(*refs):
-    place_ref, vec_ref, w_ref, mid_ref, hits_ref, v_in = refs[0:6]
+def attention_backward_kernel(fast, *refs):
+    refs = (places(fast),) + refs
+    place, vec_ref, w_ref, mid_ref, hits_ref, v_in = refs[0:6]
     kept = [ref.at[0] for ref in refs[6:16]]
     keep_ref, send_ref, v_out = refs[17:20]
     g_ref, v_ref, mid16_ref, out16_ref = refs[20:24]
@@ -627,7 +636,7 @@
             quarter = small[8 * (block // 4) : 8 * (block // 4) + 8]
             g_ref[16 * block : 16 * block + 8, GRAD_SMALL:] = quarter[:, 0:128]
             g_ref[16 * block + 8 : 16 * block + 16, GRAD_SMALL:] = quarter[:, 128:256]
-        disperse(g_ref, place_ref, keep_ref, send_ref, HALF_GRAD_REST)
+        disperse(g_ref, place, keep_ref, send_ref, HALF_GRAD_REST)
 
 
 def pack_layer(attn, proj, up, down, layer, out):
@@ -638,7 +647,7 @@
     out[:, 1024:1536] = down[layer].astype(BF16)
 
 
-def pack_kernel(place_ref, table, attn, proj, up, down, head, side, first, second, pad_ref):
+def pack_kernel(fast, table, attn, proj, up, down, head, side, first, second, pad_ref):
     pack_layer(attn, proj, up, down, 0, first)
     pack_layer(attn, proj, up, down, 1, second)
     second[:, 1536:1792] = head[...].astype(BF16)
@@ -651,16 +660,15 @@
     pad_ref[...] = jnp.zeros(pad_ref.shape, F32)
     pad_ref[:, 0:5] = dot_nt(eye, side[...].astype(BF16))
     high = jnp.concatenate([table[:, 512:896], pad_ref[...]], axis=1)
-    first[:, 1536:2048] = jnp.where(place_ref[1] == 0, table[:, 0:512], high).astype(BF16)
-
-
-def finish_kernel(*refs):
-    count = (len(refs) - 6) // 2
-    place_ref = refs[0]
-    scalar_ref = refs[2 * count + 1]
-    out_rest, out_other, out_table, out_small = refs[2 * count + 2 :]
+    first[:, 1536:2048] = jnp.where(places(fast)[1] == 0, table[:, 0:512], high).astype(BF16)
+
+
+def finish_kernel(fast, *refs):
+    count = (len(refs) - 5) // 2
+    scalar_ref = refs[2 * count]
+    out_rest, out_other, out_table, out_small = refs[2 * count + 1 :]
     square = jnp.zeros((1, 1), F32)
-    for pieces, out in ((refs[1 : count + 1], out_rest), (refs[count + 1 : 2 * count + 1], out_other)):
+    for pieces, out in ((refs[0:count], out_rest), (refs[count : 2 * count], out_other)):
         total = pieces[0][...]
         for piece in pieces[1:]:
             total = total + piece[...].astype(F32)
@@ -668,13 +676,15 @@
         square = square + column_sum(jnp.sum(total * total, axis=1, keepdims=True))
     small = out_rest[:, 896:1024]
     extra = column_sum(jnp.sum(small * small, axis=1, keepdims=True))
-    square = square - jnp.where(place_ref[1] == 0, 0.0, extra)
+    square = square - jnp.where(places(fast)[1] == 0, 0.0, extra)
     out_table[...] = out_rest[:, 512:1024]
     rows = small.shape[0]
-    out_small[0:rows] = small
     lane = lax.broadcasted_iota(jnp.int32, (8, 128), 1)
     top = lax.broadcasted_iota(jnp.int32, (8, 128), 0) == 0
-    out_small[rows : rows + 8] = scalar_ref[...] + jnp.where(top & (lane == 2), square, 0.0)
+    scalars = scalar_ref[...] + jnp.where(top & (lane == 2), square, 0.0)
+    for i in range(out_small.shape[0]):
+        out_small[i, 0:rows] = small
+        out_small[i, rows : rows + 8] = scalars
 
 
 def adam_rule(weight, moment, second, gradient, step_rate, decay_rate):
@@ -688,22 +698,29 @@
     return (weight_new, moment_new, second_new)
 
 
-def adam_kernel(fast, place_ref, rest, others, swapped, gathered, *refs):
+def adam_kernel(fast, rest, others, swapped, gathered, beside, *refs):
     rows = rest.shape[0]
-    quarters = [gathered.at[4 * z] for z in range(4)] if fast else [refs[0].at[z] for z in range(4)]
-    refs = refs if fast else refs[1:]
+    _, core, wide = places(fast)
+    is_first = core == 0
+    if fast:
+        quarters = [jnp.where(is_first, beside[4 * z], gathered[4 * z]) for z in range(4)]
+    else:
+        quarters = [refs[0][z] for z in range(4)]
+        refs = refs[1:]
     params = [refs[3 * i : 3 * i + 3] for i in range(9)]
     loss_ref, valid_ref, norm_ref = refs[27:30]
     outs = [refs[30 + 3 * i : 33 + 3 * i] for i in range(9)]
     small_ref = refs[57]
-    wide = place_ref[2]
-    is_first = place_ref[1] == 0
     for z in range(4):
         small_ref[8 * z : 8 * z + 8, 0:128] = quarters[z][0:8]
         small_ref[8 * z : 8 * z + 8, 128:256] = quarters[z][8:16]
-    scalars = gathered[0, rows : rows + 1]
-    for i in range(1, gathered.shape[0]):
-        scalars = scalars + gathered[i, rows : rows + 1]
+    sums = []
+    for source in (gathered, beside):
+        total = source[0, rows : rows + 1]
+        for i in range(1, source.shape[0]):
+            total = total + source[i, rows : rows + 1]
+        sums.append(total)
+    scalars = sums[0] + sums[1]
     small = small_ref[...]
     loss, valid, square = scalars[:, 0:1], scalars[:, 1:2], scalars[:, 2:3]
     square = square + column_sum(jnp.sum(small * small, axis=1, keepdims=True))
@@ -803,6 +820,10 @@
     return [pltpu.with_memory_space_constraint(a, pltpu.VMEM) for a in arrays]
 
 
+def in_hbm(arrays):
+    return [pltpu.with_memory_space_constraint(a, pltpu.HBM) for a in arrays]
+
+
 def full_spec(a):
     return pl.BlockSpec(a.shape, lambda *_: (0,) * len(a.shape))
 
@@ -823,10 +844,10 @@
 VMEM_MIB = {
     "pack": 58,
     "prepare": 58,
-    "first_forward": 36,
-    "middle": 34,
-    "ff_backward": 30,
-    "attention_backward": 30,
+    "first_forward": 24,
+    "middle": 27,
+    "ff_backward": 17,
+    "attention_backward": 20,
     "finish": 58,
     "adam": 58,
 }
@@ -921,10 +942,9 @@
     side_second,
 ):
     n_high = lax.axis_size("wide") // 4
-    wide, core = lax.axis_index("wide"), lax.axis_index("narrow")
+    wide = lax.axis_index("wide")
     rows = side_weight.shape[0]
     fast = rows == 16
-    place = jnp.stack([wide if fast else jnp.zeros_like(wide), core, wide]).astype(jnp.int32)
 
     def flat(a):
         return jnp.swapaxes(a, -1, -2)
@@ -943,37 +963,38 @@
     table, attn, proj, up, _, down, _, head, side = (group[0] for group in params)
 
     piece_first, piece_second = call(
-        pack_kernel,
+        functools.partial(pack_kernel, fast),
         None,
-        [SMEM_SPEC] + [VMEM_SPEC] * 7,
+        [VMEM_SPEC] * 7,
         [VMEM_SPEC] * 2,
         [shaped((rows, HALF_FIRST_COLS), BF16), shaped((rows, HALF_SECOND_COLS), BF16)],
         [pltpu.VMEM((rows, 128), F32)],
         10**6,
         10**6,
         "pack",
-    )(place, table, attn, proj, up, down, head, side)
+    )(table, attn, proj, up, down, head, side)
     other_bias = swap(up_bias, "narrow", 1)
     column = swap_column(piece_first, n_high)
 
+    column, other_bias = lax.optimization_barrier((column, other_bias))
+    first_column = jnp.stack(column)
+    beside, above = swap(first_column, "wide", 1), swap(first_column, "wide", 2)
+
     count = tokens.shape[0] // lax.axis_size("narrow")
+    ids, first_column = lax.optimization_barrier((flat(tokens), first_column))
     meta, frame_meta = call(
-        prepare_kernel,
+        functools.partial(prepare_kernel, fast),
         None,
-        [SMEM_SPEC] * 2 + [VMEM_SPEC] * 5 + [ANY_SPEC],
+        [SMEM_SPEC] + [VMEM_SPEC] * 5,
         [VMEM_SPEC] * 2,
         [shaped((count, SEQ, 128), jnp.int32), shaped((count, SIDE_ROWS, 128), jnp.int32)],
         [pltpu.VMEM((24, FRAMES), jnp.int32)],
         10**6,
         10**6,
         "prepare",
-    )(place, game_ids, flat(tokens), actions, valid_steps, rewards, end_flags, piece_first)
-    column, meta, other_bias = lax.optimization_barrier((column, meta, other_bias))
-    first_column = jnp.stack(column)
-    beside, above = swap(first_column, "wide", 1), swap(first_column, "wide", 2)
-    beside, first_column, piece_second = lax.optimization_barrier(
-        (beside, first_column, piece_second)
-    )
+    )(game_ids, ids, actions, valid_steps, rewards, end_flags)
+    beside, first_column, meta = lax.optimization_barrier((beside, first_column, meta))
+    above, piece_second = lax.optimization_barrier((above, piece_second))
     across = swap(first_column, "wide", 3)
     second_column = jnp.stack(swap_column(piece_second, n_high))
     second_column, across = lax.optimization_barrier((second_column, across))
@@ -992,9 +1013,9 @@
     side_spec = pl.BlockSpec((D, 128), lambda i: (0, 0))
     hits_spec = row_spec((SEQ, ROWS))
     results = call(
-        first_forward_kernel,
+        functools.partial(first_forward_kernel, fast),
         (count,),
-        [SMEM_SPEC, meta_spec] + vec_specs + [VMEM_SPEC] * 8,
+        [meta_spec] + vec_specs + [VMEM_SPEC] * 8,
         [w_attention_spec, w_ff_spec, side_spec, row_spec((SEQ, D)), hits_spec, row_spec((SEQ, D))]
         + kept_specs,
         [shaped((D, 1024), BF16), shaped((D, 2048), BF16), shaped((D, 128), BF16), row_f32]
@@ -1004,7 +1025,7 @@
         4 * 10**9,
         20 * 10**6,
         "first_forward",
-    )(place, meta, vectors, up_bias, other_bias, *resident(first_parts))
+    )(*in_hbm([meta, vectors, up_bias, other_bias]), *resident(first_parts))
     w_attention, w_ff, side_copy, stream, hits, stream_first = results[0:6]
     kept = results[6:]
     received, side_copy = lax.optimization_barrier((second_mine[1:], side_copy))
@@ -1023,9 +1044,9 @@
     small_scratch = pltpu.VMEM((SMALL_ROWS, 8, D), F32)
     scalar_spec = pl.BlockSpec((8, 128), lambda i: (0, 0))
     grad_stream, keep_second, send_second, small_grads, scalars = call(
-        middle_kernel,
+        functools.partial(middle_kernel, fast),
         (count,),
-        [SMEM_SPEC, meta_spec, row_spec((SIDE_ROWS, 128))]
+        [meta_spec, row_spec((SIDE_ROWS, 128))]
         + vec_specs
         + [side_spec, row_spec((SEQ, D))]
         + [VMEM_SPEC] * 8,
@@ -1038,7 +1059,8 @@
         ]
         + [pltpu.VMEM(shape, dtype) for shape, dtype in KEPT]
         + FORWARD_WORK
-        + BACKWARD_WORK
+        + BACKWARD_WORK[0:1]
+        + BACKWARD_WORK[2:]
         + [
             PROJ_WORK,
             pltpu.VMEM((SEQ, FF), BF16),
@@ -1057,14 +1079,19 @@
         15 * 10**9,
         20 * 10**6,
         "middle",
-    )(place, meta, frame_meta, vectors, up_bias, other_bias, side_copy, stream, *resident(second_parts))
+    )(
+        *in_hbm([meta, frame_meta, vectors, up_bias, other_bias]),
+        side_copy,
+        stream,
+        *resident(second_parts),
+    )
     second_sums = add_cores(keep_second, send_second, wide, n_high)
 
     kept_ff = (kept[8], kept[9], kept[10], kept[12])
     grad_mid, keep_ff, send_ff, small_grads = call(
-        ff_backward_kernel,
+        functools.partial(ff_backward_kernel, fast),
         (count,),
-        [SMEM_SPEC, full_spec(vectors), w_ff_spec, row_spec((SEQ, D)), small_spec]
+        [full_spec(vectors), w_ff_spec, row_spec((SEQ, D)), small_spec]
         + [row_spec(a.shape[1:]) for a in kept_ff],
         [row_spec((SEQ, D))] + [blocks(HALF_GRAD_COLS)] * 2 + [small_spec],
         [row_f32] + block_shapes(HALF_GRAD_COLS) + [small_shape],
@@ -1080,15 +1107,15 @@
         4 * 10**9,
         10 * 10**6,
         "ff_backward",
-    )(place, vectors, w_ff, grad_stream, small_grads, *kept_ff)
+    )(*in_hbm([vectors]), w_ff, grad_stream, small_grads, *kept_ff)
     ff_sums = add_cores(keep_ff, send_ff, wide, n_high)
     other_sums = [jnp.concatenate(pair, axis=-1) for pair in zip(second_sums, ff_sums)]
     others_received = swap_plane(other_sums)
     kept_attention = (stream_first,) + tuple(kept[0:8]) + (kept[11],)
     keep_rest, send_rest, small_grads = call(
-        attention_backward_kernel,
+        functools.partial(attention_backward_kernel, fast),
         (count,),
-        [SMEM_SPEC, full_spec(vectors), w_attention_spec, row_spec((SEQ, D)), hits_spec, small_spec]
+        [full_spec(vectors), w_attention_spec, row_spec((SEQ, D)), hits_spec, small_spec]
         + [row_spec(a.shape[1:]) for a in kept_attention]
         + [ANY_SPEC],
         [blocks(HALF_GRAD_COLS)] * 2 + [pl.BlockSpec((SMALL_ROWS, D), lambda i: (0, 0))],
@@ -1100,7 +1127,7 @@
         6 * 10**9,
         20 * 10**6,
         "attention_backward",
-    )(place, vectors, w_attention, grad_mid, hits, small_grads, *kept_attention, other_sums[0])
+    )(*in_hbm([vectors]), w_attention, grad_mid, hits, small_grads, *kept_attention, other_sums[0])
     others_received, keep_rest = lax.optimization_barrier((others_received, keep_rest))
     rest_sums = add_cores(keep_rest, send_rest, wide, n_high)
     rest_received = swap_plane(rest_sums)
@@ -1108,27 +1135,24 @@
     rest_pieces = column_pieces(add_plane(rest_sums[0], rest_received))
 
     grad_rest, grad_others, table_part, small = call(
-        finish_kernel,
+        functools.partial(finish_kernel, fast),
         None,
-        [SMEM_SPEC] + [VMEM_SPEC] * (2 * n_high + 1),
+        [VMEM_SPEC] * (2 * n_high + 1),
         [VMEM_SPEC] * 4,
         [
             shaped((rows, HALF_GRAD_COLS), F32),
             shaped((rows, HALF_GRAD_COLS + HALF_SECOND_COLS), F32),
             shaped((rows, 512), F32),
-            shaped((rows + 8, 128), F32),
+            shaped((4 * n_high, rows + 8, 128), F32),
         ],
         [],
         10**6,
         10**6,
         "finish",
-    )(place, *resident(rest_pieces + other_pieces), scalars)
-
-    beside = swap(small, "narrow", 1)
-    is_small = (jnp.arange(rows + 8) < rows)[:, None]
-    small = jnp.where(is_small, jnp.where(core == 1, small, beside), small + beside)
-    small = jnp.broadcast_to(small, (4 * n_high,) + small.shape)
+    )(*resident(rest_pieces + other_pieces), scalars)
+
     gathered = lax.all_to_all(small, "wide", 0, 0)
+    beside = swap(gathered, "narrow", 1)
     quarters = []
     if not fast:
         total = lax.psum(small_grads, ("wide", "narrow"))
@@ -1139,14 +1163,14 @@
     results = call(
         functools.partial(adam_kernel, fast),
         None,
-        [SMEM_SPEC] + [VMEM_SPEC] * (31 + len(quarters)),
+        [VMEM_SPEC] * (32 + len(quarters)),
         [VMEM_SPEC] * 30,
         [shaped((1, 1), F32)] * 3 + [shaped(a.shape, F32) for a in flat_params],
         [pltpu.VMEM((SMALL_ROWS, D), F32)],
         10**6,
         10**6,
         "adam",
-    )(place, grad_rest, grad_others, *resident([swapped, gathered]), *quarters, *flat_params)
+    )(grad_rest, grad_others, *resident([swapped, gathered, beside]), *quarters, *flat_params)
     news = list(results[3:])
     for group in (0, 2, 5, 8):
         for member in range(3 * group, 3 * group + 3):

time: 169 us -> 163 us (0.964)
  blocking collectives: 0 us -> 11.6 us
  waiting for transfers between devices: 32 us -> 26.1 us
  local copies, waits for them, and re-layouts: 6 us -> 0.39 us
  starting transfers between devices: 42.7 us -> 38 us
    all_to_all x0 -> x1, blocking collectives: none -> 11.6 us  [per_device(): gathered = lax.all_to_all(small, 'wide', 0, 0)]
    all_to_all x1 -> x0, waiting for transfers between devices: 7.49 us -> none  [per_device(): gathered = lax.all_to_all(small, 'wide', 0, 0)]
    all_to_all x1 -> x0, starting transfers between devices: 5.02 us -> none  [per_device(): gathered = lax.all_to_all(small, 'wide', 0, 0)]
    unnamed x34 -> x4, local copies, waits for them, and re-layouts: 5.27 us -> 0.34 us
  transfers between devices with their start and end apart: 39 -> 38, of which waited for: 18 -> 16; matrix products, arithmetic and copies ran while one was open for 1% -> 1% of each run, Pallas kernels for 24% -> 25%
where the time goes in v6:
time: 163 us; the launch traced here: 162 us
  Pallas kernels  82.3 us (50%)
  starting transfers between devices  38 us (23%)
  waiting for transfers between devices  26.1 us (16%)
  blocking collectives  11.6 us (7%)
  other arithmetic  2.6 us (2%)
    ppermute x38, starting transfers between devices, swap(): return lax.ppermute(a, axis, [(i, i ^ distance) for i in range(size)])  38 us
    pallas_call x1, Pallas kernels, per_device(): call(functools.partial(middle_kernel, fast), (count,), [meta_spec, row_sp...  36.4 us
    ppermute x38, waiting for transfers between devices, swap(): return lax.ppermute(a, axis, [(i, i ^ distance) for i in range(size)])  26.1 us
    pallas_call x1, Pallas kernels, per_device(): call(functools.partial(first_forward_kernel, fast), (count,), [meta_spec]...  16.2 us
    pallas_call x1, Pallas kernels, per_device(): call(functools.partial(attention_backward_kernel, fast), (count,), [full_...  14.2 us
    all_to_all x1, blocking collectives, per_device(): gathered = lax.all_to_all(small, 'wide', 0, 0)  11.6 us
    pallas_call x1, Pallas kernels, per_device(): call(functools.partial(ff_backward_kernel, fast), (count,), [full_spec(ve...  6.5 us
    pallas_call x1, Pallas kernels, per_device(): call(functools.partial(prepare_kernel, fast), None, [SMEM_SPEC] + [VMEM_S...  3.29 us
  transfers between devices with their start and end apart: 38, of which 16 were waited for; matrix products, arithmetic and copies ran while one was open for 1% of the time, Pallas kernels for 25%

profile of v6, /device:TPU:0, one launch (start us, length us, event | category | flops | bytes accessed | tf_op | source)
XLA Modules:
  0.0 162.0 jit_solution(11182256028107689840)
XLA Ops:
  0.7 1.7 %pack.1 = (bf16[16,2048]{1,0:T(8,128)(2,1)}, bf16[16,1792]{1,0:T(8,128)(2,1)}) custom-call(f32[16,896]{1,0:T(8,128)} %bitcast.83, f32[2,3,16,128]{3,2,1,0:T(8,128)} %refs_3_.3, f32[2,16,128]{2,1,0:T(8,128)} %bitcast.85, f32[2,16,512]{2,1,0:T(8,128)} %refs_9_.1, f32[2,16,512]{2,1,0:T(8,128)} %bitcast.81, f32[16,256]{1,0:T(8,128)} %refs_21_.1, f32[5,16]{1,0:T(8,128)} %bitcast.102), custom_call_target="tpu_custom_call" | custom-call | flops 1000000 | bytes 1000000 | tf_op jit(solution)/shard_map/pack/pallas_call | solution.py:965
  2.4 5.0 %collective-permute-start.2 = (bf16[16,2048]{1,0:T(8,128)(2,1)}, bf16[16,2048]{1,0:T(8,128)(2,1)S(1)}, u32[]{:S(2)}, u32[]{:S(2)}) collective-permute-start(bf16[16,2048]{1,0:T(8,128)(2,1)} %get-tuple-element.121), channel_id=1, source_target_pairs={{0,24},{2,26},{4,28},{6,30},{8,16},{10,18},{12,20},{14,22},{16,8},... | collective-permute-start | bytes 196616 | tf_op jit(solution)/shard_map/ppermute | solution.py:765
  7.5 0.6 collective-permute-start
  8.0 1.4 collective-permute-done.3.refs_3_.refs_4_
  9.4 0.9 collective-permute-done.2
  10.3 3.0 %collective-permute-done.1 = bf16[16,2048]{1,0:T(8,128)(2,1)S(1)} collective-permute-done((bf16[16,2048]{1,0:T(8,128)(2,1)}, bf16[16,2048]{1,0:T(8,128)(2,1)S(1)}, u32[]{:S(2)}, u32[]{:S(2)}) %collective-permute-start.1) | collective-permute-done | bytes 65568 | tf_op jit(solution)/shard_map/ppermute | solution.py:765
  13.3 0.9 pad_maximum_fusion.4.refs_4_
  14.1 1.6 collective-permute-start.5
  15.7 1.5 collective-permute-start.4
  17.2 4.9 %collective-permute-done.5.refs_6_ = bf16[4,16,2048]{2,1,0:T(8,128)(2,1)S(1)} collective-permute-done((bf16[4,16,2048]{2,1,0:T(8,128)(2,1)S(1)}, bf16[4,16,2048]{2,1,0:T(8,128)(2,1)S(1)}, u32[]{:S(2)}, u32[]{:S(2)}) %collective-permute-start.5) | collective-permute-done | bytes 262176 | tf_op jit(solution)/shard_map/ppermute | solution.py:765
  22.1 1.5 collective-permute-start.8
  23.7 2.8 %collective-permute-start.6 = (bf16[16,1792]{1,0:T(8,128)(2,1)}, bf16[16,1792]{1,0:T(8,128)(2,1)S(1)}, u32[]{:S(2)}, u32[]{:S(2)}) collective-permute-start(bf16[16,1792]{1,0:T(8,128)(2,1)} %get-tuple-element.132), channel_id=1, source_target_pairs={{0,8},{2,10},{4,12},{6,14},{8,0},{10,2},{12,4},{14,6},{16,24},{18,... | collective-permute-start | bytes 172040 | tf_op jit(solution)/shard_map/ppermute | solution.py:765
  26.5 3.3 %prepare.1 = (s32[4,352,128]{2,1,0:T(8,128)}, s32[4,32,128]{2,1,0:T(8,128)}) custom-call(s32[8]{0:T(128)} %games_ref.1, s32[8,16,20]{2,1,0:T(8,128)} %bitcast.89, s32[8,20]{1,0:T(8,128)} %actions.1, s32[8,20]{1,0:T(8,128)} %valid.1, s32[8,20]{1,0:T(8,128)} %rewards.1, s32[8,20]{1,0:T(8,128)} %ends.1), custom_call_target="tpu_custom_call" | custom-call | flops 1000000 | bytes 1000000 | tf_op jit(solution)/shard_map/prepare/pallas_call | solution.py:985
  29.8 2.6 %collective-permute-start.9 = (bf16[4,16,2048]{2,1,0:T(8,128)(2,1)S(1)}, bf16[4,16,2048]{2,1,0:T(8,128)(2,1)S(1)}, u32[]{:S(2)}, u32[]{:S(2)}) collective-permute-start(bf16[4,16,2048]{2,1,0:T(8,128)(2,1)S(1)} %pad_maximum_fusion.4.refs_4_), channel_id=1, source_target_pairs={{0,6},{2,4},{4,2},{6,0},{8,14},{10,12},{12,10},{14,8},{16,22},{18,... | collective-permute-start | bytes 786440 | tf_op jit(solution)/shard_map/ppermute | solution.py:765
  32.4 0.5 collective-permute-start.15
  33.0 0.8 pad_maximum_fusion.5.refs_7_
  33.8 3.2 %collective-permute-done.9.refs_7_ = bf16[4,16,2048]{2,1,0:T(8,128)(2,1)S(1)} collective-permute-done((bf16[4,16,2048]{2,1,0:T(8,128)(2,1)S(1)}, bf16[4,16,2048]{2,1,0:T(8,128)(2,1)S(1)}, u32[]{:S(2)}, u32[]{:S(2)}) %collective-permute-start.9) | collective-permute-done | bytes 262176 | tf_op jit(solution)/shard_map/ppermute | solution.py:765
  37.0 0.5 collective-permute-start.17
  37.6 2.6 %collective-permute-start.12 = (bf16[4,16,1792]{2,1,0:T(8,128)(2,1)S(1)}, bf16[4,16,1792]{2,1,0:T(8,128)(2,1)S(1)}, u32[]{:S(2)}, u32[]{:S(2)}) collective-permute-start(bf16[4,16,1792]{2,1,0:T(8,128)(2,1)S(1)} %pad_maximum_fusion.5.refs_7_), channel_id=1, source_target_pairs={{0,6},{2,4},{4,2},{6,0},{8,14},{10,12},{12,10},{14,8},{16,22},{18,... | collective-permute-start | bytes 688136 | tf_op jit(solution)/shard_map/ppermute | solution.py:765
  40.2 0.5 collective-permute-start.11
  41.1 16.2 %first_forward.1 = (bf16[256,1024]{1,0:T(8,128)(2,1)S(1)}, bf16[256,2048]{1,0:T(8,128)(2,1)S(1)}, bf16[256,128]{1,0:T(8,128)(2,1)S(1)}, f32[4,352,256]{2,1,0:T(8...) custom-call(s32[4,352,128]{2,1,0:T(8,128)} %get-tuple-element.128.re, ...), custom_call_target="tpu_custom_call" | custom-call | flops 4000000000 | bytes 20000000 | tf_op jit(solution)/shard_map/first_forward/pallas_call | solution.py:1015
  57.4 0.5 collective-permute-start.19
  57.9 0.9 collective-permute-done.18.refs_12_
  59.5 36.4 %middle.1 = (f32[4,352,256]{2,1,0:T(8,128)S(1)}, bf16[4,4,16,1792]{3,2,1,0:T(8,128)(2,1)S(1)}, bf16[4,4,16,1792]{3,2,1,0:T(8,128)(2,1)S(1)}, f32[32,8,256]{2,1,0:T(8,128)S(1)}, f32[8,128]{1,0:T(8,128)S(1)}) custom-call(s32[4,352,128]{2,1,0:T(8,128)} %get-tuple-element.128.refs_0_, s32[4,32,128]{2,1,0:T(8,128)} %get-tuple-element.129.refs_1_, ...), custom_call_target="tpu_custom_call" | custom-call | flops 15000000512 | bytes 20000000 | tf_op jit(solution)/shard_map/middle/pallas_call | solution.py:1046
  96.4 6.5 %ff_backward.1 = (f32[4,352,256]{2,1,0:T(8,128)S(1)}, bf16[4,4,16,1024]{3,2,1,0:T(8,128)(2,1)S(1)}, bf16[4,4,16,1024]{3,2,1,0:T(8,128)(2,1)S(1)}, f32[32,8,256]{2,1,0:T(8,128)S(1)}) custom-call(f32[14,256]{1,0:T(8,128)} %refs_18_.1, bf16[256,2048]{1,0:T(8,128)(2,1)S(1)} %get-tuple-element.146.refs_1_, f32[4,352,256]{2,1,0:T(8,128)S(1)} %get-tuple-element.147.refs_2_, ...), custom_call_target="tpu_custom_call" | custom-call | flops 4000000000 | bytes 10000000 | tf_op jit(solution)/shard_map/ff_backward/pallas_call | solution.py:1091
  103.2 1.7 %collective-permute-done.22 = bf16[4,4,16,1024]{3,2,1,0:T(8,128)(2,1)S(1)} collective-permute-done((bf16[4,4,16,1024]{3,2,1,0:T(8,128)(2,1)S(1)}, bf16[4,4,16,1024]{3,2,1,0:T(8,128)(2,1)S(1)}, u32[]{:S(2)}, u32[]{:S(2)}) %collective-permute-start.22) | collective-permute-done | bytes 524320 | tf_op jit(solution)/shard_map/ppermute | solution.py:765
  105.4 1.7 %collective-permute-start.23 = (bf16[4,16,2816]{2,1,0:T(8,128)(2,1)S(1)}, bf16[4,16,2816]{2,1,0:T(8,128)(2,1)S(1)}, u32[]{:S(2)}, u32[]{:S(2)}) collective-permute-start(bf16[4,16,2816]{2,1,0:T(8,128)(2,1)S(1)} %pad_maximum_fusion.1), channel_id=1, source_target_pairs={{0,2},{2,0},{4,6},{6,4},{8,10},{10,8},{12,14},{14,12},{16,18},{18,... | collective-permute-start | bytes 1081352 | tf_op jit(solution)/shard_map/ppermute | solution.py:765
  107.1 1.6 collective-permute-start.24
  109.2 14.2 %attention_backward.1 = (bf16[4,4,16,1024]{3,2,1,0:T(8,128)(2,1)S(1)}, bf16[4,4,16,1024]{3,2,1,0:T(8,128)(2,1)S(1)}, f32[32,256]{1,0:T(8,128)}) custom-call(f32[14,256]{1,0:T(8,128)} %refs_18_.1, bf16[256,1024]{1,0:T(8,128)(2,1)S(1)} %get-tuple-element.155.refs_1_, f32[4,352,256]{2,1,0:T(8,128)S(1)} %get-tuple-element.156.refs_2_, ...), custom_call_target="tpu_custom_call" | custom-call | flops 6000000000 | bytes 20000000 | tf_op jit(solution)/shard_map/attention_backward/pallas_call | solution.py:1115
  123.3 1.8 %collective-permute-done.24 = bf16[4,16,2816]{2,1,0:T(8,128)(2,1)S(1)} collective-permute-done((bf16[4,16,2816]{2,1,0:T(8,128)(2,1)S(1)}, bf16[4,16,2816]{2,1,0:T(8,128)(2,1)S(1)}, u32[]{:S(2)}, u32[]{:S(2)}) %collective-permute-start.24) | collective-permute-done | bytes 360480 | tf_op jit(solution)/shard_map/ppermute | solution.py:765
  125.3 1.4 collective-permute-start.35
  126.7 0.4 collective-permute-start.34
  127.3 1.2 collective-permute-start.27
  128.5 1.8 %collective-permute-start.29 = (bf16[4,16,1024]{2,1,0:T(8,128)(2,1)S(1)}, bf16[4,16,1024]{2,1,0:T(8,128)(2,1)S(1)}, u32[]{:S(2)}, u32[]{:S(2)}) collective-permute-start(bf16[4,16,1024]{2,1,0:T(8,128)(2,1)S(1)} %get-tuple-element.219), channel_id=1, source_target_pairs={{0,6},{2,4},{4,2},{6,0},{8,14},{10,12},{12,10},{14,8},{16,22},{18,... | collective-permute-start | bytes 393224 | tf_op jit(solution)/shard_map/ppermute | solution.py:765
  130.3 0.5 collective-permute-start.28
  130.8 2.5 %collective-permute-done.27 = bf16[4,16,1024]{2,1,0:T(8,128)(2,1)S(1)} collective-permute-done((bf16[4,16,1024]{2,1,0:T(8,128)(2,1)S(1)}, bf16[4,16,1024]{2,1,0:T(8,128)(2,1)S(1)}, u32[]{:S(2)}, u32[]{:S(2)}) %collective-permute-start.27) | collective-permute-done | bytes 131104 | tf_op jit(solution)/shard_map/ppermute | solution.py:765
  133.3 2.6 %collective-permute-start.33 = (bf16[16,2816]{1,0:T(8,128)(2,1)S(1)}, bf16[16,2816]{1,0:T(8,128)(2,1)S(1)}, u32[]{:S(2)}, u32[]{:S(2)}) collective-permute-start(bf16[16,2816]{1,0:T(8,128)(2,1)S(1)} %get-tuple-element.227), channel_id=1, source_target_pairs={{0,8},{2,10},{4,12},{6,14},{8,0},{10,2},{12,4},{14,6},{16,24},{18,... | collective-permute-start | bytes 270344 | tf_op jit(solution)/shard_map/ppermute | solution.py:765
  135.9 0.5 collective-permute-done.28
  136.5 2.4 %collective-permute-start.32 = (bf16[16,1024]{1,0:T(8,128)(2,1)S(1)}, bf16[16,1024]{1,0:T(8,128)(2,1)S(1)}, u32[]{:S(2)}, u32[]{:S(2)}) collective-permute-start(bf16[16,1024]{1,0:T(8,128)(2,1)S(1)} %get-tuple-element.228), channel_id=1, source_target_pairs={{0,24},{2,26},{4,28},{6,30},{8,16},{10,18},{12,20},{14,22},{16,8},... | collective-permute-start | bytes 98312 | tf_op jit(solution)/shard_map/ppermute | solution.py:765
  138.9 1.7 %collective-permute-start.31 = (bf16[16,1024]{1,0:T(8,128)(2,1)S(1)}, bf16[16,1024]{1,0:T(8,128)(2,1)S(1)}, u32[]{:S(2)}, u32[]{:S(2)}) collective-permute-start(bf16[16,1024]{1,0:T(8,128)(2,1)S(1)} %get-tuple-element.229), channel_id=1, source_target_pairs={{0,16},{2,18},{4,20},{6,22},{8,24},{10,26},{12,28},{14,30},{16,0},... | collective-permute-start | bytes 98312 | tf_op jit(solution)/shard_map/ppermute | solution.py:765
  141.0 1.3 collective-permute-done.32.refs_3_
  142.3 1.8 %collective-permute-done.31.refs_2_ = bf16[16,1024]{1,0:T(8,128)(2,1)S(1)} collective-permute-done((bf16[16,1024]{1,0:T(8,128)(2,1)S(1)}, bf16[16,1024]{1,0:T(8,128)(2,1)S(1)}, u32[]{:S(2)}, u32[]{:S(2)}) %collective-permute-start.31) | collective-permute-done | bytes 32800 | tf_op jit(solution)/shard_map/ppermute | solution.py:765
  144.1 0.5 collective-permute-done.30.refs_1_
  144.6 1.5 finish.1
  146.1 11.6 %all_to_all.5.gathered = f32[16,24,128]{2,1,0:T(8,128)S(1)} all-to-all(f32[16,24,128]{2,1,0:T(8,128)} %get-tuple-element.179), channel_id=1, replica_groups=mesh['wide'=16,'narrow'=2] {'wide'}, dimensions={0} | all-to-all | bytes 393216 | tf_op jit(solution)/shard_map/all_to_all | solution.py:1154
  157.8 0.5 collective-permute-start.36
  158.3 1.1 collective-permute-done.36.swapped
  159.3 2.5 %adam.1 = (f32[1,1]{1,0:T(1,128)}, f32[1,1]{1,0:T(1,128)}, f32[1,1]{1,0:T(1,128)}, f32[16,896]{1,0:T(8,128)}, f32[16,896]{1,0:T(8,128)}, /*index=5*/f32[16,896]{...) custom-call(f32[16,1024]{1,0:T(8,128)} %get-tuple-element.176.rest, ...), custom_call_target="tpu_custom_call" | custom-call | flops 1000000 | bytes 1000000 | tf_op jit(solution)/shard_map/adam/pallas_call | solution.py:1163
  (56 shorter events, 3.8 us)
Async XLA Ops:
  2.4 7.9 %collective-permute-start.2 = (bf16[16,2048]{1,0:T(8,128)(2,1)}, bf16[16,2048]{1,0:T(8,128)(2,1)S(1)}, u32[]{:S(2)}, u32[]{:S(2)}) collective-permute-start(bf16[16,2048]{1,0:T(8,128)(2,1)} %get-tuple-element.121), channel_id=1, source_target_pairs={{0,24},{2,26},{4,28},{6,30},{8,16},{10,18},{12,20},{14,22},{16,8},... | collective-permute-start | bytes 196616 | tf_op jit(solution)/shard_map/ppermute | solution.py:765
  7.4 5.8 %collective-permute-start.1 = (bf16[16,2048]{1,0:T(8,128)(2,1)}, bf16[16,2048]{1,0:T(8,128)(2,1)S(1)}, u32[]{:S(2)}, u32[]{:S(2)}) collective-permute-start(bf16[16,2048]{1,0:T(8,128)(2,1)} %get-tuple-element.121), channel_id=1, source_target_pairs={{0,16},{2,18},{4,20},{6,22},{8,24},{10,26},{12,28},{14,30},{16,0},... | collective-permute-start | bytes 196616 | tf_op jit(solution)/shard_map/ppermute | solution.py:765
  7.5 5.8 %collective-permute-start = (bf16[16,2048]{1,0:T(8,128)(2,1)}, bf16[16,2048]{1,0:T(8,128)(2,1)S(1)}, u32[]{:S(2)}, u32[]{:S(2)}) collective-permute-start(bf16[16,2048]{1,0:T(8,128)(2,1)} %get-tuple-element.121), channel_id=1, source_target_pairs={{0,8},{2,10},{4,12},{6,14},{8,0},{10,2},{12,4},{14,6},{16,24},{18,... | collective-permute-start | bytes 196616 | tf_op jit(solution)/shard_map/ppermute | solution.py:765
  8.0 1.4 collective-permute-start.3
  9.4 31.7 %copy-start.1 = (f32[2,512]{1,0:T(2,128)}, f32[2,512]{1,0:T(2,128)S(1)}, u32[]{:S(2)}) copy-start(f32[2,512]{1,0:T(2,128)S(1)} %collective-permute-done.3.refs_3_.refs_4_) | copy-start | bytes 12292
  14.1 7.9 %collective-permute-start.5 = (bf16[4,16,2048]{2,1,0:T(8,128)(2,1)S(1)}, bf16[4,16,2048]{2,1,0:T(8,128)(2,1)S(1)}, u32[]{:S(2)}, u32[]{:S(2)}) collective-permute-start(bf16[4,16,2048]{2,1,0:T(8,128)(2,1)S(1)} %pad_maximum_fusion.4.refs_4_), channel_id=1, source_target_pairs={{0,4},{2,6},{4,0},{6,2},{8,12},{10,14},{12,8},{14,10},{16,20},{18,... | collective-permute-start | bytes 786440 | tf_op jit(solution)/shard_map/ppermute | solution.py:765
  15.7 14.0 %collective-permute-start.4 = (bf16[4,16,2048]{2,1,0:T(8,128)(2,1)S(1)}, bf16[4,16,2048]{2,1,0:T(8,128)(2,1)S(1)}, u32[]{:S(2)}, u32[]{:S(2)}) collective-permute-start(bf16[4,16,2048]{2,1,0:T(8,128)(2,1)S(1)} %pad_maximum_fusion.4.refs_4_), channel_id=1, source_target_pairs={{0,2},{2,0},{4,6},{6,4},{8,10},{10,8},{12,14},{14,12},{16,18},{18,... | collective-permute-start | bytes 786440 | tf_op jit(solution)/shard_map/ppermute | solution.py:765
  22.1 10.3 %collective-permute-start.8 = (bf16[16,1792]{1,0:T(8,128)(2,1)}, bf16[16,1792]{1,0:T(8,128)(2,1)S(1)}, u32[]{:S(2)}, u32[]{:S(2)}) collective-permute-start(bf16[16,1792]{1,0:T(8,128)(2,1)} %get-tuple-element.132), channel_id=1, source_target_pairs={{0,24},{2,26},{4,28},{6,30},{8,16},{10,18},{12,20},{14,22},{16,8},... | collective-permute-start | bytes 172040 | tf_op jit(solution)/shard_map/ppermute | solution.py:765
  23.6 9.3 %collective-permute-start.7 = (bf16[16,1792]{1,0:T(8,128)(2,1)}, bf16[16,1792]{1,0:T(8,128)(2,1)S(1)}, u32[]{:S(2)}, u32[]{:S(2)}) collective-permute-start(bf16[16,1792]{1,0:T(8,128)(2,1)} %get-tuple-element.132), channel_id=1, source_target_pairs={{0,16},{2,18},{4,20},{6,22},{8,24},{10,26},{12,28},{14,30},{16,0},... | collective-permute-start | bytes 172040 | tf_op jit(solution)/shard_map/ppermute | solution.py:765
  23.7 9.3 %collective-permute-start.6 = (bf16[16,1792]{1,0:T(8,128)(2,1)}, bf16[16,1792]{1,0:T(8,128)(2,1)S(1)}, u32[]{:S(2)}, u32[]{:S(2)}) collective-permute-start(bf16[16,1792]{1,0:T(8,128)(2,1)} %get-tuple-element.132), channel_id=1, source_target_pairs={{0,8},{2,10},{4,12},{6,14},{8,0},{10,2},{12,4},{14,6},{16,24},{18,... | collective-permute-start | bytes 172040 | tf_op jit(solution)/shard_map/ppermute | solution.py:765
  29.8 7.3 %collective-permute-start.9 = (bf16[4,16,2048]{2,1,0:T(8,128)(2,1)S(1)}, bf16[4,16,2048]{2,1,0:T(8,128)(2,1)S(1)}, u32[]{:S(2)}, u32[]{:S(2)}) collective-permute-start(bf16[4,16,2048]{2,1,0:T(8,128)(2,1)S(1)} %pad_maximum_fusion.4.refs_4_), channel_id=1, source_target_pairs={{0,6},{2,4},{4,2},{6,0},{8,14},{10,12},{12,10},{14,8},{16,22},{18,... | collective-permute-start | bytes 786440 | tf_op jit(solution)/shard_map/ppermute | solution.py:765
  32.4 8.3 %collective-permute-start.13 = (bf16[4,16,2048]{2,1,0:T(8,128)(2,1)S(1)}, bf16[4,16,2048]{2,1,0:T(8,128)(2,1)S(1)}, u32[]{:S(2)}, u32[]{:S(2)}) collective-permute-start(bf16[4,16,2048]{2,1,0:T(8,128)(2,1)S(1)} %pad_maximum_fusion.4.refs_4_), channel_id=1, source_target_pairs={{0,1},{1,0},{2,3},{3,2},{4,5},{5,4},{6,7},{7,6},{8,9},{9,8},{10,11... | collective-permute-start | bytes 786440 | tf_op jit(solution)/shard_map/ppermute | solution.py:765
  32.4 5.2 %collective-permute-start.15 = (bf16[4,16,2048]{2,1,0:T(8,128)(2,1)S(1)}, bf16[4,16,2048]{2,1,0:T(8,128)(2,1)S(1)}, u32[]{:S(2)}, u32[]{:S(2)}) collective-permute-start(bf16[4,16,2048]{2,1,0:T(8,128)(2,1)S(1)} %collective-permute-done.5.refs_6_), channel_id=1, source_target_pairs={{0,1},{1,0},{2,3},{3,2},{4,5},{5,4},{6,7},{7,6},{8,9},{9,8},{10,11... | collective-permute-start | bytes 786440 | tf_op jit(solution)/shard_map/ppermute | solution.py:765
  32.9 7.3 %collective-permute-start.14 = (bf16[4,16,2048]{2,1,0:T(8,128)(2,1)S(1)}, bf16[4,16,2048]{2,1,0:T(8,128)(2,1)S(1)}, u32[]{:S(2)}, u32[]{:S(2)}) collective-permute-start(bf16[4,16,2048]{2,1,0:T(8,128)(2,1)S(1)} %collective-permute-done.4.refs_5_), channel_id=1, source_target_pairs={{0,1},{1,0},{2,3},{3,2},{4,5},{5,4},{6,7},{7,6},{8,9},{9,8},{10,11... | collective-permute-start | bytes 786440 | tf_op jit(solution)/shard_map/ppermute | solution.py:765
  37.0 4.0 %collective-permute-start.16 = (bf16[4,16,2048]{2,1,0:T(8,128)(2,1)S(1)}, bf16[4,16,2048]{2,1,0:T(8,128)(2,1)S(1)}, u32[]{:S(2)}, u32[]{:S(2)}) collective-permute-start(bf16[4,16,2048]{2,1,0:T(8,128)(2,1)S(1)} %collective-permute-done.9.refs_7_), channel_id=1, source_target_pairs={{0,1},{1,0},{2,3},{3,2},{4,5},{5,4},{6,7},{7,6},{8,9},{9,8},{10,11... | collective-permute-start | bytes 786440 | tf_op jit(solution)/shard_map/ppermute | solution.py:765
  37.0 20.9 %collective-permute-start.17 = (bf16[4,16,1792]{2,1,0:T(8,128)(2,1)S(1)}, bf16[4,16,1792]{2,1,0:T(8,128)(2,1)S(1)}, u32[]{:S(2)}, u32[]{:S(2)}) collective-permute-start(bf16[4,16,1792]{2,1,0:T(8,128)(2,1)S(1)} %pad_maximum_fusion.5.refs_7_), channel_id=1, source_target_pairs={{0,1},{1,0},{2,3},{3,2},{4,5},{5,4},{6,7},{7,6},{8,9},{9,8},{10,11... | collective-permute-start | bytes 688136 | tf_op jit(solution)/shard_map/ppermute | solution.py:765
  37.6 19.7 %collective-permute-start.12 = (bf16[4,16,1792]{2,1,0:T(8,128)(2,1)S(1)}, bf16[4,16,1792]{2,1,0:T(8,128)(2,1)S(1)}, u32[]{:S(2)}, u32[]{:S(2)}) collective-permute-start(bf16[4,16,1792]{2,1,0:T(8,128)(2,1)S(1)} %pad_maximum_fusion.5.refs_7_), channel_id=1, source_target_pairs={{0,6},{2,4},{4,2},{6,0},{8,14},{10,12},{12,10},{14,8},{16,22},{18,... | collective-permute-start | bytes 688136 | tf_op jit(solution)/shard_map/ppermute | solution.py:765
  40.2 17.1 %collective-permute-start.11 = (bf16[4,16,1792]{2,1,0:T(8,128)(2,1)S(1)}, bf16[4,16,1792]{2,1,0:T(8,128)(2,1)S(1)}, u32[]{:S(2)}, u32[]{:S(2)}) collective-permute-start(bf16[4,16,1792]{2,1,0:T(8,128)(2,1)S(1)} %pad_maximum_fusion.5.refs_7_), channel_id=1, source_target_pairs={{0,4},{2,6},{4,0},{6,2},{8,12},{10,14},{12,8},{14,10},{16,20},{18,... | collective-permute-start | bytes 688136 | tf_op jit(solution)/shard_map/ppermute | solution.py:765
  40.7 16.6 %collective-permute-start.10 = (bf16[4,16,1792]{2,1,0:T(8,128)(2,1)S(1)}, bf16[4,16,1792]{2,1,0:T(8,128)(2,1)S(1)}, u32[]{:S(2)}, u32[]{:S(2)}) collective-permute-start(bf16[4,16,1792]{2,1,0:T(8,128)(2,1)S(1)} %pad_maximum_fusion.5.refs_7_), channel_id=1, source_target_pairs={{0,2},{2,0},{4,6},{6,4},{8,10},{10,8},{12,14},{14,12},{16,18},{18,... | collective-permute-start | bytes 688136 | tf_op jit(solution)/shard_map/ppermute | solution.py:765
  57.3 1.6 collective-permute-start.18
  57.4 1.8 %collective-permute-start.19 = (bf16[4,16,1792]{2,1,0:T(8,128)(2,1)S(1)}, bf16[4,16,1792]{2,1,0:T(8,128)(2,1)S(1)}, u32[]{:S(2)}, u32[]{:S(2)}) collective-permute-start(bf16[4,16,1792]{2,1,0:T(8,128)(2,1)S(1)} %collective-permute-done.11.refs_9_), channel_id=1, source_target_pairs={{0,1},{1,0},{2,3},{3,2},{4,5},{5,4},{6,7},{7,6},{8,9},{9,8},{10,11... | collective-permute-start | bytes 688136 | tf_op jit(solution)/shard_map/ppermute | solution.py:765
  57.9 1.6 %collective-permute-start.20 = (bf16[4,16,1792]{2,1,0:T(8,128)(2,1)S(1)}, bf16[4,16,1792]{2,1,0:T(8,128)(2,1)S(1)}, u32[]{:S(2)}, u32[]{:S(2)}) collective-permute-start(bf16[4,16,1792]{2,1,0:T(8,128)(2,1)S(1)} %collective-permute-done.12.refs_10_), channel_id=1, source_target_pairs={{0,1},{1,0},{2,3},{3,2},{4,5},{5,4},{6,7},{7,6},{8,9},{9,8},{10,11... | collective-permute-start | bytes 688136 | tf_op jit(solution)/shard_map/ppermute | solution.py:765
  95.9 0.6 copy-start
  95.9 9.3 %collective-permute-start.21 = (bf16[4,4,16,1792]{3,2,1,0:T(8,128)(2,1)S(1)}, bf16[4,4,16,1792]{3,2,1,0:T(8,128)(2,1)S(1)}, u32[]{:S(2)}, u32[]{:S(2)}) collective-permute-start(bf16[4,4,16,1792]{3,2,1,0:T(8,128)(2,1)S(1)} %get-tuple-element.145), channel_id=1, source_target_pairs={{0,1},{1,0},{2,3},{3,2},{4,5},{5,4},{6,7},{7,6},{8,9},{9,8},{10,11... | collective-permute-start | bytes 2752520 | tf_op jit(solution)/shard_map/ppermute | solution.py:765
  103.0 2.0 %collective-permute-start.22 = (bf16[4,4,16,1024]{3,2,1,0:T(8,128)(2,1)S(1)}, bf16[4,4,16,1024]{3,2,1,0:T(8,128)(2,1)S(1)}, u32[]{:S(2)}, u32[]{:S(2)}) collective-permute-start(bf16[4,4,16,1024]{3,2,1,0:T(8,128)(2,1)S(1)} %get-tuple-element.154), channel_id=1, source_target_pairs={{0,1},{1,0},{2,3},{3,2},{4,5},{5,4},{6,7},{7,6},{8,9},{9,8},{10,11... | collective-permute-start | bytes 1572872 | tf_op jit(solution)/shard_map/ppermute | solution.py:765
  105.4 18.0 %collective-permute-start.23 = (bf16[4,16,2816]{2,1,0:T(8,128)(2,1)S(1)}, bf16[4,16,2816]{2,1,0:T(8,128)(2,1)S(1)}, u32[]{:S(2)}, u32[]{:S(2)}) collective-permute-start(bf16[4,16,2816]{2,1,0:T(8,128)(2,1)S(1)} %pad_maximum_fusion.1), channel_id=1, source_target_pairs={{0,2},{2,0},{4,6},{6,4},{8,10},{10,8},{12,14},{14,12},{16,18},{18,... | collective-permute-start | bytes 1081352 | tf_op jit(solution)/shard_map/ppermute | solution.py:765
  107.1 18.0 %collective-permute-start.24 = (bf16[4,16,2816]{2,1,0:T(8,128)(2,1)S(1)}, bf16[4,16,2816]{2,1,0:T(8,128)(2,1)S(1)}, u32[]{:S(2)}, u32[]{:S(2)}) collective-permute-start(bf16[4,16,2816]{2,1,0:T(8,128)(2,1)S(1)} %pad_maximum_fusion.2), channel_id=1, source_target_pairs={{0,4},{2,6},{4,0},{6,2},{8,12},{10,14},{12,8},{14,10},{16,20},{18,... | collective-permute-start | bytes 1081352 | tf_op jit(solution)/shard_map/ppermute | solution.py:765
  108.7 16.4 %collective-permute-start.25 = (bf16[4,16,2816]{2,1,0:T(8,128)(2,1)S(1)}, bf16[4,16,2816]{2,1,0:T(8,128)(2,1)S(1)}, u32[]{:S(2)}, u32[]{:S(2)}) collective-permute-start(bf16[4,16,2816]{2,1,0:T(8,128)(2,1)S(1)} %pad_maximum_fusion.3), channel_id=1, source_target_pairs={{0,6},{2,4},{4,2},{6,0},{8,14},{10,12},{12,10},{14,8},{16,22},{18,... | collective-permute-start | bytes 1081352 | tf_op jit(solution)/shard_map/ppermute | solution.py:765
  123.3 3.8 %collective-permute-start.26 = (bf16[4,4,16,1024]{3,2,1,0:T(8,128)(2,1)S(1)}, bf16[4,4,16,1024]{3,2,1,0:T(8,128)(2,1)S(1)}, u32[]{:S(2)}, u32[]{:S(2)}) collective-permute-start(bf16[4,4,16,1024]{3,2,1,0:T(8,128)(2,1)S(1)} %get-tuple-element.171), channel_id=1, source_target_pairs={{0,1},{1,0},{2,3},{3,2},{4,5},{5,4},{6,7},{7,6},{8,9},{9,8},{10,11... | collective-permute-start | bytes 1572872 | tf_op jit(solution)/shard_map/ppermute | solution.py:765
  125.3 15.3 %collective-permute-start.35 = (bf16[16,2816]{1,0:T(8,128)(2,1)S(1)}, bf16[16,2816]{1,0:T(8,128)(2,1)S(1)}, u32[]{:S(2)}, u32[]{:S(2)}) collective-permute-start(bf16[16,2816]{1,0:T(8,128)(2,1)S(1)} %get-tuple-element.225), channel_id=1, source_target_pairs={{0,24},{2,26},{4,28},{6,30},{8,16},{10,18},{12,20},{14,22},{16,8},... | collective-permute-start | bytes 270344 | tf_op jit(solution)/shard_map/ppermute | solution.py:765
  126.7 14.2 %collective-permute-start.34 = (bf16[16,2816]{1,0:T(8,128)(2,1)S(1)}, bf16[16,2816]{1,0:T(8,128)(2,1)S(1)}, u32[]{:S(2)}, u32[]{:S(2)}) collective-permute-start(bf16[16,2816]{1,0:T(8,128)(2,1)S(1)} %get-tuple-element.226), channel_id=1, source_target_pairs={{0,16},{2,18},{4,20},{6,22},{8,24},{10,26},{12,28},{14,30},{16,0},... | collective-permute-start | bytes 270344 | tf_op jit(solution)/shard_map/ppermute | solution.py:765
  127.3 6.1 %collective-permute-start.27 = (bf16[4,16,1024]{2,1,0:T(8,128)(2,1)S(1)}, bf16[4,16,1024]{2,1,0:T(8,128)(2,1)S(1)}, u32[]{:S(2)}, u32[]{:S(2)}) collective-permute-start(bf16[4,16,1024]{2,1,0:T(8,128)(2,1)S(1)} %get-tuple-element.218), channel_id=1, source_target_pairs={{0,2},{2,0},{4,6},{6,4},{8,10},{10,8},{12,14},{14,12},{16,18},{18,... | collective-permute-start | bytes 393224 | tf_op jit(solution)/shard_map/ppermute | solution.py:765
  128.5 7.4 %collective-permute-start.29 = (bf16[4,16,1024]{2,1,0:T(8,128)(2,1)S(1)}, bf16[4,16,1024]{2,1,0:T(8,128)(2,1)S(1)}, u32[]{:S(2)}, u32[]{:S(2)}) collective-permute-start(bf16[4,16,1024]{2,1,0:T(8,128)(2,1)S(1)} %get-tuple-element.219), channel_id=1, source_target_pairs={{0,6},{2,4},{4,2},{6,0},{8,14},{10,12},{12,10},{14,8},{16,22},{18,... | collective-permute-start | bytes 393224 | tf_op jit(solution)/shard_map/ppermute | solution.py:765
  130.3 6.1 %collective-permute-start.28 = (bf16[4,16,1024]{2,1,0:T(8,128)(2,1)S(1)}, bf16[4,16,1024]{2,1,0:T(8,128)(2,1)S(1)}, u32[]{:S(2)}, u32[]{:S(2)}) collective-permute-start(bf16[4,16,1024]{2,1,0:T(8,128)(2,1)S(1)} %get-tuple-element.220), channel_id=1, source_target_pairs={{0,4},{2,6},{4,0},{6,2},{8,12},{10,14},{12,8},{14,10},{16,20},{18,... | collective-permute-start | bytes 393224 | tf_op jit(solution)/shard_map/ppermute | solution.py:765
  133.3 7.6 %collective-permute-start.33 = (bf16[16,2816]{1,0:T(8,128)(2,1)S(1)}, bf16[16,2816]{1,0:T(8,128)(2,1)S(1)}, u32[]{:S(2)}, u32[]{:S(2)}) collective-permute-start(bf16[16,2816]{1,0:T(8,128)(2,1)S(1)} %get-tuple-element.227), channel_id=1, source_target_pairs={{0,8},{2,10},{4,12},{6,14},{8,0},{10,2},{12,4},{14,6},{16,24},{18,... | collective-permute-start | bytes 270344 | tf_op jit(solution)/shard_map/ppermute | solution.py:765
  136.5 5.8 %collective-permute-start.32 = (bf16[16,1024]{1,0:T(8,128)(2,1)S(1)}, bf16[16,1024]{1,0:T(8,128)(2,1)S(1)}, u32[]{:S(2)}, u32[]{:S(2)}) collective-permute-start(bf16[16,1024]{1,0:T(8,128)(2,1)S(1)} %get-tuple-element.228), channel_id=1, source_target_pairs={{0,24},{2,26},{4,28},{6,30},{8,16},{10,18},{12,20},{14,22},{16,8},... | collective-permute-start | bytes 98312 | tf_op jit(solution)/shard_map/ppermute | solution.py:765
  138.9 5.2 %collective-permute-start.31 = (bf16[16,1024]{1,0:T(8,128)(2,1)S(1)}, bf16[16,1024]{1,0:T(8,128)(2,1)S(1)}, u32[]{:S(2)}, u32[]{:S(2)}) collective-permute-start(bf16[16,1024]{1,0:T(8,128)(2,1)S(1)} %get-tuple-element.229), channel_id=1, source_target_pairs={{0,16},{2,18},{4,20},{6,22},{8,24},{10,26},{12,28},{14,30},{16,0},... | collective-permute-start | bytes 98312 | tf_op jit(solution)/shard_map/ppermute | solution.py:765
  140.7 3.9 %collective-permute-start.30 = (bf16[16,1024]{1,0:T(8,128)(2,1)S(1)}, bf16[16,1024]{1,0:T(8,128)(2,1)S(1)}, u32[]{:S(2)}, u32[]{:S(2)}) collective-permute-start(bf16[16,1024]{1,0:T(8,128)(2,1)S(1)} %get-tuple-element.230), channel_id=1, source_target_pairs={{0,8},{2,10},{4,12},{6,14},{8,0},{10,2},{12,4},{14,6},{16,24},{18,... | collective-permute-start | bytes 98312 | tf_op jit(solution)/shard_map/ppermute | solution.py:765
  157.8 1.6 collective-permute-start.37
  157.8 1.6 collective-permute-start.36

commit v7 on v6

--- a/solution.py
+++ b/solution.py
@@ -190,13 +190,13 @@
 
 def layer_forward(x_ref, w_ref, vec, bias, kept, work):
     qt_ref, kv_ref, p0, p1, p2, r_ref, ot_ref, o_ref, m_ref, h_ref, gp_ref, a_ref, c_ref = kept
-    qst_ref, vt_ref, mask_ref, wqt_ref, u_ref, y_ref = work
+    qst_ref, vt_ref, mask_ref, wqt_ref, long_ref, u_ref, y_ref = work
     for rows in tiles(SEQ, TILE):
-        a_ref[rows] = (normalise(x_ref[rows])[0] * vec[0:1] + vec[1:2]).astype(BF16)
-    a_ref[SEQ:KEYS] = jnp.zeros((KEYS - SEQ, D), BF16)
-    kv_ref[0:SEQ] = dot_nn(a_ref[0:SEQ], w_ref[:, 256:768]).astype(BF16)
+        normed16 = (normalise(x_ref[rows])[0] * vec[0:1] + vec[1:2]).astype(BF16)
+        a_ref[rows], long_ref[rows] = normed16, normed16
+    kv_ref[0:SEQ] = dot_nn(long_ref[0:SEQ], w_ref[:, 256:768]).astype(BF16)
     kv_ref[SEQ:KEYS] = jnp.zeros((KEYS - SEQ, 512), BF16)
-    qt_ref[...] = dot_nt(wqt_ref[...], a_ref[...]).astype(BF16)
+    qt_ref[...] = dot_nt(wqt_ref[...], long_ref[...]).astype(BF16)
     spread_heads(qt_ref, qst_ref)
     turned = jnp.transpose(kv_ref[:, 256:512])
     for h in range(HEADS):
@@ -234,14 +234,12 @@
     g_ref[:, column : column + right.shape[1]] += dot_tn(left, right)
 
 
-def ff_backward(grad_ref, grad16_ref, w_ref, w_up, w_down, vec, kept, g_ref, g_up, g_down, v_ref, v_row, bias_row, work, mid_ref, mid16_ref):
-    m_ref, h_ref, gp_ref, c_ref = kept
+def ff_backward(grad_ref, grad16_ref, w_ref, w_up, w_down, vec, kept, v_ref, v_row, bias_row, work, mid_ref, mid16_refs):
+    m_ref, gp_ref = kept
     du_ref, ones_ref, u_ref, y_ref = work
     u_ref[...] = dot_nn(grad16_ref[...], w_ref[:, w_down : w_down + FF])
     for rows in tiles(SEQ, TILE):
         du_ref[rows] = u_ref[rows].astype(BF16) * gp_ref[rows]
-    add_gradient(g_ref, g_down, grad16_ref[...], h_ref[...])
-    add_gradient(g_ref, g_up, c_ref[...], du_ref[...])
     bias_grad = dot_nn(ones_ref[...], du_ref[...])
     for chunk in range(4):
         v_ref[bias_row + chunk, 0:1] += bias_grad[0:1, 256 * chunk : 256 * chunk + 256]
@@ -252,7 +250,7 @@
         grad = y_ref[rows]
         mid = grad_ref[rows] + normalise_back(grad, xhat, scale, vec[3:4])
         mid_ref[rows] = mid
-        if mid16_ref is not None:
+        for mid16_ref in mid16_refs:
             mid16_ref[rows] = mid.astype(BF16)
         for i, a in enumerate((mid, grad * xhat, grad)):
             totals[i] = plus(totals[i], fold(a))
@@ -260,10 +258,9 @@
         v_ref[v_row + 2 + i] += totals[i]
 
 
-def attention_backward(mid_ref, mid16_ref, w_ref, vec, kept, g_ref, v_ref, v_row, work, out_ref):
-    x_ref, qt_ref, kv_ref, p0, p1, p2, r_ref, ot_ref, o_ref, a_ref = kept
+def attention_backward(mid_ref, mid16_ref, w_ref, vec, kept, v_ref, v_row, work, out_ref):
+    x_ref, qt_ref, kv_ref, p0, p1, p2, r_ref, ot_ref = kept
     dost_ref, qst_ref, kt_ref, dst_ref, dqt_ref, dkv_ref, dqkv_ref, proj_ref, y_ref = work
-    add_gradient(g_ref, COL_PROJ, mid16_ref[0:SEQ], o_ref[...])
     grad_o = dot_nt(proj_ref[...], mid16_ref[...]).astype(BF16).astype(F32)
     kt_ref[...] = jnp.transpose(kv_ref[:, 0:256])
     deltas = []
@@ -292,7 +289,6 @@
             dkv_ref[first:seen, at : at + 256] = out[first:]
     dqkv_ref[:, 0:256] = jnp.transpose(dqt_ref[...])[0:SEQ]
     dqkv_ref[:, 256:768] = dkv_ref[0:SEQ].astype(BF16)
-    add_gradient(g_ref, COL_QKV, a_ref[0:SEQ], dqkv_ref[...])
     y_ref[...] = dot_nt(dqkv_ref[...], w_ref[:, COL_QKV : COL_QKV + 768])
     totals = [None] * 2
     for rows in tiles(SEQ, TILE):
@@ -368,7 +364,8 @@
 
 
 def start_forward(work, w_ref):
-    qst_ref, vt_ref, mask_ref, wqt_ref, u_ref, y_ref = work
+    qst_ref, vt_ref, mask_ref, wqt_ref, long_ref, u_ref, y_ref = work
+    long_ref[SEQ:KEYS] = jnp.zeros((KEYS - SEQ, D), BF16)
     qst_ref[...] = jnp.zeros(qst_ref.shape, BF16)
     vt_ref[...] = jnp.ones(vt_ref.shape, BF16)
     mask_ref[...] = causal_mask()
@@ -382,7 +379,7 @@
     w_attention, w_ff, side_out, next_ref, hits_ref, x_ref = refs[13:19]
     kept = [ref.at[0] for ref in refs[19:32]]
     w_ref = refs[32]
-    work = refs[33:39]
+    work = refs[33:40]
 
     @pl.when(pl.program_id(0) == 0)
     def _():
@@ -398,7 +395,7 @@
     vec = vec_ref[0:6]
     layer_forward(x_ref.at[0], w_ref, vec, bias, kept, work)
     for rows in tiles(SEQ, TILE):
-        next_ref[0, rows] = kept[8][rows] + (work[5][rows] + vec[5:6])
+        next_ref[0, rows] = kept[8][rows] + (work[6][rows] + vec[5:6])
 
 
 def codebook_losses(logits, meta):
@@ -443,14 +440,14 @@
     grad_ref, keep_ref, send_ref, v_out, scalar_ref = refs[16:21]
     refs = refs[1:]
     w_ref, g_ref, v_ref = refs[20:23]
-    kept = refs[23:36]
-    m_ref, h_ref, gp_ref, a_ref, c_ref = kept[8:13]
-    forward_work = refs[36:42]
-    u_ref, y_ref = forward_work[4:6]
-    backward_work = refs[42:48]
-    proj_ref = refs[48]
-    du_ref, ones_ref, up_ref, up16_ref, mid_ref, mid16_ref = refs[49:55]
-    last_ref, final_ref, logit_ref, dlogit_ref, pick_ref, put_ref = refs[55:61]
+    kept = list(refs[23:36])
+    forward_work = refs[36:43]
+    u_ref, y_ref = forward_work[5:7]
+    backward_work = list(refs[43:49])
+    proj_ref = refs[49]
+    du_all, ones_ref, up_ref, up16_all, mid_ref, mid16_ref = refs[50:56]
+    last_ref, final_all, logit_ref, dlogit_all, pick_ref, put_ref, mid16_all = refs[56:63]
+    o_all, h_all, a_all, c_all, dqkv_all = kept[7], kept[9], kept[11], kept[12], backward_work[5]
     dost_ref = backward_work[0]
     step = pl.program_id(0)
 
@@ -469,6 +466,13 @@
         pick_ref[...] = frame_ends((SIDE_ROWS, SEQ), 0)
         put_ref[...] = frame_ends((SEQ, SIDE_ROWS), 1)
 
+    here = pl.ds(pl.multiple_of((step & 1) * SEQ, 32), SEQ)
+    for i in (7, 9, 11, 12):
+        kept[i] = kept[i].at[here]
+    m_ref, h_ref, gp_ref = kept[8:11]
+    backward_work[5] = dqkv_all.at[here]
+    du_ref, up16_ref, pair16_ref = du_all.at[here], up16_all.at[here], mid16_all.at[here]
+    final_ref, dlogit_ref = final_all.at[here], dlogit_all.at[here]
     x_ref = in_ref.at[0]
     vec = vec_ref[6:12]
     bias = own_bias(place, bias_ref[1:2], bias_other[1:2])
@@ -501,7 +505,6 @@
         jnp.where(scalar_lane == 0, loss, jnp.where(scalar_lane == 1, valid, 0.0)),
         0.0,
     )
-    add_gradient(g_ref, COL_HEAD, final_ref[...], dlogit_ref[...])
     y_ref[...] = dot_nt(dlogit_ref[...], w_ref[:, cols_head])
     totals = [None] * 3
     for rows in tiles(SEQ, TILE):
@@ -521,29 +524,33 @@
         COL_UP,
         COL_DOWN,
         vec,
-        (m_ref, h_ref, gp_ref, c_ref),
-        g_ref,
-        COL_UP,
-        COL_DOWN,
+        (m_ref, gp_ref),
         v_ref,
         6,
         SMALL_BIAS + 4,
         (du_ref, ones_ref, u_ref, y_ref),
         mid_ref,
-        mid16_ref,
+        (mid16_ref, pair16_ref),
     )
     attention_backward(
         mid_ref,
         mid16_ref,
         w_ref,
         vec,
-        (x_ref,) + tuple(kept[0:8]) + (a_ref,),
-        g_ref,
+        (x_ref,) + tuple(kept[0:7]),
         v_ref,
         6,
         (dost_ref, forward_work[0]) + tuple(backward_work[1:]) + (proj_ref, y_ref),
         grad_ref.at[0],
     )
+
+    @pl.when(step & 1 == 1)
+    def _():
+        add_gradient(g_ref, COL_QKV, a_all[...], dqkv_all[...])
+        add_gradient(g_ref, COL_PROJ, mid16_all[...], o_all[...])
+        add_gradient(g_ref, COL_UP, c_all[...], du_all[...])
+        add_gradient(g_ref, COL_DOWN, up16_all[...], h_all[...])
+        add_gradient(g_ref, COL_HEAD, final_all[...], dlogit_all[...])
 
     @pl.when(step == pl.num_programs(0) - 1)
     def _():
@@ -555,21 +562,18 @@
 
 
 def ff_backward_kernel(fast, *refs):
-    refs = (places(fast),) + refs
-    place, vec_ref, w_ref, grad_ref, v_in = refs[0:5]
-    kept = [ref.at[0] for ref in refs[5:9]]
-    mid_ref, keep_ref, send_ref, v_out = refs[9:13]
-    g_ref, v_ref, grad16_ref = refs[13:16]
-    work = refs[16:20]
-    ones_ref = work[1]
+    vec_ref, w_ref, grad_ref, v_in, m_ref, gp_ref, h_all, c_all = refs[0:8]
+    mid_ref, keep_ref, send_ref, v_out = refs[8:12]
+    g_ref, v_ref, grad16_all, du_all, ones_ref, u_ref, y_ref = refs[12:19]
     step = pl.program_id(0)
 
     @pl.when(step == 0)
     def _():
-        g_ref[...] = jnp.zeros(g_ref.shape, F32)
         v_ref[...] = v_in[...]
         ones_ref[...] = jnp.ones(ones_ref.shape, BF16)
 
+    here = pl.ds(pl.multiple_of(step * SEQ, 32), SEQ)
+    grad16_ref = grad16_all.at[here]
     total = None
     for rows in tiles(SEQ, TILE):
         grad = grad_ref[0, rows]
@@ -583,60 +587,72 @@
         GRAD_UP,
         GRAD_DOWN,
         vec_ref[0:6],
-        kept,
-        g_ref,
-        GRAD_UP,
-        GRAD_DOWN,
+        (m_ref.at[0], gp_ref.at[0]),
         v_ref,
         0,
         SMALL_BIAS,
-        work,
+        (du_all.at[here], ones_ref, u_ref, y_ref),
         mid_ref.at[0],
-        None,
+        (),
     )
 
     @pl.when(step == pl.num_programs(0) - 1)
     def _():
-        disperse(g_ref, place, keep_ref, send_ref, HALF_GRAD_FF, False)
+        g_ref[:, GRAD_UP : GRAD_UP + FF] = dot_tn(c_all[...], du_all[...])
+        g_ref[:, GRAD_DOWN : GRAD_DOWN + FF] = dot_tn(grad16_all[...], h_all[...])
+        disperse(g_ref, places(fast), keep_ref, send_ref, HALF_GRAD_FF, False)
         v_out[...] = v_ref[...]
 
 
 def attention_backward_kernel(fast, *refs):
-    refs = (places(fast),) + refs
-    place, vec_ref, w_ref, mid_ref, hits_ref, v_in = refs[0:6]
-    kept = [ref.at[0] for ref in refs[6:16]]
-    keep_ref, send_ref, v_out = refs[17:20]
-    g_ref, v_ref, mid16_ref, out16_ref = refs[20:24]
-    work = refs[24:33]
-    dost_ref, qst_ref, proj_ref = work[0], work[1], work[7]
+    vec_ref, w_ref, mid_ref, v_in = refs[0:4]
+    kept = [ref.at[0] for ref in refs[4:12]]
+    o_all, a_all, hits_all = refs[12:15]
+    keep_ref, send_ref, v_out = refs[16:19]
+    g_ref, v_ref, mid16_ref, mid16_all, out16_all, dqkv_all = refs[19:25]
+    work = list(refs[25:33])
+    dost_ref, qst_ref, proj_ref = work[0], work[1], work[6]
     step = pl.program_id(0)
 
     @pl.when(step == 0)
     def _():
-        g_ref[...] = jnp.zeros(g_ref.shape, F32)
         v_ref[...] = v_in[...]
         dost_ref[...] = jnp.zeros(dost_ref.shape, BF16)
         qst_ref[...] = jnp.zeros(qst_ref.shape, BF16)
         proj_ref[...] = jnp.transpose(w_ref[:, COL_PROJ : COL_PROJ + 256])
         mid16_ref[SEQ:KEYS] = jnp.zeros((KEYS - SEQ, D), BF16)
 
+    here = pl.ds(pl.multiple_of(step * SEQ, 32), SEQ)
+    all16_ref = mid16_all.at[here]
     spread_heads(kept[1], qst_ref)
     for rows in tiles(SEQ, TILE):
-        mid16_ref[rows] = mid_ref[0, rows].astype(BF16)
+        mid16 = mid_ref[0, rows].astype(BF16)
+        mid16_ref[rows], all16_ref[rows] = mid16, mid16
+    work.insert(6, dqkv_all.at[here])
     attention_backward(
-        mid_ref.at[0], mid16_ref, w_ref, vec_ref[0:6], kept, g_ref, v_ref, 0, work, out16_ref
-    )
-    add_gradient(g_ref, GRAD_TABLE, out16_ref[...], hits_ref[0])
+        mid_ref.at[0],
+        mid16_ref,
+        w_ref,
+        vec_ref[0:6],
+        kept,
+        v_ref,
+        0,
+        work,
+        out16_all.at[here],
+    )
 
     @pl.when(step == pl.num_programs(0) - 1)
     def _():
+        g_ref[:, COL_QKV : COL_QKV + 768] = dot_tn(a_all[...], dqkv_all[...])
+        g_ref[:, COL_PROJ : COL_PROJ + 256] = dot_tn(mid16_all[...], o_all[...])
+        g_ref[:, GRAD_TABLE : GRAD_TABLE + ROWS] = dot_tn(out16_all[...], hits_all[...])
         small = jnp.sum(v_ref[...], axis=1)
         v_out[...] = small
         for block in range(16):
             quarter = small[8 * (block // 4) : 8 * (block // 4) + 8]
             g_ref[16 * block : 16 * block + 8, GRAD_SMALL:] = quarter[:, 0:128]
             g_ref[16 * block + 8 : 16 * block + 16, GRAD_SMALL:] = quarter[:, 128:256]
-        disperse(g_ref, place, keep_ref, send_ref, HALF_GRAD_REST)
+        disperse(g_ref, places(fast), keep_ref, send_ref, HALF_GRAD_REST)
 
 
 def pack_layer(attn, proj, up, down, layer, out):
@@ -845,9 +861,9 @@
     "pack": 58,
     "prepare": 58,
     "first_forward": 24,
-    "middle": 27,
-    "ff_backward": 17,
-    "attention_backward": 20,
+    "middle": 31,
+    "ff_backward": 24,
+    "attention_backward": 26,
     "finish": 58,
     "adam": 58,
 }
@@ -882,7 +898,7 @@
     ((SEQ, D), F32),
     ((SEQ, FF), BF16),
     ((SEQ, FF), BF16),
-    ((KEYS, D), BF16),
+    ((SEQ, D), BF16),
     ((SEQ, D), BF16),
 )
 FORWARD_WORK = [
@@ -890,6 +906,7 @@
     pltpu.VMEM((HEADS * VALUE_ROWS, KEYS), BF16),
     pltpu.VMEM((BLOCK, QUERIES), F32),
     pltpu.VMEM((D, D), BF16),
+    pltpu.VMEM((KEYS, D), BF16),
     pltpu.VMEM((SEQ, FF), F32),
     pltpu.VMEM((SEQ, D), F32),
 ]
@@ -976,12 +993,7 @@
     other_bias = swap(up_bias, "narrow", 1)
     column = swap_column(piece_first, n_high)
 
-    column, other_bias = lax.optimization_barrier((column, other_bias))
-    first_column = jnp.stack(column)
-    beside, above = swap(first_column, "wide", 1), swap(first_column, "wide", 2)
-
     count = tokens.shape[0] // lax.axis_size("narrow")
-    ids, first_column = lax.optimization_barrier((flat(tokens), first_column))
     meta, frame_meta = call(
         functools.partial(prepare_kernel, fast),
         None,
@@ -992,14 +1004,15 @@
         10**6,
         10**6,
         "prepare",
-    )(game_ids, ids, actions, valid_steps, rewards, end_flags)
-    beside, first_column, meta = lax.optimization_barrier((beside, first_column, meta))
-    above, piece_second = lax.optimization_barrier((above, piece_second))
-    across = swap(first_column, "wide", 3)
+    )(game_ids, flat(tokens), actions, valid_steps, rewards, end_flags)
+    column, other_bias, meta = lax.optimization_barrier((column, other_bias, meta))
+    first_column = jnp.stack(column)
+    first_mine = gather_plane(first_column)
+    own, piece_second = lax.optimization_barrier((swap(first_column, "narrow", 1), piece_second))
     second_column = jnp.stack(swap_column(piece_second, n_high))
-    second_column, across = lax.optimization_barrier((second_column, across))
-    first_mine = [first_column, beside, above, across]
-    first_other = gather_cores(first_mine)
+    second_column, across = lax.optimization_barrier((second_column, first_mine[3]))
+    first_mine = first_mine[0:3] + [across]
+    first_other = [own] + gather_cores(first_mine[1:])
     second_mine = gather_plane(second_column)
     first_parts = in_blocks(first_mine, wide) + in_blocks(first_other, wide)
 
@@ -1057,24 +1070,29 @@
             pltpu.VMEM((D, COL_SECOND + 128), F32),
             small_scratch,
         ]
-        + [pltpu.VMEM(shape, dtype) for shape, dtype in KEPT]
+        + [pltpu.VMEM(shape, dtype) for shape, dtype in KEPT[0:7]]
+        + [pltpu.VMEM((2 * SEQ, D), BF16), pltpu.VMEM(*KEPT[8])]
+        + [pltpu.VMEM((2 * SEQ, FF), BF16), pltpu.VMEM(*KEPT[10])]
+        + [pltpu.VMEM((2 * SEQ, D), BF16)] * 2
         + FORWARD_WORK
         + BACKWARD_WORK[0:1]
-        + BACKWARD_WORK[2:]
+        + BACKWARD_WORK[2:6]
+        + [pltpu.VMEM((2 * SEQ, 768), BF16)]
         + [
             PROJ_WORK,
-            pltpu.VMEM((SEQ, FF), BF16),
+            pltpu.VMEM((2 * SEQ, FF), BF16),
             ONES_WORK,
             pltpu.VMEM((SEQ, D), F32),
-            pltpu.VMEM((SEQ, D), BF16),
+            pltpu.VMEM((2 * SEQ, D), BF16),
             pltpu.VMEM((SEQ, D), F32),
             pltpu.VMEM((KEYS, D), BF16),
             pltpu.VMEM((SEQ, D), F32),
-            pltpu.VMEM((SEQ, D), BF16),
+            pltpu.VMEM((2 * SEQ, D), BF16),
             pltpu.VMEM((SEQ, VOCAB), F32),
-            pltpu.VMEM((SEQ, VOCAB + 128), BF16),
+            pltpu.VMEM((2 * SEQ, VOCAB + 128), BF16),
             pltpu.VMEM((SIDE_ROWS, SEQ), BF16),
             pltpu.VMEM((SEQ, SIDE_ROWS), BF16),
+            pltpu.VMEM((2 * SEQ, D), BF16),
         ],
         15 * 10**9,
         20 * 10**6,
@@ -1087,19 +1105,23 @@
     )
     second_sums = add_cores(keep_second, send_second, wide, n_high)
 
-    kept_ff = (kept[8], kept[9], kept[10], kept[12])
+    def joined(a):
+        return a.reshape((count * a.shape[1],) + a.shape[2:])
+
+    joined_ff = [joined(kept[9]), joined(kept[12])]
     grad_mid, keep_ff, send_ff, small_grads = call(
         functools.partial(ff_backward_kernel, fast),
         (count,),
         [full_spec(vectors), w_ff_spec, row_spec((SEQ, D)), small_spec]
-        + [row_spec(a.shape[1:]) for a in kept_ff],
+        + [row_spec(a.shape[1:]) for a in (kept[8], kept[10])]
+        + [VMEM_SPEC] * 2,
         [row_spec((SEQ, D))] + [blocks(HALF_GRAD_COLS)] * 2 + [small_spec],
         [row_f32] + block_shapes(HALF_GRAD_COLS) + [small_shape],
         [
             pltpu.VMEM((D, 2048), F32),
             small_scratch,
-            pltpu.VMEM((SEQ, D), BF16),
-            pltpu.VMEM((SEQ, FF), BF16),
+            pltpu.VMEM((count * SEQ, D), BF16),
+            pltpu.VMEM((count * SEQ, FF), BF16),
             ONES_WORK,
             pltpu.VMEM((SEQ, FF), F32),
             pltpu.VMEM((SEQ, D), F32),
@@ -1107,27 +1129,38 @@
         4 * 10**9,
         10 * 10**6,
         "ff_backward",
-    )(*in_hbm([vectors]), w_ff, grad_stream, small_grads, *kept_ff)
+    )(*in_hbm([vectors]), w_ff, grad_stream, small_grads, kept[8], kept[10], *joined_ff)
     ff_sums = add_cores(keep_ff, send_ff, wide, n_high)
     other_sums = [jnp.concatenate(pair, axis=-1) for pair in zip(second_sums, ff_sums)]
     others_received = swap_plane(other_sums)
-    kept_attention = (stream_first,) + tuple(kept[0:8]) + (kept[11],)
+    kept_attention = (stream_first,) + tuple(kept[0:7])
+    joined_attention = [joined(kept[7]), joined(kept[11]), joined(hits)]
     keep_rest, send_rest, small_grads = call(
         functools.partial(attention_backward_kernel, fast),
         (count,),
-        [full_spec(vectors), w_attention_spec, row_spec((SEQ, D)), hits_spec, small_spec]
+        [full_spec(vectors), w_attention_spec, row_spec((SEQ, D)), small_spec]
         + [row_spec(a.shape[1:]) for a in kept_attention]
+        + [VMEM_SPEC] * 3
         + [ANY_SPEC],
         [blocks(HALF_GRAD_COLS)] * 2 + [pl.BlockSpec((SMALL_ROWS, D), lambda i: (0, 0))],
         block_shapes(HALF_GRAD_COLS) + [shaped((SMALL_ROWS, D), F32)],
-        [pltpu.VMEM((D, 2048), F32), small_scratch]
-        + [pltpu.VMEM((KEYS, D), BF16), pltpu.VMEM((SEQ, D), BF16)]
-        + BACKWARD_WORK
+        [pltpu.VMEM((D, 2048), F32), small_scratch, pltpu.VMEM((KEYS, D), BF16)]
+        + [pltpu.VMEM((count * SEQ, D), BF16)] * 2
+        + [pltpu.VMEM((count * SEQ, 768), BF16)]
+        + BACKWARD_WORK[0:6]
         + [PROJ_WORK, pltpu.VMEM((SEQ, D), F32)],
         6 * 10**9,
         20 * 10**6,
         "attention_backward",
-    )(*in_hbm([vectors]), w_attention, grad_mid, hits, small_grads, *kept_attention, other_sums[0])
+    )(
+        *in_hbm([vectors]),
+        w_attention,
+        grad_mid,
+        small_grads,
+        *kept_attention,
+        *joined_attention,
+        other_sums[0],
+    )
     others_received, keep_rest = lax.optimization_barrier((others_received, keep_rest))
     rest_sums = add_cores(keep_rest, send_rest, wide, n_high)
     rest_received = swap_plane(rest_sums)

time: 163 us -> 159 us (0.975)
  waiting for transfers between devices: 26.1 us -> 22.7 us
    ppermute x38, waiting for transfers between devices: 26.1 us -> 22.7 us  [swap(): return lax.ppermute(a, axis, [(i, i ^ distance) for i in range(size)])]
    pallas_call x1, Pallas kernels: 14.2 us -> 12.5 us  [per_device(): call(functools.partial(attention_backward_kernel, fast), (count,), [full_...]
  transfers between devices with their start and end apart: 38 -> 38, of which waited for: 16 -> 15; matrix products, arithmetic and copies ran while one was open for 1% -> 1% of each run, Pallas kernels for 25% -> 25%
where the time goes in v7:
time: 159 us
  Pallas kernels  81.5 us (51%)
  starting transfers between devices  37.7 us (24%)
  waiting for transfers between devices  22.7 us (14%)
  blocking collectives  12.9 us (8%)
  other arithmetic  2.6 us (2%)
    ppermute x38, starting transfers between devices, swap(): return lax.ppermute(a, axis, [(i, i ^ distance) for i in range(size)])  37.7 us
    pallas_call x1, Pallas kernels, per_device(): call(functools.partial(middle_kernel, fast), (count,), [meta_spec, row_sp...  36.5 us
    ppermute x38, waiting for transfers between devices, swap(): return lax.ppermute(a, axis, [(i, i ^ distance) for i in range(size)])  22.7 us
    pallas_call x1, Pallas kernels, per_device(): call(functools.partial(first_forward_kernel, fast), (count,), [meta_spec]...  16.2 us
    all_to_all x1, blocking collectives, per_device(): gathered = lax.all_to_all(small, 'wide', 0, 0)  12.9 us
    pallas_call x1, Pallas kernels, per_device(): call(functools.partial(attention_backward_kernel, fast), (count,), [full_...  12.5 us
    pallas_call x1, Pallas kernels, per_device(): call(functools.partial(ff_backward_kernel, fast), (count,), [full_spec(ve...  7.31 us
    pallas_call x1, Pallas kernels, per_device(): call(functools.partial(prepare_kernel, fast), None, [SMEM_SPEC] + [VMEM_S...  3.29 us
  transfers between devices with their start and end apart: 38, of which 15 were waited for; matrix products, arithmetic and copies ran while one was open for 1% of the time, Pallas kernels for 25%

profile of v7, /device:TPU:0, one launch (start us, length us, event | category | flops | bytes accessed | tf_op | source)
XLA Modules:
  0.0 158.6 jit_solution(7061446495031248945)
XLA Ops:
  0.7 1.7 %pack.1 = (bf16[16,2048]{1,0:T(8,128)(2,1)}, bf16[16,1792]{1,0:T(8,128)(2,1)}) custom-call(f32[16,896]{1,0:T(8,128)} %bitcast.93, f32[2,3,16,128]{3,2,1,0:T(8,128)} %refs_3_.3, f32[2,16,128]{2,1,0:T(8,128)} %bitcast.95, f32[2,16,512]{2,1,0:T(8,128)} %refs_9_.1, f32[2,16,512]{2,1,0:T(8,128)} %bitcast.91, f32[16,256]{1,0:T(8,128)} %refs_21_.1, f32[5,16]{1,0:T(8,128)} %bitcast.112), custom_call_target="tpu_custom_call" | custom-call | flops 1000000 | bytes 1000000 | tf_op jit(solution)/shard_map/pack/pallas_call | solution.py:982
  2.4 5.0 %collective-permute-start.2 = (bf16[16,2048]{1,0:T(8,128)(2,1)}, bf16[16,2048]{1,0:T(8,128)(2,1)S(1)}, u32[]{:S(2)}, u32[]{:S(2)}) collective-permute-start(bf16[16,2048]{1,0:T(8,128)(2,1)} %get-tuple-element.121), channel_id=1, source_target_pairs={{0,24},{2,26},{4,28},{6,30},{8,16},{10,18},{12,20},{14,22},{16,8},... | collective-permute-start | bytes 196616 | tf_op jit(solution)/shard_map/ppermute | solution.py:781
  7.4 0.6 collective-permute-start
  8.0 3.3 %prepare.1 = (s32[4,352,128]{2,1,0:T(8,128)}, s32[4,32,128]{2,1,0:T(8,128)}) custom-call(s32[8]{0:T(128)} %games_ref.1, s32[8,16,20]{2,1,0:T(8,128)} %bitcast.99, s32[8,20]{1,0:T(8,128)} %actions.1, s32[8,20]{1,0:T(8,128)} %valid.1, s32[8,20]{1,0:T(8,128)} %rewards.1, s32[8,20]{1,0:T(8,128)} %ends.1), custom_call_target="tpu_custom_call" | custom-call | flops 1000000 | bytes 1000000 | tf_op jit(solution)/shard_map/prepare/pallas_call | solution.py:997
  11.3 1.9 %collective-permute-done.1 = bf16[16,2048]{1,0:T(8,128)(2,1)S(1)} collective-permute-done((bf16[16,2048]{1,0:T(8,128)(2,1)}, bf16[16,2048]{1,0:T(8,128)(2,1)S(1)}, u32[]{:S(2)}, u32[]{:S(2)}) %collective-permute-start.1) | collective-permute-done | bytes 65568 | tf_op jit(solution)/shard_map/ppermute | solution.py:781
  13.3 0.9 pad_maximum_fusion.4.refs_4_
  14.2 1.6 collective-permute-start.13
  15.8 1.5 collective-permute-start.12
  17.3 2.6 %collective-permute-start.7 = (bf16[16,1792]{1,0:T(8,128)(2,1)}, bf16[16,1792]{1,0:T(8,128)(2,1)S(1)}, u32[]{:S(2)}, u32[]{:S(2)}) collective-permute-start(bf16[16,1792]{1,0:T(8,128)(2,1)} %get-tuple-element.126), channel_id=1, source_target_pairs={{0,24},{2,26},{4,28},{6,30},{8,16},{10,18},{12,20},{14,22},{16,8},... | collective-permute-start | bytes 172040 | tf_op jit(solution)/shard_map/ppermute | solution.py:781
  19.9 1.7 %collective-permute-start.5 = (bf16[16,1792]{1,0:T(8,128)(2,1)}, bf16[16,1792]{1,0:T(8,128)(2,1)S(1)}, u32[]{:S(2)}, u32[]{:S(2)}) collective-permute-start(bf16[16,1792]{1,0:T(8,128)(2,1)} %get-tuple-element.126), channel_id=1, source_target_pairs={{0,8},{2,10},{4,12},{6,14},{8,0},{10,2},{12,4},{14,6},{16,24},{18,... | collective-permute-start | bytes 172040 | tf_op jit(solution)/shard_map/ppermute | solution.py:781
  21.7 1.3 collective-permute-done.13.refs_6_
  22.9 2.4 %collective-permute-start.8 = (bf16[4,16,2048]{2,1,0:T(8,128)(2,1)S(1)}, bf16[4,16,2048]{2,1,0:T(8,128)(2,1)S(1)}, u32[]{:S(2)}, u32[]{:S(2)}) collective-permute-start(bf16[4,16,2048]{2,1,0:T(8,128)(2,1)S(1)} %pad_maximum_fusion.4.refs_4_), channel_id=1, source_target_pairs={{0,6},{2,4},{4,2},{6,0},{8,14},{10,12},{12,10},{14,8},{16,22},{18,... | collective-permute-start | bytes 786440 | tf_op jit(solution)/shard_map/ppermute | solution.py:781
  25.4 0.5 collective-permute-start.14
  25.9 0.9 pad_maximum_fusion.5.refs_7_
  26.8 4.9 %collective-permute-done.8.refs_7_ = bf16[4,16,2048]{2,1,0:T(8,128)(2,1)S(1)} collective-permute-done((bf16[4,16,2048]{2,1,0:T(8,128)(2,1)S(1)}, bf16[4,16,2048]{2,1,0:T(8,128)(2,1)S(1)}, u32[]{:S(2)}, u32[]{:S(2)}) %collective-permute-start.8) | collective-permute-done | bytes 262176 | tf_op jit(solution)/shard_map/ppermute | solution.py:781
  31.7 0.5 collective-permute-start.17
  32.2 2.4 %collective-permute-start.11 = (bf16[4,16,1792]{2,1,0:T(8,128)(2,1)S(1)}, bf16[4,16,1792]{2,1,0:T(8,128)(2,1)S(1)}, u32[]{:S(2)}, u32[]{:S(2)}) collective-permute-start(bf16[4,16,1792]{2,1,0:T(8,128)(2,1)S(1)} %pad_maximum_fusion.5.refs_7_), channel_id=1, source_target_pairs={{0,6},{2,4},{4,2},{6,0},{8,14},{10,12},{12,10},{14,8},{16,22},{18,... | collective-permute-start | bytes 688136 | tf_op jit(solution)/shard_map/ppermute | solution.py:781
  34.7 0.5 collective-permute-start.10
  35.2 0.5 collective-permute-start.9
  35.7 16.2 %first_forward.1 = (bf16[256,1024]{1,0:T(8,128)(2,1)S(1)}, bf16[256,2048]{1,0:T(8,128)(2,1)S(1)}, bf16[256,128]{1,0:T(8,128)(2,1)S(1)}, f32[4,352,256]{2,1,0:T(8...) custom-call(s32[4,352,128]{2,1,0:T(8,128)} %get-tuple-element.118.re, ...), custom_call_target="tpu_custom_call" | custom-call | flops 4000000000 | bytes 20000000 | tf_op jit(solution)/shard_map/first_forward/pallas_call | solution.py:1028
  52.0 0.5 collective-permute-start.19
  52.6 0.9 collective-permute-done.18.refs_12_
  54.1 36.5 %middle.1 = (f32[4,352,256]{2,1,0:T(8,128)S(1)}, bf16[4,4,16,1792]{3,2,1,0:T(8,128)(2,1)S(1)}, bf16[4,4,16,1792]{3,2,1,0:T(8,128)(2,1)S(1)}, f32[32,8,256]{2,1,0:T(8,128)S(1)}, f32[8,128]{1,0:T(8,128)S(1)}) custom-call(s32[4,352,128]{2,1,0:T(8,128)} %get-tuple-element.118.refs_0_, s32[4,32,128]{2,1,0:T(8,128)} %get-tuple-element.119.refs_1_, ...), custom_call_target="tpu_custom_call" | custom-call | flops 15000000512 | bytes 20000000 | tf_op jit(solution)/shard_map/middle/pallas_call | solution.py:1059
  90.9 7.3 %ff_backward.1 = (f32[4,352,256]{2,1,0:T(8,128)S(1)}, bf16[4,4,16,1024]{3,2,1,0:T(8,128)(2,1)S(1)}, bf16[4,4,16,1024]{3,2,1,0:T(8,128)(2,1)S(1)}, f32[32,8,256]{2,1,0:T(8,128)S(1)}) custom-call(f32[14,256]{1,0:T(8,128)} %refs_18_.1, bf16[256,2048]{1,0:T(8,128)(2,1)S(1)} %get-tuple-element.138.refs_1_, f32[4,352,256]{2,1,0:T(8,128)S(1)} %get-tuple-element.139.refs_2_, ...), custom_call_target="tpu_custom_call" | custom-call | flops 4000000000 | bytes 10000000 | tf_op jit(solution)/shard_map/ff_backward/pallas_call | solution.py:1112
  98.6 1.7 %collective-permute-done.22 = bf16[4,4,16,1024]{3,2,1,0:T(8,128)(2,1)S(1)} collective-permute-done((bf16[4,4,16,1024]{3,2,1,0:T(8,128)(2,1)S(1)}, bf16[4,4,16,1024]{3,2,1,0:T(8,128)(2,1)S(1)}, u32[]{:S(2)}, u32[]{:S(2)}) %collective-permute-start.22) | collective-permute-done | bytes 524320 | tf_op jit(solution)/shard_map/ppermute | solution.py:781
  100.7 1.6 collective-permute-start.23
  102.2 1.6 collective-permute-start.24
  103.8 0.5 collective-permute-start.25
  104.5 12.5 %attention_backward.1 = (bf16[4,4,16,1024]{3,2,1,0:T(8,128)(2,1)S(1)}, bf16[4,4,16,1024]{3,2,1,0:T(8,128)(2,1)S(1)}, f32[32,256]{1,0:T(8,128)}) custom-call(f32[14,256]{1,0:T(8,128)} %refs_18_.1, bf16[256,1024]{1,0:T(8,128)(2,1)S(1)} %get-tuple-element.147.refs_1_, f32[4,352,256]{2,1,0:T(8,128)S(1)} %get-tuple-element.148.refs_2_, ...), custom_call_target="tpu_custom_call" | custom-call | flops 6000000000 | bytes 20000000 | tf_op jit(solution)/shard_map/attention_backward/pallas_call | solution.py:1138
  116.9 3.4 %collective-permute-done.24 = bf16[4,16,2816]{2,1,0:T(8,128)(2,1)S(1)} collective-permute-done((bf16[4,16,2816]{2,1,0:T(8,128)(2,1)S(1)}, bf16[4,16,2816]{2,1,0:T(8,128)(2,1)S(1)}, u32[]{:S(2)}, u32[]{:S(2)}) %collective-permute-start.24) | collective-permute-done | bytes 360480 | tf_op jit(solution)/shard_map/ppermute | solution.py:781
  120.5 2.7 %collective-permute-start.35 = (bf16[16,2816]{1,0:T(8,128)(2,1)S(1)}, bf16[16,2816]{1,0:T(8,128)(2,1)S(1)}, u32[]{:S(2)}, u32[]{:S(2)}) collective-permute-start(bf16[16,2816]{1,0:T(8,128)(2,1)S(1)} %get-tuple-element.217), channel_id=1, source_target_pairs={{0,24},{2,26},{4,28},{6,30},{8,16},{10,18},{12,20},{14,22},{16,8},... | collective-permute-start | bytes 270344 | tf_op jit(solution)/shard_map/ppermute | solution.py:781
  123.4 1.2 collective-permute-start.27
  124.6 1.8 %collective-permute-start.29 = (bf16[4,16,1024]{2,1,0:T(8,128)(2,1)S(1)}, bf16[4,16,1024]{2,1,0:T(8,128)(2,1)S(1)}, u32[]{:S(2)}, u32[]{:S(2)}) collective-permute-start(bf16[4,16,1024]{2,1,0:T(8,128)(2,1)S(1)} %get-tuple-element.211), channel_id=1, source_target_pairs={{0,6},{2,4},{4,2},{6,0},{8,14},{10,12},{12,10},{14,8},{16,22},{18,... | collective-permute-start | bytes 393224 | tf_op jit(solution)/shard_map/ppermute | solution.py:781
  126.4 0.5 collective-permute-start.28
  126.9 2.2 %collective-permute-done.27 = bf16[4,16,1024]{2,1,0:T(8,128)(2,1)S(1)} collective-permute-done((bf16[4,16,1024]{2,1,0:T(8,128)(2,1)S(1)}, bf16[4,16,1024]{2,1,0:T(8,128)(2,1)S(1)}, u32[]{:S(2)}, u32[]{:S(2)}) %collective-permute-start.27) | collective-permute-done | bytes 131104 | tf_op jit(solution)/shard_map/ppermute | solution.py:781
  129.1 1.5 collective-permute-start.33
  130.6 1.0 collective-permute-done.29
  131.6 1.3 collective-permute-done.28
  133.0 1.7 %collective-permute-start.32 = (bf16[16,1024]{1,0:T(8,128)(2,1)S(1)}, bf16[16,1024]{1,0:T(8,128)(2,1)S(1)}, u32[]{:S(2)}, u32[]{:S(2)}) collective-permute-start(bf16[16,1024]{1,0:T(8,128)(2,1)S(1)} %get-tuple-element.220), channel_id=1, source_target_pairs={{0,24},{2,26},{4,28},{6,30},{8,16},{10,18},{12,20},{14,22},{16,8},... | collective-permute-start | bytes 98312 | tf_op jit(solution)/shard_map/ppermute | solution.py:781
  134.6 1.3 collective-permute-start.31
  136.0 1.5 collective-permute-start.30
  137.4 1.3 collective-permute-done.32.refs_3_
  138.7 0.7 collective-permute-done.31.refs_2_
  139.9 1.5 finish.1
  141.4 12.9 %all_to_all.5.gathered = f32[16,24,128]{2,1,0:T(8,128)S(1)} all-to-all(f32[16,24,128]{2,1,0:T(8,128)} %get-tuple-element.171), channel_id=1, replica_groups=mesh['wide'=16,'narrow'=2] {'wide'}, dimensions={0} | all-to-all | bytes 393216 | tf_op jit(solution)/shard_map/all_to_all | solution.py:1187
  154.4 0.5 collective-permute-start.36
  154.9 1.1 collective-permute-done.36.swapped
  155.9 2.5 %adam.1 = (f32[1,1]{1,0:T(1,128)}, f32[1,1]{1,0:T(1,128)}, f32[1,1]{1,0:T(1,128)}, f32[16,896]{1,0:T(8,128)}, f32[16,896]{1,0:T(8,128)}, /*index=5*/f32[16,896]{...) custom-call(f32[16,1024]{1,0:T(8,128)} %get-tuple-element.168.rest, ...), custom_call_target="tpu_custom_call" | custom-call | flops 1000000 | bytes 1000000 | tf_op jit(solution)/shard_map/adam/pallas_call | solution.py:1196
  (56 shorter events, 2.9 us)
Async XLA Ops:
  2.4 8.9 %collective-permute-start.2 = (bf16[16,2048]{1,0:T(8,128)(2,1)}, bf16[16,2048]{1,0:T(8,128)(2,1)S(1)}, u32[]{:S(2)}, u32[]{:S(2)}) collective-permute-start(bf16[16,2048]{1,0:T(8,128)(2,1)} %get-tuple-element.121), channel_id=1, source_target_pairs={{0,24},{2,26},{4,28},{6,30},{8,16},{10,18},{12,20},{14,22},{16,8},... | collective-permute-start | bytes 196616 | tf_op jit(solution)/shard_map/ppermute | solution.py:781
  7.4 5.8 %collective-permute-start.1 = (bf16[16,2048]{1,0:T(8,128)(2,1)}, bf16[16,2048]{1,0:T(8,128)(2,1)S(1)}, u32[]{:S(2)}, u32[]{:S(2)}) collective-permute-start(bf16[16,2048]{1,0:T(8,128)(2,1)} %get-tuple-element.121), channel_id=1, source_target_pairs={{0,16},{2,18},{4,20},{6,22},{8,24},{10,26},{12,28},{14,30},{16,0},... | collective-permute-start | bytes 196616 | tf_op jit(solution)/shard_map/ppermute | solution.py:781
  7.4 5.8 %collective-permute-start = (bf16[16,2048]{1,0:T(8,128)(2,1)}, bf16[16,2048]{1,0:T(8,128)(2,1)S(1)}, u32[]{:S(2)}, u32[]{:S(2)}) collective-permute-start(bf16[16,2048]{1,0:T(8,128)(2,1)} %get-tuple-element.121), channel_id=1, source_target_pairs={{0,8},{2,10},{4,12},{6,14},{8,0},{10,2},{12,4},{14,6},{16,24},{18,... | collective-permute-start | bytes 196616 | tf_op jit(solution)/shard_map/ppermute | solution.py:781
  8.0 3.3 %collective-permute-start.3 = (f32[2,512]{1,0:T(2,128)}, f32[2,512]{1,0:T(2,128)S(1)}, u32[]{:S(2)}, u32[]{:S(2)}) collective-permute-start(f32[2,512]{1,0:T(2,128)} %refs_12_.1), channel_id=1, source_target_pairs={{0,1},{1,0},{2,3},{3,2},{4,5},{5,4},{6,7},{7,6},{8,9},{9,8},{10,11... | collective-permute-start | bytes 12296 | tf_op jit(solution)/shard_map/ppermute | solution.py:781
  11.3 24.4 %copy-start.1 = (f32[2,512]{1,0:T(2,128)}, f32[2,512]{1,0:T(2,128)S(1)}, u32[]{:S(2)}) copy-start(f32[2,512]{1,0:T(2,128)S(1)} %collective-permute-done.3.refs_3_.refs_4_) | copy-start | bytes 12292
  14.1 3.2 %collective-permute-start.4 = (bf16[4,16,2048]{2,1,0:T(8,128)(2,1)S(1)}, bf16[4,16,2048]{2,1,0:T(8,128)(2,1)S(1)}, u32[]{:S(2)}, u32[]{:S(2)}) collective-permute-start(bf16[4,16,2048]{2,1,0:T(8,128)(2,1)S(1)} %pad_maximum_fusion.4.refs_4_), channel_id=1, source_target_pairs={{0,1},{1,0},{2,3},{3,2},{4,5},{5,4},{6,7},{7,6},{8,9},{9,8},{10,11... | collective-permute-start | bytes 786440 | tf_op jit(solution)/shard_map/ppermute | solution.py:781
  14.2 8.7 %collective-permute-start.13 = (bf16[4,16,2048]{2,1,0:T(8,128)(2,1)S(1)}, bf16[4,16,2048]{2,1,0:T(8,128)(2,1)S(1)}, u32[]{:S(2)}, u32[]{:S(2)}) collective-permute-start(bf16[4,16,2048]{2,1,0:T(8,128)(2,1)S(1)} %pad_maximum_fusion.4.refs_4_), channel_id=1, source_target_pairs={{0,4},{2,6},{4,0},{6,2},{8,12},{10,14},{12,8},{14,10},{16,20},{18,... | collective-permute-start | bytes 786440 | tf_op jit(solution)/shard_map/ppermute | solution.py:781
  15.8 9.6 %collective-permute-start.12 = (bf16[4,16,2048]{2,1,0:T(8,128)(2,1)S(1)}, bf16[4,16,2048]{2,1,0:T(8,128)(2,1)S(1)}, u32[]{:S(2)}, u32[]{:S(2)}) collective-permute-start(bf16[4,16,2048]{2,1,0:T(8,128)(2,1)S(1)} %pad_maximum_fusion.4.refs_4_), channel_id=1, source_target_pairs={{0,2},{2,0},{4,6},{6,4},{8,10},{10,8},{12,14},{14,12},{16,18},{18,... | collective-permute-start | bytes 786440 | tf_op jit(solution)/shard_map/ppermute | solution.py:781
  17.3 8.1 %collective-permute-start.7 = (bf16[16,1792]{1,0:T(8,128)(2,1)}, bf16[16,1792]{1,0:T(8,128)(2,1)S(1)}, u32[]{:S(2)}, u32[]{:S(2)}) collective-permute-start(bf16[16,1792]{1,0:T(8,128)(2,1)} %get-tuple-element.126), channel_id=1, source_target_pairs={{0,24},{2,26},{4,28},{6,30},{8,16},{10,18},{12,20},{14,22},{16,8},... | collective-permute-start | bytes 172040 | tf_op jit(solution)/shard_map/ppermute | solution.py:781
  19.9 6.0 %collective-permute-start.6 = (bf16[16,1792]{1,0:T(8,128)(2,1)}, bf16[16,1792]{1,0:T(8,128)(2,1)S(1)}, u32[]{:S(2)}, u32[]{:S(2)}) collective-permute-start(bf16[16,1792]{1,0:T(8,128)(2,1)} %get-tuple-element.126), channel_id=1, source_target_pairs={{0,16},{2,18},{4,20},{6,22},{8,24},{10,26},{12,28},{14,30},{16,0},... | collective-permute-start | bytes 172040 | tf_op jit(solution)/shard_map/ppermute | solution.py:781
  19.9 6.0 %collective-permute-start.5 = (bf16[16,1792]{1,0:T(8,128)(2,1)}, bf16[16,1792]{1,0:T(8,128)(2,1)S(1)}, u32[]{:S(2)}, u32[]{:S(2)}) collective-permute-start(bf16[16,1792]{1,0:T(8,128)(2,1)} %get-tuple-element.126), channel_id=1, source_target_pairs={{0,8},{2,10},{4,12},{6,14},{8,0},{10,2},{12,4},{14,6},{16,24},{18,... | collective-permute-start | bytes 172040 | tf_op jit(solution)/shard_map/ppermute | solution.py:781
  22.9 8.8 %collective-permute-start.8 = (bf16[4,16,2048]{2,1,0:T(8,128)(2,1)S(1)}, bf16[4,16,2048]{2,1,0:T(8,128)(2,1)S(1)}, u32[]{:S(2)}, u32[]{:S(2)}) collective-permute-start(bf16[4,16,2048]{2,1,0:T(8,128)(2,1)S(1)} %pad_maximum_fusion.4.refs_4_), channel_id=1, source_target_pairs={{0,6},{2,4},{4,2},{6,0},{8,14},{10,12},{12,10},{14,8},{16,22},{18,... | collective-permute-start | bytes 786440 | tf_op jit(solution)/shard_map/ppermute | solution.py:781
  25.4 9.3 %collective-permute-start.15 = (bf16[4,16,2048]{2,1,0:T(8,128)(2,1)S(1)}, bf16[4,16,2048]{2,1,0:T(8,128)(2,1)S(1)}, u32[]{:S(2)}, u32[]{:S(2)}) collective-permute-start(bf16[4,16,2048]{2,1,0:T(8,128)(2,1)S(1)} %collective-permute-done.13.refs_6_), channel_id=1, source_target_pairs={{0,1},{1,0},{2,3},{3,2},{4,5},{5,4},{6,7},{7,6},{8,9},{9,8},{10,11... | collective-permute-start | bytes 786440 | tf_op jit(solution)/shard_map/ppermute | solution.py:781
  25.4 9.8 %collective-permute-start.14 = (bf16[4,16,2048]{2,1,0:T(8,128)(2,1)S(1)}, bf16[4,16,2048]{2,1,0:T(8,128)(2,1)S(1)}, u32[]{:S(2)}, u32[]{:S(2)}) collective-permute-start(bf16[4,16,2048]{2,1,0:T(8,128)(2,1)S(1)} %collective-permute-done.12.refs_5_), channel_id=1, source_target_pairs={{0,1},{1,0},{2,3},{3,2},{4,5},{5,4},{6,7},{7,6},{8,9},{9,8},{10,11... | collective-permute-start | bytes 786440 | tf_op jit(solution)/shard_map/ppermute | solution.py:781
  31.7 4.0 %collective-permute-start.16 = (bf16[4,16,2048]{2,1,0:T(8,128)(2,1)S(1)}, bf16[4,16,2048]{2,1,0:T(8,128)(2,1)S(1)}, u32[]{:S(2)}, u32[]{:S(2)}) collective-permute-start(bf16[4,16,2048]{2,1,0:T(8,128)(2,1)S(1)} %collective-permute-done.8.refs_7_), channel_id=1, source_target_pairs={{0,1},{1,0},{2,3},{3,2},{4,5},{5,4},{6,7},{7,6},{8,9},{9,8},{10,11... | collective-permute-start | bytes 786440 | tf_op jit(solution)/shard_map/ppermute | solution.py:781
  31.7 20.9 %collective-permute-start.17 = (bf16[4,16,1792]{2,1,0:T(8,128)(2,1)S(1)}, bf16[4,16,1792]{2,1,0:T(8,128)(2,1)S(1)}, u32[]{:S(2)}, u32[]{:S(2)}) collective-permute-start(bf16[4,16,1792]{2,1,0:T(8,128)(2,1)S(1)} %pad_maximum_fusion.5.refs_7_), channel_id=1, source_target_pairs={{0,1},{1,0},{2,3},{3,2},{4,5},{5,4},{6,7},{7,6},{8,9},{9,8},{10,11... | collective-permute-start | bytes 688136 | tf_op jit(solution)/shard_map/ppermute | solution.py:781
  32.2 19.7 %collective-permute-start.11 = (bf16[4,16,1792]{2,1,0:T(8,128)(2,1)S(1)}, bf16[4,16,1792]{2,1,0:T(8,128)(2,1)S(1)}, u32[]{:S(2)}, u32[]{:S(2)}) collective-permute-start(bf16[4,16,1792]{2,1,0:T(8,128)(2,1)S(1)} %pad_maximum_fusion.5.refs_7_), channel_id=1, source_target_pairs={{0,6},{2,4},{4,2},{6,0},{8,14},{10,12},{12,10},{14,8},{16,22},{18,... | collective-permute-start | bytes 688136 | tf_op jit(solution)/shard_map/ppermute | solution.py:781
  34.7 17.2 %collective-permute-start.10 = (bf16[4,16,1792]{2,1,0:T(8,128)(2,1)S(1)}, bf16[4,16,1792]{2,1,0:T(8,128)(2,1)S(1)}, u32[]{:S(2)}, u32[]{:S(2)}) collective-permute-start(bf16[4,16,1792]{2,1,0:T(8,128)(2,1)S(1)} %pad_maximum_fusion.5.refs_7_), channel_id=1, source_target_pairs={{0,4},{2,6},{4,0},{6,2},{8,12},{10,14},{12,8},{14,10},{16,20},{18,... | collective-permute-start | bytes 688136 | tf_op jit(solution)/shard_map/ppermute | solution.py:781
  35.2 16.7 %collective-permute-start.9 = (bf16[4,16,1792]{2,1,0:T(8,128)(2,1)S(1)}, bf16[4,16,1792]{2,1,0:T(8,128)(2,1)S(1)}, u32[]{:S(2)}, u32[]{:S(2)}) collective-permute-start(bf16[4,16,1792]{2,1,0:T(8,128)(2,1)S(1)} %pad_maximum_fusion.5.refs_7_), channel_id=1, source_target_pairs={{0,2},{2,0},{4,6},{6,4},{8,10},{10,8},{12,14},{14,12},{16,18},{18,... | collective-permute-start | bytes 688136 | tf_op jit(solution)/shard_map/ppermute | solution.py:781
  51.9 1.6 collective-permute-start.18
  52.0 1.8 %collective-permute-start.19 = (bf16[4,16,1792]{2,1,0:T(8,128)(2,1)S(1)}, bf16[4,16,1792]{2,1,0:T(8,128)(2,1)S(1)}, u32[]{:S(2)}, u32[]{:S(2)}) collective-permute-start(bf16[4,16,1792]{2,1,0:T(8,128)(2,1)S(1)} %collective-permute-done.10.refs_9_), channel_id=1, source_target_pairs={{0,1},{1,0},{2,3},{3,2},{4,5},{5,4},{6,7},{7,6},{8,9},{9,8},{10,11... | collective-permute-start | bytes 688136 | tf_op jit(solution)/shard_map/ppermute | solution.py:781
  52.5 1.6 %collective-permute-start.20 = (bf16[4,16,1792]{2,1,0:T(8,128)(2,1)S(1)}, bf16[4,16,1792]{2,1,0:T(8,128)(2,1)S(1)}, u32[]{:S(2)}, u32[]{:S(2)}) collective-permute-start(bf16[4,16,1792]{2,1,0:T(8,128)(2,1)S(1)} %collective-permute-done.11.refs_10_), channel_id=1, source_target_pairs={{0,1},{1,0},{2,3},{3,2},{4,5},{5,4},{6,7},{7,6},{8,9},{9,8},{10,11... | collective-permute-start | bytes 688136 | tf_op jit(solution)/shard_map/ppermute | solution.py:781
  90.7 7.6 %copy-start = (f32[8,128]{1,0:T(8,128)}, f32[8,128]{1,0:T(8,128)S(1)}, u32[]{:S(2)}) copy-start(f32[8,128]{1,0:T(8,128)S(1)} %get-tuple-element.167.refs_8_) | copy-start | bytes 12292
  90.7 9.7 %collective-permute-start.21 = (bf16[4,4,16,1792]{3,2,1,0:T(8,128)(2,1)S(1)}, bf16[4,4,16,1792]{3,2,1,0:T(8,128)(2,1)S(1)}, u32[]{:S(2)}, u32[]{:S(2)}) collective-permute-start(bf16[4,4,16,1792]{3,2,1,0:T(8,128)(2,1)S(1)} %get-tuple-element.137), channel_id=1, source_target_pairs={{0,1},{1,0},{2,3},{3,2},{4,5},{5,4},{6,7},{7,6},{8,9},{9,8},{10,11... | collective-permute-start | bytes 2752520 | tf_op jit(solution)/shard_map/ppermute | solution.py:781
  98.2 2.0 %collective-permute-start.22 = (bf16[4,4,16,1024]{3,2,1,0:T(8,128)(2,1)S(1)}, bf16[4,4,16,1024]{3,2,1,0:T(8,128)(2,1)S(1)}, u32[]{:S(2)}, u32[]{:S(2)}) collective-permute-start(bf16[4,4,16,1024]{3,2,1,0:T(8,128)(2,1)S(1)} %get-tuple-element.146), channel_id=1, source_target_pairs={{0,1},{1,0},{2,3},{3,2},{4,5},{5,4},{6,7},{7,6},{8,9},{9,8},{10,11... | collective-permute-start | bytes 1572872 | tf_op jit(solution)/shard_map/ppermute | solution.py:781
  100.7 16.3 %collective-permute-start.23 = (bf16[4,16,2816]{2,1,0:T(8,128)(2,1)S(1)}, bf16[4,16,2816]{2,1,0:T(8,128)(2,1)S(1)}, u32[]{:S(2)}, u32[]{:S(2)}) collective-permute-start(bf16[4,16,2816]{2,1,0:T(8,128)(2,1)S(1)} %pad_maximum_fusion.1), channel_id=1, source_target_pairs={{0,2},{2,0},{4,6},{6,4},{8,10},{10,8},{12,14},{14,12},{16,18},{18,... | collective-permute-start | bytes 1081352 | tf_op jit(solution)/shard_map/ppermute | solution.py:781
  102.2 18.1 %collective-permute-start.24 = (bf16[4,16,2816]{2,1,0:T(8,128)(2,1)S(1)}, bf16[4,16,2816]{2,1,0:T(8,128)(2,1)S(1)}, u32[]{:S(2)}, u32[]{:S(2)}) collective-permute-start(bf16[4,16,2816]{2,1,0:T(8,128)(2,1)S(1)} %pad_maximum_fusion.2), channel_id=1, source_target_pairs={{0,4},{2,6},{4,0},{6,2},{8,12},{10,14},{12,8},{14,10},{16,20},{18,... | collective-permute-start | bytes 1081352 | tf_op jit(solution)/shard_map/ppermute | solution.py:781
  103.8 16.5 %collective-permute-start.25 = (bf16[4,16,2816]{2,1,0:T(8,128)(2,1)S(1)}, bf16[4,16,2816]{2,1,0:T(8,128)(2,1)S(1)}, u32[]{:S(2)}, u32[]{:S(2)}) collective-permute-start(bf16[4,16,2816]{2,1,0:T(8,128)(2,1)S(1)} %pad_maximum_fusion.3), channel_id=1, source_target_pairs={{0,6},{2,4},{4,2},{6,0},{8,14},{10,12},{12,10},{14,8},{16,22},{18,... | collective-permute-start | bytes 1081352 | tf_op jit(solution)/shard_map/ppermute | solution.py:781
  116.9 6.3 %collective-permute-start.26 = (bf16[4,4,16,1024]{3,2,1,0:T(8,128)(2,1)S(1)}, bf16[4,4,16,1024]{3,2,1,0:T(8,128)(2,1)S(1)}, u32[]{:S(2)}, u32[]{:S(2)}) collective-permute-start(bf16[4,4,16,1024]{3,2,1,0:T(8,128)(2,1)S(1)} %get-tuple-element.163), channel_id=1, source_target_pairs={{0,1},{1,0},{2,3},{3,2},{4,5},{5,4},{6,7},{7,6},{8,9},{9,8},{10,11... | collective-permute-start | bytes 1572872 | tf_op jit(solution)/shard_map/ppermute | solution.py:781
  120.5 15.4 %collective-permute-start.35 = (bf16[16,2816]{1,0:T(8,128)(2,1)S(1)}, bf16[16,2816]{1,0:T(8,128)(2,1)S(1)}, u32[]{:S(2)}, u32[]{:S(2)}) collective-permute-start(bf16[16,2816]{1,0:T(8,128)(2,1)S(1)} %get-tuple-element.217), channel_id=1, source_target_pairs={{0,24},{2,26},{4,28},{6,30},{8,16},{10,18},{12,20},{14,22},{16,8},... | collective-permute-start | bytes 270344 | tf_op jit(solution)/shard_map/ppermute | solution.py:781
  123.2 14.2 %collective-permute-start.34 = (bf16[16,2816]{1,0:T(8,128)(2,1)S(1)}, bf16[16,2816]{1,0:T(8,128)(2,1)S(1)}, u32[]{:S(2)}, u32[]{:S(2)}) collective-permute-start(bf16[16,2816]{1,0:T(8,128)(2,1)S(1)} %get-tuple-element.218), channel_id=1, source_target_pairs={{0,16},{2,18},{4,20},{6,22},{8,24},{10,26},{12,28},{14,30},{16,0},... | collective-permute-start | bytes 270344 | tf_op jit(solution)/shard_map/ppermute | solution.py:781
  123.4 5.7 %collective-permute-start.27 = (bf16[4,16,1024]{2,1,0:T(8,128)(2,1)S(1)}, bf16[4,16,1024]{2,1,0:T(8,128)(2,1)S(1)}, u32[]{:S(2)}, u32[]{:S(2)}) collective-permute-start(bf16[4,16,1024]{2,1,0:T(8,128)(2,1)S(1)} %get-tuple-element.210), channel_id=1, source_target_pairs={{0,2},{2,0},{4,6},{6,4},{8,10},{10,8},{12,14},{14,12},{16,18},{18,... | collective-permute-start | bytes 393224 | tf_op jit(solution)/shard_map/ppermute | solution.py:781
  124.6 7.0 %collective-permute-start.29 = (bf16[4,16,1024]{2,1,0:T(8,128)(2,1)S(1)}, bf16[4,16,1024]{2,1,0:T(8,128)(2,1)S(1)}, u32[]{:S(2)}, u32[]{:S(2)}) collective-permute-start(bf16[4,16,1024]{2,1,0:T(8,128)(2,1)S(1)} %get-tuple-element.211), channel_id=1, source_target_pairs={{0,6},{2,4},{4,2},{6,0},{8,14},{10,12},{12,10},{14,8},{16,22},{18,... | collective-permute-start | bytes 393224 | tf_op jit(solution)/shard_map/ppermute | solution.py:781
  126.4 6.4 %collective-permute-start.28 = (bf16[4,16,1024]{2,1,0:T(8,128)(2,1)S(1)}, bf16[4,16,1024]{2,1,0:T(8,128)(2,1)S(1)}, u32[]{:S(2)}, u32[]{:S(2)}) collective-permute-start(bf16[4,16,1024]{2,1,0:T(8,128)(2,1)S(1)} %get-tuple-element.212), channel_id=1, source_target_pairs={{0,4},{2,6},{4,0},{6,2},{8,12},{10,14},{12,8},{14,10},{16,20},{18,... | collective-permute-start | bytes 393224 | tf_op jit(solution)/shard_map/ppermute | solution.py:781
  129.1 8.3 %collective-permute-start.33 = (bf16[16,2816]{1,0:T(8,128)(2,1)S(1)}, bf16[16,2816]{1,0:T(8,128)(2,1)S(1)}, u32[]{:S(2)}, u32[]{:S(2)}) collective-permute-start(bf16[16,2816]{1,0:T(8,128)(2,1)S(1)} %get-tuple-element.219), channel_id=1, source_target_pairs={{0,8},{2,10},{4,12},{6,14},{8,0},{10,2},{12,4},{14,6},{16,24},{18,... | collective-permute-start | bytes 270344 | tf_op jit(solution)/shard_map/ppermute | solution.py:781
  133.0 5.8 %collective-permute-start.32 = (bf16[16,1024]{1,0:T(8,128)(2,1)S(1)}, bf16[16,1024]{1,0:T(8,128)(2,1)S(1)}, u32[]{:S(2)}, u32[]{:S(2)}) collective-permute-start(bf16[16,1024]{1,0:T(8,128)(2,1)S(1)} %get-tuple-element.220), channel_id=1, source_target_pairs={{0,24},{2,26},{4,28},{6,30},{8,16},{10,18},{12,20},{14,22},{16,8},... | collective-permute-start | bytes 98312 | tf_op jit(solution)/shard_map/ppermute | solution.py:781
  134.6 4.8 %collective-permute-start.31 = (bf16[16,1024]{1,0:T(8,128)(2,1)S(1)}, bf16[16,1024]{1,0:T(8,128)(2,1)S(1)}, u32[]{:S(2)}, u32[]{:S(2)}) collective-permute-start(bf16[16,1024]{1,0:T(8,128)(2,1)S(1)} %get-tuple-element.221), channel_id=1, source_target_pairs={{0,16},{2,18},{4,20},{6,22},{8,24},{10,26},{12,28},{14,30},{16,0},... | collective-permute-start | bytes 98312 | tf_op jit(solution)/shard_map/ppermute | solution.py:781
  136.0 3.9 %collective-permute-start.30 = (bf16[16,1024]{1,0:T(8,128)(2,1)S(1)}, bf16[16,1024]{1,0:T(8,128)(2,1)S(1)}, u32[]{:S(2)}, u32[]{:S(2)}) collective-permute-start(bf16[16,1024]{1,0:T(8,128)(2,1)S(1)} %get-tuple-element.222), channel_id=1, source_target_pairs={{0,8},{2,10},{4,12},{6,14},{8,0},{10,2},{12,4},{14,6},{16,24},{18,... | collective-permute-start | bytes 98312 | tf_op jit(solution)/shard_map/ppermute | solution.py:781
  154.4 1.6 collective-permute-start.37
  154.4 1.6 collective-permute-start.36

commit v8 on v7

--- a/solution.py
+++ b/solution.py
@@ -87,6 +87,16 @@
     return centred * scale, scale
 
 
+def keep_norm(rows, xhat, scale, kept):
+    kept[0][rows] = xhat.astype(BF16)
+    kept[1][rows] = jnp.broadcast_to(scale, (TILE, 128))
+
+
+def kept_norm(rows, kept):
+    scale = kept[1][rows]
+    return kept[0][rows].astype(F32), jnp.concatenate([scale, scale], axis=1)
+
+
 def normalise_back(grad, xhat, scale, gain):
     inner = grad * gain
     mean_one = jnp.mean(inner, axis=1, keepdims=True)
@@ -151,13 +161,15 @@
         lax.fori_loop(0, 4, block, 0)
 
 
-def disperse(g_ref, place, keep_ref, send_ref, halves, scaled=True):
+def disperse(g_ref, place, keep_ref, send_ref, halves, scaled=True, by_distance=True):
     me, core, _ = place
     is_first = core == 0
 
     def block(i, _):
         p, z = i >> 2, i & 3
-        row = pl.multiple_of((me ^ (4 * z + p)) * 16, 16)
+        spot = 4 * z + p
+        owner = me ^ spot if by_distance else spot ^ (me & ~3)
+        row = pl.multiple_of(owner * 16, 16)
         for src, width, dest in halves:
             low = g_ref[pl.ds(row, 16), dest : dest + width]
             high = g_ref[pl.ds(row, 16), dest + width : dest + 2 * width]
@@ -189,10 +201,13 @@
 
 
 def layer_forward(x_ref, w_ref, vec, bias, kept, work):
-    qt_ref, kv_ref, p0, p1, p2, r_ref, ot_ref, o_ref, m_ref, h_ref, gp_ref, a_ref, c_ref = kept
-    qst_ref, vt_ref, mask_ref, wqt_ref, long_ref, u_ref, y_ref = work
+    qt_ref, kv_ref, p0, p1, p2, r_ref, ot_ref, o_ref = kept[0:8]
+    h_ref, gp_ref, a_ref, c_ref = kept[9:13]
+    qst_ref, vt_ref, mask_ref, wqt_ref, long_ref, u_ref, y_ref, m_ref = work
     for rows in tiles(SEQ, TILE):
-        normed16 = (normalise(x_ref[rows])[0] * vec[0:1] + vec[1:2]).astype(BF16)
+        xhat, scale = normalise(x_ref[rows])
+        keep_norm(rows, xhat, scale, kept[14:16])
+        normed16 = (xhat * vec[0:1] + vec[1:2]).astype(BF16)
         a_ref[rows], long_ref[rows] = normed16, normed16
     kv_ref[0:SEQ] = dot_nn(long_ref[0:SEQ], w_ref[:, 256:768]).astype(BF16)
     kv_ref[SEQ:KEYS] = jnp.zeros((KEYS - SEQ, 512), BF16)
@@ -221,7 +236,9 @@
     for rows in tiles(SEQ, TILE):
         middle = x_ref[rows] + (y_ref[rows] + vec[2:3])
         m_ref[rows] = middle
-        c_ref[rows] = (normalise(middle)[0] * vec[3:4] + vec[4:5]).astype(BF16)
+        xhat, scale = normalise(middle)
+        keep_norm(rows, xhat, scale, (kept[8], kept[13]))
+        c_ref[rows] = (xhat * vec[3:4] + vec[4:5]).astype(BF16)
     u_ref[...] = dot_nn(c_ref[...], w_ref[:, COL_UP : COL_UP + FF])
     for rows in tiles(SEQ, TILE):
         for first in range(0, FF, 256):
@@ -235,7 +252,7 @@
 
 
 def ff_backward(grad_ref, grad16_ref, w_ref, w_up, w_down, vec, kept, v_ref, v_row, bias_row, work, mid_ref, mid16_refs):
-    m_ref, gp_ref = kept
+    norm_kept, gp_ref = kept
     du_ref, ones_ref, u_ref, y_ref = work
     u_ref[...] = dot_nn(grad16_ref[...], w_ref[:, w_down : w_down + FF])
     for rows in tiles(SEQ, TILE):
@@ -246,7 +263,7 @@
     y_ref[...] = dot_nt(du_ref[...], w_ref[:, w_up : w_up + FF])
     totals = [None] * 3
     for rows in tiles(SEQ, TILE):
-        xhat, scale = normalise(m_ref[rows])
+        xhat, scale = kept_norm(rows, norm_kept)
         grad = y_ref[rows]
         mid = grad_ref[rows] + normalise_back(grad, xhat, scale, vec[3:4])
         mid_ref[rows] = mid
@@ -259,7 +276,7 @@
 
 
 def attention_backward(mid_ref, mid16_ref, w_ref, vec, kept, v_ref, v_row, work, out_ref):
-    x_ref, qt_ref, kv_ref, p0, p1, p2, r_ref, ot_ref = kept
+    norm_kept, (qt_ref, kv_ref, p0, p1, p2, r_ref, ot_ref) = kept
     dost_ref, qst_ref, kt_ref, dst_ref, dqt_ref, dkv_ref, dqkv_ref, proj_ref, y_ref = work
     grad_o = dot_nt(proj_ref[...], mid16_ref[...]).astype(BF16).astype(F32)
     kt_ref[...] = jnp.transpose(kv_ref[:, 0:256])
@@ -292,7 +309,7 @@
     y_ref[...] = dot_nt(dqkv_ref[...], w_ref[:, COL_QKV : COL_QKV + 768])
     totals = [None] * 2
     for rows in tiles(SEQ, TILE):
-        xhat, scale = normalise(x_ref[rows])
+        xhat, scale = kept_norm(rows, norm_kept)
         grad = y_ref[rows]
         out = mid_ref[rows] + normalise_back(grad, xhat, scale, vec[0:1])
         out_ref[rows] = out.astype(out_ref.dtype)
@@ -364,7 +381,7 @@
 
 
 def start_forward(work, w_ref):
-    qst_ref, vt_ref, mask_ref, wqt_ref, long_ref, u_ref, y_ref = work
+    qst_ref, vt_ref, mask_ref, wqt_ref, long_ref = work[0:5]
     long_ref[SEQ:KEYS] = jnp.zeros((KEYS - SEQ, D), BF16)
     qst_ref[...] = jnp.zeros(qst_ref.shape, BF16)
     vt_ref[...] = jnp.ones(vt_ref.shape, BF16)
@@ -376,10 +393,11 @@
     refs = (places(fast),) + refs
     place, meta_ref, vec_ref, bias_ref, bias_other = refs[0:5]
     mine, other = refs[5:9], refs[9:13]
-    w_attention, w_ff, side_out, next_ref, hits_ref, x_ref = refs[13:19]
-    kept = [ref.at[0] for ref in refs[19:32]]
-    w_ref = refs[32]
-    work = refs[33:40]
+    w_attention, w_ff, side_out, next_ref, hits_ref = refs[13:18]
+    kept = [ref.at[0] for ref in refs[18:34]]
+    w_ref, x_ref = refs[34:36]
+    work = refs[36:44]
+    y_ref, m_ref = work[6:8]
 
     @pl.when(pl.program_id(0) == 0)
     def _():
@@ -390,12 +408,12 @@
         start_forward(work, w_ref)
 
     make_hits(meta_ref.at[0], hits_ref.at[0])
-    x_ref[0] = dot_nt(hits_ref[0], w_ref[:, COL_TABLE : COL_TABLE + ROWS])
+    x_ref[...] = dot_nt(hits_ref[0], w_ref[:, COL_TABLE : COL_TABLE + ROWS])
     bias = own_bias(place, bias_ref[0:1], bias_other[0:1])
     vec = vec_ref[0:6]
-    layer_forward(x_ref.at[0], w_ref, vec, bias, kept, work)
+    layer_forward(x_ref, w_ref, vec, bias, kept, work)
     for rows in tiles(SEQ, TILE):
-        next_ref[0, rows] = kept[8][rows] + (work[6][rows] + vec[5:6])
+        next_ref[0, rows] = m_ref[rows] + (y_ref[rows] + vec[5:6])
 
 
 def codebook_losses(logits, meta):
@@ -440,13 +458,14 @@
     grad_ref, keep_ref, send_ref, v_out, scalar_ref = refs[16:21]
     refs = refs[1:]
     w_ref, g_ref, v_ref = refs[20:23]
-    kept = list(refs[23:36])
-    forward_work = refs[36:43]
-    u_ref, y_ref = forward_work[5:7]
-    backward_work = list(refs[43:49])
-    proj_ref = refs[49]
-    du_all, ones_ref, up_ref, up16_all, mid_ref, mid16_ref = refs[50:56]
-    last_ref, final_all, logit_ref, dlogit_all, pick_ref, put_ref, mid16_all = refs[56:63]
+    kept = list(refs[23:39])
+    forward_work = refs[39:47]
+    u_ref, y_ref, m_ref = forward_work[5:8]
+    backward_work = list(refs[47:53])
+    proj_ref = refs[53]
+    du_all, ones_ref, up_ref, up16_all, mid_ref, mid16_ref = refs[54:60]
+    last_kept = refs[60:62]
+    final_all, logit_ref, dlogit_all, pick_ref, put_ref, mid16_all = refs[62:68]
     o_all, h_all, a_all, c_all, dqkv_all = kept[7], kept[9], kept[11], kept[12], backward_work[5]
     dost_ref = backward_work[0]
     step = pl.program_id(0)
@@ -469,7 +488,7 @@
     here = pl.ds(pl.multiple_of((step & 1) * SEQ, 32), SEQ)
     for i in (7, 9, 11, 12):
         kept[i] = kept[i].at[here]
-    m_ref, h_ref, gp_ref = kept[8:11]
+    gp_ref = kept[10]
     backward_work[5] = dqkv_all.at[here]
     du_ref, up16_ref, pair16_ref = du_all.at[here], up16_all.at[here], mid16_all.at[here]
     final_ref, dlogit_ref = final_all.at[here], dlogit_all.at[here]
@@ -481,8 +500,9 @@
     gain, offset = vec_ref[12:13], vec_ref[13:14]
     for rows in tiles(SEQ, TILE):
         last = m_ref[rows] + (y_ref[rows] + vec[5:6])
-        last_ref[rows] = last
-        final_ref[rows] = (normalise(last)[0] * gain + offset).astype(BF16)
+        xhat, scale = normalise(last)
+        keep_norm(rows, xhat, scale, last_kept)
+        final_ref[rows] = (xhat * gain + offset).astype(BF16)
     cols_head = slice(COL_HEAD, COL_HEAD + VOCAB + 128)
     logit_ref[...] = dot_nn(final_ref[...], w_ref[:, COL_HEAD : COL_HEAD + VOCAB])
     logs, picked = None, None
@@ -508,7 +528,7 @@
     y_ref[...] = dot_nt(dlogit_ref[...], w_ref[:, cols_head])
     totals = [None] * 3
     for rows in tiles(SEQ, TILE):
-        xhat, scale = normalise(last_ref[rows])
+        xhat, scale = kept_norm(rows, last_kept)
         grad = y_ref[rows]
         up = normalise_back(grad, xhat, scale, gain)
         up_ref[rows] = up
@@ -524,7 +544,7 @@
         COL_UP,
         COL_DOWN,
         vec,
-        (m_ref, gp_ref),
+        ((kept[8], kept[13]), gp_ref),
         v_ref,
         6,
         SMALL_BIAS + 4,
@@ -537,7 +557,7 @@
         mid16_ref,
         w_ref,
         vec,
-        (x_ref,) + tuple(kept[0:7]),
+        (kept[14:16], kept[0:7]),
         v_ref,
         6,
         (dost_ref, forward_work[0]) + tuple(backward_work[1:]) + (proj_ref, y_ref),
@@ -554,7 +574,7 @@
 
     @pl.when(step == pl.num_programs(0) - 1)
     def _():
-        disperse(g_ref, place, keep_ref, send_ref, HALF_SECOND)
+        disperse(g_ref, place, keep_ref, send_ref, HALF_SECOND, True, False)
         side = jnp.transpose(g_ref[:, COL_SECOND:])
         for i in range(5):
             v_ref[SMALL_SIDE + i, 0:1] = side[i : i + 1]
@@ -562,18 +582,18 @@
 
 
 def ff_backward_kernel(fast, *refs):
-    vec_ref, w_ref, grad_ref, v_in, m_ref, gp_ref, h_all, c_all = refs[0:8]
-    mid_ref, keep_ref, send_ref, v_out = refs[8:12]
-    g_ref, v_ref, grad16_all, du_all, ones_ref, u_ref, y_ref = refs[12:19]
+    vec_ref, w_ref, grad_ref, v_in = refs[0:4]
+    xhat_ref, scale_ref, h_ref, gp_ref, c_ref = [ref.at[0] for ref in refs[4:9]]
+    mid_ref, keep_ref, send_ref, v_out = refs[9:13]
+    g_ref, v_ref, grad16_ref, du_ref, ones_ref, u_ref, y_ref = refs[13:20]
     step = pl.program_id(0)
 
     @pl.when(step == 0)
     def _():
+        g_ref[...] = jnp.zeros(g_ref.shape, F32)
         v_ref[...] = v_in[...]
         ones_ref[...] = jnp.ones(ones_ref.shape, BF16)
 
-    here = pl.ds(pl.multiple_of(step * SEQ, 32), SEQ)
-    grad16_ref = grad16_all.at[here]
     total = None
     for rows in tiles(SEQ, TILE):
         grad = grad_ref[0, rows]
@@ -587,36 +607,37 @@
         GRAD_UP,
         GRAD_DOWN,
         vec_ref[0:6],
-        (m_ref.at[0], gp_ref.at[0]),
+        ((xhat_ref, scale_ref), gp_ref),
         v_ref,
         0,
         SMALL_BIAS,
-        (du_all.at[here], ones_ref, u_ref, y_ref),
+        (du_ref, ones_ref, u_ref, y_ref),
         mid_ref.at[0],
         (),
     )
+    add_gradient(g_ref, GRAD_DOWN, grad16_ref[...], h_ref[...])
+    add_gradient(g_ref, GRAD_UP, c_ref[...], du_ref[...])
 
     @pl.when(step == pl.num_programs(0) - 1)
     def _():
-        g_ref[:, GRAD_UP : GRAD_UP + FF] = dot_tn(c_all[...], du_all[...])
-        g_ref[:, GRAD_DOWN : GRAD_DOWN + FF] = dot_tn(grad16_all[...], h_all[...])
-        disperse(g_ref, places(fast), keep_ref, send_ref, HALF_GRAD_FF, False)
+        disperse(g_ref, places(fast), keep_ref, send_ref, HALF_GRAD_FF, False, False)
         v_out[...] = v_ref[...]
 
 
 def attention_backward_kernel(fast, *refs):
-    vec_ref, w_ref, mid_ref, v_in = refs[0:4]
-    kept = [ref.at[0] for ref in refs[4:12]]
-    o_all, a_all, hits_all = refs[12:15]
-    keep_ref, send_ref, v_out = refs[16:19]
-    g_ref, v_ref, mid16_ref, mid16_all, out16_all, dqkv_all = refs[19:25]
-    work = list(refs[25:33])
+    vec_ref, w_ref, mid_ref, v_in, scalar_in = refs[0:5]
+    kept = [ref.at[0] for ref in refs[5:14]]
+    o_all, a_all, hits_all = refs[14:17]
+    keep_ref, send_ref, v_out, scalar_out = refs[18:22]
+    g_ref, v_ref, mid16_ref, mid16_all, out16_all, dqkv_all = refs[22:28]
+    work = list(refs[28:36])
     dost_ref, qst_ref, proj_ref = work[0], work[1], work[6]
     step = pl.program_id(0)
 
     @pl.when(step == 0)
     def _():
         v_ref[...] = v_in[...]
+        scalar_out[...] = scalar_in[...]
         dost_ref[...] = jnp.zeros(dost_ref.shape, BF16)
         qst_ref[...] = jnp.zeros(qst_ref.shape, BF16)
         proj_ref[...] = jnp.transpose(w_ref[:, COL_PROJ : COL_PROJ + 256])
@@ -624,7 +645,7 @@
 
     here = pl.ds(pl.multiple_of(step * SEQ, 32), SEQ)
     all16_ref = mid16_all.at[here]
-    spread_heads(kept[1], qst_ref)
+    spread_heads(kept[2], qst_ref)
     for rows in tiles(SEQ, TILE):
         mid16 = mid_ref[0, rows].astype(BF16)
         mid16_ref[rows], all16_ref[rows] = mid16, mid16
@@ -634,7 +655,7 @@
         mid16_ref,
         w_ref,
         vec_ref[0:6],
-        kept,
+        (kept[0:2], kept[2:9]),
         v_ref,
         0,
         work,
@@ -802,18 +823,20 @@
     return [whole[:, p] for p in range(4)]
 
 
-def in_pieces(blocks, wide, n_high):
+def in_pieces(blocks, wide, n_high, by_distance):
     cols = blocks.shape[-1]
     if n_high == 4:
         return blocks
     rows = 64 // n_high
     whole = blocks.transpose(1, 0, 2, 3).reshape(4 * n_high, rows, cols)
-    whole = whole[wide ^ jnp.arange(4 * n_high)]
+    order = jnp.arange(4 * n_high)
+    whole = whole[wide ^ order if by_distance else order ^ (wide & ~3)]
     return whole.reshape(n_high, 4, rows, cols).transpose(1, 0, 2, 3)
 
 
-def add_cores(keep, send, wide, n_high):
-    keep, send = in_pieces(keep, wide, n_high), in_pieces(send, wide, n_high)
+def add_cores(keep, send, wide, n_high, by_distance):
+    keep = in_pieces(keep, wide, n_high, by_distance)
+    send = in_pieces(send, wide, n_high, by_distance)
     received = swap(send, "narrow", 1)
     return [keep[p].astype(F32) + received[p].astype(F32) for p in range(4)]
 
@@ -860,9 +883,9 @@
 VMEM_MIB = {
     "pack": 58,
     "prepare": 58,
-    "first_forward": 24,
-    "middle": 31,
-    "ff_backward": 24,
+    "first_forward": 26,
+    "middle": 32,
+    "ff_backward": 20,
     "attention_backward": 26,
     "finish": 58,
     "adam": 58,
@@ -895,11 +918,14 @@
     ((8, KEYS), F32),
     ((D, KEYS), BF16),
     ((SEQ, D), BF16),
-    ((SEQ, D), F32),
+    ((SEQ, D), BF16),
     ((SEQ, FF), BF16),
     ((SEQ, FF), BF16),
     ((SEQ, D), BF16),
     ((SEQ, D), BF16),
+    ((SEQ, 128), F32),
+    ((SEQ, D), BF16),
+    ((SEQ, 128), F32),
 )
 FORWARD_WORK = [
     pltpu.VMEM((D, BLOCKS * QUERIES), BF16),
@@ -908,6 +934,7 @@
     pltpu.VMEM((D, D), BF16),
     pltpu.VMEM((KEYS, D), BF16),
     pltpu.VMEM((SEQ, FF), F32),
+    pltpu.VMEM((SEQ, D), F32),
     pltpu.VMEM((SEQ, D), F32),
 ]
 BACKWARD_WORK = [
@@ -1029,18 +1056,17 @@
         functools.partial(first_forward_kernel, fast),
         (count,),
         [meta_spec] + vec_specs + [VMEM_SPEC] * 8,
-        [w_attention_spec, w_ff_spec, side_spec, row_spec((SEQ, D)), hits_spec, row_spec((SEQ, D))]
-        + kept_specs,
+        [w_attention_spec, w_ff_spec, side_spec, row_spec((SEQ, D)), hits_spec] + kept_specs,
         [shaped((D, 1024), BF16), shaped((D, 2048), BF16), shaped((D, 128), BF16), row_f32]
-        + [shaped((count, SEQ, ROWS), BF16), row_f32]
+        + [shaped((count, SEQ, ROWS), BF16)]
         + kept_shapes,
-        [pltpu.VMEM((D, COL_FIRST), BF16)] + FORWARD_WORK,
+        [pltpu.VMEM((D, COL_FIRST), BF16), pltpu.VMEM((SEQ, D), F32)] + FORWARD_WORK,
         4 * 10**9,
         20 * 10**6,
         "first_forward",
     )(*in_hbm([meta, vectors, up_bias, other_bias]), *resident(first_parts))
-    w_attention, w_ff, side_copy, stream, hits, stream_first = results[0:6]
-    kept = results[6:]
+    w_attention, w_ff, side_copy, stream, hits = results[0:5]
+    kept = results[5:]
     received, side_copy = lax.optimization_barrier((second_mine[1:], side_copy))
     second_mine = second_mine[0:1] + received
     second_other = gather_cores(second_mine)
@@ -1074,6 +1100,7 @@
         + [pltpu.VMEM((2 * SEQ, D), BF16), pltpu.VMEM(*KEPT[8])]
         + [pltpu.VMEM((2 * SEQ, FF), BF16), pltpu.VMEM(*KEPT[10])]
         + [pltpu.VMEM((2 * SEQ, D), BF16)] * 2
+        + [pltpu.VMEM(*a) for a in KEPT[13:16]]
         + FORWARD_WORK
         + BACKWARD_WORK[0:1]
         + BACKWARD_WORK[2:6]
@@ -1086,7 +1113,8 @@
             pltpu.VMEM((2 * SEQ, D), BF16),
             pltpu.VMEM((SEQ, D), F32),
             pltpu.VMEM((KEYS, D), BF16),
-            pltpu.VMEM((SEQ, D), F32),
+            pltpu.VMEM((SEQ, D), BF16),
+            pltpu.VMEM((SEQ, 128), F32),
             pltpu.VMEM((2 * SEQ, D), BF16),
             pltpu.VMEM((SEQ, VOCAB), F32),
             pltpu.VMEM((2 * SEQ, VOCAB + 128), BF16),
@@ -1103,25 +1131,24 @@
         stream,
         *resident(second_parts),
     )
-    second_sums = add_cores(keep_second, send_second, wide, n_high)
+    second_sums = add_cores(keep_second, send_second, wide, n_high, False)
 
     def joined(a):
         return a.reshape((count * a.shape[1],) + a.shape[2:])
 
-    joined_ff = [joined(kept[9]), joined(kept[12])]
+    kept_ff = (kept[8], kept[13], kept[9], kept[10], kept[12])
     grad_mid, keep_ff, send_ff, small_grads = call(
         functools.partial(ff_backward_kernel, fast),
         (count,),
         [full_spec(vectors), w_ff_spec, row_spec((SEQ, D)), small_spec]
-        + [row_spec(a.shape[1:]) for a in (kept[8], kept[10])]
-        + [VMEM_SPEC] * 2,
+        + [row_spec(a.shape[1:]) for a in kept_ff],
         [row_spec((SEQ, D))] + [blocks(HALF_GRAD_COLS)] * 2 + [small_spec],
         [row_f32] + block_shapes(HALF_GRAD_COLS) + [small_shape],
         [
             pltpu.VMEM((D, 2048), F32),
             small_scratch,
-            pltpu.VMEM((count * SEQ, D), BF16),
-            pltpu.VMEM((count * SEQ, FF), BF16),
+            pltpu.VMEM((SEQ, D), BF16),
+            pltpu.VMEM((SEQ, FF), BF16),
             ONES_WORK,
             pltpu.VMEM((SEQ, FF), F32),
             pltpu.VMEM((SEQ, D), F32),
@@ -1129,21 +1156,30 @@
         4 * 10**9,
         10 * 10**6,
         "ff_backward",
-    )(*in_hbm([vectors]), w_ff, grad_stream, small_grads, kept[8], kept[10], *joined_ff)
-    ff_sums = add_cores(keep_ff, send_ff, wide, n_high)
-    other_sums = [jnp.concatenate(pair, axis=-1) for pair in zip(second_sums, ff_sums)]
-    others_received = swap_plane(other_sums)
-    kept_attention = (stream_first,) + tuple(kept[0:7])
+    )(*in_hbm([vectors]), w_ff, grad_stream, small_grads, *kept_ff)
+    ff_sums = add_cores(keep_ff, send_ff, wide, n_high, False)
+    other_sums = jnp.concatenate(
+        [
+            jnp.stack([a.astype(BF16) for a in second_sums]),
+            jnp.stack([a.astype(BF16) for a in ff_sums]),
+        ],
+        axis=-1,
+    )
+    plane = [[4 * h + p for p in range(4)] for h in range(n_high)]
+    others = lax.all_to_all(other_sums, "wide", 0, 0, axis_index_groups=plane)
+
+    kept_attention = (kept[14], kept[15]) + tuple(kept[0:7])
     joined_attention = [joined(kept[7]), joined(kept[11]), joined(hits)]
-    keep_rest, send_rest, small_grads = call(
+    keep_rest, send_rest, small_grads, scalars = call(
         functools.partial(attention_backward_kernel, fast),
         (count,),
-        [full_spec(vectors), w_attention_spec, row_spec((SEQ, D)), small_spec]
+        [full_spec(vectors), w_attention_spec, row_spec((SEQ, D)), small_spec, scalar_spec]
         + [row_spec(a.shape[1:]) for a in kept_attention]
         + [VMEM_SPEC] * 3
         + [ANY_SPEC],
-        [blocks(HALF_GRAD_COLS)] * 2 + [pl.BlockSpec((SMALL_ROWS, D), lambda i: (0, 0))],
-        block_shapes(HALF_GRAD_COLS) + [shaped((SMALL_ROWS, D), F32)],
+        [blocks(HALF_GRAD_COLS)] * 2
+        + [pl.BlockSpec((SMALL_ROWS, D), lambda i: (0, 0)), scalar_spec],
+        block_shapes(HALF_GRAD_COLS) + [shaped((SMALL_ROWS, D), F32), shaped((8, 128), F32)],
         [pltpu.VMEM((D, 2048), F32), small_scratch, pltpu.VMEM((KEYS, D), BF16)]
         + [pltpu.VMEM((count * SEQ, D), BF16)] * 2
         + [pltpu.VMEM((count * SEQ, 768), BF16)]
@@ -1157,14 +1193,17 @@
         w_attention,
         grad_mid,
         small_grads,
+        scalars,
         *kept_attention,
         *joined_attention,
-        other_sums[0],
-    )
-    others_received, keep_rest = lax.optimization_barrier((others_received, keep_rest))
-    rest_sums = add_cores(keep_rest, send_rest, wide, n_high)
+        other_sums,
+    )
+    others, scalars = lax.optimization_barrier((others, scalars))
+    rest_sums = add_cores(keep_rest, send_rest, wide, n_high, True)
     rest_received = swap_plane(rest_sums)
-    other_pieces = column_pieces(add_plane(other_sums[0], others_received))
+    others, rest_sums[0] = lax.optimization_barrier((others, rest_sums[0]))
+    others = [others[p].astype(F32) for p in range(4)]
+    other_pieces = column_pieces((others[0] + others[1]) + (others[2] + others[3]))
     rest_pieces = column_pieces(add_plane(rest_sums[0], rest_received))
 
     grad_rest, grad_others, table_part, small = call(

time: 159 us -> 184 us (1.16)
  local copies, waits for them, and re-layouts: 0.06 us -> 18.1 us
  waiting for transfers between devices: 22.7 us -> 27 us
  other arithmetic: 2.6 us -> 5.07 us
    unnamed x4 -> x52, local copies, waits for them, and re-layouts: 0.01 us -> 18.1 us
    all_to_all x0 -> x1, starting transfers between devices: none -> 4.33 us  [per_device(): others = lax.all_to_all(other_sums, 'wide', 0, 0, axis_index_groups=plane)]
    ppermute x38 -> x35, waiting for transfers between devices: 22.7 us -> 27 us  [swap(): return lax.ppermute(a, axis, [(i, i ^ distance) for i in range(size)])]
    ppermute x38 -> x35, starting transfers between devices: 37.7 us -> 34.6 us  [swap(): return lax.ppermute(a, axis, [(i, i ^ distance) for i in range(size)])]
  transfers between devices with their start and end apart: 38 -> 36, of which waited for: 15 -> 14; matrix products, arithmetic and copies ran while one was open for 1% -> 1% of each run, Pallas kernels for 25% -> 21%
where the time goes in v8:
time: 184 us; the launch traced here: 183 us
  Pallas kernels  79.9 us (43%)
  starting transfers between devices  39 us (21%)
  waiting for transfers between devices  27 us (15%)
  local copies, waits for them, and re-layouts  18.1 us (10%)
  blocking collectives  12.7 us (7%)
  other arithmetic  5.07 us (3%)
    pallas_call x1, Pallas kernels, per_device(): call(functools.partial(middle_kernel, fast), (count,), [meta_spec, row_sp...  35.8 us
    ppermute x35, starting transfers between devices, swap(): return lax.ppermute(a, axis, [(i, i ^ distance) for i in range(size)])  34.6 us
    ppermute x35, waiting for transfers between devices, swap(): return lax.ppermute(a, axis, [(i, i ^ distance) for i in range(size)])  27 us
    unnamed x52, local copies, waits for them, and re-layouts  18.1 us
    pallas_call x1, Pallas kernels, per_device(): call(functools.partial(first_forward_kernel, fast), (count,), [meta_spec]...  16.2 us
    all_to_all x1, blocking collectives, per_device(): gathered = lax.all_to_all(small, 'wide', 0, 0)  12.7 us
    pallas_call x1, Pallas kernels, per_device(): call(functools.partial(attention_backward_kernel, fast), (count,), [full_...  12.4 us
    pallas_call x1, Pallas kernels, per_device(): call(functools.partial(ff_backward_kernel, fast), (count,), [full_spec(ve...  6.44 us
  transfers between devices with their start and end apart: 36, of which 14 were waited for; matrix products, arithmetic and copies ran while one was open for 1% of the time, Pallas kernels for 21%

profile of v8, /device:TPU:0, one launch (start us, length us, event | category | flops | bytes accessed | tf_op | source)
XLA Modules:
  0.0 182.9 jit_solution(12162163033439716623)
XLA Ops:
  0.7 1.7 pack.1
  2.4 5.0 %collective-permute-start.2 = (bf16[16,2048]{1,0:T(8,128)(2,1)}, bf16[16,2048]{1,0:T(8,128)(2,1)S(1)}, u32[]{:S(2)}, u32[]{:S(2)}) collective-permute-start(bf16[16,2048]{1,0:T(8,128)(2,1)} %get-tuple-element.124), channel_id=1, source_target_pairs={{0,24},{2,26},{4,28},{6,30},{8,16},{10,18},{12,20},{14,22},{16,8},... | collective-permute-start | bytes 196616 | tf_op jit(solution)/shard_map/ppermute | solution.py:802
  8.0 3.3 %prepare.1 = (s32[4,352,128]{2,1,0:T(8,128)}, s32[4,32,128]{2,1,0:T(8,128)}) custom-call(s32[8]{0:T(128)} %games_ref.1, s32[8,16,20]{2,1,0:T(8,128)} %bitcast.74, s32[8,20]{1,0:T(8,128)} %actions.1, s32[8,20]{1,0:T(8,128)} %valid.1, s32[8,20]{1,0:T(8,128)} %rewards.1, s32[8,20]{1,0:T(8,128)} %ends.1), custom_call_target="tpu_custom_call" | custom-call | flops 1000000 | bytes 1000000 | tf_op jit(solution)/shard_map/prepare/pallas_call | solution.py:1024
  11.3 1.9 %collective-permute-done.1 = bf16[16,2048]{1,0:T(8,128)(2,1)S(1)} collective-permute-done((bf16[16,2048]{1,0:T(8,128)(2,1)}, bf16[16,2048]{1,0:T(8,128)(2,1)S(1)}, u32[]{:S(2)}, u32[]{:S(2)}) %collective-permute-start.1) | collective-permute-done | bytes 65568 | tf_op jit(solution)/shard_map/ppermute | solution.py:802
  14.2 1.6 collective-permute-start.13
  15.8 1.5 collective-permute-start.12
  17.3 2.6 %collective-permute-start.7 = (bf16[16,1792]{1,0:T(8,128)(2,1)}, bf16[16,1792]{1,0:T(8,128)(2,1)S(1)}, u32[]{:S(2)}, u32[]{:S(2)}) collective-permute-start(bf16[16,1792]{1,0:T(8,128)(2,1)} %get-tuple-element.129), channel_id=1, source_target_pairs={{0,24},{2,26},{4,28},{6,30},{8,16},{10,18},{12,20},{14,22},{16,8},... | collective-permute-start | bytes 172040 | tf_op jit(solution)/shard_map/ppermute | solution.py:802
  19.9 1.7 collective-permute-start.5
  21.7 1.3 collective-permute-done.13.refs_6_
  22.9 2.4 %collective-permute-start.8 = (bf16[4,16,2048]{2,1,0:T(8,128)(2,1)S(1)}, bf16[4,16,2048]{2,1,0:T(8,128)(2,1)S(1)}, u32[]{:S(2)}, u32[]{:S(2)}) collective-permute-start(bf16[4,16,2048]{2,1,0:T(8,128)(2,1)S(1)} %pad_maximum_fusion.refs_4_), channel_id=1, source_target_pairs={{0,6},{2,4},{4,2},{6,0},{8,14},{10,12},{12,10},{14,8},{16,22},{18,... | collective-permute-start | bytes 786440 | tf_op jit(solution)/shard_map/ppermute | solution.py:802
  26.8 4.9 %collective-permute-done.8.refs_7_ = bf16[4,16,2048]{2,1,0:T(8,128)(2,1)S(1)} collective-permute-done((bf16[4,16,2048]{2,1,0:T(8,128)(2,1)S(1)}, bf16[4,16,2048]{2,1,0:T(8,128)(2,1)S(1)}, u32[]{:S(2)}, u32[]{:S(2)}) %collective-permute-start.8) | collective-permute-done | bytes 262176 | tf_op jit(solution)/shard_map/ppermute | solution.py:802
  32.2 2.4 %collective-permute-start.11 = (bf16[4,16,1792]{2,1,0:T(8,128)(2,1)S(1)}, bf16[4,16,1792]{2,1,0:T(8,128)(2,1)S(1)}, u32[]{:S(2)}, u32[]{:S(2)}) collective-permute-start(bf16[4,16,1792]{2,1,0:T(8,128)(2,1)S(1)} %pad_maximum_fusion.1.refs_7_), channel_id=1, source_target_pairs={{0,6},{2,4},{4,2},{6,0},{8,14},{10,12},{12,10},{14,8},{16,22},{18,... | collective-permute-start | bytes 688136 | tf_op jit(solution)/shard_map/ppermute | solution.py:802
  35.7 16.2 %first_forward.1 = (bf16[256,1024]{1,0:T(8,128)(2,1)S(1)}, bf16[256,2048]{1,0:T(8,128)(2,1)S(1)}, bf16[256,128]{1,0:T(8,128)(2,1)S(1)}, f32[4,352,256]{2,1,0:T(8...) custom-call(s32[4,352,128]{2,1,0:T(8,128)} %get-tuple-element.121.re, ...), custom_call_target="tpu_custom_call" | custom-call | flops 4000000000 | bytes 20000000 | tf_op jit(solution)/shard_map/first_forward/pallas_call | solution.py:1055
  51.9 1.2 copy-done.5
  53.1 1.1 copy-done.7
  54.2 1.1 copy-done.9
  58.4 35.8 %middle.1 = (f32[4,352,256]{2,1,0:T(8,128)S(1)}, bf16[4,4,16,1792]{3,2,1,0:T(8,128)(2,1)S(1)}, bf16[4,4,16,1792]{3,2,1,0:T(8,128)(2,1)S(1)}, f32[32,8,256]{2,1,0:T(8,128)S(1)}, f32[8,128]{1,0:T(8,128)S(1)}) custom-call(s32[4,352,128]{2,1,0:T(8,128)} %get-tuple-element.121.refs_0_, s32[4,32,128]{2,1,0:T(8,128)} %get-tuple-element.122.refs_1_, ...), custom_call_target="tpu_custom_call" | custom-call | flops 15000000512 | bytes 20000000 | tf_op jit(solution)/shard_map/middle/pallas_call | solution.py:1085
  94.5 6.4 %ff_backward.1 = (f32[4,352,256]{2,1,0:T(8,128)S(1)}, bf16[4,4,16,1024]{3,2,1,0:T(8,128)(2,1)S(1)}, bf16[4,4,16,1024]{3,2,1,0:T(8,128)(2,1)S(1)}, f32[32,8,256]{2,1,0:T(8,128)S(1)}) custom-call(f32[14,256]{1,0:T(8,128)} %refs_18_.1, bf16[256,2048]{1,0:T(8,128)(2,1)S(1)} %get-tuple-element.141.refs_1_, f32[4,352,256]{2,1,0:T(8,128)S(1)} %get-tuple-element.142.refs_2_, ...), custom_call_target="tpu_custom_call" | custom-call | flops 4000000000 | bytes 10000000 | tf_op jit(solution)/shard_map/ff_backward/pallas_call | solution.py:1140
  101.3 1.7 collective-permute-done.22
  103.4 1.2 maximum_maximum_fusion.refs_17_
  104.6 4.3 %all-to-all-start = ((bf16[4,4,16,2816]{3,2,1,0:T(8,128)(2,1)}), bf16[4,4,16,2816]{3,2,1,0:T(8,128)(2,1)}, u32[]{:S(2)}, u32[]{:S(2)}) async-start(bf16[4,4,16,2816]{3,2,1,0:T(8,128)(2,1)} %maximum_maximum_fusion.refs_17_), calls=%async_computation | async-start | bytes 2883584 | tf_op jit(solution)/shard_map/all_to_all | solution.py:1169
  109.0 1.1 copy-done.2
  110.1 1.4 copy-done.4
  111.5 1.4 copy-done.6
  112.9 1.4 copy-done.8
  114.3 1.2 copy-done.10
  115.5 1.1 copy-done.12
  116.6 1.1 copy-done.14
  117.8 1.1 copy-done.16
  118.9 1.1 copy-done.18
  122.8 12.4 %attention_backward.1 = (bf16[4,4,16,1024]{3,2,1,0:T(8,128)(2,1)S(1)}, bf16[4,4,16,1024]{3,2,1,0:T(8,128)(2,1)S(1)}, f32[32,256]{1,0:T(8,128)}, f32[8,128]{1,0:T(8,128)S(1)}) custom-call(f32[14,256]{1,0:T(8,128)} %refs_18_.1, bf16[256,1024]{1,0:T(8,128)(2,1)S(1)} %copy-done.20, f32[4,352,256]{2,1,0:T(8,128)S(1)} %copy-done.4, ...), custom_call_target="tpu_custom_call" | custom-call | flops 6000000000 | bytes 20000000 | tf_op jit(solution)/shard_map/attention_backward/pallas_call | solution.py:1173
  135.4 1.7 collective-permute-done.23
  137.3 2.0 %collective-permute-start.24 = (bf16[4,16,1024]{2,1,0:T(8,128)(2,1)S(1)}, bf16[4,16,1024]{2,1,0:T(8,128)(2,1)S(1)}, u32[]{:S(2)}, u32[]{:S(2)}) collective-permute-start(bf16[4,16,1024]{2,1,0:T(8,128)(2,1)S(1)} %get-tuple-element.216), channel_id=1, source_target_pairs={{0,2},{2,0},{4,6},{6,4},{8,10},{10,8},{12,14},{14,12},{16,18},{18,... | collective-permute-start | bytes 393224 | tf_op jit(solution)/shard_map/ppermute | solution.py:802
  139.3 1.5 collective-permute-start.26
  140.9 2.6 %collective-permute-done.24 = bf16[4,16,1024]{2,1,0:T(8,128)(2,1)S(1)} collective-permute-done((bf16[4,16,1024]{2,1,0:T(8,128)(2,1)S(1)}, bf16[4,16,1024]{2,1,0:T(8,128)(2,1)S(1)}, u32[]{:S(2)}, u32[]{:S(2)}) %collective-permute-start.24) | collective-permute-done | bytes 131104 | tf_op jit(solution)/shard_map/ppermute | solution.py:802
  143.5 3.7 %collective-permute-done.26 = bf16[4,16,1024]{2,1,0:T(8,128)(2,1)S(1)} collective-permute-done((bf16[4,16,1024]{2,1,0:T(8,128)(2,1)S(1)}, bf16[4,16,1024]{2,1,0:T(8,128)(2,1)S(1)}, u32[]{:S(2)}, u32[]{:S(2)}) %collective-permute-start.26) | collective-permute-done | bytes 131104 | tf_op jit(solution)/shard_map/ppermute | solution.py:802
  147.2 1.4 collective-permute-done.25
  148.7 2.7 %collective-permute-start.29 = (bf16[16,1024]{1,0:T(8,128)(2,1)S(1)}, bf16[16,1024]{1,0:T(8,128)(2,1)S(1)}, u32[]{:S(2)}, u32[]{:S(2)}) collective-permute-start(bf16[16,1024]{1,0:T(8,128)(2,1)S(1)} %get-tuple-element.227), channel_id=1, source_target_pairs={{0,24},{2,26},{4,28},{6,30},{8,16},{10,18},{12,20},{14,22},{16,8},... | collective-permute-start | bytes 98312 | tf_op jit(solution)/shard_map/ppermute | solution.py:802
  151.4 1.7 collective-permute-start.27
  153.1 1.5 fusion.3
  154.6 2.7 %collective-permute-start.32 = (bf16[16,2816]{1,0:T(8,128)(2,1)S(1)}, bf16[16,2816]{1,0:T(8,128)(2,1)S(1)}, u32[]{:S(2)}, u32[]{:S(2)}) collective-permute-start(bf16[16,2816]{1,0:T(8,128)(2,1)S(1)} %get-tuple-element.224), channel_id=1, source_target_pairs={{0,24},{2,26},{4,28},{6,30},{8,16},{10,18},{12,20},{14,22},{16,8},... | collective-permute-start | bytes 270344 | tf_op jit(solution)/shard_map/ppermute | solution.py:802
  157.4 1.8 collective-permute-start.30
  159.2 2.8 %collective-permute-done.32.refs_7_ = bf16[16,2816]{1,0:T(8,128)(2,1)S(1)} collective-permute-done((bf16[16,2816]{1,0:T(8,128)(2,1)S(1)}, bf16[16,2816]{1,0:T(8,128)(2,1)S(1)}, u32[]{:S(2)}, u32[]{:S(2)}) %collective-permute-start.32) | collective-permute-done | bytes 90144 | tf_op jit(solution)/shard_map/ppermute | solution.py:802
  162.0 2.4 %collective-permute-done.31.refs_6_ = bf16[16,2816]{1,0:T(8,128)(2,1)S(1)} collective-permute-done((bf16[16,2816]{1,0:T(8,128)(2,1)S(1)}, bf16[16,2816]{1,0:T(8,128)(2,1)S(1)}, u32[]{:S(2)}, u32[]{:S(2)}) %collective-permute-start.31) | collective-permute-done | bytes 90144 | tf_op jit(solution)/shard_map/ppermute | solution.py:802
  164.4 1.5 finish.1
  166.0 12.7 %all_to_all.10.gathered = f32[16,24,128]{2,1,0:T(8,128)S(1)} all-to-all(f32[16,24,128]{2,1,0:T(8,128)} %get-tuple-element.177), channel_id=1, replica_groups=mesh['wide'=16,'narrow'=2] {'wide'}, dimensions={0} | all-to-all | bytes 393216 | tf_op jit(solution)/shard_map/all_to_all | solution.py:1226
  179.2 1.1 collective-permute-done.33.swapped
  180.2 2.5 %adam.1 = (f32[1,1]{1,0:T(1,128)}, f32[1,1]{1,0:T(1,128)}, f32[1,1]{1,0:T(1,128)}, f32[16,896]{1,0:T(8,128)}, f32[16,896]{1,0:T(8,128)}, /*index=5*/f32[16,896]{...) custom-call(f32[16,1024]{1,0:T(8,128)} %get-tuple-element.174.rest, ...), custom_call_target="tpu_custom_call" | custom-call | flops 1000000 | bytes 1000000 | tf_op jit(solution)/shard_map/adam/pallas_call | solution.py:1235
  (97 shorter events, 12.5 us)
Async XLA Ops:
  2.4 8.9 %collective-permute-start.2 = (bf16[16,2048]{1,0:T(8,128)(2,1)}, bf16[16,2048]{1,0:T(8,128)(2,1)S(1)}, u32[]{:S(2)}, u32[]{:S(2)}) collective-permute-start(bf16[16,2048]{1,0:T(8,128)(2,1)} %get-tuple-element.124), channel_id=1, source_target_pairs={{0,24},{2,26},{4,28},{6,30},{8,16},{10,18},{12,20},{14,22},{16,8},... | collective-permute-start | bytes 196616 | tf_op jit(solution)/shard_map/ppermute | solution.py:802
  7.4 5.8 %collective-permute-start.1 = (bf16[16,2048]{1,0:T(8,128)(2,1)}, bf16[16,2048]{1,0:T(8,128)(2,1)S(1)}, u32[]{:S(2)}, u32[]{:S(2)}) collective-permute-start(bf16[16,2048]{1,0:T(8,128)(2,1)} %get-tuple-element.124), channel_id=1, source_target_pairs={{0,16},{2,18},{4,20},{6,22},{8,24},{10,26},{12,28},{14,30},{16,0},... | collective-permute-start | bytes 196616 | tf_op jit(solution)/shard_map/ppermute | solution.py:802
  7.5 5.8 %collective-permute-start = (bf16[16,2048]{1,0:T(8,128)(2,1)}, bf16[16,2048]{1,0:T(8,128)(2,1)S(1)}, u32[]{:S(2)}, u32[]{:S(2)}) collective-permute-start(bf16[16,2048]{1,0:T(8,128)(2,1)} %get-tuple-element.124), channel_id=1, source_target_pairs={{0,8},{2,10},{4,12},{6,14},{8,0},{10,2},{12,4},{14,6},{16,24},{18,... | collective-permute-start | bytes 196616 | tf_op jit(solution)/shard_map/ppermute | solution.py:802
  8.0 3.3 %collective-permute-start.3 = (f32[2,512]{1,0:T(2,128)}, f32[2,512]{1,0:T(2,128)S(1)}, u32[]{:S(2)}, u32[]{:S(2)}) collective-permute-start(f32[2,512]{1,0:T(2,128)} %refs_12_.1), channel_id=1, source_target_pairs={{0,1},{1,0},{2,3},{3,2},{4,5},{5,4},{6,7},{7,6},{8,9},{9,8},{10,11... | collective-permute-start | bytes 12296 | tf_op jit(solution)/shard_map/ppermute | solution.py:802
  11.3 24.4 %copy-start.25 = (f32[2,512]{1,0:T(2,128)}, f32[2,512]{1,0:T(2,128)S(1)}, u32[]{:S(2)}) copy-start(f32[2,512]{1,0:T(2,128)S(1)} %collective-permute-done.3.refs_3_.refs_4_) | copy-start | bytes 12292
  14.1 3.2 %collective-permute-start.4 = (bf16[4,16,2048]{2,1,0:T(8,128)(2,1)S(1)}, bf16[4,16,2048]{2,1,0:T(8,128)(2,1)S(1)}, u32[]{:S(2)}, u32[]{:S(2)}) collective-permute-start(bf16[4,16,2048]{2,1,0:T(8,128)(2,1)S(1)} %pad_maximum_fusion.refs_4_), channel_id=1, source_target_pairs={{0,1},{1,0},{2,3},{3,2},{4,5},{5,4},{6,7},{7,6},{8,9},{9,8},{10,11... | collective-permute-start | bytes 786440 | tf_op jit(solution)/shard_map/ppermute | solution.py:802
  14.2 8.7 %collective-permute-start.13 = (bf16[4,16,2048]{2,1,0:T(8,128)(2,1)S(1)}, bf16[4,16,2048]{2,1,0:T(8,128)(2,1)S(1)}, u32[]{:S(2)}, u32[]{:S(2)}) collective-permute-start(bf16[4,16,2048]{2,1,0:T(8,128)(2,1)S(1)} %pad_maximum_fusion.refs_4_), channel_id=1, source_target_pairs={{0,4},{2,6},{4,0},{6,2},{8,12},{10,14},{12,8},{14,10},{16,20},{18,... | collective-permute-start | bytes 786440 | tf_op jit(solution)/shard_map/ppermute | solution.py:802
  15.8 9.6 %collective-permute-start.12 = (bf16[4,16,2048]{2,1,0:T(8,128)(2,1)S(1)}, bf16[4,16,2048]{2,1,0:T(8,128)(2,1)S(1)}, u32[]{:S(2)}, u32[]{:S(2)}) collective-permute-start(bf16[4,16,2048]{2,1,0:T(8,128)(2,1)S(1)} %pad_maximum_fusion.refs_4_), channel_id=1, source_target_pairs={{0,2},{2,0},{4,6},{6,4},{8,10},{10,8},{12,14},{14,12},{16,18},{18,... | collective-permute-start | bytes 786440 | tf_op jit(solution)/shard_map/ppermute | solution.py:802
  17.3 8.1 %collective-permute-start.7 = (bf16[16,1792]{1,0:T(8,128)(2,1)}, bf16[16,1792]{1,0:T(8,128)(2,1)S(1)}, u32[]{:S(2)}, u32[]{:S(2)}) collective-permute-start(bf16[16,1792]{1,0:T(8,128)(2,1)} %get-tuple-element.129), channel_id=1, source_target_pairs={{0,24},{2,26},{4,28},{6,30},{8,16},{10,18},{12,20},{14,22},{16,8},... | collective-permute-start | bytes 172040 | tf_op jit(solution)/shard_map/ppermute | solution.py:802
  19.9 6.0 %collective-permute-start.6 = (bf16[16,1792]{1,0:T(8,128)(2,1)}, bf16[16,1792]{1,0:T(8,128)(2,1)S(1)}, u32[]{:S(2)}, u32[]{:S(2)}) collective-permute-start(bf16[16,1792]{1,0:T(8,128)(2,1)} %get-tuple-element.129), channel_id=1, source_target_pairs={{0,16},{2,18},{4,20},{6,22},{8,24},{10,26},{12,28},{14,30},{16,0},... | collective-permute-start | bytes 172040 | tf_op jit(solution)/shard_map/ppermute | solution.py:802
  19.9 6.0 %collective-permute-start.5 = (bf16[16,1792]{1,0:T(8,128)(2,1)}, bf16[16,1792]{1,0:T(8,128)(2,1)S(1)}, u32[]{:S(2)}, u32[]{:S(2)}) collective-permute-start(bf16[16,1792]{1,0:T(8,128)(2,1)} %get-tuple-element.129), channel_id=1, source_target_pairs={{0,8},{2,10},{4,12},{6,14},{8,0},{10,2},{12,4},{14,6},{16,24},{18,... | collective-permute-start | bytes 172040 | tf_op jit(solution)/shard_map/ppermute | solution.py:802
  22.9 8.8 %collective-permute-start.8 = (bf16[4,16,2048]{2,1,0:T(8,128)(2,1)S(1)}, bf16[4,16,2048]{2,1,0:T(8,128)(2,1)S(1)}, u32[]{:S(2)}, u32[]{:S(2)}) collective-permute-start(bf16[4,16,2048]{2,1,0:T(8,128)(2,1)S(1)} %pad_maximum_fusion.refs_4_), channel_id=1, source_target_pairs={{0,6},{2,4},{4,2},{6,0},{8,14},{10,12},{12,10},{14,8},{16,22},{18,... | collective-permute-start | bytes 786440 | tf_op jit(solution)/shard_map/ppermute | solution.py:802
  25.4 9.3 %collective-permute-start.15 = (bf16[4,16,2048]{2,1,0:T(8,128)(2,1)S(1)}, bf16[4,16,2048]{2,1,0:T(8,128)(2,1)S(1)}, u32[]{:S(2)}, u32[]{:S(2)}) collective-permute-start(bf16[4,16,2048]{2,1,0:T(8,128)(2,1)S(1)} %collective-permute-done.13.refs_6_), channel_id=1, source_target_pairs={{0,1},{1,0},{2,3},{3,2},{4,5},{5,4},{6,7},{7,6},{8,9},{9,8},{10,11... | collective-permute-start | bytes 786440 | tf_op jit(solution)/shard_map/ppermute | solution.py:802
  25.4 9.8 %collective-permute-start.14 = (bf16[4,16,2048]{2,1,0:T(8,128)(2,1)S(1)}, bf16[4,16,2048]{2,1,0:T(8,128)(2,1)S(1)}, u32[]{:S(2)}, u32[]{:S(2)}) collective-permute-start(bf16[4,16,2048]{2,1,0:T(8,128)(2,1)S(1)} %collective-permute-done.12.refs_5_), channel_id=1, source_target_pairs={{0,1},{1,0},{2,3},{3,2},{4,5},{5,4},{6,7},{7,6},{8,9},{9,8},{10,11... | collective-permute-start | bytes 786440 | tf_op jit(solution)/shard_map/ppermute | solution.py:802
  31.7 4.0 %collective-permute-start.16 = (bf16[4,16,2048]{2,1,0:T(8,128)(2,1)S(1)}, bf16[4,16,2048]{2,1,0:T(8,128)(2,1)S(1)}, u32[]{:S(2)}, u32[]{:S(2)}) collective-permute-start(bf16[4,16,2048]{2,1,0:T(8,128)(2,1)S(1)} %collective-permute-done.8.refs_7_), channel_id=1, source_target_pairs={{0,1},{1,0},{2,3},{3,2},{4,5},{5,4},{6,7},{7,6},{8,9},{9,8},{10,11... | collective-permute-start | bytes 786440 | tf_op jit(solution)/shard_map/ppermute | solution.py:802
  31.7 25.2 %collective-permute-start.17 = (bf16[4,16,1792]{2,1,0:T(8,128)(2,1)S(1)}, bf16[4,16,1792]{2,1,0:T(8,128)(2,1)S(1)}, u32[]{:S(2)}, u32[]{:S(2)}) collective-permute-start(bf16[4,16,1792]{2,1,0:T(8,128)(2,1)S(1)} %pad_maximum_fusion.1.refs_7_), channel_id=1, source_target_pairs={{0,1},{1,0},{2,3},{3,2},{4,5},{5,4},{6,7},{7,6},{8,9},{9,8},{10,11... | collective-permute-start | bytes 688136 | tf_op jit(solution)/shard_map/ppermute | solution.py:802
  32.2 24.0 %collective-permute-start.11 = (bf16[4,16,1792]{2,1,0:T(8,128)(2,1)S(1)}, bf16[4,16,1792]{2,1,0:T(8,128)(2,1)S(1)}, u32[]{:S(2)}, u32[]{:S(2)}) collective-permute-start(bf16[4,16,1792]{2,1,0:T(8,128)(2,1)S(1)} %pad_maximum_fusion.1.refs_7_), channel_id=1, source_target_pairs={{0,6},{2,4},{4,2},{6,0},{8,14},{10,12},{12,10},{14,8},{16,22},{18,... | collective-permute-start | bytes 688136 | tf_op jit(solution)/shard_map/ppermute | solution.py:802
  34.7 21.5 %collective-permute-start.10 = (bf16[4,16,1792]{2,1,0:T(8,128)(2,1)S(1)}, bf16[4,16,1792]{2,1,0:T(8,128)(2,1)S(1)}, u32[]{:S(2)}, u32[]{:S(2)}) collective-permute-start(bf16[4,16,1792]{2,1,0:T(8,128)(2,1)S(1)} %pad_maximum_fusion.1.refs_7_), channel_id=1, source_target_pairs={{0,4},{2,6},{4,0},{6,2},{8,12},{10,14},{12,8},{14,10},{16,20},{18,... | collective-permute-start | bytes 688136 | tf_op jit(solution)/shard_map/ppermute | solution.py:802
  35.2 21.0 %collective-permute-start.9 = (bf16[4,16,1792]{2,1,0:T(8,128)(2,1)S(1)}, bf16[4,16,1792]{2,1,0:T(8,128)(2,1)S(1)}, u32[]{:S(2)}, u32[]{:S(2)}) collective-permute-start(bf16[4,16,1792]{2,1,0:T(8,128)(2,1)S(1)} %pad_maximum_fusion.1.refs_7_), channel_id=1, source_target_pairs={{0,2},{2,0},{4,6},{6,4},{8,10},{10,8},{12,14},{14,12},{16,18},{18,... | collective-permute-start | bytes 688136 | tf_op jit(solution)/shard_map/ppermute | solution.py:802
  56.2 38.0 %copy-start.1 = (bf16[4,352,256]{2,1,0:T(8,128)(2,1)}, bf16[4,352,256]{2,1,0:T(8,128)(2,1)S(1)}, u32[]{:S(2)}) copy-start(bf16[4,352,256]{2,1,0:T(8,128)(2,1)S(1)} %get-tuple-element.165) | copy-start | bytes 2162692
  56.2 38.1 %copy-start.13 = (bf16[4,256,384]{2,1,0:T(8,128)(2,1)}, bf16[4,256,384]{2,1,0:T(8,128)(2,1)S(1)}, u32[]{:S(2)}) copy-start(bf16[4,256,384]{2,1,0:T(8,128)(2,1)S(1)} %get-tuple-element.163.refs_13_) | copy-start | bytes 2359300
  56.2 38.1 %copy-start.15 = (bf16[4,352,256]{2,1,0:T(8,128)(2,1)}, bf16[4,352,256]{2,1,0:T(8,128)(2,1)S(1)}, u32[]{:S(2)}) copy-start(bf16[4,352,256]{2,1,0:T(8,128)(2,1)S(1)} %get-tuple-element.155.refs_5_) | copy-start | bytes 2162692
  56.2 38.1 %copy-start.17 = (f32[4,352,128]{2,1,0:T(8,128)}, f32[4,352,128]{2,1,0:T(8,128)S(1)}, u32[]{:S(2)}) copy-start(f32[4,352,128]{2,1,0:T(8,128)S(1)} %get-tuple-element.156.refs_6_) | copy-start | bytes 2162692
  56.2 38.1 %copy-start.19 = (bf16[256,1024]{1,0:T(8,128)(2,1)}, bf16[256,1024]{1,0:T(8,128)(2,1)S(1)}, u32[]{:S(2)}) copy-start(bf16[256,1024]{1,0:T(8,128)(2,1)S(1)} %get-tuple-element.151.refs_1_) | copy-start | bytes 1572868
  56.2 38.1 %copy-start.21 = (bf16[4,128,512]{2,1,0:T(8,128)(2,1)}, bf16[4,128,512]{2,1,0:T(8,128)(2,1)S(1)}, u32[]{:S(2)}) copy-start(bf16[4,128,512]{2,1,0:T(8,128)(2,1)S(1)} %get-tuple-element.159.refs_9_) | copy-start | bytes 1572868
  56.2 1.6 collective-permute-start.18
  56.3 1.8 collective-permute-start.19
  56.8 1.6 collective-permute-start.20
  94.3 6.7 %copy-start.23 = (f32[8,128]{1,0:T(8,128)}, f32[8,128]{1,0:T(8,128)S(1)}, u32[]{:S(2)}) copy-start(f32[8,128]{1,0:T(8,128)S(1)} %get-tuple-element.154.refs_4_) | copy-start | bytes 12292
  94.3 8.9 %collective-permute-start.21 = (bf16[4,4,16,1792]{3,2,1,0:T(8,128)(2,1)S(1)}, bf16[4,4,16,1792]{3,2,1,0:T(8,128)(2,1)S(1)}, u32[]{:S(2)}, u32[]{:S(2)}) collective-permute-start(bf16[4,4,16,1792]{3,2,1,0:T(8,128)(2,1)S(1)} %get-tuple-element.140), channel_id=1, source_target_pairs={{0,1},{1,0},{2,3},{3,2},{4,5},{5,4},{6,7},{7,6},{8,9},{9,8},{10,11... | collective-permute-start | bytes 2752520 | tf_op jit(solution)/shard_map/ppermute | solution.py:802
  101.0 2.4 %copy-start.3 = (f32[4,352,256]{2,1,0:T(8,128)}, f32[4,352,256]{2,1,0:T(8,128)S(1)}, u32[]{:S(2)}) copy-start(f32[4,352,256]{2,1,0:T(8,128)S(1)} %get-tuple-element.152.refs_2_) | copy-start | bytes 4325380
  101.0 2.0 %collective-permute-start.22 = (bf16[4,4,16,1024]{3,2,1,0:T(8,128)(2,1)S(1)}, bf16[4,4,16,1024]{3,2,1,0:T(8,128)(2,1)S(1)}, u32[]{:S(2)}, u32[]{:S(2)}) collective-permute-start(bf16[4,4,16,1024]{3,2,1,0:T(8,128)(2,1)S(1)} %get-tuple-element.150), channel_id=1, source_target_pairs={{0,1},{1,0},{2,3},{3,2},{4,5},{5,4},{6,7},{7,6},{8,9},{9,8},{10,11... | collective-permute-start | bytes 1572872 | tf_op jit(solution)/shard_map/ppermute | solution.py:802
  104.6 36.2 %all-to-all-start = ((bf16[4,4,16,2816]{3,2,1,0:T(8,128)(2,1)}), bf16[4,4,16,2816]{3,2,1,0:T(8,128)(2,1)}, u32[]{:S(2)}, u32[]{:S(2)}) async-start(bf16[4,4,16,2816]{3,2,1,0:T(8,128)(2,1)} %maximum_maximum_fusion.refs_17_), calls=%async_computation | async-start | bytes 2883584 | tf_op jit(solution)/shard_map/all_to_all | solution.py:1169
  111.5 1.4 copy-start.6
  112.9 1.4 copy-start.8
  135.2 2.1 %copy-start = (f32[8,128]{1,0:T(8,128)}, f32[8,128]{1,0:T(8,128)S(1)}, u32[]{:S(2)}) copy-start(f32[8,128]{1,0:T(8,128)S(1)} %get-tuple-element.173.refs_8_) | copy-start | bytes 12292
  135.2 1.9 %collective-permute-start.23 = (bf16[4,4,16,1024]{3,2,1,0:T(8,128)(2,1)S(1)}, bf16[4,4,16,1024]{3,2,1,0:T(8,128)(2,1)S(1)}, u32[]{:S(2)}, u32[]{:S(2)}) collective-permute-start(bf16[4,4,16,1024]{3,2,1,0:T(8,128)(2,1)S(1)} %get-tuple-element.170), channel_id=1, source_target_pairs={{0,1},{1,0},{2,3},{3,2},{4,5},{5,4},{6,7},{7,6},{8,9},{9,8},{10,11... | collective-permute-start | bytes 1572872 | tf_op jit(solution)/shard_map/ppermute | solution.py:802
  137.3 6.2 %collective-permute-start.24 = (bf16[4,16,1024]{2,1,0:T(8,128)(2,1)S(1)}, bf16[4,16,1024]{2,1,0:T(8,128)(2,1)S(1)}, u32[]{:S(2)}, u32[]{:S(2)}) collective-permute-start(bf16[4,16,1024]{2,1,0:T(8,128)(2,1)S(1)} %get-tuple-element.216), channel_id=1, source_target_pairs={{0,2},{2,0},{4,6},{6,4},{8,10},{10,8},{12,14},{14,12},{16,18},{18,... | collective-permute-start | bytes 393224 | tf_op jit(solution)/shard_map/ppermute | solution.py:802
  139.3 7.9 %collective-permute-start.26 = (bf16[4,16,1024]{2,1,0:T(8,128)(2,1)S(1)}, bf16[4,16,1024]{2,1,0:T(8,128)(2,1)S(1)}, u32[]{:S(2)}, u32[]{:S(2)}) collective-permute-start(bf16[4,16,1024]{2,1,0:T(8,128)(2,1)S(1)} %get-tuple-element.217), channel_id=1, source_target_pairs={{0,6},{2,4},{4,2},{6,0},{8,14},{10,12},{12,10},{14,8},{16,22},{18,... | collective-permute-start | bytes 393224 | tf_op jit(solution)/shard_map/ppermute | solution.py:802
  140.8 7.8 %collective-permute-start.25 = (bf16[4,16,1024]{2,1,0:T(8,128)(2,1)S(1)}, bf16[4,16,1024]{2,1,0:T(8,128)(2,1)S(1)}, u32[]{:S(2)}, u32[]{:S(2)}) collective-permute-start(bf16[4,16,1024]{2,1,0:T(8,128)(2,1)S(1)} %get-tuple-element.218), channel_id=1, source_target_pairs={{0,4},{2,6},{4,0},{6,2},{8,12},{10,14},{12,8},{14,10},{16,20},{18,... | collective-permute-start | bytes 393224 | tf_op jit(solution)/shard_map/ppermute | solution.py:802
  148.7 8.7 %collective-permute-start.29 = (bf16[16,1024]{1,0:T(8,128)(2,1)S(1)}, bf16[16,1024]{1,0:T(8,128)(2,1)S(1)}, u32[]{:S(2)}, u32[]{:S(2)}) collective-permute-start(bf16[16,1024]{1,0:T(8,128)(2,1)S(1)} %get-tuple-element.227), channel_id=1, source_target_pairs={{0,24},{2,26},{4,28},{6,30},{8,16},{10,18},{12,20},{14,22},{16,8},... | collective-permute-start | bytes 98312 | tf_op jit(solution)/shard_map/ppermute | solution.py:802
  151.4 7.8 %collective-permute-start.28 = (bf16[16,1024]{1,0:T(8,128)(2,1)S(1)}, bf16[16,1024]{1,0:T(8,128)(2,1)S(1)}, u32[]{:S(2)}, u32[]{:S(2)}) collective-permute-start(bf16[16,1024]{1,0:T(8,128)(2,1)S(1)} %get-tuple-element.228), channel_id=1, source_target_pairs={{0,16},{2,18},{4,20},{6,22},{8,24},{10,26},{12,28},{14,30},{16,0},... | collective-permute-start | bytes 98312 | tf_op jit(solution)/shard_map/ppermute | solution.py:802
  151.4 7.8 %collective-permute-start.27 = (bf16[16,1024]{1,0:T(8,128)(2,1)S(1)}, bf16[16,1024]{1,0:T(8,128)(2,1)S(1)}, u32[]{:S(2)}, u32[]{:S(2)}) collective-permute-start(bf16[16,1024]{1,0:T(8,128)(2,1)S(1)} %get-tuple-element.229), channel_id=1, source_target_pairs={{0,8},{2,10},{4,12},{6,14},{8,0},{10,2},{12,4},{14,6},{16,24},{18,... | collective-permute-start | bytes 98312 | tf_op jit(solution)/shard_map/ppermute | solution.py:802
  154.6 7.3 %collective-permute-start.32 = (bf16[16,2816]{1,0:T(8,128)(2,1)S(1)}, bf16[16,2816]{1,0:T(8,128)(2,1)S(1)}, u32[]{:S(2)}, u32[]{:S(2)}) collective-permute-start(bf16[16,2816]{1,0:T(8,128)(2,1)S(1)} %get-tuple-element.224), channel_id=1, source_target_pairs={{0,24},{2,26},{4,28},{6,30},{8,16},{10,18},{12,20},{14,22},{16,8},... | collective-permute-start | bytes 270344 | tf_op jit(solution)/shard_map/ppermute | solution.py:802
  157.3 7.1 %collective-permute-start.31 = (bf16[16,2816]{1,0:T(8,128)(2,1)S(1)}, bf16[16,2816]{1,0:T(8,128)(2,1)S(1)}, u32[]{:S(2)}, u32[]{:S(2)}) collective-permute-start(bf16[16,2816]{1,0:T(8,128)(2,1)S(1)} %get-tuple-element.225), channel_id=1, source_target_pairs={{0,16},{2,18},{4,20},{6,22},{8,24},{10,26},{12,28},{14,30},{16,0},... | collective-permute-start | bytes 270344 | tf_op jit(solution)/shard_map/ppermute | solution.py:802
  157.4 7.0 %collective-permute-start.30 = (bf16[16,2816]{1,0:T(8,128)(2,1)S(1)}, bf16[16,2816]{1,0:T(8,128)(2,1)S(1)}, u32[]{:S(2)}, u32[]{:S(2)}) collective-permute-start(bf16[16,2816]{1,0:T(8,128)(2,1)S(1)} %get-tuple-element.226), channel_id=1, source_target_pairs={{0,8},{2,10},{4,12},{6,14},{8,0},{10,2},{12,4},{14,6},{16,24},{18,... | collective-permute-start | bytes 270344 | tf_op jit(solution)/shard_map/ppermute | solution.py:802
  178.7 1.6 collective-permute-start.34
  178.7 1.6 collective-permute-start.33
  (14 other events, 15.2 us)

commit v9 on v8

--- a/solution.py
+++ b/solution.py
@@ -161,15 +161,13 @@
         lax.fori_loop(0, 4, block, 0)
 
 
-def disperse(g_ref, place, keep_ref, send_ref, halves, scaled=True, by_distance=True):
+def disperse(g_ref, place, keep_ref, send_ref, halves, scaled=True):
     me, core, _ = place
     is_first = core == 0
 
     def block(i, _):
         p, z = i >> 2, i & 3
-        spot = 4 * z + p
-        owner = me ^ spot if by_distance else spot ^ (me & ~3)
-        row = pl.multiple_of(owner * 16, 16)
+        row = pl.multiple_of((me ^ (4 * z + p)) * 16, 16)
         for src, width, dest in halves:
             low = g_ref[pl.ds(row, 16), dest : dest + width]
             high = g_ref[pl.ds(row, 16), dest + width : dest + 2 * width]
@@ -574,7 +572,7 @@
 
     @pl.when(step == pl.num_programs(0) - 1)
     def _():
-        disperse(g_ref, place, keep_ref, send_ref, HALF_SECOND, True, False)
+        disperse(g_ref, place, keep_ref, send_ref, HALF_SECOND)
         side = jnp.transpose(g_ref[:, COL_SECOND:])
         for i in range(5):
             v_ref[SMALL_SIDE + i, 0:1] = side[i : i + 1]
@@ -620,24 +618,23 @@
 
     @pl.when(step == pl.num_programs(0) - 1)
     def _():
-        disperse(g_ref, places(fast), keep_ref, send_ref, HALF_GRAD_FF, False, False)
+        disperse(g_ref, places(fast), keep_ref, send_ref, HALF_GRAD_FF, False)
         v_out[...] = v_ref[...]
 
 
 def attention_backward_kernel(fast, *refs):
-    vec_ref, w_ref, mid_ref, v_in, scalar_in = refs[0:5]
-    kept = [ref.at[0] for ref in refs[5:14]]
-    o_all, a_all, hits_all = refs[14:17]
-    keep_ref, send_ref, v_out, scalar_out = refs[18:22]
-    g_ref, v_ref, mid16_ref, mid16_all, out16_all, dqkv_all = refs[22:28]
-    work = list(refs[28:36])
+    vec_ref, w_ref, mid_ref, v_in = refs[0:4]
+    kept = [ref.at[0] for ref in refs[4:13]]
+    o_all, a_all, hits_all = refs[13:16]
+    keep_ref, send_ref, v_out = refs[17:20]
+    g_ref, v_ref, mid16_ref, mid16_all, out16_all, dqkv_all = refs[20:26]
+    work = list(refs[26:34])
     dost_ref, qst_ref, proj_ref = work[0], work[1], work[6]
     step = pl.program_id(0)
 
     @pl.when(step == 0)
     def _():
         v_ref[...] = v_in[...]
-        scalar_out[...] = scalar_in[...]
         dost_ref[...] = jnp.zeros(dost_ref.shape, BF16)
         qst_ref[...] = jnp.zeros(qst_ref.shape, BF16)
         proj_ref[...] = jnp.transpose(w_ref[:, COL_PROJ : COL_PROJ + 256])
@@ -715,13 +712,16 @@
     extra = column_sum(jnp.sum(small * small, axis=1, keepdims=True))
     square = square - jnp.where(places(fast)[1] == 0, 0.0, extra)
     out_table[...] = out_rest[:, 512:1024]
-    rows = small.shape[0]
     lane = lax.broadcasted_iota(jnp.int32, (8, 128), 1)
-    top = lax.broadcasted_iota(jnp.int32, (8, 128), 0) == 0
-    scalars = scalar_ref[...] + jnp.where(top & (lane == 2), square, 0.0)
+    row = lax.broadcasted_iota(jnp.int32, (8, 128), 0)
+    message = scalar_ref[...] + jnp.where((row == 0) & (lane == 2), square, 0.0)
+    if fast:
+        spot = places(fast)[2] & 3
+        part = jnp.where(spot & 1 == 0, small[0:4], small[4:8])
+        part = jnp.where(spot & 2 == 0, part, jnp.where(spot & 1 == 0, small[8:12], small[12:16]))
+        message = jnp.concatenate([part, message[0:4]], axis=0)
     for i in range(out_small.shape[0]):
-        out_small[i, 0:rows] = small
-        out_small[i, rows : rows + 8] = scalars
+        out_small[i] = message
 
 
 def adam_rule(weight, moment, second, gradient, step_rate, decay_rate):
@@ -740,7 +740,11 @@
     _, core, wide = places(fast)
     is_first = core == 0
     if fast:
-        quarters = [jnp.where(is_first, beside[4 * z], gathered[4 * z]) for z in range(4)]
+        small_parts = jnp.where(is_first, beside[...], gathered[...])
+        quarters = [
+            jnp.concatenate([small_parts[4 * z + p, 0:4] for p in range(4)], axis=0)
+            for z in range(4)
+        ]
     else:
         quarters = [refs[0][z] for z in range(4)]
         refs = refs[1:]
@@ -753,9 +757,10 @@
         small_ref[8 * z : 8 * z + 8, 128:256] = quarters[z][8:16]
     sums = []
     for source in (gathered, beside):
-        total = source[0, rows : rows + 1]
+        line = 4 if fast else 0
+        total = source[0, line : line + 1]
         for i in range(1, source.shape[0]):
-            total = total + source[i, rows : rows + 1]
+            total = total + source[i, line : line + 1]
         sums.append(total)
     scalars = sums[0] + sums[1]
     small = small_ref[...]
@@ -823,20 +828,18 @@
     return [whole[:, p] for p in range(4)]
 
 
-def in_pieces(blocks, wide, n_high, by_distance):
+def in_pieces(blocks, wide, n_high):
     cols = blocks.shape[-1]
     if n_high == 4:
         return blocks
     rows = 64 // n_high
     whole = blocks.transpose(1, 0, 2, 3).reshape(4 * n_high, rows, cols)
-    order = jnp.arange(4 * n_high)
-    whole = whole[wide ^ order if by_distance else order ^ (wide & ~3)]
+    whole = whole[wide ^ jnp.arange(4 * n_high)]
     return whole.reshape(n_high, 4, rows, cols).transpose(1, 0, 2, 3)
 
 
-def add_cores(keep, send, wide, n_high, by_distance):
-    keep = in_pieces(keep, wide, n_high, by_distance)
-    send = in_pieces(send, wide, n_high, by_distance)
+def add_cores(keep, send, wide, n_high):
+    keep, send = in_pieces(keep, wide, n_high), in_pieces(send, wide, n_high)
     received = swap(send, "narrow", 1)
     return [keep[p].astype(F32) + received[p].astype(F32) for p in range(4)]
 
@@ -883,10 +886,10 @@
 VMEM_MIB = {
     "pack": 58,
     "prepare": 58,
-    "first_forward": 26,
-    "middle": 32,
-    "ff_backward": 20,
-    "attention_backward": 26,
+    "first_forward": 22,
+    "middle": 28,
+    "ff_backward": 15,
+    "attention_backward": 22,
     "finish": 58,
     "adam": 58,
 }
@@ -1131,7 +1134,7 @@
         stream,
         *resident(second_parts),
     )
-    second_sums = add_cores(keep_second, send_second, wide, n_high, False)
+    second_sums = add_cores(keep_second, send_second, wide, n_high)
 
     def joined(a):
         return a.reshape((count * a.shape[1],) + a.shape[2:])
@@ -1157,29 +1160,20 @@
         10 * 10**6,
         "ff_backward",
     )(*in_hbm([vectors]), w_ff, grad_stream, small_grads, *kept_ff)
-    ff_sums = add_cores(keep_ff, send_ff, wide, n_high, False)
-    other_sums = jnp.concatenate(
-        [
-            jnp.stack([a.astype(BF16) for a in second_sums]),
-            jnp.stack([a.astype(BF16) for a in ff_sums]),
-        ],
-        axis=-1,
-    )
-    plane = [[4 * h + p for p in range(4)] for h in range(n_high)]
-    others = lax.all_to_all(other_sums, "wide", 0, 0, axis_index_groups=plane)
-
+    ff_sums = add_cores(keep_ff, send_ff, wide, n_high)
+    other_sums = [jnp.concatenate(pair, axis=-1) for pair in zip(second_sums, ff_sums)]
+    others_received = swap_plane(other_sums)
     kept_attention = (kept[14], kept[15]) + tuple(kept[0:7])
     joined_attention = [joined(kept[7]), joined(kept[11]), joined(hits)]
-    keep_rest, send_rest, small_grads, scalars = call(
+    keep_rest, send_rest, small_grads = call(
         functools.partial(attention_backward_kernel, fast),
         (count,),
-        [full_spec(vectors), w_attention_spec, row_spec((SEQ, D)), small_spec, scalar_spec]
+        [full_spec(vectors), w_attention_spec, row_spec((SEQ, D)), small_spec]
         + [row_spec(a.shape[1:]) for a in kept_attention]
         + [VMEM_SPEC] * 3
         + [ANY_SPEC],
-        [blocks(HALF_GRAD_COLS)] * 2
-        + [pl.BlockSpec((SMALL_ROWS, D), lambda i: (0, 0)), scalar_spec],
-        block_shapes(HALF_GRAD_COLS) + [shaped((SMALL_ROWS, D), F32), shaped((8, 128), F32)],
+        [blocks(HALF_GRAD_COLS)] * 2 + [pl.BlockSpec((SMALL_ROWS, D), lambda i: (0, 0))],
+        block_shapes(HALF_GRAD_COLS) + [shaped((SMALL_ROWS, D), F32)],
         [pltpu.VMEM((D, 2048), F32), small_scratch, pltpu.VMEM((KEYS, D), BF16)]
         + [pltpu.VMEM((count * SEQ, D), BF16)] * 2
         + [pltpu.VMEM((count * SEQ, 768), BF16)]
@@ -1193,17 +1187,14 @@
         w_attention,
         grad_mid,
         small_grads,
-        scalars,
         *kept_attention,
         *joined_attention,
-        other_sums,
-    )
-    others, scalars = lax.optimization_barrier((others, scalars))
-    rest_sums = add_cores(keep_rest, send_rest, wide, n_high, True)
+        other_sums[0],
+    )
+    others_received, keep_rest = lax.optimization_barrier((others_received, keep_rest))
+    rest_sums = add_cores(keep_rest, send_rest, wide, n_high)
     rest_received = swap_plane(rest_sums)
-    others, rest_sums[0] = lax.optimization_barrier((others, rest_sums[0]))
-    others = [others[p].astype(F32) for p in range(4)]
-    other_pieces = column_pieces((others[0] + others[1]) + (others[2] + others[3]))
+    other_pieces = column_pieces(add_plane(other_sums[0], others_received))
     rest_pieces = column_pieces(add_plane(rest_sums[0], rest_received))
 
     grad_rest, grad_others, table_part, small = call(
@@ -1215,7 +1206,7 @@
             shaped((rows, HALF_GRAD_COLS), F32),
             shaped((rows, HALF_GRAD_COLS + HALF_SECOND_COLS), F32),
             shaped((rows, 512), F32),
-            shaped((4 * n_high, rows + 8, 128), F32),
+            shaped((4 * n_high, 8, 128), F32),
         ],
         [],
         10**6,

time: 184 us -> 157 us (0.85)
  local copies, waits for them, and re-layouts: 18.1 us -> 0.06 us
  waiting for transfers between devices: 27 us -> 22.7 us
  other arithmetic: 5.07 us -> 2.59 us
    unnamed x52 -> x4, local copies, waits for them, and re-layouts: 18.1 us -> 0.01 us
    all_to_all x1 -> x0, starting transfers between devices: 4.33 us -> none  [per_device(): others = lax.all_to_all(other_sums, 'wide', 0, 0, axis_index_groups=plane)]
    ppermute x35 -> x38, waiting for transfers between devices: 27 us -> 22.7 us  [swap(): return lax.ppermute(a, axis, [(i, i ^ distance) for i in range(size)])]
    ppermute x35 -> x38, starting transfers between devices: 34.6 us -> 37.7 us  [swap(): return lax.ppermute(a, axis, [(i, i ^ distance) for i in range(size)])]
  transfers between devices with their start and end apart: 36 -> 38, of which waited for: 14 -> 15; matrix products, arithmetic and copies ran while one was open for 1% -> 1% of each run, Pallas kernels for 21% -> 25%
where the time goes in v9:
time: 157 us; the launch traced here: 156 us
  Pallas kernels  79.9 us (51%)
  starting transfers between devices  37.7 us (24%)
  waiting for transfers between devices  22.7 us (14%)
  blocking collectives  12.4 us (8%)
  other arithmetic  2.59 us (2%)
    ppermute x38, starting transfers between devices, swap(): return lax.ppermute(a, axis, [(i, i ^ distance) for i in range(size)])  37.7 us
    pallas_call x1, Pallas kernels, per_device(): call(functools.partial(middle_kernel, fast), (count,), [meta_spec, row_sp...  35.8 us
    ppermute x38, waiting for transfers between devices, swap(): return lax.ppermute(a, axis, [(i, i ^ distance) for i in range(size)])  22.7 us
    pallas_call x1, Pallas kernels, per_device(): call(functools.partial(first_forward_kernel, fast), (count,), [meta_spec]...  16.2 us
    pallas_call x1, Pallas kernels, per_device(): call(functools.partial(attention_backward_kernel, fast), (count,), [full_...  12.5 us
    all_to_all x1, blocking collectives, per_device(): gathered = lax.all_to_all(small, 'wide', 0, 0)  12.4 us
    pallas_call x1, Pallas kernels, per_device(): call(functools.partial(ff_backward_kernel, fast), (count,), [full_spec(ve...  6.43 us
    pallas_call x1, Pallas kernels, per_device(): call(functools.partial(prepare_kernel, fast), None, [SMEM_SPEC] + [VMEM_S...  3.29 us
  transfers between devices with their start and end apart: 38, of which 15 were waited for; matrix products, arithmetic and copies ran while one was open for 1% of the time, Pallas kernels for 25%

profile of v9, /device:TPU:0, one launch (start us, length us, event | category | flops | bytes accessed | tf_op | source)
XLA Modules:
  0.0 156.4 jit_solution(14615040026724989190)
XLA Ops:
  0.7 1.7 %pack.1 = (bf16[16,2048]{1,0:T(8,128)(2,1)}, bf16[16,1792]{1,0:T(8,128)(2,1)}) custom-call(f32[16,896]{1,0:T(8,128)} %bitcast.89, f32[2,3,16,128]{3,2,1,0:T(8,128)} %refs_3_.3, f32[2,16,128]{2,1,0:T(8,128)} %bitcast.91, f32[2,16,512]{2,1,0:T(8,128)} %refs_9_.1, f32[2,16,512]{2,1,0:T(8,128)} %bitcast.87, f32[16,256]{1,0:T(8,128)} %refs_21_.1, f32[5,16]{1,0:T(8,128)} %bitcast.108), custom_call_target="tpu_custom_call" | custom-call | flops 1000000 | bytes 1000000 | tf_op jit(solution)/shard_map/pack/pallas_call | solution.py:1012
  2.4 5.0 %collective-permute-start.2 = (bf16[16,2048]{1,0:T(8,128)(2,1)}, bf16[16,2048]{1,0:T(8,128)(2,1)S(1)}, u32[]{:S(2)}, u32[]{:S(2)}) collective-permute-start(bf16[16,2048]{1,0:T(8,128)(2,1)} %get-tuple-element.123), channel_id=1, source_target_pairs={{0,24},{2,26},{4,28},{6,30},{8,16},{10,18},{12,20},{14,22},{16,8},... | collective-permute-start | bytes 196616 | tf_op jit(solution)/shard_map/ppermute | solution.py:807
  7.4 0.6 collective-permute-start
  8.0 3.3 %prepare.1 = (s32[4,352,128]{2,1,0:T(8,128)}, s32[4,32,128]{2,1,0:T(8,128)}) custom-call(s32[8]{0:T(128)} %games_ref.1, s32[8,16,20]{2,1,0:T(8,128)} %bitcast.95, s32[8,20]{1,0:T(8,128)} %actions.1, s32[8,20]{1,0:T(8,128)} %valid.1, s32[8,20]{1,0:T(8,128)} %rewards.1, s32[8,20]{1,0:T(8,128)} %ends.1), custom_call_target="tpu_custom_call" | custom-call | flops 1000000 | bytes 1000000 | tf_op jit(solution)/shard_map/prepare/pallas_call | solution.py:1027
  11.3 1.9 %collective-permute-done.1 = bf16[16,2048]{1,0:T(8,128)(2,1)S(1)} collective-permute-done((bf16[16,2048]{1,0:T(8,128)(2,1)}, bf16[16,2048]{1,0:T(8,128)(2,1)S(1)}, u32[]{:S(2)}, u32[]{:S(2)}) %collective-permute-start.1) | collective-permute-done | bytes 65568 | tf_op jit(solution)/shard_map/ppermute | solution.py:807
  13.3 0.9 pad_maximum_fusion.4.refs_4_
  14.2 1.6 %collective-permute-start.13 = (bf16[4,16,2048]{2,1,0:T(8,128)(2,1)S(1)}, bf16[4,16,2048]{2,1,0:T(8,128)(2,1)S(1)}, u32[]{:S(2)}, u32[]{:S(2)}) collective-permute-start(bf16[4,16,2048]{2,1,0:T(8,128)(2,1)S(1)} %pad_maximum_fusion.4.refs_4_), channel_id=1, source_target_pairs={{0,4},{2,6},{4,0},{6,2},{8,12},{10,14},{12,8},{14,10},{16,20},{18,... | collective-permute-start | bytes 786440 | tf_op jit(solution)/shard_map/ppermute | solution.py:807
  15.8 1.5 collective-permute-start.12
  17.3 2.6 %collective-permute-start.7 = (bf16[16,1792]{1,0:T(8,128)(2,1)}, bf16[16,1792]{1,0:T(8,128)(2,1)S(1)}, u32[]{:S(2)}, u32[]{:S(2)}) collective-permute-start(bf16[16,1792]{1,0:T(8,128)(2,1)} %get-tuple-element.128), channel_id=1, source_target_pairs={{0,24},{2,26},{4,28},{6,30},{8,16},{10,18},{12,20},{14,22},{16,8},... | collective-permute-start | bytes 172040 | tf_op jit(solution)/shard_map/ppermute | solution.py:807
  19.9 1.7 %collective-permute-start.5 = (bf16[16,1792]{1,0:T(8,128)(2,1)}, bf16[16,1792]{1,0:T(8,128)(2,1)S(1)}, u32[]{:S(2)}, u32[]{:S(2)}) collective-permute-start(bf16[16,1792]{1,0:T(8,128)(2,1)} %get-tuple-element.128), channel_id=1, source_target_pairs={{0,8},{2,10},{4,12},{6,14},{8,0},{10,2},{12,4},{14,6},{16,24},{18,... | collective-permute-start | bytes 172040 | tf_op jit(solution)/shard_map/ppermute | solution.py:807
  21.7 1.3 collective-permute-done.13.refs_6_
  22.9 2.4 %collective-permute-start.8 = (bf16[4,16,2048]{2,1,0:T(8,128)(2,1)S(1)}, bf16[4,16,2048]{2,1,0:T(8,128)(2,1)S(1)}, u32[]{:S(2)}, u32[]{:S(2)}) collective-permute-start(bf16[4,16,2048]{2,1,0:T(8,128)(2,1)S(1)} %pad_maximum_fusion.4.refs_4_), channel_id=1, source_target_pairs={{0,6},{2,4},{4,2},{6,0},{8,14},{10,12},{12,10},{14,8},{16,22},{18,... | collective-permute-start | bytes 786440 | tf_op jit(solution)/shard_map/ppermute | solution.py:807
  25.4 0.5 collective-permute-start.14
  25.9 0.9 pad_maximum_fusion.5.refs_7_
  26.8 4.9 %collective-permute-done.8.refs_7_ = bf16[4,16,2048]{2,1,0:T(8,128)(2,1)S(1)} collective-permute-done((bf16[4,16,2048]{2,1,0:T(8,128)(2,1)S(1)}, bf16[4,16,2048]{2,1,0:T(8,128)(2,1)S(1)}, u32[]{:S(2)}, u32[]{:S(2)}) %collective-permute-start.8) | collective-permute-done | bytes 262176 | tf_op jit(solution)/shard_map/ppermute | solution.py:807
  31.7 0.5 collective-permute-start.17
  32.2 2.4 %collective-permute-start.11 = (bf16[4,16,1792]{2,1,0:T(8,128)(2,1)S(1)}, bf16[4,16,1792]{2,1,0:T(8,128)(2,1)S(1)}, u32[]{:S(2)}, u32[]{:S(2)}) collective-permute-start(bf16[4,16,1792]{2,1,0:T(8,128)(2,1)S(1)} %pad_maximum_fusion.5.refs_7_), channel_id=1, source_target_pairs={{0,6},{2,4},{4,2},{6,0},{8,14},{10,12},{12,10},{14,8},{16,22},{18,... | collective-permute-start | bytes 688136 | tf_op jit(solution)/shard_map/ppermute | solution.py:807
  34.7 0.5 collective-permute-start.10
  35.2 0.5 collective-permute-start.9
  35.7 16.2 %first_forward.1 = (bf16[256,1024]{1,0:T(8,128)(2,1)S(1)}, bf16[256,2048]{1,0:T(8,128)(2,1)S(1)}, bf16[256,128]{1,0:T(8,128)(2,1)S(1)}, f32[4,352,256]{2,1,0:T(8...) custom-call(s32[4,352,128]{2,1,0:T(8,128)} %get-tuple-element.120.re, ...), custom_call_target="tpu_custom_call" | custom-call | flops 4000000000 | bytes 20000000 | tf_op jit(solution)/shard_map/first_forward/pallas_call | solution.py:1058
  52.0 0.5 collective-permute-start.19
  52.6 0.9 collective-permute-done.18.refs_12_
  54.1 35.8 %middle.1 = (f32[4,352,256]{2,1,0:T(8,128)S(1)}, bf16[4,4,16,1792]{3,2,1,0:T(8,128)(2,1)S(1)}, bf16[4,4,16,1792]{3,2,1,0:T(8,128)(2,1)S(1)}, f32[32,8,256]{2,1,0:T(8,128)S(1)}, f32[8,128]{1,0:T(8,128)S(1)}) custom-call(s32[4,352,128]{2,1,0:T(8,128)} %get-tuple-element.120.refs_0_, s32[4,32,128]{2,1,0:T(8,128)} %get-tuple-element.121.refs_1_, ...), custom_call_target="tpu_custom_call" | custom-call | flops 15000000512 | bytes 20000000 | tf_op jit(solution)/shard_map/middle/pallas_call | solution.py:1088
  90.2 6.4 %ff_backward.1 = (f32[4,352,256]{2,1,0:T(8,128)S(1)}, bf16[4,4,16,1024]{3,2,1,0:T(8,128)(2,1)S(1)}, bf16[4,4,16,1024]{3,2,1,0:T(8,128)(2,1)S(1)}, f32[32,8,256]{2,1,0:T(8,128)S(1)}) custom-call(f32[14,256]{1,0:T(8,128)} %refs_18_.1, bf16[256,2048]{1,0:T(8,128)(2,1)S(1)} %get-tuple-element.140.refs_1_, f32[4,352,256]{2,1,0:T(8,128)S(1)} %get-tuple-element.141.refs_2_, ...), custom_call_target="tpu_custom_call" | custom-call | flops 4000000000 | bytes 10000000 | tf_op jit(solution)/shard_map/ff_backward/pallas_call | solution.py:1143
  96.9 1.7 %collective-permute-done.22 = bf16[4,4,16,1024]{3,2,1,0:T(8,128)(2,1)S(1)} collective-permute-done((bf16[4,4,16,1024]{3,2,1,0:T(8,128)(2,1)S(1)}, bf16[4,4,16,1024]{3,2,1,0:T(8,128)(2,1)S(1)}, u32[]{:S(2)}, u32[]{:S(2)}) %collective-permute-start.22) | collective-permute-done | bytes 524320 | tf_op jit(solution)/shard_map/ppermute | solution.py:807
  99.0 1.6 %collective-permute-start.23 = (bf16[4,16,2816]{2,1,0:T(8,128)(2,1)S(1)}, bf16[4,16,2816]{2,1,0:T(8,128)(2,1)S(1)}, u32[]{:S(2)}, u32[]{:S(2)}) collective-permute-start(bf16[4,16,2816]{2,1,0:T(8,128)(2,1)S(1)} %pad_maximum_fusion.1), channel_id=1, source_target_pairs={{0,2},{2,0},{4,6},{6,4},{8,10},{10,8},{12,14},{14,12},{16,18},{18,... | collective-permute-start | bytes 1081352 | tf_op jit(solution)/shard_map/ppermute | solution.py:807
  100.6 1.6 %collective-permute-start.24 = (bf16[4,16,2816]{2,1,0:T(8,128)(2,1)S(1)}, bf16[4,16,2816]{2,1,0:T(8,128)(2,1)S(1)}, u32[]{:S(2)}, u32[]{:S(2)}) collective-permute-start(bf16[4,16,2816]{2,1,0:T(8,128)(2,1)S(1)} %pad_maximum_fusion.2), channel_id=1, source_target_pairs={{0,4},{2,6},{4,0},{6,2},{8,12},{10,14},{12,8},{14,10},{16,20},{18,... | collective-permute-start | bytes 1081352 | tf_op jit(solution)/shard_map/ppermute | solution.py:807
  102.2 0.5 collective-permute-start.25
  102.8 12.5 %attention_backward.1 = (bf16[4,4,16,1024]{3,2,1,0:T(8,128)(2,1)S(1)}, bf16[4,4,16,1024]{3,2,1,0:T(8,128)(2,1)S(1)}, f32[32,256]{1,0:T(8,128)}) custom-call(f32[14,256]{1,0:T(8,128)} %refs_18_.1, bf16[256,1024]{1,0:T(8,128)(2,1)S(1)} %get-tuple-element.150.refs_1_, f32[4,352,256]{2,1,0:T(8,128)S(1)} %get-tuple-element.151.refs_2_, ...), custom_call_target="tpu_custom_call" | custom-call | flops 6000000000 | bytes 20000000 | tf_op jit(solution)/shard_map/attention_backward/pallas_call | solution.py:1168
  115.3 3.4 %collective-permute-done.24 = bf16[4,16,2816]{2,1,0:T(8,128)(2,1)S(1)} collective-permute-done((bf16[4,16,2816]{2,1,0:T(8,128)(2,1)S(1)}, bf16[4,16,2816]{2,1,0:T(8,128)(2,1)S(1)}, u32[]{:S(2)}, u32[]{:S(2)}) %collective-permute-start.24) | collective-permute-done | bytes 360480 | tf_op jit(solution)/shard_map/ppermute | solution.py:807
  118.9 2.7 %collective-permute-start.35 = (bf16[16,2816]{1,0:T(8,128)(2,1)S(1)}, bf16[16,2816]{1,0:T(8,128)(2,1)S(1)}, u32[]{:S(2)}, u32[]{:S(2)}) collective-permute-start(bf16[16,2816]{1,0:T(8,128)(2,1)S(1)} %get-tuple-element.221), channel_id=1, source_target_pairs={{0,24},{2,26},{4,28},{6,30},{8,16},{10,18},{12,20},{14,22},{16,8},... | collective-permute-start | bytes 270344 | tf_op jit(solution)/shard_map/ppermute | solution.py:807
  121.7 1.2 collective-permute-start.27
  122.9 1.8 %collective-permute-start.29 = (bf16[4,16,1024]{2,1,0:T(8,128)(2,1)S(1)}, bf16[4,16,1024]{2,1,0:T(8,128)(2,1)S(1)}, u32[]{:S(2)}, u32[]{:S(2)}) collective-permute-start(bf16[4,16,1024]{2,1,0:T(8,128)(2,1)S(1)} %get-tuple-element.215), channel_id=1, source_target_pairs={{0,6},{2,4},{4,2},{6,0},{8,14},{10,12},{12,10},{14,8},{16,22},{18,... | collective-permute-start | bytes 393224 | tf_op jit(solution)/shard_map/ppermute | solution.py:807
  124.8 0.5 collective-permute-start.28
  125.3 2.1 %collective-permute-done.27 = bf16[4,16,1024]{2,1,0:T(8,128)(2,1)S(1)} collective-permute-done((bf16[4,16,1024]{2,1,0:T(8,128)(2,1)S(1)}, bf16[4,16,1024]{2,1,0:T(8,128)(2,1)S(1)}, u32[]{:S(2)}, u32[]{:S(2)}) %collective-permute-start.27) | collective-permute-done | bytes 131104 | tf_op jit(solution)/shard_map/ppermute | solution.py:807
  127.5 1.5 collective-permute-start.33
  128.9 1.0 collective-permute-done.29
  129.9 1.3 collective-permute-done.28
  131.3 1.6 %collective-permute-start.32 = (bf16[16,1024]{1,0:T(8,128)(2,1)S(1)}, bf16[16,1024]{1,0:T(8,128)(2,1)S(1)}, u32[]{:S(2)}, u32[]{:S(2)}) collective-permute-start(bf16[16,1024]{1,0:T(8,128)(2,1)S(1)} %get-tuple-element.224), channel_id=1, source_target_pairs={{0,24},{2,26},{4,28},{6,30},{8,16},{10,18},{12,20},{14,22},{16,8},... | collective-permute-start | bytes 98312 | tf_op jit(solution)/shard_map/ppermute | solution.py:807
  133.0 1.3 collective-permute-start.31
  134.3 1.5 collective-permute-start.30
  135.8 1.3 collective-permute-done.32.refs_3_
  137.1 0.7 collective-permute-done.31.refs_2_
  138.2 1.5 finish.1
  139.7 12.4 %all_to_all.5.gathered = f32[16,8,128]{2,1,0:T(8,128)S(1)} all-to-all(f32[16,8,128]{2,1,0:T(8,128)} %get-tuple-element.175), channel_id=1, replica_groups=mesh['wide'=16,'narrow'=2] {'wide'}, dimensions={0} | all-to-all | bytes 131072 | tf_op jit(solution)/shard_map/all_to_all | solution.py:1217
  152.1 0.5 collective-permute-start.36
  152.6 1.1 collective-permute-done.36.swapped
  153.7 2.5 %adam.1 = (f32[1,1]{1,0:T(1,128)}, f32[1,1]{1,0:T(1,128)}, f32[1,1]{1,0:T(1,128)}, f32[16,896]{1,0:T(8,128)}, f32[16,896]{1,0:T(8,128)}, /*index=5*/f32[16,896]{...) custom-call(f32[16,1024]{1,0:T(8,128)} %get-tuple-element.172.rest, ...), custom_call_target="tpu_custom_call" | custom-call | flops 1000000 | bytes 1000000 | tf_op jit(solution)/shard_map/adam/pallas_call | solution.py:1226
  (56 shorter events, 2.9 us)
Async XLA Ops:
  2.4 8.9 %collective-permute-start.2 = (bf16[16,2048]{1,0:T(8,128)(2,1)}, bf16[16,2048]{1,0:T(8,128)(2,1)S(1)}, u32[]{:S(2)}, u32[]{:S(2)}) collective-permute-start(bf16[16,2048]{1,0:T(8,128)(2,1)} %get-tuple-element.123), channel_id=1, source_target_pairs={{0,24},{2,26},{4,28},{6,30},{8,16},{10,18},{12,20},{14,22},{16,8},... | collective-permute-start | bytes 196616 | tf_op jit(solution)/shard_map/ppermute | solution.py:807
  7.4 5.8 %collective-permute-start.1 = (bf16[16,2048]{1,0:T(8,128)(2,1)}, bf16[16,2048]{1,0:T(8,128)(2,1)S(1)}, u32[]{:S(2)}, u32[]{:S(2)}) collective-permute-start(bf16[16,2048]{1,0:T(8,128)(2,1)} %get-tuple-element.123), channel_id=1, source_target_pairs={{0,16},{2,18},{4,20},{6,22},{8,24},{10,26},{12,28},{14,30},{16,0},... | collective-permute-start | bytes 196616 | tf_op jit(solution)/shard_map/ppermute | solution.py:807
  7.4 5.8 %collective-permute-start = (bf16[16,2048]{1,0:T(8,128)(2,1)}, bf16[16,2048]{1,0:T(8,128)(2,1)S(1)}, u32[]{:S(2)}, u32[]{:S(2)}) collective-permute-start(bf16[16,2048]{1,0:T(8,128)(2,1)} %get-tuple-element.123), channel_id=1, source_target_pairs={{0,8},{2,10},{4,12},{6,14},{8,0},{10,2},{12,4},{14,6},{16,24},{18,... | collective-permute-start | bytes 196616 | tf_op jit(solution)/shard_map/ppermute | solution.py:807
  8.0 3.3 %collective-permute-start.3 = (f32[2,512]{1,0:T(2,128)}, f32[2,512]{1,0:T(2,128)S(1)}, u32[]{:S(2)}, u32[]{:S(2)}) collective-permute-start(f32[2,512]{1,0:T(2,128)} %refs_12_.1), channel_id=1, source_target_pairs={{0,1},{1,0},{2,3},{3,2},{4,5},{5,4},{6,7},{7,6},{8,9},{9,8},{10,11... | collective-permute-start | bytes 12296 | tf_op jit(solution)/shard_map/ppermute | solution.py:807
  11.3 24.4 %copy-start.1 = (f32[2,512]{1,0:T(2,128)}, f32[2,512]{1,0:T(2,128)S(1)}, u32[]{:S(2)}) copy-start(f32[2,512]{1,0:T(2,128)S(1)} %collective-permute-done.3.refs_3_.refs_4_) | copy-start | bytes 12292
  14.1 3.2 %collective-permute-start.4 = (bf16[4,16,2048]{2,1,0:T(8,128)(2,1)S(1)}, bf16[4,16,2048]{2,1,0:T(8,128)(2,1)S(1)}, u32[]{:S(2)}, u32[]{:S(2)}) collective-permute-start(bf16[4,16,2048]{2,1,0:T(8,128)(2,1)S(1)} %pad_maximum_fusion.4.refs_4_), channel_id=1, source_target_pairs={{0,1},{1,0},{2,3},{3,2},{4,5},{5,4},{6,7},{7,6},{8,9},{9,8},{10,11... | collective-permute-start | bytes 786440 | tf_op jit(solution)/shard_map/ppermute | solution.py:807
  14.2 8.7 %collective-permute-start.13 = (bf16[4,16,2048]{2,1,0:T(8,128)(2,1)S(1)}, bf16[4,16,2048]{2,1,0:T(8,128)(2,1)S(1)}, u32[]{:S(2)}, u32[]{:S(2)}) collective-permute-start(bf16[4,16,2048]{2,1,0:T(8,128)(2,1)S(1)} %pad_maximum_fusion.4.refs_4_), channel_id=1, source_target_pairs={{0,4},{2,6},{4,0},{6,2},{8,12},{10,14},{12,8},{14,10},{16,20},{18,... | collective-permute-start | bytes 786440 | tf_op jit(solution)/shard_map/ppermute | solution.py:807
  15.8 9.6 %collective-permute-start.12 = (bf16[4,16,2048]{2,1,0:T(8,128)(2,1)S(1)}, bf16[4,16,2048]{2,1,0:T(8,128)(2,1)S(1)}, u32[]{:S(2)}, u32[]{:S(2)}) collective-permute-start(bf16[4,16,2048]{2,1,0:T(8,128)(2,1)S(1)} %pad_maximum_fusion.4.refs_4_), channel_id=1, source_target_pairs={{0,2},{2,0},{4,6},{6,4},{8,10},{10,8},{12,14},{14,12},{16,18},{18,... | collective-permute-start | bytes 786440 | tf_op jit(solution)/shard_map/ppermute | solution.py:807
  17.3 8.1 %collective-permute-start.7 = (bf16[16,1792]{1,0:T(8,128)(2,1)}, bf16[16,1792]{1,0:T(8,128)(2,1)S(1)}, u32[]{:S(2)}, u32[]{:S(2)}) collective-permute-start(bf16[16,1792]{1,0:T(8,128)(2,1)} %get-tuple-element.128), channel_id=1, source_target_pairs={{0,24},{2,26},{4,28},{6,30},{8,16},{10,18},{12,20},{14,22},{16,8},... | collective-permute-start | bytes 172040 | tf_op jit(solution)/shard_map/ppermute | solution.py:807
  19.9 6.0 %collective-permute-start.6 = (bf16[16,1792]{1,0:T(8,128)(2,1)}, bf16[16,1792]{1,0:T(8,128)(2,1)S(1)}, u32[]{:S(2)}, u32[]{:S(2)}) collective-permute-start(bf16[16,1792]{1,0:T(8,128)(2,1)} %get-tuple-element.128), channel_id=1, source_target_pairs={{0,16},{2,18},{4,20},{6,22},{8,24},{10,26},{12,28},{14,30},{16,0},... | collective-permute-start | bytes 172040 | tf_op jit(solution)/shard_map/ppermute | solution.py:807
  19.9 6.0 %collective-permute-start.5 = (bf16[16,1792]{1,0:T(8,128)(2,1)}, bf16[16,1792]{1,0:T(8,128)(2,1)S(1)}, u32[]{:S(2)}, u32[]{:S(2)}) collective-permute-start(bf16[16,1792]{1,0:T(8,128)(2,1)} %get-tuple-element.128), channel_id=1, source_target_pairs={{0,8},{2,10},{4,12},{6,14},{8,0},{10,2},{12,4},{14,6},{16,24},{18,... | collective-permute-start | bytes 172040 | tf_op jit(solution)/shard_map/ppermute | solution.py:807
  22.9 8.8 %collective-permute-start.8 = (bf16[4,16,2048]{2,1,0:T(8,128)(2,1)S(1)}, bf16[4,16,2048]{2,1,0:T(8,128)(2,1)S(1)}, u32[]{:S(2)}, u32[]{:S(2)}) collective-permute-start(bf16[4,16,2048]{2,1,0:T(8,128)(2,1)S(1)} %pad_maximum_fusion.4.refs_4_), channel_id=1, source_target_pairs={{0,6},{2,4},{4,2},{6,0},{8,14},{10,12},{12,10},{14,8},{16,22},{18,... | collective-permute-start | bytes 786440 | tf_op jit(solution)/shard_map/ppermute | solution.py:807
  25.4 9.3 %collective-permute-start.15 = (bf16[4,16,2048]{2,1,0:T(8,128)(2,1)S(1)}, bf16[4,16,2048]{2,1,0:T(8,128)(2,1)S(1)}, u32[]{:S(2)}, u32[]{:S(2)}) collective-permute-start(bf16[4,16,2048]{2,1,0:T(8,128)(2,1)S(1)} %collective-permute-done.13.refs_6_), channel_id=1, source_target_pairs={{0,1},{1,0},{2,3},{3,2},{4,5},{5,4},{6,7},{7,6},{8,9},{9,8},{10,11... | collective-permute-start | bytes 786440 | tf_op jit(solution)/shard_map/ppermute | solution.py:807
  25.4 9.8 %collective-permute-start.14 = (bf16[4,16,2048]{2,1,0:T(8,128)(2,1)S(1)}, bf16[4,16,2048]{2,1,0:T(8,128)(2,1)S(1)}, u32[]{:S(2)}, u32[]{:S(2)}) collective-permute-start(bf16[4,16,2048]{2,1,0:T(8,128)(2,1)S(1)} %collective-permute-done.12.refs_5_), channel_id=1, source_target_pairs={{0,1},{1,0},{2,3},{3,2},{4,5},{5,4},{6,7},{7,6},{8,9},{9,8},{10,11... | collective-permute-start | bytes 786440 | tf_op jit(solution)/shard_map/ppermute | solution.py:807
  31.7 4.0 %collective-permute-start.16 = (bf16[4,16,2048]{2,1,0:T(8,128)(2,1)S(1)}, bf16[4,16,2048]{2,1,0:T(8,128)(2,1)S(1)}, u32[]{:S(2)}, u32[]{:S(2)}) collective-permute-start(bf16[4,16,2048]{2,1,0:T(8,128)(2,1)S(1)} %collective-permute-done.8.refs_7_), channel_id=1, source_target_pairs={{0,1},{1,0},{2,3},{3,2},{4,5},{5,4},{6,7},{7,6},{8,9},{9,8},{10,11... | collective-permute-start | bytes 786440 | tf_op jit(solution)/shard_map/ppermute | solution.py:807
  31.7 20.9 %collective-permute-start.17 = (bf16[4,16,1792]{2,1,0:T(8,128)(2,1)S(1)}, bf16[4,16,1792]{2,1,0:T(8,128)(2,1)S(1)}, u32[]{:S(2)}, u32[]{:S(2)}) collective-permute-start(bf16[4,16,1792]{2,1,0:T(8,128)(2,1)S(1)} %pad_maximum_fusion.5.refs_7_), channel_id=1, source_target_pairs={{0,1},{1,0},{2,3},{3,2},{4,5},{5,4},{6,7},{7,6},{8,9},{9,8},{10,11... | collective-permute-start | bytes 688136 | tf_op jit(solution)/shard_map/ppermute | solution.py:807
  32.2 19.7 %collective-permute-start.11 = (bf16[4,16,1792]{2,1,0:T(8,128)(2,1)S(1)}, bf16[4,16,1792]{2,1,0:T(8,128)(2,1)S(1)}, u32[]{:S(2)}, u32[]{:S(2)}) collective-permute-start(bf16[4,16,1792]{2,1,0:T(8,128)(2,1)S(1)} %pad_maximum_fusion.5.refs_7_), channel_id=1, source_target_pairs={{0,6},{2,4},{4,2},{6,0},{8,14},{10,12},{12,10},{14,8},{16,22},{18,... | collective-permute-start | bytes 688136 | tf_op jit(solution)/shard_map/ppermute | solution.py:807
  34.7 17.2 %collective-permute-start.10 = (bf16[4,16,1792]{2,1,0:T(8,128)(2,1)S(1)}, bf16[4,16,1792]{2,1,0:T(8,128)(2,1)S(1)}, u32[]{:S(2)}, u32[]{:S(2)}) collective-permute-start(bf16[4,16,1792]{2,1,0:T(8,128)(2,1)S(1)} %pad_maximum_fusion.5.refs_7_), channel_id=1, source_target_pairs={{0,4},{2,6},{4,0},{6,2},{8,12},{10,14},{12,8},{14,10},{16,20},{18,... | collective-permute-start | bytes 688136 | tf_op jit(solution)/shard_map/ppermute | solution.py:807
  35.2 16.7 %collective-permute-start.9 = (bf16[4,16,1792]{2,1,0:T(8,128)(2,1)S(1)}, bf16[4,16,1792]{2,1,0:T(8,128)(2,1)S(1)}, u32[]{:S(2)}, u32[]{:S(2)}) collective-permute-start(bf16[4,16,1792]{2,1,0:T(8,128)(2,1)S(1)} %pad_maximum_fusion.5.refs_7_), channel_id=1, source_target_pairs={{0,2},{2,0},{4,6},{6,4},{8,10},{10,8},{12,14},{14,12},{16,18},{18,... | collective-permute-start | bytes 688136 | tf_op jit(solution)/shard_map/ppermute | solution.py:807
  51.9 1.6 collective-permute-start.18
  52.0 1.8 %collective-permute-start.19 = (bf16[4,16,1792]{2,1,0:T(8,128)(2,1)S(1)}, bf16[4,16,1792]{2,1,0:T(8,128)(2,1)S(1)}, u32[]{:S(2)}, u32[]{:S(2)}) collective-permute-start(bf16[4,16,1792]{2,1,0:T(8,128)(2,1)S(1)} %collective-permute-done.10.refs_9_), channel_id=1, source_target_pairs={{0,1},{1,0},{2,3},{3,2},{4,5},{5,4},{6,7},{7,6},{8,9},{9,8},{10,11... | collective-permute-start | bytes 688136 | tf_op jit(solution)/shard_map/ppermute | solution.py:807
  52.5 1.6 %collective-permute-start.20 = (bf16[4,16,1792]{2,1,0:T(8,128)(2,1)S(1)}, bf16[4,16,1792]{2,1,0:T(8,128)(2,1)S(1)}, u32[]{:S(2)}, u32[]{:S(2)}) collective-permute-start(bf16[4,16,1792]{2,1,0:T(8,128)(2,1)S(1)} %collective-permute-done.11.refs_10_), channel_id=1, source_target_pairs={{0,1},{1,0},{2,3},{3,2},{4,5},{5,4},{6,7},{7,6},{8,9},{9,8},{10,11... | collective-permute-start | bytes 688136 | tf_op jit(solution)/shard_map/ppermute | solution.py:807
  89.9 6.7 %copy-start = (f32[8,128]{1,0:T(8,128)}, f32[8,128]{1,0:T(8,128)S(1)}, u32[]{:S(2)}) copy-start(f32[8,128]{1,0:T(8,128)S(1)} %get-tuple-element.171.refs_8_) | copy-start | bytes 12292
  89.9 8.9 %collective-permute-start.21 = (bf16[4,4,16,1792]{3,2,1,0:T(8,128)(2,1)S(1)}, bf16[4,4,16,1792]{3,2,1,0:T(8,128)(2,1)S(1)}, u32[]{:S(2)}, u32[]{:S(2)}) collective-permute-start(bf16[4,4,16,1792]{3,2,1,0:T(8,128)(2,1)S(1)} %get-tuple-element.139), channel_id=1, source_target_pairs={{0,1},{1,0},{2,3},{3,2},{4,5},{5,4},{6,7},{7,6},{8,9},{9,8},{10,11... | collective-permute-start | bytes 2752520 | tf_op jit(solution)/shard_map/ppermute | solution.py:807
  96.6 2.0 %collective-permute-start.22 = (bf16[4,4,16,1024]{3,2,1,0:T(8,128)(2,1)S(1)}, bf16[4,4,16,1024]{3,2,1,0:T(8,128)(2,1)S(1)}, u32[]{:S(2)}, u32[]{:S(2)}) collective-permute-start(bf16[4,4,16,1024]{3,2,1,0:T(8,128)(2,1)S(1)} %get-tuple-element.149), channel_id=1, source_target_pairs={{0,1},{1,0},{2,3},{3,2},{4,5},{5,4},{6,7},{7,6},{8,9},{9,8},{10,11... | collective-permute-start | bytes 1572872 | tf_op jit(solution)/shard_map/ppermute | solution.py:807
  99.0 16.3 %collective-permute-start.23 = (bf16[4,16,2816]{2,1,0:T(8,128)(2,1)S(1)}, bf16[4,16,2816]{2,1,0:T(8,128)(2,1)S(1)}, u32[]{:S(2)}, u32[]{:S(2)}) collective-permute-start(bf16[4,16,2816]{2,1,0:T(8,128)(2,1)S(1)} %pad_maximum_fusion.1), channel_id=1, source_target_pairs={{0,2},{2,0},{4,6},{6,4},{8,10},{10,8},{12,14},{14,12},{16,18},{18,... | collective-permute-start | bytes 1081352 | tf_op jit(solution)/shard_map/ppermute | solution.py:807
  100.6 18.1 %collective-permute-start.24 = (bf16[4,16,2816]{2,1,0:T(8,128)(2,1)S(1)}, bf16[4,16,2816]{2,1,0:T(8,128)(2,1)S(1)}, u32[]{:S(2)}, u32[]{:S(2)}) collective-permute-start(bf16[4,16,2816]{2,1,0:T(8,128)(2,1)S(1)} %pad_maximum_fusion.2), channel_id=1, source_target_pairs={{0,4},{2,6},{4,0},{6,2},{8,12},{10,14},{12,8},{14,10},{16,20},{18,... | collective-permute-start | bytes 1081352 | tf_op jit(solution)/shard_map/ppermute | solution.py:807
  102.2 16.5 %collective-permute-start.25 = (bf16[4,16,2816]{2,1,0:T(8,128)(2,1)S(1)}, bf16[4,16,2816]{2,1,0:T(8,128)(2,1)S(1)}, u32[]{:S(2)}, u32[]{:S(2)}) collective-permute-start(bf16[4,16,2816]{2,1,0:T(8,128)(2,1)S(1)} %pad_maximum_fusion.3), channel_id=1, source_target_pairs={{0,6},{2,4},{4,2},{6,0},{8,14},{10,12},{12,10},{14,8},{16,22},{18,... | collective-permute-start | bytes 1081352 | tf_op jit(solution)/shard_map/ppermute | solution.py:807
  115.3 6.3 %collective-permute-start.26 = (bf16[4,4,16,1024]{3,2,1,0:T(8,128)(2,1)S(1)}, bf16[4,4,16,1024]{3,2,1,0:T(8,128)(2,1)S(1)}, u32[]{:S(2)}, u32[]{:S(2)}) collective-permute-start(bf16[4,4,16,1024]{3,2,1,0:T(8,128)(2,1)S(1)} %get-tuple-element.167), channel_id=1, source_target_pairs={{0,1},{1,0},{2,3},{3,2},{4,5},{5,4},{6,7},{7,6},{8,9},{9,8},{10,11... | collective-permute-start | bytes 1572872 | tf_op jit(solution)/shard_map/ppermute | solution.py:807
  118.9 15.4 %collective-permute-start.35 = (bf16[16,2816]{1,0:T(8,128)(2,1)S(1)}, bf16[16,2816]{1,0:T(8,128)(2,1)S(1)}, u32[]{:S(2)}, u32[]{:S(2)}) collective-permute-start(bf16[16,2816]{1,0:T(8,128)(2,1)S(1)} %get-tuple-element.221), channel_id=1, source_target_pairs={{0,24},{2,26},{4,28},{6,30},{8,16},{10,18},{12,20},{14,22},{16,8},... | collective-permute-start | bytes 270344 | tf_op jit(solution)/shard_map/ppermute | solution.py:807
  121.6 14.2 %collective-permute-start.34 = (bf16[16,2816]{1,0:T(8,128)(2,1)S(1)}, bf16[16,2816]{1,0:T(8,128)(2,1)S(1)}, u32[]{:S(2)}, u32[]{:S(2)}) collective-permute-start(bf16[16,2816]{1,0:T(8,128)(2,1)S(1)} %get-tuple-element.222), channel_id=1, source_target_pairs={{0,16},{2,18},{4,20},{6,22},{8,24},{10,26},{12,28},{14,30},{16,0},... | collective-permute-start | bytes 270344 | tf_op jit(solution)/shard_map/ppermute | solution.py:807
  121.7 5.7 %collective-permute-start.27 = (bf16[4,16,1024]{2,1,0:T(8,128)(2,1)S(1)}, bf16[4,16,1024]{2,1,0:T(8,128)(2,1)S(1)}, u32[]{:S(2)}, u32[]{:S(2)}) collective-permute-start(bf16[4,16,1024]{2,1,0:T(8,128)(2,1)S(1)} %get-tuple-element.214), channel_id=1, source_target_pairs={{0,2},{2,0},{4,6},{6,4},{8,10},{10,8},{12,14},{14,12},{16,18},{18,... | collective-permute-start | bytes 393224 | tf_op jit(solution)/shard_map/ppermute | solution.py:807
  122.9 7.0 %collective-permute-start.29 = (bf16[4,16,1024]{2,1,0:T(8,128)(2,1)S(1)}, bf16[4,16,1024]{2,1,0:T(8,128)(2,1)S(1)}, u32[]{:S(2)}, u32[]{:S(2)}) collective-permute-start(bf16[4,16,1024]{2,1,0:T(8,128)(2,1)S(1)} %get-tuple-element.215), channel_id=1, source_target_pairs={{0,6},{2,4},{4,2},{6,0},{8,14},{10,12},{12,10},{14,8},{16,22},{18,... | collective-permute-start | bytes 393224 | tf_op jit(solution)/shard_map/ppermute | solution.py:807
  124.8 6.4 %collective-permute-start.28 = (bf16[4,16,1024]{2,1,0:T(8,128)(2,1)S(1)}, bf16[4,16,1024]{2,1,0:T(8,128)(2,1)S(1)}, u32[]{:S(2)}, u32[]{:S(2)}) collective-permute-start(bf16[4,16,1024]{2,1,0:T(8,128)(2,1)S(1)} %get-tuple-element.216), channel_id=1, source_target_pairs={{0,4},{2,6},{4,0},{6,2},{8,12},{10,14},{12,8},{14,10},{16,20},{18,... | collective-permute-start | bytes 393224 | tf_op jit(solution)/shard_map/ppermute | solution.py:807
  127.5 8.3 %collective-permute-start.33 = (bf16[16,2816]{1,0:T(8,128)(2,1)S(1)}, bf16[16,2816]{1,0:T(8,128)(2,1)S(1)}, u32[]{:S(2)}, u32[]{:S(2)}) collective-permute-start(bf16[16,2816]{1,0:T(8,128)(2,1)S(1)} %get-tuple-element.223), channel_id=1, source_target_pairs={{0,8},{2,10},{4,12},{6,14},{8,0},{10,2},{12,4},{14,6},{16,24},{18,... | collective-permute-start | bytes 270344 | tf_op jit(solution)/shard_map/ppermute | solution.py:807
  131.3 5.8 %collective-permute-start.32 = (bf16[16,1024]{1,0:T(8,128)(2,1)S(1)}, bf16[16,1024]{1,0:T(8,128)(2,1)S(1)}, u32[]{:S(2)}, u32[]{:S(2)}) collective-permute-start(bf16[16,1024]{1,0:T(8,128)(2,1)S(1)} %get-tuple-element.224), channel_id=1, source_target_pairs={{0,24},{2,26},{4,28},{6,30},{8,16},{10,18},{12,20},{14,22},{16,8},... | collective-permute-start | bytes 98312 | tf_op jit(solution)/shard_map/ppermute | solution.py:807
  133.0 4.8 %collective-permute-start.31 = (bf16[16,1024]{1,0:T(8,128)(2,1)S(1)}, bf16[16,1024]{1,0:T(8,128)(2,1)S(1)}, u32[]{:S(2)}, u32[]{:S(2)}) collective-permute-start(bf16[16,1024]{1,0:T(8,128)(2,1)S(1)} %get-tuple-element.225), channel_id=1, source_target_pairs={{0,16},{2,18},{4,20},{6,22},{8,24},{10,26},{12,28},{14,30},{16,0},... | collective-permute-start | bytes 98312 | tf_op jit(solution)/shard_map/ppermute | solution.py:807
  134.3 3.9 %collective-permute-start.30 = (bf16[16,1024]{1,0:T(8,128)(2,1)S(1)}, bf16[16,1024]{1,0:T(8,128)(2,1)S(1)}, u32[]{:S(2)}, u32[]{:S(2)}) collective-permute-start(bf16[16,1024]{1,0:T(8,128)(2,1)S(1)} %get-tuple-element.226), channel_id=1, source_target_pairs={{0,8},{2,10},{4,12},{6,14},{8,0},{10,2},{12,4},{14,6},{16,24},{18,... | collective-permute-start | bytes 98312 | tf_op jit(solution)/shard_map/ppermute | solution.py:807
  152.1 1.6 %collective-permute-start.37 = (f32[16,8,128]{2,1,0:T(8,128)S(1)}, f32[16,8,128]{2,1,0:T(8,128)S(1)}, u32[]{:S(2)}, u32[]{:S(2)}) collective-permute-start(f32[16,8,128]{2,1,0:T(8,128)S(1)} %all_to_all.5.gathered), channel_id=1, source_target_pairs={{0,1},{1,0},{2,3},{3,2},{4,5},{5,4},{6,7},{7,6},{8,9},{9,8},{10,11... | collective-permute-start | bytes 196616 | tf_op jit(solution)/shard_map/ppermute | solution.py:807
  152.1 1.6 %collective-permute-start.36 = (f32[16,512]{1,0:T(8,128)}, f32[16,512]{1,0:T(8,128)S(1)}, u32[]{:S(2)}, u32[]{:S(2)}) collective-permute-start(f32[16,512]{1,0:T(8,128)} %get-tuple-element.174), channel_id=1, source_target_pairs={{0,1},{1,0},{2,3},{3,2},{4,5},{5,4},{6,7},{7,6},{8,9},{9,8},{10,11... | collective-permute-start | bytes 98312 | tf_op jit(solution)/shard_map/ppermute | solution.py:807

commit v10 on v9

--- a/solution.py
+++ b/solution.py
@@ -180,12 +180,11 @@
     lax.fori_loop(0, 16, block, 0)
 
 
-def make_hits(meta_ref, hits_ref):
+def make_hits(ids, game, hits_ref):
+    lane = lax.broadcasted_iota(jnp.int32, (TILE, ROWS), 1)
     for rows in tiles(SEQ, TILE):
-        lane = lax.broadcasted_iota(jnp.int32, (TILE, ROWS), 1)
         place = lax.broadcasted_iota(jnp.int32, (TILE, 1), 0) + (VOCAB + ACTIONS + GAMES + rows.start)
-        meta = meta_ref[rows]
-        hit = (lane == meta[:, 0:1]) | (lane == meta[:, 1:2]) | (lane == place)
+        hit = (lane == ids[rows]) | (lane == game[rows]) | (lane == place)
         hits_ref[rows] = jnp.where(hit, 1.0, 0.0).astype(BF16)
 
 
@@ -276,7 +275,7 @@
 def attention_backward(mid_ref, mid16_ref, w_ref, vec, kept, v_ref, v_row, work, out_ref):
     norm_kept, (qt_ref, kv_ref, p0, p1, p2, r_ref, ot_ref) = kept
     dost_ref, qst_ref, kt_ref, dst_ref, dqt_ref, dkv_ref, dqkv_ref, proj_ref, y_ref = work
-    grad_o = dot_nt(proj_ref[...], mid16_ref[...]).astype(BF16).astype(F32)
+    grad_o = dot_nt(proj_ref[...], mid16_ref[...])
     kt_ref[...] = jnp.transpose(kv_ref[:, 0:256])
     deltas = []
     for h in range(HEADS):
@@ -325,7 +324,7 @@
 
 
 def prepare_kernel(
-    fast, games_ref, tokens, actions, valid, rewards, ends, out, out_side, x_ref
+    fast, games_ref, tokens, actions, valid, rewards, ends, out, out_side, out_hits, x_ref
 ):
     count = out.shape[0]
     frames = tokens.shape[2]
@@ -358,18 +357,19 @@
         now = dot_nt(here, high) * 16.0 + dot_nt(here, low)
         soon = dot_nt(coming, high) * 16.0 + dot_nt(coming, low)
 
-        def pick(condition, a):
-            return jnp.sum(jnp.where(condition, a, 0.0), axis=1, keepdims=True).astype(jnp.int32)
-
-        ids = jnp.where(inside, pick(lane == spot, now), -1)
+        at_end = spot == 16
+        packed = jnp.where(lane == spot, now, 0.0)
+        target = jnp.where((lane == spot + 1) & (spot < 15), now, 0.0)
+        target = target + jnp.where((lane == 0) & at_end, soon, 0.0)
+        weight = jnp.where((lane == 17) & (spot < 15), now, 0.0)
+        weight = weight + jnp.where((lane == 17) & at_end, soon, 0.0)
+        packed = packed + 1024.0 * target + 1048576.0 * weight
+        packed = jnp.sum(packed, axis=1, keepdims=True).astype(jnp.int32)
+        ids = jnp.where(inside, packed & 1023, -1)
         game = jnp.where(inside, games_ref[base + s] + (VOCAB + ACTIONS), -1)
-        target = pick((lane == spot + 1) & (spot < 15), now)
-        target = target + pick((lane == 0) & (spot == 16), soon)
-        weight = pick((lane == 17) & (spot < 15), now) + pick((lane == 17) & (spot == 16), soon)
-        result = jnp.zeros((SEQ, 128), jnp.int32)
-        for c, column in enumerate((ids, game, target, weight)):
-            result = jnp.where(wide_lane == c, column, result)
-        out[s] = result
+        target, weight = (packed >> 10) & 1023, packed >> 20
+        out[s] = jnp.where(wide_lane == 2, target, jnp.where(wide_lane == 3, weight, 0))
+        make_hits(ids, game, out_hits.at[s])
         by_frame = dot_nt(one_frame, high) * 16.0 + dot_nt(one_frame, low)
         result = jnp.zeros((SIDE_ROWS, 128), jnp.int32)
         for c in range(3):
@@ -389,12 +389,12 @@
 
 def first_forward_kernel(fast, *refs):
     refs = (places(fast),) + refs
-    place, meta_ref, vec_ref, bias_ref, bias_other = refs[0:5]
+    place, hits_ref, vec_ref, bias_ref, bias_other = refs[0:5]
     mine, other = refs[5:9], refs[9:13]
-    w_attention, w_ff, side_out, next_ref, hits_ref = refs[13:18]
-    kept = [ref.at[0] for ref in refs[18:34]]
-    w_ref, x_ref = refs[34:36]
-    work = refs[36:44]
+    w_attention, w_ff, side_out, next_ref = refs[13:17]
+    kept = [ref.at[0] for ref in refs[17:33]]
+    w_ref, x_ref = refs[33:35]
+    work = refs[35:43]
     y_ref, m_ref = work[6:8]
 
     @pl.when(pl.program_id(0) == 0)
@@ -405,7 +405,6 @@
         side_out[...] = w_ref[:, COL_SMALL:]
         start_forward(work, w_ref)
 
-    make_hits(meta_ref.at[0], hits_ref.at[0])
     x_ref[...] = dot_nt(hits_ref[0], w_ref[:, COL_TABLE : COL_TABLE + ROWS])
     bias = own_bias(place, bias_ref[0:1], bias_other[0:1])
     vec = vec_ref[0:6]
@@ -885,7 +884,7 @@
 
 VMEM_MIB = {
     "pack": 58,
-    "prepare": 58,
+    "prepare": 24,
     "first_forward": 22,
     "middle": 28,
     "ff_backward": 15,
@@ -1024,25 +1023,29 @@
     column = swap_column(piece_first, n_high)
 
     count = tokens.shape[0] // lax.axis_size("narrow")
-    meta, frame_meta = call(
+    meta, frame_meta, hits = call(
         functools.partial(prepare_kernel, fast),
         None,
         [SMEM_SPEC] + [VMEM_SPEC] * 5,
-        [VMEM_SPEC] * 2,
-        [shaped((count, SEQ, 128), jnp.int32), shaped((count, SIDE_ROWS, 128), jnp.int32)],
+        [VMEM_SPEC] * 3,
+        [
+            shaped((count, SEQ, 128), jnp.int32),
+            shaped((count, SIDE_ROWS, 128), jnp.int32),
+            shaped((count, SEQ, ROWS), BF16),
+        ],
         [pltpu.VMEM((24, FRAMES), jnp.int32)],
         10**6,
         10**6,
         "prepare",
-    )(game_ids, flat(tokens), actions, valid_steps, rewards, end_flags)
-    column, other_bias, meta = lax.optimization_barrier((column, other_bias, meta))
+    )(*in_hbm([game_ids, flat(tokens), actions, valid_steps, rewards, end_flags]))
+    column, other_bias, hits = lax.optimization_barrier((column, other_bias, hits))
     first_column = jnp.stack(column)
     first_mine = gather_plane(first_column)
     own, piece_second = lax.optimization_barrier((swap(first_column, "narrow", 1), piece_second))
+    first_other = [own] + gather_cores(first_mine[1:])
     second_column = jnp.stack(swap_column(piece_second, n_high))
-    second_column, across = lax.optimization_barrier((second_column, first_mine[3]))
-    first_mine = first_mine[0:3] + [across]
-    first_other = [own] + gather_cores(first_mine[1:])
+    second_column, across = lax.optimization_barrier((second_column, first_other[3]))
+    first_other = first_other[0:3] + [across]
     second_mine = gather_plane(second_column)
     first_parts = in_blocks(first_mine, wide) + in_blocks(first_other, wide)
 
@@ -1058,18 +1061,17 @@
     results = call(
         functools.partial(first_forward_kernel, fast),
         (count,),
-        [meta_spec] + vec_specs + [VMEM_SPEC] * 8,
-        [w_attention_spec, w_ff_spec, side_spec, row_spec((SEQ, D)), hits_spec] + kept_specs,
+        [hits_spec] + vec_specs + [VMEM_SPEC] * 8,
+        [w_attention_spec, w_ff_spec, side_spec, row_spec((SEQ, D))] + kept_specs,
         [shaped((D, 1024), BF16), shaped((D, 2048), BF16), shaped((D, 128), BF16), row_f32]
-        + [shaped((count, SEQ, ROWS), BF16)]
         + kept_shapes,
         [pltpu.VMEM((D, COL_FIRST), BF16), pltpu.VMEM((SEQ, D), F32)] + FORWARD_WORK,
         4 * 10**9,
         20 * 10**6,
         "first_forward",
-    )(*in_hbm([meta, vectors, up_bias, other_bias]), *resident(first_parts))
-    w_attention, w_ff, side_copy, stream, hits = results[0:5]
-    kept = results[5:]
+    )(hits, *in_hbm([vectors, up_bias, other_bias]), *resident(first_parts))
+    w_attention, w_ff, side_copy, stream = results[0:4]
+    kept = results[4:]
     received, side_copy = lax.optimization_barrier((second_mine[1:], side_copy))
     second_mine = second_mine[0:1] + received
     second_other = gather_cores(second_mine)

time: 157 us -> 158 us (level)
  waiting for transfers between devices: 22.7 us -> 28 us
  starting transfers between devices: 37.7 us -> 34.7 us
  Pallas kernels: 79.9 us -> 78.2 us
    ppermute x38, waiting for transfers between devices: 22.7 us -> 28 us  [swap(): return lax.ppermute(a, axis, [(i, i ^ distance) for i in range(size)])]
    ppermute x38, starting transfers between devices: 37.7 us -> 34.7 us  [swap(): return lax.ppermute(a, axis, [(i, i ^ distance) for i in range(size)])]
  transfers between devices with their start and end apart: 38 -> 38, of which waited for: 15 -> 16; matrix products, arithmetic and copies ran while one was open for 1% -> 1% of each run, Pallas kernels for 25% -> 23%
where the time goes in v10:
time: 158 us; the launch traced here: 157 us
  Pallas kernels  78.2 us (49%)
  starting transfers between devices  34.7 us (22%)
  waiting for transfers between devices  28 us (18%)
  blocking collectives  12.4 us (8%)
  other arithmetic  2.59 us (2%)
    pallas_call x1, Pallas kernels, per_device(): call(functools.partial(middle_kernel, fast), (count,), [meta_spec, row_sp...  35.7 us
    ppermute x38, starting transfers between devices, swap(): return lax.ppermute(a, axis, [(i, i ^ distance) for i in range(size)])  34.7 us
    ppermute x38, waiting for transfers between devices, swap(): return lax.ppermute(a, axis, [(i, i ^ distance) for i in range(size)])  28 us
    pallas_call x1, Pallas kernels, per_device(): call(functools.partial(first_forward_kernel, fast), (count,), [hits_spec]...  15.1 us
    pallas_call x1, Pallas kernels, per_device(): call(functools.partial(attention_backward_kernel, fast), (count,), [full_...  12.5 us
    all_to_all x1, blocking collectives, per_device(): gathered = lax.all_to_all(small, 'wide', 0, 0)  12.4 us
    pallas_call x1, Pallas kernels, per_device(): call(functools.partial(ff_backward_kernel, fast), (count,), [full_spec(ve...  6.43 us
  transfers between devices with their start and end apart: 38, of which 16 were waited for; matrix products, arithmetic and copies ran while one was open for 1% of the time, Pallas kernels for 23%

profile of v10, /device:TPU:0, one launch (start us, length us, event | category | flops | bytes accessed | tf_op | source)
XLA Modules:
  0.0 157.1 jit_solution(6894282870419454281)
XLA Ops:
  0.7 1.7 %pack.1 = (bf16[16,2048]{1,0:T(8,128)(2,1)}, bf16[16,1792]{1,0:T(8,128)(2,1)}) custom-call(f32[16,896]{1,0:T(8,128)} %bitcast.89, f32[2,3,16,128]{3,2,1,0:T(8,128)} %refs_3_.3, f32[2,16,128]{2,1,0:T(8,128)} %bitcast.91, f32[2,16,512]{2,1,0:T(8,128)} %refs_9_.1, f32[2,16,512]{2,1,0:T(8,128)} %bitcast.87, f32[16,256]{1,0:T(8,128)} %refs_21_.1, f32[5,16]{1,0:T(8,128)} %bitcast.108), custom_call_target="tpu_custom_call" | custom-call | flops 1000000 | bytes 1000000 | tf_op jit(solution)/shard_map/pack/pallas_call | solution.py:1011
  2.4 5.0 %collective-permute-start.2 = (bf16[16,2048]{1,0:T(8,128)(2,1)}, bf16[16,2048]{1,0:T(8,128)(2,1)S(1)}, u32[]{:S(2)}, u32[]{:S(2)}) collective-permute-start(bf16[16,2048]{1,0:T(8,128)(2,1)} %get-tuple-element.123), channel_id=1, source_target_pairs={{0,24},{2,26},{4,28},{6,30},{8,16},{10,18},{12,20},{14,22},{16,8},... | collective-permute-start | bytes 196616 | tf_op jit(solution)/shard_map/ppermute | solution.py:806
  7.4 0.6 collective-permute-start
  8.0 2.7 %prepare.1 = (s32[4,352,128]{2,1,0:T(8,128)S(1)}, s32[4,32,128]{2,1,0:T(8,128)S(1)}, bf16[4,352,896]{2,1,0:T(8,128)(2,1)S(1)}) custom-call(s32[8]{0:T(128)} %games_ref.1, s32[8,16,20]{2,1,0:T(8,128)} %bitcast.95, s32[8,20]{1,0:T(8,128)} %actions.1, s32[8,20]{1,0:T(8,128)} %valid.1, s32[8,20]{1,0:T(8,128)} %rewards.1, s32[8,20]{1,0:T(8,128)} %ends.1), custom_call_target="tpu_custom_call" | custom-call | flops 1000000 | bytes 1000000 | tf_op jit(solution)/shard_map/prepare/pallas_call | solution.py:1026
  10.8 2.5 %collective-permute-done.1 = bf16[16,2048]{1,0:T(8,128)(2,1)S(1)} collective-permute-done((bf16[16,2048]{1,0:T(8,128)(2,1)}, bf16[16,2048]{1,0:T(8,128)(2,1)S(1)}, u32[]{:S(2)}, u32[]{:S(2)}) %collective-permute-start.1) | collective-permute-done | bytes 65568 | tf_op jit(solution)/shard_map/ppermute | solution.py:806
  13.3 0.9 pad_maximum_fusion.4.refs_4_
  14.2 1.6 %collective-permute-start.14 = (bf16[4,16,2048]{2,1,0:T(8,128)(2,1)S(1)}, bf16[4,16,2048]{2,1,0:T(8,128)(2,1)S(1)}, u32[]{:S(2)}, u32[]{:S(2)}) collective-permute-start(bf16[4,16,2048]{2,1,0:T(8,128)(2,1)S(1)} %pad_maximum_fusion.4.refs_4_), channel_id=1, source_target_pairs={{0,4},{2,6},{4,0},{6,2},{8,12},{10,14},{12,8},{14,10},{16,20},{18,... | collective-permute-start | bytes 786440 | tf_op jit(solution)/shard_map/ppermute | solution.py:806
  15.8 1.4 collective-permute-start.8
  17.2 0.5 collective-permute-start.13
  17.8 2.6 %collective-permute-start.7 = (bf16[16,1792]{1,0:T(8,128)(2,1)}, bf16[16,1792]{1,0:T(8,128)(2,1)S(1)}, u32[]{:S(2)}, u32[]{:S(2)}) collective-permute-start(bf16[16,1792]{1,0:T(8,128)(2,1)} %get-tuple-element.128), channel_id=1, source_target_pairs={{0,24},{2,26},{4,28},{6,30},{8,16},{10,18},{12,20},{14,22},{16,8},... | collective-permute-start | bytes 172040 | tf_op jit(solution)/shard_map/ppermute | solution.py:806
  20.4 8.1 %collective-permute-done.14.refs_6_ = bf16[4,16,2048]{2,1,0:T(8,128)(2,1)S(1)} collective-permute-done((bf16[4,16,2048]{2,1,0:T(8,128)(2,1)S(1)}, bf16[4,16,2048]{2,1,0:T(8,128)(2,1)S(1)}, u32[]{:S(2)}, u32[]{:S(2)}) %collective-permute-start.14) | collective-permute-done | bytes 262176 | tf_op jit(solution)/shard_map/ppermute | solution.py:806
  28.6 1.1 collective-permute-start.5
  29.8 0.4 collective-permute-start.16
  30.3 2.6 %collective-permute-done.5 = bf16[16,1792]{1,0:T(8,128)(2,1)S(1)} collective-permute-done((bf16[16,1792]{1,0:T(8,128)(2,1)}, bf16[16,1792]{1,0:T(8,128)(2,1)S(1)}, u32[]{:S(2)}, u32[]{:S(2)}) %collective-permute-start.5) | collective-permute-done | bytes 57376 | tf_op jit(solution)/shard_map/ppermute | solution.py:806
  32.9 0.8 pad_maximum_fusion.5.refs_7_
  33.9 2.5 %collective-permute-start.12 = (bf16[4,16,1792]{2,1,0:T(8,128)(2,1)S(1)}, bf16[4,16,1792]{2,1,0:T(8,128)(2,1)S(1)}, u32[]{:S(2)}, u32[]{:S(2)}) collective-permute-start(bf16[4,16,1792]{2,1,0:T(8,128)(2,1)S(1)} %pad_maximum_fusion.5.refs_7_), channel_id=1, source_target_pairs={{0,6},{2,4},{4,2},{6,0},{8,14},{10,12},{12,10},{14,8},{16,22},{18,... | collective-permute-start | bytes 688136 | tf_op jit(solution)/shard_map/ppermute | solution.py:806
  36.4 0.5 collective-permute-start.11
  36.9 0.5 collective-permute-start.10
  37.5 15.1 %first_forward.1 = (bf16[256,1024]{1,0:T(8,128)(2,1)S(1)}, bf16[256,2048]{1,0:T(8,128)(2,1)S(1)}, bf16[256,128]{1,0:T(8,128)(2,1)S(1)}, f32[4,352,256]{2,1,0:T(8...) custom-call(bf16[4,352,896]{2,1,0:T(8,128)(2,1)S(1)} %get-tuple-elem, ...), custom_call_target="tpu_custom_call" | custom-call | flops 4000000000 | bytes 20000000 | tf_op jit(solution)/shard_map/first_forward/pallas_call | solution.py:1061
  52.7 0.5 collective-permute-start.19
  53.3 0.9 collective-permute-done.18.refs_12_
  54.9 35.7 %middle.1 = (f32[4,352,256]{2,1,0:T(8,128)S(1)}, bf16[4,4,16,1792]{3,2,1,0:T(8,128)(2,1)S(1)}, bf16[4,4,16,1792]{3,2,1,0:T(8,128)(2,1)S(1)}, f32[32,8,256]{2,1,0:T(8,128)S(1)}, f32[8,128]{1,0:T(8,128)S(1)}) custom-call(s32[4,352,128]{2,1,0:T(8,128)} %copy-done.1, s32[4,32,128]{2,1,0:T(8,128)} %copy-done.2, f32[14,256]{1,0:T(8,128)} %refs_18_.1, ...), custom_call_target="tpu_custom_call" | custom-call | flops 15000000512 | bytes 20000000 | tf_op jit(solution)/shard_map/middle/pallas_call | solution.py:1090
  90.9 6.4 %ff_backward.1 = (f32[4,352,256]{2,1,0:T(8,128)S(1)}, bf16[4,4,16,1024]{3,2,1,0:T(8,128)(2,1)S(1)}, bf16[4,4,16,1024]{3,2,1,0:T(8,128)(2,1)S(1)}, f32[32,8,256]{2,1,0:T(8,128)S(1)}) custom-call(f32[14,256]{1,0:T(8,128)} %refs_18_.1, bf16[256,2048]{1,0:T(8,128)(2,1)S(1)} %get-tuple-element.141.refs_1_, f32[4,352,256]{2,1,0:T(8,128)S(1)} %get-tuple-element.142.refs_2_, ...), custom_call_target="tpu_custom_call" | custom-call | flops 4000000000 | bytes 10000000 | tf_op jit(solution)/shard_map/ff_backward/pallas_call | solution.py:1145
  97.6 1.7 %collective-permute-done.22 = bf16[4,4,16,1024]{3,2,1,0:T(8,128)(2,1)S(1)} collective-permute-done((bf16[4,4,16,1024]{3,2,1,0:T(8,128)(2,1)S(1)}, bf16[4,4,16,1024]{3,2,1,0:T(8,128)(2,1)S(1)}, u32[]{:S(2)}, u32[]{:S(2)}) %collective-permute-start.22) | collective-permute-done | bytes 524320 | tf_op jit(solution)/shard_map/ppermute | solution.py:806
  99.7 1.5 collective-permute-start.23
  101.3 1.6 %collective-permute-start.24 = (bf16[4,16,2816]{2,1,0:T(8,128)(2,1)S(1)}, bf16[4,16,2816]{2,1,0:T(8,128)(2,1)S(1)}, u32[]{:S(2)}, u32[]{:S(2)}) collective-permute-start(bf16[4,16,2816]{2,1,0:T(8,128)(2,1)S(1)} %pad_maximum_fusion.2), channel_id=1, source_target_pairs={{0,4},{2,6},{4,0},{6,2},{8,12},{10,14},{12,8},{14,10},{16,20},{18,... | collective-permute-start | bytes 1081352 | tf_op jit(solution)/shard_map/ppermute | solution.py:806
  102.9 0.6 collective-permute-start.25
  103.5 12.5 %attention_backward.1 = (bf16[4,4,16,1024]{3,2,1,0:T(8,128)(2,1)S(1)}, bf16[4,4,16,1024]{3,2,1,0:T(8,128)(2,1)S(1)}, f32[32,256]{1,0:T(8,128)}) custom-call(f32[14,256]{1,0:T(8,128)} %refs_18_.1, bf16[256,1024]{1,0:T(8,128)(2,1)S(1)} %get-tuple-element.151.refs_1_, f32[4,352,256]{2,1,0:T(8,128)S(1)} %get-tuple-element.152.refs_2_, ...), custom_call_target="tpu_custom_call" | custom-call | flops 6000000000 | bytes 20000000 | tf_op jit(solution)/shard_map/attention_backward/pallas_call | solution.py:1170
  116.0 3.4 %collective-permute-done.24 = bf16[4,16,2816]{2,1,0:T(8,128)(2,1)S(1)} collective-permute-done((bf16[4,16,2816]{2,1,0:T(8,128)(2,1)S(1)}, bf16[4,16,2816]{2,1,0:T(8,128)(2,1)S(1)}, u32[]{:S(2)}, u32[]{:S(2)}) %collective-permute-start.24) | collective-permute-done | bytes 360480 | tf_op jit(solution)/shard_map/ppermute | solution.py:806
  119.6 2.7 %collective-permute-start.35 = (bf16[16,2816]{1,0:T(8,128)(2,1)S(1)}, bf16[16,2816]{1,0:T(8,128)(2,1)S(1)}, u32[]{:S(2)}, u32[]{:S(2)}) collective-permute-start(bf16[16,2816]{1,0:T(8,128)(2,1)S(1)} %get-tuple-element.221), channel_id=1, source_target_pairs={{0,24},{2,26},{4,28},{6,30},{8,16},{10,18},{12,20},{14,22},{16,8},... | collective-permute-start | bytes 270344 | tf_op jit(solution)/shard_map/ppermute | solution.py:806
  122.4 1.2 collective-permute-start.27
  123.6 1.8 %collective-permute-start.29 = (bf16[4,16,1024]{2,1,0:T(8,128)(2,1)S(1)}, bf16[4,16,1024]{2,1,0:T(8,128)(2,1)S(1)}, u32[]{:S(2)}, u32[]{:S(2)}) collective-permute-start(bf16[4,16,1024]{2,1,0:T(8,128)(2,1)S(1)} %get-tuple-element.215), channel_id=1, source_target_pairs={{0,6},{2,4},{4,2},{6,0},{8,14},{10,12},{12,10},{14,8},{16,22},{18,... | collective-permute-start | bytes 393224 | tf_op jit(solution)/shard_map/ppermute | solution.py:806
  125.5 0.5 collective-permute-start.28
  126.0 2.2 %collective-permute-done.27 = bf16[4,16,1024]{2,1,0:T(8,128)(2,1)S(1)} collective-permute-done((bf16[4,16,1024]{2,1,0:T(8,128)(2,1)S(1)}, bf16[4,16,1024]{2,1,0:T(8,128)(2,1)S(1)}, u32[]{:S(2)}, u32[]{:S(2)}) %collective-permute-start.27) | collective-permute-done | bytes 131104 | tf_op jit(solution)/shard_map/ppermute | solution.py:806
  128.2 1.5 collective-permute-start.33
  129.6 1.0 collective-permute-done.29
  130.6 1.3 collective-permute-done.28
  132.0 1.7 %collective-permute-start.32 = (bf16[16,1024]{1,0:T(8,128)(2,1)S(1)}, bf16[16,1024]{1,0:T(8,128)(2,1)S(1)}, u32[]{:S(2)}, u32[]{:S(2)}) collective-permute-start(bf16[16,1024]{1,0:T(8,128)(2,1)S(1)} %get-tuple-element.224), channel_id=1, source_target_pairs={{0,24},{2,26},{4,28},{6,30},{8,16},{10,18},{12,20},{14,22},{16,8},... | collective-permute-start | bytes 98312 | tf_op jit(solution)/shard_map/ppermute | solution.py:806
  133.7 1.3 collective-permute-start.31
  135.0 1.5 collective-permute-start.30
  136.5 1.3 collective-permute-done.32.refs_3_
  137.8 0.7 collective-permute-done.31.refs_2_
  138.5 0.4 collective-permute-done.30.refs_1_
  138.9 1.5 finish.1
  140.4 12.4 %all_to_all.5.gathered = f32[16,8,128]{2,1,0:T(8,128)S(1)} all-to-all(f32[16,8,128]{2,1,0:T(8,128)} %get-tuple-element.175), channel_id=1, replica_groups=mesh['wide'=16,'narrow'=2] {'wide'}, dimensions={0} | all-to-all | bytes 131072 | tf_op jit(solution)/shard_map/all_to_all | solution.py:1219
  152.8 0.5 collective-permute-start.36
  153.3 1.1 collective-permute-done.36.swapped
  154.4 2.5 %adam.1 = (f32[1,1]{1,0:T(1,128)}, f32[1,1]{1,0:T(1,128)}, f32[1,1]{1,0:T(1,128)}, f32[16,896]{1,0:T(8,128)}, f32[16,896]{1,0:T(8,128)}, /*index=5*/f32[16,896]{...) custom-call(f32[16,1024]{1,0:T(8,128)} %get-tuple-element.172.rest, ...), custom_call_target="tpu_custom_call" | custom-call | flops 1000000 | bytes 1000000 | tf_op jit(solution)/shard_map/adam/pallas_call | solution.py:1228
  (60 shorter events, 2.8 us)
Async XLA Ops:
  2.4 8.4 %collective-permute-start.2 = (bf16[16,2048]{1,0:T(8,128)(2,1)}, bf16[16,2048]{1,0:T(8,128)(2,1)S(1)}, u32[]{:S(2)}, u32[]{:S(2)}) collective-permute-start(bf16[16,2048]{1,0:T(8,128)(2,1)} %get-tuple-element.123), channel_id=1, source_target_pairs={{0,24},{2,26},{4,28},{6,30},{8,16},{10,18},{12,20},{14,22},{16,8},... | collective-permute-start | bytes 196616 | tf_op jit(solution)/shard_map/ppermute | solution.py:806
  7.4 5.8 %collective-permute-start.1 = (bf16[16,2048]{1,0:T(8,128)(2,1)}, bf16[16,2048]{1,0:T(8,128)(2,1)S(1)}, u32[]{:S(2)}, u32[]{:S(2)}) collective-permute-start(bf16[16,2048]{1,0:T(8,128)(2,1)} %get-tuple-element.123), channel_id=1, source_target_pairs={{0,16},{2,18},{4,20},{6,22},{8,24},{10,26},{12,28},{14,30},{16,0},... | collective-permute-start | bytes 196616 | tf_op jit(solution)/shard_map/ppermute | solution.py:806
  7.4 5.8 %collective-permute-start = (bf16[16,2048]{1,0:T(8,128)(2,1)}, bf16[16,2048]{1,0:T(8,128)(2,1)S(1)}, u32[]{:S(2)}, u32[]{:S(2)}) collective-permute-start(bf16[16,2048]{1,0:T(8,128)(2,1)} %get-tuple-element.123), channel_id=1, source_target_pairs={{0,8},{2,10},{4,12},{6,14},{8,0},{10,2},{12,4},{14,6},{16,24},{18,... | collective-permute-start | bytes 196616 | tf_op jit(solution)/shard_map/ppermute | solution.py:806
  8.0 2.7 %collective-permute-start.3 = (f32[2,512]{1,0:T(2,128)}, f32[2,512]{1,0:T(2,128)S(1)}, u32[]{:S(2)}, u32[]{:S(2)}) collective-permute-start(f32[2,512]{1,0:T(2,128)} %refs_12_.1), channel_id=1, source_target_pairs={{0,1},{1,0},{2,3},{3,2},{4,5},{5,4},{6,7},{7,6},{8,9},{9,8},{10,11... | collective-permute-start | bytes 12296 | tf_op jit(solution)/shard_map/ppermute | solution.py:806
  10.7 26.2 %copy-start.1 = (s32[4,352,128]{2,1,0:T(8,128)}, s32[4,352,128]{2,1,0:T(8,128)S(1)}, u32[]{:S(2)}) copy-start(s32[4,352,128]{2,1,0:T(8,128)S(1)} %get-tuple-element.118.refs_0_) | copy-start | bytes 2162692
  10.7 41.9 %copy-start.2 = (s32[4,32,128]{2,1,0:T(8,128)}, s32[4,32,128]{2,1,0:T(8,128)S(1)}, u32[]{:S(2)}) copy-start(s32[4,32,128]{2,1,0:T(8,128)S(1)} %get-tuple-element.119.refs_1_) | copy-start | bytes 196612
  10.7 26.7 %copy-start.3 = (f32[2,512]{1,0:T(2,128)}, f32[2,512]{1,0:T(2,128)S(1)}, u32[]{:S(2)}) copy-start(f32[2,512]{1,0:T(2,128)S(1)} %collective-permute-done.3.refs_3_.refs_4_) | copy-start | bytes 12292
  14.1 3.6 %collective-permute-start.4 = (bf16[4,16,2048]{2,1,0:T(8,128)(2,1)S(1)}, bf16[4,16,2048]{2,1,0:T(8,128)(2,1)S(1)}, u32[]{:S(2)}, u32[]{:S(2)}) collective-permute-start(bf16[4,16,2048]{2,1,0:T(8,128)(2,1)S(1)} %pad_maximum_fusion.4.refs_4_), channel_id=1, source_target_pairs={{0,1},{1,0},{2,3},{3,2},{4,5},{5,4},{6,7},{7,6},{8,9},{9,8},{10,11... | collective-permute-start | bytes 786440 | tf_op jit(solution)/shard_map/ppermute | solution.py:806
  14.2 14.3 %collective-permute-start.14 = (bf16[4,16,2048]{2,1,0:T(8,128)(2,1)S(1)}, bf16[4,16,2048]{2,1,0:T(8,128)(2,1)S(1)}, u32[]{:S(2)}, u32[]{:S(2)}) collective-permute-start(bf16[4,16,2048]{2,1,0:T(8,128)(2,1)S(1)} %pad_maximum_fusion.4.refs_4_), channel_id=1, source_target_pairs={{0,4},{2,6},{4,0},{6,2},{8,12},{10,14},{12,8},{14,10},{16,20},{18,... | collective-permute-start | bytes 786440 | tf_op jit(solution)/shard_map/ppermute | solution.py:806
  15.8 13.8 %collective-permute-start.8 = (bf16[4,16,2048]{2,1,0:T(8,128)(2,1)S(1)}, bf16[4,16,2048]{2,1,0:T(8,128)(2,1)S(1)}, u32[]{:S(2)}, u32[]{:S(2)}) collective-permute-start(bf16[4,16,2048]{2,1,0:T(8,128)(2,1)S(1)} %pad_maximum_fusion.4.refs_4_), channel_id=1, source_target_pairs={{0,6},{2,4},{4,2},{6,0},{8,14},{10,12},{12,10},{14,8},{16,22},{18,... | collective-permute-start | bytes 786440 | tf_op jit(solution)/shard_map/ppermute | solution.py:806
  17.2 12.6 %collective-permute-start.13 = (bf16[4,16,2048]{2,1,0:T(8,128)(2,1)S(1)}, bf16[4,16,2048]{2,1,0:T(8,128)(2,1)S(1)}, u32[]{:S(2)}, u32[]{:S(2)}) collective-permute-start(bf16[4,16,2048]{2,1,0:T(8,128)(2,1)S(1)} %pad_maximum_fusion.4.refs_4_), channel_id=1, source_target_pairs={{0,2},{2,0},{4,6},{6,4},{8,10},{10,8},{12,14},{14,12},{16,18},{18,... | collective-permute-start | bytes 786440 | tf_op jit(solution)/shard_map/ppermute | solution.py:806
  17.8 12.4 %collective-permute-start.7 = (bf16[16,1792]{1,0:T(8,128)(2,1)}, bf16[16,1792]{1,0:T(8,128)(2,1)S(1)}, u32[]{:S(2)}, u32[]{:S(2)}) collective-permute-start(bf16[16,1792]{1,0:T(8,128)(2,1)} %get-tuple-element.128), channel_id=1, source_target_pairs={{0,24},{2,26},{4,28},{6,30},{8,16},{10,18},{12,20},{14,22},{16,8},... | collective-permute-start | bytes 172040 | tf_op jit(solution)/shard_map/ppermute | solution.py:806
  20.4 9.9 %collective-permute-start.6 = (bf16[16,1792]{1,0:T(8,128)(2,1)}, bf16[16,1792]{1,0:T(8,128)(2,1)S(1)}, u32[]{:S(2)}, u32[]{:S(2)}) collective-permute-start(bf16[16,1792]{1,0:T(8,128)(2,1)} %get-tuple-element.128), channel_id=1, source_target_pairs={{0,16},{2,18},{4,20},{6,22},{8,24},{10,26},{12,28},{14,30},{16,0},... | collective-permute-start | bytes 172040 | tf_op jit(solution)/shard_map/ppermute | solution.py:806
  28.6 4.4 %collective-permute-start.5 = (bf16[16,1792]{1,0:T(8,128)(2,1)}, bf16[16,1792]{1,0:T(8,128)(2,1)S(1)}, u32[]{:S(2)}, u32[]{:S(2)}) collective-permute-start(bf16[16,1792]{1,0:T(8,128)(2,1)} %get-tuple-element.128), channel_id=1, source_target_pairs={{0,8},{2,10},{4,12},{6,14},{8,0},{10,2},{12,4},{14,6},{16,24},{18,... | collective-permute-start | bytes 172040 | tf_op jit(solution)/shard_map/ppermute | solution.py:806
  29.6 4.2 %collective-permute-start.9 = (bf16[4,16,2048]{2,1,0:T(8,128)(2,1)S(1)}, bf16[4,16,2048]{2,1,0:T(8,128)(2,1)S(1)}, u32[]{:S(2)}, u32[]{:S(2)}) collective-permute-start(bf16[4,16,2048]{2,1,0:T(8,128)(2,1)S(1)} %collective-permute-done.8.refs_7_), channel_id=1, source_target_pairs={{0,1},{1,0},{2,3},{3,2},{4,5},{5,4},{6,7},{7,6},{8,9},{9,8},{10,11... | collective-permute-start | bytes 786440 | tf_op jit(solution)/shard_map/ppermute | solution.py:806
  29.8 7.1 %collective-permute-start.16 = (bf16[4,16,2048]{2,1,0:T(8,128)(2,1)S(1)}, bf16[4,16,2048]{2,1,0:T(8,128)(2,1)S(1)}, u32[]{:S(2)}, u32[]{:S(2)}) collective-permute-start(bf16[4,16,2048]{2,1,0:T(8,128)(2,1)S(1)} %collective-permute-done.14.refs_6_), channel_id=1, source_target_pairs={{0,1},{1,0},{2,3},{3,2},{4,5},{5,4},{6,7},{7,6},{8,9},{9,8},{10,11... | collective-permute-start | bytes 786440 | tf_op jit(solution)/shard_map/ppermute | solution.py:806
  30.2 7.3 %collective-permute-start.15 = (bf16[4,16,2048]{2,1,0:T(8,128)(2,1)S(1)}, bf16[4,16,2048]{2,1,0:T(8,128)(2,1)S(1)}, u32[]{:S(2)}, u32[]{:S(2)}) collective-permute-start(bf16[4,16,2048]{2,1,0:T(8,128)(2,1)S(1)} %collective-permute-done.13.refs_5_), channel_id=1, source_target_pairs={{0,1},{1,0},{2,3},{3,2},{4,5},{5,4},{6,7},{7,6},{8,9},{9,8},{10,11... | collective-permute-start | bytes 786440 | tf_op jit(solution)/shard_map/ppermute | solution.py:806
  33.8 19.5 %collective-permute-start.17 = (bf16[4,16,1792]{2,1,0:T(8,128)(2,1)S(1)}, bf16[4,16,1792]{2,1,0:T(8,128)(2,1)S(1)}, u32[]{:S(2)}, u32[]{:S(2)}) collective-permute-start(bf16[4,16,1792]{2,1,0:T(8,128)(2,1)S(1)} %pad_maximum_fusion.5.refs_7_), channel_id=1, source_target_pairs={{0,1},{1,0},{2,3},{3,2},{4,5},{5,4},{6,7},{7,6},{8,9},{9,8},{10,11... | collective-permute-start | bytes 688136 | tf_op jit(solution)/shard_map/ppermute | solution.py:806
  33.9 18.7 %collective-permute-start.12 = (bf16[4,16,1792]{2,1,0:T(8,128)(2,1)S(1)}, bf16[4,16,1792]{2,1,0:T(8,128)(2,1)S(1)}, u32[]{:S(2)}, u32[]{:S(2)}) collective-permute-start(bf16[4,16,1792]{2,1,0:T(8,128)(2,1)S(1)} %pad_maximum_fusion.5.refs_7_), channel_id=1, source_target_pairs={{0,6},{2,4},{4,2},{6,0},{8,14},{10,12},{12,10},{14,8},{16,22},{18,... | collective-permute-start | bytes 688136 | tf_op jit(solution)/shard_map/ppermute | solution.py:806
  36.4 16.2 %collective-permute-start.11 = (bf16[4,16,1792]{2,1,0:T(8,128)(2,1)S(1)}, bf16[4,16,1792]{2,1,0:T(8,128)(2,1)S(1)}, u32[]{:S(2)}, u32[]{:S(2)}) collective-permute-start(bf16[4,16,1792]{2,1,0:T(8,128)(2,1)S(1)} %pad_maximum_fusion.5.refs_7_), channel_id=1, source_target_pairs={{0,4},{2,6},{4,0},{6,2},{8,12},{10,14},{12,8},{14,10},{16,20},{18,... | collective-permute-start | bytes 688136 | tf_op jit(solution)/shard_map/ppermute | solution.py:806
  36.9 15.7 %collective-permute-start.10 = (bf16[4,16,1792]{2,1,0:T(8,128)(2,1)S(1)}, bf16[4,16,1792]{2,1,0:T(8,128)(2,1)S(1)}, u32[]{:S(2)}, u32[]{:S(2)}) collective-permute-start(bf16[4,16,1792]{2,1,0:T(8,128)(2,1)S(1)} %pad_maximum_fusion.5.refs_7_), channel_id=1, source_target_pairs={{0,2},{2,0},{4,6},{6,4},{8,10},{10,8},{12,14},{14,12},{16,18},{18,... | collective-permute-start | bytes 688136 | tf_op jit(solution)/shard_map/ppermute | solution.py:806
  52.6 1.6 collective-permute-start.18
  52.7 1.8 %collective-permute-start.19 = (bf16[4,16,1792]{2,1,0:T(8,128)(2,1)S(1)}, bf16[4,16,1792]{2,1,0:T(8,128)(2,1)S(1)}, u32[]{:S(2)}, u32[]{:S(2)}) collective-permute-start(bf16[4,16,1792]{2,1,0:T(8,128)(2,1)S(1)} %collective-permute-done.11.refs_9_), channel_id=1, source_target_pairs={{0,1},{1,0},{2,3},{3,2},{4,5},{5,4},{6,7},{7,6},{8,9},{9,8},{10,11... | collective-permute-start | bytes 688136 | tf_op jit(solution)/shard_map/ppermute | solution.py:806
  53.2 1.6 %collective-permute-start.20 = (bf16[4,16,1792]{2,1,0:T(8,128)(2,1)S(1)}, bf16[4,16,1792]{2,1,0:T(8,128)(2,1)S(1)}, u32[]{:S(2)}, u32[]{:S(2)}) collective-permute-start(bf16[4,16,1792]{2,1,0:T(8,128)(2,1)S(1)} %collective-permute-done.12.refs_10_), channel_id=1, source_target_pairs={{0,1},{1,0},{2,3},{3,2},{4,5},{5,4},{6,7},{7,6},{8,9},{9,8},{10,11... | collective-permute-start | bytes 688136 | tf_op jit(solution)/shard_map/ppermute | solution.py:806
  90.6 6.7 %copy-start = (f32[8,128]{1,0:T(8,128)}, f32[8,128]{1,0:T(8,128)S(1)}, u32[]{:S(2)}) copy-start(f32[8,128]{1,0:T(8,128)S(1)} %get-tuple-element.171.refs_8_) | copy-start | bytes 12292
  90.6 8.9 %collective-permute-start.21 = (bf16[4,4,16,1792]{3,2,1,0:T(8,128)(2,1)S(1)}, bf16[4,4,16,1792]{3,2,1,0:T(8,128)(2,1)S(1)}, u32[]{:S(2)}, u32[]{:S(2)}) collective-permute-start(bf16[4,4,16,1792]{3,2,1,0:T(8,128)(2,1)S(1)} %get-tuple-element.140), channel_id=1, source_target_pairs={{0,1},{1,0},{2,3},{3,2},{4,5},{5,4},{6,7},{7,6},{8,9},{9,8},{10,11... | collective-permute-start | bytes 2752520 | tf_op jit(solution)/shard_map/ppermute | solution.py:806
  97.3 2.0 %collective-permute-start.22 = (bf16[4,4,16,1024]{3,2,1,0:T(8,128)(2,1)S(1)}, bf16[4,4,16,1024]{3,2,1,0:T(8,128)(2,1)S(1)}, u32[]{:S(2)}, u32[]{:S(2)}) collective-permute-start(bf16[4,4,16,1024]{3,2,1,0:T(8,128)(2,1)S(1)} %get-tuple-element.150), channel_id=1, source_target_pairs={{0,1},{1,0},{2,3},{3,2},{4,5},{5,4},{6,7},{7,6},{8,9},{9,8},{10,11... | collective-permute-start | bytes 1572872 | tf_op jit(solution)/shard_map/ppermute | solution.py:806
  99.7 16.3 %collective-permute-start.23 = (bf16[4,16,2816]{2,1,0:T(8,128)(2,1)S(1)}, bf16[4,16,2816]{2,1,0:T(8,128)(2,1)S(1)}, u32[]{:S(2)}, u32[]{:S(2)}) collective-permute-start(bf16[4,16,2816]{2,1,0:T(8,128)(2,1)S(1)} %pad_maximum_fusion.1), channel_id=1, source_target_pairs={{0,2},{2,0},{4,6},{6,4},{8,10},{10,8},{12,14},{14,12},{16,18},{18,... | collective-permute-start | bytes 1081352 | tf_op jit(solution)/shard_map/ppermute | solution.py:806
  101.3 18.1 %collective-permute-start.24 = (bf16[4,16,2816]{2,1,0:T(8,128)(2,1)S(1)}, bf16[4,16,2816]{2,1,0:T(8,128)(2,1)S(1)}, u32[]{:S(2)}, u32[]{:S(2)}) collective-permute-start(bf16[4,16,2816]{2,1,0:T(8,128)(2,1)S(1)} %pad_maximum_fusion.2), channel_id=1, source_target_pairs={{0,4},{2,6},{4,0},{6,2},{8,12},{10,14},{12,8},{14,10},{16,20},{18,... | collective-permute-start | bytes 1081352 | tf_op jit(solution)/shard_map/ppermute | solution.py:806
  102.9 16.5 %collective-permute-start.25 = (bf16[4,16,2816]{2,1,0:T(8,128)(2,1)S(1)}, bf16[4,16,2816]{2,1,0:T(8,128)(2,1)S(1)}, u32[]{:S(2)}, u32[]{:S(2)}) collective-permute-start(bf16[4,16,2816]{2,1,0:T(8,128)(2,1)S(1)} %pad_maximum_fusion.3), channel_id=1, source_target_pairs={{0,6},{2,4},{4,2},{6,0},{8,14},{10,12},{12,10},{14,8},{16,22},{18,... | collective-permute-start | bytes 1081352 | tf_op jit(solution)/shard_map/ppermute | solution.py:806
  116.0 6.3 %collective-permute-start.26 = (bf16[4,4,16,1024]{3,2,1,0:T(8,128)(2,1)S(1)}, bf16[4,4,16,1024]{3,2,1,0:T(8,128)(2,1)S(1)}, u32[]{:S(2)}, u32[]{:S(2)}) collective-permute-start(bf16[4,4,16,1024]{3,2,1,0:T(8,128)(2,1)S(1)} %get-tuple-element.167), channel_id=1, source_target_pairs={{0,1},{1,0},{2,3},{3,2},{4,5},{5,4},{6,7},{7,6},{8,9},{9,8},{10,11... | collective-permute-start | bytes 1572872 | tf_op jit(solution)/shard_map/ppermute | solution.py:806
  119.6 15.4 %collective-permute-start.35 = (bf16[16,2816]{1,0:T(8,128)(2,1)S(1)}, bf16[16,2816]{1,0:T(8,128)(2,1)S(1)}, u32[]{:S(2)}, u32[]{:S(2)}) collective-permute-start(bf16[16,2816]{1,0:T(8,128)(2,1)S(1)} %get-tuple-element.221), channel_id=1, source_target_pairs={{0,24},{2,26},{4,28},{6,30},{8,16},{10,18},{12,20},{14,22},{16,8},... | collective-permute-start | bytes 270344 | tf_op jit(solution)/shard_map/ppermute | solution.py:806
  122.3 14.2 %collective-permute-start.34 = (bf16[16,2816]{1,0:T(8,128)(2,1)S(1)}, bf16[16,2816]{1,0:T(8,128)(2,1)S(1)}, u32[]{:S(2)}, u32[]{:S(2)}) collective-permute-start(bf16[16,2816]{1,0:T(8,128)(2,1)S(1)} %get-tuple-element.222), channel_id=1, source_target_pairs={{0,16},{2,18},{4,20},{6,22},{8,24},{10,26},{12,28},{14,30},{16,0},... | collective-permute-start | bytes 270344 | tf_op jit(solution)/shard_map/ppermute | solution.py:806
  122.4 5.7 %collective-permute-start.27 = (bf16[4,16,1024]{2,1,0:T(8,128)(2,1)S(1)}, bf16[4,16,1024]{2,1,0:T(8,128)(2,1)S(1)}, u32[]{:S(2)}, u32[]{:S(2)}) collective-permute-start(bf16[4,16,1024]{2,1,0:T(8,128)(2,1)S(1)} %get-tuple-element.214), channel_id=1, source_target_pairs={{0,2},{2,0},{4,6},{6,4},{8,10},{10,8},{12,14},{14,12},{16,18},{18,... | collective-permute-start | bytes 393224 | tf_op jit(solution)/shard_map/ppermute | solution.py:806
  123.6 7.0 %collective-permute-start.29 = (bf16[4,16,1024]{2,1,0:T(8,128)(2,1)S(1)}, bf16[4,16,1024]{2,1,0:T(8,128)(2,1)S(1)}, u32[]{:S(2)}, u32[]{:S(2)}) collective-permute-start(bf16[4,16,1024]{2,1,0:T(8,128)(2,1)S(1)} %get-tuple-element.215), channel_id=1, source_target_pairs={{0,6},{2,4},{4,2},{6,0},{8,14},{10,12},{12,10},{14,8},{16,22},{18,... | collective-permute-start | bytes 393224 | tf_op jit(solution)/shard_map/ppermute | solution.py:806
  125.5 6.4 %collective-permute-start.28 = (bf16[4,16,1024]{2,1,0:T(8,128)(2,1)S(1)}, bf16[4,16,1024]{2,1,0:T(8,128)(2,1)S(1)}, u32[]{:S(2)}, u32[]{:S(2)}) collective-permute-start(bf16[4,16,1024]{2,1,0:T(8,128)(2,1)S(1)} %get-tuple-element.216), channel_id=1, source_target_pairs={{0,4},{2,6},{4,0},{6,2},{8,12},{10,14},{12,8},{14,10},{16,20},{18,... | collective-permute-start | bytes 393224 | tf_op jit(solution)/shard_map/ppermute | solution.py:806
  128.2 8.3 %collective-permute-start.33 = (bf16[16,2816]{1,0:T(8,128)(2,1)S(1)}, bf16[16,2816]{1,0:T(8,128)(2,1)S(1)}, u32[]{:S(2)}, u32[]{:S(2)}) collective-permute-start(bf16[16,2816]{1,0:T(8,128)(2,1)S(1)} %get-tuple-element.223), channel_id=1, source_target_pairs={{0,8},{2,10},{4,12},{6,14},{8,0},{10,2},{12,4},{14,6},{16,24},{18,... | collective-permute-start | bytes 270344 | tf_op jit(solution)/shard_map/ppermute | solution.py:806
  132.0 5.8 %collective-permute-start.32 = (bf16[16,1024]{1,0:T(8,128)(2,1)S(1)}, bf16[16,1024]{1,0:T(8,128)(2,1)S(1)}, u32[]{:S(2)}, u32[]{:S(2)}) collective-permute-start(bf16[16,1024]{1,0:T(8,128)(2,1)S(1)} %get-tuple-element.224), channel_id=1, source_target_pairs={{0,24},{2,26},{4,28},{6,30},{8,16},{10,18},{12,20},{14,22},{16,8},... | collective-permute-start | bytes 98312 | tf_op jit(solution)/shard_map/ppermute | solution.py:806
  133.7 4.8 %collective-permute-start.31 = (bf16[16,1024]{1,0:T(8,128)(2,1)S(1)}, bf16[16,1024]{1,0:T(8,128)(2,1)S(1)}, u32[]{:S(2)}, u32[]{:S(2)}) collective-permute-start(bf16[16,1024]{1,0:T(8,128)(2,1)S(1)} %get-tuple-element.225), channel_id=1, source_target_pairs={{0,16},{2,18},{4,20},{6,22},{8,24},{10,26},{12,28},{14,30},{16,0},... | collective-permute-start | bytes 98312 | tf_op jit(solution)/shard_map/ppermute | solution.py:806
  135.0 3.9 %collective-permute-start.30 = (bf16[16,1024]{1,0:T(8,128)(2,1)S(1)}, bf16[16,1024]{1,0:T(8,128)(2,1)S(1)}, u32[]{:S(2)}, u32[]{:S(2)}) collective-permute-start(bf16[16,1024]{1,0:T(8,128)(2,1)S(1)} %get-tuple-element.226), channel_id=1, source_target_pairs={{0,8},{2,10},{4,12},{6,14},{8,0},{10,2},{12,4},{14,6},{16,24},{18,... | collective-permute-start | bytes 98312 | tf_op jit(solution)/shard_map/ppermute | solution.py:806
  152.8 1.6 %collective-permute-start.37 = (f32[16,8,128]{2,1,0:T(8,128)S(1)}, f32[16,8,128]{2,1,0:T(8,128)S(1)}, u32[]{:S(2)}, u32[]{:S(2)}) collective-permute-start(f32[16,8,128]{2,1,0:T(8,128)S(1)} %all_to_all.5.gathered), channel_id=1, source_target_pairs={{0,1},{1,0},{2,3},{3,2},{4,5},{5,4},{6,7},{7,6},{8,9},{9,8},{10,11... | collective-permute-start | bytes 196616 | tf_op jit(solution)/shard_map/ppermute | solution.py:806
  152.8 1.6 %collective-permute-start.36 = (f32[16,512]{1,0:T(8,128)}, f32[16,512]{1,0:T(8,128)S(1)}, u32[]{:S(2)}, u32[]{:S(2)}) collective-permute-start(f32[16,512]{1,0:T(8,128)} %get-tuple-element.174), channel_id=1, source_target_pairs={{0,1},{1,0},{2,3},{3,2},{4,5},{5,4},{6,7},{7,6},{8,9},{9,8},{10,11... | collective-permute-start | bytes 98312 | tf_op jit(solution)/shard_map/ppermute | solution.py:806

commit v11 on v10

--- a/solution.py
+++ b/solution.py
@@ -1043,8 +1043,13 @@
     first_mine = gather_plane(first_column)
     own, piece_second = lax.optimization_barrier((swap(first_column, "narrow", 1), piece_second))
     first_other = [own] + gather_cores(first_mine[1:])
-    second_column = jnp.stack(swap_column(piece_second, n_high))
-    second_column, across = lax.optimization_barrier((second_column, first_other[3]))
+    near = swap(piece_second, "wide", 4)
+    near, far_piece = lax.optimization_barrier((near, piece_second))
+    second_column = [piece_second, near, swap(piece_second, "wide", 8)]
+    second_column += [swap(far_piece, "wide", 4 * k) for k in range(3, n_high)]
+    second_column, across = lax.optimization_barrier(
+        (jnp.stack(second_column), first_other[3])
+    )
     first_other = first_other[0:3] + [across]
     second_mine = gather_plane(second_column)
     first_parts = in_blocks(first_mine, wide) + in_blocks(first_other, wide)
@@ -1194,9 +1199,13 @@
         other_sums[0],
     )
     others_received, keep_rest = lax.optimization_barrier((others_received, keep_rest))
-    rest_sums = add_cores(keep_rest, send_rest, wide, n_high)
+    others = add_plane(other_sums[0], others_received)
+    keep_rest = in_pieces(keep_rest, wide, n_high)
+    received = swap(in_pieces(send_rest, wide, n_high), "narrow", 1)
+    others, received = lax.optimization_barrier((others, received))
+    rest_sums = [keep_rest[p].astype(F32) + received[p].astype(F32) for p in range(4)]
     rest_received = swap_plane(rest_sums)
-    other_pieces = column_pieces(add_plane(other_sums[0], others_received))
+    other_pieces = column_pieces(others)
     rest_pieces = column_pieces(add_plane(rest_sums[0], rest_received))
 
     grad_rest, grad_others, table_part, small = call(

time: 158 us -> 152 us (0.962)
  waiting for transfers between devices: 28 us -> 20.4 us
  starting transfers between devices: 34.7 us -> 36.9 us
    ppermute x38, waiting for transfers between devices: 28 us -> 20.4 us  [swap(): return lax.ppermute(a, axis, [(i, i ^ distance) for i in range(size)])]
    ppermute x38, starting transfers between devices: 34.7 us -> 36.9 us  [swap(): return lax.ppermute(a, axis, [(i, i ^ distance) for i in range(size)])]
  transfers between devices with their start and end apart: 38 -> 38, of which waited for: 16 -> 14; matrix products, arithmetic and copies ran while one was open for 1% -> 1% of each run, Pallas kernels for 23% -> 24%
where the time goes in v11:
time: 152 us; the launch traced here: 151 us
  Pallas kernels  78.2 us (51%)
  starting transfers between devices  36.9 us (24%)
  waiting for transfers between devices  20.4 us (13%)
  blocking collectives  11.8 us (8%)
  other arithmetic  2.63 us (2%)
    ppermute x38, starting transfers between devices, swap(): return lax.ppermute(a, axis, [(i, i ^ distance) for i in range(size)])  36.9 us
    pallas_call x1, Pallas kernels, per_device(): call(functools.partial(middle_kernel, fast), (count,), [meta_spec, row_sp...  35.7 us
    ppermute x38, waiting for transfers between devices, swap(): return lax.ppermute(a, axis, [(i, i ^ distance) for i in range(size)])  20.4 us
    pallas_call x1, Pallas kernels, per_device(): call(functools.partial(first_forward_kernel, fast), (count,), [hits_spec]...  15.1 us
    pallas_call x1, Pallas kernels, per_device(): call(functools.partial(attention_backward_kernel, fast), (count,), [full_...  12.5 us
    all_to_all x1, blocking collectives, per_device(): gathered = lax.all_to_all(small, 'wide', 0, 0)  11.8 us
    pallas_call x1, Pallas kernels, per_device(): call(functools.partial(ff_backward_kernel, fast), (count,), [full_spec(ve...  6.43 us
  transfers between devices with their start and end apart: 38, of which 14 were waited for; matrix products, arithmetic and copies ran while one was open for 1% of the time, Pallas kernels for 24%

profile of v11, /device:TPU:0, one launch (start us, length us, event | category | flops | bytes accessed | tf_op | source)
XLA Modules:
  0.0 151.2 jit_solution(1634940202491871963)
XLA Ops:
  0.7 1.7 %pack.1 = (bf16[16,2048]{1,0:T(8,128)(2,1)}, bf16[16,1792]{1,0:T(8,128)(2,1)}) custom-call(f32[16,896]{1,0:T(8,128)} %bitcast.89, f32[2,3,16,128]{3,2,1,0:T(8,128)} %refs_3_.3, f32[2,16,128]{2,1,0:T(8,128)} %bitcast.91, f32[2,16,512]{2,1,0:T(8,128)} %refs_9_.1, f32[2,16,512]{2,1,0:T(8,128)} %bitcast.87, f32[16,256]{1,0:T(8,128)} %refs_21_.1, f32[5,16]{1,0:T(8,128)} %bitcast.108), custom_call_target="tpu_custom_call" | custom-call | flops 1000000 | bytes 1000000 | tf_op jit(solution)/shard_map/pack/pallas_call | solution.py:1011
  2.4 5.0 %collective-permute-start.2 = (bf16[16,2048]{1,0:T(8,128)(2,1)}, bf16[16,2048]{1,0:T(8,128)(2,1)S(1)}, u32[]{:S(2)}, u32[]{:S(2)}) collective-permute-start(bf16[16,2048]{1,0:T(8,128)(2,1)} %get-tuple-element.127), channel_id=1, source_target_pairs={{0,24},{2,26},{4,28},{6,30},{8,16},{10,18},{12,20},{14,22},{16,8},... | collective-permute-start | bytes 196616 | tf_op jit(solution)/shard_map/ppermute | solution.py:806
  7.4 0.6 collective-permute-start
  8.0 2.7 %prepare.1 = (s32[4,352,128]{2,1,0:T(8,128)S(1)}, s32[4,32,128]{2,1,0:T(8,128)S(1)}, bf16[4,352,896]{2,1,0:T(8,128)(2,1)S(1)}) custom-call(s32[8]{0:T(128)} %games_ref.1, s32[8,16,20]{2,1,0:T(8,128)} %bitcast.95, s32[8,20]{1,0:T(8,128)} %actions.1, s32[8,20]{1,0:T(8,128)} %valid.1, s32[8,20]{1,0:T(8,128)} %rewards.1, s32[8,20]{1,0:T(8,128)} %ends.1), custom_call_target="tpu_custom_call" | custom-call | flops 1000000 | bytes 1000000 | tf_op jit(solution)/shard_map/prepare/pallas_call | solution.py:1026
  10.8 2.5 %collective-permute-done.1 = bf16[16,2048]{1,0:T(8,128)(2,1)S(1)} collective-permute-done((bf16[16,2048]{1,0:T(8,128)(2,1)}, bf16[16,2048]{1,0:T(8,128)(2,1)S(1)}, u32[]{:S(2)}, u32[]{:S(2)}) %collective-permute-start.1) | collective-permute-done | bytes 65568 | tf_op jit(solution)/shard_map/ppermute | solution.py:806
  13.3 0.9 pad_maximum_fusion.4.refs_4_
  14.2 2.5 %collective-permute-start.8 = (bf16[4,16,2048]{2,1,0:T(8,128)(2,1)S(1)}, bf16[4,16,2048]{2,1,0:T(8,128)(2,1)S(1)}, u32[]{:S(2)}, u32[]{:S(2)}) collective-permute-start(bf16[4,16,2048]{2,1,0:T(8,128)(2,1)S(1)} %pad_maximum_fusion.4.refs_4_), channel_id=1, source_target_pairs={{0,6},{2,4},{4,2},{6,0},{8,14},{10,12},{12,10},{14,8},{16,22},{18,... | collective-permute-start | bytes 786440 | tf_op jit(solution)/shard_map/ppermute | solution.py:806
  16.7 0.5 collective-permute-start.14
  17.2 0.5 collective-permute-start.13
  17.8 1.1 collective-permute-start.5
  18.9 2.1 %collective-permute-start.6 = (bf16[16,1792]{1,0:T(8,128)(2,1)}, bf16[16,1792]{1,0:T(8,128)(2,1)S(1)}, u32[]{:S(2)}, u32[]{:S(2)}) collective-permute-start(bf16[16,1792]{1,0:T(8,128)(2,1)} %get-tuple-element.134), channel_id=1, source_target_pairs={{0,16},{2,18},{4,20},{6,22},{8,24},{10,26},{12,28},{14,30},{16,0},... | collective-permute-start | bytes 172040 | tf_op jit(solution)/shard_map/ppermute | solution.py:806
  21.0 1.7 %collective-permute-done.5 = bf16[16,1792]{1,0:T(8,128)(2,1)S(1)} collective-permute-done((bf16[16,1792]{1,0:T(8,128)(2,1)}, bf16[16,1792]{1,0:T(8,128)(2,1)S(1)}, u32[]{:S(2)}, u32[]{:S(2)}) %collective-permute-start.5) | collective-permute-done | bytes 57376 | tf_op jit(solution)/shard_map/ppermute | solution.py:806
  22.6 2.4 %collective-permute-start.7 = (bf16[16,1792]{1,0:T(8,128)(2,1)}, bf16[16,1792]{1,0:T(8,128)(2,1)S(1)}, u32[]{:S(2)}, u32[]{:S(2)}) collective-permute-start(bf16[16,1792]{1,0:T(8,128)(2,1)} %get-tuple-element.134), channel_id=1, source_target_pairs={{0,24},{2,26},{4,28},{6,30},{8,16},{10,18},{12,20},{14,22},{16,8},... | collective-permute-start | bytes 172040 | tf_op jit(solution)/shard_map/ppermute | solution.py:806
  25.1 4.4 %collective-permute-done.14.refs_6_ = bf16[4,16,2048]{2,1,0:T(8,128)(2,1)S(1)} collective-permute-done((bf16[4,16,2048]{2,1,0:T(8,128)(2,1)S(1)}, bf16[4,16,2048]{2,1,0:T(8,128)(2,1)S(1)}, u32[]{:S(2)}, u32[]{:S(2)}) %collective-permute-start.14) | collective-permute-done | bytes 262176 | tf_op jit(solution)/shard_map/ppermute | solution.py:806
  29.6 0.4 collective-permute-start.15
  30.0 0.9 pad_maximum_fusion.5.refs_7_
  31.0 1.7 %collective-permute-start.12 = (bf16[4,16,1792]{2,1,0:T(8,128)(2,1)S(1)}, bf16[4,16,1792]{2,1,0:T(8,128)(2,1)S(1)}, u32[]{:S(2)}, u32[]{:S(2)}) collective-permute-start(bf16[4,16,1792]{2,1,0:T(8,128)(2,1)S(1)} %pad_maximum_fusion.5.refs_7_), channel_id=1, source_target_pairs={{0,6},{2,4},{4,2},{6,0},{8,14},{10,12},{12,10},{14,8},{16,22},{18,... | collective-permute-start | bytes 688136 | tf_op jit(solution)/shard_map/ppermute | solution.py:806
  32.7 1.2 collective-permute-start.11
  34.0 0.5 collective-permute-start.10
  34.5 15.1 %first_forward.1 = (bf16[256,1024]{1,0:T(8,128)(2,1)S(1)}, bf16[256,2048]{1,0:T(8,128)(2,1)S(1)}, bf16[256,128]{1,0:T(8,128)(2,1)S(1)}, f32[4,352,256]{2,1,0:T(8...) custom-call(bf16[4,352,896]{2,1,0:T(8,128)(2,1)S(1)} %get-tuple-elem, ...), custom_call_target="tpu_custom_call" | custom-call | flops 4000000000 | bytes 20000000 | tf_op jit(solution)/shard_map/first_forward/pallas_call | solution.py:1066
  49.8 0.5 collective-permute-start.19
  50.3 0.9 collective-permute-done.18.refs_12_
  51.2 0.3 collective-permute-done.19.refs_13_
  51.6 0.3 collective-permute-done.20.refs_14_
  51.9 35.7 %middle.1 = (f32[4,352,256]{2,1,0:T(8,128)S(1)}, bf16[4,4,16,1792]{3,2,1,0:T(8,128)(2,1)S(1)}, bf16[4,4,16,1792]{3,2,1,0:T(8,128)(2,1)S(1)}, f32[32,8,256]{2,1,0:T(8,128)S(1)}, f32[8,128]{1,0:T(8,128)S(1)}) custom-call(s32[4,352,128]{2,1,0:T(8,128)} %copy-done.1, s32[4,32,128]{2,1,0:T(8,128)} %copy-done.2, f32[14,256]{1,0:T(8,128)} %refs_18_.1, ...), custom_call_target="tpu_custom_call" | custom-call | flops 15000000512 | bytes 20000000 | tf_op jit(solution)/shard_map/middle/pallas_call | solution.py:1095
  87.9 6.4 %ff_backward.1 = (f32[4,352,256]{2,1,0:T(8,128)S(1)}, bf16[4,4,16,1024]{3,2,1,0:T(8,128)(2,1)S(1)}, bf16[4,4,16,1024]{3,2,1,0:T(8,128)(2,1)S(1)}, f32[32,8,256]{2,1,0:T(8,128)S(1)}) custom-call(f32[14,256]{1,0:T(8,128)} %refs_18_.1, bf16[256,2048]{1,0:T(8,128)(2,1)S(1)} %get-tuple-element.147.refs_1_, f32[4,352,256]{2,1,0:T(8,128)S(1)} %get-tuple-element.148.refs_2_, ...), custom_call_target="tpu_custom_call" | custom-call | flops 4000000000 | bytes 10000000 | tf_op jit(solution)/shard_map/ff_backward/pallas_call | solution.py:1150
  94.7 1.7 %collective-permute-done.22 = bf16[4,4,16,1024]{3,2,1,0:T(8,128)(2,1)S(1)} collective-permute-done((bf16[4,4,16,1024]{3,2,1,0:T(8,128)(2,1)S(1)}, bf16[4,4,16,1024]{3,2,1,0:T(8,128)(2,1)S(1)}, u32[]{:S(2)}, u32[]{:S(2)}) %collective-permute-start.22) | collective-permute-done | bytes 524320 | tf_op jit(solution)/shard_map/ppermute | solution.py:806
  96.8 1.6 %collective-permute-start.23 = (bf16[4,16,2816]{2,1,0:T(8,128)(2,1)S(1)}, bf16[4,16,2816]{2,1,0:T(8,128)(2,1)S(1)}, u32[]{:S(2)}, u32[]{:S(2)}) collective-permute-start(bf16[4,16,2816]{2,1,0:T(8,128)(2,1)S(1)} %pad_maximum_fusion.1), channel_id=1, source_target_pairs={{0,2},{2,0},{4,6},{6,4},{8,10},{10,8},{12,14},{14,12},{16,18},{18,... | collective-permute-start | bytes 1081352 | tf_op jit(solution)/shard_map/ppermute | solution.py:806
  98.4 0.9 collective-permute-start.24
  99.3 1.3 collective-permute-start.25
  100.6 12.5 %attention_backward.1 = (bf16[4,4,16,1024]{3,2,1,0:T(8,128)(2,1)S(1)}, bf16[4,4,16,1024]{3,2,1,0:T(8,128)(2,1)S(1)}, f32[32,256]{1,0:T(8,128)}) custom-call(f32[14,256]{1,0:T(8,128)} %refs_18_.1, bf16[256,1024]{1,0:T(8,128)(2,1)S(1)} %get-tuple-element.157.refs_1_, f32[4,352,256]{2,1,0:T(8,128)S(1)} %get-tuple-element.158.refs_2_, ...), custom_call_target="tpu_custom_call" | custom-call | flops 6000000000 | bytes 20000000 | tf_op jit(solution)/shard_map/attention_backward/pallas_call | solution.py:1175
  113.0 3.4 %collective-permute-done.24 = bf16[4,16,2816]{2,1,0:T(8,128)(2,1)S(1)} collective-permute-done((bf16[4,16,2816]{2,1,0:T(8,128)(2,1)S(1)}, bf16[4,16,2816]{2,1,0:T(8,128)(2,1)S(1)}, u32[]{:S(2)}, u32[]{:S(2)}) %collective-permute-start.24) | collective-permute-done | bytes 360480 | tf_op jit(solution)/shard_map/ppermute | solution.py:806
  116.8 0.6 collective-permute-start.27
  117.4 1.7 %collective-permute-start.29 = (bf16[4,16,1024]{2,1,0:T(8,128)(2,1)S(1)}, bf16[4,16,1024]{2,1,0:T(8,128)(2,1)S(1)}, u32[]{:S(2)}, u32[]{:S(2)}) collective-permute-start(bf16[4,16,1024]{2,1,0:T(8,128)(2,1)S(1)} %get-tuple-element.221), channel_id=1, source_target_pairs={{0,6},{2,4},{4,2},{6,0},{8,14},{10,12},{12,10},{14,8},{16,22},{18,... | collective-permute-start | bytes 393224 | tf_op jit(solution)/shard_map/ppermute | solution.py:806
  119.1 1.2 collective-permute-start.28
  120.4 2.7 %collective-permute-start.35 = (bf16[16,2816]{1,0:T(8,128)(2,1)S(1)}, bf16[16,2816]{1,0:T(8,128)(2,1)S(1)}, u32[]{:S(2)}, u32[]{:S(2)}) collective-permute-start(bf16[16,2816]{1,0:T(8,128)(2,1)S(1)} %get-tuple-element.227), channel_id=1, source_target_pairs={{0,24},{2,26},{4,28},{6,30},{8,16},{10,18},{12,20},{14,22},{16,8},... | collective-permute-start | bytes 270344 | tf_op jit(solution)/shard_map/ppermute | solution.py:806
  123.1 1.7 %collective-permute-start.33 = (bf16[16,2816]{1,0:T(8,128)(2,1)S(1)}, bf16[16,2816]{1,0:T(8,128)(2,1)S(1)}, u32[]{:S(2)}, u32[]{:S(2)}) collective-permute-start(bf16[16,2816]{1,0:T(8,128)(2,1)S(1)} %get-tuple-element.229), channel_id=1, source_target_pairs={{0,8},{2,10},{4,12},{6,14},{8,0},{10,2},{12,4},{14,6},{16,24},{18,... | collective-permute-start | bytes 270344 | tf_op jit(solution)/shard_map/ppermute | solution.py:806
  124.8 1.1 collective-permute-done.28
  126.0 2.7 %collective-permute-start.32 = (bf16[16,1024]{1,0:T(8,128)(2,1)S(1)}, bf16[16,1024]{1,0:T(8,128)(2,1)S(1)}, u32[]{:S(2)}, u32[]{:S(2)}) collective-permute-start(bf16[16,1024]{1,0:T(8,128)(2,1)S(1)} %get-tuple-element.230), channel_id=1, source_target_pairs={{0,24},{2,26},{4,28},{6,30},{8,16},{10,18},{12,20},{14,22},{16,8},... | collective-permute-start | bytes 98312 | tf_op jit(solution)/shard_map/ppermute | solution.py:806
  128.7 1.7 %collective-permute-start.30 = (bf16[16,1024]{1,0:T(8,128)(2,1)S(1)}, bf16[16,1024]{1,0:T(8,128)(2,1)S(1)}, u32[]{:S(2)}, u32[]{:S(2)}) collective-permute-start(bf16[16,1024]{1,0:T(8,128)(2,1)S(1)} %get-tuple-element.232), channel_id=1, source_target_pairs={{0,8},{2,10},{4,12},{6,14},{8,0},{10,2},{12,4},{14,6},{16,24},{18,... | collective-permute-start | bytes 98312 | tf_op jit(solution)/shard_map/ppermute | solution.py:806
  130.5 0.5 collective-permute-done.34.refs_6_
  130.9 1.0 collective-permute-done.32.refs_3_
  131.9 1.7 %collective-permute-done.31.refs_2_ = bf16[16,1024]{1,0:T(8,128)(2,1)S(1)} collective-permute-done((bf16[16,1024]{1,0:T(8,128)(2,1)S(1)}, bf16[16,1024]{1,0:T(8,128)(2,1)S(1)}, u32[]{:S(2)}, u32[]{:S(2)}) %collective-permute-start.31) | collective-permute-done | bytes 32800 | tf_op jit(solution)/shard_map/ppermute | solution.py:806
  133.6 1.5 finish.1
  135.0 11.8 %all_to_all.5.gathered = f32[16,8,128]{2,1,0:T(8,128)S(1)} all-to-all(f32[16,8,128]{2,1,0:T(8,128)} %get-tuple-element.183), channel_id=1, replica_groups=mesh['wide'=16,'narrow'=2] {'wide'}, dimensions={0} | all-to-all | bytes 131072 | tf_op jit(solution)/shard_map/all_to_all | solution.py:1228
  146.9 0.5 collective-permute-start.36
  147.4 1.1 collective-permute-done.36.swapped
  148.5 2.5 %adam.1 = (f32[1,1]{1,0:T(1,128)}, f32[1,1]{1,0:T(1,128)}, f32[1,1]{1,0:T(1,128)}, f32[16,896]{1,0:T(8,128)}, f32[16,896]{1,0:T(8,128)}, /*index=5*/f32[16,896]{...) custom-call(f32[16,1024]{1,0:T(8,128)} %get-tuple-element.180.rest, ...), custom_call_target="tpu_custom_call" | custom-call | flops 1000000 | bytes 1000000 | tf_op jit(solution)/shard_map/adam/pallas_call | solution.py:1237
  (61 shorter events, 2.1 us)
Async XLA Ops:
  2.4 8.4 %collective-permute-start.2 = (bf16[16,2048]{1,0:T(8,128)(2,1)}, bf16[16,2048]{1,0:T(8,128)(2,1)S(1)}, u32[]{:S(2)}, u32[]{:S(2)}) collective-permute-start(bf16[16,2048]{1,0:T(8,128)(2,1)} %get-tuple-element.127), channel_id=1, source_target_pairs={{0,24},{2,26},{4,28},{6,30},{8,16},{10,18},{12,20},{14,22},{16,8},... | collective-permute-start | bytes 196616 | tf_op jit(solution)/shard_map/ppermute | solution.py:806
  7.4 5.8 %collective-permute-start.1 = (bf16[16,2048]{1,0:T(8,128)(2,1)}, bf16[16,2048]{1,0:T(8,128)(2,1)S(1)}, u32[]{:S(2)}, u32[]{:S(2)}) collective-permute-start(bf16[16,2048]{1,0:T(8,128)(2,1)} %get-tuple-element.127), channel_id=1, source_target_pairs={{0,16},{2,18},{4,20},{6,22},{8,24},{10,26},{12,28},{14,30},{16,0},... | collective-permute-start | bytes 196616 | tf_op jit(solution)/shard_map/ppermute | solution.py:806
  7.4 5.8 %collective-permute-start = (bf16[16,2048]{1,0:T(8,128)(2,1)}, bf16[16,2048]{1,0:T(8,128)(2,1)S(1)}, u32[]{:S(2)}, u32[]{:S(2)}) collective-permute-start(bf16[16,2048]{1,0:T(8,128)(2,1)} %get-tuple-element.127), channel_id=1, source_target_pairs={{0,8},{2,10},{4,12},{6,14},{8,0},{10,2},{12,4},{14,6},{16,24},{18,... | collective-permute-start | bytes 196616 | tf_op jit(solution)/shard_map/ppermute | solution.py:806
  8.0 2.7 %collective-permute-start.3 = (f32[2,512]{1,0:T(2,128)}, f32[2,512]{1,0:T(2,128)S(1)}, u32[]{:S(2)}, u32[]{:S(2)}) collective-permute-start(f32[2,512]{1,0:T(2,128)} %refs_12_.1), channel_id=1, source_target_pairs={{0,1},{1,0},{2,3},{3,2},{4,5},{5,4},{6,7},{7,6},{8,9},{9,8},{10,11... | collective-permute-start | bytes 12296 | tf_op jit(solution)/shard_map/ppermute | solution.py:806
  10.7 23.3 %copy-start.1 = (s32[4,352,128]{2,1,0:T(8,128)}, s32[4,352,128]{2,1,0:T(8,128)S(1)}, u32[]{:S(2)}) copy-start(s32[4,352,128]{2,1,0:T(8,128)S(1)} %get-tuple-element.122.refs_0_) | copy-start | bytes 2162692
  10.7 38.9 %copy-start.2 = (s32[4,32,128]{2,1,0:T(8,128)}, s32[4,32,128]{2,1,0:T(8,128)S(1)}, u32[]{:S(2)}) copy-start(s32[4,32,128]{2,1,0:T(8,128)S(1)} %get-tuple-element.123.refs_1_) | copy-start | bytes 196612
  10.7 23.8 %copy-start.3 = (f32[2,512]{1,0:T(2,128)}, f32[2,512]{1,0:T(2,128)S(1)}, u32[]{:S(2)}) copy-start(f32[2,512]{1,0:T(2,128)S(1)} %collective-permute-done.3.refs_3_.refs_4_) | copy-start | bytes 12292
  14.1 3.6 %collective-permute-start.4 = (bf16[4,16,2048]{2,1,0:T(8,128)(2,1)S(1)}, bf16[4,16,2048]{2,1,0:T(8,128)(2,1)S(1)}, u32[]{:S(2)}, u32[]{:S(2)}) collective-permute-start(bf16[4,16,2048]{2,1,0:T(8,128)(2,1)S(1)} %pad_maximum_fusion.4.refs_4_), channel_id=1, source_target_pairs={{0,1},{1,0},{2,3},{3,2},{4,5},{5,4},{6,7},{7,6},{8,9},{9,8},{10,11... | collective-permute-start | bytes 786440 | tf_op jit(solution)/shard_map/ppermute | solution.py:806
  14.2 10.9 %collective-permute-start.8 = (bf16[4,16,2048]{2,1,0:T(8,128)(2,1)S(1)}, bf16[4,16,2048]{2,1,0:T(8,128)(2,1)S(1)}, u32[]{:S(2)}, u32[]{:S(2)}) collective-permute-start(bf16[4,16,2048]{2,1,0:T(8,128)(2,1)S(1)} %pad_maximum_fusion.4.refs_4_), channel_id=1, source_target_pairs={{0,6},{2,4},{4,2},{6,0},{8,14},{10,12},{12,10},{14,8},{16,22},{18,... | collective-permute-start | bytes 786440 | tf_op jit(solution)/shard_map/ppermute | solution.py:806
  16.7 12.7 %collective-permute-start.14 = (bf16[4,16,2048]{2,1,0:T(8,128)(2,1)S(1)}, bf16[4,16,2048]{2,1,0:T(8,128)(2,1)S(1)}, u32[]{:S(2)}, u32[]{:S(2)}) collective-permute-start(bf16[4,16,2048]{2,1,0:T(8,128)(2,1)S(1)} %pad_maximum_fusion.4.refs_4_), channel_id=1, source_target_pairs={{0,4},{2,6},{4,0},{6,2},{8,12},{10,14},{12,8},{14,10},{16,20},{18,... | collective-permute-start | bytes 786440 | tf_op jit(solution)/shard_map/ppermute | solution.py:806
  17.2 12.3 %collective-permute-start.13 = (bf16[4,16,2048]{2,1,0:T(8,128)(2,1)S(1)}, bf16[4,16,2048]{2,1,0:T(8,128)(2,1)S(1)}, u32[]{:S(2)}, u32[]{:S(2)}) collective-permute-start(bf16[4,16,2048]{2,1,0:T(8,128)(2,1)S(1)} %pad_maximum_fusion.4.refs_4_), channel_id=1, source_target_pairs={{0,2},{2,0},{4,6},{6,4},{8,10},{10,8},{12,14},{14,12},{16,18},{18,... | collective-permute-start | bytes 786440 | tf_op jit(solution)/shard_map/ppermute | solution.py:806
  17.8 4.9 %collective-permute-start.5 = (bf16[16,1792]{1,0:T(8,128)(2,1)}, bf16[16,1792]{1,0:T(8,128)(2,1)S(1)}, u32[]{:S(2)}, u32[]{:S(2)}) collective-permute-start(bf16[16,1792]{1,0:T(8,128)(2,1)} %get-tuple-element.134), channel_id=1, source_target_pairs={{0,8},{2,10},{4,12},{6,14},{8,0},{10,2},{12,4},{14,6},{16,24},{18,... | collective-permute-start | bytes 172040 | tf_op jit(solution)/shard_map/ppermute | solution.py:806
  18.9 11.1 %collective-permute-start.6 = (bf16[16,1792]{1,0:T(8,128)(2,1)}, bf16[16,1792]{1,0:T(8,128)(2,1)S(1)}, u32[]{:S(2)}, u32[]{:S(2)}) collective-permute-start(bf16[16,1792]{1,0:T(8,128)(2,1)} %get-tuple-element.134), channel_id=1, source_target_pairs={{0,16},{2,18},{4,20},{6,22},{8,24},{10,26},{12,28},{14,30},{16,0},... | collective-permute-start | bytes 172040 | tf_op jit(solution)/shard_map/ppermute | solution.py:806
  22.6 7.3 %collective-permute-start.7 = (bf16[16,1792]{1,0:T(8,128)(2,1)}, bf16[16,1792]{1,0:T(8,128)(2,1)S(1)}, u32[]{:S(2)}, u32[]{:S(2)}) collective-permute-start(bf16[16,1792]{1,0:T(8,128)(2,1)} %get-tuple-element.134), channel_id=1, source_target_pairs={{0,24},{2,26},{4,28},{6,30},{8,16},{10,18},{12,20},{14,22},{16,8},... | collective-permute-start | bytes 172040 | tf_op jit(solution)/shard_map/ppermute | solution.py:806
  25.1 5.7 %collective-permute-start.9 = (bf16[4,16,2048]{2,1,0:T(8,128)(2,1)S(1)}, bf16[4,16,2048]{2,1,0:T(8,128)(2,1)S(1)}, u32[]{:S(2)}, u32[]{:S(2)}) collective-permute-start(bf16[4,16,2048]{2,1,0:T(8,128)(2,1)S(1)} %collective-permute-done.8.refs_7_), channel_id=1, source_target_pairs={{0,1},{1,0},{2,3},{3,2},{4,5},{5,4},{6,7},{7,6},{8,9},{9,8},{10,11... | collective-permute-start | bytes 786440 | tf_op jit(solution)/shard_map/ppermute | solution.py:806
  29.5 4.5 %collective-permute-start.16 = (bf16[4,16,2048]{2,1,0:T(8,128)(2,1)S(1)}, bf16[4,16,2048]{2,1,0:T(8,128)(2,1)S(1)}, u32[]{:S(2)}, u32[]{:S(2)}) collective-permute-start(bf16[4,16,2048]{2,1,0:T(8,128)(2,1)S(1)} %collective-permute-done.14.refs_6_), channel_id=1, source_target_pairs={{0,1},{1,0},{2,3},{3,2},{4,5},{5,4},{6,7},{7,6},{8,9},{9,8},{10,11... | collective-permute-start | bytes 786440 | tf_op jit(solution)/shard_map/ppermute | solution.py:806
  29.6 4.9 %collective-permute-start.15 = (bf16[4,16,2048]{2,1,0:T(8,128)(2,1)S(1)}, bf16[4,16,2048]{2,1,0:T(8,128)(2,1)S(1)}, u32[]{:S(2)}, u32[]{:S(2)}) collective-permute-start(bf16[4,16,2048]{2,1,0:T(8,128)(2,1)S(1)} %collective-permute-done.13.refs_5_), channel_id=1, source_target_pairs={{0,1},{1,0},{2,3},{3,2},{4,5},{5,4},{6,7},{7,6},{8,9},{9,8},{10,11... | collective-permute-start | bytes 786440 | tf_op jit(solution)/shard_map/ppermute | solution.py:806
  30.8 19.5 %collective-permute-start.17 = (bf16[4,16,1792]{2,1,0:T(8,128)(2,1)S(1)}, bf16[4,16,1792]{2,1,0:T(8,128)(2,1)S(1)}, u32[]{:S(2)}, u32[]{:S(2)}) collective-permute-start(bf16[4,16,1792]{2,1,0:T(8,128)(2,1)S(1)} %pad_maximum_fusion.5.refs_7_), channel_id=1, source_target_pairs={{0,1},{1,0},{2,3},{3,2},{4,5},{5,4},{6,7},{7,6},{8,9},{9,8},{10,11... | collective-permute-start | bytes 688136 | tf_op jit(solution)/shard_map/ppermute | solution.py:806
  31.0 18.7 %collective-permute-start.12 = (bf16[4,16,1792]{2,1,0:T(8,128)(2,1)S(1)}, bf16[4,16,1792]{2,1,0:T(8,128)(2,1)S(1)}, u32[]{:S(2)}, u32[]{:S(2)}) collective-permute-start(bf16[4,16,1792]{2,1,0:T(8,128)(2,1)S(1)} %pad_maximum_fusion.5.refs_7_), channel_id=1, source_target_pairs={{0,6},{2,4},{4,2},{6,0},{8,14},{10,12},{12,10},{14,8},{16,22},{18,... | collective-permute-start | bytes 688136 | tf_op jit(solution)/shard_map/ppermute | solution.py:806
  32.7 16.9 %collective-permute-start.11 = (bf16[4,16,1792]{2,1,0:T(8,128)(2,1)S(1)}, bf16[4,16,1792]{2,1,0:T(8,128)(2,1)S(1)}, u32[]{:S(2)}, u32[]{:S(2)}) collective-permute-start(bf16[4,16,1792]{2,1,0:T(8,128)(2,1)S(1)} %pad_maximum_fusion.5.refs_7_), channel_id=1, source_target_pairs={{0,4},{2,6},{4,0},{6,2},{8,12},{10,14},{12,8},{14,10},{16,20},{18,... | collective-permute-start | bytes 688136 | tf_op jit(solution)/shard_map/ppermute | solution.py:806
  34.0 15.7 %collective-permute-start.10 = (bf16[4,16,1792]{2,1,0:T(8,128)(2,1)S(1)}, bf16[4,16,1792]{2,1,0:T(8,128)(2,1)S(1)}, u32[]{:S(2)}, u32[]{:S(2)}) collective-permute-start(bf16[4,16,1792]{2,1,0:T(8,128)(2,1)S(1)} %pad_maximum_fusion.5.refs_7_), channel_id=1, source_target_pairs={{0,2},{2,0},{4,6},{6,4},{8,10},{10,8},{12,14},{14,12},{16,18},{18,... | collective-permute-start | bytes 688136 | tf_op jit(solution)/shard_map/ppermute | solution.py:806
  49.7 1.6 %collective-permute-start.18 = (bf16[4,16,1792]{2,1,0:T(8,128)(2,1)S(1)}, bf16[4,16,1792]{2,1,0:T(8,128)(2,1)S(1)}, u32[]{:S(2)}, u32[]{:S(2)}) collective-permute-start(bf16[4,16,1792]{2,1,0:T(8,128)(2,1)S(1)} %collective-permute-done.10.refs_8_), channel_id=1, source_target_pairs={{0,1},{1,0},{2,3},{3,2},{4,5},{5,4},{6,7},{7,6},{8,9},{9,8},{10,11... | collective-permute-start | bytes 688136 | tf_op jit(solution)/shard_map/ppermute | solution.py:806
  49.8 1.8 %collective-permute-start.19 = (bf16[4,16,1792]{2,1,0:T(8,128)(2,1)S(1)}, bf16[4,16,1792]{2,1,0:T(8,128)(2,1)S(1)}, u32[]{:S(2)}, u32[]{:S(2)}) collective-permute-start(bf16[4,16,1792]{2,1,0:T(8,128)(2,1)S(1)} %collective-permute-done.11.refs_9_), channel_id=1, source_target_pairs={{0,1},{1,0},{2,3},{3,2},{4,5},{5,4},{6,7},{7,6},{8,9},{9,8},{10,11... | collective-permute-start | bytes 688136 | tf_op jit(solution)/shard_map/ppermute | solution.py:806
  50.3 1.6 %collective-permute-start.20 = (bf16[4,16,1792]{2,1,0:T(8,128)(2,1)S(1)}, bf16[4,16,1792]{2,1,0:T(8,128)(2,1)S(1)}, u32[]{:S(2)}, u32[]{:S(2)}) collective-permute-start(bf16[4,16,1792]{2,1,0:T(8,128)(2,1)S(1)} %collective-permute-done.12.refs_10_), channel_id=1, source_target_pairs={{0,1},{1,0},{2,3},{3,2},{4,5},{5,4},{6,7},{7,6},{8,9},{9,8},{10,11... | collective-permute-start | bytes 688136 | tf_op jit(solution)/shard_map/ppermute | solution.py:806
  87.6 6.7 %copy-start = (f32[8,128]{1,0:T(8,128)}, f32[8,128]{1,0:T(8,128)S(1)}, u32[]{:S(2)}) copy-start(f32[8,128]{1,0:T(8,128)S(1)} %get-tuple-element.179.refs_8_) | copy-start | bytes 12292
  87.7 8.9 %collective-permute-start.21 = (bf16[4,4,16,1792]{3,2,1,0:T(8,128)(2,1)S(1)}, bf16[4,4,16,1792]{3,2,1,0:T(8,128)(2,1)S(1)}, u32[]{:S(2)}, u32[]{:S(2)}) collective-permute-start(bf16[4,4,16,1792]{3,2,1,0:T(8,128)(2,1)S(1)} %get-tuple-element.146), channel_id=1, source_target_pairs={{0,1},{1,0},{2,3},{3,2},{4,5},{5,4},{6,7},{7,6},{8,9},{9,8},{10,11... | collective-permute-start | bytes 2752520 | tf_op jit(solution)/shard_map/ppermute | solution.py:806
  94.4 2.0 %collective-permute-start.22 = (bf16[4,4,16,1024]{3,2,1,0:T(8,128)(2,1)S(1)}, bf16[4,4,16,1024]{3,2,1,0:T(8,128)(2,1)S(1)}, u32[]{:S(2)}, u32[]{:S(2)}) collective-permute-start(bf16[4,4,16,1024]{3,2,1,0:T(8,128)(2,1)S(1)} %get-tuple-element.156), channel_id=1, source_target_pairs={{0,1},{1,0},{2,3},{3,2},{4,5},{5,4},{6,7},{7,6},{8,9},{9,8},{10,11... | collective-permute-start | bytes 1572872 | tf_op jit(solution)/shard_map/ppermute | solution.py:806
  96.8 16.3 %collective-permute-start.23 = (bf16[4,16,2816]{2,1,0:T(8,128)(2,1)S(1)}, bf16[4,16,2816]{2,1,0:T(8,128)(2,1)S(1)}, u32[]{:S(2)}, u32[]{:S(2)}) collective-permute-start(bf16[4,16,2816]{2,1,0:T(8,128)(2,1)S(1)} %pad_maximum_fusion.1), channel_id=1, source_target_pairs={{0,2},{2,0},{4,6},{6,4},{8,10},{10,8},{12,14},{14,12},{16,18},{18,... | collective-permute-start | bytes 1081352 | tf_op jit(solution)/shard_map/ppermute | solution.py:806
  98.4 18.1 %collective-permute-start.24 = (bf16[4,16,2816]{2,1,0:T(8,128)(2,1)S(1)}, bf16[4,16,2816]{2,1,0:T(8,128)(2,1)S(1)}, u32[]{:S(2)}, u32[]{:S(2)}) collective-permute-start(bf16[4,16,2816]{2,1,0:T(8,128)(2,1)S(1)} %pad_maximum_fusion.2), channel_id=1, source_target_pairs={{0,4},{2,6},{4,0},{6,2},{8,12},{10,14},{12,8},{14,10},{16,20},{18,... | collective-permute-start | bytes 1081352 | tf_op jit(solution)/shard_map/ppermute | solution.py:806
  99.3 17.2 %collective-permute-start.25 = (bf16[4,16,2816]{2,1,0:T(8,128)(2,1)S(1)}, bf16[4,16,2816]{2,1,0:T(8,128)(2,1)S(1)}, u32[]{:S(2)}, u32[]{:S(2)}) collective-permute-start(bf16[4,16,2816]{2,1,0:T(8,128)(2,1)S(1)} %pad_maximum_fusion.3), channel_id=1, source_target_pairs={{0,6},{2,4},{4,2},{6,0},{8,14},{10,12},{12,10},{14,8},{16,22},{18,... | collective-permute-start | bytes 1081352 | tf_op jit(solution)/shard_map/ppermute | solution.py:806
  113.0 3.6 %collective-permute-start.26 = (bf16[4,4,16,1024]{3,2,1,0:T(8,128)(2,1)S(1)}, bf16[4,4,16,1024]{3,2,1,0:T(8,128)(2,1)S(1)}, u32[]{:S(2)}, u32[]{:S(2)}) collective-permute-start(bf16[4,4,16,1024]{3,2,1,0:T(8,128)(2,1)S(1)} %get-tuple-element.176), channel_id=1, source_target_pairs={{0,1},{1,0},{2,3},{3,2},{4,5},{5,4},{6,7},{7,6},{8,9},{9,8},{10,11... | collective-permute-start | bytes 1572872 | tf_op jit(solution)/shard_map/ppermute | solution.py:806
  116.8 6.3 %collective-permute-start.27 = (bf16[4,16,1024]{2,1,0:T(8,128)(2,1)S(1)}, bf16[4,16,1024]{2,1,0:T(8,128)(2,1)S(1)}, u32[]{:S(2)}, u32[]{:S(2)}) collective-permute-start(bf16[4,16,1024]{2,1,0:T(8,128)(2,1)S(1)} %get-tuple-element.220), channel_id=1, source_target_pairs={{0,2},{2,0},{4,6},{6,4},{8,10},{10,8},{12,14},{14,12},{16,18},{18,... | collective-permute-start | bytes 393224 | tf_op jit(solution)/shard_map/ppermute | solution.py:806
  117.4 7.4 %collective-permute-start.29 = (bf16[4,16,1024]{2,1,0:T(8,128)(2,1)S(1)}, bf16[4,16,1024]{2,1,0:T(8,128)(2,1)S(1)}, u32[]{:S(2)}, u32[]{:S(2)}) collective-permute-start(bf16[4,16,1024]{2,1,0:T(8,128)(2,1)S(1)} %get-tuple-element.221), channel_id=1, source_target_pairs={{0,6},{2,4},{4,2},{6,0},{8,14},{10,12},{12,10},{14,8},{16,22},{18,... | collective-permute-start | bytes 393224 | tf_op jit(solution)/shard_map/ppermute | solution.py:806
  119.1 6.8 %collective-permute-start.28 = (bf16[4,16,1024]{2,1,0:T(8,128)(2,1)S(1)}, bf16[4,16,1024]{2,1,0:T(8,128)(2,1)S(1)}, u32[]{:S(2)}, u32[]{:S(2)}) collective-permute-start(bf16[4,16,1024]{2,1,0:T(8,128)(2,1)S(1)} %get-tuple-element.222), channel_id=1, source_target_pairs={{0,4},{2,6},{4,0},{6,2},{8,12},{10,14},{12,8},{14,10},{16,20},{18,... | collective-permute-start | bytes 393224 | tf_op jit(solution)/shard_map/ppermute | solution.py:806
  120.4 8.4 %collective-permute-start.35 = (bf16[16,2816]{1,0:T(8,128)(2,1)S(1)}, bf16[16,2816]{1,0:T(8,128)(2,1)S(1)}, u32[]{:S(2)}, u32[]{:S(2)}) collective-permute-start(bf16[16,2816]{1,0:T(8,128)(2,1)S(1)} %get-tuple-element.227), channel_id=1, source_target_pairs={{0,24},{2,26},{4,28},{6,30},{8,16},{10,18},{12,20},{14,22},{16,8},... | collective-permute-start | bytes 270344 | tf_op jit(solution)/shard_map/ppermute | solution.py:806
  123.1 7.8 %collective-permute-start.34 = (bf16[16,2816]{1,0:T(8,128)(2,1)S(1)}, bf16[16,2816]{1,0:T(8,128)(2,1)S(1)}, u32[]{:S(2)}, u32[]{:S(2)}) collective-permute-start(bf16[16,2816]{1,0:T(8,128)(2,1)S(1)} %get-tuple-element.228), channel_id=1, source_target_pairs={{0,16},{2,18},{4,20},{6,22},{8,24},{10,26},{12,28},{14,30},{16,0},... | collective-permute-start | bytes 270344 | tf_op jit(solution)/shard_map/ppermute | solution.py:806
  123.1 7.8 %collective-permute-start.33 = (bf16[16,2816]{1,0:T(8,128)(2,1)S(1)}, bf16[16,2816]{1,0:T(8,128)(2,1)S(1)}, u32[]{:S(2)}, u32[]{:S(2)}) collective-permute-start(bf16[16,2816]{1,0:T(8,128)(2,1)S(1)} %get-tuple-element.229), channel_id=1, source_target_pairs={{0,8},{2,10},{4,12},{6,14},{8,0},{10,2},{12,4},{14,6},{16,24},{18,... | collective-permute-start | bytes 270344 | tf_op jit(solution)/shard_map/ppermute | solution.py:806
  126.0 5.9 %collective-permute-start.32 = (bf16[16,1024]{1,0:T(8,128)(2,1)S(1)}, bf16[16,1024]{1,0:T(8,128)(2,1)S(1)}, u32[]{:S(2)}, u32[]{:S(2)}) collective-permute-start(bf16[16,1024]{1,0:T(8,128)(2,1)S(1)} %get-tuple-element.230), channel_id=1, source_target_pairs={{0,24},{2,26},{4,28},{6,30},{8,16},{10,18},{12,20},{14,22},{16,8},... | collective-permute-start | bytes 98312 | tf_op jit(solution)/shard_map/ppermute | solution.py:806
  128.7 4.8 %collective-permute-start.31 = (bf16[16,1024]{1,0:T(8,128)(2,1)S(1)}, bf16[16,1024]{1,0:T(8,128)(2,1)S(1)}, u32[]{:S(2)}, u32[]{:S(2)}) collective-permute-start(bf16[16,1024]{1,0:T(8,128)(2,1)S(1)} %get-tuple-element.231), channel_id=1, source_target_pairs={{0,16},{2,18},{4,20},{6,22},{8,24},{10,26},{12,28},{14,30},{16,0},... | collective-permute-start | bytes 98312 | tf_op jit(solution)/shard_map/ppermute | solution.py:806
  128.7 4.8 %collective-permute-start.30 = (bf16[16,1024]{1,0:T(8,128)(2,1)S(1)}, bf16[16,1024]{1,0:T(8,128)(2,1)S(1)}, u32[]{:S(2)}, u32[]{:S(2)}) collective-permute-start(bf16[16,1024]{1,0:T(8,128)(2,1)S(1)} %get-tuple-element.232), channel_id=1, source_target_pairs={{0,8},{2,10},{4,12},{6,14},{8,0},{10,2},{12,4},{14,6},{16,24},{18,... | collective-permute-start | bytes 98312 | tf_op jit(solution)/shard_map/ppermute | solution.py:806
  146.9 1.6 %collective-permute-start.37 = (f32[16,8,128]{2,1,0:T(8,128)S(1)}, f32[16,8,128]{2,1,0:T(8,128)S(1)}, u32[]{:S(2)}, u32[]{:S(2)}) collective-permute-start(f32[16,8,128]{2,1,0:T(8,128)S(1)} %all_to_all.5.gathered), channel_id=1, source_target_pairs={{0,1},{1,0},{2,3},{3,2},{4,5},{5,4},{6,7},{7,6},{8,9},{9,8},{10,11... | collective-permute-start | bytes 196616 | tf_op jit(solution)/shard_map/ppermute | solution.py:806
  146.9 1.6 %collective-permute-start.36 = (f32[16,512]{1,0:T(8,128)}, f32[16,512]{1,0:T(8,128)S(1)}, u32[]{:S(2)}, u32[]{:S(2)}) collective-permute-start(f32[16,512]{1,0:T(8,128)} %get-tuple-element.182), channel_id=1, source_target_pairs={{0,1},{1,0},{2,3},{3,2},{4,5},{5,4},{6,7},{7,6},{8,9},{9,8},{10,11... | collective-permute-start | bytes 98312 | tf_op jit(solution)/shard_map/ppermute | solution.py:806

commit v12 on v11

--- a/solution.py
+++ b/solution.py
@@ -680,10 +680,13 @@
     out[:, 1024:1536] = down[layer].astype(BF16)
 
 
-def pack_kernel(fast, table, attn, proj, up, down, head, side, first, second, pad_ref):
+def pack_second_kernel(attn, proj, up, down, head, second):
+    pack_layer(attn, proj, up, down, 0, second)
+    second[:, 1536:1792] = head[...].astype(BF16)
+
+
+def pack_kernel(fast, attn, proj, up, down, table, side, first, pad_ref):
     pack_layer(attn, proj, up, down, 0, first)
-    pack_layer(attn, proj, up, down, 1, second)
-    second[:, 1536:1792] = head[...].astype(BF16)
     rows = side.shape[1]
     eye = (
         lax.broadcasted_iota(jnp.int32, (rows, rows), 0)
@@ -884,13 +887,14 @@
 
 VMEM_MIB = {
     "pack": 58,
+    "pack_second": 58,
     "prepare": 24,
     "first_forward": 22,
     "middle": 28,
     "ff_backward": 15,
     "attention_backward": 22,
-    "finish": 58,
-    "adam": 58,
+    "finish": 24,
+    "adam": 20,
 }
 
 
@@ -1008,17 +1012,34 @@
     )
     table, attn, proj, up, _, down, _, head, side = (group[0] for group in params)
 
-    piece_first, piece_second = call(
+    def one_layer(layer):
+        return [
+            pl.BlockSpec((1,) + a.shape[1:], lambda i, n=len(a.shape): (layer,) + (0,) * (n - 1))
+            for a in (attn, proj, up, down)
+        ]
+
+    piece_first = call(
         functools.partial(pack_kernel, fast),
-        None,
-        [VMEM_SPEC] * 7,
-        [VMEM_SPEC] * 2,
-        [shaped((rows, HALF_FIRST_COLS), BF16), shaped((rows, HALF_SECOND_COLS), BF16)],
+        (1,),
+        one_layer(0) + [VMEM_SPEC] * 2,
+        VMEM_SPEC,
+        shaped((rows, HALF_FIRST_COLS), BF16),
         [pltpu.VMEM((rows, 128), F32)],
         10**6,
         10**6,
         "pack",
-    )(table, attn, proj, up, down, head, side)
+    )(attn, proj, up, down, table, side)
+    piece_second = call(
+        pack_second_kernel,
+        (1,),
+        one_layer(1) + [VMEM_SPEC],
+        VMEM_SPEC,
+        shaped((rows, HALF_SECOND_COLS), BF16),
+        [],
+        10**6,
+        10**6,
+        "pack_second",
+    )(attn, proj, up, down, head)
     other_bias = swap(up_bias, "narrow", 1)
     column = swap_column(piece_first, n_high)
 

time: 152 us -> 150 us (0.987)
  waiting for transfers between devices: 20.4 us -> 18.7 us
    ppermute x38, waiting for transfers between devices: 20.4 us -> 18.7 us  [swap(): return lax.ppermute(a, axis, [(i, i ^ distance) for i in range(size)])]
    pallas_call x1 -> x2, Pallas kernels: 1.73 us -> 3.09 us  [the longest x1 1.65 us: per_device(): call(functools.partial(pack_kernel, fast), (1,), one_layer(0) + [VMEM_SPE...]
  transfers between devices with their start and end apart: 38 -> 38, of which waited for: 14 -> 16; matrix products, arithmetic and copies ran while one was open for 1% -> 1% of each run, Pallas kernels for 24% -> 26%
where the time goes in v12:
time: 150 us
  Pallas kernels  77.4 us (52%)
  starting transfers between devices  36.7 us (24%)
  waiting for transfers between devices  18.7 us (12%)
  blocking collectives  11.6 us (8%)
  other arithmetic  2.63 us (2%)
  between operations  1.5 us (1%)
    ppermute x38, starting transfers between devices, swap(): return lax.ppermute(a, axis, [(i, i ^ distance) for i in range(size)])  36.7 us
    pallas_call x1, Pallas kernels, per_device(): call(functools.partial(middle_kernel, fast), (count,), [meta_spec, row_sp...  35.8 us
    ppermute x38, waiting for transfers between devices, swap(): return lax.ppermute(a, axis, [(i, i ^ distance) for i in range(size)])  18.7 us
    pallas_call x1, Pallas kernels, per_device(): call(functools.partial(first_forward_kernel, fast), (count,), [hits_spec]...  15.2 us
    pallas_call x1, Pallas kernels, per_device(): call(functools.partial(attention_backward_kernel, fast), (count,), [full_...  12.6 us
    all_to_all x1, blocking collectives, per_device(): gathered = lax.all_to_all(small, 'wide', 0, 0)  11.6 us
    pallas_call x1, Pallas kernels, per_device(): call(functools.partial(ff_backward_kernel, fast), (count,), [full_spec(ve...  6.58 us
  transfers between devices with their start and end apart: 38, of which 16 were waited for; matrix products, arithmetic and copies ran while one was open for 1% of the time, Pallas kernels for 26%

profile of v12, /device:TPU:0, one launch (start us, length us, event | category | flops | bytes accessed | tf_op | source)
XLA Modules:
  0.0 149.6 jit_solution(12675935999143240383)
XLA Ops:
  0.7 1.7 %pack.1 = bf16[16,2048]{1,0:T(8,128)(2,1)} custom-call(f32[2,3,16,128]{3,2,1,0:T(8,128)} %refs_3_.3, f32[2,16,128]{2,1,0:T(8,128)} %bitcast.89, f32[2,16,512]{2,1,0:T(8,128)} %refs_9_.1, f32[2,16,512]{2,1,0:T(8,128)} %bitcast.84, f32[16,896]{1,0:T(8,128)} %bitcast.87, f32[5,16]{1,0:T(8,128)} %bitcast.98), custom_call_target="tpu_custom_call" | custom-call | flops 1000000 | bytes 1000000 | tf_op jit(solution)/shard_map/pack/pallas_call | solution.py:1021
  2.3 5.0 %collective-permute-start.2 = (bf16[16,2048]{1,0:T(8,128)(2,1)}, bf16[16,2048]{1,0:T(8,128)(2,1)S(1)}, u32[]{:S(2)}, u32[]{:S(2)}) collective-permute-start(bf16[16,2048]{1,0:T(8,128)(2,1)} %pack.1), channel_id=1, source_target_pairs={{0,24},{2,26},{4,28},{6,30},{8,16},{10,18},{12,20},{14,22},{16,8},... | collective-permute-start | bytes 196616 | tf_op jit(solution)/shard_map/ppermute | solution.py:809
  7.4 0.6 collective-permute-start
  7.9 2.7 %prepare.1 = (s32[4,352,128]{2,1,0:T(8,128)S(1)}, s32[4,32,128]{2,1,0:T(8,128)S(1)}, bf16[4,352,896]{2,1,0:T(8,128)(2,1)S(1)}) custom-call(s32[8]{0:T(128)} %games_ref.1, s32[8,16,20]{2,1,0:T(8,128)} %bitcast.107, s32[8,20]{1,0:T(8,128)} %actions.1, s32[8,20]{1,0:T(8,128)} %valid.1, s32[8,20]{1,0:T(8,128)} %rewards.1, s32[8,20]{1,0:T(8,128)} %ends.1), custom_call_target="tpu_custom_call" | custom-call | flops 1000000 | bytes 1000000 | tf_op jit(solution)/shard_map/prepare/pallas_call | solution.py:1047
  10.6 0.9 copy-done.27
  11.5 1.6 %collective-permute-done.1 = bf16[16,2048]{1,0:T(8,128)(2,1)S(1)} collective-permute-done((bf16[16,2048]{1,0:T(8,128)(2,1)}, bf16[16,2048]{1,0:T(8,128)(2,1)S(1)}, u32[]{:S(2)}, u32[]{:S(2)}) %collective-permute-start.1) | collective-permute-done | bytes 65568 | tf_op jit(solution)/shard_map/ppermute | solution.py:809
  13.2 0.9 pad_maximum_fusion.4.refs_4_
  14.1 2.5 %collective-permute-start.8 = (bf16[4,16,2048]{2,1,0:T(8,128)(2,1)S(1)}, bf16[4,16,2048]{2,1,0:T(8,128)(2,1)S(1)}, u32[]{:S(2)}, u32[]{:S(2)}) collective-permute-start(bf16[4,16,2048]{2,1,0:T(8,128)(2,1)S(1)} %pad_maximum_fusion.4.refs_4_), channel_id=1, source_target_pairs={{0,6},{2,4},{4,2},{6,0},{8,14},{10,12},{12,10},{14,8},{16,22},{18,... | collective-permute-start | bytes 786440 | tf_op jit(solution)/shard_map/ppermute | solution.py:809
  16.7 0.5 collective-permute-start.14
  17.2 0.5 collective-permute-start.13
  17.7 1.4 pack_second.1
  19.1 1.1 collective-permute-start.5
  20.2 2.1 %collective-permute-start.6 = (bf16[16,1792]{1,0:T(8,128)(2,1)}, bf16[16,1792]{1,0:T(8,128)(2,1)S(1)}, u32[]{:S(2)}, u32[]{:S(2)}) collective-permute-start(bf16[16,1792]{1,0:T(8,128)(2,1)} %pack_second.1), channel_id=1, source_target_pairs={{0,16},{2,18},{4,20},{6,22},{8,24},{10,26},{12,28},{14,30},{16,0},... | collective-permute-start | bytes 172040 | tf_op jit(solution)/shard_map/ppermute | solution.py:809
  22.4 1.7 %collective-permute-done.5 = bf16[16,1792]{1,0:T(8,128)(2,1)S(1)} collective-permute-done((bf16[16,1792]{1,0:T(8,128)(2,1)}, bf16[16,1792]{1,0:T(8,128)(2,1)S(1)}, u32[]{:S(2)}, u32[]{:S(2)}) %collective-permute-start.5) | collective-permute-done | bytes 57376 | tf_op jit(solution)/shard_map/ppermute | solution.py:809
  24.0 2.4 %collective-permute-start.7 = (bf16[16,1792]{1,0:T(8,128)(2,1)}, bf16[16,1792]{1,0:T(8,128)(2,1)S(1)}, u32[]{:S(2)}, u32[]{:S(2)}) collective-permute-start(bf16[16,1792]{1,0:T(8,128)(2,1)} %pack_second.1), channel_id=1, source_target_pairs={{0,24},{2,26},{4,28},{6,30},{8,16},{10,18},{12,20},{14,22},{16,8},... | collective-permute-start | bytes 172040 | tf_op jit(solution)/shard_map/ppermute | solution.py:809
  26.5 2.9 %collective-permute-done.14.refs_6_ = bf16[4,16,2048]{2,1,0:T(8,128)(2,1)S(1)} collective-permute-done((bf16[4,16,2048]{2,1,0:T(8,128)(2,1)S(1)}, bf16[4,16,2048]{2,1,0:T(8,128)(2,1)S(1)}, u32[]{:S(2)}, u32[]{:S(2)}) %collective-permute-start.14) | collective-permute-done | bytes 262176 | tf_op jit(solution)/shard_map/ppermute | solution.py:809
  29.5 0.4 collective-permute-start.15
  30.2 0.8 pad_maximum_fusion.5.refs_7_
  31.1 2.5 %collective-permute-start.12 = (bf16[4,16,1792]{2,1,0:T(8,128)(2,1)S(1)}, bf16[4,16,1792]{2,1,0:T(8,128)(2,1)S(1)}, u32[]{:S(2)}, u32[]{:S(2)}) collective-permute-start(bf16[4,16,1792]{2,1,0:T(8,128)(2,1)S(1)} %pad_maximum_fusion.5.refs_7_), channel_id=1, source_target_pairs={{0,6},{2,4},{4,2},{6,0},{8,14},{10,12},{12,10},{14,8},{16,22},{18,... | collective-permute-start | bytes 688136 | tf_op jit(solution)/shard_map/ppermute | solution.py:809
  33.7 0.5 collective-permute-start.11
  34.2 0.5 collective-permute-start.10
  34.7 15.2 %first_forward.1 = (bf16[256,1024]{1,0:T(8,128)(2,1)S(1)}, bf16[256,2048]{1,0:T(8,128)(2,1)S(1)}, bf16[256,128]{1,0:T(8,128)(2,1)S(1)}, f32[4,352,256]{2,1,0:T(8...) custom-call(bf16[4,352,896]{2,1,0:T(8,128)(2,1)S(1)} %get-tuple-elem, ...), custom_call_target="tpu_custom_call" | custom-call | flops 4000000000 | bytes 20000000 | tf_op jit(solution)/shard_map/first_forward/pallas_call | solution.py:1087
  50.0 0.5 collective-permute-start.19
  50.6 0.9 collective-permute-done.18.refs_12_
  51.8 0.3 collective-permute-done.20.refs_14_
  52.1 35.8 %middle.1 = (f32[4,352,256]{2,1,0:T(8,128)S(1)}, bf16[4,4,16,1792]{3,2,1,0:T(8,128)(2,1)S(1)}, bf16[4,4,16,1792]{3,2,1,0:T(8,128)(2,1)S(1)}, f32[32,8,256]{2,1,0:T(8,128)S(1)}, f32[8,128]{1,0:T(8,128)S(1)}) custom-call(s32[4,352,128]{2,1,0:T(8,128)} %copy-done.27, s32[4,32,128]{2,1,0:T(8,128)} %copy-done.28, f32[14,256]{1,0:T(8,128)} %refs_18_.1, ...), custom_call_target="tpu_custom_call" | custom-call | flops 15000000512 | bytes 20000000 | tf_op jit(solution)/shard_map/middle/pallas_call | solution.py:1116
  88.2 6.6 %ff_backward.1 = (f32[4,352,256]{2,1,0:T(8,128)S(1)}, bf16[4,4,16,1024]{3,2,1,0:T(8,128)(2,1)S(1)}, bf16[4,4,16,1024]{3,2,1,0:T(8,128)(2,1)S(1)}, f32[32,8,256]{2,1,0:T(8,128)S(1)}) custom-call(f32[14,256]{1,0:T(8,128)} %refs_18_.1, bf16[256,2048]{1,0:T(8,128)(2,1)S(1)} %get-tuple-element.143.refs_1_, f32[4,352,256]{2,1,0:T(8,128)S(1)} %get-tuple-element.144.refs_2_, ...), custom_call_target="tpu_custom_call" | custom-call | flops 4000000000 | bytes 10000000 | tf_op jit(solution)/shard_map/ff_backward/pallas_call | solution.py:1171
  95.1 1.7 %collective-permute-done.22 = bf16[4,4,16,1024]{3,2,1,0:T(8,128)(2,1)S(1)} collective-permute-done((bf16[4,4,16,1024]{3,2,1,0:T(8,128)(2,1)S(1)}, bf16[4,4,16,1024]{3,2,1,0:T(8,128)(2,1)S(1)}, u32[]{:S(2)}, u32[]{:S(2)}) %collective-permute-start.22) | collective-permute-done | bytes 524320 | tf_op jit(solution)/shard_map/ppermute | solution.py:809
  97.2 1.6 %collective-permute-start.23 = (bf16[4,16,2816]{2,1,0:T(8,128)(2,1)S(1)}, bf16[4,16,2816]{2,1,0:T(8,128)(2,1)S(1)}, u32[]{:S(2)}, u32[]{:S(2)}) collective-permute-start(bf16[4,16,2816]{2,1,0:T(8,128)(2,1)S(1)} %pad_maximum_fusion.1), channel_id=1, source_target_pairs={{0,2},{2,0},{4,6},{6,4},{8,10},{10,8},{12,14},{14,12},{16,18},{18,... | collective-permute-start | bytes 1081352 | tf_op jit(solution)/shard_map/ppermute | solution.py:809
  98.8 1.6 %collective-permute-start.24 = (bf16[4,16,2816]{2,1,0:T(8,128)(2,1)S(1)}, bf16[4,16,2816]{2,1,0:T(8,128)(2,1)S(1)}, u32[]{:S(2)}, u32[]{:S(2)}) collective-permute-start(bf16[4,16,2816]{2,1,0:T(8,128)(2,1)S(1)} %pad_maximum_fusion.2), channel_id=1, source_target_pairs={{0,4},{2,6},{4,0},{6,2},{8,12},{10,14},{12,8},{14,10},{16,20},{18,... | collective-permute-start | bytes 1081352 | tf_op jit(solution)/shard_map/ppermute | solution.py:809
  100.4 0.5 collective-permute-start.25
  101.0 12.6 %attention_backward.1 = (bf16[4,4,16,1024]{3,2,1,0:T(8,128)(2,1)S(1)}, bf16[4,4,16,1024]{3,2,1,0:T(8,128)(2,1)S(1)}, f32[32,256]{1,0:T(8,128)}) custom-call(f32[14,256]{1,0:T(8,128)} %refs_18_.1, bf16[256,1024]{1,0:T(8,128)(2,1)S(1)} %get-tuple-element.153.refs_1_, f32[4,352,256]{2,1,0:T(8,128)S(1)} %get-tuple-element.154.refs_2_, ...), custom_call_target="tpu_custom_call" | custom-call | flops 6000000000 | bytes 20000000 | tf_op jit(solution)/shard_map/attention_backward/pallas_call | solution.py:1196
  113.6 3.3 %collective-permute-done.24 = bf16[4,16,2816]{2,1,0:T(8,128)(2,1)S(1)} collective-permute-done((bf16[4,16,2816]{2,1,0:T(8,128)(2,1)S(1)}, bf16[4,16,2816]{2,1,0:T(8,128)(2,1)S(1)}, u32[]{:S(2)}, u32[]{:S(2)}) %collective-permute-start.24) | collective-permute-done | bytes 360480 | tf_op jit(solution)/shard_map/ppermute | solution.py:809
  117.5 1.2 collective-permute-start.27
  118.7 1.8 %collective-permute-start.29 = (bf16[4,16,1024]{2,1,0:T(8,128)(2,1)S(1)}, bf16[4,16,1024]{2,1,0:T(8,128)(2,1)S(1)}, u32[]{:S(2)}, u32[]{:S(2)}) collective-permute-start(bf16[4,16,1024]{2,1,0:T(8,128)(2,1)S(1)} %get-tuple-element.217), channel_id=1, source_target_pairs={{0,6},{2,4},{4,2},{6,0},{8,14},{10,12},{12,10},{14,8},{16,22},{18,... | collective-permute-start | bytes 393224 | tf_op jit(solution)/shard_map/ppermute | solution.py:809
  120.6 0.5 collective-permute-start.28
  121.1 2.5 %collective-permute-start.35 = (bf16[16,2816]{1,0:T(8,128)(2,1)S(1)}, bf16[16,2816]{1,0:T(8,128)(2,1)S(1)}, u32[]{:S(2)}, u32[]{:S(2)}) collective-permute-start(bf16[16,2816]{1,0:T(8,128)(2,1)S(1)} %get-tuple-element.223), channel_id=1, source_target_pairs={{0,24},{2,26},{4,28},{6,30},{8,16},{10,18},{12,20},{14,22},{16,8},... | collective-permute-start | bytes 270344 | tf_op jit(solution)/shard_map/ppermute | solution.py:809
  123.8 1.8 %collective-permute-start.33 = (bf16[16,2816]{1,0:T(8,128)(2,1)S(1)}, bf16[16,2816]{1,0:T(8,128)(2,1)S(1)}, u32[]{:S(2)}, u32[]{:S(2)}) collective-permute-start(bf16[16,2816]{1,0:T(8,128)(2,1)S(1)} %get-tuple-element.225), channel_id=1, source_target_pairs={{0,8},{2,10},{4,12},{6,14},{8,0},{10,2},{12,4},{14,6},{16,24},{18,... | collective-permute-start | bytes 270344 | tf_op jit(solution)/shard_map/ppermute | solution.py:809
  125.6 0.4 collective-permute-done.29
  126.0 1.3 collective-permute-done.28
  127.4 2.5 %collective-permute-start.32 = (bf16[16,1024]{1,0:T(8,128)(2,1)S(1)}, bf16[16,1024]{1,0:T(8,128)(2,1)S(1)}, u32[]{:S(2)}, u32[]{:S(2)}) collective-permute-start(bf16[16,1024]{1,0:T(8,128)(2,1)S(1)} %get-tuple-element.226), channel_id=1, source_target_pairs={{0,24},{2,26},{4,28},{6,30},{8,16},{10,18},{12,20},{14,22},{16,8},... | collective-permute-start | bytes 98312 | tf_op jit(solution)/shard_map/ppermute | solution.py:809
  129.9 1.9 %collective-permute-start.30 = (bf16[16,1024]{1,0:T(8,128)(2,1)S(1)}, bf16[16,1024]{1,0:T(8,128)(2,1)S(1)}, u32[]{:S(2)}, u32[]{:S(2)}) collective-permute-start(bf16[16,1024]{1,0:T(8,128)(2,1)S(1)} %get-tuple-element.228), channel_id=1, source_target_pairs={{0,8},{2,10},{4,12},{6,14},{8,0},{10,2},{12,4},{14,6},{16,24},{18,... | collective-permute-start | bytes 98312 | tf_op jit(solution)/shard_map/ppermute | solution.py:809
  131.9 1.3 collective-permute-done.32.refs_3_
  133.2 1.5 %collective-permute-done.31.refs_2_ = bf16[16,1024]{1,0:T(8,128)(2,1)S(1)} collective-permute-done((bf16[16,1024]{1,0:T(8,128)(2,1)S(1)}, bf16[16,1024]{1,0:T(8,128)(2,1)S(1)}, u32[]{:S(2)}, u32[]{:S(2)}) %collective-permute-start.31) | collective-permute-done | bytes 32800 | tf_op jit(solution)/shard_map/ppermute | solution.py:809
  134.9 11.6 %all_to_all.5.gathered = f32[16,8,128]{2,1,0:T(8,128)S(1)} all-to-all(f32[16,8,128]{2,1,0:T(8,128)S(1)} %get-tuple-element.179), channel_id=1, replica_groups=mesh['wide'=16,'narrow'=2] {'wide'}, dimensions={0} | all-to-all | bytes 131072 | tf_op jit(solution)/shard_map/all_to_all | solution.py:1249
  146.5 0.5 collective-permute-start.36
  147.0 0.9 collective-permute-done.36.swapped
  148.1 1.3 adam.1
  (114 shorter events, 3.1 us)
Async XLA Ops:
  2.3 9.2 %collective-permute-start.2 = (bf16[16,2048]{1,0:T(8,128)(2,1)}, bf16[16,2048]{1,0:T(8,128)(2,1)S(1)}, u32[]{:S(2)}, u32[]{:S(2)}) collective-permute-start(bf16[16,2048]{1,0:T(8,128)(2,1)} %pack.1), channel_id=1, source_target_pairs={{0,24},{2,26},{4,28},{6,30},{8,16},{10,18},{12,20},{14,22},{16,8},... | collective-permute-start | bytes 196616 | tf_op jit(solution)/shard_map/ppermute | solution.py:809
  7.4 5.8 %collective-permute-start.1 = (bf16[16,2048]{1,0:T(8,128)(2,1)}, bf16[16,2048]{1,0:T(8,128)(2,1)S(1)}, u32[]{:S(2)}, u32[]{:S(2)}) collective-permute-start(bf16[16,2048]{1,0:T(8,128)(2,1)} %pack.1), channel_id=1, source_target_pairs={{0,16},{2,18},{4,20},{6,22},{8,24},{10,26},{12,28},{14,30},{16,0},... | collective-permute-start | bytes 196616 | tf_op jit(solution)/shard_map/ppermute | solution.py:809
  7.4 5.8 %collective-permute-start = (bf16[16,2048]{1,0:T(8,128)(2,1)}, bf16[16,2048]{1,0:T(8,128)(2,1)S(1)}, u32[]{:S(2)}, u32[]{:S(2)}) collective-permute-start(bf16[16,2048]{1,0:T(8,128)(2,1)} %pack.1), channel_id=1, source_target_pairs={{0,8},{2,10},{4,12},{6,14},{8,0},{10,2},{12,4},{14,6},{16,24},{18,... | collective-permute-start | bytes 196616 | tf_op jit(solution)/shard_map/ppermute | solution.py:809
  7.9 3.6 %collective-permute-start.3 = (f32[2,512]{1,0:T(2,128)}, f32[2,512]{1,0:T(2,128)S(1)}, u32[]{:S(2)}, u32[]{:S(2)}) collective-permute-start(f32[2,512]{1,0:T(2,128)} %refs_12_.1), channel_id=1, source_target_pairs={{0,1},{1,0},{2,3},{3,2},{4,5},{5,4},{6,7},{7,6},{8,9},{9,8},{10,11... | collective-permute-start | bytes 12296 | tf_op jit(solution)/shard_map/ppermute | solution.py:809
  14.1 5.1 %collective-permute-start.4 = (bf16[4,16,2048]{2,1,0:T(8,128)(2,1)S(1)}, bf16[4,16,2048]{2,1,0:T(8,128)(2,1)S(1)}, u32[]{:S(2)}, u32[]{:S(2)}) collective-permute-start(bf16[4,16,2048]{2,1,0:T(8,128)(2,1)S(1)} %pad_maximum_fusion.4.refs_4_), channel_id=1, source_target_pairs={{0,1},{1,0},{2,3},{3,2},{4,5},{5,4},{6,7},{7,6},{8,9},{9,8},{10,11... | collective-permute-start | bytes 786440 | tf_op jit(solution)/shard_map/ppermute | solution.py:809
  14.1 12.3 %collective-permute-start.8 = (bf16[4,16,2048]{2,1,0:T(8,128)(2,1)S(1)}, bf16[4,16,2048]{2,1,0:T(8,128)(2,1)S(1)}, u32[]{:S(2)}, u32[]{:S(2)}) collective-permute-start(bf16[4,16,2048]{2,1,0:T(8,128)(2,1)S(1)} %pad_maximum_fusion.4.refs_4_), channel_id=1, source_target_pairs={{0,6},{2,4},{4,2},{6,0},{8,14},{10,12},{12,10},{14,8},{16,22},{18,... | collective-permute-start | bytes 786440 | tf_op jit(solution)/shard_map/ppermute | solution.py:809
  16.7 12.7 %collective-permute-start.14 = (bf16[4,16,2048]{2,1,0:T(8,128)(2,1)S(1)}, bf16[4,16,2048]{2,1,0:T(8,128)(2,1)S(1)}, u32[]{:S(2)}, u32[]{:S(2)}) collective-permute-start(bf16[4,16,2048]{2,1,0:T(8,128)(2,1)S(1)} %pad_maximum_fusion.4.refs_4_), channel_id=1, source_target_pairs={{0,4},{2,6},{4,0},{6,2},{8,12},{10,14},{12,8},{14,10},{16,20},{18,... | collective-permute-start | bytes 786440 | tf_op jit(solution)/shard_map/ppermute | solution.py:809
  17.2 12.3 %collective-permute-start.13 = (bf16[4,16,2048]{2,1,0:T(8,128)(2,1)S(1)}, bf16[4,16,2048]{2,1,0:T(8,128)(2,1)S(1)}, u32[]{:S(2)}, u32[]{:S(2)}) collective-permute-start(bf16[4,16,2048]{2,1,0:T(8,128)(2,1)S(1)} %pad_maximum_fusion.4.refs_4_), channel_id=1, source_target_pairs={{0,2},{2,0},{4,6},{6,4},{8,10},{10,8},{12,14},{14,12},{16,18},{18,... | collective-permute-start | bytes 786440 | tf_op jit(solution)/shard_map/ppermute | solution.py:809
  19.1 4.9 %collective-permute-start.5 = (bf16[16,1792]{1,0:T(8,128)(2,1)}, bf16[16,1792]{1,0:T(8,128)(2,1)S(1)}, u32[]{:S(2)}, u32[]{:S(2)}) collective-permute-start(bf16[16,1792]{1,0:T(8,128)(2,1)} %pack_second.1), channel_id=1, source_target_pairs={{0,8},{2,10},{4,12},{6,14},{8,0},{10,2},{12,4},{14,6},{16,24},{18,... | collective-permute-start | bytes 172040 | tf_op jit(solution)/shard_map/ppermute | solution.py:809
  20.2 9.7 %collective-permute-start.6 = (bf16[16,1792]{1,0:T(8,128)(2,1)}, bf16[16,1792]{1,0:T(8,128)(2,1)S(1)}, u32[]{:S(2)}, u32[]{:S(2)}) collective-permute-start(bf16[16,1792]{1,0:T(8,128)(2,1)} %pack_second.1), channel_id=1, source_target_pairs={{0,16},{2,18},{4,20},{6,22},{8,24},{10,26},{12,28},{14,30},{16,0},... | collective-permute-start | bytes 172040 | tf_op jit(solution)/shard_map/ppermute | solution.py:809
  24.0 6.2 %collective-permute-start.7 = (bf16[16,1792]{1,0:T(8,128)(2,1)}, bf16[16,1792]{1,0:T(8,128)(2,1)S(1)}, u32[]{:S(2)}, u32[]{:S(2)}) collective-permute-start(bf16[16,1792]{1,0:T(8,128)(2,1)} %pack_second.1), channel_id=1, source_target_pairs={{0,24},{2,26},{4,28},{6,30},{8,16},{10,18},{12,20},{14,22},{16,8},... | collective-permute-start | bytes 172040 | tf_op jit(solution)/shard_map/ppermute | solution.py:809
  26.5 4.6 %collective-permute-start.9 = (bf16[4,16,2048]{2,1,0:T(8,128)(2,1)S(1)}, bf16[4,16,2048]{2,1,0:T(8,128)(2,1)S(1)}, u32[]{:S(2)}, u32[]{:S(2)}) collective-permute-start(bf16[4,16,2048]{2,1,0:T(8,128)(2,1)S(1)} %collective-permute-done.8.refs_7_), channel_id=1, source_target_pairs={{0,1},{1,0},{2,3},{3,2},{4,5},{5,4},{6,7},{7,6},{8,9},{9,8},{10,11... | collective-permute-start | bytes 786440 | tf_op jit(solution)/shard_map/ppermute | solution.py:809
  29.4 4.8 %collective-permute-start.16 = (bf16[4,16,2048]{2,1,0:T(8,128)(2,1)S(1)}, bf16[4,16,2048]{2,1,0:T(8,128)(2,1)S(1)}, u32[]{:S(2)}, u32[]{:S(2)}) collective-permute-start(bf16[4,16,2048]{2,1,0:T(8,128)(2,1)S(1)} %collective-permute-done.14.refs_6_), channel_id=1, source_target_pairs={{0,1},{1,0},{2,3},{3,2},{4,5},{5,4},{6,7},{7,6},{8,9},{9,8},{10,11... | collective-permute-start | bytes 786440 | tf_op jit(solution)/shard_map/ppermute | solution.py:809
  29.5 5.2 %collective-permute-start.15 = (bf16[4,16,2048]{2,1,0:T(8,128)(2,1)S(1)}, bf16[4,16,2048]{2,1,0:T(8,128)(2,1)S(1)}, u32[]{:S(2)}, u32[]{:S(2)}) collective-permute-start(bf16[4,16,2048]{2,1,0:T(8,128)(2,1)S(1)} %collective-permute-done.13.refs_5_), channel_id=1, source_target_pairs={{0,1},{1,0},{2,3},{3,2},{4,5},{5,4},{6,7},{7,6},{8,9},{9,8},{10,11... | collective-permute-start | bytes 786440 | tf_op jit(solution)/shard_map/ppermute | solution.py:809
  31.1 19.5 %collective-permute-start.17 = (bf16[4,16,1792]{2,1,0:T(8,128)(2,1)S(1)}, bf16[4,16,1792]{2,1,0:T(8,128)(2,1)S(1)}, u32[]{:S(2)}, u32[]{:S(2)}) collective-permute-start(bf16[4,16,1792]{2,1,0:T(8,128)(2,1)S(1)} %pad_maximum_fusion.5.refs_7_), channel_id=1, source_target_pairs={{0,1},{1,0},{2,3},{3,2},{4,5},{5,4},{6,7},{7,6},{8,9},{9,8},{10,11... | collective-permute-start | bytes 688136 | tf_op jit(solution)/shard_map/ppermute | solution.py:809
  31.1 18.7 %collective-permute-start.12 = (bf16[4,16,1792]{2,1,0:T(8,128)(2,1)S(1)}, bf16[4,16,1792]{2,1,0:T(8,128)(2,1)S(1)}, u32[]{:S(2)}, u32[]{:S(2)}) collective-permute-start(bf16[4,16,1792]{2,1,0:T(8,128)(2,1)S(1)} %pad_maximum_fusion.5.refs_7_), channel_id=1, source_target_pairs={{0,6},{2,4},{4,2},{6,0},{8,14},{10,12},{12,10},{14,8},{16,22},{18,... | collective-permute-start | bytes 688136 | tf_op jit(solution)/shard_map/ppermute | solution.py:809
  33.7 16.2 %collective-permute-start.11 = (bf16[4,16,1792]{2,1,0:T(8,128)(2,1)S(1)}, bf16[4,16,1792]{2,1,0:T(8,128)(2,1)S(1)}, u32[]{:S(2)}, u32[]{:S(2)}) collective-permute-start(bf16[4,16,1792]{2,1,0:T(8,128)(2,1)S(1)} %pad_maximum_fusion.5.refs_7_), channel_id=1, source_target_pairs={{0,4},{2,6},{4,0},{6,2},{8,12},{10,14},{12,8},{14,10},{16,20},{18,... | collective-permute-start | bytes 688136 | tf_op jit(solution)/shard_map/ppermute | solution.py:809
  34.2 15.7 %collective-permute-start.10 = (bf16[4,16,1792]{2,1,0:T(8,128)(2,1)S(1)}, bf16[4,16,1792]{2,1,0:T(8,128)(2,1)S(1)}, u32[]{:S(2)}, u32[]{:S(2)}) collective-permute-start(bf16[4,16,1792]{2,1,0:T(8,128)(2,1)S(1)} %pad_maximum_fusion.5.refs_7_), channel_id=1, source_target_pairs={{0,2},{2,0},{4,6},{6,4},{8,10},{10,8},{12,14},{14,12},{16,18},{18,... | collective-permute-start | bytes 688136 | tf_op jit(solution)/shard_map/ppermute | solution.py:809
  49.9 1.6 %collective-permute-start.18 = (bf16[4,16,1792]{2,1,0:T(8,128)(2,1)S(1)}, bf16[4,16,1792]{2,1,0:T(8,128)(2,1)S(1)}, u32[]{:S(2)}, u32[]{:S(2)}) collective-permute-start(bf16[4,16,1792]{2,1,0:T(8,128)(2,1)S(1)} %collective-permute-done.10.refs_8_), channel_id=1, source_target_pairs={{0,1},{1,0},{2,3},{3,2},{4,5},{5,4},{6,7},{7,6},{8,9},{9,8},{10,11... | collective-permute-start | bytes 688136 | tf_op jit(solution)/shard_map/ppermute | solution.py:809
  50.0 1.8 %collective-permute-start.19 = (bf16[4,16,1792]{2,1,0:T(8,128)(2,1)S(1)}, bf16[4,16,1792]{2,1,0:T(8,128)(2,1)S(1)}, u32[]{:S(2)}, u32[]{:S(2)}) collective-permute-start(bf16[4,16,1792]{2,1,0:T(8,128)(2,1)S(1)} %collective-permute-done.11.refs_9_), channel_id=1, source_target_pairs={{0,1},{1,0},{2,3},{3,2},{4,5},{5,4},{6,7},{7,6},{8,9},{9,8},{10,11... | collective-permute-start | bytes 688136 | tf_op jit(solution)/shard_map/ppermute | solution.py:809
  50.5 1.6 %collective-permute-start.20 = (bf16[4,16,1792]{2,1,0:T(8,128)(2,1)S(1)}, bf16[4,16,1792]{2,1,0:T(8,128)(2,1)S(1)}, u32[]{:S(2)}, u32[]{:S(2)}) collective-permute-start(bf16[4,16,1792]{2,1,0:T(8,128)(2,1)S(1)} %collective-permute-done.12.refs_10_), channel_id=1, source_target_pairs={{0,1},{1,0},{2,3},{3,2},{4,5},{5,4},{6,7},{7,6},{8,9},{9,8},{10,11... | collective-permute-start | bytes 688136 | tf_op jit(solution)/shard_map/ppermute | solution.py:809
  87.9 9.0 %collective-permute-start.21 = (bf16[4,4,16,1792]{3,2,1,0:T(8,128)(2,1)S(1)}, bf16[4,4,16,1792]{3,2,1,0:T(8,128)(2,1)S(1)}, u32[]{:S(2)}, u32[]{:S(2)}) collective-permute-start(bf16[4,4,16,1792]{3,2,1,0:T(8,128)(2,1)S(1)} %get-tuple-element.142), channel_id=1, source_target_pairs={{0,1},{1,0},{2,3},{3,2},{4,5},{5,4},{6,7},{7,6},{8,9},{9,8},{10,11... | collective-permute-start | bytes 2752520 | tf_op jit(solution)/shard_map/ppermute | solution.py:809
  94.8 2.0 %collective-permute-start.22 = (bf16[4,4,16,1024]{3,2,1,0:T(8,128)(2,1)S(1)}, bf16[4,4,16,1024]{3,2,1,0:T(8,128)(2,1)S(1)}, u32[]{:S(2)}, u32[]{:S(2)}) collective-permute-start(bf16[4,4,16,1024]{3,2,1,0:T(8,128)(2,1)S(1)} %get-tuple-element.152), channel_id=1, source_target_pairs={{0,1},{1,0},{2,3},{3,2},{4,5},{5,4},{6,7},{7,6},{8,9},{9,8},{10,11... | collective-permute-start | bytes 1572872 | tf_op jit(solution)/shard_map/ppermute | solution.py:809
  97.2 16.4 %collective-permute-start.23 = (bf16[4,16,2816]{2,1,0:T(8,128)(2,1)S(1)}, bf16[4,16,2816]{2,1,0:T(8,128)(2,1)S(1)}, u32[]{:S(2)}, u32[]{:S(2)}) collective-permute-start(bf16[4,16,2816]{2,1,0:T(8,128)(2,1)S(1)} %pad_maximum_fusion.1), channel_id=1, source_target_pairs={{0,2},{2,0},{4,6},{6,4},{8,10},{10,8},{12,14},{14,12},{16,18},{18,... | collective-permute-start | bytes 1081352 | tf_op jit(solution)/shard_map/ppermute | solution.py:809
  98.8 18.1 %collective-permute-start.24 = (bf16[4,16,2816]{2,1,0:T(8,128)(2,1)S(1)}, bf16[4,16,2816]{2,1,0:T(8,128)(2,1)S(1)}, u32[]{:S(2)}, u32[]{:S(2)}) collective-permute-start(bf16[4,16,2816]{2,1,0:T(8,128)(2,1)S(1)} %pad_maximum_fusion.2), channel_id=1, source_target_pairs={{0,4},{2,6},{4,0},{6,2},{8,12},{10,14},{12,8},{14,10},{16,20},{18,... | collective-permute-start | bytes 1081352 | tf_op jit(solution)/shard_map/ppermute | solution.py:809
  100.4 16.5 %collective-permute-start.25 = (bf16[4,16,2816]{2,1,0:T(8,128)(2,1)S(1)}, bf16[4,16,2816]{2,1,0:T(8,128)(2,1)S(1)}, u32[]{:S(2)}, u32[]{:S(2)}) collective-permute-start(bf16[4,16,2816]{2,1,0:T(8,128)(2,1)S(1)} %pad_maximum_fusion.3), channel_id=1, source_target_pairs={{0,6},{2,4},{4,2},{6,0},{8,14},{10,12},{12,10},{14,8},{16,22},{18,... | collective-permute-start | bytes 1081352 | tf_op jit(solution)/shard_map/ppermute | solution.py:809
  113.5 3.4 %collective-permute-start.26 = (bf16[4,4,16,1024]{3,2,1,0:T(8,128)(2,1)S(1)}, bf16[4,4,16,1024]{3,2,1,0:T(8,128)(2,1)S(1)}, u32[]{:S(2)}, u32[]{:S(2)}) collective-permute-start(bf16[4,4,16,1024]{3,2,1,0:T(8,128)(2,1)S(1)} %get-tuple-element.172), channel_id=1, source_target_pairs={{0,1},{1,0},{2,3},{3,2},{4,5},{5,4},{6,7},{7,6},{8,9},{9,8},{10,11... | collective-permute-start | bytes 1572872 | tf_op jit(solution)/shard_map/ppermute | solution.py:809
  117.2 30.7 %copy-start = (f32[2,16,512]{2,1,0:T(8,128)S(1)}, f32[2,16,512]{2,1,0:T(8,128)}, u32[]{:S(2)}) copy-start(f32[2,16,512]{2,1,0:T(8,128)} %refs_9_.1) | copy-start | bytes 196612
  117.2 30.6 %copy-start.1 = (f32[2,512,16]{1,2,0:T(8,128)S(1)}, f32[2,512,16]{1,2,0:T(8,128)}, u32[]{:S(2)}) copy-start(f32[2,512,16]{1,2,0:T(8,128)} %param.54) | copy-start | bytes 196612
  117.2 30.6 %copy-start.2 = (f32[2,3,16,128]{3,2,1,0:T(8,128)S(1)}, f32[2,3,16,128]{3,2,1,0:T(8,128)}, u32[]{:S(2)}) copy-start(f32[2,3,16,128]{3,2,1,0:T(8,128)} %refs_3_.3) | copy-start | bytes 147460
  117.2 30.6 %copy-start.3 = (f32[896,16]{0,1:T(8,128)S(1)}, f32[896,16]{0,1:T(8,128)}, u32[]{:S(2)}) copy-start(f32[896,16]{0,1:T(8,128)} %param.39) | copy-start | bytes 172036
  117.2 30.6 %copy-start.4 = (f32[2,128,16]{1,2,0:T(8,128)S(1)}, f32[2,128,16]{1,2,0:T(8,128)}, u32[]{:S(2)}) copy-start(f32[2,128,16]{1,2,0:T(8,128)} %param.45) | copy-start | bytes 49156
  117.3 30.6 %copy-start.5 = (f32[16,256]{1,0:T(8,128)S(1)}, f32[16,256]{1,0:T(8,128)}, u32[]{:S(2)}) copy-start(f32[16,256]{1,0:T(8,128)} %refs_21_.1) | copy-start | bytes 49156
  117.3 30.6 %copy-start.6 = (f32[2,16,512]{2,1,0:T(8,128)S(1)}, f32[2,16,512]{2,1,0:T(8,128)}, u32[]{:S(2)}) copy-start(f32[2,16,512]{2,1,0:T(8,128)} %refs_10_.1) | copy-start | bytes 196612
  117.3 30.6 %copy-start.7 = (f32[2,16,512]{2,1,0:T(8,128)S(1)}, f32[2,16,512]{2,1,0:T(8,128)}, u32[]{:S(2)}) copy-start(f32[2,16,512]{2,1,0:T(8,128)} %refs_11_.1) | copy-start | bytes 196612
  117.3 30.6 %copy-start.8 = (f32[2,512,16]{1,2,0:T(8,128)S(1)}, f32[2,512,16]{1,2,0:T(8,128)}, u32[]{:S(2)}) copy-start(f32[2,512,16]{1,2,0:T(8,128)} %param.55) | copy-start | bytes 196612
  117.3 30.6 %copy-start.9 = (f32[2,512,16]{1,2,0:T(8,128)S(1)}, f32[2,512,16]{1,2,0:T(8,128)}, u32[]{:S(2)}) copy-start(f32[2,512,16]{1,2,0:T(8,128)} %param.56) | copy-start | bytes 196612
  117.5 6.2 %collective-permute-start.27 = (bf16[4,16,1024]{2,1,0:T(8,128)(2,1)S(1)}, bf16[4,16,1024]{2,1,0:T(8,128)(2,1)S(1)}, u32[]{:S(2)}, u32[]{:S(2)}) collective-permute-start(bf16[4,16,1024]{2,1,0:T(8,128)(2,1)S(1)} %get-tuple-element.216), channel_id=1, source_target_pairs={{0,2},{2,0},{4,6},{6,4},{8,10},{10,8},{12,14},{14,12},{16,18},{18,... | collective-permute-start | bytes 393224 | tf_op jit(solution)/shard_map/ppermute | solution.py:809
  118.7 7.2 %collective-permute-start.29 = (bf16[4,16,1024]{2,1,0:T(8,128)(2,1)S(1)}, bf16[4,16,1024]{2,1,0:T(8,128)(2,1)S(1)}, u32[]{:S(2)}, u32[]{:S(2)}) collective-permute-start(bf16[4,16,1024]{2,1,0:T(8,128)(2,1)S(1)} %get-tuple-element.217), channel_id=1, source_target_pairs={{0,6},{2,4},{4,2},{6,0},{8,14},{10,12},{12,10},{14,8},{16,22},{18,... | collective-permute-start | bytes 393224 | tf_op jit(solution)/shard_map/ppermute | solution.py:809
  120.6 6.7 %collective-permute-start.28 = (bf16[4,16,1024]{2,1,0:T(8,128)(2,1)S(1)}, bf16[4,16,1024]{2,1,0:T(8,128)(2,1)S(1)}, u32[]{:S(2)}, u32[]{:S(2)}) collective-permute-start(bf16[4,16,1024]{2,1,0:T(8,128)(2,1)S(1)} %get-tuple-element.218), channel_id=1, source_target_pairs={{0,4},{2,6},{4,0},{6,2},{8,12},{10,14},{12,8},{14,10},{16,20},{18,... | collective-permute-start | bytes 393224 | tf_op jit(solution)/shard_map/ppermute | solution.py:809
  121.1 8.8 %collective-permute-start.35 = (bf16[16,2816]{1,0:T(8,128)(2,1)S(1)}, bf16[16,2816]{1,0:T(8,128)(2,1)S(1)}, u32[]{:S(2)}, u32[]{:S(2)}) collective-permute-start(bf16[16,2816]{1,0:T(8,128)(2,1)S(1)} %get-tuple-element.223), channel_id=1, source_target_pairs={{0,24},{2,26},{4,28},{6,30},{8,16},{10,18},{12,20},{14,22},{16,8},... | collective-permute-start | bytes 270344 | tf_op jit(solution)/shard_map/ppermute | solution.py:809
  123.6 8.2 %collective-permute-start.34 = (bf16[16,2816]{1,0:T(8,128)(2,1)S(1)}, bf16[16,2816]{1,0:T(8,128)(2,1)S(1)}, u32[]{:S(2)}, u32[]{:S(2)}) collective-permute-start(bf16[16,2816]{1,0:T(8,128)(2,1)S(1)} %get-tuple-element.224), channel_id=1, source_target_pairs={{0,16},{2,18},{4,20},{6,22},{8,24},{10,26},{12,28},{14,30},{16,0},... | collective-permute-start | bytes 270344 | tf_op jit(solution)/shard_map/ppermute | solution.py:809
  123.8 8.1 %collective-permute-start.33 = (bf16[16,2816]{1,0:T(8,128)(2,1)S(1)}, bf16[16,2816]{1,0:T(8,128)(2,1)S(1)}, u32[]{:S(2)}, u32[]{:S(2)}) collective-permute-start(bf16[16,2816]{1,0:T(8,128)(2,1)S(1)} %get-tuple-element.225), channel_id=1, source_target_pairs={{0,8},{2,10},{4,12},{6,14},{8,0},{10,2},{12,4},{14,6},{16,24},{18,... | collective-permute-start | bytes 270344 | tf_op jit(solution)/shard_map/ppermute | solution.py:809
  127.4 5.8 %collective-permute-start.32 = (bf16[16,1024]{1,0:T(8,128)(2,1)S(1)}, bf16[16,1024]{1,0:T(8,128)(2,1)S(1)}, u32[]{:S(2)}, u32[]{:S(2)}) collective-permute-start(bf16[16,1024]{1,0:T(8,128)(2,1)S(1)} %get-tuple-element.226), channel_id=1, source_target_pairs={{0,24},{2,26},{4,28},{6,30},{8,16},{10,18},{12,20},{14,22},{16,8},... | collective-permute-start | bytes 98312 | tf_op jit(solution)/shard_map/ppermute | solution.py:809
  129.9 4.8 %collective-permute-start.31 = (bf16[16,1024]{1,0:T(8,128)(2,1)S(1)}, bf16[16,1024]{1,0:T(8,128)(2,1)S(1)}, u32[]{:S(2)}, u32[]{:S(2)}) collective-permute-start(bf16[16,1024]{1,0:T(8,128)(2,1)S(1)} %get-tuple-element.227), channel_id=1, source_target_pairs={{0,16},{2,18},{4,20},{6,22},{8,24},{10,26},{12,28},{14,30},{16,0},... | collective-permute-start | bytes 98312 | tf_op jit(solution)/shard_map/ppermute | solution.py:809
  129.9 4.8 %collective-permute-start.30 = (bf16[16,1024]{1,0:T(8,128)(2,1)S(1)}, bf16[16,1024]{1,0:T(8,128)(2,1)S(1)}, u32[]{:S(2)}, u32[]{:S(2)}) collective-permute-start(bf16[16,1024]{1,0:T(8,128)(2,1)S(1)} %get-tuple-element.228), channel_id=1, source_target_pairs={{0,8},{2,10},{4,12},{6,14},{8,0},{10,2},{12,4},{14,6},{16,24},{18,... | collective-permute-start | bytes 98312 | tf_op jit(solution)/shard_map/ppermute | solution.py:809
  146.5 1.4 collective-permute-start.37
  146.5 1.4 collective-permute-start.36
  (20 other events, 549.3 us)

commit v13 on v11

--- a/solution.py
+++ b/solution.py
@@ -889,8 +889,8 @@
     "middle": 28,
     "ff_backward": 15,
     "attention_backward": 22,
-    "finish": 58,
-    "adam": 58,
+    "finish": 24,
+    "adam": 20,
 }
 
 
@@ -1136,7 +1136,9 @@
         20 * 10**6,
         "middle",
     )(
-        *in_hbm([meta, frame_meta, vectors, up_bias, other_bias]),
+        meta,
+        frame_meta,
+        *in_hbm([vectors, up_bias, other_bias]),
         side_copy,
         stream,
         *resident(second_parts),

time: 152 us -> 149 us (0.980)
  Pallas kernels: 78.2 us -> 75.5 us
  transfers between devices with their start and end apart: 38 -> 38, of which waited for: 14 -> 14; matrix products, arithmetic and copies ran while one was open for 1% -> 1% of each run, Pallas kernels for 24% -> 25%
where the time goes in v13:
time: 149 us
  Pallas kernels  75.5 us (51%)
  starting transfers between devices  36.9 us (25%)
  waiting for transfers between devices  20.3 us (14%)
  blocking collectives  11.6 us (8%)
  other arithmetic  2.62 us (2%)
  between operations  1.49 us (1%)
    ppermute x38, starting transfers between devices, swap(): return lax.ppermute(a, axis, [(i, i ^ distance) for i in range(size)])  36.9 us
    pallas_call x1, Pallas kernels, per_device(): call(functools.partial(middle_kernel, fast), (count,), [meta_spec, row_sp...  35.5 us
    ppermute x38, waiting for transfers between devices, swap(): return lax.ppermute(a, axis, [(i, i ^ distance) for i in range(size)])  20.3 us
    pallas_call x1, Pallas kernels, per_device(): call(functools.partial(first_forward_kernel, fast), (count,), [hits_spec]...  15.1 us
    pallas_call x1, Pallas kernels, per_device(): call(functools.partial(attention_backward_kernel, fast), (count,), [full_...  12.5 us
    all_to_all x1, blocking collectives, per_device(): gathered = lax.all_to_all(small, 'wide', 0, 0)  11.6 us
    pallas_call x1, Pallas kernels, per_device(): call(functools.partial(ff_backward_kernel, fast), (count,), [full_spec(ve...  6.5 us
  transfers between devices with their start and end apart: 38, of which 14 were waited for; matrix products, arithmetic and copies ran while one was open for 1% of the time, Pallas kernels for 25%

profile of v13, /device:TPU:0, one launch (start us, length us, event | category | flops | bytes accessed | tf_op | source)
XLA Modules:
  0.0 148.6 jit_solution(464481350940186416)
XLA Ops:
  0.7 1.7 %pack.1 = (bf16[16,2048]{1,0:T(8,128)(2,1)}, bf16[16,1792]{1,0:T(8,128)(2,1)}) custom-call(f32[16,896]{1,0:T(8,128)} %bitcast.86, f32[2,3,16,128]{3,2,1,0:T(8,128)} %refs_3_.3, f32[2,16,128]{2,1,0:T(8,128)} %bitcast.88, f32[2,16,512]{2,1,0:T(8,128)} %refs_9_.1, f32[2,16,512]{2,1,0:T(8,128)} %bitcast.84, f32[16,256]{1,0:T(8,128)} %refs_21_.1, f32[5,16]{1,0:T(8,128)} %bitcast.96), custom_call_target="tpu_custom_call" | custom-call | flops 1000000 | bytes 1000000 | tf_op jit(solution)/shard_map/pack/pallas_call | solution.py:1011
  2.4 5.0 %collective-permute-start.2 = (bf16[16,2048]{1,0:T(8,128)(2,1)}, bf16[16,2048]{1,0:T(8,128)(2,1)S(1)}, u32[]{:S(2)}, u32[]{:S(2)}) collective-permute-start(bf16[16,2048]{1,0:T(8,128)(2,1)} %get-tuple-element.127), channel_id=1, source_target_pairs={{0,24},{2,26},{4,28},{6,30},{8,16},{10,18},{12,20},{14,22},{16,8},... | collective-permute-start | bytes 196616 | tf_op jit(solution)/shard_map/ppermute | solution.py:806
  7.5 0.6 collective-permute-start
  8.0 2.7 %prepare.1 = (s32[4,352,128]{2,1,0:T(8,128)S(1)}, s32[4,32,128]{2,1,0:T(8,128)S(1)}, bf16[4,352,896]{2,1,0:T(8,128)(2,1)S(1)}) custom-call(s32[8]{0:T(128)} %games_ref.1, s32[8,16,20]{2,1,0:T(8,128)} %bitcast.103, s32[8,20]{1,0:T(8,128)} %actions.1, s32[8,20]{1,0:T(8,128)} %valid.1, s32[8,20]{1,0:T(8,128)} %rewards.1, s32[8,20]{1,0:T(8,128)} %ends.1), custom_call_target="tpu_custom_call" | custom-call | flops 1000000 | bytes 1000000 | tf_op jit(solution)/shard_map/prepare/pallas_call | solution.py:1026
  10.7 2.5 %collective-permute-done.1 = bf16[16,2048]{1,0:T(8,128)(2,1)S(1)} collective-permute-done((bf16[16,2048]{1,0:T(8,128)(2,1)}, bf16[16,2048]{1,0:T(8,128)(2,1)S(1)}, u32[]{:S(2)}, u32[]{:S(2)}) %collective-permute-start.1) | collective-permute-done | bytes 65568 | tf_op jit(solution)/shard_map/ppermute | solution.py:806
  13.3 0.9 pad_maximum_fusion.4.refs_4_
  14.2 2.5 %collective-permute-start.8 = (bf16[4,16,2048]{2,1,0:T(8,128)(2,1)S(1)}, bf16[4,16,2048]{2,1,0:T(8,128)(2,1)S(1)}, u32[]{:S(2)}, u32[]{:S(2)}) collective-permute-start(bf16[4,16,2048]{2,1,0:T(8,128)(2,1)S(1)} %pad_maximum_fusion.4.refs_4_), channel_id=1, source_target_pairs={{0,6},{2,4},{4,2},{6,0},{8,14},{10,12},{12,10},{14,8},{16,22},{18,... | collective-permute-start | bytes 786440 | tf_op jit(solution)/shard_map/ppermute | solution.py:806
  16.7 0.5 collective-permute-start.14
  17.2 0.5 collective-permute-start.13
  17.8 1.1 collective-permute-start.5
  18.9 2.1 %collective-permute-start.6 = (bf16[16,1792]{1,0:T(8,128)(2,1)}, bf16[16,1792]{1,0:T(8,128)(2,1)S(1)}, u32[]{:S(2)}, u32[]{:S(2)}) collective-permute-start(bf16[16,1792]{1,0:T(8,128)(2,1)} %get-tuple-element.134), channel_id=1, source_target_pairs={{0,16},{2,18},{4,20},{6,22},{8,24},{10,26},{12,28},{14,30},{16,0},... | collective-permute-start | bytes 172040 | tf_op jit(solution)/shard_map/ppermute | solution.py:806
  21.0 1.7 %collective-permute-done.5 = bf16[16,1792]{1,0:T(8,128)(2,1)S(1)} collective-permute-done((bf16[16,1792]{1,0:T(8,128)(2,1)}, bf16[16,1792]{1,0:T(8,128)(2,1)S(1)}, u32[]{:S(2)}, u32[]{:S(2)}) %collective-permute-start.5) | collective-permute-done | bytes 57376 | tf_op jit(solution)/shard_map/ppermute | solution.py:806
  22.6 2.4 %collective-permute-start.7 = (bf16[16,1792]{1,0:T(8,128)(2,1)}, bf16[16,1792]{1,0:T(8,128)(2,1)S(1)}, u32[]{:S(2)}, u32[]{:S(2)}) collective-permute-start(bf16[16,1792]{1,0:T(8,128)(2,1)} %get-tuple-element.134), channel_id=1, source_target_pairs={{0,24},{2,26},{4,28},{6,30},{8,16},{10,18},{12,20},{14,22},{16,8},... | collective-permute-start | bytes 172040 | tf_op jit(solution)/shard_map/ppermute | solution.py:806
  25.1 4.4 %collective-permute-done.14.refs_6_ = bf16[4,16,2048]{2,1,0:T(8,128)(2,1)S(1)} collective-permute-done((bf16[4,16,2048]{2,1,0:T(8,128)(2,1)S(1)}, bf16[4,16,2048]{2,1,0:T(8,128)(2,1)S(1)}, u32[]{:S(2)}, u32[]{:S(2)}) %collective-permute-start.14) | collective-permute-done | bytes 262176 | tf_op jit(solution)/shard_map/ppermute | solution.py:806
  29.6 0.4 collective-permute-start.15
  30.0 0.9 pad_maximum_fusion.5.refs_7_
  31.0 1.7 %collective-permute-start.12 = (bf16[4,16,1792]{2,1,0:T(8,128)(2,1)S(1)}, bf16[4,16,1792]{2,1,0:T(8,128)(2,1)S(1)}, u32[]{:S(2)}, u32[]{:S(2)}) collective-permute-start(bf16[4,16,1792]{2,1,0:T(8,128)(2,1)S(1)} %pad_maximum_fusion.5.refs_7_), channel_id=1, source_target_pairs={{0,6},{2,4},{4,2},{6,0},{8,14},{10,12},{12,10},{14,8},{16,22},{18,... | collective-permute-start | bytes 688136 | tf_op jit(solution)/shard_map/ppermute | solution.py:806
  32.7 1.2 collective-permute-start.11
  34.0 0.5 collective-permute-start.10
  34.5 15.1 %first_forward.1 = (bf16[256,1024]{1,0:T(8,128)(2,1)S(1)}, bf16[256,2048]{1,0:T(8,128)(2,1)S(1)}, bf16[256,128]{1,0:T(8,128)(2,1)S(1)}, f32[4,352,256]{2,1,0:T(8...) custom-call(bf16[4,352,896]{2,1,0:T(8,128)(2,1)S(1)} %get-tuple-elem, ...), custom_call_target="tpu_custom_call" | custom-call | flops 4000000000 | bytes 20000000 | tf_op jit(solution)/shard_map/first_forward/pallas_call | solution.py:1066
  49.8 0.5 collective-permute-start.19
  50.3 0.9 collective-permute-done.18.refs_12_
  51.2 0.3 collective-permute-done.19.refs_13_
  51.6 0.3 collective-permute-done.20.refs_14_
  51.9 35.5 %middle.1 = (f32[4,352,256]{2,1,0:T(8,128)S(1)}, bf16[4,4,16,1792]{3,2,1,0:T(8,128)(2,1)S(1)}, bf16[4,4,16,1792]{3,2,1,0:T(8,128)(2,1)S(1)}, f32[32,8,256]{2,1,0:T(8,128)S(1)}, f32[8,128]{1,0:T(8,128)S(1)}) custom-call(s32[4,352,128]{2,1,0:T(8,128)S(1)} %get-tuple-element.122.refs_0_, s32[4,32,128]{2,1,0:T(8,128)S(1)} %get-tuple-element.123.refs_1_, ...), custom_call_target="tpu_custom_call" | custom-call | flops 15000000512 | bytes 20000000 | tf_op jit(solution)/shard_map/middle/pallas_call | solution.py:1095
  87.6 6.5 %ff_backward.1 = (f32[4,352,256]{2,1,0:T(8,128)S(1)}, bf16[4,4,16,1024]{3,2,1,0:T(8,128)(2,1)S(1)}, bf16[4,4,16,1024]{3,2,1,0:T(8,128)(2,1)S(1)}, f32[32,8,256]{2,1,0:T(8,128)S(1)}) custom-call(f32[14,256]{1,0:T(8,128)} %refs_18_.1, bf16[256,2048]{1,0:T(8,128)(2,1)S(1)} %get-tuple-element.147.refs_1_, f32[4,352,256]{2,1,0:T(8,128)S(1)} %get-tuple-element.148.refs_2_, ...), custom_call_target="tpu_custom_call" | custom-call | flops 4000000000 | bytes 10000000 | tf_op jit(solution)/shard_map/ff_backward/pallas_call | solution.py:1152
  94.1 0.3 collective-permute-start.22
  94.5 1.7 %collective-permute-done.22 = bf16[4,4,16,1024]{3,2,1,0:T(8,128)(2,1)S(1)} collective-permute-done((bf16[4,4,16,1024]{3,2,1,0:T(8,128)(2,1)S(1)}, bf16[4,4,16,1024]{3,2,1,0:T(8,128)(2,1)S(1)}, u32[]{:S(2)}, u32[]{:S(2)}) %collective-permute-start.22) | collective-permute-done | bytes 524320 | tf_op jit(solution)/shard_map/ppermute | solution.py:806
  96.6 1.5 %collective-permute-start.23 = (bf16[4,16,2816]{2,1,0:T(8,128)(2,1)S(1)}, bf16[4,16,2816]{2,1,0:T(8,128)(2,1)S(1)}, u32[]{:S(2)}, u32[]{:S(2)}) collective-permute-start(bf16[4,16,2816]{2,1,0:T(8,128)(2,1)S(1)} %pad_maximum_fusion.1), channel_id=1, source_target_pairs={{0,2},{2,0},{4,6},{6,4},{8,10},{10,8},{12,14},{14,12},{16,18},{18,... | collective-permute-start | bytes 1081352 | tf_op jit(solution)/shard_map/ppermute | solution.py:806
  98.1 0.9 collective-permute-start.24
  99.0 1.3 collective-permute-start.25
  100.3 12.5 %attention_backward.1 = (bf16[4,4,16,1024]{3,2,1,0:T(8,128)(2,1)S(1)}, bf16[4,4,16,1024]{3,2,1,0:T(8,128)(2,1)S(1)}, f32[32,256]{1,0:T(8,128)}) custom-call(f32[14,256]{1,0:T(8,128)} %refs_18_.1, bf16[256,1024]{1,0:T(8,128)(2,1)S(1)} %get-tuple-element.157.refs_1_, f32[4,352,256]{2,1,0:T(8,128)S(1)} %get-tuple-element.158.refs_2_, ...), custom_call_target="tpu_custom_call" | custom-call | flops 6000000000 | bytes 20000000 | tf_op jit(solution)/shard_map/attention_backward/pallas_call | solution.py:1177
  112.8 3.4 %collective-permute-done.24 = bf16[4,16,2816]{2,1,0:T(8,128)(2,1)S(1)} collective-permute-done((bf16[4,16,2816]{2,1,0:T(8,128)(2,1)S(1)}, bf16[4,16,2816]{2,1,0:T(8,128)(2,1)S(1)}, u32[]{:S(2)}, u32[]{:S(2)}) %collective-permute-start.24) | collective-permute-done | bytes 360480 | tf_op jit(solution)/shard_map/ppermute | solution.py:806
  116.9 0.6 collective-permute-start.27
  117.5 1.7 %collective-permute-start.29 = (bf16[4,16,1024]{2,1,0:T(8,128)(2,1)S(1)}, bf16[4,16,1024]{2,1,0:T(8,128)(2,1)S(1)}, u32[]{:S(2)}, u32[]{:S(2)}) collective-permute-start(bf16[4,16,1024]{2,1,0:T(8,128)(2,1)S(1)} %get-tuple-element.221), channel_id=1, source_target_pairs={{0,6},{2,4},{4,2},{6,0},{8,14},{10,12},{12,10},{14,8},{16,22},{18,... | collective-permute-start | bytes 393224 | tf_op jit(solution)/shard_map/ppermute | solution.py:806
  119.2 1.2 collective-permute-start.28
  120.5 2.7 %collective-permute-start.35 = (bf16[16,2816]{1,0:T(8,128)(2,1)S(1)}, bf16[16,2816]{1,0:T(8,128)(2,1)S(1)}, u32[]{:S(2)}, u32[]{:S(2)}) collective-permute-start(bf16[16,2816]{1,0:T(8,128)(2,1)S(1)} %get-tuple-element.227), channel_id=1, source_target_pairs={{0,24},{2,26},{4,28},{6,30},{8,16},{10,18},{12,20},{14,22},{16,8},... | collective-permute-start | bytes 270344 | tf_op jit(solution)/shard_map/ppermute | solution.py:806
  123.2 1.7 %collective-permute-start.33 = (bf16[16,2816]{1,0:T(8,128)(2,1)S(1)}, bf16[16,2816]{1,0:T(8,128)(2,1)S(1)}, u32[]{:S(2)}, u32[]{:S(2)}) collective-permute-start(bf16[16,2816]{1,0:T(8,128)(2,1)S(1)} %get-tuple-element.229), channel_id=1, source_target_pairs={{0,8},{2,10},{4,12},{6,14},{8,0},{10,2},{12,4},{14,6},{16,24},{18,... | collective-permute-start | bytes 270344 | tf_op jit(solution)/shard_map/ppermute | solution.py:806
  124.9 1.1 collective-permute-done.28
  126.1 2.7 %collective-permute-start.32 = (bf16[16,1024]{1,0:T(8,128)(2,1)S(1)}, bf16[16,1024]{1,0:T(8,128)(2,1)S(1)}, u32[]{:S(2)}, u32[]{:S(2)}) collective-permute-start(bf16[16,1024]{1,0:T(8,128)(2,1)S(1)} %get-tuple-element.230), channel_id=1, source_target_pairs={{0,24},{2,26},{4,28},{6,30},{8,16},{10,18},{12,20},{14,22},{16,8},... | collective-permute-start | bytes 98312 | tf_op jit(solution)/shard_map/ppermute | solution.py:806
  128.8 1.7 %collective-permute-start.30 = (bf16[16,1024]{1,0:T(8,128)(2,1)S(1)}, bf16[16,1024]{1,0:T(8,128)(2,1)S(1)}, u32[]{:S(2)}, u32[]{:S(2)}) collective-permute-start(bf16[16,1024]{1,0:T(8,128)(2,1)S(1)} %get-tuple-element.232), channel_id=1, source_target_pairs={{0,8},{2,10},{4,12},{6,14},{8,0},{10,2},{12,4},{14,6},{16,24},{18,... | collective-permute-start | bytes 98312 | tf_op jit(solution)/shard_map/ppermute | solution.py:806
  130.6 0.4 collective-permute-done.34.refs_6_
  131.0 1.0 collective-permute-done.32.refs_3_
  132.0 1.6 %collective-permute-done.31.refs_2_ = bf16[16,1024]{1,0:T(8,128)(2,1)S(1)} collective-permute-done((bf16[16,1024]{1,0:T(8,128)(2,1)S(1)}, bf16[16,1024]{1,0:T(8,128)(2,1)S(1)}, u32[]{:S(2)}, u32[]{:S(2)}) %collective-permute-start.31) | collective-permute-done | bytes 32800 | tf_op jit(solution)/shard_map/ppermute | solution.py:806
  133.8 11.6 %all_to_all.5.gathered = f32[16,8,128]{2,1,0:T(8,128)S(1)} all-to-all(f32[16,8,128]{2,1,0:T(8,128)S(1)} %get-tuple-element.183), channel_id=1, replica_groups=mesh['wide'=16,'narrow'=2] {'wide'}, dimensions={0} | all-to-all | bytes 131072 | tf_op jit(solution)/shard_map/all_to_all | solution.py:1230
  145.4 0.5 collective-permute-start.36
  145.9 0.9 collective-permute-done.36.swapped
  147.1 1.3 adam.1
  (109 shorter events, 2.1 us)
Async XLA Ops:
  2.4 8.3 %collective-permute-start.2 = (bf16[16,2048]{1,0:T(8,128)(2,1)}, bf16[16,2048]{1,0:T(8,128)(2,1)S(1)}, u32[]{:S(2)}, u32[]{:S(2)}) collective-permute-start(bf16[16,2048]{1,0:T(8,128)(2,1)} %get-tuple-element.127), channel_id=1, source_target_pairs={{0,24},{2,26},{4,28},{6,30},{8,16},{10,18},{12,20},{14,22},{16,8},... | collective-permute-start | bytes 196616 | tf_op jit(solution)/shard_map/ppermute | solution.py:806
  7.4 5.8 %collective-permute-start.1 = (bf16[16,2048]{1,0:T(8,128)(2,1)}, bf16[16,2048]{1,0:T(8,128)(2,1)S(1)}, u32[]{:S(2)}, u32[]{:S(2)}) collective-permute-start(bf16[16,2048]{1,0:T(8,128)(2,1)} %get-tuple-element.127), channel_id=1, source_target_pairs={{0,16},{2,18},{4,20},{6,22},{8,24},{10,26},{12,28},{14,30},{16,0},... | collective-permute-start | bytes 196616 | tf_op jit(solution)/shard_map/ppermute | solution.py:806
  7.5 5.8 %collective-permute-start = (bf16[16,2048]{1,0:T(8,128)(2,1)}, bf16[16,2048]{1,0:T(8,128)(2,1)S(1)}, u32[]{:S(2)}, u32[]{:S(2)}) collective-permute-start(bf16[16,2048]{1,0:T(8,128)(2,1)} %get-tuple-element.127), channel_id=1, source_target_pairs={{0,8},{2,10},{4,12},{6,14},{8,0},{10,2},{12,4},{14,6},{16,24},{18,... | collective-permute-start | bytes 196616 | tf_op jit(solution)/shard_map/ppermute | solution.py:806
  8.0 2.7 %collective-permute-start.3 = (f32[2,512]{1,0:T(2,128)}, f32[2,512]{1,0:T(2,128)S(1)}, u32[]{:S(2)}, u32[]{:S(2)}) collective-permute-start(f32[2,512]{1,0:T(2,128)} %refs_12_.1), channel_id=1, source_target_pairs={{0,1},{1,0},{2,3},{3,2},{4,5},{5,4},{6,7},{7,6},{8,9},{9,8},{10,11... | collective-permute-start | bytes 12296 | tf_op jit(solution)/shard_map/ppermute | solution.py:806
  14.1 3.6 %collective-permute-start.4 = (bf16[4,16,2048]{2,1,0:T(8,128)(2,1)S(1)}, bf16[4,16,2048]{2,1,0:T(8,128)(2,1)S(1)}, u32[]{:S(2)}, u32[]{:S(2)}) collective-permute-start(bf16[4,16,2048]{2,1,0:T(8,128)(2,1)S(1)} %pad_maximum_fusion.4.refs_4_), channel_id=1, source_target_pairs={{0,1},{1,0},{2,3},{3,2},{4,5},{5,4},{6,7},{7,6},{8,9},{9,8},{10,11... | collective-permute-start | bytes 786440 | tf_op jit(solution)/shard_map/ppermute | solution.py:806
  14.2 10.9 %collective-permute-start.8 = (bf16[4,16,2048]{2,1,0:T(8,128)(2,1)S(1)}, bf16[4,16,2048]{2,1,0:T(8,128)(2,1)S(1)}, u32[]{:S(2)}, u32[]{:S(2)}) collective-permute-start(bf16[4,16,2048]{2,1,0:T(8,128)(2,1)S(1)} %pad_maximum_fusion.4.refs_4_), channel_id=1, source_target_pairs={{0,6},{2,4},{4,2},{6,0},{8,14},{10,12},{12,10},{14,8},{16,22},{18,... | collective-permute-start | bytes 786440 | tf_op jit(solution)/shard_map/ppermute | solution.py:806
  16.7 12.7 %collective-permute-start.14 = (bf16[4,16,2048]{2,1,0:T(8,128)(2,1)S(1)}, bf16[4,16,2048]{2,1,0:T(8,128)(2,1)S(1)}, u32[]{:S(2)}, u32[]{:S(2)}) collective-permute-start(bf16[4,16,2048]{2,1,0:T(8,128)(2,1)S(1)} %pad_maximum_fusion.4.refs_4_), channel_id=1, source_target_pairs={{0,4},{2,6},{4,0},{6,2},{8,12},{10,14},{12,8},{14,10},{16,20},{18,... | collective-permute-start | bytes 786440 | tf_op jit(solution)/shard_map/ppermute | solution.py:806
  17.2 12.3 %collective-permute-start.13 = (bf16[4,16,2048]{2,1,0:T(8,128)(2,1)S(1)}, bf16[4,16,2048]{2,1,0:T(8,128)(2,1)S(1)}, u32[]{:S(2)}, u32[]{:S(2)}) collective-permute-start(bf16[4,16,2048]{2,1,0:T(8,128)(2,1)S(1)} %pad_maximum_fusion.4.refs_4_), channel_id=1, source_target_pairs={{0,2},{2,0},{4,6},{6,4},{8,10},{10,8},{12,14},{14,12},{16,18},{18,... | collective-permute-start | bytes 786440 | tf_op jit(solution)/shard_map/ppermute | solution.py:806
  17.8 4.9 %collective-permute-start.5 = (bf16[16,1792]{1,0:T(8,128)(2,1)}, bf16[16,1792]{1,0:T(8,128)(2,1)S(1)}, u32[]{:S(2)}, u32[]{:S(2)}) collective-permute-start(bf16[16,1792]{1,0:T(8,128)(2,1)} %get-tuple-element.134), channel_id=1, source_target_pairs={{0,8},{2,10},{4,12},{6,14},{8,0},{10,2},{12,4},{14,6},{16,24},{18,... | collective-permute-start | bytes 172040 | tf_op jit(solution)/shard_map/ppermute | solution.py:806
  18.9 11.1 %collective-permute-start.6 = (bf16[16,1792]{1,0:T(8,128)(2,1)}, bf16[16,1792]{1,0:T(8,128)(2,1)S(1)}, u32[]{:S(2)}, u32[]{:S(2)}) collective-permute-start(bf16[16,1792]{1,0:T(8,128)(2,1)} %get-tuple-element.134), channel_id=1, source_target_pairs={{0,16},{2,18},{4,20},{6,22},{8,24},{10,26},{12,28},{14,30},{16,0},... | collective-permute-start | bytes 172040 | tf_op jit(solution)/shard_map/ppermute | solution.py:806
  22.6 7.3 %collective-permute-start.7 = (bf16[16,1792]{1,0:T(8,128)(2,1)}, bf16[16,1792]{1,0:T(8,128)(2,1)S(1)}, u32[]{:S(2)}, u32[]{:S(2)}) collective-permute-start(bf16[16,1792]{1,0:T(8,128)(2,1)} %get-tuple-element.134), channel_id=1, source_target_pairs={{0,24},{2,26},{4,28},{6,30},{8,16},{10,18},{12,20},{14,22},{16,8},... | collective-permute-start | bytes 172040 | tf_op jit(solution)/shard_map/ppermute | solution.py:806
  25.1 5.7 %collective-permute-start.9 = (bf16[4,16,2048]{2,1,0:T(8,128)(2,1)S(1)}, bf16[4,16,2048]{2,1,0:T(8,128)(2,1)S(1)}, u32[]{:S(2)}, u32[]{:S(2)}) collective-permute-start(bf16[4,16,2048]{2,1,0:T(8,128)(2,1)S(1)} %collective-permute-done.8.refs_7_), channel_id=1, source_target_pairs={{0,1},{1,0},{2,3},{3,2},{4,5},{5,4},{6,7},{7,6},{8,9},{9,8},{10,11... | collective-permute-start | bytes 786440 | tf_op jit(solution)/shard_map/ppermute | solution.py:806
  29.5 4.5 %collective-permute-start.16 = (bf16[4,16,2048]{2,1,0:T(8,128)(2,1)S(1)}, bf16[4,16,2048]{2,1,0:T(8,128)(2,1)S(1)}, u32[]{:S(2)}, u32[]{:S(2)}) collective-permute-start(bf16[4,16,2048]{2,1,0:T(8,128)(2,1)S(1)} %collective-permute-done.14.refs_6_), channel_id=1, source_target_pairs={{0,1},{1,0},{2,3},{3,2},{4,5},{5,4},{6,7},{7,6},{8,9},{9,8},{10,11... | collective-permute-start | bytes 786440 | tf_op jit(solution)/shard_map/ppermute | solution.py:806
  29.6 4.9 %collective-permute-start.15 = (bf16[4,16,2048]{2,1,0:T(8,128)(2,1)S(1)}, bf16[4,16,2048]{2,1,0:T(8,128)(2,1)S(1)}, u32[]{:S(2)}, u32[]{:S(2)}) collective-permute-start(bf16[4,16,2048]{2,1,0:T(8,128)(2,1)S(1)} %collective-permute-done.13.refs_5_), channel_id=1, source_target_pairs={{0,1},{1,0},{2,3},{3,2},{4,5},{5,4},{6,7},{7,6},{8,9},{9,8},{10,11... | collective-permute-start | bytes 786440 | tf_op jit(solution)/shard_map/ppermute | solution.py:806
  30.8 19.5 %collective-permute-start.17 = (bf16[4,16,1792]{2,1,0:T(8,128)(2,1)S(1)}, bf16[4,16,1792]{2,1,0:T(8,128)(2,1)S(1)}, u32[]{:S(2)}, u32[]{:S(2)}) collective-permute-start(bf16[4,16,1792]{2,1,0:T(8,128)(2,1)S(1)} %pad_maximum_fusion.5.refs_7_), channel_id=1, source_target_pairs={{0,1},{1,0},{2,3},{3,2},{4,5},{5,4},{6,7},{7,6},{8,9},{9,8},{10,11... | collective-permute-start | bytes 688136 | tf_op jit(solution)/shard_map/ppermute | solution.py:806
  31.0 18.7 %collective-permute-start.12 = (bf16[4,16,1792]{2,1,0:T(8,128)(2,1)S(1)}, bf16[4,16,1792]{2,1,0:T(8,128)(2,1)S(1)}, u32[]{:S(2)}, u32[]{:S(2)}) collective-permute-start(bf16[4,16,1792]{2,1,0:T(8,128)(2,1)S(1)} %pad_maximum_fusion.5.refs_7_), channel_id=1, source_target_pairs={{0,6},{2,4},{4,2},{6,0},{8,14},{10,12},{12,10},{14,8},{16,22},{18,... | collective-permute-start | bytes 688136 | tf_op jit(solution)/shard_map/ppermute | solution.py:806
  32.7 16.9 %collective-permute-start.11 = (bf16[4,16,1792]{2,1,0:T(8,128)(2,1)S(1)}, bf16[4,16,1792]{2,1,0:T(8,128)(2,1)S(1)}, u32[]{:S(2)}, u32[]{:S(2)}) collective-permute-start(bf16[4,16,1792]{2,1,0:T(8,128)(2,1)S(1)} %pad_maximum_fusion.5.refs_7_), channel_id=1, source_target_pairs={{0,4},{2,6},{4,0},{6,2},{8,12},{10,14},{12,8},{14,10},{16,20},{18,... | collective-permute-start | bytes 688136 | tf_op jit(solution)/shard_map/ppermute | solution.py:806
  34.0 15.7 %collective-permute-start.10 = (bf16[4,16,1792]{2,1,0:T(8,128)(2,1)S(1)}, bf16[4,16,1792]{2,1,0:T(8,128)(2,1)S(1)}, u32[]{:S(2)}, u32[]{:S(2)}) collective-permute-start(bf16[4,16,1792]{2,1,0:T(8,128)(2,1)S(1)} %pad_maximum_fusion.5.refs_7_), channel_id=1, source_target_pairs={{0,2},{2,0},{4,6},{6,4},{8,10},{10,8},{12,14},{14,12},{16,18},{18,... | collective-permute-start | bytes 688136 | tf_op jit(solution)/shard_map/ppermute | solution.py:806
  49.7 1.6 %collective-permute-start.18 = (bf16[4,16,1792]{2,1,0:T(8,128)(2,1)S(1)}, bf16[4,16,1792]{2,1,0:T(8,128)(2,1)S(1)}, u32[]{:S(2)}, u32[]{:S(2)}) collective-permute-start(bf16[4,16,1792]{2,1,0:T(8,128)(2,1)S(1)} %collective-permute-done.10.refs_8_), channel_id=1, source_target_pairs={{0,1},{1,0},{2,3},{3,2},{4,5},{5,4},{6,7},{7,6},{8,9},{9,8},{10,11... | collective-permute-start | bytes 688136 | tf_op jit(solution)/shard_map/ppermute | solution.py:806
  49.8 1.8 %collective-permute-start.19 = (bf16[4,16,1792]{2,1,0:T(8,128)(2,1)S(1)}, bf16[4,16,1792]{2,1,0:T(8,128)(2,1)S(1)}, u32[]{:S(2)}, u32[]{:S(2)}) collective-permute-start(bf16[4,16,1792]{2,1,0:T(8,128)(2,1)S(1)} %collective-permute-done.11.refs_9_), channel_id=1, source_target_pairs={{0,1},{1,0},{2,3},{3,2},{4,5},{5,4},{6,7},{7,6},{8,9},{9,8},{10,11... | collective-permute-start | bytes 688136 | tf_op jit(solution)/shard_map/ppermute | solution.py:806
  50.3 1.6 %collective-permute-start.20 = (bf16[4,16,1792]{2,1,0:T(8,128)(2,1)S(1)}, bf16[4,16,1792]{2,1,0:T(8,128)(2,1)S(1)}, u32[]{:S(2)}, u32[]{:S(2)}) collective-permute-start(bf16[4,16,1792]{2,1,0:T(8,128)(2,1)S(1)} %collective-permute-done.12.refs_10_), channel_id=1, source_target_pairs={{0,1},{1,0},{2,3},{3,2},{4,5},{5,4},{6,7},{7,6},{8,9},{9,8},{10,11... | collective-permute-start | bytes 688136 | tf_op jit(solution)/shard_map/ppermute | solution.py:806
  87.4 8.9 %collective-permute-start.21 = (bf16[4,4,16,1792]{3,2,1,0:T(8,128)(2,1)S(1)}, bf16[4,4,16,1792]{3,2,1,0:T(8,128)(2,1)S(1)}, u32[]{:S(2)}, u32[]{:S(2)}) collective-permute-start(bf16[4,4,16,1792]{3,2,1,0:T(8,128)(2,1)S(1)} %get-tuple-element.146), channel_id=1, source_target_pairs={{0,1},{1,0},{2,3},{3,2},{4,5},{5,4},{6,7},{7,6},{8,9},{9,8},{10,11... | collective-permute-start | bytes 2752520 | tf_op jit(solution)/shard_map/ppermute | solution.py:806
  94.1 2.0 %collective-permute-start.22 = (bf16[4,4,16,1024]{3,2,1,0:T(8,128)(2,1)S(1)}, bf16[4,4,16,1024]{3,2,1,0:T(8,128)(2,1)S(1)}, u32[]{:S(2)}, u32[]{:S(2)}) collective-permute-start(bf16[4,4,16,1024]{3,2,1,0:T(8,128)(2,1)S(1)} %get-tuple-element.156), channel_id=1, source_target_pairs={{0,1},{1,0},{2,3},{3,2},{4,5},{5,4},{6,7},{7,6},{8,9},{9,8},{10,11... | collective-permute-start | bytes 1572872 | tf_op jit(solution)/shard_map/ppermute | solution.py:806
  96.6 16.3 %collective-permute-start.23 = (bf16[4,16,2816]{2,1,0:T(8,128)(2,1)S(1)}, bf16[4,16,2816]{2,1,0:T(8,128)(2,1)S(1)}, u32[]{:S(2)}, u32[]{:S(2)}) collective-permute-start(bf16[4,16,2816]{2,1,0:T(8,128)(2,1)S(1)} %pad_maximum_fusion.1), channel_id=1, source_target_pairs={{0,2},{2,0},{4,6},{6,4},{8,10},{10,8},{12,14},{14,12},{16,18},{18,... | collective-permute-start | bytes 1081352 | tf_op jit(solution)/shard_map/ppermute | solution.py:806
  98.1 18.1 %collective-permute-start.24 = (bf16[4,16,2816]{2,1,0:T(8,128)(2,1)S(1)}, bf16[4,16,2816]{2,1,0:T(8,128)(2,1)S(1)}, u32[]{:S(2)}, u32[]{:S(2)}) collective-permute-start(bf16[4,16,2816]{2,1,0:T(8,128)(2,1)S(1)} %pad_maximum_fusion.2), channel_id=1, source_target_pairs={{0,4},{2,6},{4,0},{6,2},{8,12},{10,14},{12,8},{14,10},{16,20},{18,... | collective-permute-start | bytes 1081352 | tf_op jit(solution)/shard_map/ppermute | solution.py:806
  99.0 17.2 %collective-permute-start.25 = (bf16[4,16,2816]{2,1,0:T(8,128)(2,1)S(1)}, bf16[4,16,2816]{2,1,0:T(8,128)(2,1)S(1)}, u32[]{:S(2)}, u32[]{:S(2)}) collective-permute-start(bf16[4,16,2816]{2,1,0:T(8,128)(2,1)S(1)} %pad_maximum_fusion.3), channel_id=1, source_target_pairs={{0,6},{2,4},{4,2},{6,0},{8,14},{10,12},{12,10},{14,8},{16,22},{18,... | collective-permute-start | bytes 1081352 | tf_op jit(solution)/shard_map/ppermute | solution.py:806
  112.8 3.6 %collective-permute-start.26 = (bf16[4,4,16,1024]{3,2,1,0:T(8,128)(2,1)S(1)}, bf16[4,4,16,1024]{3,2,1,0:T(8,128)(2,1)S(1)}, u32[]{:S(2)}, u32[]{:S(2)}) collective-permute-start(bf16[4,4,16,1024]{3,2,1,0:T(8,128)(2,1)S(1)} %get-tuple-element.176), channel_id=1, source_target_pairs={{0,1},{1,0},{2,3},{3,2},{4,5},{5,4},{6,7},{7,6},{8,9},{9,8},{10,11... | collective-permute-start | bytes 1572872 | tf_op jit(solution)/shard_map/ppermute | solution.py:806
  116.6 30.2 %copy-start = (f32[2,16,512]{2,1,0:T(8,128)S(1)}, f32[2,16,512]{2,1,0:T(8,128)}, u32[]{:S(2)}) copy-start(f32[2,16,512]{2,1,0:T(8,128)} %refs_9_.1) | copy-start | bytes 196612
  116.6 30.2 %copy-start.1 = (f32[2,512,16]{1,2,0:T(8,128)S(1)}, f32[2,512,16]{1,2,0:T(8,128)}, u32[]{:S(2)}) copy-start(f32[2,512,16]{1,2,0:T(8,128)} %param.54) | copy-start | bytes 196612
  116.6 30.2 %copy-start.2 = (f32[896,16]{0,1:T(8,128)S(1)}, f32[896,16]{0,1:T(8,128)}, u32[]{:S(2)}) copy-start(f32[896,16]{0,1:T(8,128)} %param.39) | copy-start | bytes 172036
  116.6 30.2 %copy-start.3 = (f32[2,3,16,128]{3,2,1,0:T(8,128)S(1)}, f32[2,3,16,128]{3,2,1,0:T(8,128)}, u32[]{:S(2)}) copy-start(f32[2,3,16,128]{3,2,1,0:T(8,128)} %refs_3_.3) | copy-start | bytes 147460
  116.6 30.2 %copy-start.4 = (f32[2,128,16]{1,2,0:T(8,128)S(1)}, f32[2,128,16]{1,2,0:T(8,128)}, u32[]{:S(2)}) copy-start(f32[2,128,16]{1,2,0:T(8,128)} %param.45) | copy-start | bytes 49156
  116.6 30.2 %copy-start.5 = (f32[16,256]{1,0:T(8,128)S(1)}, f32[16,256]{1,0:T(8,128)}, u32[]{:S(2)}) copy-start(f32[16,256]{1,0:T(8,128)} %refs_21_.1) | copy-start | bytes 49156
  116.6 30.2 %copy-start.6 = (f32[2,16,512]{2,1,0:T(8,128)S(1)}, f32[2,16,512]{2,1,0:T(8,128)}, u32[]{:S(2)}) copy-start(f32[2,16,512]{2,1,0:T(8,128)} %refs_10_.1) | copy-start | bytes 196612
  116.7 30.2 %copy-start.7 = (f32[2,16,512]{2,1,0:T(8,128)S(1)}, f32[2,16,512]{2,1,0:T(8,128)}, u32[]{:S(2)}) copy-start(f32[2,16,512]{2,1,0:T(8,128)} %refs_11_.1) | copy-start | bytes 196612
  116.7 30.2 %copy-start.8 = (f32[2,512,16]{1,2,0:T(8,128)S(1)}, f32[2,512,16]{1,2,0:T(8,128)}, u32[]{:S(2)}) copy-start(f32[2,512,16]{1,2,0:T(8,128)} %param.55) | copy-start | bytes 196612
  116.7 30.2 %copy-start.9 = (f32[2,512,16]{1,2,0:T(8,128)S(1)}, f32[2,512,16]{1,2,0:T(8,128)}, u32[]{:S(2)}) copy-start(f32[2,512,16]{1,2,0:T(8,128)} %param.56) | copy-start | bytes 196612
  116.9 6.3 %collective-permute-start.27 = (bf16[4,16,1024]{2,1,0:T(8,128)(2,1)S(1)}, bf16[4,16,1024]{2,1,0:T(8,128)(2,1)S(1)}, u32[]{:S(2)}, u32[]{:S(2)}) collective-permute-start(bf16[4,16,1024]{2,1,0:T(8,128)(2,1)S(1)} %get-tuple-element.220), channel_id=1, source_target_pairs={{0,2},{2,0},{4,6},{6,4},{8,10},{10,8},{12,14},{14,12},{16,18},{18,... | collective-permute-start | bytes 393224 | tf_op jit(solution)/shard_map/ppermute | solution.py:806
  117.5 7.4 %collective-permute-start.29 = (bf16[4,16,1024]{2,1,0:T(8,128)(2,1)S(1)}, bf16[4,16,1024]{2,1,0:T(8,128)(2,1)S(1)}, u32[]{:S(2)}, u32[]{:S(2)}) collective-permute-start(bf16[4,16,1024]{2,1,0:T(8,128)(2,1)S(1)} %get-tuple-element.221), channel_id=1, source_target_pairs={{0,6},{2,4},{4,2},{6,0},{8,14},{10,12},{12,10},{14,8},{16,22},{18,... | collective-permute-start | bytes 393224 | tf_op jit(solution)/shard_map/ppermute | solution.py:806
  119.2 6.8 %collective-permute-start.28 = (bf16[4,16,1024]{2,1,0:T(8,128)(2,1)S(1)}, bf16[4,16,1024]{2,1,0:T(8,128)(2,1)S(1)}, u32[]{:S(2)}, u32[]{:S(2)}) collective-permute-start(bf16[4,16,1024]{2,1,0:T(8,128)(2,1)S(1)} %get-tuple-element.222), channel_id=1, source_target_pairs={{0,4},{2,6},{4,0},{6,2},{8,12},{10,14},{12,8},{14,10},{16,20},{18,... | collective-permute-start | bytes 393224 | tf_op jit(solution)/shard_map/ppermute | solution.py:806
  120.5 8.3 %collective-permute-start.35 = (bf16[16,2816]{1,0:T(8,128)(2,1)S(1)}, bf16[16,2816]{1,0:T(8,128)(2,1)S(1)}, u32[]{:S(2)}, u32[]{:S(2)}) collective-permute-start(bf16[16,2816]{1,0:T(8,128)(2,1)S(1)} %get-tuple-element.227), channel_id=1, source_target_pairs={{0,24},{2,26},{4,28},{6,30},{8,16},{10,18},{12,20},{14,22},{16,8},... | collective-permute-start | bytes 270344 | tf_op jit(solution)/shard_map/ppermute | solution.py:806
  123.2 7.8 %collective-permute-start.34 = (bf16[16,2816]{1,0:T(8,128)(2,1)S(1)}, bf16[16,2816]{1,0:T(8,128)(2,1)S(1)}, u32[]{:S(2)}, u32[]{:S(2)}) collective-permute-start(bf16[16,2816]{1,0:T(8,128)(2,1)S(1)} %get-tuple-element.228), channel_id=1, source_target_pairs={{0,16},{2,18},{4,20},{6,22},{8,24},{10,26},{12,28},{14,30},{16,0},... | collective-permute-start | bytes 270344 | tf_op jit(solution)/shard_map/ppermute | solution.py:806
  123.2 7.8 %collective-permute-start.33 = (bf16[16,2816]{1,0:T(8,128)(2,1)S(1)}, bf16[16,2816]{1,0:T(8,128)(2,1)S(1)}, u32[]{:S(2)}, u32[]{:S(2)}) collective-permute-start(bf16[16,2816]{1,0:T(8,128)(2,1)S(1)} %get-tuple-element.229), channel_id=1, source_target_pairs={{0,8},{2,10},{4,12},{6,14},{8,0},{10,2},{12,4},{14,6},{16,24},{18,... | collective-permute-start | bytes 270344 | tf_op jit(solution)/shard_map/ppermute | solution.py:806
  126.1 5.9 %collective-permute-start.32 = (bf16[16,1024]{1,0:T(8,128)(2,1)S(1)}, bf16[16,1024]{1,0:T(8,128)(2,1)S(1)}, u32[]{:S(2)}, u32[]{:S(2)}) collective-permute-start(bf16[16,1024]{1,0:T(8,128)(2,1)S(1)} %get-tuple-element.230), channel_id=1, source_target_pairs={{0,24},{2,26},{4,28},{6,30},{8,16},{10,18},{12,20},{14,22},{16,8},... | collective-permute-start | bytes 98312 | tf_op jit(solution)/shard_map/ppermute | solution.py:806
  128.8 4.8 %collective-permute-start.31 = (bf16[16,1024]{1,0:T(8,128)(2,1)S(1)}, bf16[16,1024]{1,0:T(8,128)(2,1)S(1)}, u32[]{:S(2)}, u32[]{:S(2)}) collective-permute-start(bf16[16,1024]{1,0:T(8,128)(2,1)S(1)} %get-tuple-element.231), channel_id=1, source_target_pairs={{0,16},{2,18},{4,20},{6,22},{8,24},{10,26},{12,28},{14,30},{16,0},... | collective-permute-start | bytes 98312 | tf_op jit(solution)/shard_map/ppermute | solution.py:806
  128.8 4.8 %collective-permute-start.30 = (bf16[16,1024]{1,0:T(8,128)(2,1)S(1)}, bf16[16,1024]{1,0:T(8,128)(2,1)S(1)}, u32[]{:S(2)}, u32[]{:S(2)}) collective-permute-start(bf16[16,1024]{1,0:T(8,128)(2,1)S(1)} %get-tuple-element.232), channel_id=1, source_target_pairs={{0,8},{2,10},{4,12},{6,14},{8,0},{10,2},{12,4},{14,6},{16,24},{18,... | collective-permute-start | bytes 98312 | tf_op jit(solution)/shard_map/ppermute | solution.py:806
  145.4 1.4 collective-permute-start.37
  145.4 1.4 collective-permute-start.36
  (18 other events, 536.8 us)
